TPU v7x, 32 devices: a whole 2x2x4 slice. The times are simulated.
32 devices in a mesh: groups: 2 (over y), train: 4 (over x, core), test: 4 (over z).
Axes of the slice: x: 2, y: 2, z: 4, core: 2. Of those that a mesh axis runs over, the one named last changes fastest.
Arguments:
- train_grads: bfloat16 [4096, 8192], P(('groups', 'train'), 'test'), parts along dimension 0, may hold values from -0.0625 to 0.0625
- test_grads: bfloat16 [4096, 8192], P(('groups', 'test'), 'train'), parts along dimension 0, may hold values from -6 to 6
- fisher: bfloat16 [8192, 8192], P('train', 'test')
- chosen_ids: int32 [4096, 16], P(('groups', 'test')), parts along dimension 0, may hold values from 0 to 2047
Outputs:
- scores: float32 [4096, 2048], P(('groups', 'train'), 'test'), parts along dimension 0
- chosen_sums: float32 [4096], P(('groups', 'test')), parts along dimension 0
There are 2 independent parts, one for each index of `groups`. A program takes and returns all parts, laid end to end along the dimension named above; an argument that names none is the same for every part. Nothing has to cross between parts.
Inputs may be any that keep to these rules, and one draw needn't show every extreme that they name: `chosen_ids`: each id names a train row of the same group; ids may repeat.
All inputs are finite; a program needn't handle non-finite values.
Results may differ from a plain program's by a relative error of at most 0.003.
Values may be sent and summed in bfloat16 or wider, within the bound.
No kernel may reach another device: no remote copies, remote signals or barrier semaphores. Data moves between devices by JAX's collectives and lax.ppermute only.
A program may use at most 128 MiB of HBM per device.

v0:
```python
import jax
import jax.numpy as jnp
from jax import lax
from jax.sharding import PartitionSpec as P


def on_device(train_grads, test_grads, fisher, chosen_ids):
    train_whole = lax.all_gather(train_grads, "test", axis=1, tiled=True)
    partial_value = jnp.dot(
        test_grads,
        lax.all_gather(fisher, "test", axis=1, tiled=True),
        preferred_element_type=jnp.float32,
    )
    precond = lax.psum_scatter(partial_value, "train", scatter_dimension=1, tiled=True).astype(
        jnp.bfloat16
    )
    scores = lax.dot_general(
        train_whole,
        lax.all_gather(precond, "train", axis=1, tiled=True),
        (((1,), (1,)), ((), ())),
        preferred_element_type=jnp.float32,
    )
    local_rows = scores.shape[0]
    offset = lax.axis_index("train") * local_rows
    row_ids = jnp.arange(local_rows, dtype=jnp.int32)[None, :, None] + offset
    matches = (chosen_ids.T[:, None, :] == row_ids).astype(jnp.float32)
    counts = jnp.sum(matches, axis=0)
    local_sums = jnp.sum(counts * scores, axis=0)
    chosen_sums = lax.psum(local_sums, "train")
    return (scores, chosen_sums)


def solution(mesh):
    return jax.shard_map(
        on_device,
        mesh=mesh,
        in_specs=(
            P(("groups", "train"), "test"),
            P(("groups", "test"), "train"),
            P("train", "test"),
            P(("groups", "test"), None),
        ),
        out_specs=(P(("groups", "train"), "test"), P(("groups", "test"))),
        check_vma=False,
    )
```

profile of v0, /device:TPU:0, one launch (start us, length us, event | category | flops | bytes accessed | tf_op | source)
XLA Modules:
  0.0 958.6 jit_solution(4488929967980256346)
XLA Ops:
  7.2 0.0 copy-start
  7.2 0.0 all-gather.4.cloned.1.call-start
  7.2 0.7 all-gather.4.cloned.1.call-update
  7.9 0.0 reduce-scatter.2.cloned.1.call-start
  8.0 565.8 %all-gather.4.cloned.1.call-done = bf16[2048,8192]{1,0:T(8,128)(2,1)} async-done(((bf16[2048,2048]{1,0:T(8,128)(2,1)}), bf16[2048,8192]{1,0:T(8,128)(2,1)}) %all-gather.4.cloned.1.call-update) | async-done | bytes 33554448 | tf_op jit(solution)/shard_map/all_gather | solution.py:11
  573.7 0.0 copy-done
  573.7 26.6 %fusion = f32[512,8192]{1,0:T(8,128)} fusion(bf16[512,2048]{1,0:T(8,128)(2,1)S(1)} %copy-done, bf16[2048,8192]{1,0:T(8,128)(2,1)} %all-gather.4.cloned.1.call-done), kind=kOutput, calls=%fused_computation.4 | convolution fusion | flops 17179869184 | bytes 52428800 | tf_op jit(solution)/shard_map/dot_general | solution.py:9
  600.4 0.0 reduce-scatter.2.cloned.1.call-update
  600.4 0.0 copy-start.2
  600.4 0.0 all-gather.8.cloned.1.call-start
  600.5 0.7 all-gather.8.cloned.1.call-update
  601.1 0.2 all-gather.6.cloned.1.call-start
  601.4 123.5 %reduce-scatter.2.cloned.1.call-done = f32[512,2048]{1,0:T(8,128)} async-done(((f32[512,8192]{1,0:T(8,128)}), f32[512,2048]{1,0:T(8,128)}) %reduce-scatter.2.cloned.1.call-update) | async-done | bytes 4194320 | tf_op jit(solution)/shard_map/reduce_scatter | solution.py:14
  724.9 3.8 convert_element_type.6
  728.7 0.0 all-gather.6.cloned.1.call-update
  728.7 0.0 copy-done.2
  728.7 1.7 convert_reduce_fusion
  730.5 145.7 %all-gather.8.cloned.1.call-done = bf16[512,8192]{1,0:T(8,128)(2,1)} async-done(((bf16[512,2048]{1,0:T(8,128)(2,1)}), bf16[512,8192]{1,0:T(8,128)(2,1)}) %all-gather.8.cloned.1.call-update) | async-done | bytes 8388624 | tf_op jit(solution)/shard_map/all_gather | solution.py:8
  876.2 58.0 %all-gather.6.cloned.1.call-done = bf16[512,8192]{1,0:T(8,128)(2,1)} async-done(((bf16[512,2048]{1,0:T(8,128)(2,1)}), bf16[512,8192]{1,0:T(8,128)(2,1)}) %all-gather.6.cloned.1.call-update) | async-done | bytes 8388624 | tf_op jit(solution)/shard_map/all_gather | solution.py:19
  934.2 0.0 copy-start.1
  934.2 11.4 %multiply_reduce_fusion = (f32[512]{0:T(512)S(1)}, f32[512,512]{1,0:T(8,128)}) fusion(f32[512,512]{1,0:T(8,128)S(1)} %convert_reduce_fusion, bf16[512,8192]{1,0:T(8,128)(2,1)} %all-gather.6.cloned.1.call-done, bf16[512,8192]{1,0:T(8,128)(2,1)} %all-gather.8.cloned.1.call-done), kind=kOutput, calls=%fused_computation.2 | convolution fusion | flops 4295491072 | bytes 18876416 | tf_op jit(solution)/shard_map/dot_general | solution.py:17
  945.6 6.5 psum.7
  952.0 0.0 copy-done.1
  (1 shorter events, 0.0 us)
Async XLA Ops:
  7.2 566.6 %copy-start = (bf16[512,2048]{1,0:T(8,128)(2,1)S(1)}, bf16[512,2048]{1,0:T(8,128)(2,1)}, u32[]{:S(2)}) copy-start(bf16[512,2048]{1,0:T(8,128)(2,1)} %param.5) | copy-start | bytes 6291460
  7.2 566.6 %all-gather.4.cloned.1.call-start = ((), (), s32[]{:S(2)}) async-start(), calls=%async_computation.1 | async-start | bytes 41943040 | tf_op jit(solution)/shard_map/all_gather | solution.py:11
  7.9 716.9 %reduce-scatter.2.cloned.1.call-start = ((), (), s32[]{:S(2)}) async-start(), calls=%async_computation.2 | async-start | bytes 20971520 | tf_op jit(solution)/shard_map/reduce_scatter | solution.py:14
  600.4 128.3 %copy-start.2 = (s32[512,16]{0,1:T(8,128)S(1)}, s32[512,16]{0,1:T(8,128)}, u32[]{:S(2)}) copy-start(s32[512,16]{0,1:T(8,128)} %param.7) | copy-start | bytes 98308
  600.4 275.8 %all-gather.8.cloned.1.call-start = ((), (), s32[]{:S(2)}) async-start(), calls=%async_computation.4 | async-start | bytes 10485760 | tf_op jit(solution)/shard_map/all_gather | solution.py:8
  601.1 333.0 %all-gather.6.cloned.1.call-start = ((), (), s32[]{:S(2)}) async-start(), calls=%async_computation.3 | async-start | bytes 10485760 | tf_op jit(solution)/shard_map/all_gather | solution.py:19
  934.2 17.9 %copy-start.1 = (bf16[512,2048]{1,0:T(8,128)(2,1)S(1)}, bf16[512,2048]{1,0:T(8,128)(2,1)}, u32[]{:S(2)}) copy-start(bf16[512,2048]{1,0:T(8,128)(2,1)} %param.5) | copy-start | bytes 6291460
Sparse Core Ops, SparseCore 0:
  9.6 564.0 all-gather.3
  600.5 124.2 reduce-scatter.1
  726.5 149.6 all-gather.7
  877.7 56.4 all-gather.5
where the time goes:
time: 959 us
  waiting for transfers between devices  894 us (93%)
  matrix products  38 us (4%)
  between operations  13.8 us (1%)
    all_gather x1, waiting for transfers between devices, on_device(): lax.all_gather(fisher, 'test', axis=1, tiled=True)  566 us
    all_gather x1, waiting for transfers between devices, on_device(): train_whole = lax.all_gather(train_grads, 'test', axis=1, tiled=True)  146 us
    reduce_scatter x1, waiting for transfers between devices, on_device(): lax.psum_scatter(partial_value, 'train', scatter_dimension=1, tiled=True)  123 us
    all_gather x1, waiting for transfers between devices, on_device(): lax.all_gather(precond, 'train', axis=1, tiled=True)  58 us
    dot_general x1, matrix products, on_device(): jnp.dot(test_grads, lax.all_gather(fisher, 'test', axis=1, tiled=True), p...  26.6 us
  transfers between devices with their start and end apart: 4, of which 4 were waited for; matrix products, arithmetic and copies ran while one was open for 1% of the time, Pallas kernels for 0%

commit v1 on v0

v1 whole, which is shorter than its diff:
```python
import jax
import jax.numpy as jnp
from jax import lax
from jax.sharding import PartitionSpec as P

CHUNKS = 4

F32 = jnp.float32
BF16 = jnp.bfloat16


def dot_t(a, b):
    return lax.dot_general(a, b, (((1,), (1,)), ((), ())), preferred_element_type=F32)


def selection_counts(chosen_ids, first_row, rows):
    row_ids = first_row + lax.broadcasted_iota(jnp.int32, (rows, chosen_ids.shape[0]), 0)
    ids = chosen_ids.T
    counts = jnp.zeros(row_ids.shape, F32)
    for k in range(ids.shape[0]):
        counts = counts + (row_ids == ids[k][None, :]).astype(F32)
    return counts


def any_mesh(train_grads, test_grads, fisher, chosen_ids):
    test_whole = lax.all_gather(test_grads, "test", axis=0, tiled=True)
    partial_value = jnp.dot(test_whole, fisher, preferred_element_type=F32)
    precond = lax.psum(partial_value, "train").astype(BF16)
    partial_scores = dot_t(train_grads, precond)
    scores = lax.psum_scatter(partial_scores, "test", scatter_dimension=1, tiled=True)
    rows = scores.shape[0]
    counts = selection_counts(chosen_ids, lax.axis_index("train") * rows, rows)
    return scores, lax.psum(jnp.sum(counts * scores, axis=0), "train")


def four_by_four(train_grads, test_grads, fisher, chosen_ids):
    z = lax.axis_index("test")
    i = lax.axis_index("train")
    chip, core = i // 2, i % 2
    inner = (z == 1) | (z == 2)
    quarter = test_grads.shape[0] // CHUNKS // 4
    own_rows = train_grads.shape[0]

    def along(value, pairs):
        return lax.ppermute(value, "test", pairs)

    def to_other(value, r):
        return lax.ppermute(value, "train", [(k, k ^ r) for k in range(4)])

    pair = [(0, 1), (1, 0), (2, 3), (3, 2)]
    middle = [(1, 2), (2, 1)]
    outward = [(1, 0), (2, 3)]
    inward = [(0, 1), (3, 2)]

    def reorder(parts):
        parts = [jnp.where(core == 0, parts[r], parts[r ^ 1]) for r in range(4)]
        return [jnp.where(chip == 0, parts[r], parts[r ^ 2]) for r in range(4)]

    in_quarters = test_grads.reshape(CHUNKS, 4, quarter, -1)
    relative = reorder([in_quarters[:, q] for q in range(4)])
    chunked = jnp.concatenate([relative[r] for r in (0, 2, 1, 3)], axis=1)

    grads = [train_grads, to_other(train_grads, 1), to_other(train_grads, 2)]
    grads = jnp.concatenate(grads + [to_other(grads[2], 1)])

    def scores_part(block):
        part = jnp.dot(block, fisher, preferred_element_type=F32)
        chip_part = part[: 2 * quarter] + to_other(part[2 * quarter :], 1)
        precond = chip_part[:quarter] + to_other(chip_part[quarter:], 2)
        return dot_t(precond.astype(BF16), grads)

    own, near, second, third = [], [], [], []
    for c in range(CHUNKS):
        block = chunked[c]
        near.append(along(block, pair))
        second.append(along(block, middle))
    for c in range(CHUNKS):
        third.append(along(near[c], middle))
    for c in range(CHUNKS):
        second[c] = jnp.where(inner, second[c], along(second[c], outward))
    for c in range(CHUNKS):
        third[c] = jnp.where(inner, third[c], along(third[c], outward))

    pieces = []
    for c in range(CHUNKS):
        own.append(scores_part(chunked[c]))
    for c in range(CHUNKS):
        near[c] = scores_part(near[c])
    for c in range(CHUNKS):
        value = scores_part(second[c])
        value = value + along(value.astype(BF16), inward).astype(F32)
        own[c] = own[c] + along(value.astype(BF16), middle).astype(F32)
    for c in range(CHUNKS):
        value = scores_part(third[c])
        value = value + along(value.astype(BF16), inward).astype(F32)
        value = near[c] + along(value.astype(BF16), middle).astype(F32)
        pieces.append(own[c] + along(value.astype(BF16), pair).astype(F32))

    ids = reorder([chosen_ids.reshape(CHUNKS, 4, quarter, -1)[:, q] for q in range(4)])[0]
    blocks = jnp.stack([i, i ^ 1, i ^ 2, i ^ 3])
    row_ids = (blocks[:, None] * own_rows + jnp.arange(own_rows)[None, :]).reshape(1, 1, -1)
    outs, sums = [], []
    for c in range(CHUNKS):
        counts = jnp.sum((ids[c][:, :, None] == row_ids).astype(F32), axis=1)
        chosen = jnp.sum(counts * pieces[c], axis=1)
        parts = [pieces[c][:, r * own_rows : (r + 1) * own_rows] for r in range(4)]
        outs += reorder([parts[0]] + [to_other(parts[r], r) for r in range(1, 4)])
        sums += reorder([chosen] + [to_other(chosen, r) for r in range(1, 4)])
    return jnp.concatenate(outs).T, jnp.concatenate(sums)


def solution(mesh):
    sizes = (mesh.shape["train"], mesh.shape["test"])
    return jax.shard_map(
        four_by_four if sizes == (4, 4) else any_mesh,
        mesh=mesh,
        in_specs=(
            P(("groups", "train"), "test"),
            P(("groups", "test"), "train"),
            P("train", "test"),
            P(("groups", "test"), None),
        ),
        out_specs=(P(("groups", "train"), "test"), P(("groups", "test"))),
        check_vma=False,
    )
```

time: 959 us -> 436 us (0.45)
  waiting for transfers between devices: 894 us -> 209 us
  starting transfers between devices: 0.34 us -> 116 us
  matrix products: 38 us -> 75.3 us
  local copies, waits for them, and re-layouts: 0.02 us -> 14.9 us
  between operations: 13.8 us -> 2.21 us
    all_gather x3 -> x0, waiting for transfers between devices: 770 us -> none  [the longest x1 566 us: on_device(): lax.all_gather(fisher, 'test', axis=1, tiled=True)]
    ppermute x0 -> x99, waiting for transfers between devices: none -> 209 us  [the longest x40 143 us: along(): return lax.ppermute(value, 'test', pairs)]
    reduce_scatter x1 -> x0, waiting for transfers between devices: 123 us -> none  [on_device(): lax.psum_scatter(partial_value, 'train', scatter_dimension=1, tiled=True)]
    ppermute x0 -> x99, starting transfers between devices: none -> 116 us  [the longest x40 81.9 us: along(): return lax.ppermute(value, 'test', pairs)]
    dot_general x2 -> x32, matrix products: 38 us -> 75.3 us  [the longest x16 41.9 us: dot_t(): lax.dot_general(a, b, (((1,), (1,)), ((), ())), preferred_element_type=F32)]
  transfers between devices with their start and end apart: 4 -> 99, of which waited for: 4 -> 42; matrix products, arithmetic and copies ran while one was open for 1% -> 23% of each run, Pallas kernels for 0% -> 0%
where the time goes in v1:
time: 436 us; the launch traced here: 430 us
  waiting for transfers between devices  209 us (48%)
  starting transfers between devices  116 us (27%)
  matrix products  75.3 us (17%)
  local copies, waits for them, and re-layouts  14.9 us (3%)
  other arithmetic  12 us (3%)
    ppermute x40, waiting for transfers between devices, along(): return lax.ppermute(value, 'test', pairs)  143 us
    ppermute x40, starting transfers between devices, along(): return lax.ppermute(value, 'test', pairs)  81.9 us
    ppermute x59, waiting for transfers between devices, to_other(): return lax.ppermute(value, 'train', [(k, k ^ r) for k in range(4)])  66.5 us
    dot_general x16, matrix products, dot_t(): lax.dot_general(a, b, (((1,), (1,)), ((), ())), preferred_element_type=F32)  41.9 us
    ppermute x59, starting transfers between devices, to_other(): return lax.ppermute(value, 'train', [(k, k ^ r) for k in range(4)])  34.3 us
    dot_general x16, matrix products, scores_part(): part = jnp.dot(block, fisher, preferred_element_type=F32)  33.4 us
  transfers between devices with their start and end apart: 99, of which 42 were waited for; matrix products, arithmetic and copies ran while one was open for 23% of the time, Pallas kernels for 0%

profile of v1, /device:TPU:0, one launch (start us, length us, event | category | flops | bytes accessed | tf_op | source)
XLA Modules:
  0.0 429.7 jit_solution(17133576905199479666)
XLA Ops:
  1.1 2.6 collective-permute-start.3
  5.5 1.9 select_bitcast_fusion.1
  15.1 5.8 %fusion.75 = f32[128,2048]{1,0:T(8,128)} fusion(bf16[2048,2048]{1,0:T(8,128)(2,1)} %param.6, bf16[4,128,2048]{2,1,0:T(8,128)(2,1)S(1)} %pad_maximum_fusion), kind=kOutput, calls=%fused_computation.203 | convolution fusion | flops 1073741824 | bytes 9961472 | tf_op jit(solution)/shard_map/dot_general | solution.py:67
  20.9 5.8 %fusion.76 = f32[128,2048]{1,0:T(8,128)} fusion(bf16[2048,2048]{1,0:T(8,128)(2,1)} %param.6, bf16[4,128,2048]{2,1,0:T(8,128)(2,1)S(1)} %pad_maximum_fusion), kind=kOutput, calls=%fused_computation.204 | convolution fusion | flops 1073741824 | bytes 9961472 | tf_op jit(solution)/shard_map/dot_general | solution.py:67
  33.5 5.3 %convert_reduce_fusion = (f32[32,2048]{1,0:T(8,128)S(1)}, f32[32,2048]{1,0:T(8,128)S(1)}, f32[32,2048]{1,0:T(8,128)S(1)}, f32[32,2048]{1,0:T(8,128)S(1)}) fusion(s32[32,16]{1,0:T(8,128)S(1)} %copy.32, s32[2048]{0:T(1024)S(1)} %bitcast.136, s32[32,16]{1,0:T(8,128)S(1)} %copy.30, s32[32,16]{1,0:T(8,128)S(1)} %copy.31, s32[32,16]{1,0:T(8,128)S(1)} %copy.29), kind=kLoop, calls=%fused_computation | loop fusion | flops 12320768 | bytes 1064960 | tf_op jit(solution)/shard_map/reduce_sum | solution.py:104
  38.8 3.7 collective-permute-start.32
  42.5 4.8 %fusion.91 = f32[128,2048]{1,0:T(8,128)S(1)} fusion(bf16[128,2048]{1,0:T(8,128)(2,1)} %collective-permute-done.11, bf16[2048,2048]{1,0:T(8,128)(2,1)} %param.6), kind=kOutput, calls=%fused_computation.219 | convolution fusion | flops 1073741824 | bytes 9961472 | tf_op jit(solution)/shard_map/dot_general | solution.py:67
  47.3 8.0 %collective-permute-done.32 = bf16[128,2048]{1,0:T(8,128)(2,1)S(1)} collective-permute-done((bf16[128,2048]{1,0:T(8,128)(2,1)}, bf16[128,2048]{1,0:T(8,128)(2,1)S(1)}, u32[]{:S(2)}, u32[]{:S(2)}) %collective-permute-start.32) | collective-permute-done | bytes 524320 | tf_op jit(solution)/shard_map/ppermute | solution.py:45
  58.4 10.7 %collective-permute-done.53 = bf16[128,2048]{1,0:T(8,128)(2,1)S(1)} collective-permute-done((bf16[128,2048]{1,0:T(8,128)(2,1)S(1)}, bf16[128,2048]{1,0:T(8,128)(2,1)S(1)}, u32[]{:S(2)}, u32[]{:S(2)}) %collective-permute-start.53) | collective-permute-done | bytes 524320 | tf_op jit(solution)/shard_map/ppermute | solution.py:45
  72.0 10.0 %collective-permute-done.74 = bf16[128,2048]{1,0:T(8,128)(2,1)S(1)} collective-permute-done((bf16[128,2048]{1,0:T(8,128)(2,1)S(1)}, bf16[128,2048]{1,0:T(8,128)(2,1)S(1)}, u32[]{:S(2)}, u32[]{:S(2)}) %collective-permute-start.74) | collective-permute-done | bytes 524320 | tf_op jit(solution)/shard_map/ppermute | solution.py:45
  89.1 13.4 %collective-permute-done.6 = bf16[128,2048]{1,0:T(8,128)(2,1)S(1)} collective-permute-done((bf16[128,2048]{1,0:T(8,128)(2,1)}, bf16[128,2048]{1,0:T(8,128)(2,1)S(1)}, u32[]{:S(2)}, u32[]{:S(2)}) %collective-permute-start.6) | collective-permute-done | bytes 524320 | tf_op jit(solution)/shard_map/ppermute | solution.py:45
  105.2 12.8 %collective-permute-done.27 = bf16[128,2048]{1,0:T(8,128)(2,1)S(1)} collective-permute-done((bf16[128,2048]{1,0:T(8,128)(2,1)S(1)}, bf16[128,2048]{1,0:T(8,128)(2,1)S(1)}, u32[]{:S(2)}, u32[]{:S(2)}) %collective-permute-start.27) | collective-permute-done | bytes 524320 | tf_op jit(solution)/shard_map/ppermute | solution.py:45
  121.1 11.5 %collective-permute-done.48 = bf16[128,2048]{1,0:T(8,128)(2,1)S(1)} collective-permute-done((bf16[128,2048]{1,0:T(8,128)(2,1)S(1)}, bf16[128,2048]{1,0:T(8,128)(2,1)S(1)}, u32[]{:S(2)}, u32[]{:S(2)}) %collective-permute-start.48) | collective-permute-done | bytes 524320 | tf_op jit(solution)/shard_map/ppermute | solution.py:45
  139.1 13.1 %collective-permute-done.69 = bf16[128,2048]{1,0:T(8,128)(2,1)S(1)} collective-permute-done((bf16[128,2048]{1,0:T(8,128)(2,1)S(1)}, bf16[128,2048]{1,0:T(8,128)(2,1)S(1)}, u32[]{:S(2)}, u32[]{:S(2)}) %collective-permute-start.69) | collective-permute-done | bytes 524320 | tf_op jit(solution)/shard_map/ppermute | solution.py:45
  155.5 11.9 %collective-permute-done.15 = bf16[128,2048]{1,0:T(8,128)(2,1)S(1)} collective-permute-done((bf16[128,2048]{1,0:T(8,128)(2,1)S(1)}, bf16[128,2048]{1,0:T(8,128)(2,1)S(1)}, u32[]{:S(2)}, u32[]{:S(2)}) %collective-permute-start.15) | collective-permute-done | bytes 524320 | tf_op jit(solution)/shard_map/ppermute | solution.py:45
  170.7 11.0 %collective-permute-done.36 = bf16[128,2048]{1,0:T(8,128)(2,1)S(1)} collective-permute-done((bf16[128,2048]{1,0:T(8,128)(2,1)S(1)}, bf16[128,2048]{1,0:T(8,128)(2,1)S(1)}, u32[]{:S(2)}, u32[]{:S(2)}) %collective-permute-start.36) | collective-permute-done | bytes 524320 | tf_op jit(solution)/shard_map/ppermute | solution.py:45
  184.5 10.7 %collective-permute-done.57 = bf16[128,2048]{1,0:T(8,128)(2,1)S(1)} collective-permute-done((bf16[128,2048]{1,0:T(8,128)(2,1)S(1)}, bf16[128,2048]{1,0:T(8,128)(2,1)S(1)}, u32[]{:S(2)}, u32[]{:S(2)}) %collective-permute-start.57) | collective-permute-done | bytes 524320 | tf_op jit(solution)/shard_map/ppermute | solution.py:45
  198.0 10.1 %collective-permute-done.78 = bf16[128,2048]{1,0:T(8,128)(2,1)S(1)} collective-permute-done((bf16[128,2048]{1,0:T(8,128)(2,1)S(1)}, bf16[128,2048]{1,0:T(8,128)(2,1)S(1)}, u32[]{:S(2)}, u32[]{:S(2)}) %collective-permute-start.78) | collective-permute-done | bytes 524320 | tf_op jit(solution)/shard_map/ppermute | solution.py:45
  215.7 3.1 collective-permute-done.79
  225.2 15.3 %collective-permute-done.17 = f32[32,2048]{1,0:T(8,128)S(1)} collective-permute-done((f32[32,2048]{1,0:T(8,128)S(1)}, f32[32,2048]{1,0:T(8,128)S(1)}, u32[]{:S(2)}, u32[]{:S(2)}) %collective-permute-start.17) | collective-permute-done | bytes 262176 | tf_op jit(solution)/shard_map/ppermute | solution.py:48
  241.0 2.6 fusion.83
  243.6 4.6 %collective-permute-done.8 = f32[32,2048]{1,0:T(8,128)S(1)} collective-permute-done((f32[32,2048]{1,0:T(8,128)S(1)}, f32[32,2048]{1,0:T(8,128)S(1)}, u32[]{:S(2)}, u32[]{:S(2)}) %collective-permute-start.8) | collective-permute-done | bytes 262176 | tf_op jit(solution)/shard_map/ppermute | solution.py:48
  248.8 2.6 fusion.84
  251.3 3.7 collective-permute-done.38
  255.6 2.6 fusion.85
  258.2 4.0 collective-permute-done.29
  262.7 2.8 fusion.86
  265.5 5.0 %collective-permute-done.59 = f32[32,2048]{1,0:T(8,128)S(1)} collective-permute-done((f32[32,2048]{1,0:T(8,128)S(1)}, f32[32,2048]{1,0:T(8,128)S(1)}, u32[]{:S(2)}, u32[]{:S(2)}) %collective-permute-start.59) | collective-permute-done | bytes 262176 | tf_op jit(solution)/shard_map/ppermute | solution.py:48
  271.0 2.6 fusion.87
  273.6 5.8 %collective-permute-done.50 = f32[32,2048]{1,0:T(8,128)S(1)} collective-permute-done((f32[32,2048]{1,0:T(8,128)S(1)}, f32[32,2048]{1,0:T(8,128)S(1)}, u32[]{:S(2)}, u32[]{:S(2)}) %collective-permute-start.50) | collective-permute-done | bytes 262176 | tf_op jit(solution)/shard_map/ppermute | solution.py:48
  280.0 2.6 fusion.88
  282.5 4.9 %collective-permute-done.80 = f32[32,2048]{1,0:T(8,128)S(1)} collective-permute-done((f32[32,2048]{1,0:T(8,128)S(1)}, f32[32,2048]{1,0:T(8,128)S(1)}, u32[]{:S(2)}, u32[]{:S(2)}) %collective-permute-start.80) | collective-permute-done | bytes 262176 | tf_op jit(solution)/shard_map/ppermute | solution.py:48
  288.0 2.6 fusion.89
  290.6 3.2 collective-permute-done.71
  295.3 2.6 fusion.90
  297.9 4.2 collective-permute-start.9
  302.2 2.5 collective-permute-done.9
  304.7 4.3 %collective-permute-start.39 = (bf16[32,2048]{1,0:T(8,128)(2,1)S(1)}, bf16[32,2048]{1,0:T(8,128)(2,1)S(1)}, u32[]{:S(2)}, u32[]{:S(2)}) collective-permute-start(bf16[32,2048]{1,0:T(8,128)(2,1)S(1)} %get-tuple-element.53), channel_id=1, source_target_pairs={{0,1},{3,2},{4,5},{7,6},{8,9},{11,10},{12,13},{15,14},{16,17},{19,... | collective-permute-start | bytes 393224 | tf_op jit(solution)/shard_map/ppermute | solution.py:45
  309.0 2.7 collective-permute-done.39
  311.7 4.4 %collective-permute-start.30 = (bf16[32,2048]{1,0:T(8,128)(2,1)S(1)}, bf16[32,2048]{1,0:T(8,128)(2,1)S(1)}, u32[]{:S(2)}, u32[]{:S(2)}) collective-permute-start(bf16[32,2048]{1,0:T(8,128)(2,1)S(1)} %get-tuple-element.55), channel_id=1, source_target_pairs={{0,1},{3,2},{4,5},{7,6},{8,9},{11,10},{12,13},{15,14},{16,17},{19,... | collective-permute-start | bytes 393224 | tf_op jit(solution)/shard_map/ppermute | solution.py:45
  316.1 3.8 collective-permute-done.30
  319.9 4.4 %collective-permute-start.60 = (bf16[32,2048]{1,0:T(8,128)(2,1)S(1)}, bf16[32,2048]{1,0:T(8,128)(2,1)S(1)}, u32[]{:S(2)}, u32[]{:S(2)}) collective-permute-start(bf16[32,2048]{1,0:T(8,128)(2,1)S(1)} %get-tuple-element.57), channel_id=1, source_target_pairs={{0,1},{3,2},{4,5},{7,6},{8,9},{11,10},{12,13},{15,14},{16,17},{19,... | collective-permute-start | bytes 393224 | tf_op jit(solution)/shard_map/ppermute | solution.py:45
  324.3 3.0 collective-permute-done.60
  327.3 4.4 %collective-permute-start.51 = (bf16[32,2048]{1,0:T(8,128)(2,1)S(1)}, bf16[32,2048]{1,0:T(8,128)(2,1)S(1)}, u32[]{:S(2)}, u32[]{:S(2)}) collective-permute-start(bf16[32,2048]{1,0:T(8,128)(2,1)S(1)} %get-tuple-element.59), channel_id=1, source_target_pairs={{0,1},{3,2},{4,5},{7,6},{8,9},{11,10},{12,13},{15,14},{16,17},{19,... | collective-permute-start | bytes 393224 | tf_op jit(solution)/shard_map/ppermute | solution.py:45
  331.7 2.5 collective-permute-done.51
  334.2 4.3 %collective-permute-start.81 = (bf16[32,2048]{1,0:T(8,128)(2,1)S(1)}, bf16[32,2048]{1,0:T(8,128)(2,1)S(1)}, u32[]{:S(2)}, u32[]{:S(2)}) collective-permute-start(bf16[32,2048]{1,0:T(8,128)(2,1)S(1)} %get-tuple-element.61), channel_id=1, source_target_pairs={{0,1},{3,2},{4,5},{7,6},{8,9},{11,10},{12,13},{15,14},{16,17},{19,... | collective-permute-start | bytes 393224 | tf_op jit(solution)/shard_map/ppermute | solution.py:45
  338.6 2.5 collective-permute-done.81
  341.1 4.3 %collective-permute-start.72 = (bf16[32,2048]{1,0:T(8,128)(2,1)S(1)}, bf16[32,2048]{1,0:T(8,128)(2,1)S(1)}, u32[]{:S(2)}, u32[]{:S(2)}) collective-permute-start(bf16[32,2048]{1,0:T(8,128)(2,1)S(1)} %get-tuple-element.63), channel_id=1, source_target_pairs={{0,1},{3,2},{4,5},{7,6},{8,9},{11,10},{12,13},{15,14},{16,17},{19,... | collective-permute-start | bytes 393224 | tf_op jit(solution)/shard_map/ppermute | solution.py:45
  345.4 2.5 collective-permute-done.72
  350.3 2.6 fusion.4
  352.9 2.2 collective-permute-done.34
  356.3 2.6 fusion.5
  358.8 2.6 collective-permute-done.55
  362.7 2.6 fusion.6
  365.2 4.0 collective-permute-done.76
  369.9 11.5 %collective-permute-start.20 = (bf16[32,2048]{1,0:T(8,128)(2,1)S(1)}, bf16[32,2048]{1,0:T(8,128)(2,1)S(1)}, u32[]{:S(2)}, u32[]{:S(2)}) collective-permute-start(bf16[32,2048]{1,0:T(8,128)(2,1)S(1)} %fusion.4), channel_id=1, source_target_pairs={{0,1},{1,0},{2,3},{3,2},{4,5},{5,4},{6,7},{7,6},{8,9},{9,8},{10,11... | collective-permute-start | bytes 393224 | tf_op jit(solution)/shard_map/ppermute | solution.py:45
  381.4 2.6 fusion.7
  386.1 2.2 collective-permute-start.41
  388.3 2.7 multiply_reduce_fusion.3
  392.5 4.6 %collective-permute-start.62 = (bf16[32,2048]{1,0:T(8,128)(2,1)S(1)}, bf16[32,2048]{1,0:T(8,128)(2,1)S(1)}, u32[]{:S(2)}, u32[]{:S(2)}) collective-permute-start(bf16[32,2048]{1,0:T(8,128)(2,1)S(1)} %fusion.6), channel_id=1, source_target_pairs={{0,1},{1,0},{2,3},{3,2},{4,5},{5,4},{6,7},{7,6},{8,9},{9,8},{10,11... | collective-permute-start | bytes 393224 | tf_op jit(solution)/shard_map/ppermute | solution.py:45
  397.1 2.7 multiply_reduce_fusion.2
  401.5 2.7 multiply_reduce_fusion.1
  406.5 2.7 multiply_reduce_fusion
  425.4 2.4 collective-permute-done.85
  (297 shorter events, 103.6 us)
Async XLA Ops:
  0.6 218.8 %collective-permute-start.2 = (bf16[512,2048]{1,0:T(8,128)(2,1)}, bf16[512,2048]{1,0:T(8,128)(2,1)}, u32[]{:S(2)}, u32[]{:S(2)}) collective-permute-start(bf16[512,2048]{1,0:T(8,128)(2,1)} %param.4), channel_id=1, source_target_pairs={{0,4},{4,0},{8,12},{12,8},{1,5},{5,1},{9,13},{13,9},{2,6},{6,2},{1... | collective-permute-start | bytes 6291464 | tf_op jit(solution)/shard_map/ppermute | solution.py:48
  1.1 211.8 %collective-permute-start.3 = (bf16[512,2048]{1,0:T(8,128)(2,1)}, bf16[512,2048]{1,0:T(8,128)(2,1)}, u32[]{:S(2)}, u32[]{:S(2)}) collective-permute-start(bf16[512,2048]{1,0:T(8,128)(2,1)} %param.4), channel_id=1, source_target_pairs={{0,8},{4,12},{8,0},{12,4},{1,9},{5,13},{9,1},{13,5},{2,10},{6,14},... | collective-permute-start | bytes 6291464 | tf_op jit(solution)/shard_map/ppermute | solution.py:48
  9.0 29.8 %collective-permute-start.11 = (bf16[128,2048]{1,0:T(8,128)(2,1)}, bf16[128,2048]{1,0:T(8,128)(2,1)}, u32[]{:S(2)}, u32[]{:S(2)}) collective-permute-start(bf16[128,2048]{1,0:T(8,128)(2,1)} %get-tuple-element.13), channel_id=1, source_target_pairs={{0,1},{1,0},{2,3},{3,2},{4,5},{5,4},{6,7},{7,6},{8,9},{9,8},{10,11... | collective-permute-start | bytes 1572872 | tf_op jit(solution)/shard_map/ppermute | solution.py:45
  10.6 74.5 %collective-permute-start.5 = (bf16[128,2048]{1,0:T(8,128)(2,1)}, bf16[128,2048]{1,0:T(8,128)(2,1)}, u32[]{:S(2)}, u32[]{:S(2)}) collective-permute-start(bf16[128,2048]{1,0:T(8,128)(2,1)} %get-tuple-element.13), channel_id=1, source_target_pairs={{1,2},{2,1},{5,6},{6,5},{9,10},{10,9},{13,14},{14,13},{17,18},{18,... | collective-permute-start | bytes 1572872 | tf_op jit(solution)/shard_map/ppermute | solution.py:45
  15.1 68.2 %collective-permute-start = (f32[64,2048]{1,0:T(8,128)}, f32[64,2048]{1,0:T(8,128)}, u32[]{:S(2)}, u32[]{:S(2)}) collective-permute-start(f32[64,2048]{1,0:T(8,128)} %slice.398), channel_id=1, source_target_pairs={{0,4},{4,0},{8,12},{12,8},{1,5},{5,1},{9,13},{13,9},{2,6},{6,2},{1... | collective-permute-start | bytes 1572872 | tf_op jit(solution)/shard_map/ppermute | solution.py:48
  38.8 16.5 %collective-permute-start.32 = (bf16[128,2048]{1,0:T(8,128)(2,1)}, bf16[128,2048]{1,0:T(8,128)(2,1)S(1)}, u32[]{:S(2)}, u32[]{:S(2)}) collective-permute-start(bf16[128,2048]{1,0:T(8,128)(2,1)} %get-tuple-element.12), channel_id=1, source_target_pairs={{0,1},{1,0},{2,3},{3,2},{4,5},{5,4},{6,7},{7,6},{8,9},{9,8},{10,11... | collective-permute-start | bytes 1572872 | tf_op jit(solution)/shard_map/ppermute | solution.py:45
  55.3 13.8 %collective-permute-start.53 = (bf16[128,2048]{1,0:T(8,128)(2,1)S(1)}, bf16[128,2048]{1,0:T(8,128)(2,1)S(1)}, u32[]{:S(2)}, u32[]{:S(2)}) collective-permute-start(bf16[128,2048]{1,0:T(8,128)(2,1)S(1)} %copy-done.7), channel_id=1, source_target_pairs={{0,1},{1,0},{2,3},{3,2},{4,5},{5,4},{6,7},{7,6},{8,9},{9,8},{10,11... | collective-permute-start | bytes 1572872 | tf_op jit(solution)/shard_map/ppermute | solution.py:45
  69.1 12.9 %collective-permute-start.74 = (bf16[128,2048]{1,0:T(8,128)(2,1)S(1)}, bf16[128,2048]{1,0:T(8,128)(2,1)S(1)}, u32[]{:S(2)}, u32[]{:S(2)}) collective-permute-start(bf16[128,2048]{1,0:T(8,128)(2,1)S(1)} %copy-done.6), channel_id=1, source_target_pairs={{0,1},{1,0},{2,3},{3,2},{4,5},{5,4},{6,7},{7,6},{8,9},{9,8},{10,11... | collective-permute-start | bytes 1572872 | tf_op jit(solution)/shard_map/ppermute | solution.py:45
  85.9 16.6 %collective-permute-start.6 = (bf16[128,2048]{1,0:T(8,128)(2,1)}, bf16[128,2048]{1,0:T(8,128)(2,1)S(1)}, u32[]{:S(2)}, u32[]{:S(2)}) collective-permute-start(bf16[128,2048]{1,0:T(8,128)(2,1)} %collective-permute-done.5), channel_id=1, source_target_pairs={{1,0},{2,3},{5,4},{6,7},{9,8},{10,11},{13,12},{14,15},{17,16},{18,... | collective-permute-start | bytes 1572872 | tf_op jit(solution)/shard_map/ppermute | solution.py:45
  87.5 17.6 %collective-permute-start.47 = (bf16[128,2048]{1,0:T(8,128)(2,1)S(1)}, bf16[128,2048]{1,0:T(8,128)(2,1)S(1)}, u32[]{:S(2)}, u32[]{:S(2)}) collective-permute-start(bf16[128,2048]{1,0:T(8,128)(2,1)S(1)} %copy-done.7), channel_id=1, source_target_pairs={{1,2},{2,1},{5,6},{6,5},{9,10},{10,9},{13,14},{14,13},{17,18},{18,... | collective-permute-start | bytes 1572872 | tf_op jit(solution)/shard_map/ppermute | solution.py:45
  88.4 46.4 %collective-permute-start.68 = (bf16[128,2048]{1,0:T(8,128)(2,1)S(1)}, bf16[128,2048]{1,0:T(8,128)(2,1)S(1)}, u32[]{:S(2)}, u32[]{:S(2)}) collective-permute-start(bf16[128,2048]{1,0:T(8,128)(2,1)S(1)} %copy-done.6), channel_id=1, source_target_pairs={{1,2},{2,1},{5,6},{6,5},{9,10},{10,9},{13,14},{14,13},{17,18},{18,... | collective-permute-start | bytes 1572872 | tf_op jit(solution)/shard_map/ppermute | solution.py:45
  102.5 15.5 %collective-permute-start.27 = (bf16[128,2048]{1,0:T(8,128)(2,1)S(1)}, bf16[128,2048]{1,0:T(8,128)(2,1)S(1)}, u32[]{:S(2)}, u32[]{:S(2)}) collective-permute-start(bf16[128,2048]{1,0:T(8,128)(2,1)S(1)} %collective-permute-done.26), channel_id=1, source_target_pairs={{1,0},{2,3},{5,4},{6,7},{9,8},{10,11},{13,12},{14,15},{17,16},{18,... | collective-permute-start | bytes 1572872 | tf_op jit(solution)/shard_map/ppermute | solution.py:45
  105.1 28.8 %collective-permute-start.12 = (f32[64,2048]{1,0:T(8,128)S(1)}, f32[64,2048]{1,0:T(8,128)S(1)}, u32[]{:S(2)}, u32[]{:S(2)}) collective-permute-start(f32[64,2048]{1,0:T(8,128)S(1)} %slice.406), channel_id=1, source_target_pairs={{0,4},{4,0},{8,12},{12,8},{1,5},{5,1},{9,13},{13,9},{2,6},{6,2},{1... | collective-permute-start | bytes 1572872 | tf_op jit(solution)/shard_map/ppermute | solution.py:48
  118.0 14.6 %collective-permute-start.48 = (bf16[128,2048]{1,0:T(8,128)(2,1)S(1)}, bf16[128,2048]{1,0:T(8,128)(2,1)S(1)}, u32[]{:S(2)}, u32[]{:S(2)}) collective-permute-start(bf16[128,2048]{1,0:T(8,128)(2,1)S(1)} %collective-permute-done.47), channel_id=1, source_target_pairs={{1,0},{2,3},{5,4},{6,7},{9,8},{10,11},{13,12},{14,15},{17,16},{18,... | collective-permute-start | bytes 1572872 | tf_op jit(solution)/shard_map/ppermute | solution.py:45
  136.1 16.1 %collective-permute-start.69 = (bf16[128,2048]{1,0:T(8,128)(2,1)S(1)}, bf16[128,2048]{1,0:T(8,128)(2,1)S(1)}, u32[]{:S(2)}, u32[]{:S(2)}) collective-permute-start(bf16[128,2048]{1,0:T(8,128)(2,1)S(1)} %collective-permute-done.68), channel_id=1, source_target_pairs={{1,0},{2,3},{5,4},{6,7},{9,8},{10,11},{13,12},{14,15},{17,16},{18,... | collective-permute-start | bytes 1572872 | tf_op jit(solution)/shard_map/ppermute | solution.py:45
  137.6 246.4 %collective-permute-start.1 = (f32[32,2048]{1,0:T(8,128)S(1)}, f32[32,2048]{1,0:T(8,128)S(1)}, u32[]{:S(2)}, u32[]{:S(2)}) collective-permute-start(f32[32,2048]{1,0:T(8,128)S(1)} %slice.400), channel_id=1, source_target_pairs={{0,8},{4,12},{8,0},{12,4},{1,9},{5,13},{9,1},{13,5},{2,10},{6,14},... | collective-permute-start | bytes 786440 | tf_op jit(solution)/shard_map/ppermute | solution.py:48
  138.4 16.5 %collective-permute-start.35 = (bf16[128,2048]{1,0:T(8,128)(2,1)S(1)}, bf16[128,2048]{1,0:T(8,128)(2,1)S(1)}, u32[]{:S(2)}, u32[]{:S(2)}) collective-permute-start(bf16[128,2048]{1,0:T(8,128)(2,1)S(1)} %collective-permute-done.32), channel_id=1, source_target_pairs={{1,2},{2,1},{5,6},{6,5},{9,10},{10,9},{13,14},{14,13},{17,18},{18,... | collective-permute-start | bytes 1572872 | tf_op jit(solution)/shard_map/ppermute | solution.py:45
  152.2 15.3 %collective-permute-start.15 = (bf16[128,2048]{1,0:T(8,128)(2,1)S(1)}, bf16[128,2048]{1,0:T(8,128)(2,1)S(1)}, u32[]{:S(2)}, u32[]{:S(2)}) collective-permute-start(bf16[128,2048]{1,0:T(8,128)(2,1)S(1)} %collective-permute-done.14), channel_id=1, source_target_pairs={{1,0},{2,3},{5,4},{6,7},{9,8},{10,11},{13,12},{14,15},{17,16},{18,... | collective-permute-start | bytes 1572872 | tf_op jit(solution)/shard_map/ppermute | solution.py:45
  154.8 15.2 %collective-permute-start.56 = (bf16[128,2048]{1,0:T(8,128)(2,1)S(1)}, bf16[128,2048]{1,0:T(8,128)(2,1)S(1)}, u32[]{:S(2)}, u32[]{:S(2)}) collective-permute-start(bf16[128,2048]{1,0:T(8,128)(2,1)S(1)} %collective-permute-done.53), channel_id=1, source_target_pairs={{1,2},{2,1},{5,6},{6,5},{9,10},{10,9},{13,14},{14,13},{17,18},{18,... | collective-permute-start | bytes 1572872 | tf_op jit(solution)/shard_map/ppermute | solution.py:45
  167.4 14.4 %collective-permute-start.36 = (bf16[128,2048]{1,0:T(8,128)(2,1)S(1)}, bf16[128,2048]{1,0:T(8,128)(2,1)S(1)}, u32[]{:S(2)}, u32[]{:S(2)}) collective-permute-start(bf16[128,2048]{1,0:T(8,128)(2,1)S(1)} %collective-permute-done.35), channel_id=1, source_target_pairs={{1,0},{2,3},{5,4},{6,7},{9,8},{10,11},{13,12},{14,15},{17,16},{18,... | collective-permute-start | bytes 1572872 | tf_op jit(solution)/shard_map/ppermute | solution.py:45
  170.0 14.3 %collective-permute-start.77 = (bf16[128,2048]{1,0:T(8,128)(2,1)S(1)}, bf16[128,2048]{1,0:T(8,128)(2,1)S(1)}, u32[]{:S(2)}, u32[]{:S(2)}) collective-permute-start(bf16[128,2048]{1,0:T(8,128)(2,1)S(1)} %collective-permute-done.74), channel_id=1, source_target_pairs={{1,2},{2,1},{5,6},{6,5},{9,10},{10,9},{13,14},{14,13},{17,18},{18,... | collective-permute-start | bytes 1572872 | tf_op jit(solution)/shard_map/ppermute | solution.py:45
  181.8 13.4 %collective-permute-start.57 = (bf16[128,2048]{1,0:T(8,128)(2,1)S(1)}, bf16[128,2048]{1,0:T(8,128)(2,1)S(1)}, u32[]{:S(2)}, u32[]{:S(2)}) collective-permute-start(bf16[128,2048]{1,0:T(8,128)(2,1)S(1)} %collective-permute-done.56), channel_id=1, source_target_pairs={{1,0},{2,3},{5,4},{6,7},{9,8},{10,11},{13,12},{14,15},{17,16},{18,... | collective-permute-start | bytes 1572872 | tf_op jit(solution)/shard_map/ppermute | solution.py:45
  184.4 25.1 %collective-permute-start.7 = (f32[64,2048]{1,0:T(8,128)S(1)}, f32[64,2048]{1,0:T(8,128)S(1)}, u32[]{:S(2)}, u32[]{:S(2)}) collective-permute-start(f32[64,2048]{1,0:T(8,128)S(1)} %slice.402), channel_id=1, source_target_pairs={{0,4},{4,0},{8,12},{12,8},{1,5},{5,1},{9,13},{13,9},{2,6},{6,2},{1... | collective-permute-start | bytes 1572872 | tf_op jit(solution)/shard_map/ppermute | solution.py:48
  195.2 12.9 %collective-permute-start.78 = (bf16[128,2048]{1,0:T(8,128)(2,1)S(1)}, bf16[128,2048]{1,0:T(8,128)(2,1)S(1)}, u32[]{:S(2)}, u32[]{:S(2)}) collective-permute-start(bf16[128,2048]{1,0:T(8,128)(2,1)S(1)} %collective-permute-done.77), channel_id=1, source_target_pairs={{1,0},{2,3},{5,4},{6,7},{9,8},{10,11},{13,12},{14,15},{17,16},{18,... | collective-permute-start | bytes 1572872 | tf_op jit(solution)/shard_map/ppermute | solution.py:45
  213.5 10.9 %collective-permute-start.4 = (bf16[512,2048]{1,0:T(8,128)(2,1)}, bf16[512,2048]{1,0:T(8,128)(2,1)S(1)}, u32[]{:S(2)}, u32[]{:S(2)}) collective-permute-start(bf16[512,2048]{1,0:T(8,128)(2,1)} %collective-permute-done.3), channel_id=1, source_target_pairs={{0,4},{4,0},{8,12},{12,8},{1,5},{5,1},{9,13},{13,9},{2,6},{6,2},{1... | collective-permute-start | bytes 6291464 | tf_op jit(solution)/shard_map/ppermute | solution.py:48
  215.0 176.0 %collective-permute-start.25 = (f32[32,2048]{1,0:T(8,128)S(1)}, f32[32,2048]{1,0:T(8,128)S(1)}, u32[]{:S(2)}, u32[]{:S(2)}) collective-permute-start(f32[32,2048]{1,0:T(8,128)S(1)} %slice.421), channel_id=1, source_target_pairs={{0,8},{4,12},{8,0},{12,4},{1,9},{5,13},{9,1},{13,5},{2,10},{6,14},... | collective-permute-start | bytes 786440 | tf_op jit(solution)/shard_map/ppermute | solution.py:48
  218.8 181.1 %collective-permute-start.46 = (f32[32,2048]{1,0:T(8,128)S(1)}, f32[32,2048]{1,0:T(8,128)S(1)}, u32[]{:S(2)}, u32[]{:S(2)}) collective-permute-start(f32[32,2048]{1,0:T(8,128)S(1)} %slice.442), channel_id=1, source_target_pairs={{0,8},{4,12},{8,0},{12,4},{1,9},{5,13},{9,1},{13,5},{2,10},{6,14},... | collective-permute-start | bytes 786440 | tf_op jit(solution)/shard_map/ppermute | solution.py:48
  219.4 129.2 %collective-permute-start.13 = (f32[32,2048]{1,0:T(8,128)S(1)}, f32[32,2048]{1,0:T(8,128)S(1)}, u32[]{:S(2)}, u32[]{:S(2)}) collective-permute-start(f32[32,2048]{1,0:T(8,128)S(1)} %slice.408), channel_id=1, source_target_pairs={{0,8},{4,12},{8,0},{12,4},{1,9},{5,13},{9,1},{13,5},{2,10},{6,14},... | collective-permute-start | bytes 786440 | tf_op jit(solution)/shard_map/ppermute | solution.py:48
  224.4 16.0 %collective-permute-start.17 = (f32[32,2048]{1,0:T(8,128)S(1)}, f32[32,2048]{1,0:T(8,128)S(1)}, u32[]{:S(2)}, u32[]{:S(2)}) collective-permute-start(f32[32,2048]{1,0:T(8,128)S(1)} %slice.412), channel_id=1, source_target_pairs={{0,8},{4,12},{8,0},{12,4},{1,9},{5,13},{9,1},{13,5},{2,10},{6,14},... | collective-permute-start | bytes 786440 | tf_op jit(solution)/shard_map/ppermute | solution.py:48
  240.4 7.8 %collective-permute-start.8 = (f32[32,2048]{1,0:T(8,128)S(1)}, f32[32,2048]{1,0:T(8,128)S(1)}, u32[]{:S(2)}, u32[]{:S(2)}) collective-permute-start(f32[32,2048]{1,0:T(8,128)S(1)} %slice.404), channel_id=1, source_target_pairs={{0,8},{4,12},{8,0},{12,4},{1,9},{5,13},{9,1},{13,5},{2,10},{6,14},... | collective-permute-start | bytes 786440 | tf_op jit(solution)/shard_map/ppermute | solution.py:48
  248.2 6.9 %collective-permute-start.38 = (f32[32,2048]{1,0:T(8,128)S(1)}, f32[32,2048]{1,0:T(8,128)S(1)}, u32[]{:S(2)}, u32[]{:S(2)}) collective-permute-start(f32[32,2048]{1,0:T(8,128)S(1)} %slice.433), channel_id=1, source_target_pairs={{0,8},{4,12},{8,0},{12,4},{1,9},{5,13},{9,1},{13,5},{2,10},{6,14},... | collective-permute-start | bytes 786440 | tf_op jit(solution)/shard_map/ppermute | solution.py:48
  255.1 7.1 %collective-permute-start.29 = (f32[32,2048]{1,0:T(8,128)S(1)}, f32[32,2048]{1,0:T(8,128)S(1)}, u32[]{:S(2)}, u32[]{:S(2)}) collective-permute-start(f32[32,2048]{1,0:T(8,128)S(1)} %slice.425), channel_id=1, source_target_pairs={{0,8},{4,12},{8,0},{12,4},{1,9},{5,13},{9,1},{13,5},{2,10},{6,14},... | collective-permute-start | bytes 786440 | tf_op jit(solution)/shard_map/ppermute | solution.py:48
  262.2 8.3 %collective-permute-start.59 = (f32[32,2048]{1,0:T(8,128)S(1)}, f32[32,2048]{1,0:T(8,128)S(1)}, u32[]{:S(2)}, u32[]{:S(2)}) collective-permute-start(f32[32,2048]{1,0:T(8,128)S(1)} %slice.454), channel_id=1, source_target_pairs={{0,8},{4,12},{8,0},{12,4},{1,9},{5,13},{9,1},{13,5},{2,10},{6,14},... | collective-permute-start | bytes 786440 | tf_op jit(solution)/shard_map/ppermute | solution.py:48
  270.5 8.9 %collective-permute-start.50 = (f32[32,2048]{1,0:T(8,128)S(1)}, f32[32,2048]{1,0:T(8,128)S(1)}, u32[]{:S(2)}, u32[]{:S(2)}) collective-permute-start(f32[32,2048]{1,0:T(8,128)S(1)} %slice.446), channel_id=1, source_target_pairs={{0,8},{4,12},{8,0},{12,4},{1,9},{5,13},{9,1},{13,5},{2,10},{6,14},... | collective-permute-start | bytes 786440 | tf_op jit(solution)/shard_map/ppermute | solution.py:48
  279.4 8.1 %collective-permute-start.80 = (f32[32,2048]{1,0:T(8,128)S(1)}, f32[32,2048]{1,0:T(8,128)S(1)}, u32[]{:S(2)}, u32[]{:S(2)}) collective-permute-start(f32[32,2048]{1,0:T(8,128)S(1)} %slice.475), channel_id=1, source_target_pairs={{0,8},{4,12},{8,0},{12,4},{1,9},{5,13},{9,1},{13,5},{2,10},{6,14},... | collective-permute-start | bytes 786440 | tf_op jit(solution)/shard_map/ppermute | solution.py:48
  287.5 6.4 %collective-permute-start.71 = (f32[32,2048]{1,0:T(8,128)S(1)}, f32[32,2048]{1,0:T(8,128)S(1)}, u32[]{:S(2)}, u32[]{:S(2)}) collective-permute-start(f32[32,2048]{1,0:T(8,128)S(1)} %slice.467), channel_id=1, source_target_pairs={{0,8},{4,12},{8,0},{12,4},{1,9},{5,13},{9,1},{13,5},{2,10},{6,14},... | collective-permute-start | bytes 786440 | tf_op jit(solution)/shard_map/ppermute | solution.py:48
  297.9 6.7 %collective-permute-start.9 = (bf16[32,2048]{1,0:T(8,128)(2,1)S(1)}, bf16[32,2048]{1,0:T(8,128)(2,1)S(1)}, u32[]{:S(2)}, u32[]{:S(2)}) collective-permute-start(bf16[32,2048]{1,0:T(8,128)(2,1)S(1)} %get-tuple-element.51), channel_id=1, source_target_pairs={{0,1},{3,2},{4,5},{7,6},{8,9},{11,10},{12,13},{15,14},{16,17},{19,... | collective-permute-start | bytes 393224 | tf_op jit(solution)/shard_map/ppermute | solution.py:45
  304.7 7.0 %collective-permute-start.39 = (bf16[32,2048]{1,0:T(8,128)(2,1)S(1)}, bf16[32,2048]{1,0:T(8,128)(2,1)S(1)}, u32[]{:S(2)}, u32[]{:S(2)}) collective-permute-start(bf16[32,2048]{1,0:T(8,128)(2,1)S(1)} %get-tuple-element.53), channel_id=1, source_target_pairs={{0,1},{3,2},{4,5},{7,6},{8,9},{11,10},{12,13},{15,14},{16,17},{19,... | collective-permute-start | bytes 393224 | tf_op jit(solution)/shard_map/ppermute | solution.py:45
  311.7 8.2 %collective-permute-start.30 = (bf16[32,2048]{1,0:T(8,128)(2,1)S(1)}, bf16[32,2048]{1,0:T(8,128)(2,1)S(1)}, u32[]{:S(2)}, u32[]{:S(2)}) collective-permute-start(bf16[32,2048]{1,0:T(8,128)(2,1)S(1)} %get-tuple-element.55), channel_id=1, source_target_pairs={{0,1},{3,2},{4,5},{7,6},{8,9},{11,10},{12,13},{15,14},{16,17},{19,... | collective-permute-start | bytes 393224 | tf_op jit(solution)/shard_map/ppermute | solution.py:45
  319.9 7.4 %collective-permute-start.60 = (bf16[32,2048]{1,0:T(8,128)(2,1)S(1)}, bf16[32,2048]{1,0:T(8,128)(2,1)S(1)}, u32[]{:S(2)}, u32[]{:S(2)}) collective-permute-start(bf16[32,2048]{1,0:T(8,128)(2,1)S(1)} %get-tuple-element.57), channel_id=1, source_target_pairs={{0,1},{3,2},{4,5},{7,6},{8,9},{11,10},{12,13},{15,14},{16,17},{19,... | collective-permute-start | bytes 393224 | tf_op jit(solution)/shard_map/ppermute | solution.py:45
  327.3 6.9 %collective-permute-start.51 = (bf16[32,2048]{1,0:T(8,128)(2,1)S(1)}, bf16[32,2048]{1,0:T(8,128)(2,1)S(1)}, u32[]{:S(2)}, u32[]{:S(2)}) collective-permute-start(bf16[32,2048]{1,0:T(8,128)(2,1)S(1)} %get-tuple-element.59), channel_id=1, source_target_pairs={{0,1},{3,2},{4,5},{7,6},{8,9},{11,10},{12,13},{15,14},{16,17},{19,... | collective-permute-start | bytes 393224 | tf_op jit(solution)/shard_map/ppermute | solution.py:45
  334.2 6.8 %collective-permute-start.81 = (bf16[32,2048]{1,0:T(8,128)(2,1)S(1)}, bf16[32,2048]{1,0:T(8,128)(2,1)S(1)}, u32[]{:S(2)}, u32[]{:S(2)}) collective-permute-start(bf16[32,2048]{1,0:T(8,128)(2,1)S(1)} %get-tuple-element.61), channel_id=1, source_target_pairs={{0,1},{3,2},{4,5},{7,6},{8,9},{11,10},{12,13},{15,14},{16,17},{19,... | collective-permute-start | bytes 393224 | tf_op jit(solution)/shard_map/ppermute | solution.py:45
  341.1 6.8 %collective-permute-start.72 = (bf16[32,2048]{1,0:T(8,128)(2,1)S(1)}, bf16[32,2048]{1,0:T(8,128)(2,1)S(1)}, u32[]{:S(2)}, u32[]{:S(2)}) collective-permute-start(bf16[32,2048]{1,0:T(8,128)(2,1)S(1)} %get-tuple-element.63), channel_id=1, source_target_pairs={{0,1},{3,2},{4,5},{7,6},{8,9},{11,10},{12,13},{15,14},{16,17},{19,... | collective-permute-start | bytes 393224 | tf_op jit(solution)/shard_map/ppermute | solution.py:45
  348.6 6.4 %collective-permute-start.34 = (f32[32,2048]{1,0:T(8,128)S(1)}, f32[32,2048]{1,0:T(8,128)S(1)}, u32[]{:S(2)}, u32[]{:S(2)}) collective-permute-start(f32[32,2048]{1,0:T(8,128)S(1)} %slice.429), channel_id=1, source_target_pairs={{0,8},{4,12},{8,0},{12,4},{1,9},{5,13},{9,1},{13,5},{2,10},{6,14},... | collective-permute-start | bytes 786440 | tf_op jit(solution)/shard_map/ppermute | solution.py:48
  349.2 6.4 %collective-permute-start.40 = (bf16[32,2048]{1,0:T(8,128)(2,1)S(1)}, bf16[32,2048]{1,0:T(8,128)(2,1)S(1)}, u32[]{:S(2)}, u32[]{:S(2)}) collective-permute-start(bf16[32,2048]{1,0:T(8,128)(2,1)S(1)} %add_convert_fusion.4), channel_id=1, source_target_pairs={{1,2},{2,1},{5,6},{6,5},{9,10},{10,9},{13,14},{14,13},{17,18},{18,... | collective-permute-start | bytes 393224 | tf_op jit(solution)/shard_map/ppermute | solution.py:45
  355.1 6.4 %collective-permute-start.55 = (f32[32,2048]{1,0:T(8,128)S(1)}, f32[32,2048]{1,0:T(8,128)S(1)}, u32[]{:S(2)}, u32[]{:S(2)}) collective-permute-start(f32[32,2048]{1,0:T(8,128)S(1)} %slice.450), channel_id=1, source_target_pairs={{0,8},{4,12},{8,0},{12,4},{1,9},{5,13},{9,1},{13,5},{2,10},{6,14},... | collective-permute-start | bytes 786440 | tf_op jit(solution)/shard_map/ppermute | solution.py:48
  355.6 6.4 %collective-permute-start.61 = (bf16[32,2048]{1,0:T(8,128)(2,1)S(1)}, bf16[32,2048]{1,0:T(8,128)(2,1)S(1)}, u32[]{:S(2)}, u32[]{:S(2)}) collective-permute-start(bf16[32,2048]{1,0:T(8,128)(2,1)S(1)} %add_convert_fusion.2), channel_id=1, source_target_pairs={{1,2},{2,1},{5,6},{6,5},{9,10},{10,9},{13,14},{14,13},{17,18},{18,... | collective-permute-start | bytes 393224 | tf_op jit(solution)/shard_map/ppermute | solution.py:45
  361.4 7.8 %collective-permute-start.76 = (f32[32,2048]{1,0:T(8,128)S(1)}, f32[32,2048]{1,0:T(8,128)S(1)}, u32[]{:S(2)}, u32[]{:S(2)}) collective-permute-start(f32[32,2048]{1,0:T(8,128)S(1)} %slice.471), channel_id=1, source_target_pairs={{0,8},{4,12},{8,0},{12,4},{1,9},{5,13},{9,1},{13,5},{2,10},{6,14},... | collective-permute-start | bytes 786440 | tf_op jit(solution)/shard_map/ppermute | solution.py:48
  362.0 7.9 %collective-permute-start.82 = (bf16[32,2048]{1,0:T(8,128)(2,1)S(1)}, bf16[32,2048]{1,0:T(8,128)(2,1)S(1)}, u32[]{:S(2)}, u32[]{:S(2)}) collective-permute-start(bf16[32,2048]{1,0:T(8,128)(2,1)S(1)} %add_convert_fusion), channel_id=1, source_target_pairs={{1,2},{2,1},{5,6},{6,5},{9,10},{10,9},{13,14},{14,13},{17,18},{18,... | collective-permute-start | bytes 393224 | tf_op jit(solution)/shard_map/ppermute | solution.py:45
  369.2 16.2 %collective-permute-start.10 = (bf16[32,2048]{1,0:T(8,128)(2,1)S(1)}, bf16[32,2048]{1,0:T(8,128)(2,1)S(1)}, u32[]{:S(2)}, u32[]{:S(2)}) collective-permute-start(bf16[32,2048]{1,0:T(8,128)(2,1)S(1)} %add_convert_fusion.7), channel_id=1, source_target_pairs={{1,2},{2,1},{5,6},{6,5},{9,10},{10,9},{13,14},{14,13},{17,18},{18,... | collective-permute-start | bytes 393224 | tf_op jit(solution)/shard_map/ppermute | solution.py:45
  369.9 16.2 %collective-permute-start.20 = (bf16[32,2048]{1,0:T(8,128)(2,1)S(1)}, bf16[32,2048]{1,0:T(8,128)(2,1)S(1)}, u32[]{:S(2)}, u32[]{:S(2)}) collective-permute-start(bf16[32,2048]{1,0:T(8,128)(2,1)S(1)} %fusion.4), channel_id=1, source_target_pairs={{0,1},{1,0},{2,3},{3,2},{4,5},{5,4},{6,7},{7,6},{8,9},{9,8},{10,11... | collective-permute-start | bytes 393224 | tf_op jit(solution)/shard_map/ppermute | solution.py:45
  384.0 20.3 %collective-permute-start.67 = (f32[32,2048]{1,0:T(8,128)S(1)}, f32[32,2048]{1,0:T(8,128)S(1)}, u32[]{:S(2)}, u32[]{:S(2)}) collective-permute-start(f32[32,2048]{1,0:T(8,128)S(1)} %slice.463), channel_id=1, source_target_pairs={{0,8},{4,12},{8,0},{12,4},{1,9},{5,13},{9,1},{13,5},{2,10},{6,14},... | collective-permute-start | bytes 786440 | tf_op jit(solution)/shard_map/ppermute | solution.py:48
  385.4 6.2 %collective-permute-start.31 = (bf16[32,2048]{1,0:T(8,128)(2,1)S(1)}, bf16[32,2048]{1,0:T(8,128)(2,1)S(1)}, u32[]{:S(2)}, u32[]{:S(2)}) collective-permute-start(bf16[32,2048]{1,0:T(8,128)(2,1)S(1)} %add_convert_fusion.5), channel_id=1, source_target_pairs={{1,2},{2,1},{5,6},{6,5},{9,10},{10,9},{13,14},{14,13},{17,18},{18,... | collective-permute-start | bytes 393224 | tf_op jit(solution)/shard_map/ppermute | solution.py:45
  386.1 6.4 %collective-permute-start.41 = (bf16[32,2048]{1,0:T(8,128)(2,1)S(1)}, bf16[32,2048]{1,0:T(8,128)(2,1)S(1)}, u32[]{:S(2)}, u32[]{:S(2)}) collective-permute-start(bf16[32,2048]{1,0:T(8,128)(2,1)S(1)} %fusion.5), channel_id=1, source_target_pairs={{0,1},{1,0},{2,3},{3,2},{4,5},{5,4},{6,7},{7,6},{8,9},{9,8},{10,11... | collective-permute-start | bytes 393224 | tf_op jit(solution)/shard_map/ppermute | solution.py:45
  391.0 9.0 %collective-permute-start.52 = (bf16[32,2048]{1,0:T(8,128)(2,1)S(1)}, bf16[32,2048]{1,0:T(8,128)(2,1)S(1)}, u32[]{:S(2)}, u32[]{:S(2)}) collective-permute-start(bf16[32,2048]{1,0:T(8,128)(2,1)S(1)} %add_convert_fusion.3), channel_id=1, source_target_pairs={{1,2},{2,1},{5,6},{6,5},{9,10},{10,9},{13,14},{14,13},{17,18},{18,... | collective-permute-start | bytes 393224 | tf_op jit(solution)/shard_map/ppermute | solution.py:45
  391.7 13.3 %collective-permute-start.73 = (bf16[32,2048]{1,0:T(8,128)(2,1)S(1)}, bf16[32,2048]{1,0:T(8,128)(2,1)S(1)}, u32[]{:S(2)}, u32[]{:S(2)}) collective-permute-start(bf16[32,2048]{1,0:T(8,128)(2,1)S(1)} %add_convert_fusion.1), channel_id=1, source_target_pairs={{1,2},{2,1},{5,6},{6,5},{9,10},{10,9},{13,14},{14,13},{17,18},{18,... | collective-permute-start | bytes 393224 | tf_op jit(solution)/shard_map/ppermute | solution.py:45
  392.5 7.5 %collective-permute-start.62 = (bf16[32,2048]{1,0:T(8,128)(2,1)S(1)}, bf16[32,2048]{1,0:T(8,128)(2,1)S(1)}, u32[]{:S(2)}, u32[]{:S(2)}) collective-permute-start(bf16[32,2048]{1,0:T(8,128)(2,1)S(1)} %fusion.6), channel_id=1, source_target_pairs={{0,1},{1,0},{2,3},{3,2},{4,5},{5,4},{6,7},{7,6},{8,9},{9,8},{10,11... | collective-permute-start | bytes 393224 | tf_op jit(solution)/shard_map/ppermute | solution.py:45
  399.9 5.1 %collective-permute-start.83 = (bf16[32,2048]{1,0:T(8,128)(2,1)S(1)}, bf16[32,2048]{1,0:T(8,128)(2,1)S(1)}, u32[]{:S(2)}, u32[]{:S(2)}) collective-permute-start(bf16[32,2048]{1,0:T(8,128)(2,1)S(1)} %fusion.7), channel_id=1, source_target_pairs={{0,1},{1,0},{2,3},{3,2},{4,5},{5,4},{6,7},{7,6},{8,9},{9,8},{10,11... | collective-permute-start | bytes 393224 | tf_op jit(solution)/shard_map/ppermute | solution.py:45
  400.0 9.3 %collective-permute-start.87 = (f32[32]{0:T(128)S(1)}, f32[32]{0:T(128)S(1)}, u32[]{:S(2)}, u32[]{:S(2)}) collective-permute-start(f32[32]{0:T(128)S(1)} %get-tuple-element.65), channel_id=1, source_target_pairs={{0,4},{4,0},{8,12},{12,8},{1,5},{5,1},{9,13},{13,9},{2,6},{6,2},{1... | collective-permute-start | bytes 392 | tf_op jit(solution)/shard_map/ppermute | solution.py:48
  400.1 9.9 %collective-permute-start.89 = (f32[32]{0:T(128)S(1)}, f32[32]{0:T(128)S(1)}, u32[]{:S(2)}, u32[]{:S(2)}) collective-permute-start(f32[32]{0:T(128)S(1)} %get-tuple-element.65), channel_id=1, source_target_pairs={{0,12},{4,8},{8,4},{12,0},{1,13},{5,9},{9,5},{13,1},{2,14},{6,10},... | collective-permute-start | bytes 392 | tf_op jit(solution)/shard_map/ppermute | solution.py:48
  404.3 5.7 %collective-permute-start.88 = (f32[32]{0:T(128)S(1)}, f32[32]{0:T(128)S(1)}, u32[]{:S(2)}, u32[]{:S(2)}) collective-permute-start(f32[32]{0:T(128)S(1)} %get-tuple-element.65), channel_id=1, source_target_pairs={{0,8},{4,12},{8,0},{12,4},{1,9},{5,13},{9,1},{13,5},{2,10},{6,14},... | collective-permute-start | bytes 392 | tf_op jit(solution)/shard_map/ppermute | solution.py:48
  405.0 6.4 %collective-permute-start.90 = (f32[32]{0:T(128)S(1)}, f32[32]{0:T(128)S(1)}, u32[]{:S(2)}, u32[]{:S(2)}) collective-permute-start(f32[32]{0:T(128)S(1)} %get-tuple-element.67), channel_id=1, source_target_pairs={{0,4},{4,0},{8,12},{12,8},{1,5},{5,1},{9,13},{13,9},{2,6},{6,2},{1... | collective-permute-start | bytes 392 | tf_op jit(solution)/shard_map/ppermute | solution.py:48
  405.0 7.2 %collective-permute-start.92 = (f32[32]{0:T(128)S(1)}, f32[32]{0:T(128)S(1)}, u32[]{:S(2)}, u32[]{:S(2)}) collective-permute-start(f32[32]{0:T(128)S(1)} %get-tuple-element.67), channel_id=1, source_target_pairs={{0,12},{4,8},{8,4},{12,0},{1,13},{5,9},{9,5},{13,1},{2,14},{6,10},... | collective-permute-start | bytes 392 | tf_op jit(solution)/shard_map/ppermute | solution.py:48
  416.7 5.1 %collective-permute-start.43 = (f32[32,512]{1,0:T(8,128)S(1)}, f32[32,512]{1,0:T(8,128)S(1)}, u32[]{:S(2)}, u32[]{:S(2)}) collective-permute-start(f32[32,512]{1,0:T(8,128)S(1)} %get-tuple-element.25), channel_id=1, source_target_pairs={{0,8},{4,12},{8,0},{12,4},{1,9},{5,13},{9,1},{13,5},{2,10},{6,14},... | collective-permute-start | bytes 196616 | tf_op jit(solution)/shard_map/ppermute | solution.py:48
  (49 other events, 311.2 us)

commit v2 on v1

v2 whole, which is shorter than its diff:
```python
import jax
import jax.numpy as jnp
from jax import lax
from jax.sharding import PartitionSpec as P

CHUNK_ROWS = (160, 160, 128, 64)

F32 = jnp.float32
BF16 = jnp.bfloat16


def dot_t(a, b):
    return lax.dot_general(a, b, (((1,), (1,)), ((), ())), preferred_element_type=F32)


def selection_counts(chosen_ids, first_row, rows):
    row_ids = first_row + lax.broadcasted_iota(jnp.int32, (rows, chosen_ids.shape[0]), 0)
    ids = chosen_ids.T
    counts = jnp.zeros(row_ids.shape, F32)
    for k in range(ids.shape[0]):
        counts = counts + (row_ids == ids[k][None, :]).astype(F32)
    return counts


def any_mesh(train_grads, test_grads, fisher, chosen_ids):
    test_whole = lax.all_gather(test_grads, "test", axis=0, tiled=True)
    partial_value = jnp.dot(test_whole, fisher, preferred_element_type=F32)
    precond = lax.psum(partial_value, "train").astype(BF16)
    partial_scores = dot_t(train_grads, precond)
    scores = lax.psum_scatter(partial_scores, "test", scatter_dimension=1, tiled=True)
    rows = scores.shape[0]
    counts = selection_counts(chosen_ids, lax.axis_index("train") * rows, rows)
    return scores, lax.psum(jnp.sum(counts * scores, axis=0), "train")


def four_by_four(train_grads, test_grads, fisher, chosen_ids):
    z = lax.axis_index("test")
    i = lax.axis_index("train")
    chip, core = i // 2, i % 2
    own_rows = train_grads.shape[0]

    def along(value, pairs):
        return lax.ppermute(value.astype(BF16), "test", pairs).astype(F32)

    def to_other(value, r):
        return lax.ppermute(value, "train", [(k, k ^ r) for k in range(4)])

    pair = [(0, 1), (1, 0), (2, 3), (3, 2)]
    middle = [(1, 2), (2, 1)]
    inward = [(0, 1), (3, 2)]

    def reorder(parts):
        parts = [jnp.where(core == 0, parts[r], parts[r ^ 1]) for r in range(4)]
        return [jnp.where(chip == 0, parts[r], parts[r ^ 2]) for r in range(4)]

    grads = [train_grads, to_other(train_grads, 1), to_other(train_grads, 2)]
    grads = jnp.concatenate(grads + [to_other(grads[2], 1)])

    blocks = jnp.stack([i, i ^ 1, i ^ 2, i ^ 3])
    row_ids = (blocks[:, None] * own_rows + jnp.arange(own_rows)[None, :]).reshape(1, 1, -1)

    outs, sums = [], []
    first = 0
    for rows in CHUNK_ROWS:
        quarter = rows // 4
        piece = test_grads[first : first + rows]
        relative = reorder([piece[q * quarter : (q + 1) * quarter] for q in range(4)])
        relative = jnp.concatenate([relative[r] for r in (0, 2, 1, 3)])
        block = lax.all_gather(relative, "test", axis=0, tiled=True)

        part = jnp.dot(block, fisher, preferred_element_type=F32).reshape(4, 4, quarter, -1)
        chip_part = part[:, :2] + to_other(part[:, 2:], 1)
        other = to_other(chip_part[:, 1].astype(BF16), 2).astype(F32)
        precond = (chip_part[:, 0] + other).reshape(rows, -1)
        high = precond.astype(BF16)
        low = (precond - high.astype(F32)).astype(BF16)
        both = dot_t(jnp.concatenate([high, low]), grads)
        value = (both[:rows] + both[rows:]).reshape(4, quarter, -1)

        own = value[z]
        near = value[z ^ 1]
        if first + rows == test_grads.shape[0]:
            total = own + along(near, pair)
            total = total + along(value[z ^ 2], [(0, 2), (1, 3), (2, 0), (3, 1)])
            total = total + along(value[z ^ 3], [(0, 3), (1, 2), (2, 1), (3, 0)])
        else:
            low_half = z < 2
            far = jnp.where(low_half, value[2:], value[1::-1])
            far = far + along(far, inward)
            got = along(far, middle)
            total = own + got[0] + along(near + got[1], pair)

        ids = reorder([chosen_ids[first + q * quarter : first + (q + 1) * quarter] for q in range(4)])[0]
        counts = jnp.sum((ids[:, :, None] == row_ids).astype(F32), axis=1)
        chosen = jnp.sum(counts * total, axis=1)
        parts = [total[:, r * own_rows : (r + 1) * own_rows] for r in range(4)]
        outs += reorder([parts[0]] + [to_other(parts[r], r) for r in range(1, 4)])
        sums += reorder([chosen] + [to_other(chosen, r) for r in range(1, 4)])
        first += rows
    return jnp.concatenate(outs).T, jnp.concatenate(sums)


def solution(mesh):
    sizes = (mesh.shape["train"], mesh.shape["test"])
    return jax.shard_map(
        four_by_four if sizes == (4, 4) else any_mesh,
        mesh=mesh,
        in_specs=(
            P(("groups", "train"), "test"),
            P(("groups", "test"), "train"),
            P("train", "test"),
            P(("groups", "test"), None),
        ),
        out_specs=(P(("groups", "train"), "test"), P(("groups", "test"))),
        check_vma=False,
    )
```

time: 436 us -> 359 us (0.82); the launches traced: 430 us -> 359 us
  starting transfers between devices: 116 us -> 59.4 us
  waiting for transfers between devices: 209 us -> 186 us
  matrix products: 75.3 us -> 54 us
  other arithmetic: 12 us -> 24.5 us
  between operations: 2.21 us -> 14.7 us
  local copies, waits for them, and re-layouts: 14.9 us -> 20.1 us
    ppermute x40 -> x12, waiting for transfers between devices: 143 us -> 15.2 us  [along(): return lax.ppermute(value.astype(BF16), 'test', pairs).astype(F32)]
    all_gather x0 -> x4, waiting for transfers between devices: none -> 126 us  [four_by_four(): block = lax.all_gather(relative, 'test', axis=0, tiled=True)]
    ppermute x40 -> x12, starting transfers between devices: 81.9 us -> 31.7 us  [along(): return lax.ppermute(value.astype(BF16), 'test', pairs).astype(F32)]
    ppermute x59 -> x35, waiting for transfers between devices: 66.5 us -> 45.1 us  [to_other(): return lax.ppermute(value, 'train', [(k, k ^ r) for k in range(4)])]
    dot_general x16 -> x4, matrix products: 41.9 us -> 22.8 us  [dot_t(): lax.dot_general(a, b, (((1,), (1,)), ((), ())), preferred_element_type=F32)]
    ppermute x59 -> x35, starting transfers between devices: 34.3 us -> 27.5 us  [to_other(): return lax.ppermute(value, 'train', [(k, k ^ r) for k in range(4)])]
    unnamed x33 -> x47, local copies, waits for them, and re-layouts: 7.52 us -> 11.6 us
    dot_general x16 -> x4, matrix products: 33.4 us -> 31.2 us  [four_by_four(): jnp.dot(block, fisher, preferred_element_type=F32)]
  transfers between devices with their start and end apart: 99 -> 51, of which waited for: 42 -> 22; matrix products, arithmetic and copies ran while one was open for 23% -> 25% of each run, Pallas kernels for 0% -> 0%
where the time goes in v2:
time: 359 us
  waiting for transfers between devices  186 us (52%)
  starting transfers between devices  59.4 us (17%)
  matrix products  54 us (15%)
  other arithmetic  24.5 us (7%)
  local copies, waits for them, and re-layouts  20.1 us (6%)
  between operations  14.7 us (4%)
    all_gather x4, waiting for transfers between devices, four_by_four(): block = lax.all_gather(relative, 'test', axis=0, tiled=True)  126 us
    ppermute x35, waiting for transfers between devices, to_other(): return lax.ppermute(value, 'train', [(k, k ^ r) for k in range(4)])  45.1 us
    ppermute x12, starting transfers between devices, along(): return lax.ppermute(value.astype(BF16), 'test', pairs).astype(F32)  31.7 us
    dot_general x4, matrix products, four_by_four(): jnp.dot(block, fisher, preferred_element_type=F32)  31.2 us
    ppermute x35, starting transfers between devices, to_other(): return lax.ppermute(value, 'train', [(k, k ^ r) for k in range(4)])  27.5 us
    dot_general x4, matrix products, dot_t(): lax.dot_general(a, b, (((1,), (1,)), ((), ())), preferred_element_type=F32)  22.8 us
    ppermute x12, waiting for transfers between devices, along(): return lax.ppermute(value.astype(BF16), 'test', pairs).astype(F32)  15.2 us
    unnamed x47, local copies, waits for them, and re-layouts  11.6 us
  transfers between devices with their start and end apart: 51, of which 22 were waited for; matrix products, arithmetic and copies ran while one was open for 25% of the time, Pallas kernels for 0%

profile of v2, /device:TPU:0, one launch (start us, length us, event | category | flops | bytes accessed | tf_op | source)
XLA Modules:
  0.0 358.6 jit_solution(2938289618234929279)
XLA Ops:
  7.2 1.1 broadcast_select_fusion.31
  9.2 1.1 broadcast_select_fusion.23
  12.9 2.6 collective-permute-start.3
  17.2 23.1 %all-gather.11.cloned.1.call-done = bf16[256,2048]{1,0:T(8,128)(2,1)} async-done(((bf16[64,2048]{1,0:T(8,128)(2,1)}), bf16[256,2048]{1,0:T(8,128)(2,1)}) %all-gather.11.cloned.1.call-update) | async-done | bytes 1048592 | tf_op jit(solution)/shard_map/all_gather | solution.py:69
  40.2 6.0 %fusion.66 = f32[256,2048]{1,0:T(8,128)S(1)} fusion(bf16[256,2048]{1,0:T(8,128)(2,1)} %all-gather.11.cloned.1.call-done, bf16[2048,2048]{1,0:T(8,128)(2,1)} %param.6), kind=kOutput, calls=%fused_computation.220 | convolution fusion | flops 2147483648 | bytes 11534336 | tf_op jit(solution)/shard_map/dot_general | solution.py:71
  46.5 1.3 convert_reduce_fusion.3
  47.8 2.1 convert_reduce_fusion.2
  49.8 2.7 convert_reduce_fusion
  52.5 1.4 constant_dynamic-update-slice_fusion.3
  53.9 8.1 %collective-permute-done.3 = bf16[512,2048]{1,0:T(8,128)(2,1)} collective-permute-done((bf16[512,2048]{1,0:T(8,128)(2,1)}, bf16[512,2048]{1,0:T(8,128)(2,1)}, u32[]{:S(2)}, u32[]{:S(2)}) %collective-permute-start.3) | collective-permute-done | bytes 2097184 | tf_op jit(solution)/shard_map/ppermute | solution.py:46
  62.0 1.5 constant_dynamic-update-slice_fusion.2
  63.7 1.8 collective-permute-start.28
  65.5 3.2 constant_dynamic-update-slice_fusion.1
  68.8 3.8 %collective-permute-done.28 = bf16[4,16,2048]{2,1,0:T(8,128)(2,1)S(1)} collective-permute-done((bf16[4,16,2048]{2,1,0:T(8,128)(2,1)S(1)}, bf16[4,16,2048]{2,1,0:T(8,128)(2,1)S(1)}, u32[]{:S(2)}, u32[]{:S(2)}) %collective-permute-start.28) | collective-permute-done | bytes 262176 | tf_op jit(solution)/shard_map/ppermute | solution.py:46
  73.3 13.9 %all-gather.9.cloned.1.call-done = bf16[512,2048]{1,0:T(8,128)(2,1)} async-done(((bf16[128,2048]{1,0:T(8,128)(2,1)}), bf16[512,2048]{1,0:T(8,128)(2,1)}) %all-gather.9.cloned.1.call-update) | async-done | bytes 2097168 | tf_op jit(solution)/shard_map/all_gather | solution.py:69
  87.3 7.6 %fusion.65 = f32[512,2048]{1,0:T(8,128)S(1)} fusion(bf16[512,2048]{1,0:T(8,128)(2,1)} %all-gather.9.cloned.1.call-done, bf16[2048,2048]{1,0:T(8,128)(2,1)} %param.6), kind=kOutput, calls=%fused_computation.219 | convolution fusion | flops 4294967296 | bytes 14680064 | tf_op jit(solution)/shard_map/dot_general | solution.py:71
  94.9 2.0 copy-done.2
  96.8 1.5 slice.413
  98.3 44.7 %all-gather.5.cloned.1.call-done = bf16[640,2048]{1,0:T(8,128)(2,1)} async-done(((bf16[160,2048]{1,0:T(8,128)(2,1)}), bf16[640,2048]{1,0:T(8,128)(2,1)}) %all-gather.5.cloned.1.call-update) | async-done | bytes 2621456 | tf_op jit(solution)/shard_map/all_gather | solution.py:69
  143.0 8.8 %fusion.63 = f32[640,2048]{1,0:T(8,128)S(1)} fusion(bf16[640,2048]{1,0:T(8,128)(2,1)} %all-gather.5.cloned.1.call-done, bf16[2048,2048]{1,0:T(8,128)(2,1)} %param.6), kind=kOutput, calls=%fused_computation.217 | convolution fusion | flops 5368709120 | bytes 16252928 | tf_op jit(solution)/shard_map/dot_general | solution.py:71
  152.1 2.1 copy-done.1
  154.2 43.8 %all-gather.7.cloned.1.call-done = bf16[640,2048]{1,0:T(8,128)(2,1)} async-done(((bf16[160,2048]{1,0:T(8,128)(2,1)}), bf16[640,2048]{1,0:T(8,128)(2,1)}) %all-gather.7.cloned.1.call-update) | async-done | bytes 2621456 | tf_op jit(solution)/shard_map/all_gather | solution.py:69
  198.0 8.8 %fusion.64 = f32[640,2048]{1,0:T(8,128)S(1)} fusion(bf16[640,2048]{1,0:T(8,128)(2,1)} %all-gather.7.cloned.1.call-done, bf16[2048,2048]{1,0:T(8,128)(2,1)} %param.6), kind=kOutput, calls=%fused_computation.218 | convolution fusion | flops 5368709120 | bytes 16252928 | tf_op jit(solution)/shard_map/dot_general | solution.py:71
  207.2 3.4 constant_dynamic-update-slice_fusion
  210.6 2.0 slice_add_fusion.2
  212.7 1.5 collective-permute-start.20
  214.2 6.3 %fusion.22 = f32[128,2048]{1,0:T(8,128)S(1)} fusion(bf16[2048,2048]{1,0:T(8,128)(2,1)} %constant_dynamic-update-slice_fusion, bf16[64,2048]{1,0:T(8,128)(2,1)S(1)} %get-tuple-element.16, bf16[64,2048]{1,0:T(8,128)(2,1)S(1)} %copy-done.5), kind=kOutput, calls=%fused_computation.55 | convolution fusion | flops 1074790400 | bytes 9961472 | tf_op jit(solution)/shard_map/dot_general | solution.py:13
  220.5 6.8 %collective-permute-done.20 = bf16[4,32,2048]{2,1,0:T(8,128)(2,1)S(1)} collective-permute-done((bf16[4,32,2048]{2,1,0:T(8,128)(2,1)S(1)}, bf16[4,32,2048]{2,1,0:T(8,128)(2,1)S(1)}, u32[]{:S(2)}, u32[]{:S(2)}) %collective-permute-start.20) | collective-permute-done | bytes 524320 | tf_op jit(solution)/shard_map/ppermute | solution.py:46
  227.6 5.9 %fusion.13 = f32[256,2048]{1,0:T(8,128)S(1)} fusion(bf16[2048,2048]{1,0:T(8,128)(2,1)} %constant_dynamic-update-slice_fusion, bf16[128,2048]{1,0:T(8,128)(2,1)S(1)} %get-tuple-element.18, bf16[128,2048]{1,0:T(8,128)(2,1)S(1)} %get-tuple-element.19), kind=kOutput, calls=%fused_computation.34 | convolution fusion | flops 2149580800 | bytes 11534336 | tf_op jit(solution)/shard_map/dot_general | solution.py:13
  233.8 1.8 collective-permute-start.21
  235.7 3.1 collective-permute-start.31
  238.9 3.2 collective-permute-done.21
  242.1 2.5 collective-permute-start.29
  244.6 2.4 collective-permute-done.31
  248.0 1.6 collective-permute-start.46
  250.8 1.5 collective-permute-start.33
  252.4 3.6 %collective-permute-start.23 = (bf16[32,2048]{1,0:T(8,128)(2,1)S(1)}, bf16[32,2048]{1,0:T(8,128)(2,1)S(1)}, u32[]{:S(2)}, u32[]{:S(2)}) collective-permute-start(bf16[32,2048]{1,0:T(8,128)(2,1)S(1)} %fusion.42), channel_id=1, source_target_pairs={{0,1},{1,0},{2,3},{3,2},{4,5},{5,4},{6,7},{7,6},{8,9},{9,8},{10,11... | collective-permute-start | bytes 393224 | tf_op jit(solution)/shard_map/ppermute | solution.py:43
  256.0 2.9 collective-permute-done.23
  259.2 1.6 collective-permute-start.43
  262.2 1.5 collective-permute-start.34
  263.7 1.3 collective-permute-done.42
  265.6 2.2 slice_add_fusion.1
  269.2 1.5 collective-permute-start.12
  270.7 15.0 %collective-permute-done.1 = bf16[4,40,2048]{2,1,0:T(8,128)(2,1)S(1)} collective-permute-done((bf16[4,40,2048]{2,1,0:T(8,128)(2,1)S(1)}, bf16[4,40,2048]{2,1,0:T(8,128)(2,1)S(1)}, u32[]{:S(2)}, u32[]{:S(2)}) %collective-permute-start.1) | collective-permute-done | bytes 655392 | tf_op jit(solution)/shard_map/ppermute | solution.py:46
  286.0 5.3 %fusion.2 = f32[320,2048]{1,0:T(8,128)S(1)} fusion(bf16[2048,2048]{1,0:T(8,128)(2,1)} %constant_dynamic-update-slice_fusion, bf16[160,2048]{1,0:T(8,128)(2,1)S(1)} %get-tuple-element.22, bf16[160,2048]{1,0:T(8,128)(2,1)S(1)} %get-tuple-element.23), kind=kOutput, calls=%fused_computation.15 | convolution fusion | flops 2686976000 | bytes 12320768 | tf_op jit(solution)/shard_map/dot_general | solution.py:13
  291.7 4.0 %collective-permute-start.5 = (bf16[2,40,2048]{2,1,0:T(8,128)(2,1)S(1)}, bf16[2,40,2048]{2,1,0:T(8,128)(2,1)S(1)}, u32[]{:S(2)}, u32[]{:S(2)}) collective-permute-start(bf16[2,40,2048]{2,1,0:T(8,128)(2,1)S(1)} %fusion.37), channel_id=1, source_target_pairs={{0,1},{3,2},{4,5},{7,6},{8,9},{11,10},{12,13},{15,14},{16,17},{19,... | collective-permute-start | bytes 983048 | tf_op jit(solution)/shard_map/ppermute | solution.py:43
  295.7 2.0 collective-permute-done.12
  297.9 5.3 %fusion.6 = f32[320,2048]{1,0:T(8,128)S(1)} fusion(bf16[2048,2048]{1,0:T(8,128)(2,1)} %constant_dynamic-update-slice_fusion, bf16[160,2048]{1,0:T(8,128)(2,1)S(1)} %get-tuple-element.20, bf16[160,2048]{1,0:T(8,128)(2,1)S(1)} %get-tuple-element.21), kind=kOutput, calls=%fused_computation.19 | convolution fusion | flops 2686976000 | bytes 12320768 | tf_op jit(solution)/shard_map/dot_general | solution.py:13
  303.6 3.9 %collective-permute-start.13 = (bf16[2,40,2048]{2,1,0:T(8,128)(2,1)S(1)}, bf16[2,40,2048]{2,1,0:T(8,128)(2,1)S(1)}, u32[]{:S(2)}, u32[]{:S(2)}) collective-permute-start(bf16[2,40,2048]{2,1,0:T(8,128)(2,1)S(1)} %fusion.38), channel_id=1, source_target_pairs={{0,1},{3,2},{4,5},{7,6},{8,9},{11,10},{12,13},{15,14},{16,17},{19,... | collective-permute-start | bytes 983048 | tf_op jit(solution)/shard_map/ppermute | solution.py:43
  308.4 4.3 %collective-permute-done.13 = bf16[2,40,2048]{2,1,0:T(8,128)(2,1)S(1)} collective-permute-done((bf16[2,40,2048]{2,1,0:T(8,128)(2,1)S(1)}, bf16[2,40,2048]{2,1,0:T(8,128)(2,1)S(1)}, u32[]{:S(2)}, u32[]{:S(2)}) %collective-permute-start.13) | collective-permute-done | bytes 327712 | tf_op jit(solution)/shard_map/ppermute | solution.py:43
  313.6 5.0 %collective-permute-start.7 = (bf16[40,2048]{1,0:T(8,128)(2,1)S(1)}, bf16[40,2048]{1,0:T(8,128)(2,1)S(1)}, u32[]{:S(2)}, u32[]{:S(2)}) collective-permute-start(bf16[40,2048]{1,0:T(8,128)(2,1)S(1)} %fusion.40), channel_id=1, source_target_pairs={{0,1},{1,0},{2,3},{3,2},{4,5},{5,4},{6,7},{7,6},{8,9},{9,8},{10,11... | collective-permute-start | bytes 491528 | tf_op jit(solution)/shard_map/ppermute | solution.py:43
  318.7 5.7 %collective-permute-start.15 = (bf16[40,2048]{1,0:T(8,128)(2,1)S(1)}, bf16[40,2048]{1,0:T(8,128)(2,1)S(1)}, u32[]{:S(2)}, u32[]{:S(2)}) collective-permute-start(bf16[40,2048]{1,0:T(8,128)(2,1)S(1)} %fusion.41), channel_id=1, source_target_pairs={{0,1},{1,0},{2,3},{3,2},{4,5},{5,4},{6,7},{7,6},{8,9},{9,8},{10,11... | collective-permute-start | bytes 491528 | tf_op jit(solution)/shard_map/ppermute | solution.py:43
  325.4 2.3 collective-permute-done.15
  328.6 1.6 collective-permute-start.40
  330.1 1.1 collective-permute-done.36
  331.8 1.5 collective-permute-start.9
  333.4 1.4 collective-permute-done.39
  336.3 2.3 collective-permute-start.17
  339.4 1.7 collective-permute-done.17
  341.1 2.4 collective-permute-start.25
  343.4 0.9 collective-permute-start.26
  344.5 1.2 collective-permute-done.25
  345.7 1.8 collective-permute-done.26
  350.8 1.3 copy.47
  (188 shorter events, 24.2 us)
Async XLA Ops:
  7.2 33.1 %all-gather.11.cloned.1.call-start = ((), (), s32[]{:S(2)}) async-start(), calls=%async_computation.3 | async-start | bytes 1310720 | tf_op jit(solution)/shard_map/all_gather | solution.py:69
  9.1 78.2 %all-gather.9.cloned.1.call-start = ((), (), s32[]{:S(2)}) async-start(), calls=%async_computation.2 | async-start | bytes 2621440 | tf_op jit(solution)/shard_map/all_gather | solution.py:69
  11.2 131.8 %all-gather.5.cloned.1.call-start = ((), (), s32[]{:S(2)}) async-start(), calls=%async_computation | async-start | bytes 3276800 | tf_op jit(solution)/shard_map/all_gather | solution.py:69
  12.3 185.7 %all-gather.7.cloned.1.call-start = ((), (), s32[]{:S(2)}) async-start(), calls=%async_computation.1 | async-start | bytes 3276800 | tf_op jit(solution)/shard_map/all_gather | solution.py:69
  12.4 49.6 %collective-permute-start.2 = (bf16[512,2048]{1,0:T(8,128)(2,1)}, bf16[512,2048]{1,0:T(8,128)(2,1)S(1)}, u32[]{:S(2)}, u32[]{:S(2)}) collective-permute-start(bf16[512,2048]{1,0:T(8,128)(2,1)} %param.4), channel_id=1, source_target_pairs={{0,4},{4,0},{8,12},{12,8},{1,5},{5,1},{9,13},{13,9},{2,6},{6,2},{1... | collective-permute-start | bytes 6291464 | tf_op jit(solution)/shard_map/ppermute | solution.py:46
  12.9 49.1 %collective-permute-start.3 = (bf16[512,2048]{1,0:T(8,128)(2,1)}, bf16[512,2048]{1,0:T(8,128)(2,1)}, u32[]{:S(2)}, u32[]{:S(2)}) collective-permute-start(bf16[512,2048]{1,0:T(8,128)(2,1)} %param.4), channel_id=1, source_target_pairs={{0,8},{4,12},{8,0},{12,4},{1,9},{5,13},{9,1},{13,5},{2,10},{6,14},... | collective-permute-start | bytes 6291464 | tf_op jit(solution)/shard_map/ppermute | solution.py:46
  46.4 17.1 %collective-permute-start.27 = (f32[4,2,16,2048]{3,2,1,0:T(8,128)S(1)}, f32[4,2,16,2048]{3,2,1,0:T(8,128)S(1)}, u32[]{:S(2)}, u32[]{:S(2)}) collective-permute-start(f32[4,2,16,2048]{3,2,1,0:T(8,128)S(1)} %slice.427), channel_id=1, source_target_pairs={{0,4},{4,0},{8,12},{12,8},{1,5},{5,1},{9,13},{13,9},{2,6},{6,2},{1... | collective-permute-start | bytes 3145736 | tf_op jit(solution)/shard_map/ppermute | solution.py:46
  62.0 145.2 %collective-permute-start.4 = (bf16[512,2048]{1,0:T(8,128)(2,1)}, bf16[512,2048]{1,0:T(8,128)(2,1)}, u32[]{:S(2)}, u32[]{:S(2)}) collective-permute-start(bf16[512,2048]{1,0:T(8,128)(2,1)} %collective-permute-done.3), channel_id=1, source_target_pairs={{0,4},{4,0},{8,12},{12,8},{1,5},{5,1},{9,13},{13,9},{2,6},{6,2},{1... | collective-permute-start | bytes 6291464 | tf_op jit(solution)/shard_map/ppermute | solution.py:46
  63.7 8.8 %collective-permute-start.28 = (bf16[4,16,2048]{2,1,0:T(8,128)(2,1)S(1)}, bf16[4,16,2048]{2,1,0:T(8,128)(2,1)S(1)}, u32[]{:S(2)}, u32[]{:S(2)}) collective-permute-start(bf16[4,16,2048]{2,1,0:T(8,128)(2,1)S(1)} %fusion.33), channel_id=1, source_target_pairs={{0,8},{4,12},{8,0},{12,4},{1,9},{5,13},{9,1},{13,5},{2,10},{6,14},... | collective-permute-start | bytes 786440 | tf_op jit(solution)/shard_map/ppermute | solution.py:46
  98.3 112.3 %collective-permute-start.19 = (f32[4,2,32,2048]{3,2,1,0:T(8,128)}, f32[4,2,32,2048]{3,2,1,0:T(8,128)}, u32[]{:S(2)}, u32[]{:S(2)}) collective-permute-start(f32[4,2,32,2048]{3,2,1,0:T(8,128)} %slice.413), channel_id=1, source_target_pairs={{0,4},{4,0},{8,12},{12,8},{1,5},{5,1},{9,13},{13,9},{2,6},{6,2},{1... | collective-permute-start | bytes 6291464 | tf_op jit(solution)/shard_map/ppermute | solution.py:46
  154.2 111.4 %collective-permute-start = (f32[4,2,40,2048]{3,2,1,0:T(8,128)S(1)}, f32[4,2,40,2048]{3,2,1,0:T(8,128)}, u32[]{:S(2)}, u32[]{:S(2)}) collective-permute-start(f32[4,2,40,2048]{3,2,1,0:T(8,128)S(1)} %slice.385), channel_id=1, source_target_pairs={{0,4},{4,0},{8,12},{12,8},{1,5},{5,1},{9,13},{13,9},{2,6},{6,2},{1... | collective-permute-start | bytes 7864328 | tf_op jit(solution)/shard_map/ppermute | solution.py:46
  207.1 61.5 %collective-permute-start.11 = (f32[4,2,40,2048]{3,2,1,0:T(8,128)S(1)}, f32[4,2,40,2048]{3,2,1,0:T(8,128)S(1)}, u32[]{:S(2)}, u32[]{:S(2)}) collective-permute-start(f32[4,2,40,2048]{3,2,1,0:T(8,128)S(1)} %slice.399), channel_id=1, source_target_pairs={{0,4},{4,0},{8,12},{12,8},{1,5},{5,1},{9,13},{13,9},{2,6},{6,2},{1... | collective-permute-start | bytes 7864328 | tf_op jit(solution)/shard_map/ppermute | solution.py:46
  212.7 14.6 %collective-permute-start.20 = (bf16[4,32,2048]{2,1,0:T(8,128)(2,1)S(1)}, bf16[4,32,2048]{2,1,0:T(8,128)(2,1)S(1)}, u32[]{:S(2)}, u32[]{:S(2)}) collective-permute-start(bf16[4,32,2048]{2,1,0:T(8,128)(2,1)S(1)} %fusion.20), channel_id=1, source_target_pairs={{0,8},{4,12},{8,0},{12,4},{1,9},{5,13},{9,1},{13,5},{2,10},{6,14},... | collective-permute-start | bytes 1572872 | tf_op jit(solution)/shard_map/ppermute | solution.py:46
  227.5 38.1 %slice-start = ((s8[5242880]{0:T(1024)(128)(4,1)}), s8[4194304]{0:T(1024)(128)(4,1)S(1)}, s32[]{:S(2)}) async-start(s8[5242880]{0:T(1024)(128)(4,1)} %bitcast.141), calls=%async_computation.4 | async-start | bytes 8388608
  227.6 38.1 %slice-start.1 = ((s8[5242880]{0:T(1024)(128)(4,1)}), s8[1048576]{0:T(1024)(128)(4,1)S(1)}, s32[]{:S(2)}) async-start(s8[5242880]{0:T(1024)(128)(4,1)} %bitcast.141), calls=%async_computation.5 | async-start | bytes 2097152
  233.7 14.0 %copy-start.10 = (f32[16,2048]{1,0:T(8,128)S(1)}, f32[16,2048]{1,0:T(8,128)}, u32[]{:S(2)}) copy-start(f32[16,2048]{1,0:T(8,128)} %convert_reduce_fusion.3) | copy-start | bytes 393220
  233.8 25.2 %copy-start.6 = (f32[32,2048]{1,0:T(8,128)S(1)}, f32[32,2048]{1,0:T(8,128)}, u32[]{:S(2)}) copy-start(f32[32,2048]{1,0:T(8,128)} %convert_reduce_fusion.2) | copy-start | bytes 786436
  233.8 8.3 %collective-permute-start.21 = (bf16[2,32,2048]{2,1,0:T(8,128)(2,1)S(1)}, bf16[2,32,2048]{2,1,0:T(8,128)(2,1)S(1)}, u32[]{:S(2)}, u32[]{:S(2)}) collective-permute-start(bf16[2,32,2048]{2,1,0:T(8,128)(2,1)S(1)} %fusion.39), channel_id=1, source_target_pairs={{0,1},{3,2},{4,5},{7,6},{8,9},{11,10},{12,13},{15,14},{16,17},{19,... | collective-permute-start | bytes 786440 | tf_op jit(solution)/shard_map/ppermute | solution.py:43
  235.7 11.3 %collective-permute-start.31 = (bf16[16,2048]{1,0:T(8,128)(2,1)S(1)}, bf16[16,2048]{1,0:T(8,128)(2,1)S(1)}, u32[]{:S(2)}, u32[]{:S(2)}) collective-permute-start(bf16[16,2048]{1,0:T(8,128)(2,1)S(1)} %get-tuple-element.47), channel_id=1, source_target_pairs={{0,3},{1,2},{2,1},{3,0},{4,7},{5,6},{6,5},{7,4},{8,11},{9,10},{10,... | collective-permute-start | bytes 196616 | tf_op jit(solution)/shard_map/ppermute | solution.py:43
  238.9 8.8 %collective-permute-start.30 = (bf16[16,2048]{1,0:T(8,128)(2,1)S(1)}, bf16[16,2048]{1,0:T(8,128)(2,1)S(1)}, u32[]{:S(2)}, u32[]{:S(2)}) collective-permute-start(bf16[16,2048]{1,0:T(8,128)(2,1)S(1)} %get-tuple-element.48), channel_id=1, source_target_pairs={{0,2},{1,3},{2,0},{3,1},{4,6},{5,7},{6,4},{7,5},{8,10},{9,11},{10,... | collective-permute-start | bytes 196616 | tf_op jit(solution)/shard_map/ppermute | solution.py:43
  242.1 5.6 %collective-permute-start.29 = (bf16[16,2048]{1,0:T(8,128)(2,1)S(1)}, bf16[16,2048]{1,0:T(8,128)(2,1)S(1)}, u32[]{:S(2)}, u32[]{:S(2)}) collective-permute-start(bf16[16,2048]{1,0:T(8,128)(2,1)S(1)} %get-tuple-element.46), channel_id=1, source_target_pairs={{0,1},{1,0},{2,3},{3,2},{4,5},{5,4},{6,7},{7,6},{8,9},{9,8},{10,11... | collective-permute-start | bytes 196616 | tf_op jit(solution)/shard_map/ppermute | solution.py:43
  247.0 3.2 collective-permute-start.22
  247.9 3.0 collective-permute-start.44
  248.0 4.4 %collective-permute-start.46 = (f32[16]{0:T(128)S(1)}, f32[16]{0:T(128)S(1)}, u32[]{:S(2)}, u32[]{:S(2)}) collective-permute-start(f32[16]{0:T(128)S(1)} %get-tuple-element.8), channel_id=1, source_target_pairs={{0,12},{4,8},{8,4},{12,0},{1,13},{5,9},{9,5},{13,1},{2,14},{6,10},... | collective-permute-start | bytes 200 | tf_op jit(solution)/shard_map/ppermute | solution.py:46
  250.2 5.8 %collective-permute-start.45 = (f32[16]{0:T(128)S(1)}, f32[16]{0:T(128)S(1)}, u32[]{:S(2)}, u32[]{:S(2)}) collective-permute-start(f32[16]{0:T(128)S(1)} %get-tuple-element.8), channel_id=1, source_target_pairs={{0,8},{4,12},{8,0},{12,4},{1,9},{5,13},{9,1},{13,5},{2,10},{6,14},... | collective-permute-start | bytes 200 | tf_op jit(solution)/shard_map/ppermute | solution.py:46
  250.8 96.8 %collective-permute-start.33 = (f32[16,512]{1,0:T(8,128)}, f32[16,512]{1,0:T(8,128)}, u32[]{:S(2)}, u32[]{:S(2)}) collective-permute-start(f32[16,512]{1,0:T(8,128)} %get-tuple-element.60), channel_id=1, source_target_pairs={{0,8},{4,12},{8,0},{12,4},{1,9},{5,13},{9,1},{13,5},{2,10},{6,14},... | collective-permute-start | bytes 98312 | tf_op jit(solution)/shard_map/ppermute | solution.py:46
  252.4 6.6 %collective-permute-start.23 = (bf16[32,2048]{1,0:T(8,128)(2,1)S(1)}, bf16[32,2048]{1,0:T(8,128)(2,1)S(1)}, u32[]{:S(2)}, u32[]{:S(2)}) collective-permute-start(bf16[32,2048]{1,0:T(8,128)(2,1)S(1)} %fusion.42), channel_id=1, source_target_pairs={{0,1},{1,0},{2,3},{3,2},{4,5},{5,4},{6,7},{7,6},{8,9},{9,8},{10,11... | collective-permute-start | bytes 393224 | tf_op jit(solution)/shard_map/ppermute | solution.py:43
  259.1 2.4 collective-permute-start.41
  259.2 3.0 collective-permute-start.43
  261.5 3.5 collective-permute-start.42
  262.2 85.4 %collective-permute-start.34 = (f32[16,512]{1,0:T(8,128)}, f32[16,512]{1,0:T(8,128)}, u32[]{:S(2)}, u32[]{:S(2)}) collective-permute-start(f32[16,512]{1,0:T(8,128)} %get-tuple-element.59), channel_id=1, source_target_pairs={{0,12},{4,8},{8,4},{12,0},{1,13},{5,9},{9,5},{13,1},{2,14},{6,10},... | collective-permute-start | bytes 98312 | tf_op jit(solution)/shard_map/ppermute | solution.py:46
  268.0 17.7 %collective-permute-start.1 = (bf16[4,40,2048]{2,1,0:T(8,128)(2,1)S(1)}, bf16[4,40,2048]{2,1,0:T(8,128)(2,1)S(1)}, u32[]{:S(2)}, u32[]{:S(2)}) collective-permute-start(bf16[4,40,2048]{2,1,0:T(8,128)(2,1)S(1)} %fusion.18), channel_id=1, source_target_pairs={{0,8},{4,12},{8,0},{12,4},{1,9},{5,13},{9,1},{13,5},{2,10},{6,14},... | collective-permute-start | bytes 1966088 | tf_op jit(solution)/shard_map/ppermute | solution.py:46
  269.2 28.5 %collective-permute-start.12 = (bf16[4,40,2048]{2,1,0:T(8,128)(2,1)S(1)}, bf16[4,40,2048]{2,1,0:T(8,128)(2,1)S(1)}, u32[]{:S(2)}, u32[]{:S(2)}) collective-permute-start(bf16[4,40,2048]{2,1,0:T(8,128)(2,1)S(1)} %fusion.19), channel_id=1, source_target_pairs={{0,8},{4,12},{8,0},{12,4},{1,9},{5,13},{9,1},{13,5},{2,10},{6,14},... | collective-permute-start | bytes 1966088 | tf_op jit(solution)/shard_map/ppermute | solution.py:46
  291.7 15.9 %collective-permute-start.5 = (bf16[2,40,2048]{2,1,0:T(8,128)(2,1)S(1)}, bf16[2,40,2048]{2,1,0:T(8,128)(2,1)S(1)}, u32[]{:S(2)}, u32[]{:S(2)}) collective-permute-start(bf16[2,40,2048]{2,1,0:T(8,128)(2,1)S(1)} %fusion.37), channel_id=1, source_target_pairs={{0,1},{3,2},{4,5},{7,6},{8,9},{11,10},{12,13},{15,14},{16,17},{19,... | collective-permute-start | bytes 983048 | tf_op jit(solution)/shard_map/ppermute | solution.py:43
  303.6 9.0 %collective-permute-start.13 = (bf16[2,40,2048]{2,1,0:T(8,128)(2,1)S(1)}, bf16[2,40,2048]{2,1,0:T(8,128)(2,1)S(1)}, u32[]{:S(2)}, u32[]{:S(2)}) collective-permute-start(bf16[2,40,2048]{2,1,0:T(8,128)(2,1)S(1)} %fusion.38), channel_id=1, source_target_pairs={{0,1},{3,2},{4,5},{7,6},{8,9},{11,10},{12,13},{15,14},{16,17},{19,... | collective-permute-start | bytes 983048 | tf_op jit(solution)/shard_map/ppermute | solution.py:43
  307.7 5.8 %collective-permute-start.6 = (bf16[2,40,2048]{2,1,0:T(8,128)(2,1)S(1)}, bf16[2,40,2048]{2,1,0:T(8,128)(2,1)S(1)}, u32[]{:S(2)}, u32[]{:S(2)}) collective-permute-start(bf16[2,40,2048]{2,1,0:T(8,128)(2,1)S(1)} %add_convert_fusion.1), channel_id=1, source_target_pairs={{1,2},{2,1},{5,6},{6,5},{9,10},{10,9},{13,14},{14,13},{17,18},{18,... | collective-permute-start | bytes 983048 | tf_op jit(solution)/shard_map/ppermute | solution.py:43
  312.8 5.9 %collective-permute-start.14 = (bf16[2,40,2048]{2,1,0:T(8,128)(2,1)S(1)}, bf16[2,40,2048]{2,1,0:T(8,128)(2,1)S(1)}, u32[]{:S(2)}, u32[]{:S(2)}) collective-permute-start(bf16[2,40,2048]{2,1,0:T(8,128)(2,1)S(1)} %add_convert_fusion), channel_id=1, source_target_pairs={{1,2},{2,1},{5,6},{6,5},{9,10},{10,9},{13,14},{14,13},{17,18},{18,... | collective-permute-start | bytes 983048 | tf_op jit(solution)/shard_map/ppermute | solution.py:43
  313.6 10.9 %collective-permute-start.7 = (bf16[40,2048]{1,0:T(8,128)(2,1)S(1)}, bf16[40,2048]{1,0:T(8,128)(2,1)S(1)}, u32[]{:S(2)}, u32[]{:S(2)}) collective-permute-start(bf16[40,2048]{1,0:T(8,128)(2,1)S(1)} %fusion.40), channel_id=1, source_target_pairs={{0,1},{1,0},{2,3},{3,2},{4,5},{5,4},{6,7},{7,6},{8,9},{9,8},{10,11... | collective-permute-start | bytes 491528 | tf_op jit(solution)/shard_map/ppermute | solution.py:43
  318.7 16.1 %copy-start.15 = (f32[32]{0:T(128)S(1)}, f32[32]{0:T(128)}, u32[]{:S(2)}) copy-start(f32[32]{0:T(128)} %get-tuple-element.67) | copy-start | bytes 388
  318.7 16.1 %copy-start.16 = (f32[32]{0:T(128)S(1)}, f32[32]{0:T(128)}, u32[]{:S(2)}) copy-start(f32[32]{0:T(128)} %get-tuple-element.68) | copy-start | bytes 388
  318.7 16.1 %copy-start.17 = (f32[32]{0:T(128)S(1)}, f32[32]{0:T(128)}, u32[]{:S(2)}) copy-start(f32[32]{0:T(128)} %get-tuple-element.69) | copy-start | bytes 388
  318.7 16.1 %copy-start.18 = (f32[32]{0:T(128)S(1)}, f32[32]{0:T(128)}, u32[]{:S(2)}) copy-start(f32[32]{0:T(128)} %get-tuple-element.70) | copy-start | bytes 388
  318.7 9.0 %collective-permute-start.15 = (bf16[40,2048]{1,0:T(8,128)(2,1)S(1)}, bf16[40,2048]{1,0:T(8,128)(2,1)S(1)}, u32[]{:S(2)}, u32[]{:S(2)}) collective-permute-start(bf16[40,2048]{1,0:T(8,128)(2,1)S(1)} %fusion.41), channel_id=1, source_target_pairs={{0,1},{1,0},{2,3},{3,2},{4,5},{5,4},{6,7},{7,6},{8,9},{9,8},{10,11... | collective-permute-start | bytes 491528 | tf_op jit(solution)/shard_map/ppermute | solution.py:43
  324.6 16.5 %copy-start.13 = (f32[32,512]{1,0:T(8,128)S(1)}, f32[32,512]{1,0:T(8,128)}, u32[]{:S(2)}) copy-start(f32[32,512]{1,0:T(8,128)} %get-tuple-element.57) | copy-start | bytes 196612
  324.6 18.9 %copy-start.12 = (f32[32,512]{1,0:T(8,128)S(1)}, f32[32,512]{1,0:T(8,128)}, u32[]{:S(2)}) copy-start(f32[32,512]{1,0:T(8,128)} %get-tuple-element.56) | copy-start | bytes 196612
  324.6 19.8 %copy-start.11 = (f32[32,512]{1,0:T(8,128)S(1)}, f32[32,512]{1,0:T(8,128)}, u32[]{:S(2)}) copy-start(f32[32,512]{1,0:T(8,128)} %get-tuple-element.55) | copy-start | bytes 196612
  324.6 3.9 %collective-permute-start.35 = (f32[40]{0:T(128)S(1)}, f32[40]{0:T(128)S(1)}, u32[]{:S(2)}, u32[]{:S(2)}) collective-permute-start(f32[40]{0:T(128)S(1)} %get-tuple-element.14), channel_id=1, source_target_pairs={{0,4},{4,0},{8,12},{12,8},{1,5},{5,1},{9,13},{13,9},{2,6},{6,2},{1... | collective-permute-start | bytes 488 | tf_op jit(solution)/shard_map/ppermute | solution.py:46
  324.7 3.9 %collective-permute-start.37 = (f32[40]{0:T(128)S(1)}, f32[40]{0:T(128)S(1)}, u32[]{:S(2)}, u32[]{:S(2)}) collective-permute-start(f32[40]{0:T(128)S(1)} %get-tuple-element.14), channel_id=1, source_target_pairs={{0,12},{4,8},{8,4},{12,0},{1,13},{5,9},{9,5},{13,1},{2,14},{6,10},... | collective-permute-start | bytes 488 | tf_op jit(solution)/shard_map/ppermute | solution.py:46
  327.7 3.5 collective-permute-start.36
  328.3 17.4 %copy-start.14 = (f32[16,512]{1,0:T(8,128)S(1)}, f32[16,512]{1,0:T(8,128)}, u32[]{:S(2)}) copy-start(f32[16,512]{1,0:T(8,128)} %get-tuple-element.58) | copy-start | bytes 98308
  328.4 19.2 %copy-start.8 = (f32[16,2048]{1,0:T(8,128)S(1)}, f32[16,2048]{1,0:T(8,128)}, u32[]{:S(2)}) copy-start(f32[16,2048]{1,0:T(8,128)} %copy-done.7) | copy-start | bytes 393220
  328.5 3.3 collective-permute-start.38
  328.6 4.8 %collective-permute-start.40 = (f32[40]{0:T(128)S(1)}, f32[40]{0:T(128)S(1)}, u32[]{:S(2)}, u32[]{:S(2)}) collective-permute-start(f32[40]{0:T(128)S(1)} %get-tuple-element.12), channel_id=1, source_target_pairs={{0,12},{4,8},{8,4},{12,0},{1,13},{5,9},{9,5},{13,1},{2,14},{6,10},... | collective-permute-start | bytes 488 | tf_op jit(solution)/shard_map/ppermute | solution.py:46
  331.2 3.5 collective-permute-start.39
  331.8 4.5 %collective-permute-start.9 = (f32[40,512]{1,0:T(8,128)S(1)}, f32[40,512]{1,0:T(8,128)S(1)}, u32[]{:S(2)}, u32[]{:S(2)}) collective-permute-start(f32[40,512]{1,0:T(8,128)S(1)} %get-tuple-element.54), channel_id=1, source_target_pairs={{0,8},{4,12},{8,0},{12,4},{1,9},{5,13},{9,1},{13,5},{2,10},{6,14},... | collective-permute-start | bytes 245768 | tf_op jit(solution)/shard_map/ppermute | solution.py:46
  333.4 5.3 %collective-permute-start.10 = (f32[40,512]{1,0:T(8,128)S(1)}, f32[40,512]{1,0:T(8,128)S(1)}, u32[]{:S(2)}, u32[]{:S(2)}) collective-permute-start(f32[40,512]{1,0:T(8,128)S(1)} %get-tuple-element.53), channel_id=1, source_target_pairs={{0,12},{4,8},{8,4},{12,0},{1,13},{5,9},{9,5},{13,1},{2,14},{6,10},... | collective-permute-start | bytes 245768 | tf_op jit(solution)/shard_map/ppermute | solution.py:46
  334.8 4.5 %collective-permute-start.8 = (f32[40,512]{1,0:T(8,128)S(1)}, f32[40,512]{1,0:T(8,128)S(1)}, u32[]{:S(2)}, u32[]{:S(2)}) collective-permute-start(f32[40,512]{1,0:T(8,128)S(1)} %get-tuple-element.52), channel_id=1, source_target_pairs={{0,4},{4,0},{8,12},{12,8},{1,5},{5,1},{9,13},{13,9},{2,6},{6,2},{1... | collective-permute-start | bytes 245768 | tf_op jit(solution)/shard_map/ppermute | solution.py:46
  336.3 4.8 %collective-permute-start.17 = (f32[40,512]{1,0:T(8,128)S(1)}, f32[40,512]{1,0:T(8,128)S(1)}, u32[]{:S(2)}, u32[]{:S(2)}) collective-permute-start(f32[40,512]{1,0:T(8,128)S(1)} %get-tuple-element.51), channel_id=1, source_target_pairs={{0,8},{4,12},{8,0},{12,4},{1,9},{5,13},{9,1},{13,5},{2,10},{6,14},... | collective-permute-start | bytes 245768 | tf_op jit(solution)/shard_map/ppermute | solution.py:46
  338.7 4.8 %collective-permute-start.18 = (f32[40,512]{1,0:T(8,128)S(1)}, f32[40,512]{1,0:T(8,128)S(1)}, u32[]{:S(2)}, u32[]{:S(2)}) collective-permute-start(f32[40,512]{1,0:T(8,128)S(1)} %get-tuple-element.50), channel_id=1, source_target_pairs={{0,12},{4,8},{8,4},{12,0},{1,13},{5,9},{9,5},{13,1},{2,14},{6,10},... | collective-permute-start | bytes 245768 | tf_op jit(solution)/shard_map/ppermute | solution.py:46
  339.3 5.1 %collective-permute-start.16 = (f32[40,512]{1,0:T(8,128)S(1)}, f32[40,512]{1,0:T(8,128)S(1)}, u32[]{:S(2)}, u32[]{:S(2)}) collective-permute-start(f32[40,512]{1,0:T(8,128)S(1)} %get-tuple-element.49), channel_id=1, source_target_pairs={{0,4},{4,0},{8,12},{12,8},{1,5},{5,1},{9,13},{13,9},{2,6},{6,2},{1... | collective-permute-start | bytes 245768 | tf_op jit(solution)/shard_map/ppermute | solution.py:46
  341.1 4.6 %collective-permute-start.25 = (f32[32,512]{1,0:T(8,128)S(1)}, f32[32,512]{1,0:T(8,128)S(1)}, u32[]{:S(2)}, u32[]{:S(2)}) collective-permute-start(f32[32,512]{1,0:T(8,128)S(1)} %copy-done.13), channel_id=1, source_target_pairs={{0,8},{4,12},{8,0},{12,4},{1,9},{5,13},{9,1},{13,5},{2,10},{6,14},... | collective-permute-start | bytes 196616 | tf_op jit(solution)/shard_map/ppermute | solution.py:46
  343.4 4.1 %collective-permute-start.26 = (f32[32,512]{1,0:T(8,128)S(1)}, f32[32,512]{1,0:T(8,128)S(1)}, u32[]{:S(2)}, u32[]{:S(2)}) collective-permute-start(f32[32,512]{1,0:T(8,128)S(1)} %copy-done.12), channel_id=1, source_target_pairs={{0,12},{4,8},{8,4},{12,0},{1,13},{5,9},{9,5},{13,1},{2,14},{6,10},... | collective-permute-start | bytes 196616 | tf_op jit(solution)/shard_map/ppermute | solution.py:46
  344.4 3.1 collective-permute-start.24
  345.7 2.0 collective-permute-start.32
  (8 other events, 35.0 us)
Sparse Core Ops, SparseCore 0:
  9.6 30.6 all-gather.10
  41.8 45.4 all-gather.8
  89.4 53.5 all-gather.4
  144.4 53.5 all-gather.6

commit v3 on v2

v3 whole, which is shorter than its diff:
```python
import jax
import jax.numpy as jnp
from jax import lax
from jax.sharding import PartitionSpec as P

LAST_ROWS = 128

F32 = jnp.float32
BF16 = jnp.bfloat16


def dot_t(a, b):
    return lax.dot_general(a, b, (((1,), (1,)), ((), ())), preferred_element_type=F32)


def selection_counts(chosen_ids, first_row, rows):
    row_ids = first_row + lax.broadcasted_iota(jnp.int32, (rows, chosen_ids.shape[0]), 0)
    ids = chosen_ids.T
    counts = jnp.zeros(row_ids.shape, F32)
    for k in range(ids.shape[0]):
        counts = counts + (row_ids == ids[k][None, :]).astype(F32)
    return counts


def any_mesh(train_grads, test_grads, fisher, chosen_ids):
    test_whole = lax.all_gather(test_grads, "test", axis=0, tiled=True)
    partial_value = jnp.dot(test_whole, fisher, preferred_element_type=F32)
    precond = lax.psum(partial_value, "train").astype(BF16)
    partial_scores = dot_t(train_grads, precond)
    scores = lax.psum_scatter(partial_scores, "test", scatter_dimension=1, tiled=True)
    rows = scores.shape[0]
    counts = selection_counts(chosen_ids, lax.axis_index("train") * rows, rows)
    return scores, lax.psum(jnp.sum(counts * scores, axis=0), "train")


def four_by_four(train_grads, test_grads, fisher, chosen_ids):
    z = lax.axis_index("test")
    i = lax.axis_index("train")
    chip, core = i // 2, i % 2
    inner = (z == 1) | (z == 2)
    own_rows = train_grads.shape[0]
    queries = test_grads.shape[0]
    pieces = ((0, queries - LAST_ROWS), (queries - LAST_ROWS, LAST_ROWS))

    def along(value, pairs):
        return lax.ppermute(value, "test", pairs)

    def scores_along(value, pairs):
        return along(value.astype(BF16), pairs).astype(F32)

    def to_other(value, r):
        return lax.ppermute(value, "train", [(k, k ^ r) for k in range(4)])

    def tied(*values):
        return lax.optimization_barrier(values)

    pair = [(0, 1), (1, 0), (2, 3), (3, 2)]
    middle = [(1, 2), (2, 1)]
    outward = [(1, 0), (2, 3)]
    far_pairs = [(0, 3), (3, 0), (1, 2), (2, 1)]

    def portion(value, cuts, which, of):
        return jnp.concatenate(
            [
                lax.dynamic_slice_in_dim(value, first + which * (rows // of), rows // of)
                for first, rows in cuts
            ]
        )

    def cut(sizes):
        return [(sum(sizes[:p]), sizes[p]) for p in range(len(sizes))]

    def core_sum(block, sizes):
        part = jnp.dot(block, fisher, preferred_element_type=F32)
        sent = to_other(portion(part, cut(sizes), 1 - core, 2), 1)
        return portion(part, cut(sizes), core, 2) + sent

    def chip_sum(part, sizes):
        halves = cut([rows // 2 for rows in sizes])
        sent = to_other(portion(part, halves, 1 - chip, 2), 2)
        return (portion(part, halves, chip, 2) + sent).astype(BF16)

    whole = [rows for _, rows in pieces]

    near = along(test_grads, pair)
    third = along(test_grads, middle)
    grads = [train_grads, to_other(train_grads, 1), to_other(train_grads, 2)]
    own_part = core_sum(test_grads, whole)
    near, third, grads, own_part = tied(near, third, grads, own_part)

    second_in = along(near, middle)
    second_edge = along(third, outward)
    own_precond = chip_sum(own_part, whole)
    grads = jnp.concatenate(grads + [to_other(grads[2], 1)])
    near_precond = chip_sum(core_sum(near, whole), whole)
    own = dot_t(own_precond, grads)
    near = dot_t(near_precond, grads)
    second_in, second_edge, own, near, grads = tied(second_in, second_edge, own, near, grads)

    last_in = second_in[pieces[1][0] :]
    first_edge = along(second_in[: pieces[0][1]], outward)
    second = jnp.where(inner, second_in, second_edge)
    second = dot_t(chip_sum(core_sum(second, whole), whole), grads)
    total = own + scores_along(second, [(0, 2), (3, 1)])
    near = near + scores_along(second, middle)
    total = total + scores_along(near, pair)
    first_edge, last_in, total = tied(first_edge, last_in, total)
    last_edge = along(last_in, outward)

    blocks = jnp.stack([i, i ^ 1, i ^ 2, i ^ 3])
    row_ids = (blocks[:, None] * own_rows + jnp.arange(own_rows)[None, :]).reshape(1, 1, -1)

    outs = []
    edges = (first_edge, last_edge)
    for (first, rows), edge in zip(pieces, edges):
        quarter = rows // 4
        block = jnp.where(inner, third[first : first + rows], edge)
        value = dot_t(chip_sum(core_sum(block, [rows]), [rows]), grads)
        value = total[first // 4 : first // 4 + quarter] + scores_along(value, far_pairs)
        ids = lax.dynamic_slice_in_dim(chosen_ids, first + (core * 2 + chip) * quarter, quarter)
        counts = jnp.sum((ids[:, :, None] == row_ids).astype(F32), axis=1)
        chosen = jnp.sum(counts * value, axis=1, keepdims=True)
        parts = [value[:, r * own_rows : (r + 1) * own_rows] for r in range(4)]
        parts = [jnp.pad(part, ((0, 0), (0, 128))) for part in parts]
        column = lax.broadcasted_iota(jnp.int32, parts[0].shape, 1)
        parts = [jnp.where(column < own_rows, part, chosen) for part in parts]
        got = [parts[0]] + [to_other(parts[r], r) for r in range(1, 4)]
        got = [got[0], got[2], got[1], got[3]]
        got = [jnp.where(chip == 0, got[q], got[q ^ 1]) for q in range(4)]
        outs += [jnp.where(core == 0, got[q], got[q ^ 2]) for q in range(4)]
    turned = jnp.concatenate(outs).T
    return turned[:own_rows], turned[own_rows]


def solution(mesh):
    sizes = (mesh.shape["train"], mesh.shape["test"])
    return jax.shard_map(
        four_by_four if sizes == (4, 4) else any_mesh,
        mesh=mesh,
        in_specs=(
            P(("groups", "train"), "test"),
            P(("groups", "test"), "train"),
            P("train", "test"),
            P(("groups", "test"), None),
        ),
        out_specs=(P(("groups", "train"), "test"), P(("groups", "test"))),
        check_vma=False,
    )
```

time: 359 us -> 308 us (0.86); the launches traced: 359 us -> 304 us
  waiting for transfers between devices: 186 us -> 171 us
  between operations: 14.7 us -> 1.37 us
  other arithmetic: 24.5 us -> 14.6 us
  starting transfers between devices: 59.4 us -> 52 us
  matrix products: 54 us -> 48.4 us
  local copies, waits for them, and re-layouts: 20.1 us -> 15.8 us
    all_gather x4 -> x0, waiting for transfers between devices: 126 us -> none  [four_by_four(): block = lax.all_gather(relative, 'test', axis=0, tiled=True)]
    ppermute x12 -> x11, waiting for transfers between devices: 15.2 us -> 80.9 us  [along(): return lax.ppermute(value, 'test', pairs)]
    ppermute x35 -> x19, waiting for transfers between devices: 45.1 us -> 90.5 us  [to_other(): return lax.ppermute(value, 'train', [(k, k ^ r) for k in range(4)])]
    ppermute x35 -> x19, starting transfers between devices: 27.5 us -> 11.7 us  [to_other(): return lax.ppermute(value, 'train', [(k, k ^ r) for k in range(4)])]
    ppermute x12 -> x11, starting transfers between devices: 31.7 us -> 40.3 us  [along(): return lax.ppermute(value, 'test', pairs)]
    dynamic_slice x0 -> x20, local copies, waits for them, and re-layouts: none -> 8.04 us  [the longest x16 7.71 us: portion(): lax.dynamic_slice_in_dim(value, first + which * (rows // of), rows // of)]
    unnamed x47 -> x51, local copies, waits for them, and re-layouts: 11.6 us -> 5.28 us
    dot_general x4 -> x5, matrix products: 22.8 us -> 18.2 us  [dot_t(): lax.dot_general(a, b, (((1,), (1,)), ((), ())), preferred_element_type=F32)]
  transfers between devices with their start and end apart: 51 -> 30, of which waited for: 22 -> 16; matrix products, arithmetic and copies ran while one was open for 25% -> 13% of each run, Pallas kernels for 0% -> 0%
where the time goes in v3:
time: 308 us; the launch traced here: 304 us
  waiting for transfers between devices  171 us (56%)
  starting transfers between devices  52 us (17%)
  matrix products  48.4 us (16%)
  local copies, waits for them, and re-layouts  15.8 us (5%)
  other arithmetic  14.6 us (5%)
    ppermute x19, waiting for transfers between devices, to_other(): return lax.ppermute(value, 'train', [(k, k ^ r) for k in range(4)])  90.5 us
    ppermute x11, waiting for transfers between devices, along(): return lax.ppermute(value, 'test', pairs)  80.9 us
    ppermute x11, starting transfers between devices, along(): return lax.ppermute(value, 'test', pairs)  40.3 us
    dot_general x5, matrix products, core_sum(): part = jnp.dot(block, fisher, preferred_element_type=F32)  30.2 us
    dot_general x5, matrix products, dot_t(): lax.dot_general(a, b, (((1,), (1,)), ((), ())), preferred_element_type=F32)  18.2 us
    ppermute x19, starting transfers between devices, to_other(): return lax.ppermute(value, 'train', [(k, k ^ r) for k in range(4)])  11.7 us
    dynamic_slice x16, local copies, waits for them, and re-layouts, portion(): lax.dynamic_slice_in_dim(value, first + which * (rows // of), rows // of)  7.71 us
  transfers between devices with their start and end apart: 30, of which 16 were waited for; matrix products, arithmetic and copies ran while one was open for 13% of the time, Pallas kernels for 0%

profile of v3, /device:TPU:0, one launch (start us, length us, event | category | flops | bytes accessed | tf_op | source)
XLA Modules:
  0.0 303.5 jit_solution(1327599424095021336)
XLA Ops:
  0.7 10.5 %fusion.32 = f32[512,2048]{1,0:T(8,128)} fusion(bf16[512,2048]{1,0:T(8,128)(2,1)} %param.5, bf16[2048,2048]{1,0:T(8,128)(2,1)} %param.6), kind=kOutput, calls=%fused_computation.114 | convolution fusion | flops 4294967296 | bytes 14680064 | tf_op jit(solution)/shard_map/dot_general | solution.py:74
  11.2 2.3 constant_dynamic-slice_fusion.29
  13.5 1.4 constant_dynamic-slice_fusion.28
  15.6 2.8 collective-permute-start
  18.4 2.0 collective-permute-start.1
  20.5 1.5 collective-permute-start.3
  22.3 42.3 %collective-permute-done = bf16[512,2048]{1,0:T(8,128)(2,1)S(1)} collective-permute-done((bf16[512,2048]{1,0:T(8,128)(2,1)S(1)}, bf16[512,2048]{1,0:T(8,128)(2,1)S(1)}, u32[]{:S(2)}, u32[]{:S(2)}) %collective-permute-start) | collective-permute-done | bytes 2097184 | tf_op jit(solution)/shard_map/ppermute | solution.py:46
  64.5 3.9 %collective-permute-done.3 = bf16[512,2048]{1,0:T(8,128)(2,1)S(1)} collective-permute-done((bf16[512,2048]{1,0:T(8,128)(2,1)S(1)}, bf16[512,2048]{1,0:T(8,128)(2,1)S(1)}, u32[]{:S(2)}, u32[]{:S(2)}) %collective-permute-start.3) | collective-permute-done | bytes 2097184 | tf_op jit(solution)/shard_map/ppermute | solution.py:52
  68.5 4.5 %fusion.33 = f32[512,2048]{1,0:T(8,128)S(1)} fusion(bf16[512,2048]{1,0:T(8,128)(2,1)S(1)} %collective-permute-done, bf16[2048,2048]{1,0:T(8,128)(2,1)S(1)} %bitcast.23), kind=kOutput, calls=%fused_computation.115 | convolution fusion | flops 4294967296 | bytes 14680064 | tf_op jit(solution)/shard_map/dot_general | solution.py:74
  73.0 1.4 constant_dynamic-slice_fusion.21
  74.5 1.4 pad_maximum_fusion.1
  76.0 0.8 collective-permute-start.5
  76.8 0.6 collective-permute-start.8
  77.6 1.6 collective-permute-start.7
  79.2 1.5 collective-permute-start.6
  81.1 1.2 copy-done.2
  82.3 1.9 maximum_add_fusion.1
  84.5 0.7 collective-permute-start.10
  85.3 0.7 copy-done.9
  86.4 17.3 %collective-permute-done.7 = f32[128,2048]{1,0:T(8,128)S(1)} collective-permute-done((f32[128,2048]{1,0:T(8,128)S(1)}, f32[128,2048]{1,0:T(8,128)S(1)}, u32[]{:S(2)}, u32[]{:S(2)}) %collective-permute-start.7) | collective-permute-done | bytes 1048608 | tf_op jit(solution)/shard_map/ppermute | solution.py:52
  103.7 2.9 fusion.13
  106.6 18.7 %collective-permute-done.10 = f32[128,2048]{1,0:T(8,128)S(1)} collective-permute-done((f32[128,2048]{1,0:T(8,128)S(1)}, f32[128,2048]{1,0:T(8,128)S(1)}, u32[]{:S(2)}, u32[]{:S(2)}) %collective-permute-start.10) | collective-permute-done | bytes 1048608 | tf_op jit(solution)/shard_map/ppermute | solution.py:52
  125.3 2.9 fusion.11
  128.2 1.4 copy-done.4
  129.6 1.0 collective-permute-done.6
  130.6 5.9 %fusion = f32[512,2048]{1,0:T(8,128)S(1)} fusion(bf16[2048,2048]{1,0:T(8,128)(2,1)S(1)} %bitcast.25, bf16[512,2048]{1,0:T(8,128)(2,1)} %copy-done.4, bf16[512,2048]{1,0:T(8,128)(2,1)} %collective-permute-done.6, pred[]{:T(512)S(6)} %or.3), kind=kOutput, calls=%fused_computation.11 | convolution fusion | flops 4296015872 | bytes 16777216 | tf_op jit(solution)/shard_map/dot_general | solution.py:74
  137.2 4.1 %collective-permute-done.12 = f32[256,2048]{1,0:T(8,128)S(1)} collective-permute-done((f32[256,2048]{1,0:T(8,128)S(1)}, f32[256,2048]{1,0:T(8,128)S(1)}, u32[]{:S(2)}, u32[]{:S(2)}) %collective-permute-start.12) | collective-permute-done | bytes 2097184 | tf_op jit(solution)/shard_map/ppermute | solution.py:52
  142.0 0.7 collective-permute-start.13
  142.7 24.5 %collective-permute-done.13 = f32[128,2048]{1,0:T(8,128)S(1)} collective-permute-done((f32[128,2048]{1,0:T(8,128)S(1)}, f32[128,2048]{1,0:T(8,128)S(1)}, u32[]{:S(2)}, u32[]{:S(2)}) %collective-permute-start.13) | collective-permute-done | bytes 1048608 | tf_op jit(solution)/shard_map/ppermute | solution.py:52
  167.2 3.7 %convolution_convert_fusion = bf16[128,2048]{1,0:T(8,128)(2,1)} fusion(bf16[2048,2048]{1,0:T(8,128)(2,1)S(1)} %constant_dynamic-update-slice_fusion, f32[128,2048]{1,0:T(8,128)S(1)} %collective-permute-done.13, f32[32,2048]{1,0:T(8,128)S(1)} %get-tuple-element.54, f32[96,2048]{1,0:T(8,128)S(1)} %get-tuple-element.52), kind=kOutput, calls=%fused_computation.2 | convolution fusion | flops 1074790400 | bytes 11010048 | tf_op jit(solution)/shard_map/dot_general | solution.py:13
  170.9 0.7 collective-permute-start.15
  171.6 1.3 slice.50
  172.9 1.3 collective-permute-start.11
  174.2 9.8 %collective-permute-start.14 = (bf16[128,2048]{1,0:T(8,128)(2,1)}, bf16[128,2048]{1,0:T(8,128)(2,1)}, u32[]{:S(2)}, u32[]{:S(2)}) collective-permute-start(bf16[128,2048]{1,0:T(8,128)(2,1)} %convolution_convert_fusion), channel_id=1, source_target_pairs={{0,2},{3,1},{4,6},{7,5},{8,10},{11,9},{12,14},{15,13},{16,18},{19,... | collective-permute-start | bytes 1572872 | tf_op jit(solution)/shard_map/ppermute | solution.py:46
  184.0 0.9 add_convert_fusion
  184.9 16.9 %collective-permute-start.16 = (bf16[128,2048]{1,0:T(8,128)(2,1)}, bf16[128,2048]{1,0:T(8,128)(2,1)}, u32[]{:S(2)}, u32[]{:S(2)}) collective-permute-start(bf16[128,2048]{1,0:T(8,128)(2,1)} %add_convert_fusion), channel_id=1, source_target_pairs={{0,1},{1,0},{2,3},{3,2},{4,5},{5,4},{6,7},{7,6},{8,9},{9,8},{10,11... | collective-permute-start | bytes 1572872 | tf_op jit(solution)/shard_map/ppermute | solution.py:46
  201.8 23.9 %collective-permute-done.16 = bf16[128,2048]{1,0:T(8,128)(2,1)} collective-permute-done((bf16[128,2048]{1,0:T(8,128)(2,1)}, bf16[128,2048]{1,0:T(8,128)(2,1)}, u32[]{:S(2)}, u32[]{:S(2)}) %collective-permute-start.16) | collective-permute-done | bytes 524320 | tf_op jit(solution)/shard_map/ppermute | solution.py:46
  225.8 1.5 convert_add_fusion
  227.3 1.6 collective-permute-start.23
  228.9 7.0 %fusion.3 = f32[384,2048]{1,0:T(8,128)S(1)} fusion(bf16[2048,2048]{1,0:T(8,128)(2,1)} %param.6, bf16[384,2048]{1,0:T(8,128)(2,1)} %collective-permute-done.11, bf16[512,2048]{1,0:T(8,128)(2,1)} %collective-permute-done.1, pred[]{:T(512)S(6)} %or.3), kind=kOutput, calls=%fused_computation.15 | convolution fusion | flops 3222011904 | bytes 14680065 | tf_op jit(solution)/shard_map/dot_general | solution.py:74
  235.9 1.4 constant_dynamic-slice_fusion.5
  237.3 4.3 %collective-permute-done.23 = bf16[128,2048]{1,0:T(8,128)(2,1)S(1)} collective-permute-done((bf16[128,2048]{1,0:T(8,128)(2,1)S(1)}, bf16[128,2048]{1,0:T(8,128)(2,1)S(1)}, u32[]{:S(2)}, u32[]{:S(2)}) %collective-permute-start.23) | collective-permute-done | bytes 524320 | tf_op jit(solution)/shard_map/ppermute | solution.py:46
  241.7 2.3 fusion.15
  244.7 1.4 collective-permute-done.24
  246.1 1.6 collective-permute-start.25
  247.7 2.2 dynamic-slice_add_fusion
  250.0 0.6 collective-permute-start.18
  250.6 2.6 convert_reduce_fusion
  253.2 2.1 collective-permute-done.25
  255.4 6.1 %convolution_convert_fusion.2 = bf16[32,2048]{1,0:T(8,128)(2,1)S(1)} fusion(bf16[2048,2048]{1,0:T(8,128)(2,1)} %copy-done.1, f32[32,2048]{1,0:T(8,128)S(1)} %collective-permute-done.25, f32[64,2048]{1,0:T(8,128)S(1)} %dynamic-slice_add_fusion.1, s32[]{:T(128)S(6)} %select_n.246), kind=kOutput, calls=%fused_computation.4 | convolution fusion | flops 268632064 | bytes 9043972 | tf_op jit(solution)/shard_map/dot_general | solution.py:13
  261.4 1.5 collective-permute-start.26
  262.9 8.5 %collective-permute-done.18 = f32[96,2048]{1,0:T(8,128)S(1)} collective-permute-done((f32[96,2048]{1,0:T(8,128)S(1)}, f32[96,2048]{1,0:T(8,128)S(1)}, u32[]{:S(2)}, u32[]{:S(2)}) %collective-permute-start.18) | collective-permute-done | bytes 786464 | tf_op jit(solution)/shard_map/ppermute | solution.py:52
  271.4 2.7 convolution_convert_fusion.1
  274.1 1.5 collective-permute-start.19
  275.6 1.3 convert_reduce_fusion.1
  277.1 9.3 %collective-permute-done.19 = bf16[96,2048]{1,0:T(8,128)(2,1)S(1)} collective-permute-done((bf16[96,2048]{1,0:T(8,128)(2,1)S(1)}, bf16[96,2048]{1,0:T(8,128)(2,1)S(1)}, u32[]{:S(2)}, u32[]{:S(2)}) %collective-permute-start.19) | collective-permute-done | bytes 393248 | tf_op jit(solution)/shard_map/ppermute | solution.py:46
  286.8 1.6 collective-permute-start.20
  288.4 0.6 collective-permute-start.22
  289.1 1.6 collective-permute-start.27
  290.7 4.1 %collective-permute-done.20 = f32[96,640]{1,0:T(8,128)S(1)} collective-permute-done((f32[96,640]{1,0:T(8,128)S(1)}, f32[96,640]{1,0:T(8,128)S(1)}, u32[]{:S(2)}, u32[]{:S(2)}) %collective-permute-start.20) | collective-permute-done | bytes 245792 | tf_op jit(solution)/shard_map/ppermute | solution.py:52
  294.8 3.9 %collective-permute-done.22 = f32[96,640]{1,0:T(8,128)S(1)} collective-permute-done((f32[96,640]{1,0:T(8,128)S(1)}, f32[96,640]{1,0:T(8,128)S(1)}, u32[]{:S(2)}, u32[]{:S(2)}) %collective-permute-start.22) | collective-permute-done | bytes 245792 | tf_op jit(solution)/shard_map/ppermute | solution.py:52
  299.2 1.8 collective-permute-done.27
  301.5 0.7 slice_reduce_fusion
  302.2 1.3 copy.14
  (118 shorter events, 6.0 us)
Async XLA Ops:
  0.6 243.5 %copy-start = (s32[512,16]{0,1:T(8,128)S(1)}, s32[512,16]{0,1:T(8,128)}, u32[]{:S(2)}) copy-start(s32[512,16]{0,1:T(8,128)} %param.7) | copy-start | bytes 98308
  11.2 57.3 %slice-start.2 = ((s8[8388608]{0:T(1024)(128)(4,1)}), s8[4194304]{0:T(1024)(128)(4,1)S(1)}, s32[]{:S(2)}) async-start(s8[8388608]{0:T(1024)(128)(4,1)} %bitcast.22), calls=%async_computation.2 | async-start | bytes 8388608
  13.5 2.1 copy-start.13
  13.5 6.9 %copy-start.6 = (bf16[512,2048]{1,0:T(8,128)(2,1)S(1)}, bf16[512,2048]{1,0:T(8,128)(2,1)}, u32[]{:S(2)}) copy-start(bf16[512,2048]{1,0:T(8,128)(2,1)} %param.4) | copy-start | bytes 6291460
  15.0 53.5 %slice-start.3 = ((s8[8388608]{0:T(1024)(128)(4,1)}), s8[4194304]{0:T(1024)(128)(4,1)S(1)}, s32[]{:S(2)}) async-start(s8[8388608]{0:T(1024)(128)(4,1)} %bitcast.22), calls=%async_computation.3 | async-start | bytes 8388608
  15.1 6.8 %collective-permute-start.4 = (f32[256,2048]{1,0:T(8,128)S(1)}, f32[256,2048]{1,0:T(8,128)S(1)}, u32[]{:S(2)}, u32[]{:S(2)}) collective-permute-start(f32[256,2048]{1,0:T(8,128)S(1)} %pad_maximum_fusion), channel_id=1, source_target_pairs={{0,4},{4,0},{8,12},{12,8},{1,5},{5,1},{9,13},{13,9},{2,6},{6,2},{1... | collective-permute-start | bytes 6291464 | tf_op jit(solution)/shard_map/ppermute | solution.py:52
  15.6 48.9 %collective-permute-start = (bf16[512,2048]{1,0:T(8,128)(2,1)S(1)}, bf16[512,2048]{1,0:T(8,128)(2,1)S(1)}, u32[]{:S(2)}, u32[]{:S(2)}) collective-permute-start(bf16[512,2048]{1,0:T(8,128)(2,1)S(1)} %copy-done.13), channel_id=1, source_target_pairs={{0,1},{1,0},{2,3},{3,2},{4,5},{5,4},{6,7},{7,6},{8,9},{9,8},{10,11... | collective-permute-start | bytes 6291464 | tf_op jit(solution)/shard_map/ppermute | solution.py:46
  18.4 46.1 %collective-permute-start.1 = (bf16[512,2048]{1,0:T(8,128)(2,1)S(1)}, bf16[512,2048]{1,0:T(8,128)(2,1)}, u32[]{:S(2)}, u32[]{:S(2)}) collective-permute-start(bf16[512,2048]{1,0:T(8,128)(2,1)S(1)} %copy-done.13), channel_id=1, source_target_pairs={{1,2},{2,1},{5,6},{6,5},{9,10},{10,9},{13,14},{14,13},{17,18},{18,... | collective-permute-start | bytes 6291464 | tf_op jit(solution)/shard_map/ppermute | solution.py:46
  20.4 44.1 %collective-permute-start.2 = (bf16[512,2048]{1,0:T(8,128)(2,1)S(1)}, bf16[512,2048]{1,0:T(8,128)(2,1)S(1)}, u32[]{:S(2)}, u32[]{:S(2)}) collective-permute-start(bf16[512,2048]{1,0:T(8,128)(2,1)S(1)} %copy-done.6), channel_id=1, source_target_pairs={{0,4},{4,0},{8,12},{12,8},{1,5},{5,1},{9,13},{13,9},{2,6},{6,2},{1... | collective-permute-start | bytes 6291464 | tf_op jit(solution)/shard_map/ppermute | solution.py:52
  20.5 48.0 %collective-permute-start.3 = (bf16[512,2048]{1,0:T(8,128)(2,1)S(1)}, bf16[512,2048]{1,0:T(8,128)(2,1)S(1)}, u32[]{:S(2)}, u32[]{:S(2)}) collective-permute-start(bf16[512,2048]{1,0:T(8,128)(2,1)S(1)} %copy-done.6), channel_id=1, source_target_pairs={{0,8},{4,12},{8,0},{12,4},{1,9},{5,13},{9,1},{13,5},{2,10},{6,14},... | collective-permute-start | bytes 6291464 | tf_op jit(solution)/shard_map/ppermute | solution.py:52
  64.5 8.5 %copy-start.14 = (bf16[512,2048]{1,0:T(8,128)(2,1)}, bf16[512,2048]{1,0:T(8,128)(2,1)S(1)}, u32[]{:S(2)}) copy-start(bf16[512,2048]{1,0:T(8,128)(2,1)S(1)} %collective-permute-done) | copy-start | bytes 6291460
  64.5 8.5 %copy-start.10 = (bf16[512,2048]{1,0:T(8,128)(2,1)}, bf16[512,2048]{1,0:T(8,128)(2,1)S(1)}, u32[]{:S(2)}) copy-start(bf16[512,2048]{1,0:T(8,128)(2,1)S(1)} %collective-permute-done.2) | copy-start | bytes 6291460
  68.5 4.5 %copy-start.8 = (bf16[512,2048]{1,0:T(8,128)(2,1)}, bf16[512,2048]{1,0:T(8,128)(2,1)S(1)}, u32[]{:S(2)}) copy-start(bf16[512,2048]{1,0:T(8,128)(2,1)S(1)} %collective-permute-done.3) | copy-start | bytes 6291460
  76.0 5.1 %collective-permute-start.9 = (f32[256,2048]{1,0:T(8,128)}, f32[256,2048]{1,0:T(8,128)}, u32[]{:S(2)}, u32[]{:S(2)}) collective-permute-start(f32[256,2048]{1,0:T(8,128)} %pad_maximum_fusion.1), channel_id=1, source_target_pairs={{0,4},{4,0},{8,12},{12,8},{1,5},{5,1},{9,13},{13,9},{2,6},{6,2},{1... | collective-permute-start | bytes 6291464 | tf_op jit(solution)/shard_map/ppermute | solution.py:52
  76.0 52.2 %collective-permute-start.5 = (bf16[512,2048]{1,0:T(8,128)(2,1)}, bf16[512,2048]{1,0:T(8,128)(2,1)S(1)}, u32[]{:S(2)}, u32[]{:S(2)}) collective-permute-start(bf16[512,2048]{1,0:T(8,128)(2,1)} %copy-done.14), channel_id=1, source_target_pairs={{1,2},{2,1},{5,6},{6,5},{9,10},{10,9},{13,14},{14,13},{17,18},{18,... | collective-permute-start | bytes 6291464 | tf_op jit(solution)/shard_map/ppermute | solution.py:46
  76.8 9.3 %collective-permute-start.8 = (bf16[512,2048]{1,0:T(8,128)(2,1)}, bf16[512,2048]{1,0:T(8,128)(2,1)S(1)}, u32[]{:S(2)}, u32[]{:S(2)}) collective-permute-start(bf16[512,2048]{1,0:T(8,128)(2,1)} %copy-done.8), channel_id=1, source_target_pairs={{0,4},{4,0},{8,12},{12,8},{1,5},{5,1},{9,13},{13,9},{2,6},{6,2},{1... | collective-permute-start | bytes 6291464 | tf_op jit(solution)/shard_map/ppermute | solution.py:52
  77.4 3.3 %copy-start.7 = (bf16[512,2048]{1,0:T(8,128)(2,1)S(1)}, bf16[512,2048]{1,0:T(8,128)(2,1)}, u32[]{:S(2)}) copy-start(bf16[512,2048]{1,0:T(8,128)(2,1)} %param.4) | copy-start | bytes 6291460
  77.6 3.3 %copy-start.11 = (bf16[512,2048]{1,0:T(8,128)(2,1)S(1)}, bf16[512,2048]{1,0:T(8,128)(2,1)}, u32[]{:S(2)}) copy-start(bf16[512,2048]{1,0:T(8,128)(2,1)} %copy-done.10) | copy-start | bytes 6291460
  77.6 26.1 %collective-permute-start.7 = (f32[128,2048]{1,0:T(8,128)S(1)}, f32[128,2048]{1,0:T(8,128)S(1)}, u32[]{:S(2)}, u32[]{:S(2)}) collective-permute-start(f32[128,2048]{1,0:T(8,128)S(1)} %pad_maximum_fusion.3), channel_id=1, source_target_pairs={{0,8},{4,12},{8,0},{12,4},{1,9},{5,13},{9,1},{13,5},{2,10},{6,14},... | collective-permute-start | bytes 3145736 | tf_op jit(solution)/shard_map/ppermute | solution.py:52
  79.2 51.4 %collective-permute-start.6 = (bf16[512,2048]{1,0:T(8,128)(2,1)}, bf16[512,2048]{1,0:T(8,128)(2,1)}, u32[]{:S(2)}, u32[]{:S(2)}) collective-permute-start(bf16[512,2048]{1,0:T(8,128)(2,1)} %collective-permute-done.1), channel_id=1, source_target_pairs={{1,0},{2,3},{5,4},{6,7},{9,8},{10,11},{13,12},{14,15},{17,16},{18,... | collective-permute-start | bytes 6291464 | tf_op jit(solution)/shard_map/ppermute | solution.py:46
  80.9 1.4 copy-start.2
  84.4 1.6 copy-start.9
  84.5 40.7 %collective-permute-start.10 = (f32[128,2048]{1,0:T(8,128)S(1)}, f32[128,2048]{1,0:T(8,128)S(1)}, u32[]{:S(2)}, u32[]{:S(2)}) collective-permute-start(f32[128,2048]{1,0:T(8,128)S(1)} %pad_maximum_fusion.4), channel_id=1, source_target_pairs={{0,8},{4,12},{8,0},{12,4},{1,9},{5,13},{9,1},{13,5},{2,10},{6,14},... | collective-permute-start | bytes 3145736 | tf_op jit(solution)/shard_map/ppermute | solution.py:52
  86.4 80.8 %copy-start.1 = (bf16[2048,2048]{1,0:T(8,128)(2,1)}, bf16[2048,2048]{1,0:T(8,128)(2,1)S(1)}, u32[]{:S(2)}) copy-start(bf16[2048,2048]{1,0:T(8,128)(2,1)S(1)} %constant_dynamic-update-slice_fusion) | copy-start | bytes 25165828
  103.7 26.9 %slice-start.4 = ((s8[8388608]{0:T(1024)(128)(4,1)}), s8[4194304]{0:T(1024)(128)(4,1)S(1)}, s32[]{:S(2)}) async-start(s8[8388608]{0:T(1024)(128)(4,1)} %bitcast.24), calls=%async_computation.4 | async-start | bytes 8388608
  125.3 5.3 %slice-start.5 = ((s8[8388608]{0:T(1024)(128)(4,1)}), s8[4194304]{0:T(1024)(128)(4,1)S(1)}, s32[]{:S(2)}) async-start(s8[8388608]{0:T(1024)(128)(4,1)} %bitcast.24), calls=%async_computation.5 | async-start | bytes 8388608
  128.2 1.4 copy-start.4
  137.1 4.2 %collective-permute-start.12 = (f32[256,2048]{1,0:T(8,128)S(1)}, f32[256,2048]{1,0:T(8,128)S(1)}, u32[]{:S(2)}, u32[]{:S(2)}) collective-permute-start(f32[256,2048]{1,0:T(8,128)S(1)} %pad_maximum_fusion.2), channel_id=1, source_target_pairs={{0,4},{4,0},{8,12},{12,8},{1,5},{5,1},{9,13},{13,9},{2,6},{6,2},{1... | collective-permute-start | bytes 6291464 | tf_op jit(solution)/shard_map/ppermute | solution.py:52
  142.0 25.3 %collective-permute-start.13 = (f32[128,2048]{1,0:T(8,128)S(1)}, f32[128,2048]{1,0:T(8,128)S(1)}, u32[]{:S(2)}, u32[]{:S(2)}) collective-permute-start(f32[128,2048]{1,0:T(8,128)S(1)} %pad_maximum_fusion.5), channel_id=1, source_target_pairs={{0,8},{4,12},{8,0},{12,4},{1,9},{5,13},{9,1},{13,5},{2,10},{6,14},... | collective-permute-start | bytes 3145736 | tf_op jit(solution)/shard_map/ppermute | solution.py:52
  167.2 4.4 %copy-start.5 = (bf16[512,2048]{1,0:T(8,128)(2,1)S(1)}, bf16[512,2048]{1,0:T(8,128)(2,1)}, u32[]{:S(2)}) copy-start(bf16[512,2048]{1,0:T(8,128)(2,1)} %copy-done.4) | copy-start | bytes 6291460
  170.9 13.1 %collective-permute-start.15 = (bf16[128,2048]{1,0:T(8,128)(2,1)}, bf16[128,2048]{1,0:T(8,128)(2,1)S(1)}, u32[]{:S(2)}, u32[]{:S(2)}) collective-permute-start(bf16[128,2048]{1,0:T(8,128)(2,1)} %convolution_convert_fusion), channel_id=1, source_target_pairs={{1,2},{2,1},{5,6},{6,5},{9,10},{10,9},{13,14},{14,13},{17,18},{18,... | collective-permute-start | bytes 1572872 | tf_op jit(solution)/shard_map/ppermute | solution.py:46
  172.9 54.4 %collective-permute-start.11 = (bf16[384,2048]{1,0:T(8,128)(2,1)}, bf16[384,2048]{1,0:T(8,128)(2,1)}, u32[]{:S(2)}, u32[]{:S(2)}) collective-permute-start(bf16[384,2048]{1,0:T(8,128)(2,1)} %slice.50), channel_id=1, source_target_pairs={{1,0},{2,3},{5,4},{6,7},{9,8},{10,11},{13,12},{14,15},{17,16},{18,... | collective-permute-start | bytes 4718600 | tf_op jit(solution)/shard_map/ppermute | solution.py:46
  174.2 27.6 %collective-permute-start.14 = (bf16[128,2048]{1,0:T(8,128)(2,1)}, bf16[128,2048]{1,0:T(8,128)(2,1)}, u32[]{:S(2)}, u32[]{:S(2)}) collective-permute-start(bf16[128,2048]{1,0:T(8,128)(2,1)} %convolution_convert_fusion), channel_id=1, source_target_pairs={{0,2},{3,1},{4,6},{7,5},{8,10},{11,9},{12,14},{15,13},{16,18},{19,... | collective-permute-start | bytes 1572872 | tf_op jit(solution)/shard_map/ppermute | solution.py:46
  184.9 40.9 %collective-permute-start.16 = (bf16[128,2048]{1,0:T(8,128)(2,1)}, bf16[128,2048]{1,0:T(8,128)(2,1)}, u32[]{:S(2)}, u32[]{:S(2)}) collective-permute-start(bf16[128,2048]{1,0:T(8,128)(2,1)} %add_convert_fusion), channel_id=1, source_target_pairs={{0,1},{1,0},{2,3},{3,2},{4,5},{5,4},{6,7},{7,6},{8,9},{9,8},{10,11... | collective-permute-start | bytes 1572872 | tf_op jit(solution)/shard_map/ppermute | solution.py:46
  225.8 15.9 %slice-start.6 = ((s8[8388608]{0:T(1024)(128)(4,1)}), s8[4194304]{0:T(1024)(128)(4,1)S(1)}, s32[]{:S(2)}) async-start(s8[8388608]{0:T(1024)(128)(4,1)} %bitcast.26), calls=%async_computation.6 | async-start | bytes 8388608
  227.3 14.4 %slice-start.7 = ((s8[8388608]{0:T(1024)(128)(4,1)}), s8[4194304]{0:T(1024)(128)(4,1)S(1)}, s32[]{:S(2)}) async-start(s8[8388608]{0:T(1024)(128)(4,1)} %bitcast.26), calls=%async_computation.7 | async-start | bytes 8388608
  227.3 14.4 %collective-permute-start.23 = (bf16[128,2048]{1,0:T(8,128)(2,1)S(1)}, bf16[128,2048]{1,0:T(8,128)(2,1)S(1)}, u32[]{:S(2)}, u32[]{:S(2)}) collective-permute-start(bf16[128,2048]{1,0:T(8,128)(2,1)S(1)} %slice.51), channel_id=1, source_target_pairs={{1,0},{2,3},{5,4},{6,7},{9,8},{10,11},{13,12},{14,15},{17,16},{18,... | collective-permute-start | bytes 1572872 | tf_op jit(solution)/shard_map/ppermute | solution.py:46
  235.9 8.1 %copy-start.3 = (f32[384,2048]{1,0:T(8,128)}, f32[384,2048]{1,0:T(8,128)S(1)}, u32[]{:S(2)}) copy-start(f32[384,2048]{1,0:T(8,128)S(1)} %fusion.3) | copy-start | bytes 9437188
  237.3 10.4 %collective-permute-start.17 = (f32[192,2048]{1,0:T(8,128)}, f32[192,2048]{1,0:T(8,128)}, u32[]{:S(2)}, u32[]{:S(2)}) collective-permute-start(f32[192,2048]{1,0:T(8,128)} %constant_dynamic-slice_fusion.5), channel_id=1, source_target_pairs={{0,4},{4,0},{8,12},{12,8},{1,5},{5,1},{9,13},{13,9},{2,6},{6,2},{1... | collective-permute-start | bytes 4718600 | tf_op jit(solution)/shard_map/ppermute | solution.py:52
  244.1 2.0 collective-permute-start.24
  246.1 9.2 %collective-permute-start.25 = (f32[32,2048]{1,0:T(8,128)S(1)}, f32[32,2048]{1,0:T(8,128)S(1)}, u32[]{:S(2)}, u32[]{:S(2)}) collective-permute-start(f32[32,2048]{1,0:T(8,128)S(1)} %constant_dynamic-slice_fusion.1), channel_id=1, source_target_pairs={{0,8},{4,12},{8,0},{12,4},{1,9},{5,13},{9,1},{13,5},{2,10},{6,14},... | collective-permute-start | bytes 786440 | tf_op jit(solution)/shard_map/ppermute | solution.py:52
  247.7 23.7 %slice-start = ((s8[8388608]{0:T(1024)(128)(4,1)}), s8[4194304]{0:T(1024)(128)(4,1)S(1)}, s32[]{:S(2)}) async-start(s8[8388608]{0:T(1024)(128)(4,1)} %bitcast.20), calls=%async_computation | async-start | bytes 8388608
  250.0 21.4 %collective-permute-start.18 = (f32[96,2048]{1,0:T(8,128)S(1)}, f32[96,2048]{1,0:T(8,128)S(1)}, u32[]{:S(2)}, u32[]{:S(2)}) collective-permute-start(f32[96,2048]{1,0:T(8,128)S(1)} %constant_dynamic-slice_fusion.4), channel_id=1, source_target_pairs={{0,8},{4,12},{8,0},{12,4},{1,9},{5,13},{9,1},{13,5},{2,10},{6,14},... | collective-permute-start | bytes 2359304 | tf_op jit(solution)/shard_map/ppermute | solution.py:52
  253.2 18.2 %slice-start.1 = ((s8[8388608]{0:T(1024)(128)(4,1)}), s8[4194304]{0:T(1024)(128)(4,1)S(1)}, s32[]{:S(2)}) async-start(s8[8388608]{0:T(1024)(128)(4,1)} %bitcast.20), calls=%async_computation.1 | async-start | bytes 8388608
  261.4 15.5 %collective-permute-start.26 = (bf16[32,2048]{1,0:T(8,128)(2,1)S(1)}, bf16[32,2048]{1,0:T(8,128)(2,1)S(1)}, u32[]{:S(2)}, u32[]{:S(2)}) collective-permute-start(bf16[32,2048]{1,0:T(8,128)(2,1)S(1)} %convolution_convert_fusion.2), channel_id=1, source_target_pairs={{0,3},{3,0},{1,2},{2,1},{4,7},{7,4},{5,6},{6,5},{8,11},{11,8},{9,1... | collective-permute-start | bytes 393224 | tf_op jit(solution)/shard_map/ppermute | solution.py:46
  274.1 12.3 %collective-permute-start.19 = (bf16[96,2048]{1,0:T(8,128)(2,1)S(1)}, bf16[96,2048]{1,0:T(8,128)(2,1)S(1)}, u32[]{:S(2)}, u32[]{:S(2)}) collective-permute-start(bf16[96,2048]{1,0:T(8,128)(2,1)S(1)} %convolution_convert_fusion.1), channel_id=1, source_target_pairs={{0,3},{3,0},{1,2},{2,1},{4,7},{7,4},{5,6},{6,5},{8,11},{11,8},{9,1... | collective-permute-start | bytes 1179656 | tf_op jit(solution)/shard_map/ppermute | solution.py:46
  286.6 12.1 %copy-start.12 = (pred[640]{0:T(1024)(128)(4,1)S(1)}, pred[640]{0:T(1024)(128)(4,1)}, u32[]{:S(2)}) copy-start(pred[640]{0:T(1024)(128)(4,1)} %constant.55.clone.1) | copy-start | bytes 1924
  286.8 8.0 %collective-permute-start.20 = (f32[96,640]{1,0:T(8,128)S(1)}, f32[96,640]{1,0:T(8,128)S(1)}, u32[]{:S(2)}, u32[]{:S(2)}) collective-permute-start(f32[96,640]{1,0:T(8,128)S(1)} %get-tuple-element.73), channel_id=1, source_target_pairs={{0,8},{4,12},{8,0},{12,4},{1,9},{5,13},{9,1},{13,5},{2,10},{6,14},... | collective-permute-start | bytes 737288 | tf_op jit(solution)/shard_map/ppermute | solution.py:52
  288.4 6.5 %collective-permute-start.21 = (f32[96,640]{1,0:T(8,128)S(1)}, f32[96,640]{1,0:T(8,128)S(1)}, u32[]{:S(2)}, u32[]{:S(2)}) collective-permute-start(f32[96,640]{1,0:T(8,128)S(1)} %get-tuple-element.74), channel_id=1, source_target_pairs={{0,4},{4,0},{8,12},{12,8},{1,5},{5,1},{9,13},{13,9},{2,6},{6,2},{1... | collective-permute-start | bytes 737288 | tf_op jit(solution)/shard_map/ppermute | solution.py:52
  288.4 10.3 %collective-permute-start.22 = (f32[96,640]{1,0:T(8,128)S(1)}, f32[96,640]{1,0:T(8,128)S(1)}, u32[]{:S(2)}, u32[]{:S(2)}) collective-permute-start(f32[96,640]{1,0:T(8,128)S(1)} %get-tuple-element.75), channel_id=1, source_target_pairs={{0,12},{4,8},{8,4},{12,0},{1,13},{5,9},{9,5},{13,1},{2,14},{6,10},... | collective-permute-start | bytes 737288 | tf_op jit(solution)/shard_map/ppermute | solution.py:52
  289.1 11.9 %collective-permute-start.27 = (f32[32,640]{1,0:T(8,128)S(1)}, f32[32,640]{1,0:T(8,128)S(1)}, u32[]{:S(2)}, u32[]{:S(2)}) collective-permute-start(f32[32,640]{1,0:T(8,128)S(1)} %get-tuple-element.70), channel_id=1, source_target_pairs={{0,8},{4,12},{8,0},{12,4},{1,9},{5,13},{9,1},{13,5},{2,10},{6,14},... | collective-permute-start | bytes 245768 | tf_op jit(solution)/shard_map/ppermute | solution.py:52
  290.7 10.3 %collective-permute-start.28 = (f32[32,640]{1,0:T(8,128)S(1)}, f32[32,640]{1,0:T(8,128)S(1)}, u32[]{:S(2)}, u32[]{:S(2)}) collective-permute-start(f32[32,640]{1,0:T(8,128)S(1)} %get-tuple-element.71), channel_id=1, source_target_pairs={{0,4},{4,0},{8,12},{12,8},{1,5},{5,1},{9,13},{13,9},{2,6},{6,2},{1... | collective-permute-start | bytes 245768 | tf_op jit(solution)/shard_map/ppermute | solution.py:52
  294.8 6.2 %collective-permute-start.29 = (f32[32,640]{1,0:T(8,128)S(1)}, f32[32,640]{1,0:T(8,128)S(1)}, u32[]{:S(2)}, u32[]{:S(2)}) collective-permute-start(f32[32,640]{1,0:T(8,128)S(1)} %get-tuple-element.72), channel_id=1, source_target_pairs={{0,12},{4,8},{8,4},{12,0},{1,13},{5,9},{9,5},{13,1},{2,14},{6,10},... | collective-permute-start | bytes 245768 | tf_op jit(solution)/shard_map/ppermute | solution.py:52

commit v4 on v3

--- a/solution.py
+++ b/solution.py
@@ -70,52 +70,75 @@
     def cut(sizes):
         return [(sum(sizes[:p]), sizes[p]) for p in range(len(sizes))]
 
-    def core_sum(block, sizes):
-        part = jnp.dot(block, fisher, preferred_element_type=F32)
-        sent = to_other(portion(part, cut(sizes), 1 - core, 2), 1)
-        return portion(part, cut(sizes), core, 2) + sent
+    def product(block):
+        return jnp.dot(block, fisher, preferred_element_type=F32)
 
-    def chip_sum(part, sizes):
+    def core_sum(part, sizes, ways=2):
+        kept = portion(part, cut(sizes), core, 2)
+        sent = portion(part, cut(sizes), 1 - core, 2)
+        step = sent.shape[0] // ways
+        got = [to_other(sent[w * step : (w + 1) * step], 1) for w in range(ways)]
+        return kept + jnp.concatenate(got)
+
+    def chip_sum(part, sizes, sent_as=F32):
         halves = cut([rows // 2 for rows in sizes])
-        sent = to_other(portion(part, halves, 1 - chip, 2), 2)
-        return (portion(part, halves, chip, 2) + sent).astype(BF16)
+        sent = to_other(portion(part, halves, 1 - chip, 2).astype(sent_as), 2)
+        return (portion(part, halves, chip, 2) + sent.astype(F32)).astype(BF16)
 
     whole = [rows for _, rows in pieces]
+    first_rows = pieces[0][1]
 
     near = along(test_grads, pair)
     third = along(test_grads, middle)
     grads = [train_grads, to_other(train_grads, 1), to_other(train_grads, 2)]
-    own_part = core_sum(test_grads, whole)
-    near, third, grads, own_part = tied(near, third, grads, own_part)
+    own = product(test_grads)
+    near, third, grads, own = tied(near, third, grads, own)
 
     second_in = along(near, middle)
     second_edge = along(third, outward)
-    own_precond = chip_sum(own_part, whole)
-    grads = jnp.concatenate(grads + [to_other(grads[2], 1)])
-    near_precond = chip_sum(core_sum(near, whole), whole)
-    own = dot_t(own_precond, grads)
-    near = dot_t(near_precond, grads)
+    own = chip_sum(core_sum(own, whole), whole)
+    near = core_sum(product(near), whole)
     second_in, second_edge, own, near, grads = tied(second_in, second_edge, own, near, grads)
 
-    last_in = second_in[pieces[1][0] :]
-    first_edge = along(second_in[: pieces[0][1]], outward)
-    second = jnp.where(inner, second_in, second_edge)
-    second = dot_t(chip_sum(core_sum(second, whole), whole), grads)
-    total = own + scores_along(second, [(0, 2), (3, 1)])
-    near = near + scores_along(second, middle)
-    total = total + scores_along(near, pair)
-    first_edge, last_in, total = tied(first_edge, last_in, total)
+    grads = jnp.concatenate(grads + [to_other(grads[2], 1)])
+    first_edge = along(second_in[:first_rows], outward)
+    near = chip_sum(near, whole)
+    second = core_sum(product(jnp.where(inner, second_in, second_edge)), whole)
+    last_in = second_in[first_rows:]
+    first_edge, last_in, own, near, second, grads = tied(
+        first_edge, last_in, own, near, second, grads
+    )
+
     last_edge = along(last_in, outward)
+    own = dot_t(own, grads)
+    near = dot_t(near, grads)
+    second = chip_sum(second, whole, BF16)
+    block = jnp.where(inner, third[:first_rows], first_edge)
+    first_part = core_sum(product(block), whole[:1], 3)
+    last_edge, second, first_part, own, near, grads = tied(
+        last_edge, second, first_part, own, near, grads
+    )
+
+    second = dot_t(second, grads)
+    got_in = scores_along(second, middle)
+    first_value = chip_sum(first_part, whole[:1], BF16)
+    block = jnp.where(inner, third[first_rows:], last_edge)
+    last_part = core_sum(product(block), whole[1:], 1)
+    got_in, second, first_value, last_part, own, near, grads = tied(
+        got_in, second, first_value, last_part, own, near, grads
+    )
+    near_got = scores_along(near + got_in, pair)
+    edge_got = scores_along(second, [(0, 2), (3, 1)])
+    total = own + near_got + edge_got
+    last_value = chip_sum(last_part, whole[1:], BF16)
 
     blocks = jnp.stack([i, i ^ 1, i ^ 2, i ^ 3])
     row_ids = (blocks[:, None] * own_rows + jnp.arange(own_rows)[None, :]).reshape(1, 1, -1)
 
     outs = []
-    edges = (first_edge, last_edge)
-    for (first, rows), edge in zip(pieces, edges):
+    for (first, rows), value in zip(pieces, (first_value, last_value)):
         quarter = rows // 4
-        block = jnp.where(inner, third[first : first + rows], edge)
-        value = dot_t(chip_sum(core_sum(block, [rows]), [rows]), grads)
+        value = dot_t(value, grads)
         value = total[first // 4 : first // 4 + quarter] + scores_along(value, far_pairs)
         ids = lax.dynamic_slice_in_dim(chosen_ids, first + (core * 2 + chip) * quarter, quarter)
         counts = jnp.sum((ids[:, :, None] == row_ids).astype(F32), axis=1)

time: 308 us -> 266 us (0.86)
  waiting for transfers between devices: 171 us -> 130 us
  other arithmetic: 14.6 us -> 34.3 us
  starting transfers between devices: 52 us -> 39.2 us
  matrix products: 48.4 us -> 43.1 us
  local copies, waits for them, and re-layouts: 15.8 us -> 12.2 us
    ppermute x19 -> x24, waiting for transfers between devices: 90.5 us -> 61.1 us  [to_other(): return lax.ppermute(value, 'train', [(k, k ^ r) for k in range(4)])]
    ppermute x11, starting transfers between devices: 40.3 us -> 24.7 us  [along(): return lax.ppermute(value, 'test', pairs)]
    concatenate x0 -> x1, other arithmetic: none -> 13.2 us  [four_by_four(): grads = jnp.concatenate(grads + [to_other(grads[2], 1)])]
    ppermute x11, waiting for transfers between devices: 80.9 us -> 69.2 us  [along(): return lax.ppermute(value, 'test', pairs)]
    slice x2 -> x6, local copies, waits for them, and re-layouts: 1.33 us -> 7.03 us  [the longest x1 2.76 us: four_by_four(): first_edge = along(second_in[:first_rows], outward)]
    dynamic_slice x16 -> x13, local copies, waits for them, and re-layouts: 7.71 us -> 2.16 us  [portion(): lax.dynamic_slice_in_dim(value, first + which * (rows // of), rows // of)]
    convert_element_type x0 -> x4, other arithmetic: none -> 4.86 us  [chip_sum(): return (portion(part, halves, chip, 2) + sent.astype(F32)).astype(BF16)]
    dot_general x5, matrix products: 18.2 us -> 13.9 us  [dot_t(): lax.dot_general(a, b, (((1,), (1,)), ((), ())), preferred_element_type=F32)]
  transfers between devices with their start and end apart: 30 -> 35, of which waited for: 16 -> 18; matrix products, arithmetic and copies ran while one was open for 13% -> 27% of each run, Pallas kernels for 0% -> 0%
where the time goes in v4:
time: 266 us; the launch traced here: 261 us
  waiting for transfers between devices  130 us (49%)
  matrix products  43.1 us (16%)
  starting transfers between devices  39.2 us (15%)
  other arithmetic  34.3 us (13%)
  local copies, waits for them, and re-layouts  12.2 us (5%)
    ppermute x11, waiting for transfers between devices, along(): return lax.ppermute(value, 'test', pairs)  69.2 us
    ppermute x24, waiting for transfers between devices, to_other(): return lax.ppermute(value, 'train', [(k, k ^ r) for k in range(4)])  61.1 us
    dot_general x5, matrix products, product(): return jnp.dot(block, fisher, preferred_element_type=F32)  29.2 us
    ppermute x11, starting transfers between devices, along(): return lax.ppermute(value, 'test', pairs)  24.7 us
    ppermute x24, starting transfers between devices, to_other(): return lax.ppermute(value, 'train', [(k, k ^ r) for k in range(4)])  14.5 us
    dot_general x5, matrix products, dot_t(): lax.dot_general(a, b, (((1,), (1,)), ((), ())), preferred_element_type=F32)  13.9 us
    concatenate x1, other arithmetic, four_by_four(): grads = jnp.concatenate(grads + [to_other(grads[2], 1)])  13.2 us
  transfers between devices with their start and end apart: 35, of which 18 were waited for; matrix products, arithmetic and copies ran while one was open for 27% of the time, Pallas kernels for 0%

profile of v4, /device:TPU:0, one launch (start us, length us, event | category | flops | bytes accessed | tf_op | source)
XLA Modules:
  0.0 260.7 jit_solution(11193859416286722457)
XLA Ops:
  0.6 3.1 %collective-permute-start = (bf16[512,2048]{1,0:T(8,128)(2,1)}, bf16[512,2048]{1,0:T(8,128)(2,1)}, u32[]{:S(2)}, u32[]{:S(2)}) collective-permute-start(bf16[512,2048]{1,0:T(8,128)(2,1)} %param.5), channel_id=1, source_target_pairs={{0,1},{1,0},{2,3},{3,2},{4,5},{5,4},{6,7},{7,6},{8,9},{9,8},{10,11... | collective-permute-start | bytes 6291464 | tf_op jit(solution)/shard_map/ppermute | solution.py:46
  3.7 2.0 collective-permute-start.1
  5.7 1.5 collective-permute-start.3
  7.2 7.7 %fusion.23 = f32[512,2048]{1,0:T(8,128)S(1)} fusion(bf16[512,2048]{1,0:T(8,128)(2,1)} %param.5, bf16[2048,2048]{1,0:T(8,128)(2,1)} %param.6), kind=kOutput, calls=%fused_computation.109 | convolution fusion | flops 4294967296 | bytes 14680064 | tf_op jit(solution)/shard_map/dot_general | solution.py:74
  14.9 34.7 %collective-permute-done = bf16[512,2048]{1,0:T(8,128)(2,1)} collective-permute-done((bf16[512,2048]{1,0:T(8,128)(2,1)}, bf16[512,2048]{1,0:T(8,128)(2,1)}, u32[]{:S(2)}, u32[]{:S(2)}) %collective-permute-start) | collective-permute-done | bytes 2097184 | tf_op jit(solution)/shard_map/ppermute | solution.py:46
  49.7 4.4 %collective-permute-done.3 = bf16[512,2048]{1,0:T(8,128)(2,1)} collective-permute-done((bf16[512,2048]{1,0:T(8,128)(2,1)}, bf16[512,2048]{1,0:T(8,128)(2,1)}, u32[]{:S(2)}, u32[]{:S(2)}) %collective-permute-start.3) | collective-permute-done | bytes 2097184 | tf_op jit(solution)/shard_map/ppermute | solution.py:52
  54.1 2.0 collective-permute-start.4
  56.2 6.1 %fusion.24 = f32[512,2048]{1,0:T(8,128)S(1)} fusion(bf16[512,2048]{1,0:T(8,128)(2,1)} %collective-permute-done, bf16[2048,2048]{1,0:T(8,128)(2,1)S(1)} %copy-done.2), kind=kOutput, calls=%fused_computation.110 | convolution fusion | flops 4294967296 | bytes 14680064 | tf_op jit(solution)/shard_map/dot_general | solution.py:74
  62.2 1.8 collective-permute-start.5
  65.5 1.1 pad_maximum_fusion.2
  66.7 1.1 constant_dynamic-slice_fusion.3
  68.2 0.7 collective-permute-done.6
  69.4 1.0 pad_maximum_fusion.4
  70.4 1.5 collective-permute-start.8
  72.2 1.8 maximum_add_fusion.1
  74.0 21.9 %collective-permute-done.8 = f32[128,2048]{1,0:T(8,128)} collective-permute-done((f32[128,2048]{1,0:T(8,128)}, f32[128,2048]{1,0:T(8,128)}, u32[]{:S(2)}, u32[]{:S(2)}) %collective-permute-start.8) | collective-permute-done | bytes 1048608 | tf_op jit(solution)/shard_map/ppermute | solution.py:52
  95.9 2.1 fusion.7
  98.1 14.3 %collective-permute-done.5 = bf16[512,2048]{1,0:T(8,128)(2,1)} collective-permute-done((bf16[512,2048]{1,0:T(8,128)(2,1)}, bf16[512,2048]{1,0:T(8,128)(2,1)}, u32[]{:S(2)}, u32[]{:S(2)}) %collective-permute-start.5) | collective-permute-done | bytes 2097184 | tf_op jit(solution)/shard_map/ppermute | solution.py:46
  112.3 7.6 %fusion = f32[512,2048]{1,0:T(8,128)S(1)} fusion(bf16[2048,2048]{1,0:T(8,128)(2,1)} %param.6, bf16[512,2048]{1,0:T(8,128)(2,1)} %collective-permute-done.4, bf16[512,2048]{1,0:T(8,128)(2,1)} %collective-permute-done.5, pred[]{:T(512)S(6)} %or.3), kind=kOutput, calls=%fused_computation.8 | convolution fusion | flops 4296015872 | bytes 16777216 | tf_op jit(solution)/shard_map/dot_general | solution.py:74
  119.9 0.9 constant_dynamic-slice_fusion.11
  121.0 1.1 constant_dynamic-slice_fusion.2
  122.2 1.0 pad_maximum_fusion.1
  123.2 0.5 collective-permute-start.13
  123.8 1.1 pad_maximum_fusion.5
  124.9 1.5 collective-permute-start.12
  126.8 2.6 %convert_reduce_fusion = f32[96,2048]{1,0:T(8,128)S(1)} fusion(s32[2048]{0:T(1024)S(1)} %bitcast.28, s32[96,16]{1,0:T(8,128)S(1)} %copy.12), kind=kLoop, calls=%fused_computation | loop fusion | flops 9240576 | bytes 800768 | tf_op jit(solution)/shard_map/reduce_sum | solution.py:144
  129.4 2.8 %slice.81 = bf16[384,2048]{1,0:T(8,128)(2,1)} slice(bf16[512,2048]{1,0:T(8,128)(2,1)} %collective-permute-done.4), slice={[0:384], [0:2048]} | slice | bytes 3145728 | tf_op jit(solution)/shard_map/slice | solution.py:104
  132.2 1.5 collective-permute-start.11
  133.6 2.1 convert_reduce_fusion.1
  135.7 1.9 slice.82
  137.6 2.1 maximum_add_fusion.2
  139.7 11.1 %collective-permute-done.12 = f32[128,2048]{1,0:T(8,128)} collective-permute-done((f32[128,2048]{1,0:T(8,128)}, f32[128,2048]{1,0:T(8,128)}, u32[]{:S(2)}, u32[]{:S(2)}) %collective-permute-start.12) | collective-permute-done | bytes 1048608 | tf_op jit(solution)/shard_map/ppermute | solution.py:52
  150.7 1.5 fusion.8
  152.3 13.2 %pad_maximum_fusion = bf16[2048,2048]{1,0:T(8,128)(2,1)S(1)} fusion(bf16[512,2048]{1,0:T(8,128)(2,1)} %collective-permute-done.15, bf16[512,2048]{1,0:T(8,128)(2,1)} %collective-permute-done.3, bf16[512,2048]{1,0:T(8,128)(2,1)S(1)} %copy-done.6, bf16[512,2048]{1,0:T(8,128)(2,1)S(1)} %copy-done.4), kind=kLoop, calls=%fused_computation.1 | loop fusion | flops 33554432 | bytes 16777216 | tf_op jit(solution)/shard_map/concatenate | solution.py:103
  165.5 5.4 %collective-permute-done.11 = bf16[384,2048]{1,0:T(8,128)(2,1)} collective-permute-done((bf16[384,2048]{1,0:T(8,128)(2,1)}, bf16[384,2048]{1,0:T(8,128)(2,1)}, u32[]{:S(2)}, u32[]{:S(2)}) %collective-permute-start.11) | collective-permute-done | bytes 1572896 | tf_op jit(solution)/shard_map/ppermute | solution.py:46
  171.0 1.5 collective-permute-start.16
  172.5 0.8 pad_maximum_fusion.6
  173.3 0.5 collective-permute-start.17
  173.8 5.4 %fusion.3 = f32[384,2048]{1,0:T(8,128)S(1)} fusion(bf16[2048,2048]{1,0:T(8,128)(2,1)S(1)} %bitcast.25, bf16[384,2048]{1,0:T(8,128)(2,1)} %collective-permute-done.11, bf16[512,2048]{1,0:T(8,128)(2,1)} %collective-permute-done.1, pred[]{:T(512)S(6)} %or.3), kind=kOutput, calls=%fused_computation.12 | convolution fusion | flops 3222011904 | bytes 14680065 | tf_op jit(solution)/shard_map/dot_general | solution.py:74
  180.3 2.9 %fusion.25 = f32[128,2048]{1,0:T(8,128)S(1)} fusion(bf16[128,2048]{1,0:T(8,128)(2,1)S(1)} %copy-done.3, bf16[2048,2048]{1,0:T(8,128)(2,1)S(1)} %pad_maximum_fusion), kind=kOutput, calls=%fused_computation.111 | convolution fusion | flops 1073741824 | bytes 9961472 | tf_op jit(solution)/shard_map/dot_general | solution.py:13
  183.2 2.9 %fusion.26 = f32[128,2048]{1,0:T(8,128)S(1)} fusion(bf16[128,2048]{1,0:T(8,128)(2,1)S(1)} %fusion.8, bf16[2048,2048]{1,0:T(8,128)(2,1)S(1)} %pad_maximum_fusion), kind=kOutput, calls=%fused_computation.112 | convolution fusion | flops 1073741824 | bytes 9961472 | tf_op jit(solution)/shard_map/dot_general | solution.py:13
  186.9 1.2 fusion.9
  188.0 2.9 %fusion.27 = bf16[128,2048]{1,0:T(8,128)(2,1)S(1)} fusion(bf16[128,2048]{1,0:T(8,128)(2,1)S(1)} %fusion.9, bf16[2048,2048]{1,0:T(8,128)(2,1)S(1)} %pad_maximum_fusion), kind=kOutput, calls=%fused_computation.113 | convolution fusion | flops 1073741824 | bytes 9437184 | tf_op jit(solution)/shard_map/dot_general | solution.py:13
  190.9 0.9 collective-permute-start.21
  191.9 1.2 collective-permute-start.22
  193.1 2.4 fusion.10
  195.7 7.2 %collective-permute-done.22 = bf16[96,2048]{1,0:T(8,128)(2,1)S(1)} collective-permute-done((bf16[96,2048]{1,0:T(8,128)(2,1)S(1)}, bf16[96,2048]{1,0:T(8,128)(2,1)S(1)}, u32[]{:S(2)}, u32[]{:S(2)}) %collective-permute-start.22) | collective-permute-done | bytes 393248 | tf_op jit(solution)/shard_map/ppermute | solution.py:52
  203.1 2.7 %convolution_convert_fusion = bf16[96,2048]{1,0:T(8,128)(2,1)S(1)} fusion(bf16[96,2048]{1,0:T(8,128)(2,1)S(1)} %add_convert_fusion.1, bf16[2048,2048]{1,0:T(8,128)(2,1)S(1)} %pad_maximum_fusion), kind=kOutput, calls=%fused_computation.3 | convolution fusion | flops 805502976 | bytes 9175040 | tf_op jit(solution)/shard_map/dot_general | solution.py:13
  205.8 2.7 %collective-permute-start.26 = (bf16[96,2048]{1,0:T(8,128)(2,1)S(1)}, bf16[96,2048]{1,0:T(8,128)(2,1)S(1)}, u32[]{:S(2)}, u32[]{:S(2)}) collective-permute-start(bf16[96,2048]{1,0:T(8,128)(2,1)S(1)} %convolution_convert_fusion), channel_id=1, source_target_pairs={{0,3},{3,0},{1,2},{2,1},{4,7},{7,4},{5,6},{6,5},{8,11},{11,8},{9,1... | collective-permute-start | bytes 1179656 | tf_op jit(solution)/shard_map/ppermute | solution.py:46
  208.5 6.5 %collective-permute-start.25 = (bf16[128,2048]{1,0:T(8,128)(2,1)S(1)}, bf16[128,2048]{1,0:T(8,128)(2,1)S(1)}, u32[]{:S(2)}, u32[]{:S(2)}) collective-permute-start(bf16[128,2048]{1,0:T(8,128)(2,1)S(1)} %fusion.27), channel_id=1, source_target_pairs={{0,2},{3,1},{4,6},{7,5},{8,10},{11,9},{12,14},{15,13},{16,18},{19,... | collective-permute-start | bytes 1572872 | tf_op jit(solution)/shard_map/ppermute | solution.py:46
  215.0 1.6 collective-permute-start.30
  216.8 3.3 %collective-permute-done.30 = bf16[32,2048]{1,0:T(8,128)(2,1)S(1)} collective-permute-done((bf16[32,2048]{1,0:T(8,128)(2,1)S(1)}, bf16[32,2048]{1,0:T(8,128)(2,1)S(1)}, u32[]{:S(2)}, u32[]{:S(2)}) %collective-permute-start.30) | collective-permute-done | bytes 131104 | tf_op jit(solution)/shard_map/ppermute | solution.py:52
  220.1 2.6 convolution_convert_fusion.1
  222.6 2.6 %collective-permute-start.31 = (bf16[32,2048]{1,0:T(8,128)(2,1)S(1)}, bf16[32,2048]{1,0:T(8,128)(2,1)S(1)}, u32[]{:S(2)}, u32[]{:S(2)}) collective-permute-start(bf16[32,2048]{1,0:T(8,128)(2,1)S(1)} %convolution_convert_fusion.1), channel_id=1, source_target_pairs={{0,3},{3,0},{1,2},{2,1},{4,7},{7,4},{5,6},{6,5},{8,11},{11,8},{9,1... | collective-permute-start | bytes 393224 | tf_op jit(solution)/shard_map/ppermute | solution.py:46
  225.3 4.1 %collective-permute-done.25 = bf16[128,2048]{1,0:T(8,128)(2,1)S(1)} collective-permute-done((bf16[128,2048]{1,0:T(8,128)(2,1)S(1)}, bf16[128,2048]{1,0:T(8,128)(2,1)S(1)}, u32[]{:S(2)}, u32[]{:S(2)}) %collective-permute-start.25) | collective-permute-done | bytes 524320 | tf_op jit(solution)/shard_map/ppermute | solution.py:46
  229.4 10.5 %collective-permute-done.24 = bf16[128,2048]{1,0:T(8,128)(2,1)S(1)} collective-permute-done((bf16[128,2048]{1,0:T(8,128)(2,1)S(1)}, bf16[128,2048]{1,0:T(8,128)(2,1)S(1)}, u32[]{:S(2)}, u32[]{:S(2)}) %collective-permute-start.24) | collective-permute-done | bytes 524320 | tf_op jit(solution)/shard_map/ppermute | solution.py:46
  240.6 2.1 collective-permute-start.29
  243.3 2.0 collective-permute-start.34
  245.5 3.5 %collective-permute-done.29 = f32[96,640]{1,0:T(8,128)S(1)} collective-permute-done((f32[96,640]{1,0:T(8,128)S(1)}, f32[96,640]{1,0:T(8,128)S(1)}, u32[]{:S(2)}, u32[]{:S(2)}) %collective-permute-start.29) | collective-permute-done | bytes 245792 | tf_op jit(solution)/shard_map/ppermute | solution.py:52
  248.9 5.8 %collective-permute-done.27 = f32[96,640]{1,0:T(8,128)S(1)} collective-permute-done((f32[96,640]{1,0:T(8,128)S(1)}, f32[96,640]{1,0:T(8,128)S(1)}, u32[]{:S(2)}, u32[]{:S(2)}) %collective-permute-start.27) | collective-permute-done | bytes 245792 | tf_op jit(solution)/shard_map/ppermute | solution.py:52
  255.2 0.8 collective-permute-done.34
  255.9 2.0 collective-permute-done.32
  258.4 0.7 slice_reduce_fusion
  259.1 1.3 copy.14
  (108 shorter events, 8.2 us)
Async XLA Ops:
  0.6 125.8 %copy-start = (s32[512,16]{0,1:T(8,128)S(1)}, s32[512,16]{0,1:T(8,128)}, u32[]{:S(2)}) copy-start(s32[512,16]{0,1:T(8,128)} %param.7) | copy-start | bytes 98308
  0.6 49.0 %collective-permute-start = (bf16[512,2048]{1,0:T(8,128)(2,1)}, bf16[512,2048]{1,0:T(8,128)(2,1)}, u32[]{:S(2)}, u32[]{:S(2)}) collective-permute-start(bf16[512,2048]{1,0:T(8,128)(2,1)} %param.5), channel_id=1, source_target_pairs={{0,1},{1,0},{2,3},{3,2},{4,5},{5,4},{6,7},{7,6},{8,9},{9,8},{10,11... | collective-permute-start | bytes 6291464 | tf_op jit(solution)/shard_map/ppermute | solution.py:46
  3.7 45.9 %collective-permute-start.1 = (bf16[512,2048]{1,0:T(8,128)(2,1)}, bf16[512,2048]{1,0:T(8,128)(2,1)}, u32[]{:S(2)}, u32[]{:S(2)}) collective-permute-start(bf16[512,2048]{1,0:T(8,128)(2,1)} %param.5), channel_id=1, source_target_pairs={{1,2},{2,1},{5,6},{6,5},{9,10},{10,9},{13,14},{14,13},{17,18},{18,... | collective-permute-start | bytes 6291464 | tf_op jit(solution)/shard_map/ppermute | solution.py:46
  5.7 43.9 %collective-permute-start.2 = (bf16[512,2048]{1,0:T(8,128)(2,1)}, bf16[512,2048]{1,0:T(8,128)(2,1)S(1)}, u32[]{:S(2)}, u32[]{:S(2)}) collective-permute-start(bf16[512,2048]{1,0:T(8,128)(2,1)} %param.4), channel_id=1, source_target_pairs={{0,4},{4,0},{8,12},{12,8},{1,5},{5,1},{9,13},{13,9},{2,6},{6,2},{1... | collective-permute-start | bytes 6291464 | tf_op jit(solution)/shard_map/ppermute | solution.py:52
  5.7 48.4 %collective-permute-start.3 = (bf16[512,2048]{1,0:T(8,128)(2,1)}, bf16[512,2048]{1,0:T(8,128)(2,1)}, u32[]{:S(2)}, u32[]{:S(2)}) collective-permute-start(bf16[512,2048]{1,0:T(8,128)(2,1)} %param.4), channel_id=1, source_target_pairs={{0,8},{4,12},{8,0},{12,4},{1,9},{5,13},{9,1},{13,5},{2,10},{6,14},... | collective-permute-start | bytes 6291464 | tf_op jit(solution)/shard_map/ppermute | solution.py:52
  7.2 48.9 %copy-start.2 = (bf16[2048,2048]{1,0:T(8,128)(2,1)S(1)}, bf16[2048,2048]{1,0:T(8,128)(2,1)}, u32[]{:S(2)}) copy-start(bf16[2048,2048]{1,0:T(8,128)(2,1)} %param.6) | copy-start | bytes 25165828
  49.7 12.5 %copy-start.5 = (bf16[512,2048]{1,0:T(8,128)(2,1)}, bf16[512,2048]{1,0:T(8,128)(2,1)S(1)}, u32[]{:S(2)}) copy-start(bf16[512,2048]{1,0:T(8,128)(2,1)S(1)} %collective-permute-done.2) | copy-start | bytes 6291460
  54.1 44.0 %collective-permute-start.4 = (bf16[512,2048]{1,0:T(8,128)(2,1)}, bf16[512,2048]{1,0:T(8,128)(2,1)}, u32[]{:S(2)}, u32[]{:S(2)}) collective-permute-start(bf16[512,2048]{1,0:T(8,128)(2,1)} %collective-permute-done), channel_id=1, source_target_pairs={{1,2},{2,1},{5,6},{6,5},{9,10},{10,9},{13,14},{14,13},{17,18},{18,... | collective-permute-start | bytes 6291464 | tf_op jit(solution)/shard_map/ppermute | solution.py:46
  62.2 50.1 %collective-permute-start.5 = (bf16[512,2048]{1,0:T(8,128)(2,1)}, bf16[512,2048]{1,0:T(8,128)(2,1)}, u32[]{:S(2)}, u32[]{:S(2)}) collective-permute-start(bf16[512,2048]{1,0:T(8,128)(2,1)} %collective-permute-done.1), channel_id=1, source_target_pairs={{1,0},{2,3},{5,4},{6,7},{9,8},{10,11},{13,12},{14,15},{17,16},{18,... | collective-permute-start | bytes 6291464 | tf_op jit(solution)/shard_map/ppermute | solution.py:46
  64.6 3.1 %collective-permute-start.7 = (f32[128,2048]{1,0:T(8,128)S(1)}, f32[128,2048]{1,0:T(8,128)S(1)}, u32[]{:S(2)}, u32[]{:S(2)}) collective-permute-start(f32[128,2048]{1,0:T(8,128)S(1)} %pad_maximum_fusion.3), channel_id=1, source_target_pairs={{0,4},{4,0},{8,12},{12,8},{1,5},{5,1},{9,13},{13,9},{2,6},{6,2},{1... | collective-permute-start | bytes 3145736 | tf_op jit(solution)/shard_map/ppermute | solution.py:52
  64.7 4.1 %collective-permute-start.6 = (f32[128,2048]{1,0:T(8,128)S(1)}, f32[128,2048]{1,0:T(8,128)S(1)}, u32[]{:S(2)}, u32[]{:S(2)}) collective-permute-start(f32[128,2048]{1,0:T(8,128)S(1)} %constant_dynamic-slice_fusion.4), channel_id=1, source_target_pairs={{0,4},{4,0},{8,12},{12,8},{1,5},{5,1},{9,13},{13,9},{2,6},{6,2},{1... | collective-permute-start | bytes 3145736 | tf_op jit(solution)/shard_map/ppermute | solution.py:52
  66.6 5.4 %collective-permute-start.10 = (f32[128,2048]{1,0:T(8,128)}, f32[128,2048]{1,0:T(8,128)}, u32[]{:S(2)}, u32[]{:S(2)}) collective-permute-start(f32[128,2048]{1,0:T(8,128)} %pad_maximum_fusion.2), channel_id=1, source_target_pairs={{0,4},{4,0},{8,12},{12,8},{1,5},{5,1},{9,13},{13,9},{2,6},{6,2},{1... | collective-permute-start | bytes 3145736 | tf_op jit(solution)/shard_map/ppermute | solution.py:52
  67.8 4.4 %collective-permute-start.9 = (f32[128,2048]{1,0:T(8,128)}, f32[128,2048]{1,0:T(8,128)}, u32[]{:S(2)}, u32[]{:S(2)}) collective-permute-start(f32[128,2048]{1,0:T(8,128)} %constant_dynamic-slice_fusion.3), channel_id=1, source_target_pairs={{0,4},{4,0},{8,12},{12,8},{1,5},{5,1},{9,13},{13,9},{2,6},{6,2},{1... | collective-permute-start | bytes 3145736 | tf_op jit(solution)/shard_map/ppermute | solution.py:52
  70.4 25.5 %collective-permute-start.8 = (f32[128,2048]{1,0:T(8,128)}, f32[128,2048]{1,0:T(8,128)}, u32[]{:S(2)}, u32[]{:S(2)}) collective-permute-start(f32[128,2048]{1,0:T(8,128)} %pad_maximum_fusion.4), channel_id=1, source_target_pairs={{0,8},{4,12},{8,0},{12,4},{1,9},{5,13},{9,1},{13,5},{2,10},{6,14},... | collective-permute-start | bytes 3145736 | tf_op jit(solution)/shard_map/ppermute | solution.py:52
  123.2 14.3 %collective-permute-start.14 = (f32[128,2048]{1,0:T(8,128)}, f32[128,2048]{1,0:T(8,128)}, u32[]{:S(2)}, u32[]{:S(2)}) collective-permute-start(f32[128,2048]{1,0:T(8,128)} %pad_maximum_fusion.1), channel_id=1, source_target_pairs={{0,4},{4,0},{8,12},{12,8},{1,5},{5,1},{9,13},{13,9},{2,6},{6,2},{1... | collective-permute-start | bytes 3145736 | tf_op jit(solution)/shard_map/ppermute | solution.py:52
  123.2 14.3 %collective-permute-start.13 = (f32[128,2048]{1,0:T(8,128)}, f32[128,2048]{1,0:T(8,128)}, u32[]{:S(2)}, u32[]{:S(2)}) collective-permute-start(f32[128,2048]{1,0:T(8,128)} %constant_dynamic-slice_fusion.2), channel_id=1, source_target_pairs={{0,4},{4,0},{8,12},{12,8},{1,5},{5,1},{9,13},{13,9},{2,6},{6,2},{1... | collective-permute-start | bytes 3145736 | tf_op jit(solution)/shard_map/ppermute | solution.py:52
  123.7 28.5 %collective-permute-start.15 = (bf16[512,2048]{1,0:T(8,128)(2,1)}, bf16[512,2048]{1,0:T(8,128)(2,1)}, u32[]{:S(2)}, u32[]{:S(2)}) collective-permute-start(bf16[512,2048]{1,0:T(8,128)(2,1)} %collective-permute-done.3), channel_id=1, source_target_pairs={{0,4},{4,0},{8,12},{12,8},{1,5},{5,1},{9,13},{13,9},{2,6},{6,2},{1... | collective-permute-start | bytes 6291464 | tf_op jit(solution)/shard_map/ppermute | solution.py:52
  124.9 25.9 %collective-permute-start.12 = (f32[128,2048]{1,0:T(8,128)}, f32[128,2048]{1,0:T(8,128)}, u32[]{:S(2)}, u32[]{:S(2)}) collective-permute-start(f32[128,2048]{1,0:T(8,128)} %pad_maximum_fusion.5), channel_id=1, source_target_pairs={{0,8},{4,12},{8,0},{12,4},{1,9},{5,13},{9,1},{13,5},{2,10},{6,14},... | collective-permute-start | bytes 3145736 | tf_op jit(solution)/shard_map/ppermute | solution.py:52
  132.2 38.7 %collective-permute-start.11 = (bf16[384,2048]{1,0:T(8,128)(2,1)}, bf16[384,2048]{1,0:T(8,128)(2,1)}, u32[]{:S(2)}, u32[]{:S(2)}) collective-permute-start(bf16[384,2048]{1,0:T(8,128)(2,1)} %slice.81), channel_id=1, source_target_pairs={{1,0},{2,3},{5,4},{6,7},{9,8},{10,11},{13,12},{14,15},{17,16},{18,... | collective-permute-start | bytes 4718600 | tf_op jit(solution)/shard_map/ppermute | solution.py:46
  137.6 14.7 %copy-start.6 = (bf16[512,2048]{1,0:T(8,128)(2,1)S(1)}, bf16[512,2048]{1,0:T(8,128)(2,1)}, u32[]{:S(2)}) copy-start(bf16[512,2048]{1,0:T(8,128)(2,1)} %copy-done.5) | copy-start | bytes 6291460
  139.7 12.6 %copy-start.4 = (bf16[512,2048]{1,0:T(8,128)(2,1)S(1)}, bf16[512,2048]{1,0:T(8,128)(2,1)}, u32[]{:S(2)}) copy-start(bf16[512,2048]{1,0:T(8,128)(2,1)} %param.4) | copy-start | bytes 6291460
  150.7 23.1 %slice-start = ((s8[8388608]{0:T(1024)(128)(4,1)}), s8[4194304]{0:T(1024)(128)(4,1)S(1)}, s32[]{:S(2)}) async-start(s8[8388608]{0:T(1024)(128)(4,1)} %bitcast.24), calls=%async_computation | async-start | bytes 8388608
  152.2 21.6 %slice-start.1 = ((s8[8388608]{0:T(1024)(128)(4,1)}), s8[4194304]{0:T(1024)(128)(4,1)S(1)}, s32[]{:S(2)}) async-start(s8[8388608]{0:T(1024)(128)(4,1)} %bitcast.24), calls=%async_computation.1 | async-start | bytes 8388608
  171.0 17.1 %collective-permute-start.16 = (bf16[128,2048]{1,0:T(8,128)(2,1)}, bf16[128,2048]{1,0:T(8,128)(2,1)S(1)}, u32[]{:S(2)}, u32[]{:S(2)}) collective-permute-start(bf16[128,2048]{1,0:T(8,128)(2,1)} %slice.82), channel_id=1, source_target_pairs={{1,0},{2,3},{5,4},{6,7},{9,8},{10,11},{13,12},{14,15},{17,16},{18,... | collective-permute-start | bytes 1572872 | tf_op jit(solution)/shard_map/ppermute | solution.py:46
  173.3 13.6 %collective-permute-start.17 = (bf16[128,2048]{1,0:T(8,128)(2,1)}, bf16[128,2048]{1,0:T(8,128)(2,1)}, u32[]{:S(2)}, u32[]{:S(2)}) collective-permute-start(bf16[128,2048]{1,0:T(8,128)(2,1)} %pad_maximum_fusion.6), channel_id=1, source_target_pairs={{0,8},{4,12},{8,0},{12,4},{1,9},{5,13},{9,1},{13,5},{2,10},{6,14},... | collective-permute-start | bytes 1572872 | tf_op jit(solution)/shard_map/ppermute | solution.py:52
  179.3 1.0 copy-start.3
  179.4 6.8 %collective-permute-start.20 = (f32[64,2048]{1,0:T(8,128)S(1)}, f32[64,2048]{1,0:T(8,128)S(1)}, u32[]{:S(2)}, u32[]{:S(2)}) collective-permute-start(f32[64,2048]{1,0:T(8,128)S(1)} %get-tuple-element.90), channel_id=1, source_target_pairs={{0,4},{4,0},{8,12},{12,8},{1,5},{5,1},{9,13},{13,9},{2,6},{6,2},{1... | collective-permute-start | bytes 1572872 | tf_op jit(solution)/shard_map/ppermute | solution.py:52
  179.5 6.7 %collective-permute-start.19 = (f32[64,2048]{1,0:T(8,128)S(1)}, f32[64,2048]{1,0:T(8,128)S(1)}, u32[]{:S(2)}, u32[]{:S(2)}) collective-permute-start(f32[64,2048]{1,0:T(8,128)S(1)} %get-tuple-element.89), channel_id=1, source_target_pairs={{0,4},{4,0},{8,12},{12,8},{1,5},{5,1},{9,13},{13,9},{2,6},{6,2},{1... | collective-permute-start | bytes 1572872 | tf_op jit(solution)/shard_map/ppermute | solution.py:52
  180.0 6.2 %collective-permute-start.18 = (f32[64,2048]{1,0:T(8,128)S(1)}, f32[64,2048]{1,0:T(8,128)S(1)}, u32[]{:S(2)}, u32[]{:S(2)}) collective-permute-start(f32[64,2048]{1,0:T(8,128)S(1)} %get-tuple-element.88), channel_id=1, source_target_pairs={{0,4},{4,0},{8,12},{12,8},{1,5},{5,1},{9,13},{13,9},{2,6},{6,2},{1... | collective-permute-start | bytes 1572872 | tf_op jit(solution)/shard_map/ppermute | solution.py:52
  190.9 12.0 %collective-permute-start.21 = (bf16[128,2048]{1,0:T(8,128)(2,1)S(1)}, bf16[128,2048]{1,0:T(8,128)(2,1)S(1)}, u32[]{:S(2)}, u32[]{:S(2)}) collective-permute-start(bf16[128,2048]{1,0:T(8,128)(2,1)S(1)} %fusion.27), channel_id=1, source_target_pairs={{1,2},{2,1},{5,6},{6,5},{9,10},{10,9},{13,14},{14,13},{17,18},{18,... | collective-permute-start | bytes 1572872 | tf_op jit(solution)/shard_map/ppermute | solution.py:46
  191.9 10.9 %collective-permute-start.22 = (bf16[96,2048]{1,0:T(8,128)(2,1)S(1)}, bf16[96,2048]{1,0:T(8,128)(2,1)S(1)}, u32[]{:S(2)}, u32[]{:S(2)}) collective-permute-start(bf16[96,2048]{1,0:T(8,128)(2,1)S(1)} %dynamic-slice_convert_fusion), channel_id=1, source_target_pairs={{0,8},{4,12},{8,0},{12,4},{1,9},{5,13},{9,1},{13,5},{2,10},{6,14},... | collective-permute-start | bytes 1179656 | tf_op jit(solution)/shard_map/ppermute | solution.py:52
  195.6 7.5 %collective-permute-start.23 = (f32[64,2048]{1,0:T(8,128)S(1)}, f32[64,2048]{1,0:T(8,128)S(1)}, u32[]{:S(2)}, u32[]{:S(2)}) collective-permute-start(f32[64,2048]{1,0:T(8,128)S(1)} %constant_dynamic-slice_fusion.7), channel_id=1, source_target_pairs={{0,4},{4,0},{8,12},{12,8},{1,5},{5,1},{9,13},{13,9},{2,6},{6,2},{1... | collective-permute-start | bytes 1572872 | tf_op jit(solution)/shard_map/ppermute | solution.py:52
  205.8 34.3 %collective-permute-start.26 = (bf16[96,2048]{1,0:T(8,128)(2,1)S(1)}, bf16[96,2048]{1,0:T(8,128)(2,1)S(1)}, u32[]{:S(2)}, u32[]{:S(2)}) collective-permute-start(bf16[96,2048]{1,0:T(8,128)(2,1)S(1)} %convolution_convert_fusion), channel_id=1, source_target_pairs={{0,3},{3,0},{1,2},{2,1},{4,7},{7,4},{5,6},{6,5},{8,11},{11,8},{9,1... | collective-permute-start | bytes 1179656 | tf_op jit(solution)/shard_map/ppermute | solution.py:46
  208.5 20.8 %collective-permute-start.25 = (bf16[128,2048]{1,0:T(8,128)(2,1)S(1)}, bf16[128,2048]{1,0:T(8,128)(2,1)S(1)}, u32[]{:S(2)}, u32[]{:S(2)}) collective-permute-start(bf16[128,2048]{1,0:T(8,128)(2,1)S(1)} %fusion.27), channel_id=1, source_target_pairs={{0,2},{3,1},{4,6},{7,5},{8,10},{11,9},{12,14},{15,13},{16,18},{19,... | collective-permute-start | bytes 1572872 | tf_op jit(solution)/shard_map/ppermute | solution.py:46
  215.0 5.0 %collective-permute-start.30 = (bf16[32,2048]{1,0:T(8,128)(2,1)S(1)}, bf16[32,2048]{1,0:T(8,128)(2,1)S(1)}, u32[]{:S(2)}, u32[]{:S(2)}) collective-permute-start(bf16[32,2048]{1,0:T(8,128)(2,1)S(1)} %dynamic-slice_convert_fusion.2), channel_id=1, source_target_pairs={{0,8},{4,12},{8,0},{12,4},{1,9},{5,13},{9,1},{13,5},{2,10},{6,14},... | collective-permute-start | bytes 393224 | tf_op jit(solution)/shard_map/ppermute | solution.py:52
  216.7 23.2 %collective-permute-start.24 = (bf16[128,2048]{1,0:T(8,128)(2,1)S(1)}, bf16[128,2048]{1,0:T(8,128)(2,1)S(1)}, u32[]{:S(2)}, u32[]{:S(2)}) collective-permute-start(bf16[128,2048]{1,0:T(8,128)(2,1)S(1)} %add_convert_fusion), channel_id=1, source_target_pairs={{0,1},{1,0},{2,3},{3,2},{4,5},{5,4},{6,7},{7,6},{8,9},{9,8},{10,11... | collective-permute-start | bytes 1572872 | tf_op jit(solution)/shard_map/ppermute | solution.py:46
  222.6 20.3 %collective-permute-start.31 = (bf16[32,2048]{1,0:T(8,128)(2,1)S(1)}, bf16[32,2048]{1,0:T(8,128)(2,1)S(1)}, u32[]{:S(2)}, u32[]{:S(2)}) collective-permute-start(bf16[32,2048]{1,0:T(8,128)(2,1)S(1)} %convolution_convert_fusion.1), channel_id=1, source_target_pairs={{0,3},{3,0},{1,2},{2,1},{4,7},{7,4},{5,6},{6,5},{8,11},{11,8},{9,1... | collective-permute-start | bytes 393224 | tf_op jit(solution)/shard_map/ppermute | solution.py:46
  240.1 2.9 %copy-start.7 = (f32[32,2048]{1,0:T(8,128)S(1)}, f32[32,2048]{1,0:T(8,128)}, u32[]{:S(2)}) copy-start(f32[32,2048]{1,0:T(8,128)} %convert_reduce_fusion.1) | copy-start | bytes 786436
  240.3 14.4 %copy-start.8 = (pred[640]{0:T(1024)(128)(4,1)S(1)}, pred[640]{0:T(1024)(128)(4,1)}, u32[]{:S(2)}) copy-start(pred[640]{0:T(1024)(128)(4,1)} %constant.55.clone.1) | copy-start | bytes 1924
  240.5 4.8 %collective-permute-start.28 = (f32[96,640]{1,0:T(8,128)S(1)}, f32[96,640]{1,0:T(8,128)S(1)}, u32[]{:S(2)}, u32[]{:S(2)}) collective-permute-start(f32[96,640]{1,0:T(8,128)S(1)} %get-tuple-element.109), channel_id=1, source_target_pairs={{0,4},{4,0},{8,12},{12,8},{1,5},{5,1},{9,13},{13,9},{2,6},{6,2},{1... | collective-permute-start | bytes 737288 | tf_op jit(solution)/shard_map/ppermute | solution.py:52
  240.6 8.3 %collective-permute-start.29 = (f32[96,640]{1,0:T(8,128)S(1)}, f32[96,640]{1,0:T(8,128)S(1)}, u32[]{:S(2)}, u32[]{:S(2)}) collective-permute-start(f32[96,640]{1,0:T(8,128)S(1)} %get-tuple-element.110), channel_id=1, source_target_pairs={{0,12},{4,8},{8,4},{12,0},{1,13},{5,9},{9,5},{13,1},{2,14},{6,10},... | collective-permute-start | bytes 737288 | tf_op jit(solution)/shard_map/ppermute | solution.py:52
  242.6 12.1 %collective-permute-start.27 = (f32[96,640]{1,0:T(8,128)S(1)}, f32[96,640]{1,0:T(8,128)S(1)}, u32[]{:S(2)}, u32[]{:S(2)}) collective-permute-start(f32[96,640]{1,0:T(8,128)S(1)} %get-tuple-element.108), channel_id=1, source_target_pairs={{0,8},{4,12},{8,0},{12,4},{1,9},{5,13},{9,1},{13,5},{2,10},{6,14},... | collective-permute-start | bytes 737288 | tf_op jit(solution)/shard_map/ppermute | solution.py:52
  243.2 11.9 %collective-permute-start.33 = (f32[32,640]{1,0:T(8,128)S(1)}, f32[32,640]{1,0:T(8,128)S(1)}, u32[]{:S(2)}, u32[]{:S(2)}) collective-permute-start(f32[32,640]{1,0:T(8,128)S(1)} %get-tuple-element.106), channel_id=1, source_target_pairs={{0,4},{4,0},{8,12},{12,8},{1,5},{5,1},{9,13},{13,9},{2,6},{6,2},{1... | collective-permute-start | bytes 245768 | tf_op jit(solution)/shard_map/ppermute | solution.py:52
  243.3 12.6 %collective-permute-start.34 = (f32[32,640]{1,0:T(8,128)S(1)}, f32[32,640]{1,0:T(8,128)S(1)}, u32[]{:S(2)}, u32[]{:S(2)}) collective-permute-start(f32[32,640]{1,0:T(8,128)S(1)} %get-tuple-element.107), channel_id=1, source_target_pairs={{0,12},{4,8},{8,4},{12,0},{1,13},{5,9},{9,5},{13,1},{2,14},{6,10},... | collective-permute-start | bytes 245768 | tf_op jit(solution)/shard_map/ppermute | solution.py:52
  245.4 12.6 %collective-permute-start.32 = (f32[32,640]{1,0:T(8,128)S(1)}, f32[32,640]{1,0:T(8,128)S(1)}, u32[]{:S(2)}, u32[]{:S(2)}) collective-permute-start(f32[32,640]{1,0:T(8,128)S(1)} %get-tuple-element.105), channel_id=1, source_target_pairs={{0,8},{4,12},{8,0},{12,4},{1,9},{5,13},{9,1},{13,5},{2,10},{6,14},... | collective-permute-start | bytes 245768 | tf_op jit(solution)/shard_map/ppermute | solution.py:52
  258.3 2.2 copy-start.1

commit v5 on v2

v5 whole, which is shorter than its diff:
```python
import jax
import jax.numpy as jnp
from jax import lax
from jax.experimental import pallas as pl
from jax.experimental.pallas import tpu as pltpu
from jax.sharding import PartitionSpec as P

COLUMNS = 512

F32 = jnp.float32
BF16 = jnp.bfloat16


def dot_t(a, b):
    return lax.dot_general(a, b, (((1,), (1,)), ((), ())), preferred_element_type=F32)


def selection_counts(chosen_ids, first_row, rows):
    row_ids = first_row + lax.broadcasted_iota(jnp.int32, (rows, chosen_ids.shape[0]), 0)
    ids = chosen_ids.T
    counts = jnp.zeros(row_ids.shape, F32)
    for k in range(ids.shape[0]):
        counts = counts + (row_ids == ids[k][None, :]).astype(F32)
    return counts


def any_mesh(train_grads, test_grads, fisher, chosen_ids):
    test_whole = lax.all_gather(test_grads, "test", axis=0, tiled=True)
    partial_value = jnp.dot(test_whole, fisher, preferred_element_type=F32)
    precond = lax.psum(partial_value, "train").astype(BF16)
    partial_scores = dot_t(train_grads, precond)
    scores = lax.psum_scatter(partial_scores, "test", scatter_dimension=1, tiled=True)
    rows = scores.shape[0]
    counts = selection_counts(chosen_ids, lax.axis_index("train") * rows, rows)
    return scores, lax.psum(jnp.sum(counts * scores, axis=0), "train")


SMALL = pl.CostEstimate(flops=1, bytes_accessed=1, transcendentals=0)
PARAMS = pltpu.CompilerParams(vmem_limit_bytes=60 * 2**20)


def product_body(choices, parts, flags, *refs):
    count = sum(len(choice) for choice in choices)
    blocks, fisher, outs, (held, sems) = refs[:count], refs[count], refs[count + 1 : -2], refs[-2:]
    block_rows = blocks[0].shape[0]

    @pl.when(pl.program_id(0) == 0)
    def _():
        places = [held.at[pl.ds(u * block_rows, block_rows)] for u in range(len(choices))]
        first = 0
        for u, choice in enumerate(choices):
            if len(choice) == 1:
                pltpu.make_async_copy(blocks[first], places[u], sems.at[u]).start()
            else:

                @pl.when(flags[2] == 1)
                def _():
                    pltpu.make_async_copy(blocks[first], places[u], sems.at[u]).start()

                @pl.when(flags[2] == 0)
                def _():
                    pltpu.make_async_copy(blocks[first + 1], places[u], sems.at[u]).start()

            first += len(choice)
        for u in range(len(choices)):
            pltpu.make_async_copy(blocks[0], places[u], sems.at[u]).wait()

    quarter = block_rows // 4
    rows = quarter // parts
    first = flags[0] == 0
    for u in range(len(choices)):
        block = held[u * block_rows : (u + 1) * block_rows]
        value = jnp.dot(block, fisher[...], preferred_element_type=F32)
        for p in range(parts):
            kept, sent = outs[2 * (u * parts + p) :][:2]
            for chip in range(2):
                low, high = (
                    value[(2 * core + chip) * quarter + p * rows :][:rows] for core in range(2)
                )
                kept[chip * rows : (chip + 1) * rows] = jnp.where(first, low, high)
                sent[chip * rows : (chip + 1) * rows] = jnp.where(first, high, low).astype(BF16)


def product(flags, choices, fisher, parts=1):
    rows, depth = choices[0][0].shape
    columns = fisher.shape[1]
    half = rows // 2 // parts
    blocks = [block for choice in choices for block in choice]
    outs = len(choices) * parts
    return pl.pallas_call(
        lambda *refs: product_body(choices, parts, *refs),
        grid=(columns // COLUMNS,),
        in_specs=[pl.BlockSpec(memory_space=pltpu.SMEM)]
        + [pl.BlockSpec(memory_space=pl.ANY)] * len(blocks)
        + [pl.BlockSpec((depth, COLUMNS), lambda n: (0, n))],
        out_specs=[pl.BlockSpec((half, COLUMNS), lambda n: (0, n))] * (2 * outs),
        out_shape=[
            jax.ShapeDtypeStruct((half, columns), F32),
            jax.ShapeDtypeStruct((half, columns), BF16),
        ]
        * outs,
        scratch_shapes=[
            pltpu.VMEM((len(choices) * rows, depth), BF16),
            pltpu.SemaphoreType.DMA((len(choices),)),
        ],
        compiler_params=PARAMS,
        cost_estimate=SMALL,
        name="product",
    )(flags, *blocks, fisher)


def fold_body(flags, kept, got, kept_out, sent_out):
    value = kept[...] + got[...].astype(F32)
    half = value.shape[0] // 2
    first = flags[1] == 0
    low, high = value[:half], value[half:]
    kept_out[...] = jnp.where(first, low, high)
    sent_out[...] = jnp.where(first, high, low).astype(sent_out.dtype)


def fold(flags, kept, got, sent_as):
    rows, columns = kept.shape
    tile = COLUMNS
    before = pl.BlockSpec((rows, tile), lambda n: (0, n))
    after = pl.BlockSpec((rows // 2, tile), lambda n: (0, n))
    return pl.pallas_call(
        fold_body,
        grid=(columns // tile,),
        in_specs=[pl.BlockSpec(memory_space=pltpu.SMEM), before, before],
        out_specs=[after, after],
        out_shape=[
            jax.ShapeDtypeStruct((rows // 2, columns), F32),
            jax.ShapeDtypeStruct((rows // 2, columns), sent_as),
        ],
        compiler_params=PARAMS,
        cost_estimate=SMALL,
        name="fold",
    )(flags, kept, got)


def scores_body(units, *refs):
    sums, grads, outs, (held, sems) = refs[: 2 * units], refs[2 * units :][:4], refs[-2 - units : -2], refs[-2:]
    copies = [pltpu.make_async_copy(grads[r], held.at[r], sems.at[r]) for r in range(4)]
    for copy in copies:
        copy.start()
    values = [sums[2 * u][...] + sums[2 * u + 1][...].astype(F32) for u in range(units)]
    values = [(value.astype(BF16), value) for value in values]
    values = [(high, (value - high.astype(F32)).astype(BF16)) for high, value in values]
    precond = jnp.concatenate([part for value in values for part in value])
    rows = sums[0].shape[0]
    for r in range(4):
        copies[r].wait()
        both = dot_t(precond, held[r])
        for u in range(units):
            value = both[2 * u * rows :][:rows] + both[(2 * u + 1) * rows :][:rows]
            outs[u][r] = value.astype(outs[u].dtype)


def partial_scores(units, grads, out_as):
    rows = units[0][0].shape[0]
    train_rows, depth = grads[0].shape
    return pl.pallas_call(
        lambda *refs: scores_body(len(units), *refs),
        in_specs=[pl.BlockSpec(memory_space=pltpu.VMEM)] * (2 * len(units))
        + [pl.BlockSpec(memory_space=pl.ANY)] * 4,
        out_specs=[pl.BlockSpec(memory_space=pltpu.VMEM)] * len(units),
        out_shape=[jax.ShapeDtypeStruct((4, rows, train_rows), kind) for kind in out_as],
        scratch_shapes=[
            pltpu.VMEM((4, train_rows, depth), BF16),
            pltpu.SemaphoreType.DMA((4,)),
        ],
        compiler_params=PARAMS,
        cost_estimate=SMALL,
        name="scores",
    )(*[value for unit in units for value in unit], *grads)


def four_by_four(train_grads, test_grads, fisher, chosen_ids):
    z = lax.axis_index("test")
    i = lax.axis_index("train")
    chip, core = i // 2, i % 2
    inner = (z == 1) | (z == 2)
    flags = jnp.stack([core, chip, inner.astype(jnp.int32)])
    own_rows = train_grads.shape[0]
    queries, depth = test_grads.shape
    quarter = queries // 4
    split = quarter // 2

    def along(value, pairs):
        return lax.ppermute(value, "test", pairs)

    def to_other(value, r):
        return lax.ppermute(value, "train", [(k, k ^ r) for k in range(4)])

    def tied(*values):
        return lax.optimization_barrier(values)

    pair = [(0, 1), (1, 0), (2, 3), (3, 2)]
    middle = [(1, 2), (2, 1)]
    outward = [(1, 0), (2, 3)]
    inward = [(0, 1), (3, 2)]

    def core_sum(kept, sent, sent_as=BF16):
        return fold(flags, kept, to_other(sent, 1), sent_as)

    def scores_of(*units, out_as=(BF16, BF16)):
        return partial_scores(units, grads, out_as[: len(units)])

    blocks = jnp.stack([i, i ^ 1, i ^ 2, i ^ 3])
    row_ids = blocks[:, None, None, None] * own_rows + jnp.arange(own_rows)
    ids = lax.dynamic_slice_in_dim(chosen_ids, (core * 2 + chip) * quarter, quarter)
    counts = jnp.sum((ids[None, :, :, None] == row_ids).astype(F32), axis=2)

    pair_in = along(test_grads, pair)
    middle_in = along(test_grads, middle)
    grads = [train_grads, to_other(train_grads, 1), to_other(train_grads, 2)]
    own, own_sent = core_sum(*product(flags, [[test_grads]], fisher), F32)
    pair_in, middle_in, own, own_sent, counts, grads[1] = tied(
        pair_in, middle_in, own, own_sent, counts, grads[1]
    )

    far_in = along(pair_in, middle)
    second_edge = along(middle_in, outward)
    own_got = to_other(own_sent, 2)
    near, near_sent = core_sum(*product(flags, [[middle_in, pair_in]], fisher))
    near_got = to_other(near_sent, 2)
    grads = grads + [to_other(grads[2], 1)]
    far_in, second_edge, pair_in, own, own_got, near, near_got, grads = tied(
        far_in, second_edge, pair_in, own, own_got, near, near_got, grads
    )

    first_edge = along(far_in, outward)
    second, second_sent, third, third_sent = product(
        flags, [[far_in, second_edge], [pair_in]], fisher
    )
    second, second_sent = core_sum(second, second_sent)
    third, third_sent = core_sum(third, third_sent)
    second_sent, third_sent, near, own = tied(second_sent, third_sent, near, own)
    near, total = scores_of((near, near_got), (own, own_got), out_as=(BF16, F32))
    second, third = scores_of(
        (second, to_other(second_sent, 2)), (third, to_other(third_sent, 2))
    )
    total = total + along(near, inward).astype(F32) + along(near, middle).astype(F32)
    first_edge, total, second, third, grads = tied(first_edge, total, second, third, grads)

    second = along(second, [(0, 2), (3, 1), (1, 3), (2, 0)])
    third = along(third, outward)
    total = total + second.astype(F32) + third.astype(F32)
    last = product(flags, [[first_edge]], fisher, 2)

    outs = []
    for p, first in enumerate((0, split)):
        part, part_sent = core_sum(*last[2 * p : 2 * p + 2])
        (value,) = scores_of((part, to_other(part_sent, 2)))
        value = along(value, [(0, 3), (3, 0)]).astype(F32) + total[:, first : first + split]
        rows = split
        chosen = jnp.sum(value * counts[:, first : first + rows], axis=(0, 2))[:, None]
        parts = [jnp.pad(value[r], ((0, 0), (0, 128))) for r in range(4)]
        column = lax.broadcasted_iota(jnp.int32, parts[0].shape, 1)
        parts = [jnp.where(column < own_rows, part, chosen) for part in parts]
        got = [parts[0]] + [to_other(parts[r], r) for r in range(1, 4)]
        got = [got[0], got[2], got[1], got[3]]
        got = [jnp.where(chip == 0, got[q], got[q ^ 1]) for q in range(4)]
        outs.append([jnp.where(core == 0, got[q], got[q ^ 2]) for q in range(4)])
    turned = jnp.concatenate([piece[q] for q in range(4) for piece in outs]).T
    return turned[:own_rows], turned[own_rows]


def solution(mesh):
    sizes = (mesh.shape["train"], mesh.shape["test"])
    return jax.shard_map(
        four_by_four if sizes == (4, 4) else any_mesh,
        mesh=mesh,
        in_specs=(
            P(("groups", "train"), "test"),
            P(("groups", "test"), "train"),
            P("train", "test"),
            P(("groups", "test"), None),
        ),
        out_specs=(P(("groups", "train"), "test"), P(("groups", "test"))),
        check_vma=False,
    )
```

time: 359 us -> 250 us (0.70)
  waiting for transfers between devices: 186 us -> 82.9 us
  Pallas kernels: 0 us -> 100 us
  matrix products: 54 us -> 0 us
  other arithmetic: 24.5 us -> 7.91 us
  between operations: 14.7 us -> 1.01 us
  starting transfers between devices: 59.4 us -> 47.3 us
  local copies, waits for them, and re-layouts: 20.1 us -> 9.15 us
    all_gather x4 -> x0, waiting for transfers between devices: 126 us -> none  [four_by_four(): block = lax.all_gather(relative, 'test', axis=0, tiled=True)]
    pallas_call x0 -> x14, Pallas kernels: none -> 100 us  [the longest x4 44.6 us: product(): pl.pallas_call(lambda *refs: product_body(choices, parts, *refs), grid=(c...]
    dot_general x8 -> x0, matrix products: 54 us -> none  [the longest x4 31.2 us: four_by_four(): jnp.dot(block, fisher, preferred_element_type=F32)]
    ppermute x12 -> x11, waiting for transfers between devices: 15.2 us -> 32.6 us  [along(): return lax.ppermute(value, 'test', pairs)]
    ppermute x35 -> x21, starting transfers between devices: 27.5 us -> 14.7 us  [to_other(): return lax.ppermute(value, 'train', [(k, k ^ r) for k in range(4)])]
    ppermute x35 -> x21, waiting for transfers between devices: 45.1 us -> 50.3 us  [to_other(): return lax.ppermute(value, 'train', [(k, k ^ r) for k in range(4)])]
    concatenate x5 -> x1, other arithmetic: 4.19 us -> 0.09 us  [four_by_four(): turned = jnp.concatenate([piece[q] for q in range(4) for piece in outs]).T]
    concatenate x2 -> x0, local copies, waits for them, and re-layouts: 4.08 us -> none  [the longest x1 3.4 us: four_by_four(): grads = jnp.concatenate(grads + [to_other(grads[2], 1)])]
  transfers between devices with their start and end apart: 51 -> 32, of which waited for: 22 -> 14; matrix products, arithmetic and copies ran while one was open for 25% -> 3% of each run, Pallas kernels for 0% -> 36%
where the time goes in v5:
time: 250 us; the launch traced here: 249 us
  Pallas kernels  100 us (40%)
  waiting for transfers between devices  82.9 us (33%)
  starting transfers between devices  47.3 us (19%)
  local copies, waits for them, and re-layouts  9.15 us (4%)
  other arithmetic  7.91 us (3%)
    ppermute x21, waiting for transfers between devices, to_other(): return lax.ppermute(value, 'train', [(k, k ^ r) for k in range(4)])  50.3 us
    pallas_call x4, Pallas kernels, product(): pl.pallas_call(lambda *refs: product_body(choices, parts, *refs), grid=(c...  44.6 us
    pallas_call x4, Pallas kernels, partial_scores(): pl.pallas_call(lambda *refs: scores_body(len(units), *refs), in_specs=[pl...  32.9 us
    ppermute x11, starting transfers between devices, along(): return lax.ppermute(value, 'test', pairs)  32.6 us
    ppermute x11, waiting for transfers between devices, along(): return lax.ppermute(value, 'test', pairs)  32.6 us
    pallas_call x6, Pallas kernels, fold(): pl.pallas_call(fold_body, grid=(columns // tile,), in_specs=[pl.BlockSpec...  23 us
    ppermute x21, starting transfers between devices, to_other(): return lax.ppermute(value, 'train', [(k, k ^ r) for k in range(4)])  14.7 us
    unnamed x33, local copies, waits for them, and re-layouts  8.11 us
  transfers between devices with their start and end apart: 32, of which 14 were waited for; matrix products, arithmetic and copies ran while one was open for 3% of the time, Pallas kernels for 36%

profile of v5, /device:TPU:0, one launch (start us, length us, event | category | flops | bytes accessed | tf_op | source)
XLA Modules:
  0.0 248.7 jit_solution(10040642569122983153)
XLA Ops:
  0.6 3.1 %collective-permute-start = (bf16[512,2048]{1,0:T(8,128)(2,1)}, bf16[512,2048]{1,0:T(8,128)(2,1)}, u32[]{:S(2)}, u32[]{:S(2)}) collective-permute-start(bf16[512,2048]{1,0:T(8,128)(2,1)} %refs_1_.1), channel_id=1, source_target_pairs={{0,1},{1,0},{2,3},{3,2},{4,5},{5,4},{6,7},{7,6},{8,9},{9,8},{10,11... | collective-permute-start | bytes 6291464 | tf_op jit(solution)/shard_map/ppermute | solution.py:190
  3.7 2.0 collective-permute-start.1
  5.7 1.5 collective-permute-start.9
  7.2 0.7 pad_add_fusion.refs_0_.flags
  7.9 10.1 %product.4 = (f32[256,2048]{1,0:T(8,128)}, bf16[256,2048]{1,0:T(8,128)(2,1)}) custom-call(s32[3]{0:T(128)} %pad_add_fusion.refs_0_.flags, bf16[512,2048]{1,0:T(8,128)(2,1)} %refs_1_.1, bf16[2048,2048]{1,0:T(8,128)(2,1)} %refs_2_.3), custom_call_target="tpu_custom_call" | custom-call | flops 1 | bytes 1 | tf_op jit(solution)/shard_map/product/pallas_call | solution.py:90
  18.5 3.4 %convert_reduce_fusion = f32[4,128,512]{2,1,0:T(8,128)S(1)} fusion(s32[4,512]{1,0:T(4,128)S(1)} %iota_add_fusion, s32[128,16]{1,0:T(8,128)S(1)} %copy.10), kind=kLoop, calls=%fused_computation | loop fusion | flops 12320768 | bytes 1064960 | tf_op jit(solution)/shard_map/reduce_sum | solution.py:212
  21.9 4.0 %fold.6 = (f32[128,2048]{1,0:T(8,128)}, f32[128,2048]{1,0:T(8,128)}) custom-call(s32[3]{0:T(128)} %pad_add_fusion.refs_0_.flags, f32[256,2048]{1,0:T(8,128)} %get-tuple-element.59.kept, bf16[256,2048]{1,0:T(8,128)(2,1)} %collective-permute-done.2.got), custom_call_target="tpu_custom_call" | custom-call | flops 1 | bytes 1 | tf_op jit(solution)/shard_map/fold/pallas_call | solution.py:126
  25.9 23.7 %collective-permute-done.refs_2_.refs_3_ = bf16[512,2048]{1,0:T(8,128)(2,1)} collective-permute-done((bf16[512,2048]{1,0:T(8,128)(2,1)}, bf16[512,2048]{1,0:T(8,128)(2,1)}, u32[]{:S(2)}, u32[]{:S(2)}) %collective-permute-start) | collective-permute-done | bytes 2097184 | tf_op jit(solution)/shard_map/ppermute | solution.py:190
  49.7 2.1 collective-permute-start.4
  51.7 1.3 collective-permute-start.5
  53.0 1.0 collective-permute-done.9.refs_6_.refs_4_
  54.1 10.1 %product.5 = (f32[256,2048]{1,0:T(8,128)}, bf16[256,2048]{1,0:T(8,128)(2,1)}) custom-call(s32[3]{0:T(128)} %pad_add_fusion.refs_0_.flags, bf16[512,2048]{1,0:T(8,128)(2,1)} %collective-permute-done.1.refs_1_, bf16[512,2048]{1,0:T(8,128)(2,1)} %collective-permute-done.refs_2_.refs_3_, bf16[2048,2048]{1,0:T(8,128)(2,1)} %refs_2_.3), custom_call_target="tpu_custom_call" | custom-call | flops 1 | bytes 1 | tf_op jit(solution)/shard_map/product/pallas_call | solution.py:90
  64.2 0.6 collective-permute-start.7
  64.7 1.5 collective-permute-start.6
  66.2 1.0 collective-permute-done.7.got
  67.2 1.0 copy-done.6
  68.2 4.0 %fold.7 = (f32[128,2048]{1,0:T(8,128)}, bf16[128,2048]{1,0:T(8,128)(2,1)}) custom-call(s32[3]{0:T(128)} %pad_add_fusion.refs_0_.flags, f32[256,2048]{1,0:T(8,128)} %get-tuple-element.67.kept, bf16[256,2048]{1,0:T(8,128)(2,1)} %copy-done.6), custom_call_target="tpu_custom_call" | custom-call | flops 1 | bytes 1 | tf_op jit(solution)/shard_map/fold/pallas_call | solution.py:126
  72.2 1.5 collective-permute-start.8
  73.7 17.3 %collective-permute-done.6.refs_3_ = f32[128,2048]{1,0:T(8,128)S(1)} collective-permute-done((f32[128,2048]{1,0:T(8,128)}, f32[128,2048]{1,0:T(8,128)S(1)}, u32[]{:S(2)}, u32[]{:S(2)}) %collective-permute-start.6) | collective-permute-done | bytes 1048608 | tf_op jit(solution)/shard_map/ppermute | solution.py:193
  91.0 10.4 %collective-permute-done.8.refs_1_ = bf16[128,2048]{1,0:T(8,128)(2,1)S(1)} collective-permute-done((bf16[128,2048]{1,0:T(8,128)(2,1)}, bf16[128,2048]{1,0:T(8,128)(2,1)S(1)}, u32[]{:S(2)}, u32[]{:S(2)}) %collective-permute-start.8) | collective-permute-done | bytes 524320 | tf_op jit(solution)/shard_map/ppermute | solution.py:193
  101.3 2.5 %collective-permute-done.5.refs_2_ = bf16[512,2048]{1,0:T(8,128)(2,1)} collective-permute-done((bf16[512,2048]{1,0:T(8,128)(2,1)}, bf16[512,2048]{1,0:T(8,128)(2,1)}, u32[]{:S(2)}, u32[]{:S(2)}) %collective-permute-start.5) | collective-permute-done | bytes 2097184 | tf_op jit(solution)/shard_map/ppermute | solution.py:190
  103.8 1.5 collective-permute-start.11
  105.3 14.4 %product.6 = (f32[256,2048]{1,0:T(8,128)}, bf16[256,2048]{1,0:T(8,128)(2,1)}, f32[256,2048]{1,0:T(8,128)}, bf16[256,2048]{1,0:T(8,128)(2,1)}) custom-call(s32[3]{0:T(128)} %pad_add_fusion.refs_0_.flags, bf16[512,2048]{1,0:T(8,128)(2,1)} %collective-permute-done.4.refs_1_, bf16[512,2048]{1,0:T(8,128)(2,1)} %collective-permute-done.5.refs_2_, ...), custom_call_target="tpu_custom_call" | custom-call | flops 1 | bytes 1 | tf_op jit(solution)/shard_map/product/pallas_call | solution.py:90
  119.8 0.5 collective-permute-start.12
  120.3 2.4 collective-permute-done.13.got
  122.7 1.0 copy-done.7
  123.7 3.9 %fold.9 = (f32[128,2048]{1,0:T(8,128)}, bf16[128,2048]{1,0:T(8,128)(2,1)}) custom-call(s32[3]{0:T(128)} %pad_add_fusion.refs_0_.flags, f32[256,2048]{1,0:T(8,128)} %get-tuple-element.78.kept, bf16[256,2048]{1,0:T(8,128)(2,1)} %copy-done.7), custom_call_target="tpu_custom_call" | custom-call | flops 1 | bytes 1 | tf_op jit(solution)/shard_map/fold/pallas_call | solution.py:126
  127.6 1.0 copy-done.5
  128.6 4.1 %fold.8 = (f32[128,2048]{1,0:T(8,128)}, bf16[128,2048]{1,0:T(8,128)(2,1)}) custom-call(s32[3]{0:T(128)} %pad_add_fusion.refs_0_.flags, f32[256,2048]{1,0:T(8,128)} %get-tuple-element.75.kept, bf16[256,2048]{1,0:T(8,128)(2,1)} %copy-done.5), custom_call_target="tpu_custom_call" | custom-call | flops 1 | bytes 1 | tf_op jit(solution)/shard_map/fold/pallas_call | solution.py:126
  132.7 1.5 collective-permute-start.16
  134.2 0.5 collective-permute-start.17
  134.7 9.8 %scores.4 = (bf16[4,128,512]{2,1,0:T(8,128)(2,1)}, f32[4,128,512]{2,1,0:T(8,128)}) custom-call(f32[128,2048]{1,0:T(8,128)} %get-tuple-element.83.refs_0_, bf16[128,2048]{1,0:T(8,128)(2,1)} %copy-done.8, f32[128,2048]{1,0:T(8,128)} %get-tuple-element.85.refs_2_, f32[128,2048]{1,0:T(8,128)} %copy-done.3, bf16[512,2048]{1,0:T(8,128)(2,1)} %refs_2_.5, ...), custom_call_target="tpu_custom_call" | custom-call | flops 1 | bytes 1 | tf_op jit(solution)/shard_map/scores/pallas_call | solution.py:162
  144.6 7.2 %collective-permute-start.14 = (bf16[4,128,512]{2,1,0:T(8,128)(2,1)}, bf16[4,128,512]{2,1,0:T(8,128)(2,1)S(1)}, u32[]{:S(2)}, u32[]{:S(2)}) collective-permute-start(bf16[4,128,512]{2,1,0:T(8,128)(2,1)} %get-tuple-element.92), channel_id=1, source_target_pairs={{0,1},{3,2},{4,5},{7,6},{8,9},{11,10},{12,13},{15,14},{16,17},{19,... | collective-permute-start | bytes 1572872 | tf_op jit(solution)/shard_map/ppermute | solution.py:190
  151.8 1.5 collective-permute-start.15
  153.2 4.9 %collective-permute-done.17.refs_3_ = bf16[128,2048]{1,0:T(8,128)(2,1)S(1)} collective-permute-done((bf16[128,2048]{1,0:T(8,128)(2,1)S(1)}, bf16[128,2048]{1,0:T(8,128)(2,1)S(1)}, u32[]{:S(2)}, u32[]{:S(2)}) %collective-permute-start.17) | collective-permute-done | bytes 524320 | tf_op jit(solution)/shard_map/ppermute | solution.py:193
  158.1 0.8 copy-done.10
  158.9 9.7 %scores.5 = (bf16[4,128,512]{2,1,0:T(8,128)(2,1)}, bf16[4,128,512]{2,1,0:T(8,128)(2,1)}) custom-call(f32[128,2048]{1,0:T(8,128)} %get-tuple-element.93.refs_0_, bf16[128,2048]{1,0:T(8,128)(2,1)} %copy-done.9, f32[128,2048]{1,0:T(8,128)} %get-tuple-element.95.refs_2_, bf16[128,2048]{1,0:T(8,128)(2,1)} %copy-done.10, bf16[512,2048]{1,0:T(8,128)(2,1)} %refs_2_.5, ...), custom_call_target="tpu_custom_call" | custom-call | flops 1 | bytes 1 | tf_op jit(solution)/shard_map/scores/pallas_call | solution.py:162
  168.6 1.3 convert_add_fusion.1
  169.9 10.1 %product.7 = (f32[128,2048]{1,0:T(8,128)}, bf16[128,2048]{1,0:T(8,128)(2,1)}, f32[128,2048]{1,0:T(8,128)}, bf16[128,2048]{1,0:T(8,128)(2,1)}) custom-call(s32[3]{0:T(128)} %pad_add_fusion.refs_0_.flags, bf16[512,2048]{1,0:T(8,128)(2,1)} %collective-permute-done.11.refs_1_, bf16[2048,2048]{1,0:T(8,128)(2,1)} %refs_2_.3), custom_call_target="tpu_custom_call" | custom-call | flops 1 | bytes 1 | tf_op jit(solution)/shard_map/product/pallas_call | solution.py:90
  180.5 5.0 %collective-permute-start.21 = (bf16[4,128,512]{2,1,0:T(8,128)(2,1)}, bf16[4,128,512]{2,1,0:T(8,128)(2,1)S(1)}, u32[]{:S(2)}, u32[]{:S(2)}) collective-permute-start(bf16[4,128,512]{2,1,0:T(8,128)(2,1)} %get-tuple-element.109), channel_id=1, source_target_pairs={{0,2},{3,1},{1,3},{2,0},{4,6},{7,5},{5,7},{6,4},{8,10},{11,9},{9,1... | collective-permute-start | bytes 1572872 | tf_op jit(solution)/shard_map/ppermute | solution.py:190
  185.5 1.5 collective-permute-start.22
  187.0 0.8 copy-done.12
  187.8 3.5 %fold.10 = (f32[64,2048]{1,0:T(8,128)}, bf16[64,2048]{1,0:T(8,128)(2,1)}) custom-call(s32[3]{0:T(128)} %pad_add_fusion.refs_0_.flags, f32[128,2048]{1,0:T(8,128)} %get-tuple-element.100.kept, bf16[128,2048]{1,0:T(8,128)(2,1)} %copy-done.12), custom_call_target="tpu_custom_call" | custom-call | flops 1 | bytes 1 | tf_op jit(solution)/shard_map/fold/pallas_call | solution.py:126
  191.3 1.5 collective-permute-start.19
  192.8 0.8 copy-done.11
  193.6 3.5 %fold.11 = (f32[64,2048]{1,0:T(8,128)}, bf16[64,2048]{1,0:T(8,128)(2,1)}) custom-call(s32[3]{0:T(128)} %pad_add_fusion.refs_0_.flags, f32[128,2048]{1,0:T(8,128)} %get-tuple-element.112.kept, bf16[128,2048]{1,0:T(8,128)(2,1)} %copy-done.11), custom_call_target="tpu_custom_call" | custom-call | flops 1 | bytes 1 | tf_op jit(solution)/shard_map/fold/pallas_call | solution.py:126
  197.0 0.5 collective-permute-start.27
  197.6 2.1 collective-permute-done.19.refs_1_
  199.6 0.7 copy-done.13
  200.3 6.7 %scores.6 = bf16[4,64,512]{2,1,0:T(8,128)(2,1)} custom-call(f32[64,2048]{1,0:T(8,128)} %get-tuple-element.102.refs_0_, bf16[64,2048]{1,0:T(8,128)(2,1)} %copy-done.13, bf16[512,2048]{1,0:T(8,128)(2,1)} %refs_2_.5, bf16[512,2048]{1,0:T(8,128)(2,1)} %copy-done.2, bf16[512,2048]{1,0:T(8,128)(2,1)} %collective-permute-done.9.refs_6_.refs_4_, ...), custom_call_target="tpu_custom_call" | custom-call | flops 1 | bytes 1 | tf_op jit(solution)/shard_map/scores/pallas_call | solution.py:162
  207.1 4.5 %collective-permute-start.20 = (bf16[4,64,512]{2,1,0:T(8,128)(2,1)}, bf16[4,64,512]{2,1,0:T(8,128)(2,1)S(1)}, u32[]{:S(2)}, u32[]{:S(2)}) collective-permute-start(bf16[4,64,512]{2,1,0:T(8,128)(2,1)} %scores.6), channel_id=1, source_target_pairs={{0,3},{3,0},{4,7},{7,4},{8,11},{11,8},{12,15},{15,12},{16,19},{19,... | collective-permute-start | bytes 786440 | tf_op jit(solution)/shard_map/ppermute | solution.py:190
  211.7 0.7 copy-done.14
  212.4 6.7 %scores.7 = bf16[4,64,512]{2,1,0:T(8,128)(2,1)} custom-call(f32[64,2048]{1,0:T(8,128)} %get-tuple-element.114.refs_0_, bf16[64,2048]{1,0:T(8,128)(2,1)} %copy-done.14, bf16[512,2048]{1,0:T(8,128)(2,1)} %refs_2_.5, bf16[512,2048]{1,0:T(8,128)(2,1)} %copy-done.2, bf16[512,2048]{1,0:T(8,128)(2,1)} %collective-permute-done.9.refs_6_.refs_4_, ...), custom_call_target="tpu_custom_call" | custom-call | flops 1 | bytes 1 | tf_op jit(solution)/shard_map/scores/pallas_call | solution.py:162
  219.1 3.1 %collective-permute-start.28 = (bf16[4,64,512]{2,1,0:T(8,128)(2,1)}, bf16[4,64,512]{2,1,0:T(8,128)(2,1)S(1)}, u32[]{:S(2)}, u32[]{:S(2)}) collective-permute-start(bf16[4,64,512]{2,1,0:T(8,128)(2,1)} %scores.7), channel_id=1, source_target_pairs={{0,3},{3,0},{4,7},{7,4},{8,11},{11,8},{12,15},{15,12},{16,19},{19,... | collective-permute-start | bytes 786440 | tf_op jit(solution)/shard_map/ppermute | solution.py:190
  222.2 1.3 convert_add_fusion
  223.5 6.3 %collective-permute-done.28 = bf16[4,64,512]{2,1,0:T(8,128)(2,1)S(1)} collective-permute-done((bf16[4,64,512]{2,1,0:T(8,128)(2,1)}, bf16[4,64,512]{2,1,0:T(8,128)(2,1)S(1)}, u32[]{:S(2)}, u32[]{:S(2)}) %collective-permute-start.28) | collective-permute-done | bytes 262176 | tf_op jit(solution)/shard_map/ppermute | solution.py:190
  230.3 2.0 collective-permute-start.23
  232.5 1.9 collective-permute-start.29
  234.5 2.4 collective-permute-done.23
  236.9 3.5 %collective-permute-done.25 = f32[64,640]{1,0:T(8,128)S(1)} collective-permute-done((f32[64,640]{1,0:T(8,128)S(1)}, f32[64,640]{1,0:T(8,128)S(1)}, u32[]{:S(2)}, u32[]{:S(2)}) %collective-permute-start.25) | collective-permute-done | bytes 163872 | tf_op jit(solution)/shard_map/ppermute | solution.py:193
  240.5 3.2 %collective-permute-done.29 = f32[64,640]{1,0:T(8,128)S(1)} collective-permute-done((f32[64,640]{1,0:T(8,128)S(1)}, f32[64,640]{1,0:T(8,128)S(1)}, u32[]{:S(2)}, u32[]{:S(2)}) %collective-permute-start.29) | collective-permute-done | bytes 163872 | tf_op jit(solution)/shard_map/ppermute | solution.py:193
  243.8 2.1 collective-permute-done.31
  246.7 0.7 slice_reduce_fusion
  247.4 1.3 copy.11
  (69 shorter events, 2.9 us)
Async XLA Ops:
  0.6 17.6 %copy-start = (s32[512,16]{0,1:T(8,128)S(1)}, s32[512,16]{0,1:T(8,128)}, u32[]{:S(2)}) copy-start(s32[512,16]{0,1:T(8,128)} %param.7) | copy-start | bytes 98308
  0.6 49.0 %collective-permute-start = (bf16[512,2048]{1,0:T(8,128)(2,1)}, bf16[512,2048]{1,0:T(8,128)(2,1)}, u32[]{:S(2)}, u32[]{:S(2)}) collective-permute-start(bf16[512,2048]{1,0:T(8,128)(2,1)} %refs_1_.1), channel_id=1, source_target_pairs={{0,1},{1,0},{2,3},{3,2},{4,5},{5,4},{6,7},{7,6},{8,9},{9,8},{10,11... | collective-permute-start | bytes 6291464 | tf_op jit(solution)/shard_map/ppermute | solution.py:190
  3.7 46.0 %collective-permute-start.1 = (bf16[512,2048]{1,0:T(8,128)(2,1)}, bf16[512,2048]{1,0:T(8,128)(2,1)}, u32[]{:S(2)}, u32[]{:S(2)}) collective-permute-start(bf16[512,2048]{1,0:T(8,128)(2,1)} %refs_1_.1), channel_id=1, source_target_pairs={{1,2},{2,1},{5,6},{6,5},{9,10},{10,9},{13,14},{14,13},{17,18},{18,... | collective-permute-start | bytes 6291464 | tf_op jit(solution)/shard_map/ppermute | solution.py:190
  5.7 44.0 %collective-permute-start.3 = (bf16[512,2048]{1,0:T(8,128)(2,1)}, bf16[512,2048]{1,0:T(8,128)(2,1)S(1)}, u32[]{:S(2)}, u32[]{:S(2)}) collective-permute-start(bf16[512,2048]{1,0:T(8,128)(2,1)} %refs_2_.5), channel_id=1, source_target_pairs={{0,4},{4,0},{8,12},{12,8},{1,5},{5,1},{9,13},{13,9},{2,6},{6,2},{1... | collective-permute-start | bytes 6291464 | tf_op jit(solution)/shard_map/ppermute | solution.py:193
  5.7 48.4 %collective-permute-start.9 = (bf16[512,2048]{1,0:T(8,128)(2,1)}, bf16[512,2048]{1,0:T(8,128)(2,1)}, u32[]{:S(2)}, u32[]{:S(2)}) collective-permute-start(bf16[512,2048]{1,0:T(8,128)(2,1)} %refs_2_.5), channel_id=1, source_target_pairs={{0,8},{4,12},{8,0},{12,4},{1,9},{5,13},{9,1},{13,5},{2,10},{6,14},... | collective-permute-start | bytes 6291464 | tf_op jit(solution)/shard_map/ppermute | solution.py:193
  17.9 4.0 %collective-permute-start.2 = (bf16[256,2048]{1,0:T(8,128)(2,1)}, bf16[256,2048]{1,0:T(8,128)(2,1)}, u32[]{:S(2)}, u32[]{:S(2)}) collective-permute-start(bf16[256,2048]{1,0:T(8,128)(2,1)} %get-tuple-element.60), channel_id=1, source_target_pairs={{0,4},{4,0},{8,12},{12,8},{1,5},{5,1},{9,13},{13,9},{2,6},{6,2},{1... | collective-permute-start | bytes 3145736 | tf_op jit(solution)/shard_map/ppermute | solution.py:193
  49.7 14.5 %copy-start.2 = (bf16[512,2048]{1,0:T(8,128)(2,1)}, bf16[512,2048]{1,0:T(8,128)(2,1)S(1)}, u32[]{:S(2)}) copy-start(bf16[512,2048]{1,0:T(8,128)(2,1)S(1)} %collective-permute-done.3.refs_5_.refs_3_) | copy-start | bytes 6291460
  49.7 51.6 %collective-permute-start.4 = (bf16[512,2048]{1,0:T(8,128)(2,1)}, bf16[512,2048]{1,0:T(8,128)(2,1)}, u32[]{:S(2)}, u32[]{:S(2)}) collective-permute-start(bf16[512,2048]{1,0:T(8,128)(2,1)} %collective-permute-done.refs_2_.refs_3_), channel_id=1, source_target_pairs={{1,2},{2,1},{5,6},{6,5},{9,10},{10,9},{13,14},{14,13},{17,18},{18,... | collective-permute-start | bytes 6291464 | tf_op jit(solution)/shard_map/ppermute | solution.py:190
  51.7 52.1 %collective-permute-start.5 = (bf16[512,2048]{1,0:T(8,128)(2,1)}, bf16[512,2048]{1,0:T(8,128)(2,1)}, u32[]{:S(2)}, u32[]{:S(2)}) collective-permute-start(bf16[512,2048]{1,0:T(8,128)(2,1)} %collective-permute-done.1.refs_1_), channel_id=1, source_target_pairs={{1,0},{2,3},{5,4},{6,7},{9,8},{10,11},{13,12},{14,15},{17,16},{18,... | collective-permute-start | bytes 6291464 | tf_op jit(solution)/shard_map/ppermute | solution.py:190
  54.1 49.8 %collective-permute-start.10 = (bf16[512,2048]{1,0:T(8,128)(2,1)}, bf16[512,2048]{1,0:T(8,128)(2,1)}, u32[]{:S(2)}, u32[]{:S(2)}) collective-permute-start(bf16[512,2048]{1,0:T(8,128)(2,1)} %collective-permute-done.9.refs_6_.refs_4_), channel_id=1, source_target_pairs={{0,4},{4,0},{8,12},{12,8},{1,5},{5,1},{9,13},{13,9},{2,6},{6,2},{1... | collective-permute-start | bytes 6291464 | tf_op jit(solution)/shard_map/ppermute | solution.py:193
  64.2 3.1 %collective-permute-start.7 = (bf16[256,2048]{1,0:T(8,128)(2,1)}, bf16[256,2048]{1,0:T(8,128)(2,1)S(1)}, u32[]{:S(2)}, u32[]{:S(2)}) collective-permute-start(bf16[256,2048]{1,0:T(8,128)(2,1)} %get-tuple-element.68), channel_id=1, source_target_pairs={{0,4},{4,0},{8,12},{12,8},{1,5},{5,1},{9,13},{13,9},{2,6},{6,2},{1... | collective-permute-start | bytes 3145736 | tf_op jit(solution)/shard_map/ppermute | solution.py:193
  64.7 26.2 %collective-permute-start.6 = (f32[128,2048]{1,0:T(8,128)}, f32[128,2048]{1,0:T(8,128)S(1)}, u32[]{:S(2)}, u32[]{:S(2)}) collective-permute-start(f32[128,2048]{1,0:T(8,128)} %get-tuple-element.66), channel_id=1, source_target_pairs={{0,8},{4,12},{8,0},{12,4},{1,9},{5,13},{9,1},{13,5},{2,10},{6,14},... | collective-permute-start | bytes 3145736 | tf_op jit(solution)/shard_map/ppermute | solution.py:193
  67.2 1.0 copy-start.6
  72.2 29.1 %collective-permute-start.8 = (bf16[128,2048]{1,0:T(8,128)(2,1)}, bf16[128,2048]{1,0:T(8,128)(2,1)S(1)}, u32[]{:S(2)}, u32[]{:S(2)}) collective-permute-start(bf16[128,2048]{1,0:T(8,128)(2,1)} %get-tuple-element.70), channel_id=1, source_target_pairs={{0,8},{4,12},{8,0},{12,4},{1,9},{5,13},{9,1},{13,5},{2,10},{6,14},... | collective-permute-start | bytes 1572872 | tf_op jit(solution)/shard_map/ppermute | solution.py:193
  91.0 28.7 %copy-start.3 = (f32[128,2048]{1,0:T(8,128)}, f32[128,2048]{1,0:T(8,128)S(1)}, u32[]{:S(2)}) copy-start(f32[128,2048]{1,0:T(8,128)S(1)} %collective-permute-done.6.refs_3_) | copy-start | bytes 3145732
  101.3 18.4 %copy-start.8 = (bf16[128,2048]{1,0:T(8,128)(2,1)}, bf16[128,2048]{1,0:T(8,128)(2,1)S(1)}, u32[]{:S(2)}) copy-start(bf16[128,2048]{1,0:T(8,128)(2,1)S(1)} %collective-permute-done.8.refs_1_) | copy-start | bytes 1572868
  103.8 66.0 %collective-permute-start.11 = (bf16[512,2048]{1,0:T(8,128)(2,1)}, bf16[512,2048]{1,0:T(8,128)(2,1)}, u32[]{:S(2)}, u32[]{:S(2)}) collective-permute-start(bf16[512,2048]{1,0:T(8,128)(2,1)} %collective-permute-done.4.refs_1_), channel_id=1, source_target_pairs={{1,0},{2,3},{5,4},{6,7},{9,8},{10,11},{13,12},{14,15},{17,16},{18,... | collective-permute-start | bytes 6291464 | tf_op jit(solution)/shard_map/ppermute | solution.py:190
  119.7 2.9 %collective-permute-start.13 = (bf16[256,2048]{1,0:T(8,128)(2,1)}, bf16[256,2048]{1,0:T(8,128)(2,1)S(1)}, u32[]{:S(2)}, u32[]{:S(2)}) collective-permute-start(bf16[256,2048]{1,0:T(8,128)(2,1)} %get-tuple-element.79), channel_id=1, source_target_pairs={{0,4},{4,0},{8,12},{12,8},{1,5},{5,1},{9,13},{13,9},{2,6},{6,2},{1... | collective-permute-start | bytes 3145736 | tf_op jit(solution)/shard_map/ppermute | solution.py:193
  119.8 7.8 %collective-permute-start.12 = (bf16[256,2048]{1,0:T(8,128)(2,1)}, bf16[256,2048]{1,0:T(8,128)(2,1)S(1)}, u32[]{:S(2)}, u32[]{:S(2)}) collective-permute-start(bf16[256,2048]{1,0:T(8,128)(2,1)} %get-tuple-element.76), channel_id=1, source_target_pairs={{0,4},{4,0},{8,12},{12,8},{1,5},{5,1},{9,13},{13,9},{2,6},{6,2},{1... | collective-permute-start | bytes 3145736 | tf_op jit(solution)/shard_map/ppermute | solution.py:193
  122.7 1.0 copy-start.7
  127.6 1.0 copy-start.5
  128.6 5.6 %copy-start.15 = (bf16[128,2048]{1,0:T(8,128)(2,1)S(1)}, bf16[128,2048]{1,0:T(8,128)(2,1)}, u32[]{:S(2)}) copy-start(bf16[128,2048]{1,0:T(8,128)(2,1)} %get-tuple-element.96) | copy-start | bytes 1572868
  132.7 20.5 %collective-permute-start.16 = (bf16[128,2048]{1,0:T(8,128)(2,1)}, bf16[128,2048]{1,0:T(8,128)(2,1)S(1)}, u32[]{:S(2)}, u32[]{:S(2)}) collective-permute-start(bf16[128,2048]{1,0:T(8,128)(2,1)} %get-tuple-element.94), channel_id=1, source_target_pairs={{0,8},{4,12},{8,0},{12,4},{1,9},{5,13},{9,1},{13,5},{2,10},{6,14},... | collective-permute-start | bytes 1572872 | tf_op jit(solution)/shard_map/ppermute | solution.py:193
  134.2 23.9 %collective-permute-start.17 = (bf16[128,2048]{1,0:T(8,128)(2,1)S(1)}, bf16[128,2048]{1,0:T(8,128)(2,1)S(1)}, u32[]{:S(2)}, u32[]{:S(2)}) collective-permute-start(bf16[128,2048]{1,0:T(8,128)(2,1)S(1)} %copy-done.15), channel_id=1, source_target_pairs={{0,8},{4,12},{8,0},{12,4},{1,9},{5,13},{9,1},{13,5},{2,10},{6,14},... | collective-permute-start | bytes 1572872 | tf_op jit(solution)/shard_map/ppermute | solution.py:193
  144.6 24.0 %collective-permute-start.14 = (bf16[4,128,512]{2,1,0:T(8,128)(2,1)}, bf16[4,128,512]{2,1,0:T(8,128)(2,1)S(1)}, u32[]{:S(2)}, u32[]{:S(2)}) collective-permute-start(bf16[4,128,512]{2,1,0:T(8,128)(2,1)} %get-tuple-element.92), channel_id=1, source_target_pairs={{0,1},{3,2},{4,5},{7,6},{8,9},{11,10},{12,13},{15,14},{16,17},{19,... | collective-permute-start | bytes 1572872 | tf_op jit(solution)/shard_map/ppermute | solution.py:190
  151.8 16.8 %collective-permute-start.15 = (bf16[4,128,512]{2,1,0:T(8,128)(2,1)}, bf16[4,128,512]{2,1,0:T(8,128)(2,1)}, u32[]{:S(2)}, u32[]{:S(2)}) collective-permute-start(bf16[4,128,512]{2,1,0:T(8,128)(2,1)} %get-tuple-element.92), channel_id=1, source_target_pairs={{1,2},{2,1},{5,6},{6,5},{9,10},{10,9},{13,14},{14,13},{17,18},{18,... | collective-permute-start | bytes 1572872 | tf_op jit(solution)/shard_map/ppermute | solution.py:190
  153.2 4.9 %copy-start.9 = (bf16[128,2048]{1,0:T(8,128)(2,1)}, bf16[128,2048]{1,0:T(8,128)(2,1)S(1)}, u32[]{:S(2)}) copy-start(bf16[128,2048]{1,0:T(8,128)(2,1)S(1)} %collective-permute-done.16.refs_1_) | copy-start | bytes 1572868
  158.1 0.8 copy-start.10
  158.9 9.7 %copy-start.4 = (f32[4,128,512]{2,1,0:T(8,128)S(1)}, f32[4,128,512]{2,1,0:T(8,128)}, u32[]{:S(2)}) copy-start(f32[4,128,512]{2,1,0:T(8,128)} %get-tuple-element.91) | copy-start | bytes 3145732
  180.0 7.1 %collective-permute-start.18 = (bf16[128,2048]{1,0:T(8,128)(2,1)}, bf16[128,2048]{1,0:T(8,128)(2,1)S(1)}, u32[]{:S(2)}, u32[]{:S(2)}) collective-permute-start(bf16[128,2048]{1,0:T(8,128)(2,1)} %get-tuple-element.101), channel_id=1, source_target_pairs={{0,4},{4,0},{8,12},{12,8},{1,5},{5,1},{9,13},{13,9},{2,6},{6,2},{1... | collective-permute-start | bytes 1572872 | tf_op jit(solution)/shard_map/ppermute | solution.py:193
  180.0 12.7 %collective-permute-start.26 = (bf16[128,2048]{1,0:T(8,128)(2,1)}, bf16[128,2048]{1,0:T(8,128)(2,1)S(1)}, u32[]{:S(2)}, u32[]{:S(2)}) collective-permute-start(bf16[128,2048]{1,0:T(8,128)(2,1)} %get-tuple-element.113), channel_id=1, source_target_pairs={{0,4},{4,0},{8,12},{12,8},{1,5},{5,1},{9,13},{13,9},{2,6},{6,2},{1... | collective-permute-start | bytes 1572872 | tf_op jit(solution)/shard_map/ppermute | solution.py:193
  180.5 41.6 %collective-permute-start.21 = (bf16[4,128,512]{2,1,0:T(8,128)(2,1)}, bf16[4,128,512]{2,1,0:T(8,128)(2,1)S(1)}, u32[]{:S(2)}, u32[]{:S(2)}) collective-permute-start(bf16[4,128,512]{2,1,0:T(8,128)(2,1)} %get-tuple-element.109), channel_id=1, source_target_pairs={{0,2},{3,1},{1,3},{2,0},{4,6},{7,5},{5,7},{6,4},{8,10},{11,9},{9,1... | collective-permute-start | bytes 1572872 | tf_op jit(solution)/shard_map/ppermute | solution.py:190
  185.5 36.7 %collective-permute-start.22 = (bf16[4,128,512]{2,1,0:T(8,128)(2,1)}, bf16[4,128,512]{2,1,0:T(8,128)(2,1)}, u32[]{:S(2)}, u32[]{:S(2)}) collective-permute-start(bf16[4,128,512]{2,1,0:T(8,128)(2,1)} %get-tuple-element.110), channel_id=1, source_target_pairs={{1,0},{2,3},{5,4},{6,7},{9,8},{10,11},{13,12},{14,15},{17,16},{18,... | collective-permute-start | bytes 1572872 | tf_op jit(solution)/shard_map/ppermute | solution.py:190
  187.0 0.8 copy-start.12
  191.3 8.4 %collective-permute-start.19 = (bf16[64,2048]{1,0:T(8,128)(2,1)}, bf16[64,2048]{1,0:T(8,128)(2,1)S(1)}, u32[]{:S(2)}, u32[]{:S(2)}) collective-permute-start(bf16[64,2048]{1,0:T(8,128)(2,1)} %get-tuple-element.103), channel_id=1, source_target_pairs={{0,8},{4,12},{8,0},{12,4},{1,9},{5,13},{9,1},{13,5},{2,10},{6,14},... | collective-permute-start | bytes 786440 | tf_op jit(solution)/shard_map/ppermute | solution.py:193
  192.8 0.8 copy-start.11
  197.0 14.6 %collective-permute-start.27 = (bf16[64,2048]{1,0:T(8,128)(2,1)}, bf16[64,2048]{1,0:T(8,128)(2,1)S(1)}, u32[]{:S(2)}, u32[]{:S(2)}) collective-permute-start(bf16[64,2048]{1,0:T(8,128)(2,1)} %get-tuple-element.115), channel_id=1, source_target_pairs={{0,8},{4,12},{8,0},{12,4},{1,9},{5,13},{9,1},{13,5},{2,10},{6,14},... | collective-permute-start | bytes 786440 | tf_op jit(solution)/shard_map/ppermute | solution.py:193
  199.6 0.7 copy-start.13
  207.1 16.4 %collective-permute-start.20 = (bf16[4,64,512]{2,1,0:T(8,128)(2,1)}, bf16[4,64,512]{2,1,0:T(8,128)(2,1)S(1)}, u32[]{:S(2)}, u32[]{:S(2)}) collective-permute-start(bf16[4,64,512]{2,1,0:T(8,128)(2,1)} %scores.6), channel_id=1, source_target_pairs={{0,3},{3,0},{4,7},{7,4},{8,11},{11,8},{12,15},{15,12},{16,19},{19,... | collective-permute-start | bytes 786440 | tf_op jit(solution)/shard_map/ppermute | solution.py:190
  211.6 0.7 copy-start.14
  219.1 10.7 %collective-permute-start.28 = (bf16[4,64,512]{2,1,0:T(8,128)(2,1)}, bf16[4,64,512]{2,1,0:T(8,128)(2,1)S(1)}, u32[]{:S(2)}, u32[]{:S(2)}) collective-permute-start(bf16[4,64,512]{2,1,0:T(8,128)(2,1)} %scores.7), channel_id=1, source_target_pairs={{0,3},{3,0},{4,7},{7,4},{8,11},{11,8},{12,15},{15,12},{16,19},{19,... | collective-permute-start | bytes 786440 | tf_op jit(solution)/shard_map/ppermute | solution.py:190
  230.3 6.6 %collective-permute-start.23 = (f32[64,640]{1,0:T(8,128)S(1)}, f32[64,640]{1,0:T(8,128)S(1)}, u32[]{:S(2)}, u32[]{:S(2)}) collective-permute-start(f32[64,640]{1,0:T(8,128)S(1)} %get-tuple-element.142), channel_id=1, source_target_pairs={{0,8},{4,12},{8,0},{12,4},{1,9},{5,13},{9,1},{13,5},{2,10},{6,14},... | collective-permute-start | bytes 491528 | tf_op jit(solution)/shard_map/ppermute | solution.py:193
  232.3 4.6 %collective-permute-start.24 = (f32[64,640]{1,0:T(8,128)S(1)}, f32[64,640]{1,0:T(8,128)S(1)}, u32[]{:S(2)}, u32[]{:S(2)}) collective-permute-start(f32[64,640]{1,0:T(8,128)S(1)} %get-tuple-element.141), channel_id=1, source_target_pairs={{0,4},{4,0},{8,12},{12,8},{1,5},{5,1},{9,13},{13,9},{2,6},{6,2},{1... | collective-permute-start | bytes 491528 | tf_op jit(solution)/shard_map/ppermute | solution.py:193
  232.3 8.1 %collective-permute-start.25 = (f32[64,640]{1,0:T(8,128)S(1)}, f32[64,640]{1,0:T(8,128)S(1)}, u32[]{:S(2)}, u32[]{:S(2)}) collective-permute-start(f32[64,640]{1,0:T(8,128)S(1)} %get-tuple-element.140), channel_id=1, source_target_pairs={{0,12},{4,8},{8,4},{12,0},{1,13},{5,9},{9,5},{13,1},{2,14},{6,10},... | collective-permute-start | bytes 491528 | tf_op jit(solution)/shard_map/ppermute | solution.py:193
  232.5 11.2 %collective-permute-start.29 = (f32[64,640]{1,0:T(8,128)S(1)}, f32[64,640]{1,0:T(8,128)S(1)}, u32[]{:S(2)}, u32[]{:S(2)}) collective-permute-start(f32[64,640]{1,0:T(8,128)S(1)} %get-tuple-element.134), channel_id=1, source_target_pairs={{0,8},{4,12},{8,0},{12,4},{1,9},{5,13},{9,1},{13,5},{2,10},{6,14},... | collective-permute-start | bytes 491528 | tf_op jit(solution)/shard_map/ppermute | solution.py:193
  234.5 9.3 %collective-permute-start.30 = (f32[64,640]{1,0:T(8,128)S(1)}, f32[64,640]{1,0:T(8,128)S(1)}, u32[]{:S(2)}, u32[]{:S(2)}) collective-permute-start(f32[64,640]{1,0:T(8,128)S(1)} %get-tuple-element.135), channel_id=1, source_target_pairs={{0,4},{4,0},{8,12},{12,8},{1,5},{5,1},{9,13},{13,9},{2,6},{6,2},{1... | collective-permute-start | bytes 491528 | tf_op jit(solution)/shard_map/ppermute | solution.py:193
  236.9 9.0 %collective-permute-start.31 = (f32[64,640]{1,0:T(8,128)S(1)}, f32[64,640]{1,0:T(8,128)S(1)}, u32[]{:S(2)}, u32[]{:S(2)}) collective-permute-start(f32[64,640]{1,0:T(8,128)S(1)} %get-tuple-element.136), channel_id=1, source_target_pairs={{0,12},{4,8},{8,4},{12,0},{1,13},{5,9},{9,5},{13,1},{2,14},{6,10},... | collective-permute-start | bytes 491528 | tf_op jit(solution)/shard_map/ppermute | solution.py:193
  246.6 2.2 copy-start.1

commit v6 on v5

--- a/solution.py
+++ b/solution.py
@@ -36,73 +36,59 @@
 
 
 SMALL = pl.CostEstimate(flops=1, bytes_accessed=1, transcendentals=0)
-PARAMS = pltpu.CompilerParams(vmem_limit_bytes=60 * 2**20)
+PARAMS = pltpu.CompilerParams(vmem_limit_bytes=16 * 2**20)
+
+
+VMEM = pl.BlockSpec(memory_space=pltpu.VMEM)
 
 
 def product_body(choices, parts, flags, *refs):
     count = sum(len(choice) for choice in choices)
-    blocks, fisher, outs, (held, sems) = refs[:count], refs[count], refs[count + 1 : -2], refs[-2:]
-    block_rows = blocks[0].shape[0]
-
-    @pl.when(pl.program_id(0) == 0)
-    def _():
-        places = [held.at[pl.ds(u * block_rows, block_rows)] for u in range(len(choices))]
-        first = 0
-        for u, choice in enumerate(choices):
-            if len(choice) == 1:
-                pltpu.make_async_copy(blocks[first], places[u], sems.at[u]).start()
-            else:
-
-                @pl.when(flags[2] == 1)
-                def _():
-                    pltpu.make_async_copy(blocks[first], places[u], sems.at[u]).start()
-
-                @pl.when(flags[2] == 0)
-                def _():
-                    pltpu.make_async_copy(blocks[first + 1], places[u], sems.at[u]).start()
-
-            first += len(choice)
-        for u in range(len(choices)):
-            pltpu.make_async_copy(blocks[0], places[u], sems.at[u]).wait()
-
-    quarter = block_rows // 4
+    blocks, fisher, outs = refs[:count], refs[count], refs[count + 1 :]
+    quarter = blocks[0].shape[0] // 4
     rows = quarter // parts
-    first = flags[0] == 0
-    for u in range(len(choices)):
-        block = held[u * block_rows : (u + 1) * block_rows]
-        value = jnp.dot(block, fisher[...], preferred_element_type=F32)
-        for p in range(parts):
-            kept, sent = outs[2 * (u * parts + p) :][:2]
-            for chip in range(2):
-                low, high = (
-                    value[(2 * core + chip) * quarter + p * rows :][:rows] for core in range(2)
-                )
-                kept[chip * rows : (chip + 1) * rows] = jnp.where(first, low, high)
-                sent[chip * rows : (chip + 1) * rows] = jnp.where(first, high, low).astype(BF16)
+    mine = flags[0] == 0
+
+    def multiply(block, outs):
+        @pl.loop(0, fisher.shape[1] // COLUMNS)
+        def _(n):
+            columns = pl.ds(pl.multiple_of(n * COLUMNS, COLUMNS), COLUMNS)
+            value = jnp.dot(block[...], fisher[:, columns], preferred_element_type=F32)
+            for p in range(parts):
+                kept, sent = outs[2 * p : 2 * p + 2]
+                for chip in range(2):
+                    low, high = (
+                        value[(2 * core + chip) * quarter + p * rows :][:rows] for core in range(2)
+                    )
+                    place = pl.ds(chip * rows, rows)
+                    kept[place, columns] = jnp.where(mine, low, high)
+                    sent[place, columns] = jnp.where(mine, high, low).astype(BF16)
+
+    first = 0
+    for u, choice in enumerate(choices):
+        these = outs[2 * parts * u : 2 * parts * (u + 1)]
+        if len(choice) == 1:
+            multiply(blocks[first], these)
+        else:
+            pl.when(flags[2] == 1)(lambda: multiply(blocks[first], these))
+            pl.when(flags[2] == 0)(lambda: multiply(blocks[first + 1], these))
+        first += len(choice)
 
 
 def product(flags, choices, fisher, parts=1):
-    rows, depth = choices[0][0].shape
+    half = choices[0][0].shape[0] // 2 // parts
     columns = fisher.shape[1]
-    half = rows // 2 // parts
     blocks = [block for choice in choices for block in choice]
     outs = len(choices) * parts
     return pl.pallas_call(
         lambda *refs: product_body(choices, parts, *refs),
-        grid=(columns // COLUMNS,),
-        in_specs=[pl.BlockSpec(memory_space=pltpu.SMEM)]
-        + [pl.BlockSpec(memory_space=pl.ANY)] * len(blocks)
-        + [pl.BlockSpec((depth, COLUMNS), lambda n: (0, n))],
-        out_specs=[pl.BlockSpec((half, COLUMNS), lambda n: (0, n))] * (2 * outs),
+        in_specs=[pl.BlockSpec(memory_space=pltpu.SMEM)] + [VMEM] * (len(blocks) + 1),
+        out_specs=[VMEM] * (2 * outs),
         out_shape=[
             jax.ShapeDtypeStruct((half, columns), F32),
             jax.ShapeDtypeStruct((half, columns), BF16),
         ]
         * outs,
-        scratch_shapes=[
-            pltpu.VMEM((len(choices) * rows, depth), BF16),
-            pltpu.SemaphoreType.DMA((len(choices),)),
-        ],
         compiler_params=PARAMS,
         cost_estimate=SMALL,
         name="product",
@@ -110,24 +96,24 @@
 
 
 def fold_body(flags, kept, got, kept_out, sent_out):
-    value = kept[...] + got[...].astype(F32)
-    half = value.shape[0] // 2
+    half = kept.shape[0] // 2
     first = flags[1] == 0
-    low, high = value[:half], value[half:]
-    kept_out[...] = jnp.where(first, low, high)
-    sent_out[...] = jnp.where(first, high, low).astype(sent_out.dtype)
+
+    @pl.loop(0, kept.shape[1] // COLUMNS)
+    def _(n):
+        columns = pl.ds(pl.multiple_of(n * COLUMNS, COLUMNS), COLUMNS)
+        value = kept[:, columns] + got[:, columns].astype(F32)
+        low, high = value[:half], value[half:]
+        kept_out[:, columns] = jnp.where(first, low, high)
+        sent_out[:, columns] = jnp.where(first, high, low).astype(sent_out.dtype)
 
 
 def fold(flags, kept, got, sent_as):
     rows, columns = kept.shape
-    tile = COLUMNS
-    before = pl.BlockSpec((rows, tile), lambda n: (0, n))
-    after = pl.BlockSpec((rows // 2, tile), lambda n: (0, n))
     return pl.pallas_call(
         fold_body,
-        grid=(columns // tile,),
-        in_specs=[pl.BlockSpec(memory_space=pltpu.SMEM), before, before],
-        out_specs=[after, after],
+        in_specs=[pl.BlockSpec(memory_space=pltpu.SMEM), VMEM, VMEM],
+        out_specs=[VMEM, VMEM],
         out_shape=[
             jax.ShapeDtypeStruct((rows // 2, columns), F32),
             jax.ShapeDtypeStruct((rows // 2, columns), sent_as),
@@ -139,18 +125,14 @@
 
 
 def scores_body(units, *refs):
-    sums, grads, outs, (held, sems) = refs[: 2 * units], refs[2 * units :][:4], refs[-2 - units : -2], refs[-2:]
-    copies = [pltpu.make_async_copy(grads[r], held.at[r], sems.at[r]) for r in range(4)]
-    for copy in copies:
-        copy.start()
+    sums, grads, outs = refs[: 2 * units], refs[2 * units :][:4], refs[2 * units + 4 :]
     values = [sums[2 * u][...] + sums[2 * u + 1][...].astype(F32) for u in range(units)]
     values = [(value.astype(BF16), value) for value in values]
     values = [(high, (value - high.astype(F32)).astype(BF16)) for high, value in values]
     precond = jnp.concatenate([part for value in values for part in value])
     rows = sums[0].shape[0]
     for r in range(4):
-        copies[r].wait()
-        both = dot_t(precond, held[r])
+        both = dot_t(precond, grads[r][...])
         for u in range(units):
             value = both[2 * u * rows :][:rows] + both[(2 * u + 1) * rows :][:rows]
             outs[u][r] = value.astype(outs[u].dtype)
@@ -158,17 +140,12 @@
 
 def partial_scores(units, grads, out_as):
     rows = units[0][0].shape[0]
-    train_rows, depth = grads[0].shape
+    train_rows = grads[0].shape[0]
     return pl.pallas_call(
         lambda *refs: scores_body(len(units), *refs),
-        in_specs=[pl.BlockSpec(memory_space=pltpu.VMEM)] * (2 * len(units))
-        + [pl.BlockSpec(memory_space=pl.ANY)] * 4,
-        out_specs=[pl.BlockSpec(memory_space=pltpu.VMEM)] * len(units),
+        in_specs=[VMEM] * (2 * len(units) + 4),
+        out_specs=[VMEM] * len(units),
         out_shape=[jax.ShapeDtypeStruct((4, rows, train_rows), kind) for kind in out_as],
-        scratch_shapes=[
-            pltpu.VMEM((4, train_rows, depth), BF16),
-            pltpu.SemaphoreType.DMA((4,)),
-        ],
         compiler_params=PARAMS,
         cost_estimate=SMALL,
         name="scores",

time: 250 us -> 218 us (0.87)
  Pallas kernels: 100 us -> 57.5 us
  waiting for transfers between devices: 82.9 us -> 98.1 us
  starting transfers between devices: 47.3 us -> 42.1 us
  local copies, waits for them, and re-layouts: 9.15 us -> 13.7 us
  other arithmetic: 7.91 us -> 5.27 us
    pallas_call x14, Pallas kernels: 100 us -> 57.5 us  [the longest x4 31.6 us: product(): pl.pallas_call(lambda *refs: product_body(choices, parts, *refs), in_spec...]
    ppermute x21, waiting for transfers between devices: 50.3 us -> 65.8 us  [to_other(): return lax.ppermute(value, 'train', [(k, k ^ r) for k in range(4)])]
    ppermute x11, starting transfers between devices: 32.6 us -> 27.6 us  [along(): return lax.ppermute(value, 'test', pairs)]
    unnamed x33 -> x19, local copies, waits for them, and re-layouts: 8.11 us -> 12.7 us
  transfers between devices with their start and end apart: 32 -> 32, of which waited for: 14 -> 17; matrix products, arithmetic and copies ran while one was open for 3% -> 2% of each run, Pallas kernels for 36% -> 24%
where the time goes in v6:
time: 218 us
  waiting for transfers between devices  98.1 us (45%)
  Pallas kernels  57.5 us (26%)
  starting transfers between devices  42.1 us (19%)
  local copies, waits for them, and re-layouts  13.7 us (6%)
  other arithmetic  5.27 us (2%)
    ppermute x21, waiting for transfers between devices, to_other(): return lax.ppermute(value, 'train', [(k, k ^ r) for k in range(4)])  65.8 us
    ppermute x11, waiting for transfers between devices, along(): return lax.ppermute(value, 'test', pairs)  32.3 us
    pallas_call x4, Pallas kernels, product(): pl.pallas_call(lambda *refs: product_body(choices, parts, *refs), in_spec...  31.6 us
    ppermute x11, starting transfers between devices, along(): return lax.ppermute(value, 'test', pairs)  27.6 us
    pallas_call x4, Pallas kernels, partial_scores(): pl.pallas_call(lambda *refs: scores_body(len(units), *refs), in_specs=[VM...  21.2 us
    ppermute x21, starting transfers between devices, to_other(): return lax.ppermute(value, 'train', [(k, k ^ r) for k in range(4)])  14.5 us
    unnamed x19, local copies, waits for them, and re-layouts  12.7 us
    pallas_call x6, Pallas kernels, fold(): pl.pallas_call(fold_body, in_specs=[pl.BlockSpec(memory_space=pltpu.SMEM)...  4.74 us
  transfers between devices with their start and end apart: 32, of which 17 were waited for; matrix products, arithmetic and copies ran while one was open for 2% of the time, Pallas kernels for 24%

profile of v6, /device:TPU:0, one launch (start us, length us, event | category | flops | bytes accessed | tf_op | source)
XLA Modules:
  0.0 217.7 jit_solution(4113810902796046791)
XLA Ops:
  0.6 3.1 %collective-permute-start = (bf16[512,2048]{1,0:T(8,128)(2,1)}, bf16[512,2048]{1,0:T(8,128)(2,1)}, u32[]{:S(2)}, u32[]{:S(2)}) collective-permute-start(bf16[512,2048]{1,0:T(8,128)(2,1)} %refs_1_.1), channel_id=1, source_target_pairs={{0,1},{1,0},{2,3},{3,2},{4,5},{5,4},{6,7},{7,6},{8,9},{9,8},{10,11... | collective-permute-start | bytes 6291464 | tf_op jit(solution)/shard_map/ppermute | solution.py:167
  3.7 2.0 collective-permute-start.1
  5.8 1.5 collective-permute-start.9
  7.3 3.4 %copy-done.2 = bf16[2048,2048]{1,0:T(8,128)(2,1)S(1)} copy-done((bf16[2048,2048]{1,0:T(8,128)(2,1)S(1)}, bf16[2048,2048]{1,0:T(8,128)(2,1)}, u32[]{:S(2)}) %copy-start.2) | copy-done | bytes 8388632
  10.7 1.6 copy-done.8
  12.3 6.6 %product.4 = (f32[256,2048]{1,0:T(8,128)S(1)}, bf16[256,2048]{1,0:T(8,128)(2,1)}) custom-call(s32[3]{0:T(128)S(1)} %pad_add_fusion.refs_0_.flags, bf16[512,2048]{1,0:T(8,128)(2,1)S(1)} %copy-done.8, bf16[2048,2048]{1,0:T(8,128)(2,1)S(1)} %copy-done.2), custom_call_target="tpu_custom_call" | custom-call | flops 1 | bytes 1 | tf_op jit(solution)/shard_map/product/pallas_call | solution.py:83
  18.9 1.4 copy-done.6
  20.8 3.4 %convert_reduce_fusion = f32[4,128,512]{2,1,0:T(8,128)S(1)} fusion(s32[4,512]{1,0:T(4,128)S(1)} %iota_add_fusion, s32[128,16]{1,0:T(8,128)S(1)} %copy.10), kind=kLoop, calls=%fused_computation | loop fusion | flops 12320768 | bytes 1064960 | tf_op jit(solution)/shard_map/reduce_sum | solution.py:189
  24.2 1.6 copy-done.7
  25.8 0.9 fold.6
  26.7 23.0 %collective-permute-done.refs_2_.refs_3_ = bf16[512,2048]{1,0:T(8,128)(2,1)} collective-permute-done((bf16[512,2048]{1,0:T(8,128)(2,1)}, bf16[512,2048]{1,0:T(8,128)(2,1)}, u32[]{:S(2)}, u32[]{:S(2)}) %collective-permute-start) | collective-permute-done | bytes 2097184 | tf_op jit(solution)/shard_map/ppermute | solution.py:167
  49.7 0.8 collective-permute-start.4
  50.5 1.3 collective-permute-start.5
  51.8 2.4 %collective-permute-done.9.refs_6_.refs_4_ = bf16[512,2048]{1,0:T(8,128)(2,1)} collective-permute-done((bf16[512,2048]{1,0:T(8,128)(2,1)}, bf16[512,2048]{1,0:T(8,128)(2,1)}, u32[]{:S(2)}, u32[]{:S(2)}) %collective-permute-start.9) | collective-permute-done | bytes 2097184 | tf_op jit(solution)/shard_map/ppermute | solution.py:170
  54.1 3.4 %copy-done.3 = bf16[2048,2048]{1,0:T(8,128)(2,1)S(1)} copy-done((bf16[2048,2048]{1,0:T(8,128)(2,1)S(1)}, bf16[2048,2048]{1,0:T(8,128)(2,1)}, u32[]{:S(2)}) %copy-start.3) | copy-done | bytes 8388632
  57.5 7.5 %product.5 = (f32[256,2048]{1,0:T(8,128)S(1)}, bf16[256,2048]{1,0:T(8,128)(2,1)S(1)}) custom-call(s32[3]{0:T(128)S(1)} %pad_add_fusion.refs_0_.flags, bf16[512,2048]{1,0:T(8,128)(2,1)} %collective-permute-done.1.refs_1_, bf16[512,2048]{1,0:T(8,128)(2,1)} %collective-permute-done.refs_2_.refs_3_, bf16[2048,2048]{1,0:T(8,128)(2,1)S(1)} %copy-done.3), custom_call_target="tpu_custom_call" | custom-call | flops 1 | bytes 1 | tf_op jit(solution)/shard_map/product/pallas_call | solution.py:83
  65.0 0.6 collective-permute-start.7
  65.6 1.5 collective-permute-start.6
  67.1 0.8 collective-permute-done.7.got
  67.9 0.8 fold.7
  68.7 1.6 collective-permute-start.8
  70.3 21.3 %collective-permute-done.6.refs_3_ = f32[128,2048]{1,0:T(8,128)S(1)} collective-permute-done((f32[128,2048]{1,0:T(8,128)S(1)}, f32[128,2048]{1,0:T(8,128)S(1)}, u32[]{:S(2)}, u32[]{:S(2)}) %collective-permute-start.6) | collective-permute-done | bytes 1048608 | tf_op jit(solution)/shard_map/ppermute | solution.py:170
  91.6 10.4 %collective-permute-done.8.refs_1_ = bf16[128,2048]{1,0:T(8,128)(2,1)S(1)} collective-permute-done((bf16[128,2048]{1,0:T(8,128)(2,1)S(1)}, bf16[128,2048]{1,0:T(8,128)(2,1)S(1)}, u32[]{:S(2)}, u32[]{:S(2)}) %collective-permute-start.8) | collective-permute-done | bytes 524320 | tf_op jit(solution)/shard_map/ppermute | solution.py:170
  102.0 1.8 collective-permute-done.5.refs_2_
  103.7 1.3 collective-permute-start.11
  105.0 11.9 %product.6 = (f32[256,2048]{1,0:T(8,128)S(1)}, bf16[256,2048]{1,0:T(8,128)(2,1)S(1)}, f32[256,2048]{1,0:T(8,128)S(1)}, bf16[256,2048]{1,0:T(8,128)(2,1)S(1)}) custom-call(s32[3]{0:T(128)S(1)} %pad_add_fusion.refs_0_.flags, bf16[512,2048]{1,0:T(8,128)(2,1)S(1)} %collective-permute-done.4.refs_1_, bf16[512,2048]{1,0:T(8,128)(2,1)S(1)} %collective-permute-done.5.refs_2_, ...), custom_call_target="tpu_custom_call" | custom-call | flops 1 | bytes 1 | tf_op jit(solution)/shard_map/product/pallas_call | solution.py:83
  117.1 0.5 collective-permute-start.12
  117.6 2.1 collective-permute-done.13.got
  119.7 0.8 fold.9
  120.5 0.7 collective-permute-done.12.got
  121.2 0.8 fold.8
  122.0 1.6 collective-permute-start.16
  123.6 0.5 collective-permute-start.17
  124.1 6.2 %scores.4 = (bf16[4,128,512]{2,1,0:T(8,128)(2,1)S(1)}, f32[4,128,512]{2,1,0:T(8,128)S(1)}) custom-call(f32[128,2048]{1,0:T(8,128)S(1)} %get-tuple-element.83.refs_0_, bf16[128,2048]{1,0:T(8,128)(2,1)S(1)} %collective-permute-done.8.refs_1_, f32[128,2048]{1,0:T(8,128)S(1)} %get-tuple-element.85.refs_2_, f32[128,2048]{1,0:T(8,128)S(1)} %collective-permute-done.6.refs_3_, ...), custom_call_target="tpu_custom_call" | custom-call | flops 1 | bytes 1 | tf_op jit(solution)/shard_map/scores/pallas_call | solution.py:144
  130.3 5.8 %collective-permute-start.14 = (bf16[4,128,512]{2,1,0:T(8,128)(2,1)S(1)}, bf16[4,128,512]{2,1,0:T(8,128)(2,1)S(1)}, u32[]{:S(2)}, u32[]{:S(2)}) collective-permute-start(bf16[4,128,512]{2,1,0:T(8,128)(2,1)S(1)} %get-tuple-element.92), channel_id=1, source_target_pairs={{0,1},{3,2},{4,5},{7,6},{8,9},{11,10},{12,13},{15,14},{16,17},{19,... | collective-permute-start | bytes 1572872 | tf_op jit(solution)/shard_map/ppermute | solution.py:167
  136.1 0.7 collective-permute-start.15
  136.9 10.4 %collective-permute-done.17.refs_3_ = bf16[128,2048]{1,0:T(8,128)(2,1)S(1)} collective-permute-done((bf16[128,2048]{1,0:T(8,128)(2,1)S(1)}, bf16[128,2048]{1,0:T(8,128)(2,1)S(1)}, u32[]{:S(2)}, u32[]{:S(2)}) %collective-permute-start.17) | collective-permute-done | bytes 524320 | tf_op jit(solution)/shard_map/ppermute | solution.py:170
  147.3 6.1 %scores.5 = (bf16[4,128,512]{2,1,0:T(8,128)(2,1)S(1)}, bf16[4,128,512]{2,1,0:T(8,128)(2,1)S(1)}) custom-call(f32[128,2048]{1,0:T(8,128)S(1)} %get-tuple-element.93.refs_0_, bf16[128,2048]{1,0:T(8,128)(2,1)S(1)} %collective-permute-done.16.refs_1_, f32[128,2048]{1,0:T(8,128)S(1)} %get-tuple-element.95.refs_2_, ...), custom_call_target="tpu_custom_call" | custom-call | flops 1 | bytes 1 | tf_op jit(solution)/shard_map/scores/pallas_call | solution.py:144
  153.8 5.6 %product.7 = (f32[128,2048]{1,0:T(8,128)S(1)}, bf16[128,2048]{1,0:T(8,128)(2,1)S(1)}, f32[128,2048]{1,0:T(8,128)S(1)}, bf16[128,2048]{1,0:T(8,128)(2,1)S(1)}) custom-call(s32[3]{0:T(128)S(1)} %pad_add_fusion.refs_0_.flags, bf16[512,2048]{1,0:T(8,128)(2,1)S(1)} %collective-permute-done.11.refs_1_, bf16[2048,2048]{1,0:T(8,128)(2,1)S(1)} %copy-done.4), custom_call_target="tpu_custom_call" | custom-call | flops 1 | bytes 1 | tf_op jit(solution)/shard_map/product/pallas_call | solution.py:83
  159.4 0.5 collective-permute-start.26
  159.9 3.5 %collective-permute-start.21 = (bf16[4,128,512]{2,1,0:T(8,128)(2,1)S(1)}, bf16[4,128,512]{2,1,0:T(8,128)(2,1)S(1)}, u32[]{:S(2)}, u32[]{:S(2)}) collective-permute-start(bf16[4,128,512]{2,1,0:T(8,128)(2,1)S(1)} %get-tuple-element.109), channel_id=1, source_target_pairs={{0,2},{3,1},{1,3},{2,0},{4,6},{7,5},{5,7},{6,4},{8,10},{11,9},{9,1... | collective-permute-start | bytes 1572872 | tf_op jit(solution)/shard_map/ppermute | solution.py:167
  163.4 1.3 collective-permute-start.22
  164.7 0.7 fold.10
  165.4 1.6 collective-permute-start.19
  167.0 0.7 fold.11
  167.7 0.6 collective-permute-start.27
  168.3 6.4 %collective-permute-done.19.refs_1_ = bf16[64,2048]{1,0:T(8,128)(2,1)S(1)} collective-permute-done((bf16[64,2048]{1,0:T(8,128)(2,1)S(1)}, bf16[64,2048]{1,0:T(8,128)(2,1)S(1)}, u32[]{:S(2)}, u32[]{:S(2)}) %collective-permute-start.19) | collective-permute-done | bytes 262176 | tf_op jit(solution)/shard_map/ppermute | solution.py:170
  174.7 4.4 %scores.6 = bf16[4,64,512]{2,1,0:T(8,128)(2,1)S(1)} custom-call(f32[64,2048]{1,0:T(8,128)S(1)} %get-tuple-element.102.refs_0_, bf16[64,2048]{1,0:T(8,128)(2,1)S(1)} %collective-permute-done.19.refs_1_, bf16[512,2048]{1,0:T(8,128)(2,1)S(1)} %copy-done.5, bf16[512,2048]{1,0:T(8,128)(2,1)S(1)} %collective-permute-done.3.refs_5_.refs_3_, ...), custom_call_target="tpu_custom_call" | custom-call | flops 1 | bytes 1 | tf_op jit(solution)/shard_map/scores/pallas_call | solution.py:144
  179.1 4.8 %collective-permute-start.20 = (bf16[4,64,512]{2,1,0:T(8,128)(2,1)S(1)}, bf16[4,64,512]{2,1,0:T(8,128)(2,1)S(1)}, u32[]{:S(2)}, u32[]{:S(2)}) collective-permute-start(bf16[4,64,512]{2,1,0:T(8,128)(2,1)S(1)} %scores.6), channel_id=1, source_target_pairs={{0,3},{3,0},{4,7},{7,4},{8,11},{11,8},{12,15},{15,12},{16,19},{19,... | collective-permute-start | bytes 786440 | tf_op jit(solution)/shard_map/ppermute | solution.py:167
  184.0 4.4 %scores.7 = bf16[4,64,512]{2,1,0:T(8,128)(2,1)S(1)} custom-call(f32[64,2048]{1,0:T(8,128)S(1)} %get-tuple-element.114.refs_0_, bf16[64,2048]{1,0:T(8,128)(2,1)S(1)} %collective-permute-done.27.refs_1_, bf16[512,2048]{1,0:T(8,128)(2,1)S(1)} %copy-done.5, bf16[512,2048]{1,0:T(8,128)(2,1)S(1)} %collective-permute-done.3.refs_5_.refs_3_, ...), custom_call_target="tpu_custom_call" | custom-call | flops 1 | bytes 1 | tf_op jit(solution)/shard_map/scores/pallas_call | solution.py:144
  188.4 3.1 %collective-permute-start.28 = (bf16[4,64,512]{2,1,0:T(8,128)(2,1)S(1)}, bf16[4,64,512]{2,1,0:T(8,128)(2,1)S(1)}, u32[]{:S(2)}, u32[]{:S(2)}) collective-permute-start(bf16[4,64,512]{2,1,0:T(8,128)(2,1)S(1)} %scores.7), channel_id=1, source_target_pairs={{0,3},{3,0},{4,7},{7,4},{8,11},{11,8},{12,15},{15,12},{16,19},{19,... | collective-permute-start | bytes 786440 | tf_op jit(solution)/shard_map/ppermute | solution.py:167
  191.5 3.9 %collective-permute-done.21 = bf16[4,128,512]{2,1,0:T(8,128)(2,1)S(1)} collective-permute-done((bf16[4,128,512]{2,1,0:T(8,128)(2,1)S(1)}, bf16[4,128,512]{2,1,0:T(8,128)(2,1)S(1)}, u32[]{:S(2)}, u32[]{:S(2)}) %collective-permute-start.21) | collective-permute-done | bytes 524320 | tf_op jit(solution)/shard_map/ppermute | solution.py:167
  195.4 3.6 %collective-permute-done.22 = bf16[4,128,512]{2,1,0:T(8,128)(2,1)S(1)} collective-permute-done((bf16[4,128,512]{2,1,0:T(8,128)(2,1)S(1)}, bf16[4,128,512]{2,1,0:T(8,128)(2,1)S(1)}, u32[]{:S(2)}, u32[]{:S(2)}) %collective-permute-start.22) | collective-permute-done | bytes 524320 | tf_op jit(solution)/shard_map/ppermute | solution.py:167
  198.9 0.2 convert_add_fusion
  199.2 0.3 multiply_reduce_fusion
  199.7 1.6 collective-permute-start.23
  201.3 0.6 collective-permute-start.25
  201.9 1.5 collective-permute-start.29
  203.4 2.5 %collective-permute-done.23 = f32[64,640]{1,0:T(8,128)S(1)} collective-permute-done((f32[64,640]{1,0:T(8,128)S(1)}, f32[64,640]{1,0:T(8,128)S(1)}, u32[]{:S(2)}, u32[]{:S(2)}) %collective-permute-start.23) | collective-permute-done | bytes 163872 | tf_op jit(solution)/shard_map/ppermute | solution.py:170
  205.9 3.5 %collective-permute-done.25 = f32[64,640]{1,0:T(8,128)S(1)} collective-permute-done((f32[64,640]{1,0:T(8,128)S(1)}, f32[64,640]{1,0:T(8,128)S(1)}, u32[]{:S(2)}, u32[]{:S(2)}) %collective-permute-start.25) | collective-permute-done | bytes 163872 | tf_op jit(solution)/shard_map/ppermute | solution.py:170
  209.5 3.4 %collective-permute-done.29 = f32[64,640]{1,0:T(8,128)S(1)} collective-permute-done((f32[64,640]{1,0:T(8,128)S(1)}, f32[64,640]{1,0:T(8,128)S(1)}, u32[]{:S(2)}, u32[]{:S(2)}) %collective-permute-start.29) | collective-permute-done | bytes 163872 | tf_op jit(solution)/shard_map/ppermute | solution.py:170
  212.9 1.9 collective-permute-done.31
  215.6 0.7 slice_reduce_fusion
  216.4 1.3 copy.11
  (55 shorter events, 2.2 us)
Async XLA Ops:
  0.6 19.9 %copy-start = (s32[512,16]{0,1:T(8,128)S(1)}, s32[512,16]{0,1:T(8,128)}, u32[]{:S(2)}) copy-start(s32[512,16]{0,1:T(8,128)} %param.7) | copy-start | bytes 98308
  0.6 49.0 %collective-permute-start = (bf16[512,2048]{1,0:T(8,128)(2,1)}, bf16[512,2048]{1,0:T(8,128)(2,1)}, u32[]{:S(2)}, u32[]{:S(2)}) collective-permute-start(bf16[512,2048]{1,0:T(8,128)(2,1)} %refs_1_.1), channel_id=1, source_target_pairs={{0,1},{1,0},{2,3},{3,2},{4,5},{5,4},{6,7},{7,6},{8,9},{9,8},{10,11... | collective-permute-start | bytes 6291464 | tf_op jit(solution)/shard_map/ppermute | solution.py:167
  3.7 46.0 %collective-permute-start.1 = (bf16[512,2048]{1,0:T(8,128)(2,1)}, bf16[512,2048]{1,0:T(8,128)(2,1)}, u32[]{:S(2)}, u32[]{:S(2)}) collective-permute-start(bf16[512,2048]{1,0:T(8,128)(2,1)} %refs_1_.1), channel_id=1, source_target_pairs={{1,2},{2,1},{5,6},{6,5},{9,10},{10,9},{13,14},{14,13},{17,18},{18,... | collective-permute-start | bytes 6291464 | tf_op jit(solution)/shard_map/ppermute | solution.py:167
  5.8 43.9 %collective-permute-start.3 = (bf16[512,2048]{1,0:T(8,128)(2,1)}, bf16[512,2048]{1,0:T(8,128)(2,1)S(1)}, u32[]{:S(2)}, u32[]{:S(2)}) collective-permute-start(bf16[512,2048]{1,0:T(8,128)(2,1)} %refs_2_.5), channel_id=1, source_target_pairs={{0,4},{4,0},{8,12},{12,8},{1,5},{5,1},{9,13},{13,9},{2,6},{6,2},{1... | collective-permute-start | bytes 6291464 | tf_op jit(solution)/shard_map/ppermute | solution.py:170
  5.8 48.4 %collective-permute-start.9 = (bf16[512,2048]{1,0:T(8,128)(2,1)}, bf16[512,2048]{1,0:T(8,128)(2,1)}, u32[]{:S(2)}, u32[]{:S(2)}) collective-permute-start(bf16[512,2048]{1,0:T(8,128)(2,1)} %refs_2_.5), channel_id=1, source_target_pairs={{0,8},{4,12},{8,0},{12,4},{1,9},{5,13},{9,1},{13,5},{2,10},{6,14},... | collective-permute-start | bytes 6291464 | tf_op jit(solution)/shard_map/ppermute | solution.py:170
  7.3 3.4 %copy-start.2 = (bf16[2048,2048]{1,0:T(8,128)(2,1)S(1)}, bf16[2048,2048]{1,0:T(8,128)(2,1)}, u32[]{:S(2)}) copy-start(bf16[2048,2048]{1,0:T(8,128)(2,1)} %refs_2_.3) | copy-start | bytes 25165828
  10.7 1.6 copy-start.8
  18.9 1.4 copy-start.6
  20.3 3.9 %collective-permute-start.2 = (bf16[256,2048]{1,0:T(8,128)(2,1)}, bf16[256,2048]{1,0:T(8,128)(2,1)S(1)}, u32[]{:S(2)}, u32[]{:S(2)}) collective-permute-start(bf16[256,2048]{1,0:T(8,128)(2,1)} %get-tuple-element.60), channel_id=1, source_target_pairs={{0,4},{4,0},{8,12},{12,8},{1,5},{5,1},{9,13},{13,9},{2,6},{6,2},{1... | collective-permute-start | bytes 3145736 | tf_op jit(solution)/shard_map/ppermute | solution.py:170
  24.2 1.6 copy-start.7
  49.7 52.3 %collective-permute-start.4 = (bf16[512,2048]{1,0:T(8,128)(2,1)}, bf16[512,2048]{1,0:T(8,128)(2,1)S(1)}, u32[]{:S(2)}, u32[]{:S(2)}) collective-permute-start(bf16[512,2048]{1,0:T(8,128)(2,1)} %collective-permute-done.refs_2_.refs_3_), channel_id=1, source_target_pairs={{1,2},{2,1},{5,6},{6,5},{9,10},{10,9},{13,14},{14,13},{17,18},{18,... | collective-permute-start | bytes 6291464 | tf_op jit(solution)/shard_map/ppermute | solution.py:167
  50.5 53.2 %collective-permute-start.5 = (bf16[512,2048]{1,0:T(8,128)(2,1)}, bf16[512,2048]{1,0:T(8,128)(2,1)S(1)}, u32[]{:S(2)}, u32[]{:S(2)}) collective-permute-start(bf16[512,2048]{1,0:T(8,128)(2,1)} %collective-permute-done.1.refs_1_), channel_id=1, source_target_pairs={{1,0},{2,3},{5,4},{6,7},{9,8},{10,11},{13,12},{14,15},{17,16},{18,... | collective-permute-start | bytes 6291464 | tf_op jit(solution)/shard_map/ppermute | solution.py:167
  54.1 49.6 %collective-permute-start.10 = (bf16[512,2048]{1,0:T(8,128)(2,1)}, bf16[512,2048]{1,0:T(8,128)(2,1)S(1)}, u32[]{:S(2)}, u32[]{:S(2)}) collective-permute-start(bf16[512,2048]{1,0:T(8,128)(2,1)} %collective-permute-done.9.refs_6_.refs_4_), channel_id=1, source_target_pairs={{0,4},{4,0},{8,12},{12,8},{1,5},{5,1},{9,13},{13,9},{2,6},{6,2},{1... | collective-permute-start | bytes 6291464 | tf_op jit(solution)/shard_map/ppermute | solution.py:170
  54.1 3.4 %copy-start.3 = (bf16[2048,2048]{1,0:T(8,128)(2,1)S(1)}, bf16[2048,2048]{1,0:T(8,128)(2,1)}, u32[]{:S(2)}) copy-start(bf16[2048,2048]{1,0:T(8,128)(2,1)} %refs_2_.3) | copy-start | bytes 25165828
  57.5 47.5 %copy-start.4 = (bf16[2048,2048]{1,0:T(8,128)(2,1)S(1)}, bf16[2048,2048]{1,0:T(8,128)(2,1)}, u32[]{:S(2)}) copy-start(bf16[2048,2048]{1,0:T(8,128)(2,1)} %refs_2_.3) | copy-start | bytes 25165828
  65.0 2.9 %collective-permute-start.7 = (bf16[256,2048]{1,0:T(8,128)(2,1)S(1)}, bf16[256,2048]{1,0:T(8,128)(2,1)S(1)}, u32[]{:S(2)}, u32[]{:S(2)}) collective-permute-start(bf16[256,2048]{1,0:T(8,128)(2,1)S(1)} %get-tuple-element.68), channel_id=1, source_target_pairs={{0,4},{4,0},{8,12},{12,8},{1,5},{5,1},{9,13},{13,9},{2,6},{6,2},{1... | collective-permute-start | bytes 3145736 | tf_op jit(solution)/shard_map/ppermute | solution.py:170
  65.6 26.0 %collective-permute-start.6 = (f32[128,2048]{1,0:T(8,128)S(1)}, f32[128,2048]{1,0:T(8,128)S(1)}, u32[]{:S(2)}, u32[]{:S(2)}) collective-permute-start(f32[128,2048]{1,0:T(8,128)S(1)} %get-tuple-element.66), channel_id=1, source_target_pairs={{0,8},{4,12},{8,0},{12,4},{1,9},{5,13},{9,1},{13,5},{2,10},{6,14},... | collective-permute-start | bytes 3145736 | tf_op jit(solution)/shard_map/ppermute | solution.py:170
  68.7 33.3 %collective-permute-start.8 = (bf16[128,2048]{1,0:T(8,128)(2,1)S(1)}, bf16[128,2048]{1,0:T(8,128)(2,1)S(1)}, u32[]{:S(2)}, u32[]{:S(2)}) collective-permute-start(bf16[128,2048]{1,0:T(8,128)(2,1)S(1)} %get-tuple-element.70), channel_id=1, source_target_pairs={{0,8},{4,12},{8,0},{12,4},{1,9},{5,13},{9,1},{13,5},{2,10},{6,14},... | collective-permute-start | bytes 1572872 | tf_op jit(solution)/shard_map/ppermute | solution.py:170
  103.7 50.0 %collective-permute-start.11 = (bf16[512,2048]{1,0:T(8,128)(2,1)S(1)}, bf16[512,2048]{1,0:T(8,128)(2,1)S(1)}, u32[]{:S(2)}, u32[]{:S(2)}) collective-permute-start(bf16[512,2048]{1,0:T(8,128)(2,1)S(1)} %collective-permute-done.4.refs_1_), channel_id=1, source_target_pairs={{1,0},{2,3},{5,4},{6,7},{9,8},{10,11},{13,12},{14,15},{17,16},{18,... | collective-permute-start | bytes 6291464 | tf_op jit(solution)/shard_map/ppermute | solution.py:167
  117.0 2.7 %collective-permute-start.13 = (bf16[256,2048]{1,0:T(8,128)(2,1)S(1)}, bf16[256,2048]{1,0:T(8,128)(2,1)S(1)}, u32[]{:S(2)}, u32[]{:S(2)}) collective-permute-start(bf16[256,2048]{1,0:T(8,128)(2,1)S(1)} %get-tuple-element.79), channel_id=1, source_target_pairs={{0,4},{4,0},{8,12},{12,8},{1,5},{5,1},{9,13},{13,9},{2,6},{6,2},{1... | collective-permute-start | bytes 3145736 | tf_op jit(solution)/shard_map/ppermute | solution.py:170
  117.1 4.1 %collective-permute-start.12 = (bf16[256,2048]{1,0:T(8,128)(2,1)S(1)}, bf16[256,2048]{1,0:T(8,128)(2,1)S(1)}, u32[]{:S(2)}, u32[]{:S(2)}) collective-permute-start(bf16[256,2048]{1,0:T(8,128)(2,1)S(1)} %get-tuple-element.76), channel_id=1, source_target_pairs={{0,4},{4,0},{8,12},{12,8},{1,5},{5,1},{9,13},{13,9},{2,6},{6,2},{1... | collective-permute-start | bytes 3145736 | tf_op jit(solution)/shard_map/ppermute | solution.py:170
  121.2 2.9 %copy-start.5 = (bf16[512,2048]{1,0:T(8,128)(2,1)S(1)}, bf16[512,2048]{1,0:T(8,128)(2,1)}, u32[]{:S(2)}) copy-start(bf16[512,2048]{1,0:T(8,128)(2,1)} %refs_2_.5) | copy-start | bytes 6291460
  122.0 14.8 %collective-permute-start.16 = (bf16[128,2048]{1,0:T(8,128)(2,1)S(1)}, bf16[128,2048]{1,0:T(8,128)(2,1)S(1)}, u32[]{:S(2)}, u32[]{:S(2)}) collective-permute-start(bf16[128,2048]{1,0:T(8,128)(2,1)S(1)} %get-tuple-element.94), channel_id=1, source_target_pairs={{0,8},{4,12},{8,0},{12,4},{1,9},{5,13},{9,1},{13,5},{2,10},{6,14},... | collective-permute-start | bytes 1572872 | tf_op jit(solution)/shard_map/ppermute | solution.py:170
  123.6 23.7 %collective-permute-start.17 = (bf16[128,2048]{1,0:T(8,128)(2,1)S(1)}, bf16[128,2048]{1,0:T(8,128)(2,1)S(1)}, u32[]{:S(2)}, u32[]{:S(2)}) collective-permute-start(bf16[128,2048]{1,0:T(8,128)(2,1)S(1)} %get-tuple-element.96), channel_id=1, source_target_pairs={{0,8},{4,12},{8,0},{12,4},{1,9},{5,13},{9,1},{13,5},{2,10},{6,14},... | collective-permute-start | bytes 1572872 | tf_op jit(solution)/shard_map/ppermute | solution.py:170
  130.3 23.1 %collective-permute-start.14 = (bf16[4,128,512]{2,1,0:T(8,128)(2,1)S(1)}, bf16[4,128,512]{2,1,0:T(8,128)(2,1)S(1)}, u32[]{:S(2)}, u32[]{:S(2)}) collective-permute-start(bf16[4,128,512]{2,1,0:T(8,128)(2,1)S(1)} %get-tuple-element.92), channel_id=1, source_target_pairs={{0,1},{3,2},{4,5},{7,6},{8,9},{11,10},{12,13},{15,14},{16,17},{19,... | collective-permute-start | bytes 1572872 | tf_op jit(solution)/shard_map/ppermute | solution.py:167
  136.1 17.3 %collective-permute-start.15 = (bf16[4,128,512]{2,1,0:T(8,128)(2,1)S(1)}, bf16[4,128,512]{2,1,0:T(8,128)(2,1)S(1)}, u32[]{:S(2)}, u32[]{:S(2)}) collective-permute-start(bf16[4,128,512]{2,1,0:T(8,128)(2,1)S(1)} %get-tuple-element.92), channel_id=1, source_target_pairs={{1,2},{2,1},{5,6},{6,5},{9,10},{10,9},{13,14},{14,13},{17,18},{18,... | collective-permute-start | bytes 1572872 | tf_op jit(solution)/shard_map/ppermute | solution.py:167
  159.4 5.4 %collective-permute-start.18 = (bf16[128,2048]{1,0:T(8,128)(2,1)S(1)}, bf16[128,2048]{1,0:T(8,128)(2,1)S(1)}, u32[]{:S(2)}, u32[]{:S(2)}) collective-permute-start(bf16[128,2048]{1,0:T(8,128)(2,1)S(1)} %get-tuple-element.101), channel_id=1, source_target_pairs={{0,4},{4,0},{8,12},{12,8},{1,5},{5,1},{9,13},{13,9},{2,6},{6,2},{1... | collective-permute-start | bytes 1572872 | tf_op jit(solution)/shard_map/ppermute | solution.py:170
  159.4 7.6 %collective-permute-start.26 = (bf16[128,2048]{1,0:T(8,128)(2,1)S(1)}, bf16[128,2048]{1,0:T(8,128)(2,1)S(1)}, u32[]{:S(2)}, u32[]{:S(2)}) collective-permute-start(bf16[128,2048]{1,0:T(8,128)(2,1)S(1)} %get-tuple-element.113), channel_id=1, source_target_pairs={{0,4},{4,0},{8,12},{12,8},{1,5},{5,1},{9,13},{13,9},{2,6},{6,2},{1... | collective-permute-start | bytes 1572872 | tf_op jit(solution)/shard_map/ppermute | solution.py:170
  159.9 35.4 %collective-permute-start.21 = (bf16[4,128,512]{2,1,0:T(8,128)(2,1)S(1)}, bf16[4,128,512]{2,1,0:T(8,128)(2,1)S(1)}, u32[]{:S(2)}, u32[]{:S(2)}) collective-permute-start(bf16[4,128,512]{2,1,0:T(8,128)(2,1)S(1)} %get-tuple-element.109), channel_id=1, source_target_pairs={{0,2},{3,1},{1,3},{2,0},{4,6},{7,5},{5,7},{6,4},{8,10},{11,9},{9,1... | collective-permute-start | bytes 1572872 | tf_op jit(solution)/shard_map/ppermute | solution.py:167
  163.4 35.5 %collective-permute-start.22 = (bf16[4,128,512]{2,1,0:T(8,128)(2,1)S(1)}, bf16[4,128,512]{2,1,0:T(8,128)(2,1)S(1)}, u32[]{:S(2)}, u32[]{:S(2)}) collective-permute-start(bf16[4,128,512]{2,1,0:T(8,128)(2,1)S(1)} %get-tuple-element.110), channel_id=1, source_target_pairs={{1,0},{2,3},{5,4},{6,7},{9,8},{10,11},{13,12},{14,15},{17,16},{18,... | collective-permute-start | bytes 1572872 | tf_op jit(solution)/shard_map/ppermute | solution.py:167
  165.4 9.3 %collective-permute-start.19 = (bf16[64,2048]{1,0:T(8,128)(2,1)S(1)}, bf16[64,2048]{1,0:T(8,128)(2,1)S(1)}, u32[]{:S(2)}, u32[]{:S(2)}) collective-permute-start(bf16[64,2048]{1,0:T(8,128)(2,1)S(1)} %get-tuple-element.103), channel_id=1, source_target_pairs={{0,8},{4,12},{8,0},{12,4},{1,9},{5,13},{9,1},{13,5},{2,10},{6,14},... | collective-permute-start | bytes 786440 | tf_op jit(solution)/shard_map/ppermute | solution.py:170
  167.7 16.3 %collective-permute-start.27 = (bf16[64,2048]{1,0:T(8,128)(2,1)S(1)}, bf16[64,2048]{1,0:T(8,128)(2,1)S(1)}, u32[]{:S(2)}, u32[]{:S(2)}) collective-permute-start(bf16[64,2048]{1,0:T(8,128)(2,1)S(1)} %get-tuple-element.115), channel_id=1, source_target_pairs={{0,8},{4,12},{8,0},{12,4},{1,9},{5,13},{9,1},{13,5},{2,10},{6,14},... | collective-permute-start | bytes 786440 | tf_op jit(solution)/shard_map/ppermute | solution.py:170
  179.1 20.0 %collective-permute-start.20 = (bf16[4,64,512]{2,1,0:T(8,128)(2,1)S(1)}, bf16[4,64,512]{2,1,0:T(8,128)(2,1)S(1)}, u32[]{:S(2)}, u32[]{:S(2)}) collective-permute-start(bf16[4,64,512]{2,1,0:T(8,128)(2,1)S(1)} %scores.6), channel_id=1, source_target_pairs={{0,3},{3,0},{4,7},{7,4},{8,11},{11,8},{12,15},{15,12},{16,19},{19,... | collective-permute-start | bytes 786440 | tf_op jit(solution)/shard_map/ppermute | solution.py:167
  188.4 10.8 %collective-permute-start.28 = (bf16[4,64,512]{2,1,0:T(8,128)(2,1)S(1)}, bf16[4,64,512]{2,1,0:T(8,128)(2,1)S(1)}, u32[]{:S(2)}, u32[]{:S(2)}) collective-permute-start(bf16[4,64,512]{2,1,0:T(8,128)(2,1)S(1)} %scores.7), channel_id=1, source_target_pairs={{0,3},{3,0},{4,7},{7,4},{8,11},{11,8},{12,15},{15,12},{16,19},{19,... | collective-permute-start | bytes 786440 | tf_op jit(solution)/shard_map/ppermute | solution.py:167
  199.7 6.2 %collective-permute-start.23 = (f32[64,640]{1,0:T(8,128)S(1)}, f32[64,640]{1,0:T(8,128)S(1)}, u32[]{:S(2)}, u32[]{:S(2)}) collective-permute-start(f32[64,640]{1,0:T(8,128)S(1)} %get-tuple-element.142), channel_id=1, source_target_pairs={{0,8},{4,12},{8,0},{12,4},{1,9},{5,13},{9,1},{13,5},{2,10},{6,14},... | collective-permute-start | bytes 491528 | tf_op jit(solution)/shard_map/ppermute | solution.py:170
  201.3 4.6 %collective-permute-start.24 = (f32[64,640]{1,0:T(8,128)S(1)}, f32[64,640]{1,0:T(8,128)S(1)}, u32[]{:S(2)}, u32[]{:S(2)}) collective-permute-start(f32[64,640]{1,0:T(8,128)S(1)} %get-tuple-element.141), channel_id=1, source_target_pairs={{0,4},{4,0},{8,12},{12,8},{1,5},{5,1},{9,13},{13,9},{2,6},{6,2},{1... | collective-permute-start | bytes 491528 | tf_op jit(solution)/shard_map/ppermute | solution.py:170
  201.3 8.1 %collective-permute-start.25 = (f32[64,640]{1,0:T(8,128)S(1)}, f32[64,640]{1,0:T(8,128)S(1)}, u32[]{:S(2)}, u32[]{:S(2)}) collective-permute-start(f32[64,640]{1,0:T(8,128)S(1)} %get-tuple-element.140), channel_id=1, source_target_pairs={{0,12},{4,8},{8,4},{12,0},{1,13},{5,9},{9,5},{13,1},{2,14},{6,10},... | collective-permute-start | bytes 491528 | tf_op jit(solution)/shard_map/ppermute | solution.py:170
  201.9 11.0 %collective-permute-start.29 = (f32[64,640]{1,0:T(8,128)S(1)}, f32[64,640]{1,0:T(8,128)S(1)}, u32[]{:S(2)}, u32[]{:S(2)}) collective-permute-start(f32[64,640]{1,0:T(8,128)S(1)} %get-tuple-element.134), channel_id=1, source_target_pairs={{0,8},{4,12},{8,0},{12,4},{1,9},{5,13},{9,1},{13,5},{2,10},{6,14},... | collective-permute-start | bytes 491528 | tf_op jit(solution)/shard_map/ppermute | solution.py:170
  203.4 9.5 %collective-permute-start.30 = (f32[64,640]{1,0:T(8,128)S(1)}, f32[64,640]{1,0:T(8,128)S(1)}, u32[]{:S(2)}, u32[]{:S(2)}) collective-permute-start(f32[64,640]{1,0:T(8,128)S(1)} %get-tuple-element.135), channel_id=1, source_target_pairs={{0,4},{4,0},{8,12},{12,8},{1,5},{5,1},{9,13},{13,9},{2,6},{6,2},{1... | collective-permute-start | bytes 491528 | tf_op jit(solution)/shard_map/ppermute | solution.py:170
  205.9 8.9 %collective-permute-start.31 = (f32[64,640]{1,0:T(8,128)S(1)}, f32[64,640]{1,0:T(8,128)S(1)}, u32[]{:S(2)}, u32[]{:S(2)}) collective-permute-start(f32[64,640]{1,0:T(8,128)S(1)} %get-tuple-element.136), channel_id=1, source_target_pairs={{0,12},{4,8},{8,4},{12,0},{1,13},{5,9},{9,5},{13,1},{2,14},{6,10},... | collective-permute-start | bytes 491528 | tf_op jit(solution)/shard_map/ppermute | solution.py:170
  215.5 2.2 %copy-start.1 = (s32[512,16]{0,1:T(8,128)S(1)}, s32[512,16]{0,1:T(8,128)}, u32[]{:S(2)}) copy-start(s32[512,16]{0,1:T(8,128)} %param.7) | copy-start | bytes 98308

commit v7 on v6

v7 whole, which is shorter than its diff:
```python
import jax
import jax.numpy as jnp
from jax import lax
from jax.experimental import pallas as pl
from jax.experimental.pallas import tpu as pltpu
from jax.sharding import PartitionSpec as P

COLUMNS = 512

F32 = jnp.float32
BF16 = jnp.bfloat16


def dot_t(a, b):
    return lax.dot_general(a, b, (((1,), (1,)), ((), ())), preferred_element_type=F32)


def selection_counts(chosen_ids, first_row, rows):
    row_ids = first_row + lax.broadcasted_iota(jnp.int32, (rows, chosen_ids.shape[0]), 0)
    ids = chosen_ids.T
    counts = jnp.zeros(row_ids.shape, F32)
    for k in range(ids.shape[0]):
        counts = counts + (row_ids == ids[k][None, :]).astype(F32)
    return counts


def any_mesh(train_grads, test_grads, fisher, chosen_ids):
    test_whole = lax.all_gather(test_grads, "test", axis=0, tiled=True)
    partial_value = jnp.dot(test_whole, fisher, preferred_element_type=F32)
    precond = lax.psum(partial_value, "train").astype(BF16)
    partial_scores = dot_t(train_grads, precond)
    scores = lax.psum_scatter(partial_scores, "test", scatter_dimension=1, tiled=True)
    rows = scores.shape[0]
    counts = selection_counts(chosen_ids, lax.axis_index("train") * rows, rows)
    return scores, lax.psum(jnp.sum(counts * scores, axis=0), "train")


SMALL = pl.CostEstimate(flops=1, bytes_accessed=1, transcendentals=0)
PARAMS = pltpu.CompilerParams(vmem_limit_bytes=16 * 2**20)


VMEM = pl.BlockSpec(memory_space=pltpu.VMEM)


def product_body(choices, flags, *refs):
    count = sum(len(choice) for choice in choices)
    blocks, fisher, outs = refs[:count], refs[count], refs[count + 1 :]
    quarter = blocks[0].shape[0] // 4
    mine = flags[0] == 0

    def multiply(block, kept, *sent):
        @pl.loop(0, fisher.shape[1] // COLUMNS)
        def _(n):
            columns = pl.ds(pl.multiple_of(n * COLUMNS, COLUMNS), COLUMNS)
            value = jnp.dot(block[...], fisher[:, columns], preferred_element_type=F32)
            for chip in range(2):
                low, high = (value[(2 * core + chip) * quarter :][:quarter] for core in range(2))
                kept[pl.ds(chip * quarter, quarter), columns] = jnp.where(mine, low, high)
                sent[chip][:, columns] = jnp.where(mine, high, low).astype(BF16)

    first = 0
    for u, choice in enumerate(choices):
        these = outs[3 * u : 3 * (u + 1)]
        if len(choice) == 1:
            multiply(blocks[first], *these)
        else:
            pl.when(flags[2] == 1)(lambda: multiply(blocks[first], *these))
            pl.when(flags[2] == 0)(lambda: multiply(blocks[first + 1], *these))
        first += len(choice)


def product(flags, choices, fisher):
    quarter = choices[0][0].shape[0] // 4
    columns = fisher.shape[1]
    blocks = [block for choice in choices for block in choice]
    return pl.pallas_call(
        lambda *refs: product_body(choices, *refs),
        in_specs=[pl.BlockSpec(memory_space=pltpu.SMEM)] + [VMEM] * (len(blocks) + 1),
        out_specs=[VMEM] * (3 * len(choices)),
        out_shape=[
            jax.ShapeDtypeStruct((2 * quarter, columns), F32),
            jax.ShapeDtypeStruct((quarter, columns), BF16),
            jax.ShapeDtypeStruct((quarter, columns), BF16),
        ]
        * len(choices),
        compiler_params=PARAMS,
        cost_estimate=SMALL,
        name="product",
    )(flags, *blocks, fisher)


def fold_body(flags, kept, got_low, got_high, kept_out, sent_out):
    half = got_low.shape[0]
    first = flags[1] == 0

    @pl.loop(0, kept.shape[1] // COLUMNS)
    def _(n):
        columns = pl.ds(pl.multiple_of(n * COLUMNS, COLUMNS), COLUMNS)
        low = kept[:half, columns] + got_low[:, columns].astype(F32)
        high = kept[half:, columns] + got_high[:, columns].astype(F32)
        kept_out[:, columns] = jnp.where(first, low, high)
        sent_out[:, columns] = jnp.where(first, high, low).astype(sent_out.dtype)


def fold(flags, kept, got_low, got_high, sent_as):
    return pl.pallas_call(
        fold_body,
        in_specs=[pl.BlockSpec(memory_space=pltpu.SMEM)] + [VMEM] * 3,
        out_specs=[VMEM, VMEM],
        out_shape=[
            jax.ShapeDtypeStruct(got_low.shape, F32),
            jax.ShapeDtypeStruct(got_low.shape, sent_as),
        ],
        compiler_params=PARAMS,
        cost_estimate=SMALL,
        name="fold",
    )(flags, kept, got_low, got_high)


def split_sum(kept, got):
    value = kept[...] + got[...].astype(F32)
    high = value.astype(BF16)
    return high, (value - high.astype(F32)).astype(BF16)


def scores_body(units, *refs):
    sums, grads, outs = refs[: 2 * units], refs[2 * units :][:4], refs[2 * units + 4 :]
    rows = sums[0].shape[0]
    precond = jnp.concatenate(
        [part for u in range(units) for part in split_sum(sums[2 * u], sums[2 * u + 1])]
    )
    for r in range(4):
        both = dot_t(precond, grads[r][...])
        for u in range(units):
            value = both[2 * u * rows :][:rows] + both[(2 * u + 1) * rows :][:rows]
            outs[u][r] = value.astype(outs[u].dtype)


def partial_scores(units, grads, out_as):
    rows = units[0][0].shape[0]
    train_rows = grads[0].shape[0]
    return pl.pallas_call(
        lambda *refs: scores_body(len(units), *refs),
        in_specs=[VMEM] * (2 * len(units) + 4),
        out_specs=[VMEM] * len(units),
        out_shape=[jax.ShapeDtypeStruct((4, rows, train_rows), kind) for kind in out_as],
        compiler_params=PARAMS,
        cost_estimate=SMALL,
        name="scores",
    )(*[value for unit in units for value in unit], *grads)


def last_scores_body(kept, got, counts, *refs):
    grads, out = refs[:4], refs[4]
    rows = kept.shape[0]
    train_rows = grads[0].shape[0]
    precond = jnp.concatenate(split_sum(kept, got))
    chosen = jnp.zeros((rows, 1), F32)
    for r in range(4):
        both = dot_t(precond, grads[r][...])
        value = both[:rows] + both[rows:]
        out[r, :, :train_rows] = value.astype(out.dtype)
        chosen = chosen + jnp.sum(value * counts[r], axis=1, keepdims=True)
    for r in range(4):
        out[r, :, train_rows:] = jnp.broadcast_to(chosen, (rows, 128)).astype(out.dtype)


def last_scores(kept, got, counts, grads):
    rows = kept.shape[0]
    return pl.pallas_call(
        last_scores_body,
        in_specs=[VMEM] * 7,
        out_specs=VMEM,
        out_shape=jax.ShapeDtypeStruct((4, rows, grads[0].shape[0] + 128), BF16),
        compiler_params=PARAMS,
        cost_estimate=SMALL,
        name="last_scores",
    )(kept, got, counts, *grads)


def four_by_four(train_grads, test_grads, fisher, chosen_ids):
    z = lax.axis_index("test")
    i = lax.axis_index("train")
    chip, core = i // 2, i % 2
    inner = (z == 1) | (z == 2)
    flags = jnp.stack([core, chip, inner.astype(jnp.int32)])
    own_rows = train_grads.shape[0]
    quarter = test_grads.shape[0] // 4

    def along(value, pairs):
        return lax.ppermute(value, "test", pairs)

    def to_other(value, r):
        return lax.ppermute(value, "train", [(k, k ^ r) for k in range(4)])

    def tied(*values):
        return lax.optimization_barrier(values)

    pair = [(0, 1), (1, 0), (2, 3), (3, 2)]
    middle = [(1, 2), (2, 1)]
    outward = [(1, 0), (2, 3)]
    inward = [(0, 1), (3, 2)]

    def core_sum(kept, *sent, sent_as=BF16):
        return fold(flags, kept, *(to_other(part, 1) for part in sent), sent_as)

    def scores_of(*units, out_as=(BF16, BF16)):
        return partial_scores(units, grads, out_as[: len(units)])

    def straight(value, r):
        pairs = [(0, 3), (3, 0)]
        pairs = [(k * 4 + a, (k ^ r) * 4 + b) for k in range(4) for a, b in pairs]
        return lax.ppermute(value, ("train", "test"), pairs)

    def in_order(parts):
        parts = [parts[0], parts[2], parts[1], parts[3]]
        parts = [jnp.where(chip == 0, parts[q], parts[q ^ 1]) for q in range(4)]
        return jnp.concatenate([jnp.where(core == 0, parts[q], parts[q ^ 2]) for q in range(4)])

    row_ids = jnp.stack([i, i ^ 1, i ^ 2, i ^ 3])[:, None, None, None] * own_rows
    row_ids = row_ids + jnp.arange(own_rows)

    def selected(ids):
        ids = lax.dynamic_slice_in_dim(ids, (core * 2 + chip) * quarter, quarter)
        return jnp.sum((ids[None, :, :, None] == row_ids).astype(F32), axis=2)

    pair_in = along(test_grads, pair)
    middle_in = along(test_grads, middle)
    grads = [train_grads, to_other(train_grads, 1), to_other(train_grads, 2)]
    own, own_sent = core_sum(*product(flags, [[test_grads]], fisher), sent_as=F32)
    counts = selected(chosen_ids)
    far_ids = along(chosen_ids, [(0, 3), (3, 0)])
    pair_in, middle_in, own, own_sent, counts, far_ids, grads[1] = tied(
        pair_in, middle_in, own, own_sent, counts, far_ids, grads[1]
    )

    second_edge = along(middle_in, outward)
    far_in = along(pair_in, middle)
    own_got = to_other(own_sent, 2)
    near, near_sent = core_sum(*product(flags, [[middle_in, pair_in]], fisher))
    near_got = to_other(near_sent, 2)
    far_counts = selected(far_ids)
    grads = grads + [to_other(grads[2], 1)]
    far_in, second_edge, pair_in, own, own_got, near, near_got, far_counts, grads = tied(
        far_in, second_edge, pair_in, own, own_got, near, near_got, far_counts, grads
    )

    first_edge = along(far_in, outward)
    second, second_sent = core_sum(*product(flags, [[far_in, second_edge]], fisher))
    second_sent, pair_in, near, own = tied(second_sent, pair_in, near, own)
    third, third_sent = core_sum(*product(flags, [[pair_in]], fisher))
    near, total = scores_of((near, near_got), (own, own_got), out_as=(BF16, F32))
    total = total + along(near, inward).astype(F32) + along(near, middle).astype(F32)
    (second,) = scores_of((second, to_other(second_sent, 2)))
    total = total + along(second, [(0, 2), (3, 1)]).astype(F32)
    second = along(second, middle)
    third_got = to_other(third_sent, 2)
    first_edge, total, second, third, third_got, grads, far_counts = tied(
        first_edge, total, second, third, third_got, grads, far_counts
    )

    (third,) = scores_of((third, third_got), out_as=(F32,))
    third = along((third + second.astype(F32)).astype(BF16), outward)
    last, last_sent = core_sum(*product(flags, [[first_edge]], fisher))
    last = last_scores(last, to_other(last_sent, 2), far_counts, grads)
    last = in_order([straight(last[r], r) for r in range(4)])

    total = total + third.astype(F32)
    chosen = jnp.sum(total * counts, axis=(0, 2))[:, None]
    total = jnp.pad(total, ((0, 0), (0, 0), (0, 128)))
    column = lax.broadcasted_iota(jnp.int32, total.shape, 2)
    total = jnp.where(column < own_rows, total, chosen)
    total = in_order([total[0]] + [to_other(total[r], r) for r in range(1, 4)])

    turned = (total + last.astype(F32)).T
    return turned[:own_rows], turned[own_rows]


def solution(mesh):
    sizes = (mesh.shape["train"], mesh.shape["test"])
    return jax.shard_map(
        four_by_four if sizes == (4, 4) else any_mesh,
        mesh=mesh,
        in_specs=(
            P(("groups", "train"), "test"),
            P(("groups", "test"), "train"),
            P("train", "test"),
            P(("groups", "test"), None),
        ),
        out_specs=(P(("groups", "train"), "test"), P(("groups", "test"))),
        check_vma=False,
    )
```

time: 218 us -> 245 us (1.12)
  starting transfers between devices: 42.1 us -> 55.2 us
  local copies, waits for them, and re-layouts: 13.7 us -> 23.4 us
  waiting for transfers between devices: 98.1 us -> 92.2 us
  other arithmetic: 5.27 us -> 10.6 us
  Pallas kernels: 57.5 us -> 61.2 us
    ppermute x21, waiting for transfers between devices: 65.8 us -> 36.9 us  [to_other(): return lax.ppermute(value, 'train', [(k, k ^ r) for k in range(4)])]
    ppermute x11, waiting for transfers between devices: 32.3 us -> 50.7 us  [along(): return lax.ppermute(value, 'test', pairs)]
    ppermute x0 -> x4, starting transfers between devices: none -> 15.9 us  [straight(): return lax.ppermute(value, ('train', 'test'), pairs)]
    unnamed x19 -> x49, local copies, waits for them, and re-layouts: 12.7 us -> 21.2 us
    pallas_call x4 -> x6, Pallas kernels: 31.6 us -> 39.2 us  [the longest x5 34.4 us: product(): pl.pallas_call(lambda *refs: product_body(choices, *refs), in_specs=[pl.B...]
    pallas_call x4 -> x3, Pallas kernels: 21.2 us -> 16 us  [partial_scores(): pl.pallas_call(lambda *refs: scores_body(len(units), *refs), in_specs=[VM...]
    ppermute x0 -> x4, waiting for transfers between devices: none -> 4.63 us  [straight(): return lax.ppermute(value, ('train', 'test'), pairs)]
    reduce_sum x2 -> x3, other arithmetic: 3.73 us -> 8.29 us  [the longest x2 7.91 us: selected(): return jnp.sum((ids[None, :, :, None] == row_ids).astype(F32), axis=2)]
  transfers between devices with their start and end apart: 32 -> 36, of which waited for: 17 -> 13; matrix products, arithmetic and copies ran while one was open for 2% -> 5% of each run, Pallas kernels for 24% -> 23%
where the time goes in v7:
time: 245 us; the launch traced here: 244 us
  waiting for transfers between devices  92.2 us (38%)
  Pallas kernels  61.2 us (25%)
  starting transfers between devices  55.2 us (23%)
  local copies, waits for them, and re-layouts  23.4 us (10%)
  other arithmetic  10.6 us (4%)
    ppermute x11, waiting for transfers between devices, along(): return lax.ppermute(value, 'test', pairs)  50.7 us
    ppermute x21, waiting for transfers between devices, to_other(): return lax.ppermute(value, 'train', [(k, k ^ r) for k in range(4)])  36.9 us
    pallas_call x5, Pallas kernels, product(): pl.pallas_call(lambda *refs: product_body(choices, *refs), in_specs=[pl.B...  34.4 us
    ppermute x11, starting transfers between devices, along(): return lax.ppermute(value, 'test', pairs)  28.5 us
    unnamed x49, local copies, waits for them, and re-layouts  21.2 us
    pallas_call x3, Pallas kernels, partial_scores(): pl.pallas_call(lambda *refs: scores_body(len(units), *refs), in_specs=[VM...  16 us
    ppermute x4, starting transfers between devices, straight(): return lax.ppermute(value, ('train', 'test'), pairs)  15.9 us
    ppermute x21, starting transfers between devices, to_other(): return lax.ppermute(value, 'train', [(k, k ^ r) for k in range(4)])  10.8 us
  transfers between devices with their start and end apart: 36, of which 13 were waited for; matrix products, arithmetic and copies ran while one was open for 5% of the time, Pallas kernels for 23%

profile of v7, /device:TPU:0, one launch (start us, length us, event | category | flops | bytes accessed | tf_op | source)
XLA Modules:
  0.0 243.9 jit_solution(5279638232186691167)
XLA Ops:
  0.6 3.1 %collective-permute-start = (bf16[512,2048]{1,0:T(8,128)(2,1)}, bf16[512,2048]{1,0:T(8,128)(2,1)}, u32[]{:S(2)}, u32[]{:S(2)}) collective-permute-start(bf16[512,2048]{1,0:T(8,128)(2,1)} %refs_1_.1), channel_id=1, source_target_pairs={{0,1},{1,0},{2,3},{3,2},{4,5},{5,4},{6,7},{7,6},{8,9},{9,8},{10,11... | collective-permute-start | bytes 6291464 | tf_op jit(solution)/shard_map/ppermute | solution.py:191
  3.7 2.0 collective-permute-start.1
  5.7 1.5 collective-permute-start.12
  7.3 3.4 %copy-done = bf16[2048,2048]{1,0:T(8,128)(2,1)S(1)} copy-done((bf16[2048,2048]{1,0:T(8,128)(2,1)S(1)}, bf16[2048,2048]{1,0:T(8,128)(2,1)}, u32[]{:S(2)}) %copy-start) | copy-done | bytes 8388632
  10.7 1.6 copy-done.10
  12.3 6.4 %product.5 = (f32[256,2048]{1,0:T(8,128)S(1)}, bf16[128,2048]{1,0:T(8,128)(2,1)S(1)}, bf16[128,2048]{1,0:T(8,128)(2,1)}) custom-call(s32[3]{0:T(128)S(1)} %pad_add_fusion.refs_0_.flags, bf16[512,2048]{1,0:T(8,128)(2,1)S(1)} %copy-done.10, bf16[2048,2048]{1,0:T(8,128)(2,1)S(1)} %copy-done), custom_call_target="tpu_custom_call" | custom-call | flops 1 | bytes 1 | tf_op jit(solution)/shard_map/product/pallas_call | solution.py:76
  18.6 1.4 copy-done.8
  20.2 1.7 collective-permute-done.2.got_low
  22.4 1.6 collective-permute-done.3.got_high
  24.0 4.4 %collective-permute-start.4 = (s32[512,16]{0,1:T(8,128)S(1)}, s32[512,16]{0,1:T(8,128)S(1)}, u32[]{:S(2)}, u32[]{:S(2)}) collective-permute-start(s32[512,16]{0,1:T(8,128)S(1)} %copy-done.23), channel_id=1, source_target_pairs={{0,3},{3,0},{4,7},{7,4},{8,11},{11,8},{12,15},{15,12},{16,19},{19,... | collective-permute-start | bytes 98312 | tf_op jit(solution)/shard_map/ppermute | solution.py:191
  28.4 4.5 %convert_reduce_fusion.1 = f32[4,128,512]{2,1,0:T(8,128)} fusion(s32[4,512]{1,0:T(4,128)S(1)} %iota_add_fusion, s32[128,16]{1,0:T(8,128)S(1)} %copy.12), kind=kLoop, calls=%fused_computation.1 | loop fusion | flops 12320768 | bytes 1064960 | tf_op jit(solution)/shard_map/reduce_sum | solution.py:225
  32.9 1.6 copy-done.9
  34.5 1.9 fold.5
  36.4 1.0 copy-done.11
  37.4 15.2 %collective-permute-done.4 = s32[512,16]{0,1:T(8,128)S(1)} collective-permute-done((s32[512,16]{0,1:T(8,128)S(1)}, s32[512,16]{0,1:T(8,128)S(1)}, u32[]{:S(2)}, u32[]{:S(2)}) %collective-permute-start.4) | collective-permute-done | bytes 32800 | tf_op jit(solution)/shard_map/ppermute | solution.py:191
  52.6 2.1 collective-permute-start.6
  54.7 1.3 collective-permute-start.7
  56.1 3.4 %copy-done.1 = bf16[2048,2048]{1,0:T(8,128)(2,1)S(1)} copy-done((bf16[2048,2048]{1,0:T(8,128)(2,1)S(1)}, bf16[2048,2048]{1,0:T(8,128)(2,1)}, u32[]{:S(2)}) %copy-start.1) | copy-done | bytes 8388632
  59.4 7.3 %product.6 = (f32[256,2048]{1,0:T(8,128)S(1)}, bf16[128,2048]{1,0:T(8,128)(2,1)S(1)}, bf16[128,2048]{1,0:T(8,128)(2,1)S(1)}) custom-call(s32[3]{0:T(128)S(1)} %pad_add_fusion.refs_0_.flags, bf16[512,2048]{1,0:T(8,128)(2,1)} %collective-permute-done.1.refs_1_, bf16[512,2048]{1,0:T(8,128)(2,1)} %collective-permute-done.refs_2_.refs_1_, ...), custom_call_target="tpu_custom_call" | custom-call | flops 1 | bytes 1 | tf_op jit(solution)/shard_map/product/pallas_call | solution.py:76
  66.8 0.6 collective-permute-start.10
  67.4 1.5 collective-permute-done.10.got_high
  68.9 1.5 collective-permute-start.8
  70.4 0.8 fold.6
  71.2 1.0 copy-done.15
  72.2 0.7 collective-permute-start.11
  73.1 3.4 %convert_reduce_fusion.counts = f32[4,128,512]{2,1,0:T(8,128)S(1)} fusion(s32[128,16]{1,0:T(8,128)S(1)} %copy.13, s32[4,512]{1,0:T(4,128)S(1)} %iota_add_fusion), kind=kLoop, calls=%fused_computation | loop fusion | flops 12320768 | bytes 1064960 | tf_op jit(solution)/shard_map/reduce_sum | solution.py:225
  76.5 18.6 %collective-permute-done.8.refs_3_ = f32[128,2048]{1,0:T(8,128)S(1)} collective-permute-done((f32[128,2048]{1,0:T(8,128)}, f32[128,2048]{1,0:T(8,128)S(1)}, u32[]{:S(2)}, u32[]{:S(2)}) %collective-permute-start.8) | collective-permute-done | bytes 1048608 | tf_op jit(solution)/shard_map/ppermute | solution.py:194
  95.1 10.7 %collective-permute-done.11.refs_1_ = bf16[128,2048]{1,0:T(8,128)(2,1)S(1)} collective-permute-done((bf16[128,2048]{1,0:T(8,128)(2,1)S(1)}, bf16[128,2048]{1,0:T(8,128)(2,1)S(1)}, u32[]{:S(2)}, u32[]{:S(2)}) %collective-permute-start.11) | collective-permute-done | bytes 524320 | tf_op jit(solution)/shard_map/ppermute | solution.py:194
  105.8 1.3 collective-permute-start.14
  107.1 3.4 %copy-done.2 = bf16[2048,2048]{1,0:T(8,128)(2,1)S(1)} copy-done((bf16[2048,2048]{1,0:T(8,128)(2,1)S(1)}, bf16[2048,2048]{1,0:T(8,128)(2,1)}, u32[]{:S(2)}) %copy-start.2) | copy-done | bytes 8388632
  110.5 7.7 %product.7 = (f32[256,2048]{1,0:T(8,128)S(1)}, bf16[128,2048]{1,0:T(8,128)(2,1)S(1)}, bf16[128,2048]{1,0:T(8,128)(2,1)S(1)}) custom-call(s32[3]{0:T(128)S(1)} %pad_add_fusion.refs_0_.flags, bf16[512,2048]{1,0:T(8,128)(2,1)} %collective-permute-done.6.refs_1_, bf16[512,2048]{1,0:T(8,128)(2,1)} %collective-permute-done.7.refs_2_, bf16[2048,2048]{1,0:T(8,128)(2,1)S(1)} %copy-done.2), custom_call_target="tpu_custom_call" | custom-call | flops 1 | bytes 1 | tf_op jit(solution)/shard_map/product/pallas_call | solution.py:76
  118.8 1.4 collective-permute-done.15.got_low
  120.2 0.7 collective-permute-done.16.got_high
  120.9 0.8 fold.7
  121.8 1.6 collective-permute-start.19
  123.4 7.4 %product.8 = (f32[256,2048]{1,0:T(8,128)S(1)}, bf16[128,2048]{1,0:T(8,128)(2,1)S(1)}, bf16[128,2048]{1,0:T(8,128)(2,1)S(1)}) custom-call(s32[3]{0:T(128)S(1)} %pad_add_fusion.refs_0_.flags, bf16[512,2048]{1,0:T(8,128)(2,1)} %collective-permute-done.refs_2_.refs_1_, bf16[2048,2048]{1,0:T(8,128)(2,1)S(1)} %copy-done.3), custom_call_target="tpu_custom_call" | custom-call | flops 1 | bytes 1 | tf_op jit(solution)/shard_map/product/pallas_call | solution.py:76
  131.4 6.8 %scores.3 = (bf16[4,128,512]{2,1,0:T(8,128)(2,1)S(1)}, f32[4,128,512]{2,1,0:T(8,128)S(1)}) custom-call(f32[128,2048]{1,0:T(8,128)S(1)} %copy-done.16, bf16[128,2048]{1,0:T(8,128)(2,1)S(1)} %copy-done.20, f32[128,2048]{1,0:T(8,128)S(1)} %copy-done.12, f32[128,2048]{1,0:T(8,128)S(1)} %copy-done.14, bf16[512,2048]{1,0:T(8,128)(2,1)S(1)} %copy-done.4, ...), custom_call_target="tpu_custom_call" | custom-call | flops 1 | bytes 1 | tf_op jit(solution)/shard_map/scores/pallas_call | solution.py:142
  138.2 7.4 %collective-permute-start.17 = (bf16[4,128,512]{2,1,0:T(8,128)(2,1)S(1)}, bf16[4,128,512]{2,1,0:T(8,128)(2,1)S(1)}, u32[]{:S(2)}, u32[]{:S(2)}) collective-permute-start(bf16[4,128,512]{2,1,0:T(8,128)(2,1)S(1)} %get-tuple-element.96), channel_id=1, source_target_pairs={{0,1},{3,2},{4,5},{7,6},{8,9},{11,10},{12,13},{15,14},{16,17},{19,... | collective-permute-start | bytes 1572872 | tf_op jit(solution)/shard_map/ppermute | solution.py:191
  145.6 0.7 collective-permute-start.18
  146.3 4.6 %scores.4 = bf16[4,128,512]{2,1,0:T(8,128)(2,1)S(1)} custom-call(f32[128,2048]{1,0:T(8,128)S(1)} %get-tuple-element.97.refs_0_, bf16[128,2048]{1,0:T(8,128)(2,1)S(1)} %collective-permute-done.19.refs_1_, bf16[512,2048]{1,0:T(8,128)(2,1)S(1)} %copy-done.4, bf16[512,2048]{1,0:T(8,128)(2,1)S(1)} %copy-done.6, ...), custom_call_target="tpu_custom_call" | custom-call | flops 1 | bytes 1 | tf_op jit(solution)/shard_map/scores/pallas_call | solution.py:142
  150.9 4.0 %collective-permute-start.20 = (bf16[4,128,512]{2,1,0:T(8,128)(2,1)S(1)}, bf16[4,128,512]{2,1,0:T(8,128)(2,1)S(1)}, u32[]{:S(2)}, u32[]{:S(2)}) collective-permute-start(bf16[4,128,512]{2,1,0:T(8,128)(2,1)S(1)} %scores.4), channel_id=1, source_target_pairs={{0,2},{3,1},{4,6},{7,5},{8,10},{11,9},{12,14},{15,13},{16,18},{19,... | collective-permute-start | bytes 1572872 | tf_op jit(solution)/shard_map/ppermute | solution.py:191
  154.9 0.9 fold.8
  156.0 1.8 collective-permute-done.17
  157.8 0.7 collective-permute-start.21
  158.5 9.7 %collective-permute-done.20 = bf16[4,128,512]{2,1,0:T(8,128)(2,1)S(1)} collective-permute-done((bf16[4,128,512]{2,1,0:T(8,128)(2,1)S(1)}, bf16[4,128,512]{2,1,0:T(8,128)(2,1)S(1)}, u32[]{:S(2)}, u32[]{:S(2)}) %collective-permute-start.20) | collective-permute-done | bytes 524320 | tf_op jit(solution)/shard_map/ppermute | solution.py:191
  168.5 0.7 collective-permute-done.24.refs_1_
  169.2 5.6 %product.9 = (f32[256,2048]{1,0:T(8,128)S(1)}, bf16[128,2048]{1,0:T(8,128)(2,1)S(1)}, bf16[128,2048]{1,0:T(8,128)(2,1)S(1)}) custom-call(s32[3]{0:T(128)S(1)} %pad_add_fusion.refs_0_.flags, bf16[512,2048]{1,0:T(8,128)(2,1)S(1)} %collective-permute-done.14.refs_1_, bf16[2048,2048]{1,0:T(8,128)(2,1)S(1)} %copy-done.3), custom_call_target="tpu_custom_call" | custom-call | flops 1 | bytes 1 | tf_op jit(solution)/shard_map/product/pallas_call | solution.py:76
  175.4 4.6 %scores.5 = f32[4,128,512]{2,1,0:T(8,128)S(1)} custom-call(f32[128,2048]{1,0:T(8,128)S(1)} %get-tuple-element.107.refs_0_, bf16[128,2048]{1,0:T(8,128)(2,1)S(1)} %collective-permute-done.24.refs_1_, bf16[512,2048]{1,0:T(8,128)(2,1)S(1)} %copy-done.4, bf16[512,2048]{1,0:T(8,128)(2,1)S(1)} %copy-done.6, ...), custom_call_target="tpu_custom_call" | custom-call | flops 1 | bytes 1 | tf_op jit(solution)/shard_map/scores/pallas_call | solution.py:142
  180.1 1.6 collective-permute-start.25
  181.8 1.7 fold.9
  183.8 24.0 %collective-permute-done.25 = bf16[4,128,512]{2,1,0:T(8,128)(2,1)S(1)} collective-permute-done((bf16[4,128,512]{2,1,0:T(8,128)(2,1)S(1)}, bf16[4,128,512]{2,1,0:T(8,128)(2,1)S(1)}, u32[]{:S(2)}, u32[]{:S(2)}) %collective-permute-start.25) | collective-permute-done | bytes 524320 | tf_op jit(solution)/shard_map/ppermute | solution.py:191
  208.3 1.0 slice_bitcast_fusion.2
  209.9 2.0 collective-permute-start.28
  211.9 1.6 copy-done.7
  213.5 1.2 copy-done.18
  214.7 4.8 %last_scores.1 = bf16[4,128,640]{2,1,0:T(8,128)(2,1)S(1)} custom-call(f32[128,2048]{1,0:T(8,128)S(1)} %copy-done.18, bf16[128,2048]{1,0:T(8,128)(2,1)} %collective-permute-done.31.got, f32[4,128,512]{2,1,0:T(8,128)S(1)} %convert_reduce_fusion.counts, bf16[512,2048]{1,0:T(8,128)(2,1)S(1)} %copy-done.4, bf16[512,2048]{1,0:T(8,128)(2,1)S(1)} %copy-done.7, ...), custom_call_target="tpu_custom_call" | custom-call | flops 1 | bytes 1 | tf_op jit(solution)/shard_map/last_scores/pallas_call | solution.py:170
  219.6 3.1 %collective-permute-start.32 = (bf16[128,640]{1,0:T(8,128)(2,1)S(1)}, bf16[128,640]{1,0:T(8,128)(2,1)S(1)}, u32[]{:S(2)}, u32[]{:S(2)}) collective-permute-start(bf16[128,640]{1,0:T(8,128)(2,1)S(1)} %get-tuple-element.144), channel_id=1, source_target_pairs={{0,3},{3,0},{4,7},{7,4},{8,11},{11,8},{12,15},{15,12},{16,19},{19,... | collective-permute-start | bytes 491528 | tf_op jit(solution)/shard_map/ppermute | solution.py:213
  222.7 4.1 %collective-permute-start.33 = (bf16[128,640]{1,0:T(8,128)(2,1)S(1)}, bf16[128,640]{1,0:T(8,128)(2,1)S(1)}, u32[]{:S(2)}, u32[]{:S(2)}) collective-permute-start(bf16[128,640]{1,0:T(8,128)(2,1)S(1)} %get-tuple-element.143), channel_id=1, source_target_pairs={{0,11},{3,8},{4,15},{7,12},{8,3},{11,0},{12,7},{15,4},{16,27},{19,... | collective-permute-start | bytes 491528 | tf_op jit(solution)/shard_map/ppermute | solution.py:213
  226.8 2.4 collective-permute-start.34
  229.3 6.3 %collective-permute-start.35 = (bf16[128,640]{1,0:T(8,128)(2,1)S(1)}, bf16[128,640]{1,0:T(8,128)(2,1)S(1)}, u32[]{:S(2)}, u32[]{:S(2)}) collective-permute-start(bf16[128,640]{1,0:T(8,128)(2,1)S(1)} %get-tuple-element.142), channel_id=1, source_target_pairs={{0,15},{3,12},{4,11},{7,8},{8,7},{11,4},{12,3},{15,0},{16,31},{19,... | collective-permute-start | bytes 491528 | tf_op jit(solution)/shard_map/ppermute | solution.py:213
  235.5 1.3 broadcast_select_fusion.13
  236.9 4.6 %collective-permute-done.35 = bf16[128,640]{1,0:T(8,128)(2,1)S(1)} collective-permute-done((bf16[128,640]{1,0:T(8,128)(2,1)S(1)}, bf16[128,640]{1,0:T(8,128)(2,1)S(1)}, u32[]{:S(2)}, u32[]{:S(2)}) %collective-permute-start.35) | collective-permute-done | bytes 163872 | tf_op jit(solution)/shard_map/ppermute | solution.py:213
  241.8 0.7 slice_reduce_fusion
  242.6 1.3 copy.14
  (92 shorter events, 5.3 us)
Async XLA Ops:
  0.6 51.9 %collective-permute-start = (bf16[512,2048]{1,0:T(8,128)(2,1)}, bf16[512,2048]{1,0:T(8,128)(2,1)}, u32[]{:S(2)}, u32[]{:S(2)}) collective-permute-start(bf16[512,2048]{1,0:T(8,128)(2,1)} %refs_1_.1), channel_id=1, source_target_pairs={{0,1},{1,0},{2,3},{3,2},{4,5},{5,4},{6,7},{7,6},{8,9},{9,8},{10,11... | collective-permute-start | bytes 6291464 | tf_op jit(solution)/shard_map/ppermute | solution.py:191
  3.7 48.8 %collective-permute-start.1 = (bf16[512,2048]{1,0:T(8,128)(2,1)}, bf16[512,2048]{1,0:T(8,128)(2,1)}, u32[]{:S(2)}, u32[]{:S(2)}) collective-permute-start(bf16[512,2048]{1,0:T(8,128)(2,1)} %refs_1_.1), channel_id=1, source_target_pairs={{1,2},{2,1},{5,6},{6,5},{9,10},{10,9},{13,14},{14,13},{17,18},{18,... | collective-permute-start | bytes 6291464 | tf_op jit(solution)/shard_map/ppermute | solution.py:191
  5.7 46.9 %collective-permute-start.5 = (bf16[512,2048]{1,0:T(8,128)(2,1)}, bf16[512,2048]{1,0:T(8,128)(2,1)S(1)}, u32[]{:S(2)}, u32[]{:S(2)}) collective-permute-start(bf16[512,2048]{1,0:T(8,128)(2,1)} %refs_0_), channel_id=1, source_target_pairs={{0,4},{4,0},{8,12},{12,8},{1,5},{5,1},{9,13},{13,9},{2,6},{6,2},{1... | collective-permute-start | bytes 6291464 | tf_op jit(solution)/shard_map/ppermute | solution.py:194
  5.7 50.2 %collective-permute-start.12 = (bf16[512,2048]{1,0:T(8,128)(2,1)}, bf16[512,2048]{1,0:T(8,128)(2,1)}, u32[]{:S(2)}, u32[]{:S(2)}) collective-permute-start(bf16[512,2048]{1,0:T(8,128)(2,1)} %refs_0_), channel_id=1, source_target_pairs={{0,8},{4,12},{8,0},{12,4},{1,9},{5,13},{9,1},{13,5},{2,10},{6,14},... | collective-permute-start | bytes 6291464 | tf_op jit(solution)/shard_map/ppermute | solution.py:194
  7.3 3.4 %copy-start = (bf16[2048,2048]{1,0:T(8,128)(2,1)S(1)}, bf16[2048,2048]{1,0:T(8,128)(2,1)}, u32[]{:S(2)}) copy-start(bf16[2048,2048]{1,0:T(8,128)(2,1)} %refs_2_.7) | copy-start | bytes 25165828
  10.7 1.6 copy-start.10
  12.2 9.9 %copy-start.23 = (s32[512,16]{0,1:T(8,128)S(1)}, s32[512,16]{0,1:T(8,128)}, u32[]{:S(2)}) copy-start(s32[512,16]{0,1:T(8,128)} %param.7) | copy-start | bytes 98308
  18.6 1.4 copy-start.8
  20.0 1.9 collective-permute-start.2
  21.9 2.1 collective-permute-start.3
  24.0 28.5 %collective-permute-start.4 = (s32[512,16]{0,1:T(8,128)S(1)}, s32[512,16]{0,1:T(8,128)S(1)}, u32[]{:S(2)}, u32[]{:S(2)}) collective-permute-start(s32[512,16]{0,1:T(8,128)S(1)} %copy-done.23), channel_id=1, source_target_pairs={{0,3},{3,0},{4,7},{7,4},{8,11},{11,8},{12,15},{15,12},{16,19},{19,... | collective-permute-start | bytes 98312 | tf_op jit(solution)/shard_map/ppermute | solution.py:191
  32.9 1.6 copy-start.9
  36.4 1.0 copy-start.11
  52.6 14.2 %copy-start.5 = (bf16[512,2048]{1,0:T(8,128)(2,1)}, bf16[512,2048]{1,0:T(8,128)(2,1)S(1)}, u32[]{:S(2)}) copy-start(bf16[512,2048]{1,0:T(8,128)(2,1)S(1)} %collective-permute-done.5.refs_5_.refs_3_.refs_1_) | copy-start | bytes 6291460
  52.6 53.2 %collective-permute-start.6 = (bf16[512,2048]{1,0:T(8,128)(2,1)}, bf16[512,2048]{1,0:T(8,128)(2,1)}, u32[]{:S(2)}, u32[]{:S(2)}) collective-permute-start(bf16[512,2048]{1,0:T(8,128)(2,1)} %collective-permute-done.refs_2_.refs_1_), channel_id=1, source_target_pairs={{1,2},{2,1},{5,6},{6,5},{9,10},{10,9},{13,14},{14,13},{17,18},{18,... | collective-permute-start | bytes 6291464 | tf_op jit(solution)/shard_map/ppermute | solution.py:191
  54.7 51.1 %collective-permute-start.7 = (bf16[512,2048]{1,0:T(8,128)(2,1)}, bf16[512,2048]{1,0:T(8,128)(2,1)}, u32[]{:S(2)}, u32[]{:S(2)}) collective-permute-start(bf16[512,2048]{1,0:T(8,128)(2,1)} %collective-permute-done.1.refs_1_), channel_id=1, source_target_pairs={{1,0},{2,3},{5,4},{6,7},{9,8},{10,11},{13,12},{14,15},{17,16},{18,... | collective-permute-start | bytes 6291464 | tf_op jit(solution)/shard_map/ppermute | solution.py:191
  56.0 49.8 %collective-permute-start.13 = (bf16[512,2048]{1,0:T(8,128)(2,1)}, bf16[512,2048]{1,0:T(8,128)(2,1)}, u32[]{:S(2)}, u32[]{:S(2)}) collective-permute-start(bf16[512,2048]{1,0:T(8,128)(2,1)} %collective-permute-done.12.refs_6_.refs_4_.refs_2_), channel_id=1, source_target_pairs={{0,4},{4,0},{8,12},{12,8},{1,5},{5,1},{9,13},{13,9},{2,6},{6,2},{1... | collective-permute-start | bytes 6291464 | tf_op jit(solution)/shard_map/ppermute | solution.py:194
  56.0 3.4 %copy-start.1 = (bf16[2048,2048]{1,0:T(8,128)(2,1)S(1)}, bf16[2048,2048]{1,0:T(8,128)(2,1)}, u32[]{:S(2)}) copy-start(bf16[2048,2048]{1,0:T(8,128)(2,1)} %refs_2_.7) | copy-start | bytes 25165828
  66.8 2.1 collective-permute-start.10
  67.3 3.0 %collective-permute-start.9 = (bf16[128,2048]{1,0:T(8,128)(2,1)S(1)}, bf16[128,2048]{1,0:T(8,128)(2,1)S(1)}, u32[]{:S(2)}, u32[]{:S(2)}) collective-permute-start(bf16[128,2048]{1,0:T(8,128)(2,1)S(1)} %get-tuple-element.72), channel_id=1, source_target_pairs={{0,4},{4,0},{8,12},{12,8},{1,5},{5,1},{9,13},{13,9},{2,6},{6,2},{1... | collective-permute-start | bytes 1572872 | tf_op jit(solution)/shard_map/ppermute | solution.py:194
  68.9 26.2 %collective-permute-start.8 = (f32[128,2048]{1,0:T(8,128)}, f32[128,2048]{1,0:T(8,128)S(1)}, u32[]{:S(2)}, u32[]{:S(2)}) collective-permute-start(f32[128,2048]{1,0:T(8,128)} %get-tuple-element.70), channel_id=1, source_target_pairs={{0,8},{4,12},{8,0},{12,4},{1,9},{5,13},{9,1},{13,5},{2,10},{6,14},... | collective-permute-start | bytes 3145736 | tf_op jit(solution)/shard_map/ppermute | solution.py:194
  71.2 1.0 copy-start.15
  72.2 33.6 %collective-permute-start.11 = (bf16[128,2048]{1,0:T(8,128)(2,1)S(1)}, bf16[128,2048]{1,0:T(8,128)(2,1)S(1)}, u32[]{:S(2)}, u32[]{:S(2)}) collective-permute-start(bf16[128,2048]{1,0:T(8,128)(2,1)S(1)} %get-tuple-element.75), channel_id=1, source_target_pairs={{0,8},{4,12},{8,0},{12,4},{1,9},{5,13},{9,1},{13,5},{2,10},{6,14},... | collective-permute-start | bytes 1572872 | tf_op jit(solution)/shard_map/ppermute | solution.py:194
  95.1 23.1 %copy-start.13 = (f32[128,2048]{1,0:T(8,128)}, f32[128,2048]{1,0:T(8,128)S(1)}, u32[]{:S(2)}) copy-start(f32[128,2048]{1,0:T(8,128)S(1)} %collective-permute-done.8.refs_3_) | copy-start | bytes 3145732
  105.8 12.4 %copy-start.19 = (bf16[128,2048]{1,0:T(8,128)(2,1)}, bf16[128,2048]{1,0:T(8,128)(2,1)S(1)}, u32[]{:S(2)}) copy-start(bf16[128,2048]{1,0:T(8,128)(2,1)S(1)} %collective-permute-done.11.refs_1_) | copy-start | bytes 1572868
  105.8 63.4 %collective-permute-start.14 = (bf16[512,2048]{1,0:T(8,128)(2,1)}, bf16[512,2048]{1,0:T(8,128)(2,1)S(1)}, u32[]{:S(2)}, u32[]{:S(2)}) collective-permute-start(bf16[512,2048]{1,0:T(8,128)(2,1)} %collective-permute-done.6.refs_1_), channel_id=1, source_target_pairs={{1,0},{2,3},{5,4},{6,7},{9,8},{10,11},{13,12},{14,15},{17,16},{18,... | collective-permute-start | bytes 6291464 | tf_op jit(solution)/shard_map/ppermute | solution.py:191
  107.1 3.4 %copy-start.2 = (bf16[2048,2048]{1,0:T(8,128)(2,1)S(1)}, bf16[2048,2048]{1,0:T(8,128)(2,1)}, u32[]{:S(2)}) copy-start(bf16[2048,2048]{1,0:T(8,128)(2,1)} %refs_2_.7) | copy-start | bytes 25165828
  110.5 12.9 %copy-start.3 = (bf16[2048,2048]{1,0:T(8,128)(2,1)S(1)}, bf16[2048,2048]{1,0:T(8,128)(2,1)}, u32[]{:S(2)}) copy-start(bf16[2048,2048]{1,0:T(8,128)(2,1)} %refs_2_.7) | copy-start | bytes 25165828
  118.2 2.0 collective-permute-start.15
  118.3 2.6 %collective-permute-start.16 = (bf16[128,2048]{1,0:T(8,128)(2,1)S(1)}, bf16[128,2048]{1,0:T(8,128)(2,1)S(1)}, u32[]{:S(2)}, u32[]{:S(2)}) collective-permute-start(bf16[128,2048]{1,0:T(8,128)(2,1)S(1)} %get-tuple-element.82), channel_id=1, source_target_pairs={{0,4},{4,0},{8,12},{12,8},{1,5},{5,1},{9,13},{13,9},{2,6},{6,2},{1... | collective-permute-start | bytes 1572872 | tf_op jit(solution)/shard_map/ppermute | solution.py:194
  121.7 9.6 %copy-start.4 = (bf16[512,2048]{1,0:T(8,128)(2,1)S(1)}, bf16[512,2048]{1,0:T(8,128)(2,1)}, u32[]{:S(2)}) copy-start(bf16[512,2048]{1,0:T(8,128)(2,1)} %refs_0_) | copy-start | bytes 6291460
  121.7 9.6 %copy-start.6 = (bf16[512,2048]{1,0:T(8,128)(2,1)S(1)}, bf16[512,2048]{1,0:T(8,128)(2,1)}, u32[]{:S(2)}) copy-start(bf16[512,2048]{1,0:T(8,128)(2,1)} %copy-done.5) | copy-start | bytes 6291460
  121.7 9.6 %copy-start.12 = (f32[128,2048]{1,0:T(8,128)S(1)}, f32[128,2048]{1,0:T(8,128)}, u32[]{:S(2)}) copy-start(f32[128,2048]{1,0:T(8,128)} %copy-done.11) | copy-start | bytes 3145732
  121.8 9.6 %copy-start.14 = (f32[128,2048]{1,0:T(8,128)S(1)}, f32[128,2048]{1,0:T(8,128)}, u32[]{:S(2)}) copy-start(f32[128,2048]{1,0:T(8,128)} %copy-done.13) | copy-start | bytes 3145732
  121.8 9.6 %copy-start.16 = (f32[128,2048]{1,0:T(8,128)S(1)}, f32[128,2048]{1,0:T(8,128)}, u32[]{:S(2)}) copy-start(f32[128,2048]{1,0:T(8,128)} %copy-done.15) | copy-start | bytes 3145732
  121.8 9.6 %copy-start.20 = (bf16[128,2048]{1,0:T(8,128)(2,1)S(1)}, bf16[128,2048]{1,0:T(8,128)(2,1)}, u32[]{:S(2)}) copy-start(bf16[128,2048]{1,0:T(8,128)(2,1)} %copy-done.19) | copy-start | bytes 1572868
  121.8 23.8 %collective-permute-start.19 = (bf16[128,2048]{1,0:T(8,128)(2,1)S(1)}, bf16[128,2048]{1,0:T(8,128)(2,1)S(1)}, u32[]{:S(2)}, u32[]{:S(2)}) collective-permute-start(bf16[128,2048]{1,0:T(8,128)(2,1)S(1)} %get-tuple-element.98), channel_id=1, source_target_pairs={{0,8},{4,12},{8,0},{12,4},{1,9},{5,13},{9,1},{13,5},{2,10},{6,14},... | collective-permute-start | bytes 1572872 | tf_op jit(solution)/shard_map/ppermute | solution.py:194
  130.8 20.2 %collective-permute-start.22 = (bf16[128,2048]{1,0:T(8,128)(2,1)S(1)}, bf16[128,2048]{1,0:T(8,128)(2,1)S(1)}, u32[]{:S(2)}, u32[]{:S(2)}) collective-permute-start(bf16[128,2048]{1,0:T(8,128)(2,1)S(1)} %get-tuple-element.101), channel_id=1, source_target_pairs={{0,4},{4,0},{8,12},{12,8},{1,5},{5,1},{9,13},{13,9},{2,6},{6,2},{1... | collective-permute-start | bytes 1572872 | tf_op jit(solution)/shard_map/ppermute | solution.py:194
  130.8 24.1 %collective-permute-start.23 = (bf16[128,2048]{1,0:T(8,128)(2,1)S(1)}, bf16[128,2048]{1,0:T(8,128)(2,1)S(1)}, u32[]{:S(2)}, u32[]{:S(2)}) collective-permute-start(bf16[128,2048]{1,0:T(8,128)(2,1)S(1)} %get-tuple-element.102), channel_id=1, source_target_pairs={{0,4},{4,0},{8,12},{12,8},{1,5},{5,1},{9,13},{13,9},{2,6},{6,2},{1... | collective-permute-start | bytes 1572872 | tf_op jit(solution)/shard_map/ppermute | solution.py:194
  138.2 19.7 %collective-permute-start.17 = (bf16[4,128,512]{2,1,0:T(8,128)(2,1)S(1)}, bf16[4,128,512]{2,1,0:T(8,128)(2,1)S(1)}, u32[]{:S(2)}, u32[]{:S(2)}) collective-permute-start(bf16[4,128,512]{2,1,0:T(8,128)(2,1)S(1)} %get-tuple-element.96), channel_id=1, source_target_pairs={{0,1},{3,2},{4,5},{7,6},{8,9},{11,10},{12,13},{15,14},{16,17},{19,... | collective-permute-start | bytes 1572872 | tf_op jit(solution)/shard_map/ppermute | solution.py:191
  145.6 12.9 %collective-permute-start.18 = (bf16[4,128,512]{2,1,0:T(8,128)(2,1)S(1)}, bf16[4,128,512]{2,1,0:T(8,128)(2,1)S(1)}, u32[]{:S(2)}, u32[]{:S(2)}) collective-permute-start(bf16[4,128,512]{2,1,0:T(8,128)(2,1)S(1)} %get-tuple-element.96), channel_id=1, source_target_pairs={{1,2},{2,1},{5,6},{6,5},{9,10},{10,9},{13,14},{14,13},{17,18},{18,... | collective-permute-start | bytes 1572872 | tf_op jit(solution)/shard_map/ppermute | solution.py:191
  150.9 17.3 %collective-permute-start.20 = (bf16[4,128,512]{2,1,0:T(8,128)(2,1)S(1)}, bf16[4,128,512]{2,1,0:T(8,128)(2,1)S(1)}, u32[]{:S(2)}, u32[]{:S(2)}) collective-permute-start(bf16[4,128,512]{2,1,0:T(8,128)(2,1)S(1)} %scores.4), channel_id=1, source_target_pairs={{0,2},{3,1},{4,6},{7,5},{8,10},{11,9},{12,14},{15,13},{16,18},{19,... | collective-permute-start | bytes 1572872 | tf_op jit(solution)/shard_map/ppermute | solution.py:191
  155.8 13.4 %collective-permute-start.24 = (bf16[128,2048]{1,0:T(8,128)(2,1)S(1)}, bf16[128,2048]{1,0:T(8,128)(2,1)S(1)}, u32[]{:S(2)}, u32[]{:S(2)}) collective-permute-start(bf16[128,2048]{1,0:T(8,128)(2,1)S(1)} %get-tuple-element.104), channel_id=1, source_target_pairs={{0,8},{4,12},{8,0},{12,4},{1,9},{5,13},{9,1},{13,5},{2,10},{6,14},... | collective-permute-start | bytes 1572872 | tf_op jit(solution)/shard_map/ppermute | solution.py:194
  157.8 11.3 %collective-permute-start.21 = (bf16[4,128,512]{2,1,0:T(8,128)(2,1)S(1)}, bf16[4,128,512]{2,1,0:T(8,128)(2,1)S(1)}, u32[]{:S(2)}, u32[]{:S(2)}) collective-permute-start(bf16[4,128,512]{2,1,0:T(8,128)(2,1)S(1)} %scores.4), channel_id=1, source_target_pairs={{1,2},{2,1},{5,6},{6,5},{9,10},{10,9},{13,14},{14,13},{17,18},{18,... | collective-permute-start | bytes 1572872 | tf_op jit(solution)/shard_map/ppermute | solution.py:191
  174.8 7.0 %collective-permute-start.29 = (bf16[128,2048]{1,0:T(8,128)(2,1)S(1)}, bf16[128,2048]{1,0:T(8,128)(2,1)S(1)}, u32[]{:S(2)}, u32[]{:S(2)}) collective-permute-start(bf16[128,2048]{1,0:T(8,128)(2,1)S(1)} %get-tuple-element.117), channel_id=1, source_target_pairs={{0,4},{4,0},{8,12},{12,8},{1,5},{5,1},{9,13},{13,9},{2,6},{6,2},{1... | collective-permute-start | bytes 1572872 | tf_op jit(solution)/shard_map/ppermute | solution.py:194
  174.9 7.0 %collective-permute-start.30 = (bf16[128,2048]{1,0:T(8,128)(2,1)S(1)}, bf16[128,2048]{1,0:T(8,128)(2,1)S(1)}, u32[]{:S(2)}, u32[]{:S(2)}) collective-permute-start(bf16[128,2048]{1,0:T(8,128)(2,1)S(1)} %get-tuple-element.118), channel_id=1, source_target_pairs={{0,4},{4,0},{8,12},{12,8},{1,5},{5,1},{9,13},{13,9},{2,6},{6,2},{1... | collective-permute-start | bytes 1572872 | tf_op jit(solution)/shard_map/ppermute | solution.py:194
  180.1 27.6 %copy-start.22 = (f32[4,128,512]{2,1,0:T(8,128)S(1)}, f32[4,128,512]{2,1,0:T(8,128)}, u32[]{:S(2)}) copy-start(f32[4,128,512]{2,1,0:T(8,128)} %convert_reduce_fusion.1) | copy-start | bytes 3145732
  180.1 27.6 %collective-permute-start.25 = (bf16[4,128,512]{2,1,0:T(8,128)(2,1)S(1)}, bf16[4,128,512]{2,1,0:T(8,128)(2,1)S(1)}, u32[]{:S(2)}, u32[]{:S(2)}) collective-permute-start(bf16[4,128,512]{2,1,0:T(8,128)(2,1)S(1)} %add_convert_fusion), channel_id=1, source_target_pairs={{1,0},{2,3},{5,4},{6,7},{9,8},{10,11},{13,12},{14,15},{17,16},{18,... | collective-permute-start | bytes 1572872 | tf_op jit(solution)/shard_map/ppermute | solution.py:191
  183.5 24.8 %copy-start.17 = (f32[128,2048]{1,0:T(8,128)}, f32[128,2048]{1,0:T(8,128)S(1)}, u32[]{:S(2)}) copy-start(f32[128,2048]{1,0:T(8,128)S(1)} %get-tuple-element.119.kept) | copy-start | bytes 3145732
  183.5 28.4 %collective-permute-start.31 = (bf16[128,2048]{1,0:T(8,128)(2,1)}, bf16[128,2048]{1,0:T(8,128)(2,1)}, u32[]{:S(2)}, u32[]{:S(2)}) collective-permute-start(bf16[128,2048]{1,0:T(8,128)(2,1)} %get-tuple-element.120), channel_id=1, source_target_pairs={{0,8},{4,12},{8,0},{12,4},{1,9},{5,13},{9,1},{13,5},{2,10},{6,14},... | collective-permute-start | bytes 1572872 | tf_op jit(solution)/shard_map/ppermute | solution.py:194
  208.3 1.4 copy-start.21
  209.7 17.1 %collective-permute-start.26 = (f32[128,640]{1,0:T(8,128)}, f32[128,640]{1,0:T(8,128)S(1)}, u32[]{:S(2)}, u32[]{:S(2)}) collective-permute-start(f32[128,640]{1,0:T(8,128)} %get-tuple-element.134), channel_id=1, source_target_pairs={{0,8},{4,12},{8,0},{12,4},{1,9},{5,13},{9,1},{13,5},{2,10},{6,14},... | collective-permute-start | bytes 983048 | tf_op jit(solution)/shard_map/ppermute | solution.py:194
  209.9 19.4 %collective-permute-start.27 = (f32[128,640]{1,0:T(8,128)}, f32[128,640]{1,0:T(8,128)}, u32[]{:S(2)}, u32[]{:S(2)}) collective-permute-start(f32[128,640]{1,0:T(8,128)} %get-tuple-element.136), channel_id=1, source_target_pairs={{0,4},{4,0},{8,12},{12,8},{1,5},{5,1},{9,13},{13,9},{2,6},{6,2},{1... | collective-permute-start | bytes 983048 | tf_op jit(solution)/shard_map/ppermute | solution.py:194
  209.9 25.7 %collective-permute-start.28 = (f32[128,640]{1,0:T(8,128)}, f32[128,640]{1,0:T(8,128)}, u32[]{:S(2)}, u32[]{:S(2)}) collective-permute-start(f32[128,640]{1,0:T(8,128)} %get-tuple-element.135), channel_id=1, source_target_pairs={{0,12},{4,8},{8,4},{12,0},{1,13},{5,9},{9,5},{13,1},{2,14},{6,10},... | collective-permute-start | bytes 983048 | tf_op jit(solution)/shard_map/ppermute | solution.py:194
  211.9 1.6 copy-start.7
  213.5 1.2 copy-start.18
  219.6 17.3 %collective-permute-start.32 = (bf16[128,640]{1,0:T(8,128)(2,1)S(1)}, bf16[128,640]{1,0:T(8,128)(2,1)S(1)}, u32[]{:S(2)}, u32[]{:S(2)}) collective-permute-start(bf16[128,640]{1,0:T(8,128)(2,1)S(1)} %get-tuple-element.144), channel_id=1, source_target_pairs={{0,3},{3,0},{4,7},{7,4},{8,11},{11,8},{12,15},{15,12},{16,19},{19,... | collective-permute-start | bytes 491528 | tf_op jit(solution)/shard_map/ppermute | solution.py:213
  222.7 14.2 %collective-permute-start.33 = (bf16[128,640]{1,0:T(8,128)(2,1)S(1)}, bf16[128,640]{1,0:T(8,128)(2,1)S(1)}, u32[]{:S(2)}, u32[]{:S(2)}) collective-permute-start(bf16[128,640]{1,0:T(8,128)(2,1)S(1)} %get-tuple-element.143), channel_id=1, source_target_pairs={{0,11},{3,8},{4,15},{7,12},{8,3},{11,0},{12,7},{15,4},{16,27},{19,... | collective-permute-start | bytes 491528 | tf_op jit(solution)/shard_map/ppermute | solution.py:213
  226.8 10.1 %collective-permute-start.34 = (bf16[128,640]{1,0:T(8,128)(2,1)S(1)}, bf16[128,640]{1,0:T(8,128)(2,1)S(1)}, u32[]{:S(2)}, u32[]{:S(2)}) collective-permute-start(bf16[128,640]{1,0:T(8,128)(2,1)S(1)} %get-tuple-element.141), channel_id=1, source_target_pairs={{0,7},{3,4},{4,3},{7,0},{8,15},{11,12},{12,11},{15,8},{16,23},{19,... | collective-permute-start | bytes 491528 | tf_op jit(solution)/shard_map/ppermute | solution.py:213
  229.3 12.2 %collective-permute-start.35 = (bf16[128,640]{1,0:T(8,128)(2,1)S(1)}, bf16[128,640]{1,0:T(8,128)(2,1)S(1)}, u32[]{:S(2)}, u32[]{:S(2)}) collective-permute-start(bf16[128,640]{1,0:T(8,128)(2,1)S(1)} %get-tuple-element.142), channel_id=1, source_target_pairs={{0,15},{3,12},{4,11},{7,8},{8,7},{11,4},{12,3},{15,0},{16,31},{19,... | collective-permute-start | bytes 491528 | tf_op jit(solution)/shard_map/ppermute | solution.py:213

commit v8 on v7

v8 whole, which is shorter than its diff:
```python
import functools

import jax
import jax.numpy as jnp
from jax import lax
from jax.experimental import pallas as pl
from jax.experimental.pallas import tpu as pltpu
from jax.sharding import PartitionSpec as P

COLUMNS = 512
EXTRA = 16

F32 = jnp.float32
BF16 = jnp.bfloat16


def dot_t(a, b):
    return lax.dot_general(a, b, (((1,), (1,)), ((), ())), preferred_element_type=F32)


def selection_counts(chosen_ids, first_row, rows):
    row_ids = first_row + lax.broadcasted_iota(jnp.int32, (rows, chosen_ids.shape[0]), 0)
    ids = chosen_ids.T
    counts = jnp.zeros(row_ids.shape, F32)
    for k in range(ids.shape[0]):
        counts = counts + (row_ids == ids[k][None, :]).astype(F32)
    return counts


def any_mesh(train_grads, test_grads, fisher, chosen_ids):
    test_whole = lax.all_gather(test_grads, "test", axis=0, tiled=True)
    partial_value = jnp.dot(test_whole, fisher, preferred_element_type=F32)
    precond = lax.psum(partial_value, "train").astype(BF16)
    partial_scores = dot_t(train_grads, precond)
    scores = lax.psum_scatter(partial_scores, "test", scatter_dimension=1, tiled=True)
    rows = scores.shape[0]
    counts = selection_counts(chosen_ids, lax.axis_index("train") * rows, rows)
    return scores, lax.psum(jnp.sum(counts * scores, axis=0), "train")


SMALL = pl.CostEstimate(flops=1, bytes_accessed=1, transcendentals=0)
PARAMS = pltpu.CompilerParams(vmem_limit_bytes=16 * 2**20)


VMEM = pl.BlockSpec(memory_space=pltpu.VMEM)


def product_body(count, flags, *refs):
    blocks, fisher, outs = refs[:count], refs[count], refs[count + 1 :]
    quarter = blocks[0].shape[0] // 4
    mine = flags[0] == 0

    def multiply(block, kept, *sent):
        @pl.loop(0, fisher.shape[1] // COLUMNS)
        def _(n):
            columns = pl.ds(pl.multiple_of(n * COLUMNS, COLUMNS), COLUMNS)
            value = jnp.dot(block[...], fisher[:, columns], preferred_element_type=F32)
            for chip in range(2):
                low, high = (value[(2 * core + chip) * quarter :][:quarter] for core in range(2))
                kept[pl.ds(chip * quarter, quarter), columns] = jnp.where(mine, low, high)
                other = jnp.where(mine, high, low).astype(BF16)
                if len(sent) == 2:
                    sent[chip][:, columns] = other
                else:
                    sent[0][pl.ds(chip * quarter, quarter), columns] = other

    if len(blocks) == 1:
        multiply(blocks[0], *outs)
    else:
        pl.when(flags[2] == 1)(lambda: multiply(blocks[0], *outs))
        pl.when(flags[2] == 0)(lambda: multiply(blocks[1], *outs))


def product(flags, blocks, fisher, ways=2):
    half = blocks[0].shape[0] // 2
    columns = fisher.shape[1]
    sent = jax.ShapeDtypeStruct((half // ways, columns), BF16)
    return pl.pallas_call(
        functools.partial(product_body, len(blocks)),
        in_specs=[pl.BlockSpec(memory_space=pltpu.SMEM)] + [VMEM] * (len(blocks) + 1),
        out_specs=[VMEM] * (1 + ways),
        out_shape=[jax.ShapeDtypeStruct((half, columns), F32)] + [sent] * ways,
        compiler_params=PARAMS,
        cost_estimate=SMALL,
        name="product",
    )(flags, *blocks, fisher)


def fold_body(flags, kept, *refs):
    got, kept_out, sent_out = refs[:-2], refs[-2], refs[-1]
    half = kept_out.shape[0]
    first = flags[1] == 0

    @pl.loop(0, kept.shape[1] // COLUMNS)
    def _(n):
        columns = pl.ds(pl.multiple_of(n * COLUMNS, COLUMNS), COLUMNS)
        if len(got) == 2:
            low, high = got[0][:, columns], got[1][:, columns]
        else:
            low, high = got[0][:half, columns], got[0][half:, columns]
        low = kept[:half, columns] + low.astype(F32)
        high = kept[half:, columns] + high.astype(F32)
        kept_out[:, columns] = jnp.where(first, low, high)
        sent_out[:, columns] = jnp.where(first, high, low).astype(sent_out.dtype)


def fold(flags, kept, got, sent_as):
    shape = (kept.shape[0] // 2, kept.shape[1])
    return pl.pallas_call(
        fold_body,
        in_specs=[pl.BlockSpec(memory_space=pltpu.SMEM)] + [VMEM] * (1 + len(got)),
        out_specs=[VMEM, VMEM],
        out_shape=[jax.ShapeDtypeStruct(shape, F32), jax.ShapeDtypeStruct(shape, sent_as)],
        compiler_params=PARAMS,
        cost_estimate=SMALL,
        name="fold",
    )(flags, kept, *got)


def split_sum(kept, got):
    value = kept[...] + got[...].astype(F32)
    high = value.astype(BF16)
    return high, (value - high.astype(F32)).astype(BF16)


def scores_body(units, *refs):
    sums, grads, outs = refs[: 2 * units], refs[2 * units :][:4], refs[2 * units + 4 :]
    rows = sums[0].shape[0]
    precond = jnp.concatenate(
        [part for u in range(units) for part in split_sum(sums[2 * u], sums[2 * u + 1])]
    )
    for r in range(4):
        both = dot_t(grads[r][...], precond)
        for u in range(units):
            value = both[:, 2 * u * rows :][:, :rows] + both[:, (2 * u + 1) * rows :][:, :rows]
            outs[u][r] = value.astype(outs[u].dtype)


def partial_scores(units, grads, out_as):
    rows = units[0][0].shape[0]
    train_rows = grads[0].shape[0]
    return pl.pallas_call(
        lambda *refs: scores_body(len(units), *refs),
        in_specs=[VMEM] * (2 * len(units) + 4),
        out_specs=[VMEM] * len(units),
        out_shape=[jax.ShapeDtypeStruct((4, train_rows, rows), kind) for kind in out_as],
        compiler_params=PARAMS,
        cost_estimate=SMALL,
        name="scores",
    )(*[value for unit in units for value in unit], *grads)


def last_scores_body(kept, got, counts, *refs):
    grads, out = refs[:4], refs[4]
    rows = kept.shape[0]
    train_rows = grads[0].shape[0]
    precond = jnp.concatenate(split_sum(kept, got))
    chosen = jnp.zeros((1, rows), F32)
    for r in range(4):
        both = dot_t(grads[r][...], precond)
        value = both[:, :rows] + both[:, rows:]
        out[r, :train_rows] = value.astype(out.dtype)
        chosen = chosen + jnp.sum(value * counts[r], axis=0, keepdims=True)
    for r in range(4):
        out[r, train_rows:] = jnp.broadcast_to(chosen, (EXTRA, rows)).astype(out.dtype)


def last_scores(kept, got, counts, grads):
    rows = kept.shape[0]
    return pl.pallas_call(
        last_scores_body,
        in_specs=[VMEM] * 7,
        out_specs=VMEM,
        out_shape=jax.ShapeDtypeStruct((4, grads[0].shape[0] + EXTRA, rows), BF16),
        compiler_params=PARAMS,
        cost_estimate=SMALL,
        name="last_scores",
    )(kept, got, counts, *grads)


def four_by_four(train_grads, test_grads, fisher, chosen_ids):
    z = lax.axis_index("test")
    i = lax.axis_index("train")
    chip, core = i // 2, i % 2
    inner = (z == 1) | (z == 2)
    flags = jnp.stack([core, chip, inner.astype(jnp.int32)])
    own_rows = train_grads.shape[0]
    quarter = test_grads.shape[0] // 4

    def along(value, pairs):
        return lax.ppermute(value, "test", pairs)

    def to_other(value, r):
        return lax.ppermute(value, "train", [(k, k ^ r) for k in range(4)])

    def tied(*values):
        return lax.optimization_barrier(values)

    pair = [(0, 1), (1, 0), (2, 3), (3, 2)]
    middle = [(1, 2), (2, 1)]
    outward = [(1, 0), (2, 3)]
    inward = [(0, 1), (3, 2)]

    def core_sum(kept, *sent, sent_as=BF16):
        return fold(flags, kept, [to_other(part, 1) for part in sent], sent_as)

    def scores_of(*units, out_as=(BF16, BF16)):
        return partial_scores(units, grads, out_as[: len(units)])

    def straight(value, r):
        pairs = [(0, 3), (3, 0)]
        pairs = [(k * 4 + a, (k ^ r) * 4 + b) for k in range(4) for a, b in pairs]
        return lax.ppermute(value, ("train", "test"), pairs)

    def in_order(parts):
        parts = [parts[0], parts[2], parts[1], parts[3]]
        parts = [jnp.where(chip == 0, parts[q], parts[q ^ 1]) for q in range(4)]
        parts = [jnp.where(core == 0, parts[q], parts[q ^ 2]) for q in range(4)]
        return jnp.concatenate(parts, axis=1)

    row_ids = jnp.stack([i, i ^ 1, i ^ 2, i ^ 3])[:, None] * own_rows + jnp.arange(own_rows)

    def selected(ids):
        ids = lax.dynamic_slice_in_dim(ids, (core * 2 + chip) * quarter, quarter).T
        return sum((ids[k] == row_ids[:, :, None]).astype(F32) for k in range(ids.shape[0]))

    pair_in = along(test_grads, pair)
    middle_in = along(test_grads, middle)
    grads = [train_grads, to_other(train_grads, 1), to_other(train_grads, 2)]
    own, own_sent = core_sum(*product(flags, [test_grads], fisher), sent_as=F32)
    counts = selected(chosen_ids)
    far_ids = along(chosen_ids, [(0, 3), (3, 0)])
    pair_in, middle_in, own, own_sent, counts, far_ids, grads[1] = tied(
        pair_in, middle_in, own, own_sent, counts, far_ids, grads[1]
    )

    second_edge = along(middle_in, outward)
    far_in = along(pair_in, middle)
    own_got = to_other(own_sent, 2)
    near, near_sent = core_sum(*product(flags, [middle_in, pair_in], fisher))
    near_got = to_other(near_sent, 2)
    far_counts = selected(far_ids)
    grads = grads + [to_other(grads[2], 1)]
    far_in, second_edge, pair_in, own, own_got, near, near_got, far_counts, grads = tied(
        far_in, second_edge, pair_in, own, own_got, near, near_got, far_counts, grads
    )

    first_edge = along(far_in, outward)
    near, total = scores_of((near, near_got), (own, own_got), out_as=(BF16, F32))
    near_in, near_across = along(near, inward), along(near, middle)
    far_in, pair_in, near = tied(far_in, pair_in, near)
    second, second_sent = core_sum(*product(flags, [far_in, second_edge], fisher))
    third, third_sent = core_sum(*product(flags, [pair_in], fisher, 1))
    second, near_in, near_across = tied(second, near_in, near_across)
    (second,) = scores_of((second, to_other(second_sent, 2)))
    across = along(second, middle)
    (third,) = scores_of((third, to_other(third_sent, 2)), out_as=(F32,))
    first_edge, total, near_in, near_across, second, across, third, grads, far_counts = tied(
        first_edge, total, near_in, near_across, second, across, third, grads, far_counts
    )

    third = along((third + across.astype(F32)).astype(BF16), outward)
    second = along(second, [(0, 2), (3, 1)])
    last, last_sent = core_sum(*product(flags, [first_edge], fisher))
    last = last_scores(last, to_other(last_sent, 2), far_counts, grads)
    last, second, third = tied(last, second, third)
    last = in_order([straight(last[r], r) for r in range(4)])

    total = total + sum(value.astype(F32) for value in (near_in, near_across, second, third))
    chosen = jnp.sum(total * counts, axis=(0, 1))
    total = [jnp.concatenate([part, jnp.broadcast_to(chosen, (8, quarter))]) for part in total]
    total = in_order([total[0]] + [to_other(total[r], r) for r in range(1, 4)])

    scores = total[:own_rows] + last[:own_rows].astype(F32)
    return scores, total[own_rows] + last[own_rows].astype(F32)


def solution(mesh):
    sizes = (mesh.shape["train"], mesh.shape["test"])
    return jax.shard_map(
        four_by_four if sizes == (4, 4) else any_mesh,
        mesh=mesh,
        in_specs=(
            P(("groups", "train"), "test"),
            P(("groups", "test"), "train"),
            P("train", "test"),
            P(("groups", "test"), None),
        ),
        out_specs=(P(("groups", "train"), "test"), P(("groups", "test"))),
        check_vma=False,
    )
```

time: 245 us -> 234 us (0.955)
  starting transfers between devices: 55.2 us -> 62.4 us
  local copies, waits for them, and re-layouts: 23.4 us -> 16.8 us
  waiting for transfers between devices: 92.2 us -> 87.1 us
  Pallas kernels: 61.2 us -> 56.4 us
    ppermute x11, waiting for transfers between devices: 50.7 us -> 29.6 us  [along(): return lax.ppermute(value, 'test', pairs)]
    ppermute x21 -> x20, waiting for transfers between devices: 36.9 us -> 57.5 us  [to_other(): return lax.ppermute(value, 'train', [(k, k ^ r) for k in range(4)])]
    reduce_sum x3 -> x1, other arithmetic: 8.29 us -> 1.56 us  [four_by_four(): chosen = jnp.sum(total * counts, axis=(0, 1))]
    add x2 -> x5, other arithmetic: 0.35 us -> 6.01 us  [the longest x2 4.22 us: selected(): sum(((ids[k] == row_ids[:, :, None]).astype(F32) for k in range(ids.shape...]
    ppermute x11, starting transfers between devices: 28.5 us -> 33.5 us  [along(): return lax.ppermute(value, 'test', pairs)]
    ppermute x4, waiting for transfers between devices: 4.63 us -> 0.01 us  [straight(): return lax.ppermute(value, ('train', 'test'), pairs)]
    unnamed x49 -> x46, local copies, waits for them, and re-layouts: 21.2 us -> 16.7 us
    pallas_call x5, Pallas kernels: 34.4 us -> 31.8 us  [product(): pl.pallas_call(functools.partial(product_body, len(blocks)), in_specs=[pl...]
  transfers between devices with their start and end apart: 36 -> 35, of which waited for: 13 -> 16; matrix products, arithmetic and copies ran while one was open for 5% -> 3% of each run, Pallas kernels for 23% -> 21%
where the time goes in v8:
time: 234 us; the launch traced here: 233 us
  waiting for transfers between devices  87.1 us (37%)
  starting transfers between devices  62.4 us (27%)
  Pallas kernels  56.4 us (24%)
  local copies, waits for them, and re-layouts  16.8 us (7%)
  other arithmetic  9.02 us (4%)
    ppermute x20, waiting for transfers between devices, to_other(): return lax.ppermute(value, 'train', [(k, k ^ r) for k in range(4)])  57.5 us
    ppermute x11, starting transfers between devices, along(): return lax.ppermute(value, 'test', pairs)  33.5 us
    pallas_call x5, Pallas kernels, product(): pl.pallas_call(functools.partial(product_body, len(blocks)), in_specs=[pl...  31.8 us
    ppermute x11, waiting for transfers between devices, along(): return lax.ppermute(value, 'test', pairs)  29.6 us
    unnamed x46, local copies, waits for them, and re-layouts  16.7 us
    ppermute x4, starting transfers between devices, straight(): return lax.ppermute(value, ('train', 'test'), pairs)  15.9 us
    pallas_call x3, Pallas kernels, partial_scores(): pl.pallas_call(lambda *refs: scores_body(len(units), *refs), in_specs=[VM...  15.4 us
    ppermute x20, starting transfers between devices, to_other(): return lax.ppermute(value, 'train', [(k, k ^ r) for k in range(4)])  13 us
  transfers between devices with their start and end apart: 35, of which 16 were waited for; matrix products, arithmetic and copies ran while one was open for 3% of the time, Pallas kernels for 21%

profile of v8, /device:TPU:0, one launch (start us, length us, event | category | flops | bytes accessed | tf_op | source)
XLA Modules:
  0.0 232.8 jit_solution(6474499195457838544)
XLA Ops:
  0.6 3.1 %collective-permute-start = (bf16[512,2048]{1,0:T(8,128)(2,1)}, bf16[512,2048]{1,0:T(8,128)(2,1)}, u32[]{:S(2)}, u32[]{:S(2)}) collective-permute-start(bf16[512,2048]{1,0:T(8,128)(2,1)} %refs_0_.1), channel_id=1, source_target_pairs={{0,1},{1,0},{2,3},{3,2},{4,5},{5,4},{6,7},{7,6},{8,9},{9,8},{10,11... | collective-permute-start | bytes 6291464 | tf_op jit(solution)/shard_map/ppermute | solution.py:191
  3.7 2.1 collective-permute-start.1
  5.8 1.5 collective-permute-start.12
  7.3 3.4 %copy-done = bf16[2048,2048]{1,0:T(8,128)(2,1)S(1)} copy-done((bf16[2048,2048]{1,0:T(8,128)(2,1)S(1)}, bf16[2048,2048]{1,0:T(8,128)(2,1)}, u32[]{:S(2)}) %copy-start) | copy-done | bytes 8388632
  10.7 1.6 copy-done.10
  12.3 6.4 %product.5 = (f32[256,2048]{1,0:T(8,128)S(1)}, bf16[128,2048]{1,0:T(8,128)(2,1)}, bf16[128,2048]{1,0:T(8,128)(2,1)S(1)}) custom-call(s32[3]{0:T(128)S(1)} %pad_add_fusion.flags, bf16[512,2048]{1,0:T(8,128)(2,1)S(1)} %copy-done.10, bf16[2048,2048]{1,0:T(8,128)(2,1)S(1)} %copy-done), custom_call_target="tpu_custom_call" | custom-call | flops 1 | bytes 1 | tf_op jit(solution)/shard_map/product/pallas_call | solution.py:78
  18.7 1.4 copy-done.8
  20.3 1.9 collective-permute-done.2.refs_0_
  22.6 1.5 collective-permute-done.3.refs_1_
  24.1 4.4 %collective-permute-start.4 = (s32[512,16]{0,1:T(8,128)S(1)}, s32[512,16]{0,1:T(8,128)S(1)}, u32[]{:S(2)}, u32[]{:S(2)}) collective-permute-start(s32[512,16]{0,1:T(8,128)S(1)} %copy-done.20), channel_id=1, source_target_pairs={{0,3},{3,0},{4,7},{7,4},{8,11},{11,8},{12,15},{15,12},{16,19},{19,... | collective-permute-start | bytes 98312 | tf_op jit(solution)/shard_map/ppermute | solution.py:191
  28.5 2.6 %convert_add_fusion.1 = f32[4,512,128]{2,1,0:T(8,128)} fusion(s32[128]{0:T(128)S(1)} %get-tuple-element.167, s32[128]{0:T(128)S(1)} %get-tuple-element.168, s32[128]{0:T(128)S(1)} %get-tuple-element.169, s32[128]{0:T(128)S(1)} %get-tuple-element.170, s32[128]{0:T(128)S(1)} %get-tuple-element.171, s32[128]{0:T(128)S(1)} %get-tuple-element.172, ...), kind=kLoop, calls=%fused_computation.6 | loop fusion | flops 12320768 | bytes 1064960 | tf_op jit(solution)/shard_map/add | solution.py:225
  31.0 1.6 copy-done.9
  32.6 0.9 fold.5
  33.5 19.1 %collective-permute-done.4 = s32[512,16]{0,1:T(8,128)S(1)} collective-permute-done((s32[512,16]{0,1:T(8,128)S(1)}, s32[512,16]{0,1:T(8,128)S(1)}, u32[]{:S(2)}, u32[]{:S(2)}) %collective-permute-start.4) | collective-permute-done | bytes 32800 | tf_op jit(solution)/shard_map/ppermute | solution.py:191
  52.6 0.8 collective-permute-start.6
  53.4 1.3 collective-permute-start.7
  54.8 3.4 %copy-done.1 = bf16[2048,2048]{1,0:T(8,128)(2,1)S(1)} copy-done((bf16[2048,2048]{1,0:T(8,128)(2,1)S(1)}, bf16[2048,2048]{1,0:T(8,128)(2,1)}, u32[]{:S(2)}) %copy-start.1) | copy-done | bytes 8388632
  58.2 7.3 %product.6 = (f32[256,2048]{1,0:T(8,128)S(1)}, bf16[128,2048]{1,0:T(8,128)(2,1)S(1)}, bf16[128,2048]{1,0:T(8,128)(2,1)S(1)}) custom-call(s32[3]{0:T(128)S(1)} %pad_add_fusion.flags, bf16[512,2048]{1,0:T(8,128)(2,1)} %collective-permute-done.1.refs_0_, bf16[512,2048]{1,0:T(8,128)(2,1)} %collective-permute-done.refs_1_.refs_0_, bf16[2048,2048]{1,0:T(8,128)(2,1)S(1)} %copy-done.1), custom_call_target="tpu_custom_call" | custom-call | flops 1 | bytes 1 | tf_op jit(solution)/shard_map/product/pallas_call | solution.py:78
  66.2 1.5 collective-permute-done.10.refs_1_
  67.6 1.5 collective-permute-start.8
  69.1 0.8 fold.6
  70.0 0.8 collective-permute-start.11
  70.8 1.7 convert_add_fusion.counts
  72.4 21.2 %collective-permute-done.8.refs_3_ = f32[128,2048]{1,0:T(8,128)S(1)} collective-permute-done((f32[128,2048]{1,0:T(8,128)S(1)}, f32[128,2048]{1,0:T(8,128)S(1)}, u32[]{:S(2)}, u32[]{:S(2)}) %collective-permute-start.8) | collective-permute-done | bytes 1048608 | tf_op jit(solution)/shard_map/ppermute | solution.py:194
  93.6 10.7 %collective-permute-done.11.refs_1_ = bf16[128,2048]{1,0:T(8,128)(2,1)S(1)} collective-permute-done((bf16[128,2048]{1,0:T(8,128)(2,1)S(1)}, bf16[128,2048]{1,0:T(8,128)(2,1)S(1)}, u32[]{:S(2)}, u32[]{:S(2)}) %collective-permute-start.11) | collective-permute-done | bytes 524320 | tf_op jit(solution)/shard_map/ppermute | solution.py:194
  104.4 1.6 collective-permute-start.14
  106.0 6.6 %scores.3 = (bf16[4,512,128]{2,1,0:T(8,128)(2,1)S(1)}, f32[4,512,128]{2,1,0:T(8,128)S(1)}) custom-call(f32[128,2048]{1,0:T(8,128)S(1)} %get-tuple-element.84.refs_0_, bf16[128,2048]{1,0:T(8,128)(2,1)S(1)} %collective-permute-done.11.refs_1_, f32[128,2048]{1,0:T(8,128)S(1)} %get-tuple-element.86.refs_2_, f32[128,2048]{1,0:T(8,128)S(1)} %collective-permute-done.8.refs_3_, ...), custom_call_target="tpu_custom_call" | custom-call | flops 1 | bytes 1 | tf_op jit(solution)/shard_map/scores/pallas_call | solution.py:142
  112.6 1.0 copy-done.11
  113.6 5.8 %product.7 = (f32[256,2048]{1,0:T(8,128)S(1)}, bf16[128,2048]{1,0:T(8,128)(2,1)S(1)}, bf16[128,2048]{1,0:T(8,128)(2,1)S(1)}) custom-call(s32[3]{0:T(128)S(1)} %pad_add_fusion.flags, bf16[512,2048]{1,0:T(8,128)(2,1)S(1)} %collective-permute-done.6.refs_0_, bf16[512,2048]{1,0:T(8,128)(2,1)S(1)} %collective-permute-done.7.refs_1_, bf16[2048,2048]{1,0:T(8,128)(2,1)S(1)} %bitcast.93), custom_call_target="tpu_custom_call" | custom-call | flops 1 | bytes 1 | tf_op jit(solution)/shard_map/product/pallas_call | solution.py:78
  119.4 6.7 %product.8 = (f32[256,2048]{1,0:T(8,128)S(1)}, bf16[256,2048]{1,0:T(8,128)(2,1)S(1)}) custom-call(s32[3]{0:T(128)S(1)} %pad_add_fusion.flags, bf16[512,2048]{1,0:T(8,128)(2,1)} %collective-permute-done.refs_1_.refs_0_, bf16[2048,2048]{1,0:T(8,128)(2,1)S(1)} %bitcast.93), custom_call_target="tpu_custom_call" | custom-call | flops 1 | bytes 1 | tf_op jit(solution)/shard_map/product/pallas_call | solution.py:78
  126.8 7.3 %collective-permute-start.17 = (bf16[4,512,128]{2,1,0:T(8,128)(2,1)S(1)}, bf16[4,512,128]{2,1,0:T(8,128)(2,1)S(1)}, u32[]{:S(2)}, u32[]{:S(2)}) collective-permute-start(bf16[4,512,128]{2,1,0:T(8,128)(2,1)S(1)} %get-tuple-element.94), channel_id=1, source_target_pairs={{0,1},{3,2},{4,5},{7,6},{8,9},{11,10},{12,13},{15,14},{16,17},{19,... | collective-permute-start | bytes 1572872 | tf_op jit(solution)/shard_map/ppermute | solution.py:191
  134.2 0.7 collective-permute-start.18
  134.9 0.8 fold.7
  135.7 1.6 collective-permute-start.19
  137.2 8.6 %collective-permute-done.17 = bf16[4,512,128]{2,1,0:T(8,128)(2,1)S(1)} collective-permute-done((bf16[4,512,128]{2,1,0:T(8,128)(2,1)S(1)}, bf16[4,512,128]{2,1,0:T(8,128)(2,1)S(1)}, u32[]{:S(2)}, u32[]{:S(2)}) %collective-permute-start.17) | collective-permute-done | bytes 524320 | tf_op jit(solution)/shard_map/ppermute | solution.py:191
  145.9 0.8 fold.8
  146.7 1.6 collective-permute-start.22
  148.3 2.1 collective-permute-done.19.refs_1_
  150.4 4.8 %scores.4 = bf16[4,512,128]{2,1,0:T(8,128)(2,1)} custom-call(f32[128,2048]{1,0:T(8,128)S(1)} %get-tuple-element.103.refs_0_, bf16[128,2048]{1,0:T(8,128)(2,1)S(1)} %collective-permute-done.19.refs_1_, bf16[512,2048]{1,0:T(8,128)(2,1)S(1)} %copy-done.2, bf16[512,2048]{1,0:T(8,128)(2,1)S(1)} %copy-done.4, ...), custom_call_target="tpu_custom_call" | custom-call | flops 1 | bytes 1 | tf_op jit(solution)/shard_map/scores/pallas_call | solution.py:142
  155.9 5.1 %collective-permute-done.22.refs_1_ = bf16[128,2048]{1,0:T(8,128)(2,1)S(1)} collective-permute-done((bf16[128,2048]{1,0:T(8,128)(2,1)S(1)}, bf16[128,2048]{1,0:T(8,128)(2,1)S(1)}, u32[]{:S(2)}, u32[]{:S(2)}) %collective-permute-start.22) | collective-permute-done | bytes 524320 | tf_op jit(solution)/shard_map/ppermute | solution.py:194
  161.0 4.0 %scores.5 = f32[4,512,128]{2,1,0:T(8,128)S(1)} custom-call(f32[128,2048]{1,0:T(8,128)S(1)} %get-tuple-element.108.refs_0_, bf16[128,2048]{1,0:T(8,128)(2,1)S(1)} %collective-permute-done.22.refs_1_, bf16[512,2048]{1,0:T(8,128)(2,1)S(1)} %copy-done.2, bf16[512,2048]{1,0:T(8,128)(2,1)S(1)} %copy-done.4, ...), custom_call_target="tpu_custom_call" | custom-call | flops 1 | bytes 1 | tf_op jit(solution)/shard_map/scores/pallas_call | solution.py:142
  165.0 5.6 %product.9 = (f32[256,2048]{1,0:T(8,128)S(1)}, bf16[128,2048]{1,0:T(8,128)(2,1)S(1)}, bf16[128,2048]{1,0:T(8,128)(2,1)S(1)}) custom-call(s32[3]{0:T(128)S(1)} %pad_add_fusion.flags, bf16[512,2048]{1,0:T(8,128)(2,1)S(1)} %collective-permute-done.14.refs_0_, bf16[2048,2048]{1,0:T(8,128)(2,1)S(1)} %bitcast.93), custom_call_target="tpu_custom_call" | custom-call | flops 1 | bytes 1 | tf_op jit(solution)/shard_map/product/pallas_call | solution.py:78
  171.2 1.4 collective-permute-done.23.refs_0_
  172.6 0.7 collective-permute-done.24.refs_1_
  173.3 1.6 fold.9
  174.9 1.5 collective-permute-start.25
  176.4 0.9 add_convert_fusion
  177.4 1.3 collective-permute-start.27
  178.7 10.3 %collective-permute-start.26 = (bf16[4,512,128]{2,1,0:T(8,128)(2,1)}, bf16[4,512,128]{2,1,0:T(8,128)(2,1)}, u32[]{:S(2)}, u32[]{:S(2)}) collective-permute-start(bf16[4,512,128]{2,1,0:T(8,128)(2,1)} %scores.4), channel_id=1, source_target_pairs={{0,2},{3,1},{4,6},{7,5},{8,10},{11,9},{12,14},{15,13},{16,18},{19,... | collective-permute-start | bytes 1572872 | tf_op jit(solution)/shard_map/ppermute | solution.py:191
  189.2 1.6 copy-done.5
  190.8 1.6 copy-done.7
  192.4 1.2 copy-done.14
  193.6 4.3 %last_scores.1 = bf16[4,528,128]{2,1,0:T(8,128)(2,1)S(1)} custom-call(f32[128,2048]{1,0:T(8,128)S(1)} %copy-done.14, bf16[128,2048]{1,0:T(8,128)(2,1)} %collective-permute-done.25.got, f32[4,512,128]{2,1,0:T(8,128)S(1)} %convert_add_fusion.counts, bf16[512,2048]{1,0:T(8,128)(2,1)S(1)} %copy-done.2, bf16[512,2048]{1,0:T(8,128)(2,1)S(1)} %copy-done.5, ...), custom_call_target="tpu_custom_call" | custom-call | flops 1 | bytes 1 | tf_op jit(solution)/shard_map/last_scores/pallas_call | solution.py:170
  197.9 1.7 collective-permute-done.26
  199.7 3.7 %collective-permute-start.31 = (bf16[528,128]{1,0:T(8,128)(2,1)S(1)}, bf16[528,128]{1,0:T(8,128)(2,1)S(1)}, u32[]{:S(2)}, u32[]{:S(2)}) collective-permute-start(bf16[528,128]{1,0:T(8,128)(2,1)S(1)} %get-tuple-element.149), channel_id=1, source_target_pairs={{0,3},{3,0},{4,7},{7,4},{8,11},{11,8},{12,15},{15,12},{16,19},{19,... | collective-permute-start | bytes 405512 | tf_op jit(solution)/shard_map/ppermute | solution.py:213
  203.4 4.0 %collective-permute-start.32 = (bf16[528,128]{1,0:T(8,128)(2,1)S(1)}, bf16[528,128]{1,0:T(8,128)(2,1)S(1)}, u32[]{:S(2)}, u32[]{:S(2)}) collective-permute-start(bf16[528,128]{1,0:T(8,128)(2,1)S(1)} %get-tuple-element.148), channel_id=1, source_target_pairs={{0,11},{3,8},{4,15},{7,12},{8,3},{11,0},{12,7},{15,4},{16,27},{19,... | collective-permute-start | bytes 405512 | tf_op jit(solution)/shard_map/ppermute | solution.py:213
  207.5 2.6 %collective-permute-start.33 = (bf16[528,128]{1,0:T(8,128)(2,1)S(1)}, bf16[528,128]{1,0:T(8,128)(2,1)S(1)}, u32[]{:S(2)}, u32[]{:S(2)}) collective-permute-start(bf16[528,128]{1,0:T(8,128)(2,1)S(1)} %get-tuple-element.146), channel_id=1, source_target_pairs={{0,7},{3,4},{4,3},{7,0},{8,15},{11,12},{12,11},{15,8},{16,23},{19,... | collective-permute-start | bytes 405512 | tf_op jit(solution)/shard_map/ppermute | solution.py:213
  210.0 5.6 %collective-permute-start.34 = (bf16[528,128]{1,0:T(8,128)(2,1)S(1)}, bf16[528,128]{1,0:T(8,128)(2,1)S(1)}, u32[]{:S(2)}, u32[]{:S(2)}) collective-permute-start(bf16[528,128]{1,0:T(8,128)(2,1)S(1)} %get-tuple-element.147), channel_id=1, source_target_pairs={{0,15},{3,12},{4,11},{7,8},{8,7},{11,4},{12,3},{15,0},{16,31},{19,... | collective-permute-start | bytes 405512 | tf_op jit(solution)/shard_map/ppermute | solution.py:213
  215.7 1.6 multiply_reduce_fusion
  217.4 0.7 collective-permute-start.28
  218.1 1.5 collective-permute-start.30
  219.8 7.4 %collective-permute-done.28 = f32[520,128]{1,0:T(8,128)S(1)} collective-permute-done((f32[520,128]{1,0:T(8,128)S(1)}, f32[520,128]{1,0:T(8,128)S(1)}, u32[]{:S(2)}, u32[]{:S(2)}) %collective-permute-start.28) | collective-permute-done | bytes 266272 | tf_op jit(solution)/shard_map/ppermute | solution.py:194
  227.2 3.7 %collective-permute-done.30 = f32[520,128]{1,0:T(8,128)S(1)} collective-permute-done((f32[520,128]{1,0:T(8,128)S(1)}, f32[520,128]{1,0:T(8,128)S(1)}, u32[]{:S(2)}, u32[]{:S(2)}) %collective-permute-start.30) | collective-permute-done | bytes 266272 | tf_op jit(solution)/shard_map/ppermute | solution.py:194
  231.7 1.1 slice_add_fusion
  (88 shorter events, 4.9 us)
Async XLA Ops:
  0.6 51.9 %collective-permute-start = (bf16[512,2048]{1,0:T(8,128)(2,1)}, bf16[512,2048]{1,0:T(8,128)(2,1)}, u32[]{:S(2)}, u32[]{:S(2)}) collective-permute-start(bf16[512,2048]{1,0:T(8,128)(2,1)} %refs_0_.1), channel_id=1, source_target_pairs={{0,1},{1,0},{2,3},{3,2},{4,5},{5,4},{6,7},{7,6},{8,9},{9,8},{10,11... | collective-permute-start | bytes 6291464 | tf_op jit(solution)/shard_map/ppermute | solution.py:191
  3.7 48.8 %collective-permute-start.1 = (bf16[512,2048]{1,0:T(8,128)(2,1)}, bf16[512,2048]{1,0:T(8,128)(2,1)}, u32[]{:S(2)}, u32[]{:S(2)}) collective-permute-start(bf16[512,2048]{1,0:T(8,128)(2,1)} %refs_0_.1), channel_id=1, source_target_pairs={{1,2},{2,1},{5,6},{6,5},{9,10},{10,9},{13,14},{14,13},{17,18},{18,... | collective-permute-start | bytes 6291464 | tf_op jit(solution)/shard_map/ppermute | solution.py:191
  5.8 46.8 %collective-permute-start.5 = (bf16[512,2048]{1,0:T(8,128)(2,1)}, bf16[512,2048]{1,0:T(8,128)(2,1)S(1)}, u32[]{:S(2)}, u32[]{:S(2)}) collective-permute-start(bf16[512,2048]{1,0:T(8,128)(2,1)} %refs_0_.2), channel_id=1, source_target_pairs={{0,4},{4,0},{8,12},{12,8},{1,5},{5,1},{9,13},{13,9},{2,6},{6,2},{1... | collective-permute-start | bytes 6291464 | tf_op jit(solution)/shard_map/ppermute | solution.py:194
  5.8 48.9 %collective-permute-start.12 = (bf16[512,2048]{1,0:T(8,128)(2,1)}, bf16[512,2048]{1,0:T(8,128)(2,1)}, u32[]{:S(2)}, u32[]{:S(2)}) collective-permute-start(bf16[512,2048]{1,0:T(8,128)(2,1)} %refs_0_.2), channel_id=1, source_target_pairs={{0,8},{4,12},{8,0},{12,4},{1,9},{5,13},{9,1},{13,5},{2,10},{6,14},... | collective-permute-start | bytes 6291464 | tf_op jit(solution)/shard_map/ppermute | solution.py:194
  7.3 3.4 %copy-start = (bf16[2048,2048]{1,0:T(8,128)(2,1)S(1)}, bf16[2048,2048]{1,0:T(8,128)(2,1)}, u32[]{:S(2)}) copy-start(bf16[2048,2048]{1,0:T(8,128)(2,1)} %refs_1_.5) | copy-start | bytes 25165828
  10.7 1.6 copy-start.10
  12.3 8.0 %copy-start.20 = (s32[512,16]{0,1:T(8,128)S(1)}, s32[512,16]{0,1:T(8,128)}, u32[]{:S(2)}) copy-start(s32[512,16]{0,1:T(8,128)} %param.7) | copy-start | bytes 98308
  18.7 1.4 copy-start.8
  20.1 2.1 collective-permute-start.2
  22.2 1.9 collective-permute-start.3
  24.1 28.5 %collective-permute-start.4 = (s32[512,16]{0,1:T(8,128)S(1)}, s32[512,16]{0,1:T(8,128)S(1)}, u32[]{:S(2)}, u32[]{:S(2)}) collective-permute-start(s32[512,16]{0,1:T(8,128)S(1)} %copy-done.20), channel_id=1, source_target_pairs={{0,3},{3,0},{4,7},{7,4},{8,11},{11,8},{12,15},{15,12},{16,19},{19,... | collective-permute-start | bytes 98312 | tf_op jit(solution)/shard_map/ppermute | solution.py:191
  31.0 1.6 copy-start.9
  52.6 12.9 %copy-start.3 = (bf16[512,2048]{1,0:T(8,128)(2,1)}, bf16[512,2048]{1,0:T(8,128)(2,1)S(1)}, u32[]{:S(2)}) copy-start(bf16[512,2048]{1,0:T(8,128)(2,1)S(1)} %collective-permute-done.5.refs_5_.refs_3_.refs_1_) | copy-start | bytes 6291460
  52.6 51.7 %collective-permute-start.6 = (bf16[512,2048]{1,0:T(8,128)(2,1)}, bf16[512,2048]{1,0:T(8,128)(2,1)S(1)}, u32[]{:S(2)}, u32[]{:S(2)}) collective-permute-start(bf16[512,2048]{1,0:T(8,128)(2,1)} %collective-permute-done.refs_1_.refs_0_), channel_id=1, source_target_pairs={{1,2},{2,1},{5,6},{6,5},{9,10},{10,9},{13,14},{14,13},{17,18},{18,... | collective-permute-start | bytes 6291464 | tf_op jit(solution)/shard_map/ppermute | solution.py:191
  53.4 51.0 %collective-permute-start.7 = (bf16[512,2048]{1,0:T(8,128)(2,1)}, bf16[512,2048]{1,0:T(8,128)(2,1)S(1)}, u32[]{:S(2)}, u32[]{:S(2)}) collective-permute-start(bf16[512,2048]{1,0:T(8,128)(2,1)} %collective-permute-done.1.refs_0_), channel_id=1, source_target_pairs={{1,0},{2,3},{5,4},{6,7},{9,8},{10,11},{13,12},{14,15},{17,16},{18,... | collective-permute-start | bytes 6291464 | tf_op jit(solution)/shard_map/ppermute | solution.py:191
  54.7 49.7 %collective-permute-start.13 = (bf16[512,2048]{1,0:T(8,128)(2,1)}, bf16[512,2048]{1,0:T(8,128)(2,1)S(1)}, u32[]{:S(2)}, u32[]{:S(2)}) collective-permute-start(bf16[512,2048]{1,0:T(8,128)(2,1)} %collective-permute-done.12.refs_6_.refs_4_.refs_2_), channel_id=1, source_target_pairs={{0,4},{4,0},{8,12},{12,8},{1,5},{5,1},{9,13},{13,9},{2,6},{6,2},{1... | collective-permute-start | bytes 6291464 | tf_op jit(solution)/shard_map/ppermute | solution.py:194
  54.8 3.4 %copy-start.1 = (bf16[2048,2048]{1,0:T(8,128)(2,1)S(1)}, bf16[2048,2048]{1,0:T(8,128)(2,1)}, u32[]{:S(2)}) copy-start(bf16[2048,2048]{1,0:T(8,128)(2,1)} %refs_1_.5) | copy-start | bytes 25165828
  65.5 2.1 collective-permute-start.10
  66.1 3.0 %collective-permute-start.9 = (bf16[128,2048]{1,0:T(8,128)(2,1)S(1)}, bf16[128,2048]{1,0:T(8,128)(2,1)S(1)}, u32[]{:S(2)}, u32[]{:S(2)}) collective-permute-start(bf16[128,2048]{1,0:T(8,128)(2,1)S(1)} %get-tuple-element.77), channel_id=1, source_target_pairs={{0,4},{4,0},{8,12},{12,8},{1,5},{5,1},{9,13},{13,9},{2,6},{6,2},{1... | collective-permute-start | bytes 1572872 | tf_op jit(solution)/shard_map/ppermute | solution.py:194
  67.6 26.0 %collective-permute-start.8 = (f32[128,2048]{1,0:T(8,128)S(1)}, f32[128,2048]{1,0:T(8,128)S(1)}, u32[]{:S(2)}, u32[]{:S(2)}) collective-permute-start(f32[128,2048]{1,0:T(8,128)S(1)} %get-tuple-element.75), channel_id=1, source_target_pairs={{0,8},{4,12},{8,0},{12,4},{1,9},{5,13},{9,1},{13,5},{2,10},{6,14},... | collective-permute-start | bytes 3145736 | tf_op jit(solution)/shard_map/ppermute | solution.py:194
  69.1 36.9 %copy-start.2 = (bf16[512,2048]{1,0:T(8,128)(2,1)S(1)}, bf16[512,2048]{1,0:T(8,128)(2,1)}, u32[]{:S(2)}) copy-start(bf16[512,2048]{1,0:T(8,128)(2,1)} %refs_0_.2) | copy-start | bytes 6291460
  69.1 36.9 %copy-start.4 = (bf16[512,2048]{1,0:T(8,128)(2,1)S(1)}, bf16[512,2048]{1,0:T(8,128)(2,1)}, u32[]{:S(2)}) copy-start(bf16[512,2048]{1,0:T(8,128)(2,1)} %copy-done.3) | copy-start | bytes 6291460
  69.1 44.5 %slice-start = ((s8[8388608]{0:T(1024)(128)(4,1)}), s8[4194304]{0:T(1024)(128)(4,1)S(1)}, s32[]{:S(2)}) async-start(s8[8388608]{0:T(1024)(128)(4,1)} %bitcast.92), calls=%async_computation | async-start | bytes 8388608
  70.0 34.3 %collective-permute-start.11 = (bf16[128,2048]{1,0:T(8,128)(2,1)S(1)}, bf16[128,2048]{1,0:T(8,128)(2,1)S(1)}, u32[]{:S(2)}, u32[]{:S(2)}) collective-permute-start(bf16[128,2048]{1,0:T(8,128)(2,1)S(1)} %get-tuple-element.80), channel_id=1, source_target_pairs={{0,8},{4,12},{8,0},{12,4},{1,9},{5,13},{9,1},{13,5},{2,10},{6,14},... | collective-permute-start | bytes 1572872 | tf_op jit(solution)/shard_map/ppermute | solution.py:194
  104.4 56.6 %copy-start.6 = (bf16[512,2048]{1,0:T(8,128)(2,1)}, bf16[512,2048]{1,0:T(8,128)(2,1)S(1)}, u32[]{:S(2)}) copy-start(bf16[512,2048]{1,0:T(8,128)(2,1)S(1)} %collective-permute-done.13.refs_7_.refs_5_.refs_3_) | copy-start | bytes 6291460
  104.4 9.2 %slice-start.1 = ((s8[8388608]{0:T(1024)(128)(4,1)}), s8[4194304]{0:T(1024)(128)(4,1)S(1)}, s32[]{:S(2)}) async-start(s8[8388608]{0:T(1024)(128)(4,1)} %bitcast.92), calls=%async_computation.1 | async-start | bytes 8388608
  104.4 60.6 %collective-permute-start.14 = (bf16[512,2048]{1,0:T(8,128)(2,1)S(1)}, bf16[512,2048]{1,0:T(8,128)(2,1)S(1)}, u32[]{:S(2)}, u32[]{:S(2)}) collective-permute-start(bf16[512,2048]{1,0:T(8,128)(2,1)S(1)} %collective-permute-done.6.refs_0_), channel_id=1, source_target_pairs={{1,0},{2,3},{5,4},{6,7},{9,8},{10,11},{13,12},{14,15},{17,16},{18,... | collective-permute-start | bytes 6291464 | tf_op jit(solution)/shard_map/ppermute | solution.py:191
  112.6 1.0 copy-start.11
  119.4 14.8 %collective-permute-start.15 = (bf16[128,2048]{1,0:T(8,128)(2,1)S(1)}, bf16[128,2048]{1,0:T(8,128)(2,1)S(1)}, u32[]{:S(2)}, u32[]{:S(2)}) collective-permute-start(bf16[128,2048]{1,0:T(8,128)(2,1)S(1)} %get-tuple-element.98), channel_id=1, source_target_pairs={{0,4},{4,0},{8,12},{12,8},{1,5},{5,1},{9,13},{13,9},{2,6},{6,2},{1... | collective-permute-start | bytes 1572872 | tf_op jit(solution)/shard_map/ppermute | solution.py:194
  126.2 19.7 %collective-permute-start.21 = (bf16[256,2048]{1,0:T(8,128)(2,1)S(1)}, bf16[256,2048]{1,0:T(8,128)(2,1)S(1)}, u32[]{:S(2)}, u32[]{:S(2)}) collective-permute-start(bf16[256,2048]{1,0:T(8,128)(2,1)S(1)} %get-tuple-element.107), channel_id=1, source_target_pairs={{0,4},{4,0},{8,12},{12,8},{1,5},{5,1},{9,13},{13,9},{2,6},{6,2},{1... | collective-permute-start | bytes 3145736 | tf_op jit(solution)/shard_map/ppermute | solution.py:194
  126.7 8.1 %collective-permute-start.16 = (bf16[128,2048]{1,0:T(8,128)(2,1)S(1)}, bf16[128,2048]{1,0:T(8,128)(2,1)S(1)}, u32[]{:S(2)}, u32[]{:S(2)}) collective-permute-start(bf16[128,2048]{1,0:T(8,128)(2,1)S(1)} %get-tuple-element.99), channel_id=1, source_target_pairs={{0,4},{4,0},{8,12},{12,8},{1,5},{5,1},{9,13},{13,9},{2,6},{6,2},{1... | collective-permute-start | bytes 1572872 | tf_op jit(solution)/shard_map/ppermute | solution.py:194
  126.8 19.1 %collective-permute-start.17 = (bf16[4,512,128]{2,1,0:T(8,128)(2,1)S(1)}, bf16[4,512,128]{2,1,0:T(8,128)(2,1)S(1)}, u32[]{:S(2)}, u32[]{:S(2)}) collective-permute-start(bf16[4,512,128]{2,1,0:T(8,128)(2,1)S(1)} %get-tuple-element.94), channel_id=1, source_target_pairs={{0,1},{3,2},{4,5},{7,6},{8,9},{11,10},{12,13},{15,14},{16,17},{19,... | collective-permute-start | bytes 1572872 | tf_op jit(solution)/shard_map/ppermute | solution.py:191
  134.2 11.7 %collective-permute-start.18 = (bf16[4,512,128]{2,1,0:T(8,128)(2,1)S(1)}, bf16[4,512,128]{2,1,0:T(8,128)(2,1)S(1)}, u32[]{:S(2)}, u32[]{:S(2)}) collective-permute-start(bf16[4,512,128]{2,1,0:T(8,128)(2,1)S(1)} %get-tuple-element.94), channel_id=1, source_target_pairs={{1,2},{2,1},{5,6},{6,5},{9,10},{10,9},{13,14},{14,13},{17,18},{18,... | collective-permute-start | bytes 1572872 | tf_op jit(solution)/shard_map/ppermute | solution.py:191
  135.7 14.7 %collective-permute-start.19 = (bf16[128,2048]{1,0:T(8,128)(2,1)S(1)}, bf16[128,2048]{1,0:T(8,128)(2,1)S(1)}, u32[]{:S(2)}, u32[]{:S(2)}) collective-permute-start(bf16[128,2048]{1,0:T(8,128)(2,1)S(1)} %get-tuple-element.104), channel_id=1, source_target_pairs={{0,8},{4,12},{8,0},{12,4},{1,9},{5,13},{9,1},{13,5},{2,10},{6,14},... | collective-permute-start | bytes 1572872 | tf_op jit(solution)/shard_map/ppermute | solution.py:194
  145.9 2.4 %copy-start.16 = (bf16[4,512,128]{2,1,0:T(8,128)(2,1)}, bf16[4,512,128]{2,1,0:T(8,128)(2,1)S(1)}, u32[]{:S(2)}) copy-start(bf16[4,512,128]{2,1,0:T(8,128)(2,1)S(1)} %collective-permute-done.17) | copy-start | bytes 1572868
  145.9 9.3 %copy-start.18 = (bf16[4,512,128]{2,1,0:T(8,128)(2,1)}, bf16[4,512,128]{2,1,0:T(8,128)(2,1)S(1)}, u32[]{:S(2)}) copy-start(bf16[4,512,128]{2,1,0:T(8,128)(2,1)S(1)} %collective-permute-done.18) | copy-start | bytes 1572868
  146.7 14.2 %collective-permute-start.22 = (bf16[128,2048]{1,0:T(8,128)(2,1)S(1)}, bf16[128,2048]{1,0:T(8,128)(2,1)S(1)}, u32[]{:S(2)}, u32[]{:S(2)}) collective-permute-start(bf16[128,2048]{1,0:T(8,128)(2,1)S(1)} %get-tuple-element.109), channel_id=1, source_target_pairs={{0,8},{4,12},{8,0},{12,4},{1,9},{5,13},{9,1},{13,5},{2,10},{6,14},... | collective-permute-start | bytes 1572872 | tf_op jit(solution)/shard_map/ppermute | solution.py:194
  155.2 9.8 %collective-permute-start.20 = (bf16[4,512,128]{2,1,0:T(8,128)(2,1)}, bf16[4,512,128]{2,1,0:T(8,128)(2,1)S(1)}, u32[]{:S(2)}, u32[]{:S(2)}) collective-permute-start(bf16[4,512,128]{2,1,0:T(8,128)(2,1)} %scores.4), channel_id=1, source_target_pairs={{1,2},{2,1},{5,6},{6,5},{9,10},{10,9},{13,14},{14,13},{17,18},{18,... | collective-permute-start | bytes 1572872 | tf_op jit(solution)/shard_map/ppermute | solution.py:191
  170.6 2.0 collective-permute-start.23
  170.7 2.6 %collective-permute-start.24 = (bf16[128,2048]{1,0:T(8,128)(2,1)S(1)}, bf16[128,2048]{1,0:T(8,128)(2,1)S(1)}, u32[]{:S(2)}, u32[]{:S(2)}) collective-permute-start(bf16[128,2048]{1,0:T(8,128)(2,1)S(1)} %get-tuple-element.117), channel_id=1, source_target_pairs={{0,4},{4,0},{8,12},{12,8},{1,5},{5,1},{9,13},{13,9},{2,6},{6,2},{1... | collective-permute-start | bytes 1572872 | tf_op jit(solution)/shard_map/ppermute | solution.py:194
  174.9 2.4 %copy-start.13 = (f32[128,2048]{1,0:T(8,128)}, f32[128,2048]{1,0:T(8,128)S(1)}, u32[]{:S(2)}) copy-start(f32[128,2048]{1,0:T(8,128)S(1)} %get-tuple-element.118.kept) | copy-start | bytes 3145732
  174.9 14.3 %collective-permute-start.25 = (bf16[128,2048]{1,0:T(8,128)(2,1)}, bf16[128,2048]{1,0:T(8,128)(2,1)}, u32[]{:S(2)}, u32[]{:S(2)}) collective-permute-start(bf16[128,2048]{1,0:T(8,128)(2,1)} %get-tuple-element.119), channel_id=1, source_target_pairs={{0,8},{4,12},{8,0},{12,4},{1,9},{5,13},{9,1},{13,5},{2,10},{6,14},... | collective-permute-start | bytes 1572872 | tf_op jit(solution)/shard_map/ppermute | solution.py:194
  177.4 20.6 %collective-permute-start.27 = (bf16[4,512,128]{2,1,0:T(8,128)(2,1)}, bf16[4,512,128]{2,1,0:T(8,128)(2,1)}, u32[]{:S(2)}, u32[]{:S(2)}) collective-permute-start(bf16[4,512,128]{2,1,0:T(8,128)(2,1)} %add_convert_fusion), channel_id=1, source_target_pairs={{1,0},{2,3},{5,4},{6,7},{9,8},{10,11},{13,12},{14,15},{17,16},{18,... | collective-permute-start | bytes 1572872 | tf_op jit(solution)/shard_map/ppermute | solution.py:191
  178.7 21.0 %collective-permute-start.26 = (bf16[4,512,128]{2,1,0:T(8,128)(2,1)}, bf16[4,512,128]{2,1,0:T(8,128)(2,1)}, u32[]{:S(2)}, u32[]{:S(2)}) collective-permute-start(bf16[4,512,128]{2,1,0:T(8,128)(2,1)} %scores.4), channel_id=1, source_target_pairs={{0,2},{3,1},{4,6},{7,5},{8,10},{11,9},{12,14},{15,13},{16,18},{19,... | collective-permute-start | bytes 1572872 | tf_op jit(solution)/shard_map/ppermute | solution.py:191
  189.2 1.6 copy-start.5
  190.8 1.6 copy-start.7
  192.4 1.2 copy-start.14
  193.6 22.0 %copy-start.12 = (f32[4,512,128]{2,1,0:T(8,128)S(1)}, f32[4,512,128]{2,1,0:T(8,128)}, u32[]{:S(2)}) copy-start(f32[4,512,128]{2,1,0:T(8,128)} %copy-done.11) | copy-start | bytes 3145732
  193.6 22.0 %copy-start.15 = (f32[4,512,128]{2,1,0:T(8,128)S(1)}, f32[4,512,128]{2,1,0:T(8,128)}, u32[]{:S(2)}) copy-start(f32[4,512,128]{2,1,0:T(8,128)} %convert_add_fusion.1) | copy-start | bytes 3145732
  193.6 22.0 %copy-start.17 = (bf16[4,512,128]{2,1,0:T(8,128)(2,1)S(1)}, bf16[4,512,128]{2,1,0:T(8,128)(2,1)}, u32[]{:S(2)}) copy-start(bf16[4,512,128]{2,1,0:T(8,128)(2,1)} %copy-done.16) | copy-start | bytes 1572868
  193.6 22.0 %copy-start.19 = (bf16[4,512,128]{2,1,0:T(8,128)(2,1)S(1)}, bf16[4,512,128]{2,1,0:T(8,128)(2,1)}, u32[]{:S(2)}) copy-start(bf16[4,512,128]{2,1,0:T(8,128)(2,1)} %copy-done.18) | copy-start | bytes 1572868
  199.7 18.4 %collective-permute-start.31 = (bf16[528,128]{1,0:T(8,128)(2,1)S(1)}, bf16[528,128]{1,0:T(8,128)(2,1)S(1)}, u32[]{:S(2)}, u32[]{:S(2)}) collective-permute-start(bf16[528,128]{1,0:T(8,128)(2,1)S(1)} %get-tuple-element.149), channel_id=1, source_target_pairs={{0,3},{3,0},{4,7},{7,4},{8,11},{11,8},{12,15},{15,12},{16,19},{19,... | collective-permute-start | bytes 405512 | tf_op jit(solution)/shard_map/ppermute | solution.py:213
  203.4 14.7 %collective-permute-start.32 = (bf16[528,128]{1,0:T(8,128)(2,1)S(1)}, bf16[528,128]{1,0:T(8,128)(2,1)S(1)}, u32[]{:S(2)}, u32[]{:S(2)}) collective-permute-start(bf16[528,128]{1,0:T(8,128)(2,1)S(1)} %get-tuple-element.148), channel_id=1, source_target_pairs={{0,11},{3,8},{4,15},{7,12},{8,3},{11,0},{12,7},{15,4},{16,27},{19,... | collective-permute-start | bytes 405512 | tf_op jit(solution)/shard_map/ppermute | solution.py:213
  207.5 12.2 %collective-permute-start.33 = (bf16[528,128]{1,0:T(8,128)(2,1)S(1)}, bf16[528,128]{1,0:T(8,128)(2,1)S(1)}, u32[]{:S(2)}, u32[]{:S(2)}) collective-permute-start(bf16[528,128]{1,0:T(8,128)(2,1)S(1)} %get-tuple-element.146), channel_id=1, source_target_pairs={{0,7},{3,4},{4,3},{7,0},{8,15},{11,12},{12,11},{15,8},{16,23},{19,... | collective-permute-start | bytes 405512 | tf_op jit(solution)/shard_map/ppermute | solution.py:213
  210.0 9.6 %collective-permute-start.34 = (bf16[528,128]{1,0:T(8,128)(2,1)S(1)}, bf16[528,128]{1,0:T(8,128)(2,1)S(1)}, u32[]{:S(2)}, u32[]{:S(2)}) collective-permute-start(bf16[528,128]{1,0:T(8,128)(2,1)S(1)} %get-tuple-element.147), channel_id=1, source_target_pairs={{0,15},{3,12},{4,11},{7,8},{8,7},{11,4},{12,3},{15,0},{16,31},{19,... | collective-permute-start | bytes 405512 | tf_op jit(solution)/shard_map/ppermute | solution.py:213
  217.4 9.8 %collective-permute-start.28 = (f32[520,128]{1,0:T(8,128)S(1)}, f32[520,128]{1,0:T(8,128)S(1)}, u32[]{:S(2)}, u32[]{:S(2)}) collective-permute-start(f32[520,128]{1,0:T(8,128)S(1)} %get-tuple-element.182), channel_id=1, source_target_pairs={{0,8},{4,12},{8,0},{12,4},{1,9},{5,13},{9,1},{13,5},{2,10},{6,14},... | collective-permute-start | bytes 798728 | tf_op jit(solution)/shard_map/ppermute | solution.py:194
  218.1 9.1 %collective-permute-start.29 = (f32[520,128]{1,0:T(8,128)S(1)}, f32[520,128]{1,0:T(8,128)S(1)}, u32[]{:S(2)}, u32[]{:S(2)}) collective-permute-start(f32[520,128]{1,0:T(8,128)S(1)} %get-tuple-element.183), channel_id=1, source_target_pairs={{0,4},{4,0},{8,12},{12,8},{1,5},{5,1},{9,13},{13,9},{2,6},{6,2},{1... | collective-permute-start | bytes 798728 | tf_op jit(solution)/shard_map/ppermute | solution.py:194
  218.1 12.8 %collective-permute-start.30 = (f32[520,128]{1,0:T(8,128)S(1)}, f32[520,128]{1,0:T(8,128)S(1)}, u32[]{:S(2)}, u32[]{:S(2)}) collective-permute-start(f32[520,128]{1,0:T(8,128)S(1)} %get-tuple-element.184), channel_id=1, source_target_pairs={{0,12},{4,8},{8,4},{12,0},{1,13},{5,9},{9,5},{13,1},{2,14},{6,10},... | collective-permute-start | bytes 798728 | tf_op jit(solution)/shard_map/ppermute | solution.py:194

commit v9 on v8

--- a/solution.py
+++ b/solution.py
@@ -39,7 +39,7 @@
 
 
 SMALL = pl.CostEstimate(flops=1, bytes_accessed=1, transcendentals=0)
-PARAMS = pltpu.CompilerParams(vmem_limit_bytes=16 * 2**20)
+PARAMS = pltpu.CompilerParams(vmem_limit_bytes=12 * 2**20)
 
 
 VMEM = pl.BlockSpec(memory_space=pltpu.VMEM)
@@ -150,32 +150,38 @@
     )(*[value for unit in units for value in unit], *grads)
 
 
-def last_scores_body(kept, got, counts, *refs):
-    grads, out = refs[:4], refs[4]
+def last_scores_body(which, kept, got, counts, before, *refs):
+    grads, out, chosen_out = refs[: len(which)], refs[-2], refs[-1]
     rows = kept.shape[0]
     train_rows = grads[0].shape[0]
     precond = jnp.concatenate(split_sum(kept, got))
-    chosen = jnp.zeros((1, rows), F32)
-    for r in range(4):
-        both = dot_t(grads[r][...], precond)
+    chosen = before[:1]
+    for n, r in enumerate(which):
+        both = dot_t(grads[n][...], precond)
         value = both[:, :rows] + both[:, rows:]
-        out[r, :train_rows] = value.astype(out.dtype)
+        out[n, :train_rows] = value.astype(BF16)
         chosen = chosen + jnp.sum(value * counts[r], axis=0, keepdims=True)
-    for r in range(4):
-        out[r, train_rows:] = jnp.broadcast_to(chosen, (EXTRA, rows)).astype(out.dtype)
-
-
-def last_scores(kept, got, counts, grads):
+    chosen_out[...] = jnp.broadcast_to(chosen, chosen_out.shape)
+    for n in range(len(which)):
+        if out.shape[1] > train_rows:
+            out[n, train_rows:] = jnp.broadcast_to(chosen, (EXTRA, rows)).astype(BF16)
+
+
+def last_scores(kept, got, counts, before, grads, which, extra):
     rows = kept.shape[0]
+    train_rows = grads[0].shape[0]
     return pl.pallas_call(
-        last_scores_body,
-        in_specs=[VMEM] * 7,
-        out_specs=VMEM,
-        out_shape=jax.ShapeDtypeStruct((4, grads[0].shape[0] + EXTRA, rows), BF16),
+        functools.partial(last_scores_body, which),
+        in_specs=[VMEM] * (4 + len(which)),
+        out_specs=[VMEM, VMEM],
+        out_shape=[
+            jax.ShapeDtypeStruct((len(which), train_rows + extra, rows), BF16),
+            jax.ShapeDtypeStruct((8, rows), F32),
+        ],
         compiler_params=PARAMS,
         cost_estimate=SMALL,
         name="last_scores",
-    )(kept, got, counts, *grads)
+    )(kept, got, counts, before, *[grads[r] for r in which])
 
 
 def four_by_four(train_grads, test_grads, fisher, chosen_ids):
@@ -207,11 +213,6 @@
     def scores_of(*units, out_as=(BF16, BF16)):
         return partial_scores(units, grads, out_as[: len(units)])
 
-    def straight(value, r):
-        pairs = [(0, 3), (3, 0)]
-        pairs = [(k * 4 + a, (k ^ r) * 4 + b) for k in range(4) for a, b in pairs]
-        return lax.ppermute(value, ("train", "test"), pairs)
-
     def in_order(parts):
         parts = [parts[0], parts[2], parts[1], parts[3]]
         parts = [jnp.where(chip == 0, parts[q], parts[q ^ 1]) for q in range(4)]
@@ -236,25 +237,28 @@
 
     second_edge = along(middle_in, outward)
     far_in = along(pair_in, middle)
+    near, near_sent = core_sum(*product(flags, [middle_in, pair_in], fisher))
+    near_sent, own_sent = tied(near_sent, own_sent)
+    near_got = to_other(near_sent, 2)
     own_got = to_other(own_sent, 2)
-    near, near_sent = core_sum(*product(flags, [middle_in, pair_in], fisher))
-    near_got = to_other(near_sent, 2)
     far_counts = selected(far_ids)
     grads = grads + [to_other(grads[2], 1)]
-    far_in, second_edge, pair_in, own, own_got, near, near_got, far_counts, grads = tied(
-        far_in, second_edge, pair_in, own, own_got, near, near_got, far_counts, grads
+    (near,) = scores_of((near, near_got))
+    far_in, second_edge, pair_in, own, own_got, near, far_counts, grads = tied(
+        far_in, second_edge, pair_in, own, own_got, near, far_counts, grads
     )
 
     first_edge = along(far_in, outward)
-    near, total = scores_of((near, near_got), (own, own_got), out_as=(BF16, F32))
     near_in, near_across = along(near, inward), along(near, middle)
-    far_in, pair_in, near = tied(far_in, pair_in, near)
     second, second_sent = core_sum(*product(flags, [far_in, second_edge], fisher))
-    third, third_sent = core_sum(*product(flags, [pair_in], fisher, 1))
+    second_sent, pair_in = tied(second_sent, pair_in)
+    third, third_sent = core_sum(*product(flags, [pair_in], fisher))
     second, near_in, near_across = tied(second, near_in, near_across)
     (second,) = scores_of((second, to_other(second_sent, 2)))
     across = along(second, middle)
-    (third,) = scores_of((third, to_other(third_sent, 2)), out_as=(F32,))
+    third, total = scores_of(
+        (third, to_other(third_sent, 2)), (own, own_got), out_as=(F32, F32)
+    )
     first_edge, total, near_in, near_across, second, across, third, grads, far_counts = tied(
         first_edge, total, near_in, near_across, second, across, third, grads, far_counts
     )
@@ -262,17 +266,28 @@
     third = along((third + across.astype(F32)).astype(BF16), outward)
     second = along(second, [(0, 2), (3, 1)])
     last, last_sent = core_sum(*product(flags, [first_edge], fisher))
-    last = last_scores(last, to_other(last_sent, 2), far_counts, grads)
-    last, second, third = tied(last, second, third)
-    last = in_order([straight(last[r], r) for r in range(4)])
+    last_got = to_other(last_sent, 2)
+    ends = [(0, 3), (3, 0)]
+    none = jnp.zeros((8, quarter), F32)
+    away, chosen = last_scores(last, last_got, far_counts, none, grads, (2, 3), 0)
+    away = along(away, ends)
+    away = [to_other(away[0], 2), to_other(away[1], 3)]
+    here, _ = last_scores(last, last_got, far_counts, chosen, grads, (0, 1), EXTRA)
+    here, second, third = tied(here, second, third)
+    here = along(here, ends)
+    here = [here[0], to_other(here[1], 1)]
+    chosen = [part[own_rows:] for part in here]
+    chosen += [to_other(chosen[0], 2), to_other(chosen[0], 3)]
+    last = in_order([part[:own_rows] for part in here] + away)
+    last_chosen = in_order(chosen)[0]
 
     total = total + sum(value.astype(F32) for value in (near_in, near_across, second, third))
     chosen = jnp.sum(total * counts, axis=(0, 1))
     total = [jnp.concatenate([part, jnp.broadcast_to(chosen, (8, quarter))]) for part in total]
     total = in_order([total[0]] + [to_other(total[r], r) for r in range(1, 4)])
 
-    scores = total[:own_rows] + last[:own_rows].astype(F32)
-    return scores, total[own_rows] + last[own_rows].astype(F32)
+    scores = total[:own_rows] + last.astype(F32)
+    return scores, total[own_rows] + last_chosen.astype(F32)
 
 
 def solution(mesh):

time: 234 us -> 222 us (0.949)
  starting transfers between devices: 62.4 us -> 50.5 us
  waiting for transfers between devices: 87.1 us -> 96.7 us
  local copies, waits for them, and re-layouts: 16.8 us -> 11.4 us
  other arithmetic: 9.02 us -> 6.08 us
    ppermute x20 -> x26, waiting for transfers between devices: 57.5 us -> 89.2 us  [to_other(): return lax.ppermute(value, 'train', [(k, k ^ r) for k in range(4)])]
    ppermute x11 -> x13, waiting for transfers between devices: 29.6 us -> 7.54 us  [along(): return lax.ppermute(value, 'test', pairs)]
    ppermute x4 -> x0, starting transfers between devices: 15.9 us -> none  [straight(): return lax.ppermute(value, ('train', 'test'), pairs)]
    unnamed x46 -> x18, local copies, waits for them, and re-layouts: 16.7 us -> 11.3 us
    ppermute x20 -> x26, starting transfers between devices: 13 us -> 16.4 us  [to_other(): return lax.ppermute(value, 'train', [(k, k ^ r) for k in range(4)])]
    ppermute x11 -> x13, starting transfers between devices: 33.5 us -> 34.2 us  [along(): return lax.ppermute(value, 'test', pairs)]
    pallas_call x1 -> x2, Pallas kernels: 4.28 us -> 4.8 us  [last_scores(): pl.pallas_call(functools.partial(last_scores_body, which), in_specs=[VMEM...]
  transfers between devices with their start and end apart: 35 -> 39, of which waited for: 16 -> 19; matrix products, arithmetic and copies ran while one was open for 3% -> 2% of each run, Pallas kernels for 21% -> 22%
where the time goes in v9:
time: 222 us; the launch traced here: 221 us
  waiting for transfers between devices  96.7 us (44%)
  Pallas kernels  54.8 us (25%)
  starting transfers between devices  50.5 us (23%)
  local copies, waits for them, and re-layouts  11.4 us (5%)
  other arithmetic  6.08 us (3%)
    ppermute x26, waiting for transfers between devices, to_other(): return lax.ppermute(value, 'train', [(k, k ^ r) for k in range(4)])  89.2 us
    ppermute x13, starting transfers between devices, along(): return lax.ppermute(value, 'test', pairs)  34.2 us
    pallas_call x5, Pallas kernels, product(): pl.pallas_call(functools.partial(product_body, len(blocks)), in_specs=[pl...  31.8 us
    ppermute x26, starting transfers between devices, to_other(): return lax.ppermute(value, 'train', [(k, k ^ r) for k in range(4)])  16.4 us
    pallas_call x3, Pallas kernels, partial_scores(): pl.pallas_call(lambda *refs: scores_body(len(units), *refs), in_specs=[VM...  14.1 us
    unnamed x18, local copies, waits for them, and re-layouts  11.3 us
    ppermute x13, waiting for transfers between devices, along(): return lax.ppermute(value, 'test', pairs)  7.54 us
    pallas_call x2, Pallas kernels, last_scores(): pl.pallas_call(functools.partial(last_scores_body, which), in_specs=[VMEM...  4.8 us
  transfers between devices with their start and end apart: 39, of which 19 were waited for; matrix products, arithmetic and copies ran while one was open for 2% of the time, Pallas kernels for 22%

profile of v9, /device:TPU:0, one launch (start us, length us, event | category | flops | bytes accessed | tf_op | source)
XLA Modules:
  0.0 220.6 jit_solution(6927015269728976257)
XLA Ops:
  0.6 3.0 %collective-permute-start.12 = (bf16[512,2048]{1,0:T(8,128)(2,1)}, bf16[512,2048]{1,0:T(8,128)(2,1)S(1)}, u32[]{:S(2)}, u32[]{:S(2)}) collective-permute-start(bf16[512,2048]{1,0:T(8,128)(2,1)} %refs_0_.2), channel_id=1, source_target_pairs={{0,8},{4,12},{8,0},{12,4},{1,9},{5,13},{9,1},{13,5},{2,10},{6,14},... | collective-permute-start | bytes 6291464 | tf_op jit(solution)/shard_map/ppermute | solution.py:200
  3.6 1.6 collective-permute-start
  5.2 2.0 collective-permute-start.1
  7.3 3.4 %copy-done = bf16[2048,2048]{1,0:T(8,128)(2,1)S(1)} copy-done((bf16[2048,2048]{1,0:T(8,128)(2,1)S(1)}, bf16[2048,2048]{1,0:T(8,128)(2,1)}, u32[]{:S(2)}) %copy-start) | copy-done | bytes 8388632
  10.7 1.6 copy-done.5
  12.3 6.4 %product.5 = (f32[256,2048]{1,0:T(8,128)S(1)}, bf16[128,2048]{1,0:T(8,128)(2,1)}, bf16[128,2048]{1,0:T(8,128)(2,1)S(1)}) custom-call(s32[3]{0:T(128)S(1)} %pad_add_fusion.flags, bf16[512,2048]{1,0:T(8,128)(2,1)S(1)} %copy-done.5, bf16[2048,2048]{1,0:T(8,128)(2,1)S(1)} %copy-done), custom_call_target="tpu_custom_call" | custom-call | flops 1 | bytes 1 | tf_op jit(solution)/shard_map/product/pallas_call | solution.py:78
  18.7 1.4 copy-done.3
  20.6 1.7 collective-permute-done.2.refs_0_
  22.8 1.4 collective-permute-done.3.refs_1_
  24.2 4.4 %collective-permute-start.4 = (s32[512,16]{0,1:T(8,128)S(1)}, s32[512,16]{0,1:T(8,128)S(1)}, u32[]{:S(2)}, u32[]{:S(2)}) collective-permute-start(s32[512,16]{0,1:T(8,128)S(1)} %copy-done.6), channel_id=1, source_target_pairs={{0,3},{3,0},{4,7},{7,4},{8,11},{11,8},{12,15},{15,12},{16,19},{19,... | collective-permute-start | bytes 98312 | tf_op jit(solution)/shard_map/ppermute | solution.py:197
  28.6 1.7 convert_add_fusion.1
  30.3 1.6 copy-done.4
  31.9 0.9 fold.5
  32.7 16.8 %collective-permute-done.12.refs_4_.refs_6_.refs_0_ = bf16[512,2048]{1,0:T(8,128)(2,1)S(1)} collective-permute-done((bf16[512,2048]{1,0:T(8,128)(2,1)}, bf16[512,2048]{1,0:T(8,128)(2,1)S(1)}, u32[]{:S(2)}, u32[]{:S(2)}) %collective-permute-start.12) | collective-permute-done | bytes 2097184 | tf_op jit(solution)/shard_map/ppermute | solution.py:200
  49.5 4.3 %collective-permute-done.4 = s32[512,16]{0,1:T(8,128)S(1)} collective-permute-done((s32[512,16]{0,1:T(8,128)S(1)}, s32[512,16]{0,1:T(8,128)S(1)}, u32[]{:S(2)}, u32[]{:S(2)}) %collective-permute-start.4) | collective-permute-done | bytes 32800 | tf_op jit(solution)/shard_map/ppermute | solution.py:197
  53.8 0.8 collective-permute-start.6
  54.6 1.3 collective-permute-start.7
  55.9 3.4 %copy-done.1 = bf16[2048,2048]{1,0:T(8,128)(2,1)S(1)} copy-done((bf16[2048,2048]{1,0:T(8,128)(2,1)S(1)}, bf16[2048,2048]{1,0:T(8,128)(2,1)}, u32[]{:S(2)}) %copy-start.1) | copy-done | bytes 8388632
  59.3 7.5 %product.6 = (f32[256,2048]{1,0:T(8,128)S(1)}, bf16[128,2048]{1,0:T(8,128)(2,1)S(1)}, bf16[128,2048]{1,0:T(8,128)(2,1)S(1)}) custom-call(s32[3]{0:T(128)S(1)} %pad_add_fusion.flags, bf16[512,2048]{1,0:T(8,128)(2,1)} %collective-permute-done.1.refs_0_, bf16[512,2048]{1,0:T(8,128)(2,1)} %collective-permute-done.refs_1_.refs_0_, bf16[2048,2048]{1,0:T(8,128)(2,1)S(1)} %copy-done.1), custom_call_target="tpu_custom_call" | custom-call | flops 1 | bytes 1 | tf_op jit(solution)/shard_map/product/pallas_call | solution.py:78
  67.4 1.4 collective-permute-done.8.refs_0_
  68.8 0.7 collective-permute-done.9.refs_1_
  69.5 0.8 fold.6
  70.3 0.6 collective-permute-start.10
  70.9 1.5 collective-permute-start.11
  72.5 1.7 convert_add_fusion.counts
  74.1 32.7 %collective-permute-done.11.refs_1_ = bf16[128,2048]{1,0:T(8,128)(2,1)S(1)} collective-permute-done((bf16[128,2048]{1,0:T(8,128)(2,1)S(1)}, bf16[128,2048]{1,0:T(8,128)(2,1)S(1)}, u32[]{:S(2)}, u32[]{:S(2)}) %collective-permute-start.11) | collective-permute-done | bytes 524320 | tf_op jit(solution)/shard_map/ppermute | solution.py:200
  106.8 4.0 %scores.3 = bf16[4,512,128]{2,1,0:T(8,128)(2,1)S(1)} custom-call(f32[128,2048]{1,0:T(8,128)S(1)} %get-tuple-element.86.refs_0_, bf16[128,2048]{1,0:T(8,128)(2,1)S(1)} %collective-permute-done.11.refs_1_, bf16[512,2048]{1,0:T(8,128)(2,1)S(1)} %copy-done.2, bf16[512,2048]{1,0:T(8,128)(2,1)} %collective-permute-done.5.refs_3_.refs_5_.refs_1_, ...), custom_call_target="tpu_custom_call" | custom-call | flops 1 | bytes 1 | tf_op jit(solution)/shard_map/scores/pallas_call | solution.py:142
  110.8 1.3 collective-permute-start.14
  112.2 5.6 %product.7 = (f32[256,2048]{1,0:T(8,128)S(1)}, bf16[128,2048]{1,0:T(8,128)(2,1)S(1)}, bf16[128,2048]{1,0:T(8,128)(2,1)S(1)}) custom-call(s32[3]{0:T(128)S(1)} %pad_add_fusion.flags, bf16[512,2048]{1,0:T(8,128)(2,1)S(1)} %collective-permute-done.6.refs_0_, bf16[512,2048]{1,0:T(8,128)(2,1)S(1)} %collective-permute-done.7.refs_1_, bf16[2048,2048]{1,0:T(8,128)(2,1)S(1)} %bitcast.115), custom_call_target="tpu_custom_call" | custom-call | flops 1 | bytes 1 | tf_op jit(solution)/shard_map/product/pallas_call | solution.py:78
  118.3 7.6 %collective-permute-start.20 = (bf16[4,512,128]{2,1,0:T(8,128)(2,1)S(1)}, bf16[4,512,128]{2,1,0:T(8,128)(2,1)S(1)}, u32[]{:S(2)}, u32[]{:S(2)}) collective-permute-start(bf16[4,512,128]{2,1,0:T(8,128)(2,1)S(1)} %scores.3), channel_id=1, source_target_pairs={{0,1},{3,2},{4,5},{7,6},{8,9},{11,10},{12,13},{15,14},{16,17},{19,... | collective-permute-start | bytes 1572872 | tf_op jit(solution)/shard_map/ppermute | solution.py:197
  125.9 0.9 collective-permute-start.21
  126.8 0.8 fold.7
  127.7 6.7 %product.8 = (f32[256,2048]{1,0:T(8,128)S(1)}, bf16[128,2048]{1,0:T(8,128)(2,1)S(1)}, bf16[128,2048]{1,0:T(8,128)(2,1)S(1)}) custom-call(s32[3]{0:T(128)S(1)} %pad_add_fusion.flags, bf16[512,2048]{1,0:T(8,128)(2,1)} %collective-permute-done.refs_1_.refs_0_, bf16[2048,2048]{1,0:T(8,128)(2,1)S(1)} %bitcast.115), custom_call_target="tpu_custom_call" | custom-call | flops 1 | bytes 1 | tf_op jit(solution)/shard_map/product/pallas_call | solution.py:78
  134.9 2.4 %collective-permute-done.20 = bf16[4,512,128]{2,1,0:T(8,128)(2,1)S(1)} collective-permute-done((bf16[4,512,128]{2,1,0:T(8,128)(2,1)S(1)}, bf16[4,512,128]{2,1,0:T(8,128)(2,1)S(1)}, u32[]{:S(2)}, u32[]{:S(2)}) %collective-permute-start.20) | collective-permute-done | bytes 524320 | tf_op jit(solution)/shard_map/ppermute | solution.py:197
  137.9 0.8 fold.8
  138.7 1.6 collective-permute-start.19
  140.3 11.9 %collective-permute-done.22.refs_1_ = bf16[128,2048]{1,0:T(8,128)(2,1)S(1)} collective-permute-done((bf16[128,2048]{1,0:T(8,128)(2,1)S(1)}, bf16[128,2048]{1,0:T(8,128)(2,1)S(1)}, u32[]{:S(2)}, u32[]{:S(2)}) %collective-permute-start.22) | collective-permute-done | bytes 524320 | tf_op jit(solution)/shard_map/ppermute | solution.py:200
  152.2 4.0 %scores.5 = bf16[4,512,128]{2,1,0:T(8,128)(2,1)S(1)} custom-call(f32[128,2048]{1,0:T(8,128)S(1)} %get-tuple-element.114.refs_0_, bf16[128,2048]{1,0:T(8,128)(2,1)S(1)} %collective-permute-done.22.refs_1_, bf16[512,2048]{1,0:T(8,128)(2,1)S(1)} %copy-done.2, bf16[512,2048]{1,0:T(8,128)(2,1)} %collective-permute-done.5.refs_3_.refs_5_.refs_1_, ...), custom_call_target="tpu_custom_call" | custom-call | flops 1 | bytes 1 | tf_op jit(solution)/shard_map/scores/pallas_call | solution.py:142
  156.1 0.7 collective-permute-start.23
  156.8 4.8 %collective-permute-done.19.refs_1_ = bf16[128,2048]{1,0:T(8,128)(2,1)S(1)} collective-permute-done((bf16[128,2048]{1,0:T(8,128)(2,1)S(1)}, bf16[128,2048]{1,0:T(8,128)(2,1)S(1)}, u32[]{:S(2)}, u32[]{:S(2)}) %collective-permute-start.19) | collective-permute-done | bytes 524320 | tf_op jit(solution)/shard_map/ppermute | solution.py:200
  161.6 6.2 %scores.4 = (f32[4,512,128]{2,1,0:T(8,128)S(1)}, f32[4,512,128]{2,1,0:T(8,128)S(1)}) custom-call(f32[128,2048]{1,0:T(8,128)S(1)} %get-tuple-element.101.refs_0_, bf16[128,2048]{1,0:T(8,128)(2,1)S(1)} %collective-permute-done.19.refs_1_, f32[128,2048]{1,0:T(8,128)S(1)} %get-tuple-element.103.refs_2_, f32[128,2048]{1,0:T(8,128)S(1)} %collective-permute-done.10.refs_3_, ...), custom_call_target="tpu_custom_call" | custom-call | flops 1 | bytes 1 | tf_op jit(solution)/shard_map/scores/pallas_call | solution.py:142
  167.8 5.6 %product.9 = (f32[256,2048]{1,0:T(8,128)S(1)}, bf16[128,2048]{1,0:T(8,128)(2,1)S(1)}, bf16[128,2048]{1,0:T(8,128)(2,1)S(1)}) custom-call(s32[3]{0:T(128)S(1)} %pad_add_fusion.flags, bf16[512,2048]{1,0:T(8,128)(2,1)S(1)} %collective-permute-done.14.refs_0_, bf16[2048,2048]{1,0:T(8,128)(2,1)S(1)} %bitcast.115), custom_call_target="tpu_custom_call" | custom-call | flops 1 | bytes 1 | tf_op jit(solution)/shard_map/product/pallas_call | solution.py:78
  174.0 1.4 collective-permute-done.24.refs_0_
  175.4 0.7 collective-permute-done.25.refs_1_
  176.1 0.8 fold.9
  177.0 0.6 collective-permute-start.26
  177.7 1.3 collective-permute-start.28
  179.0 4.8 %collective-permute-start.27 = (bf16[4,512,128]{2,1,0:T(8,128)(2,1)S(1)}, bf16[4,512,128]{2,1,0:T(8,128)(2,1)S(1)}, u32[]{:S(2)}, u32[]{:S(2)}) collective-permute-start(bf16[4,512,128]{2,1,0:T(8,128)(2,1)S(1)} %scores.5), channel_id=1, source_target_pairs={{0,2},{3,1},{4,6},{7,5},{8,10},{11,9},{12,14},{15,13},{16,18},{19,... | collective-permute-start | bytes 1572872 | tf_op jit(solution)/shard_map/ppermute | solution.py:197
  183.7 7.3 %collective-permute-done.26.got = bf16[128,2048]{1,0:T(8,128)(2,1)S(1)} collective-permute-done((bf16[128,2048]{1,0:T(8,128)(2,1)S(1)}, bf16[128,2048]{1,0:T(8,128)(2,1)S(1)}, u32[]{:S(2)}, u32[]{:S(2)}) %collective-permute-start.26) | collective-permute-done | bytes 524320 | tf_op jit(solution)/shard_map/ppermute | solution.py:200
  191.0 1.3 last_scores.2
  192.3 3.5 %last_scores.3 = (bf16[2,528,128]{2,1,0:T(8,128)(2,1)S(1)}, f32[8,128]{1,0:T(8,128)}) custom-call(f32[128,2048]{1,0:T(8,128)S(1)} %get-tuple-element.125.kept, bf16[128,2048]{1,0:T(8,128)(2,1)S(1)} %collective-permute-done.26.got, f32[4,512,128]{2,1,0:T(8,128)S(1)} %convert_add_fusion.counts, f32[8,128]{1,0:T(8,128)S(1)} %get-tuple-element.130.before, ...), custom_call_target="tpu_custom_call" | custom-call | flops 1 | bytes 1 | tf_op jit(solution)/shard_map/last_scores/pallas_call | solution.py:173
  195.8 3.6 %collective-permute-start.33 = (bf16[2,512,128]{2,1,0:T(8,128)(2,1)S(1)}, bf16[2,512,128]{2,1,0:T(8,128)(2,1)S(1)}, u32[]{:S(2)}, u32[]{:S(2)}) collective-permute-start(bf16[2,512,128]{2,1,0:T(8,128)(2,1)S(1)} %get-tuple-element.141), channel_id=1, source_target_pairs={{0,3},{3,0},{4,7},{7,4},{8,11},{11,8},{12,15},{15,12},{16,19},{19,... | collective-permute-start | bytes 786440 | tf_op jit(solution)/shard_map/ppermute | solution.py:197
  200.0 1.6 collective-permute-start.29
  201.5 0.7 collective-permute-start.31
  202.2 4.0 %collective-permute-start.32 = (bf16[2,528,128]{2,1,0:T(8,128)(2,1)S(1)}, bf16[2,528,128]{2,1,0:T(8,128)(2,1)S(1)}, u32[]{:S(2)}, u32[]{:S(2)}) collective-permute-start(bf16[2,528,128]{2,1,0:T(8,128)(2,1)S(1)} %get-tuple-element.140), channel_id=1, source_target_pairs={{0,3},{3,0},{4,7},{7,4},{8,11},{11,8},{12,15},{15,12},{16,19},{19,... | collective-permute-start | bytes 811016 | tf_op jit(solution)/shard_map/ppermute | solution.py:197
  206.2 0.8 collective-permute-done.33
  207.0 0.6 collective-permute-start.34
  207.6 1.7 collective-permute-done.29
  209.4 4.7 %collective-permute-done.31 = f32[520,128]{1,0:T(8,128)S(1)} collective-permute-done((f32[520,128]{1,0:T(8,128)S(1)}, f32[520,128]{1,0:T(8,128)S(1)}, u32[]{:S(2)}, u32[]{:S(2)}) %collective-permute-start.31) | collective-permute-done | bytes 266272 | tf_op jit(solution)/shard_map/ppermute | solution.py:200
  214.3 1.5 collective-permute-start.37
  215.7 1.0 collective-permute-start.38
  216.9 1.6 collective-permute-done.37
  218.8 0.6 fusion.3
  219.4 1.1 slice_add_fusion
  (72 shorter events, 5.4 us)
Async XLA Ops:
  0.6 48.8 %collective-permute-start.12 = (bf16[512,2048]{1,0:T(8,128)(2,1)}, bf16[512,2048]{1,0:T(8,128)(2,1)S(1)}, u32[]{:S(2)}, u32[]{:S(2)}) collective-permute-start(bf16[512,2048]{1,0:T(8,128)(2,1)} %refs_0_.2), channel_id=1, source_target_pairs={{0,8},{4,12},{8,0},{12,4},{1,9},{5,13},{9,1},{13,5},{2,10},{6,14},... | collective-permute-start | bytes 6291464 | tf_op jit(solution)/shard_map/ppermute | solution.py:200
  3.6 50.1 %collective-permute-start = (bf16[512,2048]{1,0:T(8,128)(2,1)}, bf16[512,2048]{1,0:T(8,128)(2,1)}, u32[]{:S(2)}, u32[]{:S(2)}) collective-permute-start(bf16[512,2048]{1,0:T(8,128)(2,1)} %refs_0_.1), channel_id=1, source_target_pairs={{0,1},{1,0},{2,3},{3,2},{4,5},{5,4},{6,7},{7,6},{8,9},{9,8},{10,11... | collective-permute-start | bytes 6291464 | tf_op jit(solution)/shard_map/ppermute | solution.py:197
  5.2 48.6 %collective-permute-start.1 = (bf16[512,2048]{1,0:T(8,128)(2,1)}, bf16[512,2048]{1,0:T(8,128)(2,1)}, u32[]{:S(2)}, u32[]{:S(2)}) collective-permute-start(bf16[512,2048]{1,0:T(8,128)(2,1)} %refs_0_.1), channel_id=1, source_target_pairs={{1,2},{2,1},{5,6},{6,5},{9,10},{10,9},{13,14},{14,13},{17,18},{18,... | collective-permute-start | bytes 6291464 | tf_op jit(solution)/shard_map/ppermute | solution.py:197
  7.2 46.5 %collective-permute-start.5 = (bf16[512,2048]{1,0:T(8,128)(2,1)}, bf16[512,2048]{1,0:T(8,128)(2,1)}, u32[]{:S(2)}, u32[]{:S(2)}) collective-permute-start(bf16[512,2048]{1,0:T(8,128)(2,1)} %refs_0_.2), channel_id=1, source_target_pairs={{0,4},{4,0},{8,12},{12,8},{1,5},{5,1},{9,13},{13,9},{2,6},{6,2},{1... | collective-permute-start | bytes 6291464 | tf_op jit(solution)/shard_map/ppermute | solution.py:200
  7.3 3.4 %copy-start = (bf16[2048,2048]{1,0:T(8,128)(2,1)S(1)}, bf16[2048,2048]{1,0:T(8,128)(2,1)}, u32[]{:S(2)}) copy-start(bf16[2048,2048]{1,0:T(8,128)(2,1)} %refs_1_.5) | copy-start | bytes 25165828
  10.7 1.6 copy-start.5
  12.3 8.3 %copy-start.6 = (s32[512,16]{0,1:T(8,128)S(1)}, s32[512,16]{0,1:T(8,128)}, u32[]{:S(2)}) copy-start(s32[512,16]{0,1:T(8,128)} %param.7) | copy-start | bytes 98308
  18.7 1.4 copy-start.3
  20.0 2.3 %collective-permute-start.2 = (bf16[128,2048]{1,0:T(8,128)(2,1)}, bf16[128,2048]{1,0:T(8,128)(2,1)S(1)}, u32[]{:S(2)}, u32[]{:S(2)}) collective-permute-start(bf16[128,2048]{1,0:T(8,128)(2,1)} %get-tuple-element.73), channel_id=1, source_target_pairs={{0,4},{4,0},{8,12},{12,8},{1,5},{5,1},{9,13},{13,9},{2,6},{6,2},{1... | collective-permute-start | bytes 1572872 | tf_op jit(solution)/shard_map/ppermute | solution.py:200
  22.3 1.9 collective-permute-start.3
  24.2 29.6 %collective-permute-start.4 = (s32[512,16]{0,1:T(8,128)S(1)}, s32[512,16]{0,1:T(8,128)S(1)}, u32[]{:S(2)}, u32[]{:S(2)}) collective-permute-start(s32[512,16]{0,1:T(8,128)S(1)} %copy-done.6), channel_id=1, source_target_pairs={{0,3},{3,0},{4,7},{7,4},{8,11},{11,8},{12,15},{15,12},{16,19},{19,... | collective-permute-start | bytes 98312 | tf_op jit(solution)/shard_map/ppermute | solution.py:197
  30.3 1.6 copy-start.4
  49.5 57.4 %collective-permute-start.13 = (bf16[512,2048]{1,0:T(8,128)(2,1)S(1)}, bf16[512,2048]{1,0:T(8,128)(2,1)S(1)}, u32[]{:S(2)}, u32[]{:S(2)}) collective-permute-start(bf16[512,2048]{1,0:T(8,128)(2,1)S(1)} %collective-permute-done.12.refs_4_.refs_6_.refs_0_), channel_id=1, source_target_pairs={{0,4},{4,0},{8,12},{12,8},{1,5},{5,1},{9,13},{13,9},{2,6},{6,2},{1... | collective-permute-start | bytes 6291464 | tf_op jit(solution)/shard_map/ppermute | solution.py:200
  53.8 57.0 %collective-permute-start.6 = (bf16[512,2048]{1,0:T(8,128)(2,1)}, bf16[512,2048]{1,0:T(8,128)(2,1)S(1)}, u32[]{:S(2)}, u32[]{:S(2)}) collective-permute-start(bf16[512,2048]{1,0:T(8,128)(2,1)} %collective-permute-done.refs_1_.refs_0_), channel_id=1, source_target_pairs={{1,2},{2,1},{5,6},{6,5},{9,10},{10,9},{13,14},{14,13},{17,18},{18,... | collective-permute-start | bytes 6291464 | tf_op jit(solution)/shard_map/ppermute | solution.py:197
  54.6 56.2 %collective-permute-start.7 = (bf16[512,2048]{1,0:T(8,128)(2,1)}, bf16[512,2048]{1,0:T(8,128)(2,1)S(1)}, u32[]{:S(2)}, u32[]{:S(2)}) collective-permute-start(bf16[512,2048]{1,0:T(8,128)(2,1)} %collective-permute-done.1.refs_0_), channel_id=1, source_target_pairs={{1,0},{2,3},{5,4},{6,7},{9,8},{10,11},{13,12},{14,15},{17,16},{18,... | collective-permute-start | bytes 6291464 | tf_op jit(solution)/shard_map/ppermute | solution.py:197
  55.9 3.4 %copy-start.1 = (bf16[2048,2048]{1,0:T(8,128)(2,1)S(1)}, bf16[2048,2048]{1,0:T(8,128)(2,1)}, u32[]{:S(2)}) copy-start(bf16[2048,2048]{1,0:T(8,128)(2,1)} %refs_1_.5) | copy-start | bytes 25165828
  59.3 52.9 %slice-start = ((s8[8388608]{0:T(1024)(128)(4,1)}), s8[4194304]{0:T(1024)(128)(4,1)S(1)}, s32[]{:S(2)}) async-start(s8[8388608]{0:T(1024)(128)(4,1)} %bitcast.114), calls=%async_computation | async-start | bytes 8388608
  66.8 2.0 collective-permute-start.8
  66.9 2.6 %collective-permute-start.9 = (bf16[128,2048]{1,0:T(8,128)(2,1)S(1)}, bf16[128,2048]{1,0:T(8,128)(2,1)S(1)}, u32[]{:S(2)}, u32[]{:S(2)}) collective-permute-start(bf16[128,2048]{1,0:T(8,128)(2,1)S(1)} %get-tuple-element.82), channel_id=1, source_target_pairs={{0,4},{4,0},{8,12},{12,8},{1,5},{5,1},{9,13},{13,9},{2,6},{6,2},{1... | collective-permute-start | bytes 1572872 | tf_op jit(solution)/shard_map/ppermute | solution.py:200
  69.5 37.3 %copy-start.2 = (bf16[512,2048]{1,0:T(8,128)(2,1)S(1)}, bf16[512,2048]{1,0:T(8,128)(2,1)}, u32[]{:S(2)}) copy-start(bf16[512,2048]{1,0:T(8,128)(2,1)} %refs_0_.2) | copy-start | bytes 6291460
  69.5 42.6 %slice-start.1 = ((s8[8388608]{0:T(1024)(128)(4,1)}), s8[4194304]{0:T(1024)(128)(4,1)S(1)}, s32[]{:S(2)}) async-start(s8[8388608]{0:T(1024)(128)(4,1)} %bitcast.114), calls=%async_computation.1 | async-start | bytes 8388608
  70.3 40.5 %collective-permute-start.10 = (f32[128,2048]{1,0:T(8,128)S(1)}, f32[128,2048]{1,0:T(8,128)S(1)}, u32[]{:S(2)}, u32[]{:S(2)}) collective-permute-start(f32[128,2048]{1,0:T(8,128)S(1)} %get-tuple-element.85), channel_id=1, source_target_pairs={{0,8},{4,12},{8,0},{12,4},{1,9},{5,13},{9,1},{13,5},{2,10},{6,14},... | collective-permute-start | bytes 3145736 | tf_op jit(solution)/shard_map/ppermute | solution.py:200
  70.9 35.9 %collective-permute-start.11 = (bf16[128,2048]{1,0:T(8,128)(2,1)S(1)}, bf16[128,2048]{1,0:T(8,128)(2,1)S(1)}, u32[]{:S(2)}, u32[]{:S(2)}) collective-permute-start(bf16[128,2048]{1,0:T(8,128)(2,1)S(1)} %get-tuple-element.87), channel_id=1, source_target_pairs={{0,8},{4,12},{8,0},{12,4},{1,9},{5,13},{9,1},{13,5},{2,10},{6,14},... | collective-permute-start | bytes 1572872 | tf_op jit(solution)/shard_map/ppermute | solution.py:200
  110.8 57.0 %collective-permute-start.14 = (bf16[512,2048]{1,0:T(8,128)(2,1)S(1)}, bf16[512,2048]{1,0:T(8,128)(2,1)S(1)}, u32[]{:S(2)}, u32[]{:S(2)}) collective-permute-start(bf16[512,2048]{1,0:T(8,128)(2,1)S(1)} %collective-permute-done.6.refs_0_), channel_id=1, source_target_pairs={{1,0},{2,3},{5,4},{6,7},{9,8},{10,11},{13,12},{14,15},{17,16},{18,... | collective-permute-start | bytes 6291464 | tf_op jit(solution)/shard_map/ppermute | solution.py:197
  117.8 9.0 %collective-permute-start.15 = (bf16[128,2048]{1,0:T(8,128)(2,1)S(1)}, bf16[128,2048]{1,0:T(8,128)(2,1)S(1)}, u32[]{:S(2)}, u32[]{:S(2)}) collective-permute-start(bf16[128,2048]{1,0:T(8,128)(2,1)S(1)} %get-tuple-element.93), channel_id=1, source_target_pairs={{0,4},{4,0},{8,12},{12,8},{1,5},{5,1},{9,13},{13,9},{2,6},{6,2},{1... | collective-permute-start | bytes 1572872 | tf_op jit(solution)/shard_map/ppermute | solution.py:200
  117.8 9.0 %collective-permute-start.16 = (bf16[128,2048]{1,0:T(8,128)(2,1)S(1)}, bf16[128,2048]{1,0:T(8,128)(2,1)S(1)}, u32[]{:S(2)}, u32[]{:S(2)}) collective-permute-start(bf16[128,2048]{1,0:T(8,128)(2,1)S(1)} %get-tuple-element.94), channel_id=1, source_target_pairs={{0,4},{4,0},{8,12},{12,8},{1,5},{5,1},{9,13},{13,9},{2,6},{6,2},{1... | collective-permute-start | bytes 1572872 | tf_op jit(solution)/shard_map/ppermute | solution.py:200
  118.3 19.0 %collective-permute-start.20 = (bf16[4,512,128]{2,1,0:T(8,128)(2,1)S(1)}, bf16[4,512,128]{2,1,0:T(8,128)(2,1)S(1)}, u32[]{:S(2)}, u32[]{:S(2)}) collective-permute-start(bf16[4,512,128]{2,1,0:T(8,128)(2,1)S(1)} %scores.3), channel_id=1, source_target_pairs={{0,1},{3,2},{4,5},{7,6},{8,9},{11,10},{12,13},{15,14},{16,17},{19,... | collective-permute-start | bytes 1572872 | tf_op jit(solution)/shard_map/ppermute | solution.py:197
  125.9 11.9 %collective-permute-start.21 = (bf16[4,512,128]{2,1,0:T(8,128)(2,1)S(1)}, bf16[4,512,128]{2,1,0:T(8,128)(2,1)S(1)}, u32[]{:S(2)}, u32[]{:S(2)}) collective-permute-start(bf16[4,512,128]{2,1,0:T(8,128)(2,1)S(1)} %scores.3), channel_id=1, source_target_pairs={{1,2},{2,1},{5,6},{6,5},{9,10},{10,9},{13,14},{14,13},{17,18},{18,... | collective-permute-start | bytes 1572872 | tf_op jit(solution)/shard_map/ppermute | solution.py:197
  134.4 3.5 %collective-permute-start.17 = (bf16[128,2048]{1,0:T(8,128)(2,1)S(1)}, bf16[128,2048]{1,0:T(8,128)(2,1)S(1)}, u32[]{:S(2)}, u32[]{:S(2)}) collective-permute-start(bf16[128,2048]{1,0:T(8,128)(2,1)S(1)} %get-tuple-element.99), channel_id=1, source_target_pairs={{0,4},{4,0},{8,12},{12,8},{1,5},{5,1},{9,13},{13,9},{2,6},{6,2},{1... | collective-permute-start | bytes 1572872 | tf_op jit(solution)/shard_map/ppermute | solution.py:200
  134.4 3.4 %collective-permute-start.18 = (bf16[128,2048]{1,0:T(8,128)(2,1)S(1)}, bf16[128,2048]{1,0:T(8,128)(2,1)S(1)}, u32[]{:S(2)}, u32[]{:S(2)}) collective-permute-start(bf16[128,2048]{1,0:T(8,128)(2,1)S(1)} %get-tuple-element.100), channel_id=1, source_target_pairs={{0,4},{4,0},{8,12},{12,8},{1,5},{5,1},{9,13},{13,9},{2,6},{6,2},{1... | collective-permute-start | bytes 1572872 | tf_op jit(solution)/shard_map/ppermute | solution.py:200
  137.3 14.9 %collective-permute-start.22 = (bf16[128,2048]{1,0:T(8,128)(2,1)S(1)}, bf16[128,2048]{1,0:T(8,128)(2,1)S(1)}, u32[]{:S(2)}, u32[]{:S(2)}) collective-permute-start(bf16[128,2048]{1,0:T(8,128)(2,1)S(1)} %get-tuple-element.115), channel_id=1, source_target_pairs={{0,8},{4,12},{8,0},{12,4},{1,9},{5,13},{9,1},{13,5},{2,10},{6,14},... | collective-permute-start | bytes 1572872 | tf_op jit(solution)/shard_map/ppermute | solution.py:200
  138.7 22.9 %collective-permute-start.19 = (bf16[128,2048]{1,0:T(8,128)(2,1)S(1)}, bf16[128,2048]{1,0:T(8,128)(2,1)S(1)}, u32[]{:S(2)}, u32[]{:S(2)}) collective-permute-start(bf16[128,2048]{1,0:T(8,128)(2,1)S(1)} %get-tuple-element.102), channel_id=1, source_target_pairs={{0,8},{4,12},{8,0},{12,4},{1,9},{5,13},{9,1},{13,5},{2,10},{6,14},... | collective-permute-start | bytes 1572872 | tf_op jit(solution)/shard_map/ppermute | solution.py:200
  156.1 11.7 %collective-permute-start.23 = (bf16[4,512,128]{2,1,0:T(8,128)(2,1)S(1)}, bf16[4,512,128]{2,1,0:T(8,128)(2,1)S(1)}, u32[]{:S(2)}, u32[]{:S(2)}) collective-permute-start(bf16[4,512,128]{2,1,0:T(8,128)(2,1)S(1)} %scores.5), channel_id=1, source_target_pairs={{1,2},{2,1},{5,6},{6,5},{9,10},{10,9},{13,14},{14,13},{17,18},{18,... | collective-permute-start | bytes 1572872 | tf_op jit(solution)/shard_map/ppermute | solution.py:197
  173.4 2.0 collective-permute-start.24
  173.5 2.6 %collective-permute-start.25 = (bf16[128,2048]{1,0:T(8,128)(2,1)S(1)}, bf16[128,2048]{1,0:T(8,128)(2,1)S(1)}, u32[]{:S(2)}, u32[]{:S(2)}) collective-permute-start(bf16[128,2048]{1,0:T(8,128)(2,1)S(1)} %get-tuple-element.124), channel_id=1, source_target_pairs={{0,4},{4,0},{8,12},{12,8},{1,5},{5,1},{9,13},{13,9},{2,6},{6,2},{1... | collective-permute-start | bytes 1572872 | tf_op jit(solution)/shard_map/ppermute | solution.py:200
  177.0 14.0 %collective-permute-start.26 = (bf16[128,2048]{1,0:T(8,128)(2,1)S(1)}, bf16[128,2048]{1,0:T(8,128)(2,1)S(1)}, u32[]{:S(2)}, u32[]{:S(2)}) collective-permute-start(bf16[128,2048]{1,0:T(8,128)(2,1)S(1)} %get-tuple-element.126), channel_id=1, source_target_pairs={{0,8},{4,12},{8,0},{12,4},{1,9},{5,13},{9,1},{13,5},{2,10},{6,14},... | collective-permute-start | bytes 1572872 | tf_op jit(solution)/shard_map/ppermute | solution.py:200
  177.7 18.1 %collective-permute-start.28 = (bf16[4,512,128]{2,1,0:T(8,128)(2,1)S(1)}, bf16[4,512,128]{2,1,0:T(8,128)(2,1)S(1)}, u32[]{:S(2)}, u32[]{:S(2)}) collective-permute-start(bf16[4,512,128]{2,1,0:T(8,128)(2,1)S(1)} %add_convert_fusion), channel_id=1, source_target_pairs={{1,0},{2,3},{5,4},{6,7},{9,8},{10,11},{13,12},{14,15},{17,16},{18,... | collective-permute-start | bytes 1572872 | tf_op jit(solution)/shard_map/ppermute | solution.py:197
  179.0 16.8 %collective-permute-start.27 = (bf16[4,512,128]{2,1,0:T(8,128)(2,1)S(1)}, bf16[4,512,128]{2,1,0:T(8,128)(2,1)S(1)}, u32[]{:S(2)}, u32[]{:S(2)}) collective-permute-start(bf16[4,512,128]{2,1,0:T(8,128)(2,1)S(1)} %scores.5), channel_id=1, source_target_pairs={{0,2},{3,1},{4,6},{7,5},{8,10},{11,9},{12,14},{15,13},{16,18},{19,... | collective-permute-start | bytes 1572872 | tf_op jit(solution)/shard_map/ppermute | solution.py:197
  195.8 11.2 %collective-permute-start.33 = (bf16[2,512,128]{2,1,0:T(8,128)(2,1)S(1)}, bf16[2,512,128]{2,1,0:T(8,128)(2,1)S(1)}, u32[]{:S(2)}, u32[]{:S(2)}) collective-permute-start(bf16[2,512,128]{2,1,0:T(8,128)(2,1)S(1)} %get-tuple-element.141), channel_id=1, source_target_pairs={{0,3},{3,0},{4,7},{7,4},{8,11},{11,8},{12,15},{15,12},{16,19},{19,... | collective-permute-start | bytes 786440 | tf_op jit(solution)/shard_map/ppermute | solution.py:197
  200.0 9.4 %collective-permute-start.29 = (f32[520,128]{1,0:T(8,128)S(1)}, f32[520,128]{1,0:T(8,128)S(1)}, u32[]{:S(2)}, u32[]{:S(2)}) collective-permute-start(f32[520,128]{1,0:T(8,128)S(1)} %get-tuple-element.194), channel_id=1, source_target_pairs={{0,8},{4,12},{8,0},{12,4},{1,9},{5,13},{9,1},{13,5},{2,10},{6,14},... | collective-permute-start | bytes 798728 | tf_op jit(solution)/shard_map/ppermute | solution.py:200
  201.5 7.9 %collective-permute-start.30 = (f32[520,128]{1,0:T(8,128)S(1)}, f32[520,128]{1,0:T(8,128)S(1)}, u32[]{:S(2)}, u32[]{:S(2)}) collective-permute-start(f32[520,128]{1,0:T(8,128)S(1)} %get-tuple-element.195), channel_id=1, source_target_pairs={{0,4},{4,0},{8,12},{12,8},{1,5},{5,1},{9,13},{13,9},{2,6},{6,2},{1... | collective-permute-start | bytes 798728 | tf_op jit(solution)/shard_map/ppermute | solution.py:200
  201.5 12.6 %collective-permute-start.31 = (f32[520,128]{1,0:T(8,128)S(1)}, f32[520,128]{1,0:T(8,128)S(1)}, u32[]{:S(2)}, u32[]{:S(2)}) collective-permute-start(f32[520,128]{1,0:T(8,128)S(1)} %get-tuple-element.196), channel_id=1, source_target_pairs={{0,12},{4,8},{8,4},{12,0},{1,13},{5,9},{9,5},{13,1},{2,14},{6,10},... | collective-permute-start | bytes 798728 | tf_op jit(solution)/shard_map/ppermute | solution.py:200
  202.2 12.1 %collective-permute-start.32 = (bf16[2,528,128]{2,1,0:T(8,128)(2,1)S(1)}, bf16[2,528,128]{2,1,0:T(8,128)(2,1)S(1)}, u32[]{:S(2)}, u32[]{:S(2)}) collective-permute-start(bf16[2,528,128]{2,1,0:T(8,128)(2,1)S(1)} %get-tuple-element.140), channel_id=1, source_target_pairs={{0,3},{3,0},{4,7},{7,4},{8,11},{11,8},{12,15},{15,12},{16,19},{19,... | collective-permute-start | bytes 811016 | tf_op jit(solution)/shard_map/ppermute | solution.py:197
  207.0 12.4 %collective-permute-start.34 = (bf16[512,128]{1,0:T(8,128)(2,1)S(1)}, bf16[512,128]{1,0:T(8,128)(2,1)S(1)}, u32[]{:S(2)}, u32[]{:S(2)}) collective-permute-start(bf16[512,128]{1,0:T(8,128)(2,1)S(1)} %get-tuple-element.161), channel_id=1, source_target_pairs={{0,8},{4,12},{8,0},{12,4},{1,9},{5,13},{9,1},{13,5},{2,10},{6,14},... | collective-permute-start | bytes 393224 | tf_op jit(solution)/shard_map/ppermute | solution.py:200
  209.4 10.0 %collective-permute-start.36 = (bf16[512,128]{1,0:T(8,128)(2,1)S(1)}, bf16[512,128]{1,0:T(8,128)(2,1)S(1)}, u32[]{:S(2)}, u32[]{:S(2)}) collective-permute-start(bf16[512,128]{1,0:T(8,128)(2,1)S(1)} %get-tuple-element.160), channel_id=1, source_target_pairs={{0,12},{4,8},{8,4},{12,0},{1,13},{5,9},{9,5},{13,1},{2,14},{6,10},... | collective-permute-start | bytes 393224 | tf_op jit(solution)/shard_map/ppermute | solution.py:200
  214.3 4.2 %collective-permute-start.37 = (bf16[16,128]{1,0:T(8,128)(2,1)S(1)}, bf16[16,128]{1,0:T(8,128)(2,1)S(1)}, u32[]{:S(2)}, u32[]{:S(2)}) collective-permute-start(bf16[16,128]{1,0:T(8,128)(2,1)S(1)} %slice_bitcast_fusion.8), channel_id=1, source_target_pairs={{0,8},{4,12},{8,0},{12,4},{1,9},{5,13},{9,1},{13,5},{2,10},{6,14},... | collective-permute-start | bytes 12296 | tf_op jit(solution)/shard_map/ppermute | solution.py:200
  215.7 3.0 %collective-permute-start.38 = (bf16[16,128]{1,0:T(8,128)(2,1)S(1)}, bf16[16,128]{1,0:T(8,128)(2,1)S(1)}, u32[]{:S(2)}, u32[]{:S(2)}) collective-permute-start(bf16[16,128]{1,0:T(8,128)(2,1)S(1)} %slice_bitcast_fusion.8), channel_id=1, source_target_pairs={{0,12},{4,8},{8,4},{12,0},{1,13},{5,9},{9,5},{13,1},{2,14},{6,10},... | collective-permute-start | bytes 12296 | tf_op jit(solution)/shard_map/ppermute | solution.py:200
  216.7 2.0 collective-permute-start.35

commit v10 on v9

--- a/solution.py
+++ b/solution.py
@@ -39,6 +39,7 @@
 
 
 SMALL = pl.CostEstimate(flops=1, bytes_accessed=1, transcendentals=0)
+SOME = pl.CostEstimate(flops=2 * 10**9, bytes_accessed=2**20, transcendentals=0)
 PARAMS = pltpu.CompilerParams(vmem_limit_bytes=12 * 2**20)
 
 
@@ -136,7 +137,7 @@
             outs[u][r] = value.astype(outs[u].dtype)
 
 
-def partial_scores(units, grads, out_as):
+def partial_scores(units, grads, out_as, cost):
     rows = units[0][0].shape[0]
     train_rows = grads[0].shape[0]
     return pl.pallas_call(
@@ -145,7 +146,7 @@
         out_specs=[VMEM] * len(units),
         out_shape=[jax.ShapeDtypeStruct((4, train_rows, rows), kind) for kind in out_as],
         compiler_params=PARAMS,
-        cost_estimate=SMALL,
+        cost_estimate=cost,
         name="scores",
     )(*[value for unit in units for value in unit], *grads)
 
@@ -210,8 +211,8 @@
     def core_sum(kept, *sent, sent_as=BF16):
         return fold(flags, kept, [to_other(part, 1) for part in sent], sent_as)
 
-    def scores_of(*units, out_as=(BF16, BF16)):
-        return partial_scores(units, grads, out_as[: len(units)])
+    def scores_of(*units, out_as=(BF16, BF16), cost=SMALL):
+        return partial_scores(units, grads, out_as[: len(units)], cost)
 
     def in_order(parts):
         parts = [parts[0], parts[2], parts[1], parts[3]]
@@ -230,35 +231,36 @@
     grads = [train_grads, to_other(train_grads, 1), to_other(train_grads, 2)]
     own, own_sent = core_sum(*product(flags, [test_grads], fisher), sent_as=F32)
     counts = selected(chosen_ids)
-    far_ids = along(chosen_ids, [(0, 3), (3, 0)])
-    pair_in, middle_in, own, own_sent, counts, far_ids, grads[1] = tied(
-        pair_in, middle_in, own, own_sent, counts, far_ids, grads[1]
+    pair_in, middle_in, own, own_sent, counts, chosen_ids, grads[1] = tied(
+        pair_in, middle_in, own, own_sent, counts, chosen_ids, grads[1]
     )
 
     second_edge = along(middle_in, outward)
     far_in = along(pair_in, middle)
+    grads = grads + [to_other(grads[2], 1)]
     near, near_sent = core_sum(*product(flags, [middle_in, pair_in], fisher))
-    near_sent, own_sent = tied(near_sent, own_sent)
+    own_got = to_other(own_sent, 2)
+    near_sent, own_got, pair_in, grads[3] = tied(near_sent, own_got, pair_in, grads[3])
     near_got = to_other(near_sent, 2)
-    own_got = to_other(own_sent, 2)
-    far_counts = selected(far_ids)
-    grads = grads + [to_other(grads[2], 1)]
-    (near,) = scores_of((near, near_got))
-    far_in, second_edge, pair_in, own, own_got, near, far_counts, grads = tied(
-        far_in, second_edge, pair_in, own, own_got, near, far_counts, grads
+    third, third_sent = core_sum(*product(flags, [pair_in], fisher))
+    (near,) = scores_of((near, near_got), cost=SOME)
+    far_ids = along(chosen_ids, [(0, 3), (3, 0)])
+    far_in, second_edge, third, third_sent, own, own_got, near, far_ids, grads = tied(
+        far_in, second_edge, third, third_sent, own, own_got, near, far_ids, grads
     )
 
     first_edge = along(far_in, outward)
+    second, second_sent = core_sum(*product(flags, [far_in, second_edge], fisher))
+    second, second_sent, near = tied(second, second_sent, near)
+    second_got = to_other(second_sent, 2)
     near_in, near_across = along(near, inward), along(near, middle)
-    second, second_sent = core_sum(*product(flags, [far_in, second_edge], fisher))
-    second_sent, pair_in = tied(second_sent, pair_in)
-    third, third_sent = core_sum(*product(flags, [pair_in], fisher))
-    second, near_in, near_across = tied(second, near_in, near_across)
-    (second,) = scores_of((second, to_other(second_sent, 2)))
+    second_got, near_in, near_across = tied(second_got, near_in, near_across)
+    (second,) = scores_of((second, second_got))
     across = along(second, middle)
     third, total = scores_of(
         (third, to_other(third_sent, 2)), (own, own_got), out_as=(F32, F32)
     )
+    far_counts = selected(far_ids)
     first_edge, total, near_in, near_across, second, across, third, grads, far_counts = tied(
         first_edge, total, near_in, near_across, second, across, third, grads, far_counts
     )

time: 222 us -> 221 us (level)
    ppermute x26, waiting for transfers between devices: 89.2 us -> 85.1 us  [to_other(): return lax.ppermute(value, 'train', [(k, k ^ r) for k in range(4)])]
    ppermute x26, starting transfers between devices: 16.4 us -> 19.7 us  [to_other(): return lax.ppermute(value, 'train', [(k, k ^ r) for k in range(4)])]
    ppermute x13, starting transfers between devices: 34.2 us -> 31.5 us  [along(): return lax.ppermute(value, 'test', pairs)]
    ppermute x13, waiting for transfers between devices: 7.54 us -> 10.2 us  [along(): return lax.ppermute(value, 'test', pairs)]
    unnamed x18 -> x16, local copies, waits for them, and re-layouts: 11.3 us -> 11.3 us
  transfers between devices with their start and end apart: 39 -> 39, of which waited for: 19 -> 20; matrix products, arithmetic and copies ran while one was open for 2% -> 2% of each run, Pallas kernels for 22% -> 22%
where the time goes in v10:
time: 221 us; the launch traced here: 220 us
  waiting for transfers between devices  95.2 us (43%)
  Pallas kernels  54.8 us (25%)
  starting transfers between devices  51.1 us (23%)
  local copies, waits for them, and re-layouts  11.5 us (5%)
  other arithmetic  6.06 us (3%)
    ppermute x26, waiting for transfers between devices, to_other(): return lax.ppermute(value, 'train', [(k, k ^ r) for k in range(4)])  85.1 us
    pallas_call x5, Pallas kernels, product(): pl.pallas_call(functools.partial(product_body, len(blocks)), in_specs=[pl...  31.7 us
    ppermute x13, starting transfers between devices, along(): return lax.ppermute(value, 'test', pairs)  31.5 us
    ppermute x26, starting transfers between devices, to_other(): return lax.ppermute(value, 'train', [(k, k ^ r) for k in range(4)])  19.7 us
    pallas_call x3, Pallas kernels, partial_scores(): pl.pallas_call(lambda *refs: scores_body(len(units), *refs), in_specs=[VM...  14.1 us
    unnamed x16, local copies, waits for them, and re-layouts  11.3 us
    ppermute x13, waiting for transfers between devices, along(): return lax.ppermute(value, 'test', pairs)  10.2 us
    pallas_call x2, Pallas kernels, last_scores(): pl.pallas_call(functools.partial(last_scores_body, which), in_specs=[VMEM...  4.8 us
  transfers between devices with their start and end apart: 39, of which 20 were waited for; matrix products, arithmetic and copies ran while one was open for 2% of the time, Pallas kernels for 22%

profile of v10, /device:TPU:0, one launch (start us, length us, event | category | flops | bytes accessed | tf_op | source)
XLA Modules:
  0.0 219.7 jit_solution(11850765465171057742)
XLA Ops:
  0.6 3.0 %collective-permute-start.10 = (bf16[512,2048]{1,0:T(8,128)(2,1)}, bf16[512,2048]{1,0:T(8,128)(2,1)S(1)}, u32[]{:S(2)}, u32[]{:S(2)}) collective-permute-start(bf16[512,2048]{1,0:T(8,128)(2,1)} %refs_0_.2), channel_id=1, source_target_pairs={{0,8},{4,12},{8,0},{12,4},{1,9},{5,13},{9,1},{13,5},{2,10},{6,14},... | collective-permute-start | bytes 6291464 | tf_op jit(solution)/shard_map/ppermute | solution.py:201
  3.6 1.6 collective-permute-start
  5.2 2.0 collective-permute-start.1
  7.3 3.4 %copy-done = bf16[2048,2048]{1,0:T(8,128)(2,1)S(1)} copy-done((bf16[2048,2048]{1,0:T(8,128)(2,1)S(1)}, bf16[2048,2048]{1,0:T(8,128)(2,1)}, u32[]{:S(2)}) %copy-start) | copy-done | bytes 8388632
  10.7 1.6 copy-done.6
  12.3 6.4 %product.5 = (f32[256,2048]{1,0:T(8,128)S(1)}, bf16[128,2048]{1,0:T(8,128)(2,1)}, bf16[128,2048]{1,0:T(8,128)(2,1)S(1)}) custom-call(s32[3]{0:T(128)S(1)} %pad_add_fusion.flags, bf16[512,2048]{1,0:T(8,128)(2,1)S(1)} %copy-done.6, bf16[2048,2048]{1,0:T(8,128)(2,1)S(1)} %copy-done), custom_call_target="tpu_custom_call" | custom-call | flops 1 | bytes 1 | tf_op jit(solution)/shard_map/product/pallas_call | solution.py:79
  18.7 1.4 copy-done.4
  20.6 28.8 %collective-permute-done.10.refs_4_.refs_6_.refs_0_ = bf16[512,2048]{1,0:T(8,128)(2,1)S(1)} collective-permute-done((bf16[512,2048]{1,0:T(8,128)(2,1)}, bf16[512,2048]{1,0:T(8,128)(2,1)S(1)}, u32[]{:S(2)}, u32[]{:S(2)}) %collective-permute-start.10) | collective-permute-done | bytes 2097184 | tf_op jit(solution)/shard_map/ppermute | solution.py:201
  50.1 1.7 convert_add_fusion.1
  51.8 2.6 %collective-permute-done.3.refs_1_ = bf16[128,2048]{1,0:T(8,128)(2,1)S(1)} collective-permute-done((bf16[128,2048]{1,0:T(8,128)(2,1)S(1)}, bf16[128,2048]{1,0:T(8,128)(2,1)S(1)}, u32[]{:S(2)}, u32[]{:S(2)}) %collective-permute-start.3) | collective-permute-done | bytes 524320 | tf_op jit(solution)/shard_map/ppermute | solution.py:201
  54.4 1.6 copy-done.5
  56.0 0.9 fold.5
  56.9 0.8 collective-permute-start.5
  57.7 1.3 collective-permute-start.6
  59.0 3.4 %copy-done.1 = bf16[2048,2048]{1,0:T(8,128)(2,1)S(1)} copy-done((bf16[2048,2048]{1,0:T(8,128)(2,1)S(1)}, bf16[2048,2048]{1,0:T(8,128)(2,1)}, u32[]{:S(2)}) %copy-start.1) | copy-done | bytes 8388632
  62.4 7.5 %product.6 = (f32[256,2048]{1,0:T(8,128)S(1)}, bf16[128,2048]{1,0:T(8,128)(2,1)S(1)}, bf16[128,2048]{1,0:T(8,128)(2,1)S(1)}) custom-call(s32[3]{0:T(128)S(1)} %pad_add_fusion.flags, bf16[512,2048]{1,0:T(8,128)(2,1)} %collective-permute-done.1.refs_0_, bf16[512,2048]{1,0:T(8,128)(2,1)} %collective-permute-done.refs_1_.refs_0_, bf16[2048,2048]{1,0:T(8,128)(2,1)S(1)} %copy-done.1), custom_call_target="tpu_custom_call" | custom-call | flops 1 | bytes 1 | tf_op jit(solution)/shard_map/product/pallas_call | solution.py:79
  70.1 1.8 collective-permute-start.9
  72.0 1.8 collective-permute-done.8.refs_1_
  73.7 0.8 fold.6
  74.6 20.9 %collective-permute-done.9.refs_3_ = f32[128,2048]{1,0:T(8,128)S(1)} collective-permute-done((f32[128,2048]{1,0:T(8,128)S(1)}, f32[128,2048]{1,0:T(8,128)S(1)}, u32[]{:S(2)}, u32[]{:S(2)}) %collective-permute-start.9) | collective-permute-done | bytes 1048608 | tf_op jit(solution)/shard_map/ppermute | solution.py:201
  95.5 1.7 collective-permute-start.14
  97.2 6.7 %product.7 = (f32[256,2048]{1,0:T(8,128)S(1)}, bf16[128,2048]{1,0:T(8,128)(2,1)S(1)}, bf16[128,2048]{1,0:T(8,128)(2,1)S(1)}) custom-call(s32[3]{0:T(128)S(1)} %pad_add_fusion.flags, bf16[512,2048]{1,0:T(8,128)(2,1)} %collective-permute-done.refs_1_.refs_0_, bf16[2048,2048]{1,0:T(8,128)(2,1)S(1)} %copy-done.2), custom_call_target="tpu_custom_call" | custom-call | flops 1 | bytes 1 | tf_op jit(solution)/shard_map/product/pallas_call | solution.py:79
  104.5 4.4 %collective-permute-done.14.refs_1_ = bf16[128,2048]{1,0:T(8,128)(2,1)S(1)} collective-permute-done((bf16[128,2048]{1,0:T(8,128)(2,1)S(1)}, bf16[128,2048]{1,0:T(8,128)(2,1)S(1)}, u32[]{:S(2)}, u32[]{:S(2)}) %collective-permute-start.14) | collective-permute-done | bytes 524320 | tf_op jit(solution)/shard_map/ppermute | solution.py:201
  108.9 5.7 %collective-permute-start.15 = (s32[512,16]{0,1:T(8,128)S(1)}, s32[512,16]{0,1:T(8,128)S(1)}, u32[]{:S(2)}, u32[]{:S(2)}) collective-permute-start(s32[512,16]{0,1:T(8,128)S(1)} %copy-done.7), channel_id=1, source_target_pairs={{0,3},{3,0},{4,7},{7,4},{8,11},{11,8},{12,15},{15,12},{16,19},{19,... | collective-permute-start | bytes 98312 | tf_op jit(solution)/shard_map/ppermute | solution.py:198
  114.6 4.0 %scores.3 = bf16[4,512,128]{2,1,0:T(8,128)(2,1)S(1)} custom-call(f32[128,2048]{1,0:T(8,128)S(1)} %get-tuple-element.96.refs_0_, bf16[128,2048]{1,0:T(8,128)(2,1)S(1)} %collective-permute-done.14.refs_1_, bf16[512,2048]{1,0:T(8,128)(2,1)S(1)} %copy-done.3, bf16[512,2048]{1,0:T(8,128)(2,1)} %collective-permute-done.4.refs_3_.refs_5_.refs_1_, ...), custom_call_target="tpu_custom_call" | custom-call | flops 2000000000 | bytes 1048576 | tf_op jit(solution)/shard_map/scores/pallas_call | solution.py:143
  118.7 0.9 fold.7
  119.6 1.3 collective-permute-start.16
  120.9 5.6 %product.8 = (f32[256,2048]{1,0:T(8,128)S(1)}, bf16[128,2048]{1,0:T(8,128)(2,1)S(1)}, bf16[128,2048]{1,0:T(8,128)(2,1)S(1)}) custom-call(s32[3]{0:T(128)S(1)} %pad_add_fusion.flags, bf16[512,2048]{1,0:T(8,128)(2,1)S(1)} %collective-permute-done.5.refs_0_, bf16[512,2048]{1,0:T(8,128)(2,1)S(1)} %collective-permute-done.6.refs_1_, bf16[2048,2048]{1,0:T(8,128)(2,1)S(1)} %copy-done.2), custom_call_target="tpu_custom_call" | custom-call | flops 1 | bytes 1 | tf_op jit(solution)/shard_map/product/pallas_call | solution.py:79
  127.0 1.4 collective-permute-done.18.refs_0_
  128.4 0.7 collective-permute-done.19.refs_1_
  129.2 0.8 fold.8
  130.0 1.6 collective-permute-start.20
  131.6 4.7 %collective-permute-start.21 = (bf16[4,512,128]{2,1,0:T(8,128)(2,1)S(1)}, bf16[4,512,128]{2,1,0:T(8,128)(2,1)S(1)}, u32[]{:S(2)}, u32[]{:S(2)}) collective-permute-start(bf16[4,512,128]{2,1,0:T(8,128)(2,1)S(1)} %scores.3), channel_id=1, source_target_pairs={{0,1},{3,2},{4,5},{7,6},{8,9},{11,10},{12,13},{15,14},{16,17},{19,... | collective-permute-start | bytes 1572872 | tf_op jit(solution)/shard_map/ppermute | solution.py:198
  136.3 0.9 collective-permute-start.22
  137.7 7.1 %collective-permute-done.20.refs_1_ = bf16[128,2048]{1,0:T(8,128)(2,1)S(1)} collective-permute-done((bf16[128,2048]{1,0:T(8,128)(2,1)S(1)}, bf16[128,2048]{1,0:T(8,128)(2,1)S(1)}, u32[]{:S(2)}, u32[]{:S(2)}) %collective-permute-start.20) | collective-permute-done | bytes 524320 | tf_op jit(solution)/shard_map/ppermute | solution.py:201
  144.8 2.6 %collective-permute-done.21 = bf16[4,512,128]{2,1,0:T(8,128)(2,1)S(1)} collective-permute-done((bf16[4,512,128]{2,1,0:T(8,128)(2,1)S(1)}, bf16[4,512,128]{2,1,0:T(8,128)(2,1)S(1)}, u32[]{:S(2)}, u32[]{:S(2)}) %collective-permute-start.21) | collective-permute-done | bytes 524320 | tf_op jit(solution)/shard_map/ppermute | solution.py:198
  147.4 4.0 %scores.5 = bf16[4,512,128]{2,1,0:T(8,128)(2,1)S(1)} custom-call(f32[128,2048]{1,0:T(8,128)S(1)} %get-tuple-element.122.refs_0_, bf16[128,2048]{1,0:T(8,128)(2,1)S(1)} %collective-permute-done.20.refs_1_, bf16[512,2048]{1,0:T(8,128)(2,1)S(1)} %copy-done.3, bf16[512,2048]{1,0:T(8,128)(2,1)} %collective-permute-done.4.refs_3_.refs_5_.refs_1_, ...), custom_call_target="tpu_custom_call" | custom-call | flops 1 | bytes 1 | tf_op jit(solution)/shard_map/scores/pallas_call | solution.py:143
  152.1 1.7 convert_add_fusion.counts
  153.8 1.5 collective-permute-done.17.refs_1_
  155.3 6.2 %scores.4 = (f32[4,512,128]{2,1,0:T(8,128)S(1)}, f32[4,512,128]{2,1,0:T(8,128)S(1)}) custom-call(f32[128,2048]{1,0:T(8,128)S(1)} %get-tuple-element.102.refs_0_, bf16[128,2048]{1,0:T(8,128)(2,1)S(1)} %collective-permute-done.17.refs_1_, f32[128,2048]{1,0:T(8,128)S(1)} %get-tuple-element.104.refs_2_, f32[128,2048]{1,0:T(8,128)S(1)} %collective-permute-done.9.refs_3_, ...), custom_call_target="tpu_custom_call" | custom-call | flops 1 | bytes 1 | tf_op jit(solution)/shard_map/scores/pallas_call | solution.py:143
  161.5 5.9 %collective-permute-done.16.refs_0_ = bf16[512,2048]{1,0:T(8,128)(2,1)S(1)} collective-permute-done((bf16[512,2048]{1,0:T(8,128)(2,1)S(1)}, bf16[512,2048]{1,0:T(8,128)(2,1)S(1)}, u32[]{:S(2)}, u32[]{:S(2)}) %collective-permute-start.16) | collective-permute-done | bytes 2097184 | tf_op jit(solution)/shard_map/ppermute | solution.py:198
  167.3 5.6 %product.9 = (f32[256,2048]{1,0:T(8,128)S(1)}, bf16[128,2048]{1,0:T(8,128)(2,1)S(1)}, bf16[128,2048]{1,0:T(8,128)(2,1)S(1)}) custom-call(s32[3]{0:T(128)S(1)} %pad_add_fusion.flags, bf16[512,2048]{1,0:T(8,128)(2,1)S(1)} %collective-permute-done.16.refs_0_, bf16[2048,2048]{1,0:T(8,128)(2,1)S(1)} %copy-done.2), custom_call_target="tpu_custom_call" | custom-call | flops 1 | bytes 1 | tf_op jit(solution)/shard_map/product/pallas_call | solution.py:79
  173.5 1.4 collective-permute-done.24.refs_0_
  174.9 0.7 collective-permute-done.25.refs_1_
  175.7 0.8 fold.9
  176.5 1.6 collective-permute-start.26
  178.1 1.3 collective-permute-start.28
  179.4 3.6 %collective-permute-start.27 = (bf16[4,512,128]{2,1,0:T(8,128)(2,1)S(1)}, bf16[4,512,128]{2,1,0:T(8,128)(2,1)S(1)}, u32[]{:S(2)}, u32[]{:S(2)}) collective-permute-start(bf16[4,512,128]{2,1,0:T(8,128)(2,1)S(1)} %scores.5), channel_id=1, source_target_pairs={{0,2},{3,1},{4,6},{7,5},{8,10},{11,9},{12,14},{15,13},{16,18},{19,... | collective-permute-start | bytes 1572872 | tf_op jit(solution)/shard_map/ppermute | solution.py:198
  183.0 7.5 %collective-permute-done.26.got = bf16[128,2048]{1,0:T(8,128)(2,1)S(1)} collective-permute-done((bf16[128,2048]{1,0:T(8,128)(2,1)S(1)}, bf16[128,2048]{1,0:T(8,128)(2,1)S(1)}, u32[]{:S(2)}, u32[]{:S(2)}) %collective-permute-start.26) | collective-permute-done | bytes 524320 | tf_op jit(solution)/shard_map/ppermute | solution.py:201
  190.5 1.3 last_scores.2
  191.8 3.5 %last_scores.3 = (bf16[2,528,128]{2,1,0:T(8,128)(2,1)S(1)}, f32[8,128]{1,0:T(8,128)}) custom-call(f32[128,2048]{1,0:T(8,128)S(1)} %get-tuple-element.133.kept, bf16[128,2048]{1,0:T(8,128)(2,1)S(1)} %collective-permute-done.26.got, f32[4,512,128]{2,1,0:T(8,128)S(1)} %convert_add_fusion.counts, f32[8,128]{1,0:T(8,128)S(1)} %get-tuple-element.138.before, ...), custom_call_target="tpu_custom_call" | custom-call | flops 1 | bytes 1 | tf_op jit(solution)/shard_map/last_scores/pallas_call | solution.py:174
  195.3 3.9 %collective-permute-start.33 = (bf16[2,512,128]{2,1,0:T(8,128)(2,1)S(1)}, bf16[2,512,128]{2,1,0:T(8,128)(2,1)S(1)}, u32[]{:S(2)}, u32[]{:S(2)}) collective-permute-start(bf16[2,512,128]{2,1,0:T(8,128)(2,1)S(1)} %get-tuple-element.149), channel_id=1, source_target_pairs={{0,3},{3,0},{4,7},{7,4},{8,11},{11,8},{12,15},{15,12},{16,19},{19,... | collective-permute-start | bytes 786440 | tf_op jit(solution)/shard_map/ppermute | solution.py:198
  199.7 0.8 collective-permute-start.29
  200.5 1.4 collective-permute-start.31
  201.9 3.8 %collective-permute-start.32 = (bf16[2,528,128]{2,1,0:T(8,128)(2,1)S(1)}, bf16[2,528,128]{2,1,0:T(8,128)(2,1)S(1)}, u32[]{:S(2)}, u32[]{:S(2)}) collective-permute-start(bf16[2,528,128]{2,1,0:T(8,128)(2,1)S(1)} %get-tuple-element.148), channel_id=1, source_target_pairs={{0,3},{3,0},{4,7},{7,4},{8,11},{11,8},{12,15},{15,12},{16,19},{19,... | collective-permute-start | bytes 811016 | tf_op jit(solution)/shard_map/ppermute | solution.py:198
  205.7 0.8 collective-permute-done.33
  206.5 1.6 collective-permute-start.34
  208.1 1.0 collective-permute-done.29
  209.1 3.9 %collective-permute-done.31 = f32[520,128]{1,0:T(8,128)S(1)} collective-permute-done((f32[520,128]{1,0:T(8,128)S(1)}, f32[520,128]{1,0:T(8,128)S(1)}, u32[]{:S(2)}, u32[]{:S(2)}) %collective-permute-start.31) | collective-permute-done | bytes 266272 | tf_op jit(solution)/shard_map/ppermute | solution.py:201
  213.2 0.9 collective-permute-done.32
  214.0 0.7 collective-permute-start.37
  214.7 1.8 collective-permute-start.38
  216.7 1.2 collective-permute-done.37
  218.6 1.1 slice_add_fusion
  (69 shorter events, 6.4 us)
Async XLA Ops:
  0.6 48.8 %collective-permute-start.10 = (bf16[512,2048]{1,0:T(8,128)(2,1)}, bf16[512,2048]{1,0:T(8,128)(2,1)S(1)}, u32[]{:S(2)}, u32[]{:S(2)}) collective-permute-start(bf16[512,2048]{1,0:T(8,128)(2,1)} %refs_0_.2), channel_id=1, source_target_pairs={{0,8},{4,12},{8,0},{12,4},{1,9},{5,13},{9,1},{13,5},{2,10},{6,14},... | collective-permute-start | bytes 6291464 | tf_op jit(solution)/shard_map/ppermute | solution.py:201
  3.6 53.2 %collective-permute-start = (bf16[512,2048]{1,0:T(8,128)(2,1)}, bf16[512,2048]{1,0:T(8,128)(2,1)}, u32[]{:S(2)}, u32[]{:S(2)}) collective-permute-start(bf16[512,2048]{1,0:T(8,128)(2,1)} %refs_0_.1), channel_id=1, source_target_pairs={{0,1},{1,0},{2,3},{3,2},{4,5},{5,4},{6,7},{7,6},{8,9},{9,8},{10,11... | collective-permute-start | bytes 6291464 | tf_op jit(solution)/shard_map/ppermute | solution.py:198
  5.2 51.6 %collective-permute-start.1 = (bf16[512,2048]{1,0:T(8,128)(2,1)}, bf16[512,2048]{1,0:T(8,128)(2,1)}, u32[]{:S(2)}, u32[]{:S(2)}) collective-permute-start(bf16[512,2048]{1,0:T(8,128)(2,1)} %refs_0_.1), channel_id=1, source_target_pairs={{1,2},{2,1},{5,6},{6,5},{9,10},{10,9},{13,14},{14,13},{17,18},{18,... | collective-permute-start | bytes 6291464 | tf_op jit(solution)/shard_map/ppermute | solution.py:198
  7.2 49.6 %collective-permute-start.4 = (bf16[512,2048]{1,0:T(8,128)(2,1)}, bf16[512,2048]{1,0:T(8,128)(2,1)}, u32[]{:S(2)}, u32[]{:S(2)}) collective-permute-start(bf16[512,2048]{1,0:T(8,128)(2,1)} %refs_0_.2), channel_id=1, source_target_pairs={{0,4},{4,0},{8,12},{12,8},{1,5},{5,1},{9,13},{13,9},{2,6},{6,2},{1... | collective-permute-start | bytes 6291464 | tf_op jit(solution)/shard_map/ppermute | solution.py:201
  7.3 3.4 %copy-start = (bf16[2048,2048]{1,0:T(8,128)(2,1)S(1)}, bf16[2048,2048]{1,0:T(8,128)(2,1)}, u32[]{:S(2)}) copy-start(bf16[2048,2048]{1,0:T(8,128)(2,1)} %refs_1_.5) | copy-start | bytes 25165828
  10.7 1.6 copy-start.6
  12.3 8.4 %copy-start.7 = (s32[512,16]{0,1:T(8,128)S(1)}, s32[512,16]{0,1:T(8,128)}, u32[]{:S(2)}) copy-start(s32[512,16]{0,1:T(8,128)} %param.7) | copy-start | bytes 98308
  18.7 1.4 copy-start.4
  20.1 29.4 %collective-permute-start.2 = (bf16[128,2048]{1,0:T(8,128)(2,1)}, bf16[128,2048]{1,0:T(8,128)(2,1)S(1)}, u32[]{:S(2)}, u32[]{:S(2)}) collective-permute-start(bf16[128,2048]{1,0:T(8,128)(2,1)} %get-tuple-element.77), channel_id=1, source_target_pairs={{0,4},{4,0},{8,12},{12,8},{1,5},{5,1},{9,13},{13,9},{2,6},{6,2},{1... | collective-permute-start | bytes 1572872 | tf_op jit(solution)/shard_map/ppermute | solution.py:201
  49.5 46.0 %collective-permute-start.11 = (bf16[512,2048]{1,0:T(8,128)(2,1)S(1)}, bf16[512,2048]{1,0:T(8,128)(2,1)S(1)}, u32[]{:S(2)}, u32[]{:S(2)}) collective-permute-start(bf16[512,2048]{1,0:T(8,128)(2,1)S(1)} %collective-permute-done.10.refs_4_.refs_6_.refs_0_), channel_id=1, source_target_pairs={{0,4},{4,0},{8,12},{12,8},{1,5},{5,1},{9,13},{13,9},{2,6},{6,2},{1... | collective-permute-start | bytes 6291464 | tf_op jit(solution)/shard_map/ppermute | solution.py:201
  49.5 4.9 %collective-permute-start.3 = (bf16[128,2048]{1,0:T(8,128)(2,1)S(1)}, bf16[128,2048]{1,0:T(8,128)(2,1)S(1)}, u32[]{:S(2)}, u32[]{:S(2)}) collective-permute-start(bf16[128,2048]{1,0:T(8,128)(2,1)S(1)} %get-tuple-element.78), channel_id=1, source_target_pairs={{0,4},{4,0},{8,12},{12,8},{1,5},{5,1},{9,13},{13,9},{2,6},{6,2},{1... | collective-permute-start | bytes 1572872 | tf_op jit(solution)/shard_map/ppermute | solution.py:201
  54.4 1.6 copy-start.5
  56.9 62.7 %collective-permute-start.5 = (bf16[512,2048]{1,0:T(8,128)(2,1)}, bf16[512,2048]{1,0:T(8,128)(2,1)S(1)}, u32[]{:S(2)}, u32[]{:S(2)}) collective-permute-start(bf16[512,2048]{1,0:T(8,128)(2,1)} %collective-permute-done.refs_1_.refs_0_), channel_id=1, source_target_pairs={{1,2},{2,1},{5,6},{6,5},{9,10},{10,9},{13,14},{14,13},{17,18},{18,... | collective-permute-start | bytes 6291464 | tf_op jit(solution)/shard_map/ppermute | solution.py:198
  57.7 61.9 %collective-permute-start.6 = (bf16[512,2048]{1,0:T(8,128)(2,1)}, bf16[512,2048]{1,0:T(8,128)(2,1)S(1)}, u32[]{:S(2)}, u32[]{:S(2)}) collective-permute-start(bf16[512,2048]{1,0:T(8,128)(2,1)} %collective-permute-done.1.refs_0_), channel_id=1, source_target_pairs={{1,0},{2,3},{5,4},{6,7},{9,8},{10,11},{13,12},{14,15},{17,16},{18,... | collective-permute-start | bytes 6291464 | tf_op jit(solution)/shard_map/ppermute | solution.py:198
  59.0 3.4 %copy-start.1 = (bf16[2048,2048]{1,0:T(8,128)(2,1)S(1)}, bf16[2048,2048]{1,0:T(8,128)(2,1)}, u32[]{:S(2)}) copy-start(bf16[2048,2048]{1,0:T(8,128)(2,1)} %refs_1_.5) | copy-start | bytes 25165828
  62.4 34.9 %copy-start.2 = (bf16[2048,2048]{1,0:T(8,128)(2,1)S(1)}, bf16[2048,2048]{1,0:T(8,128)(2,1)}, u32[]{:S(2)}) copy-start(bf16[2048,2048]{1,0:T(8,128)(2,1)} %refs_1_.5) | copy-start | bytes 25165828
  69.9 2.0 collective-permute-start.7
  70.1 25.4 %collective-permute-start.9 = (f32[128,2048]{1,0:T(8,128)S(1)}, f32[128,2048]{1,0:T(8,128)S(1)}, u32[]{:S(2)}, u32[]{:S(2)}) collective-permute-start(f32[128,2048]{1,0:T(8,128)S(1)} %get-tuple-element.87), channel_id=1, source_target_pairs={{0,8},{4,12},{8,0},{12,4},{1,9},{5,13},{9,1},{13,5},{2,10},{6,14},... | collective-permute-start | bytes 3145736 | tf_op jit(solution)/shard_map/ppermute | solution.py:201
  71.8 1.9 collective-permute-start.8
  95.5 19.1 %copy-start.3 = (bf16[512,2048]{1,0:T(8,128)(2,1)S(1)}, bf16[512,2048]{1,0:T(8,128)(2,1)}, u32[]{:S(2)}) copy-start(bf16[512,2048]{1,0:T(8,128)(2,1)} %refs_0_.2) | copy-start | bytes 6291460
  95.5 13.4 %collective-permute-start.14 = (bf16[128,2048]{1,0:T(8,128)(2,1)S(1)}, bf16[128,2048]{1,0:T(8,128)(2,1)S(1)}, u32[]{:S(2)}, u32[]{:S(2)}) collective-permute-start(bf16[128,2048]{1,0:T(8,128)(2,1)S(1)} %get-tuple-element.97), channel_id=1, source_target_pairs={{0,8},{4,12},{8,0},{12,4},{1,9},{5,13},{9,1},{13,5},{2,10},{6,14},... | collective-permute-start | bytes 1572872 | tf_op jit(solution)/shard_map/ppermute | solution.py:201
  104.0 14.7 %collective-permute-start.12 = (bf16[128,2048]{1,0:T(8,128)(2,1)S(1)}, bf16[128,2048]{1,0:T(8,128)(2,1)S(1)}, u32[]{:S(2)}, u32[]{:S(2)}) collective-permute-start(bf16[128,2048]{1,0:T(8,128)(2,1)S(1)} %get-tuple-element.90), channel_id=1, source_target_pairs={{0,4},{4,0},{8,12},{12,8},{1,5},{5,1},{9,13},{13,9},{2,6},{6,2},{1... | collective-permute-start | bytes 1572872 | tf_op jit(solution)/shard_map/ppermute | solution.py:201
  104.0 14.6 %collective-permute-start.13 = (bf16[128,2048]{1,0:T(8,128)(2,1)S(1)}, bf16[128,2048]{1,0:T(8,128)(2,1)S(1)}, u32[]{:S(2)}, u32[]{:S(2)}) collective-permute-start(bf16[128,2048]{1,0:T(8,128)(2,1)S(1)} %get-tuple-element.91), channel_id=1, source_target_pairs={{0,4},{4,0},{8,12},{12,8},{1,5},{5,1},{9,13},{13,9},{2,6},{6,2},{1... | collective-permute-start | bytes 1572872 | tf_op jit(solution)/shard_map/ppermute | solution.py:201
  108.9 10.6 %collective-permute-start.15 = (s32[512,16]{0,1:T(8,128)S(1)}, s32[512,16]{0,1:T(8,128)S(1)}, u32[]{:S(2)}, u32[]{:S(2)}) collective-permute-start(s32[512,16]{0,1:T(8,128)S(1)} %copy-done.7), channel_id=1, source_target_pairs={{0,3},{3,0},{4,7},{7,4},{8,11},{11,8},{12,15},{15,12},{16,19},{19,... | collective-permute-start | bytes 98312 | tf_op jit(solution)/shard_map/ppermute | solution.py:198
  119.6 47.8 %collective-permute-start.16 = (bf16[512,2048]{1,0:T(8,128)(2,1)S(1)}, bf16[512,2048]{1,0:T(8,128)(2,1)S(1)}, u32[]{:S(2)}, u32[]{:S(2)}) collective-permute-start(bf16[512,2048]{1,0:T(8,128)(2,1)S(1)} %collective-permute-done.5.refs_0_), channel_id=1, source_target_pairs={{1,0},{2,3},{5,4},{6,7},{9,8},{10,11},{13,12},{14,15},{17,16},{18,... | collective-permute-start | bytes 6291464 | tf_op jit(solution)/shard_map/ppermute | solution.py:198
  126.5 2.0 collective-permute-start.18
  126.5 2.6 %collective-permute-start.19 = (bf16[128,2048]{1,0:T(8,128)(2,1)S(1)}, bf16[128,2048]{1,0:T(8,128)(2,1)S(1)}, u32[]{:S(2)}, u32[]{:S(2)}) collective-permute-start(bf16[128,2048]{1,0:T(8,128)(2,1)S(1)} %get-tuple-element.114), channel_id=1, source_target_pairs={{0,4},{4,0},{8,12},{12,8},{1,5},{5,1},{9,13},{13,9},{2,6},{6,2},{1... | collective-permute-start | bytes 1572872 | tf_op jit(solution)/shard_map/ppermute | solution.py:201
  130.0 14.8 %collective-permute-start.20 = (bf16[128,2048]{1,0:T(8,128)(2,1)S(1)}, bf16[128,2048]{1,0:T(8,128)(2,1)S(1)}, u32[]{:S(2)}, u32[]{:S(2)}) collective-permute-start(bf16[128,2048]{1,0:T(8,128)(2,1)S(1)} %get-tuple-element.118), channel_id=1, source_target_pairs={{0,8},{4,12},{8,0},{12,4},{1,9},{5,13},{9,1},{13,5},{2,10},{6,14},... | collective-permute-start | bytes 1572872 | tf_op jit(solution)/shard_map/ppermute | solution.py:201
  131.6 15.9 %collective-permute-start.21 = (bf16[4,512,128]{2,1,0:T(8,128)(2,1)S(1)}, bf16[4,512,128]{2,1,0:T(8,128)(2,1)S(1)}, u32[]{:S(2)}, u32[]{:S(2)}) collective-permute-start(bf16[4,512,128]{2,1,0:T(8,128)(2,1)S(1)} %scores.3), channel_id=1, source_target_pairs={{0,1},{3,2},{4,5},{7,6},{8,9},{11,10},{12,13},{15,14},{16,17},{19,... | collective-permute-start | bytes 1572872 | tf_op jit(solution)/shard_map/ppermute | solution.py:198
  136.3 11.2 %collective-permute-start.22 = (bf16[4,512,128]{2,1,0:T(8,128)(2,1)S(1)}, bf16[4,512,128]{2,1,0:T(8,128)(2,1)S(1)}, u32[]{:S(2)}, u32[]{:S(2)}) collective-permute-start(bf16[4,512,128]{2,1,0:T(8,128)(2,1)S(1)} %scores.3), channel_id=1, source_target_pairs={{1,2},{2,1},{5,6},{6,5},{9,10},{10,9},{13,14},{14,13},{17,18},{18,... | collective-permute-start | bytes 1572872 | tf_op jit(solution)/shard_map/ppermute | solution.py:198
  137.1 18.1 %collective-permute-start.17 = (bf16[128,2048]{1,0:T(8,128)(2,1)S(1)}, bf16[128,2048]{1,0:T(8,128)(2,1)S(1)}, u32[]{:S(2)}, u32[]{:S(2)}) collective-permute-start(bf16[128,2048]{1,0:T(8,128)(2,1)S(1)} %get-tuple-element.103), channel_id=1, source_target_pairs={{0,8},{4,12},{8,0},{12,4},{1,9},{5,13},{9,1},{13,5},{2,10},{6,14},... | collective-permute-start | bytes 1572872 | tf_op jit(solution)/shard_map/ppermute | solution.py:201
  151.4 10.1 %collective-permute-start.23 = (bf16[4,512,128]{2,1,0:T(8,128)(2,1)S(1)}, bf16[4,512,128]{2,1,0:T(8,128)(2,1)S(1)}, u32[]{:S(2)}, u32[]{:S(2)}) collective-permute-start(bf16[4,512,128]{2,1,0:T(8,128)(2,1)S(1)} %scores.5), channel_id=1, source_target_pairs={{1,2},{2,1},{5,6},{6,5},{9,10},{10,9},{13,14},{14,13},{17,18},{18,... | collective-permute-start | bytes 1572872 | tf_op jit(solution)/shard_map/ppermute | solution.py:198
  172.9 2.0 collective-permute-start.24
  173.0 2.6 %collective-permute-start.25 = (bf16[128,2048]{1,0:T(8,128)(2,1)S(1)}, bf16[128,2048]{1,0:T(8,128)(2,1)S(1)}, u32[]{:S(2)}, u32[]{:S(2)}) collective-permute-start(bf16[128,2048]{1,0:T(8,128)(2,1)S(1)} %get-tuple-element.132), channel_id=1, source_target_pairs={{0,4},{4,0},{8,12},{12,8},{1,5},{5,1},{9,13},{13,9},{2,6},{6,2},{1... | collective-permute-start | bytes 1572872 | tf_op jit(solution)/shard_map/ppermute | solution.py:201
  176.5 14.0 %collective-permute-start.26 = (bf16[128,2048]{1,0:T(8,128)(2,1)S(1)}, bf16[128,2048]{1,0:T(8,128)(2,1)S(1)}, u32[]{:S(2)}, u32[]{:S(2)}) collective-permute-start(bf16[128,2048]{1,0:T(8,128)(2,1)S(1)} %get-tuple-element.134), channel_id=1, source_target_pairs={{0,8},{4,12},{8,0},{12,4},{1,9},{5,13},{9,1},{13,5},{2,10},{6,14},... | collective-permute-start | bytes 1572872 | tf_op jit(solution)/shard_map/ppermute | solution.py:201
  178.1 17.2 %collective-permute-start.28 = (bf16[4,512,128]{2,1,0:T(8,128)(2,1)S(1)}, bf16[4,512,128]{2,1,0:T(8,128)(2,1)S(1)}, u32[]{:S(2)}, u32[]{:S(2)}) collective-permute-start(bf16[4,512,128]{2,1,0:T(8,128)(2,1)S(1)} %add_convert_fusion), channel_id=1, source_target_pairs={{1,0},{2,3},{5,4},{6,7},{9,8},{10,11},{13,12},{14,15},{17,16},{18,... | collective-permute-start | bytes 1572872 | tf_op jit(solution)/shard_map/ppermute | solution.py:198
  179.4 15.9 %collective-permute-start.27 = (bf16[4,512,128]{2,1,0:T(8,128)(2,1)S(1)}, bf16[4,512,128]{2,1,0:T(8,128)(2,1)S(1)}, u32[]{:S(2)}, u32[]{:S(2)}) collective-permute-start(bf16[4,512,128]{2,1,0:T(8,128)(2,1)S(1)} %scores.5), channel_id=1, source_target_pairs={{0,2},{3,1},{4,6},{7,5},{8,10},{11,9},{12,14},{15,13},{16,18},{19,... | collective-permute-start | bytes 1572872 | tf_op jit(solution)/shard_map/ppermute | solution.py:198
  195.3 11.2 %collective-permute-start.33 = (bf16[2,512,128]{2,1,0:T(8,128)(2,1)S(1)}, bf16[2,512,128]{2,1,0:T(8,128)(2,1)S(1)}, u32[]{:S(2)}, u32[]{:S(2)}) collective-permute-start(bf16[2,512,128]{2,1,0:T(8,128)(2,1)S(1)} %get-tuple-element.149), channel_id=1, source_target_pairs={{0,3},{3,0},{4,7},{7,4},{8,11},{11,8},{12,15},{15,12},{16,19},{19,... | collective-permute-start | bytes 786440 | tf_op jit(solution)/shard_map/ppermute | solution.py:198
  199.7 9.4 %collective-permute-start.29 = (f32[520,128]{1,0:T(8,128)S(1)}, f32[520,128]{1,0:T(8,128)S(1)}, u32[]{:S(2)}, u32[]{:S(2)}) collective-permute-start(f32[520,128]{1,0:T(8,128)S(1)} %get-tuple-element.202), channel_id=1, source_target_pairs={{0,8},{4,12},{8,0},{12,4},{1,9},{5,13},{9,1},{13,5},{2,10},{6,14},... | collective-permute-start | bytes 798728 | tf_op jit(solution)/shard_map/ppermute | solution.py:201
  200.5 8.6 %collective-permute-start.30 = (f32[520,128]{1,0:T(8,128)S(1)}, f32[520,128]{1,0:T(8,128)S(1)}, u32[]{:S(2)}, u32[]{:S(2)}) collective-permute-start(f32[520,128]{1,0:T(8,128)S(1)} %get-tuple-element.203), channel_id=1, source_target_pairs={{0,4},{4,0},{8,12},{12,8},{1,5},{5,1},{9,13},{13,9},{2,6},{6,2},{1... | collective-permute-start | bytes 798728 | tf_op jit(solution)/shard_map/ppermute | solution.py:201
  200.5 12.6 %collective-permute-start.31 = (f32[520,128]{1,0:T(8,128)S(1)}, f32[520,128]{1,0:T(8,128)S(1)}, u32[]{:S(2)}, u32[]{:S(2)}) collective-permute-start(f32[520,128]{1,0:T(8,128)S(1)} %get-tuple-element.204), channel_id=1, source_target_pairs={{0,12},{4,8},{8,4},{12,0},{1,13},{5,9},{9,5},{13,1},{2,14},{6,10},... | collective-permute-start | bytes 798728 | tf_op jit(solution)/shard_map/ppermute | solution.py:201
  201.9 12.1 %collective-permute-start.32 = (bf16[2,528,128]{2,1,0:T(8,128)(2,1)S(1)}, bf16[2,528,128]{2,1,0:T(8,128)(2,1)S(1)}, u32[]{:S(2)}, u32[]{:S(2)}) collective-permute-start(bf16[2,528,128]{2,1,0:T(8,128)(2,1)S(1)} %get-tuple-element.148), channel_id=1, source_target_pairs={{0,3},{3,0},{4,7},{7,4},{8,11},{11,8},{12,15},{15,12},{16,19},{19,... | collective-permute-start | bytes 811016 | tf_op jit(solution)/shard_map/ppermute | solution.py:198
  206.5 12.0 %collective-permute-start.34 = (bf16[512,128]{1,0:T(8,128)(2,1)S(1)}, bf16[512,128]{1,0:T(8,128)(2,1)S(1)}, u32[]{:S(2)}, u32[]{:S(2)}) collective-permute-start(bf16[512,128]{1,0:T(8,128)(2,1)S(1)} %get-tuple-element.169), channel_id=1, source_target_pairs={{0,8},{4,12},{8,0},{12,4},{1,9},{5,13},{9,1},{13,5},{2,10},{6,14},... | collective-permute-start | bytes 393224 | tf_op jit(solution)/shard_map/ppermute | solution.py:201
  209.1 9.4 %collective-permute-start.36 = (bf16[512,128]{1,0:T(8,128)(2,1)S(1)}, bf16[512,128]{1,0:T(8,128)(2,1)S(1)}, u32[]{:S(2)}, u32[]{:S(2)}) collective-permute-start(bf16[512,128]{1,0:T(8,128)(2,1)S(1)} %get-tuple-element.168), channel_id=1, source_target_pairs={{0,12},{4,8},{8,4},{12,0},{1,13},{5,9},{9,5},{13,1},{2,14},{6,10},... | collective-permute-start | bytes 393224 | tf_op jit(solution)/shard_map/ppermute | solution.py:201
  214.0 3.9 %collective-permute-start.37 = (bf16[16,128]{1,0:T(8,128)(2,1)S(1)}, bf16[16,128]{1,0:T(8,128)(2,1)S(1)}, u32[]{:S(2)}, u32[]{:S(2)}) collective-permute-start(bf16[16,128]{1,0:T(8,128)(2,1)S(1)} %slice_bitcast_fusion.8), channel_id=1, source_target_pairs={{0,8},{4,12},{8,0},{12,4},{1,9},{5,13},{9,1},{13,5},{2,10},{6,14},... | collective-permute-start | bytes 12296 | tf_op jit(solution)/shard_map/ppermute | solution.py:201
  214.7 3.2 %collective-permute-start.38 = (bf16[16,128]{1,0:T(8,128)(2,1)S(1)}, bf16[16,128]{1,0:T(8,128)(2,1)S(1)}, u32[]{:S(2)}, u32[]{:S(2)}) collective-permute-start(bf16[16,128]{1,0:T(8,128)(2,1)S(1)} %slice_bitcast_fusion.8), channel_id=1, source_target_pairs={{0,12},{4,8},{8,4},{12,0},{1,13},{5,9},{9,5},{13,1},{2,14},{6,10},... | collective-permute-start | bytes 12296 | tf_op jit(solution)/shard_map/ppermute | solution.py:201
  216.5 1.4 collective-permute-start.35

commit v11 on v10

--- a/solution.py
+++ b/solution.py
@@ -40,6 +40,7 @@
 
 SMALL = pl.CostEstimate(flops=1, bytes_accessed=1, transcendentals=0)
 SOME = pl.CostEstimate(flops=2 * 10**9, bytes_accessed=2**20, transcendentals=0)
+MORE = pl.CostEstimate(flops=5 * 10**9, bytes_accessed=2**20, transcendentals=0)
 PARAMS = pltpu.CompilerParams(vmem_limit_bytes=12 * 2**20)
 
 
@@ -105,7 +106,7 @@
         sent_out[:, columns] = jnp.where(first, high, low).astype(sent_out.dtype)
 
 
-def fold(flags, kept, got, sent_as):
+def fold(flags, kept, got, sent_as, cost):
     shape = (kept.shape[0] // 2, kept.shape[1])
     return pl.pallas_call(
         fold_body,
@@ -113,7 +114,7 @@
         out_specs=[VMEM, VMEM],
         out_shape=[jax.ShapeDtypeStruct(shape, F32), jax.ShapeDtypeStruct(shape, sent_as)],
         compiler_params=PARAMS,
-        cost_estimate=SMALL,
+        cost_estimate=cost,
         name="fold",
     )(flags, kept, *got)
 
@@ -124,65 +125,66 @@
     return high, (value - high.astype(F32)).astype(BF16)
 
 
-def scores_body(units, *refs):
-    sums, grads, outs = refs[: 2 * units], refs[2 * units :][:4], refs[2 * units + 4 :]
+def scores_body(places, units, *refs):
+    sums, grads, outs = refs[: 2 * units], refs[2 * units :][: len(places)], refs[-units:]
     rows = sums[0].shape[0]
     precond = jnp.concatenate(
         [part for u in range(units) for part in split_sum(sums[2 * u], sums[2 * u + 1])]
     )
-    for r in range(4):
-        both = dot_t(grads[r][...], precond)
+    for grad, (r, first) in zip(grads, places):
+        both = dot_t(grad[...], precond)
         for u in range(units):
             value = both[:, 2 * u * rows :][:, :rows] + both[:, (2 * u + 1) * rows :][:, :rows]
-            outs[u][r] = value.astype(outs[u].dtype)
+            outs[u][r, first : first + grad.shape[0]] = value.astype(outs[u].dtype)
 
 
 def partial_scores(units, grads, out_as, cost):
     rows = units[0][0].shape[0]
-    train_rows = grads[0].shape[0]
+    train_rows = grads[0][2].shape[0]
     return pl.pallas_call(
-        lambda *refs: scores_body(len(units), *refs),
-        in_specs=[VMEM] * (2 * len(units) + 4),
+        functools.partial(scores_body, [piece[:2] for piece in grads], len(units)),
+        in_specs=[VMEM] * (2 * len(units) + len(grads)),
         out_specs=[VMEM] * len(units),
         out_shape=[jax.ShapeDtypeStruct((4, train_rows, rows), kind) for kind in out_as],
         compiler_params=PARAMS,
         cost_estimate=cost,
         name="scores",
-    )(*[value for unit in units for value in unit], *grads)
-
-
-def last_scores_body(which, kept, got, counts, before, *refs):
-    grads, out, chosen_out = refs[: len(which)], refs[-2], refs[-1]
+    )(*[value for unit in units for value in unit], *[piece[2] for piece in grads])
+
+
+def last_scores_body(places, kept, got, counts, before, *refs):
+    grads, out, chosen_out = refs[: len(places)], refs[-2], refs[-1]
     rows = kept.shape[0]
-    train_rows = grads[0].shape[0]
+    low = places[0][0]
+    train_rows = counts.shape[1]
     precond = jnp.concatenate(split_sum(kept, got))
     chosen = before[:1]
-    for n, r in enumerate(which):
-        both = dot_t(grads[n][...], precond)
+    for grad, (r, first) in zip(grads, places):
+        both = dot_t(grad[...], precond)
         value = both[:, :rows] + both[:, rows:]
-        out[n, :train_rows] = value.astype(BF16)
-        chosen = chosen + jnp.sum(value * counts[r], axis=0, keepdims=True)
+        place = pl.ds(first, grad.shape[0])
+        out[r - low, place] = value.astype(BF16)
+        chosen = chosen + jnp.sum(value * counts[r, place], axis=0, keepdims=True)
     chosen_out[...] = jnp.broadcast_to(chosen, chosen_out.shape)
-    for n in range(len(which)):
+    for n in range(2):
         if out.shape[1] > train_rows:
             out[n, train_rows:] = jnp.broadcast_to(chosen, (EXTRA, rows)).astype(BF16)
 
 
-def last_scores(kept, got, counts, before, grads, which, extra):
+def last_scores(kept, got, counts, before, grads, extra):
     rows = kept.shape[0]
-    train_rows = grads[0].shape[0]
     return pl.pallas_call(
-        functools.partial(last_scores_body, which),
-        in_specs=[VMEM] * (4 + len(which)),
+        functools.partial(last_scores_body, [piece[:2] for piece in grads]),
+        in_specs=[VMEM] * (4 + len(grads)),
         out_specs=[VMEM, VMEM],
         out_shape=[
-            jax.ShapeDtypeStruct((len(which), train_rows + extra, rows), BF16),
+            jax.ShapeDtypeStruct((2, counts.shape[1] + extra, rows), BF16),
             jax.ShapeDtypeStruct((8, rows), F32),
         ],
         compiler_params=PARAMS,
         cost_estimate=SMALL,
         name="last_scores",
-    )(kept, got, counts, before, *[grads[r] for r in which])
+    )(kept, got, counts, before, *[piece[2] for piece in grads])
 
 
 def four_by_four(train_grads, test_grads, fisher, chosen_ids):
@@ -208,11 +210,12 @@
     outward = [(1, 0), (2, 3)]
     inward = [(0, 1), (3, 2)]
 
-    def core_sum(kept, *sent, sent_as=BF16):
-        return fold(flags, kept, [to_other(part, 1) for part in sent], sent_as)
+    def core_sum(kept, *sent, sent_as=BF16, cost=SMALL):
+        return fold(flags, kept, [to_other(part, 1) for part in sent], sent_as, cost)
 
     def scores_of(*units, out_as=(BF16, BF16), cost=SMALL):
-        return partial_scores(units, grads, out_as[: len(units)], cost)
+        pieces = [(*place, grad) for place, grad in zip(places, grads)]
+        return partial_scores(units, pieces, out_as[: len(units)], cost)
 
     def in_order(parts):
         parts = [parts[0], parts[2], parts[1], parts[3]]
@@ -228,19 +231,23 @@
 
     pair_in = along(test_grads, pair)
     middle_in = along(test_grads, middle)
-    grads = [train_grads, to_other(train_grads, 1), to_other(train_grads, 2)]
-    own, own_sent = core_sum(*product(flags, [test_grads], fisher), sent_as=F32)
+    other_core, other_chip = to_other(train_grads, 1), to_other(train_grads, 2)
+    own, other_core = tied(test_grads, other_core)
+    own, own_sent = core_sum(*product(flags, [own], fisher), sent_as=F32, cost=MORE)
     counts = selected(chosen_ids)
-    pair_in, middle_in, own, own_sent, counts, chosen_ids, grads[1] = tied(
-        pair_in, middle_in, own, own_sent, counts, chosen_ids, grads[1]
-    )
+    half = own_rows // 2
+    other_both = [to_other(other_chip[:half], 1), to_other(other_chip[half:], 1)]
+    grads = [train_grads, other_core, other_chip, *other_both]
+    pair_in, middle_in, own, own_sent, counts, chosen_ids, grads = tied(
+        pair_in, middle_in, own, own_sent, counts, chosen_ids, grads
+    )
+    places = ((0, 0), (1, 0), (2, 0), (3, 0), (3, half))
 
     second_edge = along(middle_in, outward)
     far_in = along(pair_in, middle)
-    grads = grads + [to_other(grads[2], 1)]
     near, near_sent = core_sum(*product(flags, [middle_in, pair_in], fisher))
     own_got = to_other(own_sent, 2)
-    near_sent, own_got, pair_in, grads[3] = tied(near_sent, own_got, pair_in, grads[3])
+    near_sent, own_got, pair_in = tied(near_sent, own_got, pair_in)
     near_got = to_other(near_sent, 2)
     third, third_sent = core_sum(*product(flags, [pair_in], fisher))
     (near,) = scores_of((near, near_got), cost=SOME)
@@ -271,10 +278,11 @@
     last_got = to_other(last_sent, 2)
     ends = [(0, 3), (3, 0)]
     none = jnp.zeros((8, quarter), F32)
-    away, chosen = last_scores(last, last_got, far_counts, none, grads, (2, 3), 0)
+    pieces = [(*place, grad) for place, grad in zip(places, grads)]
+    away, chosen = last_scores(last, last_got, far_counts, none, pieces[2:], 0)
     away = along(away, ends)
     away = [to_other(away[0], 2), to_other(away[1], 3)]
-    here, _ = last_scores(last, last_got, far_counts, chosen, grads, (0, 1), EXTRA)
+    here, _ = last_scores(last, last_got, far_counts, chosen, pieces[:2], EXTRA)
     here, second, third = tied(here, second, third)
     here = along(here, ends)
     here = [here[0], to_other(here[1], 1)]

time: 221 us -> 212 us (0.959)
  local copies, waits for them, and re-layouts: 11.5 us -> 5.94 us
  waiting for transfers between devices: 95.2 us -> 91.5 us
    unnamed x16 -> x12, local copies, waits for them, and re-layouts: 11.3 us -> 4.98 us
    ppermute x26 -> x27, waiting for transfers between devices: 85.1 us -> 79.2 us  [to_other(): return lax.ppermute(value, 'train', [(k, k ^ r) for k in range(4)])]
    ppermute x26 -> x27, starting transfers between devices: 19.7 us -> 19.7 us  [to_other(): return lax.ppermute(value, 'train', [(k, k ^ r) for k in range(4)])]
  transfers between devices with their start and end apart: 39 -> 40, of which waited for: 20 -> 22; matrix products, arithmetic and copies ran while one was open for 2% -> 3% of each run, Pallas kernels for 22% -> 22%
where the time goes in v11:
time: 212 us; the launch traced here: 211 us
  waiting for transfers between devices  91.5 us (43%)
  Pallas kernels  53.9 us (25%)
  starting transfers between devices  52.9 us (25%)
  other arithmetic  6.08 us (3%)
  local copies, waits for them, and re-layouts  5.94 us (3%)
    ppermute x27, waiting for transfers between devices, to_other(): return lax.ppermute(value, 'train', [(k, k ^ r) for k in range(4)])  79.2 us
    ppermute x13, starting transfers between devices, along(): return lax.ppermute(value, 'test', pairs)  33.3 us
    pallas_call x5, Pallas kernels, product(): pl.pallas_call(functools.partial(product_body, len(blocks)), in_specs=[pl...  30.8 us
    ppermute x27, starting transfers between devices, to_other(): return lax.ppermute(value, 'train', [(k, k ^ r) for k in range(4)])  19.7 us
    pallas_call x3, Pallas kernels, partial_scores(): pl.pallas_call(functools.partial(scores_body, [piece[:2] for piece in gra...  14.1 us
    ppermute x13, waiting for transfers between devices, along(): return lax.ppermute(value, 'test', pairs)  12.3 us
    unnamed x12, local copies, waits for them, and re-layouts  4.98 us
    pallas_call x2, Pallas kernels, last_scores(): pl.pallas_call(functools.partial(last_scores_body, [piece[:2] for piece i...  4.82 us
  transfers between devices with their start and end apart: 40, of which 22 were waited for; matrix products, arithmetic and copies ran while one was open for 3% of the time, Pallas kernels for 22%

profile of v11, /device:TPU:0, one launch (start us, length us, event | category | flops | bytes accessed | tf_op | source)
XLA Modules:
  0.0 211.4 jit_solution(12048958160836066988)
XLA Ops:
  1.1 2.6 %collective-permute-start.5 = (bf16[512,2048]{1,0:T(8,128)(2,1)}, bf16[512,2048]{1,0:T(8,128)(2,1)S(1)}, u32[]{:S(2)}, u32[]{:S(2)}) collective-permute-start(bf16[512,2048]{1,0:T(8,128)(2,1)} %refs_0_.1), channel_id=1, source_target_pairs={{0,8},{4,12},{8,0},{12,4},{1,9},{5,13},{9,1},{13,5},{2,10},{6,14},... | collective-permute-start | bytes 6291464 | tf_op jit(solution)/shard_map/ppermute | solution.py:203
  3.7 1.6 collective-permute-start
  5.3 2.0 collective-permute-start.1
  7.4 0.7 dynamic-slice_bitcast_fusion.1
  8.1 3.4 %copy-done = bf16[2048,2048]{1,0:T(8,128)(2,1)S(1)} copy-done((bf16[2048,2048]{1,0:T(8,128)(2,1)S(1)}, bf16[2048,2048]{1,0:T(8,128)(2,1)}, u32[]{:S(2)}) %copy-start) | copy-done | bytes 8388632
  11.5 1.6 copy-done.2
  13.1 5.6 %product.5 = (f32[256,2048]{1,0:T(8,128)S(1)}, bf16[128,2048]{1,0:T(8,128)(2,1)S(1)}, bf16[128,2048]{1,0:T(8,128)(2,1)S(1)}) custom-call(s32[3]{0:T(128)S(1)} %pad_add_fusion.flags, bf16[512,2048]{1,0:T(8,128)(2,1)S(1)} %copy-done.2, bf16[2048,2048]{1,0:T(8,128)(2,1)S(1)} %copy-done), custom_call_target="tpu_custom_call" | custom-call | flops 1 | bytes 1 | tf_op jit(solution)/shard_map/product/pallas_call | solution.py:80
  18.8 31.4 %collective-permute-done.5.refs_4_.refs_6_.refs_0_ = bf16[512,2048]{1,0:T(8,128)(2,1)S(1)} collective-permute-done((bf16[512,2048]{1,0:T(8,128)(2,1)}, bf16[512,2048]{1,0:T(8,128)(2,1)S(1)}, u32[]{:S(2)}, u32[]{:S(2)}) %collective-permute-start.5) | collective-permute-done | bytes 2097184 | tf_op jit(solution)/shard_map/ppermute | solution.py:203
  51.1 1.7 convert_add_fusion.1
  52.8 2.5 %collective-permute-done.4.refs_1_ = bf16[128,2048]{1,0:T(8,128)(2,1)S(1)} collective-permute-done((bf16[128,2048]{1,0:T(8,128)(2,1)S(1)}, bf16[128,2048]{1,0:T(8,128)(2,1)S(1)}, u32[]{:S(2)}, u32[]{:S(2)}) %collective-permute-start.4) | collective-permute-done | bytes 524320 | tf_op jit(solution)/shard_map/ppermute | solution.py:203
  55.3 0.8 fold.5
  56.1 0.9 collective-permute-start.8
  57.1 1.4 collective-permute-start.9
  58.5 1.8 collective-permute-start.12
  60.3 7.3 %product.6 = (f32[256,2048]{1,0:T(8,128)S(1)}, bf16[128,2048]{1,0:T(8,128)(2,1)S(1)}, bf16[128,2048]{1,0:T(8,128)(2,1)S(1)}) custom-call(s32[3]{0:T(128)S(1)} %pad_add_fusion.flags, bf16[512,2048]{1,0:T(8,128)(2,1)} %collective-permute-done.1.refs_0_, bf16[512,2048]{1,0:T(8,128)(2,1)} %collective-permute-done.refs_1_.refs_0_, bf16[2048,2048]{1,0:T(8,128)(2,1)S(1)} %bitcast.115), custom_call_target="tpu_custom_call" | custom-call | flops 1 | bytes 1 | tf_op jit(solution)/shard_map/product/pallas_call | solution.py:80
  68.3 1.4 collective-permute-done.10.refs_0_
  69.7 0.7 collective-permute-done.11.refs_1_
  70.4 0.8 fold.6
  71.2 12.6 %collective-permute-done.12.refs_3_ = f32[128,2048]{1,0:T(8,128)S(1)} collective-permute-done((f32[128,2048]{1,0:T(8,128)S(1)}, f32[128,2048]{1,0:T(8,128)S(1)}, u32[]{:S(2)}, u32[]{:S(2)}) %collective-permute-start.12) | collective-permute-done | bytes 1048608 | tf_op jit(solution)/shard_map/ppermute | solution.py:203
  83.8 1.7 collective-permute-start.15
  85.5 6.7 %product.7 = (f32[256,2048]{1,0:T(8,128)S(1)}, bf16[128,2048]{1,0:T(8,128)(2,1)S(1)}, bf16[128,2048]{1,0:T(8,128)(2,1)S(1)}) custom-call(s32[3]{0:T(128)S(1)} %pad_add_fusion.flags, bf16[512,2048]{1,0:T(8,128)(2,1)} %collective-permute-done.refs_1_.refs_0_, bf16[2048,2048]{1,0:T(8,128)(2,1)S(1)} %bitcast.115), custom_call_target="tpu_custom_call" | custom-call | flops 1 | bytes 1 | tf_op jit(solution)/shard_map/product/pallas_call | solution.py:80
  92.8 4.1 %collective-permute-done.15.refs_1_ = bf16[128,2048]{1,0:T(8,128)(2,1)S(1)} collective-permute-done((bf16[128,2048]{1,0:T(8,128)(2,1)S(1)}, bf16[128,2048]{1,0:T(8,128)(2,1)S(1)}, u32[]{:S(2)}, u32[]{:S(2)}) %collective-permute-start.15) | collective-permute-done | bytes 524320 | tf_op jit(solution)/shard_map/ppermute | solution.py:203
  97.0 5.7 %collective-permute-start.16 = (s32[512,16]{0,1:T(8,128)S(1)}, s32[512,16]{0,1:T(8,128)S(1)}, u32[]{:S(2)}, u32[]{:S(2)}) collective-permute-start(s32[512,16]{0,1:T(8,128)S(1)} %copy-done.3), channel_id=1, source_target_pairs={{0,3},{3,0},{4,7},{7,4},{8,11},{11,8},{12,15},{15,12},{16,19},{19,... | collective-permute-start | bytes 98312 | tf_op jit(solution)/shard_map/ppermute | solution.py:200
  102.7 4.0 %scores.3 = bf16[4,512,128]{2,1,0:T(8,128)(2,1)S(1)} custom-call(f32[128,2048]{1,0:T(8,128)S(1)} %get-tuple-element.105.refs_0_, bf16[128,2048]{1,0:T(8,128)(2,1)S(1)} %collective-permute-done.15.refs_1_, bf16[512,2048]{1,0:T(8,128)(2,1)S(1)} %copy-done.1, bf16[512,2048]{1,0:T(8,128)(2,1)} %collective-permute-done.2.refs_3_.refs_5_.refs_1_, ...), custom_call_target="tpu_custom_call" | custom-call | flops 2000000000 | bytes 1048576 | tf_op jit(solution)/shard_map/scores/pallas_call | solution.py:144
  106.7 0.8 fold.7
  107.6 2.0 collective-permute-done.9.refs_1_
  109.6 1.3 collective-permute-start.17
  110.9 5.6 %product.8 = (f32[256,2048]{1,0:T(8,128)S(1)}, bf16[128,2048]{1,0:T(8,128)(2,1)S(1)}, bf16[128,2048]{1,0:T(8,128)(2,1)S(1)}) custom-call(s32[3]{0:T(128)S(1)} %pad_add_fusion.flags, bf16[512,2048]{1,0:T(8,128)(2,1)S(1)} %collective-permute-done.8.refs_0_, bf16[512,2048]{1,0:T(8,128)(2,1)S(1)} %collective-permute-done.9.refs_1_, bf16[2048,2048]{1,0:T(8,128)(2,1)S(1)} %bitcast.115), custom_call_target="tpu_custom_call" | custom-call | flops 1 | bytes 1 | tf_op jit(solution)/shard_map/product/pallas_call | solution.py:80
  117.0 1.4 collective-permute-done.19.refs_0_
  118.4 0.7 collective-permute-done.20.refs_1_
  119.2 0.8 fold.8
  120.0 1.6 collective-permute-start.21
  121.6 4.7 %collective-permute-start.22 = (bf16[4,512,128]{2,1,0:T(8,128)(2,1)S(1)}, bf16[4,512,128]{2,1,0:T(8,128)(2,1)S(1)}, u32[]{:S(2)}, u32[]{:S(2)}) collective-permute-start(bf16[4,512,128]{2,1,0:T(8,128)(2,1)S(1)} %scores.3), channel_id=1, source_target_pairs={{0,1},{3,2},{4,5},{7,6},{8,9},{11,10},{12,13},{15,14},{16,17},{19,... | collective-permute-start | bytes 1572872 | tf_op jit(solution)/shard_map/ppermute | solution.py:200
  126.3 0.9 collective-permute-start.23
  127.8 7.1 %collective-permute-done.21.refs_1_ = bf16[128,2048]{1,0:T(8,128)(2,1)S(1)} collective-permute-done((bf16[128,2048]{1,0:T(8,128)(2,1)S(1)}, bf16[128,2048]{1,0:T(8,128)(2,1)S(1)}, u32[]{:S(2)}, u32[]{:S(2)}) %collective-permute-start.21) | collective-permute-done | bytes 524320 | tf_op jit(solution)/shard_map/ppermute | solution.py:203
  134.8 2.6 %collective-permute-done.22 = bf16[4,512,128]{2,1,0:T(8,128)(2,1)S(1)} collective-permute-done((bf16[4,512,128]{2,1,0:T(8,128)(2,1)S(1)}, bf16[4,512,128]{2,1,0:T(8,128)(2,1)S(1)}, u32[]{:S(2)}, u32[]{:S(2)}) %collective-permute-start.22) | collective-permute-done | bytes 524320 | tf_op jit(solution)/shard_map/ppermute | solution.py:200
  137.4 4.0 %scores.5 = bf16[4,512,128]{2,1,0:T(8,128)(2,1)S(1)} custom-call(f32[128,2048]{1,0:T(8,128)S(1)} %get-tuple-element.135.refs_0_, bf16[128,2048]{1,0:T(8,128)(2,1)S(1)} %collective-permute-done.21.refs_1_, bf16[512,2048]{1,0:T(8,128)(2,1)S(1)} %copy-done.1, bf16[512,2048]{1,0:T(8,128)(2,1)} %collective-permute-done.2.refs_3_.refs_5_.refs_1_, ...), custom_call_target="tpu_custom_call" | custom-call | flops 1 | bytes 1 | tf_op jit(solution)/shard_map/scores/pallas_call | solution.py:144
  141.4 0.7 collective-permute-start.24
  142.1 1.7 convert_add_fusion.counts
  143.8 1.5 collective-permute-done.18.refs_1_
  145.3 6.2 %scores.4 = (f32[4,512,128]{2,1,0:T(8,128)S(1)}, f32[4,512,128]{2,1,0:T(8,128)S(1)}) custom-call(f32[128,2048]{1,0:T(8,128)S(1)} %get-tuple-element.114.refs_0_, bf16[128,2048]{1,0:T(8,128)(2,1)S(1)} %collective-permute-done.18.refs_1_, f32[128,2048]{1,0:T(8,128)S(1)} %get-tuple-element.116.refs_2_, f32[128,2048]{1,0:T(8,128)S(1)} %collective-permute-done.12.refs_3_, ...), custom_call_target="tpu_custom_call" | custom-call | flops 1 | bytes 1 | tf_op jit(solution)/shard_map/scores/pallas_call | solution.py:144
  151.5 6.8 %collective-permute-done.17.refs_0_ = bf16[512,2048]{1,0:T(8,128)(2,1)S(1)} collective-permute-done((bf16[512,2048]{1,0:T(8,128)(2,1)S(1)}, bf16[512,2048]{1,0:T(8,128)(2,1)S(1)}, u32[]{:S(2)}, u32[]{:S(2)}) %collective-permute-start.17) | collective-permute-done | bytes 2097184 | tf_op jit(solution)/shard_map/ppermute | solution.py:200
  158.3 5.6 %product.9 = (f32[256,2048]{1,0:T(8,128)S(1)}, bf16[128,2048]{1,0:T(8,128)(2,1)S(1)}, bf16[128,2048]{1,0:T(8,128)(2,1)S(1)}) custom-call(s32[3]{0:T(128)S(1)} %pad_add_fusion.flags, bf16[512,2048]{1,0:T(8,128)(2,1)S(1)} %collective-permute-done.17.refs_0_, bf16[2048,2048]{1,0:T(8,128)(2,1)S(1)} %bitcast.115), custom_call_target="tpu_custom_call" | custom-call | flops 1 | bytes 1 | tf_op jit(solution)/shard_map/product/pallas_call | solution.py:80
  164.5 1.4 collective-permute-done.25.refs_0_
  165.9 0.7 collective-permute-done.26.refs_1_
  166.6 0.8 fold.9
  167.5 1.6 collective-permute-start.27
  169.1 1.3 collective-permute-start.29
  170.4 5.1 %collective-permute-start.28 = (bf16[4,512,128]{2,1,0:T(8,128)(2,1)S(1)}, bf16[4,512,128]{2,1,0:T(8,128)(2,1)S(1)}, u32[]{:S(2)}, u32[]{:S(2)}) collective-permute-start(bf16[4,512,128]{2,1,0:T(8,128)(2,1)S(1)} %scores.5), channel_id=1, source_target_pairs={{0,2},{3,1},{4,6},{7,5},{8,10},{11,9},{12,14},{15,13},{16,18},{19,... | collective-permute-start | bytes 1572872 | tf_op jit(solution)/shard_map/ppermute | solution.py:200
  175.6 5.9 %collective-permute-done.27.got = bf16[128,2048]{1,0:T(8,128)(2,1)S(1)} collective-permute-done((bf16[128,2048]{1,0:T(8,128)(2,1)S(1)}, bf16[128,2048]{1,0:T(8,128)(2,1)S(1)}, u32[]{:S(2)}, u32[]{:S(2)}) %collective-permute-start.27) | collective-permute-done | bytes 524320 | tf_op jit(solution)/shard_map/ppermute | solution.py:203
  181.5 1.3 last_scores.2
  182.8 3.5 %last_scores.3 = (bf16[2,528,128]{2,1,0:T(8,128)(2,1)S(1)}, f32[8,128]{1,0:T(8,128)}) custom-call(f32[128,2048]{1,0:T(8,128)S(1)} %get-tuple-element.146.kept, bf16[128,2048]{1,0:T(8,128)(2,1)S(1)} %collective-permute-done.27.got, f32[4,512,128]{2,1,0:T(8,128)S(1)} %convert_add_fusion.counts, f32[8,128]{1,0:T(8,128)S(1)} %get-tuple-element.152.before, ...), custom_call_target="tpu_custom_call" | custom-call | flops 1 | bytes 1 | tf_op jit(solution)/shard_map/last_scores/pallas_call | solution.py:176
  186.4 3.8 %collective-permute-start.34 = (bf16[2,512,128]{2,1,0:T(8,128)(2,1)S(1)}, bf16[2,512,128]{2,1,0:T(8,128)(2,1)S(1)}, u32[]{:S(2)}, u32[]{:S(2)}) collective-permute-start(bf16[2,512,128]{2,1,0:T(8,128)(2,1)S(1)} %get-tuple-element.163), channel_id=1, source_target_pairs={{0,3},{3,0},{4,7},{7,4},{8,11},{11,8},{12,15},{15,12},{16,19},{19,... | collective-permute-start | bytes 786440 | tf_op jit(solution)/shard_map/ppermute | solution.py:200
  190.8 1.6 collective-permute-start.30
  192.3 0.6 collective-permute-start.32
  193.0 3.8 %collective-permute-start.33 = (bf16[2,528,128]{2,1,0:T(8,128)(2,1)S(1)}, bf16[2,528,128]{2,1,0:T(8,128)(2,1)S(1)}, u32[]{:S(2)}, u32[]{:S(2)}) collective-permute-start(bf16[2,528,128]{2,1,0:T(8,128)(2,1)S(1)} %get-tuple-element.162), channel_id=1, source_target_pairs={{0,3},{3,0},{4,7},{7,4},{8,11},{11,8},{12,15},{15,12},{16,19},{19,... | collective-permute-start | bytes 811016 | tf_op jit(solution)/shard_map/ppermute | solution.py:200
  196.8 0.7 collective-permute-done.34
  197.5 1.6 collective-permute-start.35
  199.1 1.1 collective-permute-done.30
  200.2 4.7 %collective-permute-done.32 = f32[520,128]{1,0:T(8,128)S(1)} collective-permute-done((f32[520,128]{1,0:T(8,128)S(1)}, f32[520,128]{1,0:T(8,128)S(1)}, u32[]{:S(2)}, u32[]{:S(2)}) %collective-permute-start.32) | collective-permute-done | bytes 266272 | tf_op jit(solution)/shard_map/ppermute | solution.py:203
  205.0 1.5 collective-permute-start.38
  206.5 1.0 collective-permute-start.39
  207.7 1.9 collective-permute-done.38
  210.3 1.1 slice_add_fusion
  (69 shorter events, 6.3 us)
Async XLA Ops:
  0.6 7.5 %collective-permute-start.2 = (bf16[512,2048]{1,0:T(8,128)(2,1)}, bf16[512,2048]{1,0:T(8,128)(2,1)}, u32[]{:S(2)}, u32[]{:S(2)}) collective-permute-start(bf16[512,2048]{1,0:T(8,128)(2,1)} %refs_0_.1), channel_id=1, source_target_pairs={{0,4},{4,0},{8,12},{12,8},{1,5},{5,1},{9,13},{13,9},{2,6},{6,2},{1... | collective-permute-start | bytes 6291464 | tf_op jit(solution)/shard_map/ppermute | solution.py:203
  1.1 49.0 %collective-permute-start.5 = (bf16[512,2048]{1,0:T(8,128)(2,1)}, bf16[512,2048]{1,0:T(8,128)(2,1)S(1)}, u32[]{:S(2)}, u32[]{:S(2)}) collective-permute-start(bf16[512,2048]{1,0:T(8,128)(2,1)} %refs_0_.1), channel_id=1, source_target_pairs={{0,8},{4,12},{8,0},{12,4},{1,9},{5,13},{9,1},{13,5},{2,10},{6,14},... | collective-permute-start | bytes 6291464 | tf_op jit(solution)/shard_map/ppermute | solution.py:203
  3.7 52.4 %collective-permute-start = (bf16[512,2048]{1,0:T(8,128)(2,1)}, bf16[512,2048]{1,0:T(8,128)(2,1)}, u32[]{:S(2)}, u32[]{:S(2)}) collective-permute-start(bf16[512,2048]{1,0:T(8,128)(2,1)} %refs_0_), channel_id=1, source_target_pairs={{0,1},{1,0},{2,3},{3,2},{4,5},{5,4},{6,7},{7,6},{8,9},{9,8},{10,11... | collective-permute-start | bytes 6291464 | tf_op jit(solution)/shard_map/ppermute | solution.py:200
  5.3 50.8 %collective-permute-start.1 = (bf16[512,2048]{1,0:T(8,128)(2,1)}, bf16[512,2048]{1,0:T(8,128)(2,1)}, u32[]{:S(2)}, u32[]{:S(2)}) collective-permute-start(bf16[512,2048]{1,0:T(8,128)(2,1)} %refs_0_), channel_id=1, source_target_pairs={{1,2},{2,1},{5,6},{6,5},{9,10},{10,9},{13,14},{14,13},{17,18},{18,... | collective-permute-start | bytes 6291464 | tf_op jit(solution)/shard_map/ppermute | solution.py:200
  8.1 3.4 %copy-start = (bf16[2048,2048]{1,0:T(8,128)(2,1)S(1)}, bf16[2048,2048]{1,0:T(8,128)(2,1)}, u32[]{:S(2)}) copy-start(bf16[2048,2048]{1,0:T(8,128)(2,1)} %refs_1_.5) | copy-start | bytes 25165828
  11.5 1.6 copy-start.2
  18.7 32.3 %collective-permute-start.3 = (bf16[128,2048]{1,0:T(8,128)(2,1)S(1)}, bf16[128,2048]{1,0:T(8,128)(2,1)S(1)}, u32[]{:S(2)}, u32[]{:S(2)}) collective-permute-start(bf16[128,2048]{1,0:T(8,128)(2,1)S(1)} %get-tuple-element.85), channel_id=1, source_target_pairs={{0,4},{4,0},{8,12},{12,8},{1,5},{5,1},{9,13},{13,9},{2,6},{6,2},{1... | collective-permute-start | bytes 1572872 | tf_op jit(solution)/shard_map/ppermute | solution.py:203
  50.3 5.8 %collective-permute-start.6 = (bf16[256,2048]{1,0:T(8,128)(2,1)S(1)}, bf16[256,2048]{1,0:T(8,128)(2,1)S(1)}, u32[]{:S(2)}, u32[]{:S(2)}) collective-permute-start(bf16[256,2048]{1,0:T(8,128)(2,1)S(1)} %get-tuple-element.167), channel_id=1, source_target_pairs={{0,4},{4,0},{8,12},{12,8},{1,5},{5,1},{9,13},{13,9},{2,6},{6,2},{1... | collective-permute-start | bytes 3145736 | tf_op jit(solution)/shard_map/ppermute | solution.py:203
  50.4 5.8 %collective-permute-start.7 = (bf16[256,2048]{1,0:T(8,128)(2,1)S(1)}, bf16[256,2048]{1,0:T(8,128)(2,1)S(1)}, u32[]{:S(2)}, u32[]{:S(2)}) collective-permute-start(bf16[256,2048]{1,0:T(8,128)(2,1)S(1)} %get-tuple-element.166), channel_id=1, source_target_pairs={{0,4},{4,0},{8,12},{12,8},{1,5},{5,1},{9,13},{13,9},{2,6},{6,2},{1... | collective-permute-start | bytes 3145736 | tf_op jit(solution)/shard_map/ppermute | solution.py:203
  50.9 4.3 %collective-permute-start.4 = (bf16[128,2048]{1,0:T(8,128)(2,1)S(1)}, bf16[128,2048]{1,0:T(8,128)(2,1)S(1)}, u32[]{:S(2)}, u32[]{:S(2)}) collective-permute-start(bf16[128,2048]{1,0:T(8,128)(2,1)S(1)} %get-tuple-element.86), channel_id=1, source_target_pairs={{0,4},{4,0},{8,12},{12,8},{1,5},{5,1},{9,13},{13,9},{2,6},{6,2},{1... | collective-permute-start | bytes 1572872 | tf_op jit(solution)/shard_map/ppermute | solution.py:203
  55.3 5.1 %slice-start = ((s8[8388608]{0:T(1024)(128)(4,1)}), s8[4194304]{0:T(1024)(128)(4,1)S(1)}, s32[]{:S(2)}) async-start(s8[8388608]{0:T(1024)(128)(4,1)} %bitcast.114), calls=%async_computation | async-start | bytes 8388608
  55.3 5.1 %slice-start.1 = ((s8[8388608]{0:T(1024)(128)(4,1)}), s8[4194304]{0:T(1024)(128)(4,1)S(1)}, s32[]{:S(2)}) async-start(s8[8388608]{0:T(1024)(128)(4,1)} %bitcast.114), calls=%async_computation.1 | async-start | bytes 8388608
  56.1 51.4 %collective-permute-start.8 = (bf16[512,2048]{1,0:T(8,128)(2,1)}, bf16[512,2048]{1,0:T(8,128)(2,1)S(1)}, u32[]{:S(2)}, u32[]{:S(2)}) collective-permute-start(bf16[512,2048]{1,0:T(8,128)(2,1)} %collective-permute-done.refs_1_.refs_0_), channel_id=1, source_target_pairs={{1,2},{2,1},{5,6},{6,5},{9,10},{10,9},{13,14},{14,13},{17,18},{18,... | collective-permute-start | bytes 6291464 | tf_op jit(solution)/shard_map/ppermute | solution.py:200
  57.1 52.5 %collective-permute-start.9 = (bf16[512,2048]{1,0:T(8,128)(2,1)}, bf16[512,2048]{1,0:T(8,128)(2,1)S(1)}, u32[]{:S(2)}, u32[]{:S(2)}) collective-permute-start(bf16[512,2048]{1,0:T(8,128)(2,1)} %collective-permute-done.1.refs_0_), channel_id=1, source_target_pairs={{1,0},{2,3},{5,4},{6,7},{9,8},{10,11},{13,12},{14,15},{17,16},{18,... | collective-permute-start | bytes 6291464 | tf_op jit(solution)/shard_map/ppermute | solution.py:200
  58.5 25.3 %collective-permute-start.12 = (f32[128,2048]{1,0:T(8,128)S(1)}, f32[128,2048]{1,0:T(8,128)S(1)}, u32[]{:S(2)}, u32[]{:S(2)}) collective-permute-start(f32[128,2048]{1,0:T(8,128)S(1)} %get-tuple-element.96), channel_id=1, source_target_pairs={{0,8},{4,12},{8,0},{12,4},{1,9},{5,13},{9,1},{13,5},{2,10},{6,14},... | collective-permute-start | bytes 3145736 | tf_op jit(solution)/shard_map/ppermute | solution.py:203
  67.7 2.0 collective-permute-start.10
  67.8 2.6 %collective-permute-start.11 = (bf16[128,2048]{1,0:T(8,128)(2,1)S(1)}, bf16[128,2048]{1,0:T(8,128)(2,1)S(1)}, u32[]{:S(2)}, u32[]{:S(2)}) collective-permute-start(bf16[128,2048]{1,0:T(8,128)(2,1)S(1)} %get-tuple-element.94), channel_id=1, source_target_pairs={{0,4},{4,0},{8,12},{12,8},{1,5},{5,1},{9,13},{13,9},{2,6},{6,2},{1... | collective-permute-start | bytes 1572872 | tf_op jit(solution)/shard_map/ppermute | solution.py:203
  83.8 13.2 %copy-start.3 = (s32[512,16]{0,1:T(8,128)S(1)}, s32[512,16]{0,1:T(8,128)}, u32[]{:S(2)}) copy-start(s32[512,16]{0,1:T(8,128)} %param.7) | copy-start | bytes 98308
  83.8 18.9 %copy-start.1 = (bf16[512,2048]{1,0:T(8,128)(2,1)S(1)}, bf16[512,2048]{1,0:T(8,128)(2,1)}, u32[]{:S(2)}) copy-start(bf16[512,2048]{1,0:T(8,128)(2,1)} %refs_0_.1) | copy-start | bytes 6291460
  83.8 13.2 %collective-permute-start.15 = (bf16[128,2048]{1,0:T(8,128)(2,1)S(1)}, bf16[128,2048]{1,0:T(8,128)(2,1)S(1)}, u32[]{:S(2)}, u32[]{:S(2)}) collective-permute-start(bf16[128,2048]{1,0:T(8,128)(2,1)S(1)} %get-tuple-element.106), channel_id=1, source_target_pairs={{0,8},{4,12},{8,0},{12,4},{1,9},{5,13},{9,1},{13,5},{2,10},{6,14},... | collective-permute-start | bytes 1572872 | tf_op jit(solution)/shard_map/ppermute | solution.py:203
  92.2 14.5 %collective-permute-start.13 = (bf16[128,2048]{1,0:T(8,128)(2,1)S(1)}, bf16[128,2048]{1,0:T(8,128)(2,1)S(1)}, u32[]{:S(2)}, u32[]{:S(2)}) collective-permute-start(bf16[128,2048]{1,0:T(8,128)(2,1)S(1)} %get-tuple-element.99), channel_id=1, source_target_pairs={{0,4},{4,0},{8,12},{12,8},{1,5},{5,1},{9,13},{13,9},{2,6},{6,2},{1... | collective-permute-start | bytes 1572872 | tf_op jit(solution)/shard_map/ppermute | solution.py:203
  92.3 14.4 %collective-permute-start.14 = (bf16[128,2048]{1,0:T(8,128)(2,1)S(1)}, bf16[128,2048]{1,0:T(8,128)(2,1)S(1)}, u32[]{:S(2)}, u32[]{:S(2)}) collective-permute-start(bf16[128,2048]{1,0:T(8,128)(2,1)S(1)} %get-tuple-element.100), channel_id=1, source_target_pairs={{0,4},{4,0},{8,12},{12,8},{1,5},{5,1},{9,13},{13,9},{2,6},{6,2},{1... | collective-permute-start | bytes 1572872 | tf_op jit(solution)/shard_map/ppermute | solution.py:203
  97.0 10.6 %collective-permute-start.16 = (s32[512,16]{0,1:T(8,128)S(1)}, s32[512,16]{0,1:T(8,128)S(1)}, u32[]{:S(2)}, u32[]{:S(2)}) collective-permute-start(s32[512,16]{0,1:T(8,128)S(1)} %copy-done.3), channel_id=1, source_target_pairs={{0,3},{3,0},{4,7},{7,4},{8,11},{11,8},{12,15},{15,12},{16,19},{19,... | collective-permute-start | bytes 98312 | tf_op jit(solution)/shard_map/ppermute | solution.py:200
  109.6 48.7 %collective-permute-start.17 = (bf16[512,2048]{1,0:T(8,128)(2,1)S(1)}, bf16[512,2048]{1,0:T(8,128)(2,1)S(1)}, u32[]{:S(2)}, u32[]{:S(2)}) collective-permute-start(bf16[512,2048]{1,0:T(8,128)(2,1)S(1)} %collective-permute-done.8.refs_0_), channel_id=1, source_target_pairs={{1,0},{2,3},{5,4},{6,7},{9,8},{10,11},{13,12},{14,15},{17,16},{18,... | collective-permute-start | bytes 6291464 | tf_op jit(solution)/shard_map/ppermute | solution.py:200
  116.5 2.0 collective-permute-start.19
  116.5 2.6 %collective-permute-start.20 = (bf16[128,2048]{1,0:T(8,128)(2,1)S(1)}, bf16[128,2048]{1,0:T(8,128)(2,1)S(1)}, u32[]{:S(2)}, u32[]{:S(2)}) collective-permute-start(bf16[128,2048]{1,0:T(8,128)(2,1)S(1)} %get-tuple-element.127), channel_id=1, source_target_pairs={{0,4},{4,0},{8,12},{12,8},{1,5},{5,1},{9,13},{13,9},{2,6},{6,2},{1... | collective-permute-start | bytes 1572872 | tf_op jit(solution)/shard_map/ppermute | solution.py:203
  120.0 14.8 %collective-permute-start.21 = (bf16[128,2048]{1,0:T(8,128)(2,1)S(1)}, bf16[128,2048]{1,0:T(8,128)(2,1)S(1)}, u32[]{:S(2)}, u32[]{:S(2)}) collective-permute-start(bf16[128,2048]{1,0:T(8,128)(2,1)S(1)} %get-tuple-element.131), channel_id=1, source_target_pairs={{0,8},{4,12},{8,0},{12,4},{1,9},{5,13},{9,1},{13,5},{2,10},{6,14},... | collective-permute-start | bytes 1572872 | tf_op jit(solution)/shard_map/ppermute | solution.py:203
  121.6 15.9 %collective-permute-start.22 = (bf16[4,512,128]{2,1,0:T(8,128)(2,1)S(1)}, bf16[4,512,128]{2,1,0:T(8,128)(2,1)S(1)}, u32[]{:S(2)}, u32[]{:S(2)}) collective-permute-start(bf16[4,512,128]{2,1,0:T(8,128)(2,1)S(1)} %scores.3), channel_id=1, source_target_pairs={{0,1},{3,2},{4,5},{7,6},{8,9},{11,10},{12,13},{15,14},{16,17},{19,... | collective-permute-start | bytes 1572872 | tf_op jit(solution)/shard_map/ppermute | solution.py:200
  126.3 11.2 %collective-permute-start.23 = (bf16[4,512,128]{2,1,0:T(8,128)(2,1)S(1)}, bf16[4,512,128]{2,1,0:T(8,128)(2,1)S(1)}, u32[]{:S(2)}, u32[]{:S(2)}) collective-permute-start(bf16[4,512,128]{2,1,0:T(8,128)(2,1)S(1)} %scores.3), channel_id=1, source_target_pairs={{1,2},{2,1},{5,6},{6,5},{9,10},{10,9},{13,14},{14,13},{17,18},{18,... | collective-permute-start | bytes 1572872 | tf_op jit(solution)/shard_map/ppermute | solution.py:200
  127.2 18.1 %collective-permute-start.18 = (bf16[128,2048]{1,0:T(8,128)(2,1)S(1)}, bf16[128,2048]{1,0:T(8,128)(2,1)S(1)}, u32[]{:S(2)}, u32[]{:S(2)}) collective-permute-start(bf16[128,2048]{1,0:T(8,128)(2,1)S(1)} %get-tuple-element.115), channel_id=1, source_target_pairs={{0,8},{4,12},{8,0},{12,4},{1,9},{5,13},{9,1},{13,5},{2,10},{6,14},... | collective-permute-start | bytes 1572872 | tf_op jit(solution)/shard_map/ppermute | solution.py:203
  141.4 10.1 %collective-permute-start.24 = (bf16[4,512,128]{2,1,0:T(8,128)(2,1)S(1)}, bf16[4,512,128]{2,1,0:T(8,128)(2,1)S(1)}, u32[]{:S(2)}, u32[]{:S(2)}) collective-permute-start(bf16[4,512,128]{2,1,0:T(8,128)(2,1)S(1)} %scores.5), channel_id=1, source_target_pairs={{1,2},{2,1},{5,6},{6,5},{9,10},{10,9},{13,14},{14,13},{17,18},{18,... | collective-permute-start | bytes 1572872 | tf_op jit(solution)/shard_map/ppermute | solution.py:200
  163.9 2.0 collective-permute-start.25
  164.0 2.6 %collective-permute-start.26 = (bf16[128,2048]{1,0:T(8,128)(2,1)S(1)}, bf16[128,2048]{1,0:T(8,128)(2,1)S(1)}, u32[]{:S(2)}, u32[]{:S(2)}) collective-permute-start(bf16[128,2048]{1,0:T(8,128)(2,1)S(1)} %get-tuple-element.145), channel_id=1, source_target_pairs={{0,4},{4,0},{8,12},{12,8},{1,5},{5,1},{9,13},{13,9},{2,6},{6,2},{1... | collective-permute-start | bytes 1572872 | tf_op jit(solution)/shard_map/ppermute | solution.py:203
  167.5 14.0 %collective-permute-start.27 = (bf16[128,2048]{1,0:T(8,128)(2,1)S(1)}, bf16[128,2048]{1,0:T(8,128)(2,1)S(1)}, u32[]{:S(2)}, u32[]{:S(2)}) collective-permute-start(bf16[128,2048]{1,0:T(8,128)(2,1)S(1)} %get-tuple-element.147), channel_id=1, source_target_pairs={{0,8},{4,12},{8,0},{12,4},{1,9},{5,13},{9,1},{13,5},{2,10},{6,14},... | collective-permute-start | bytes 1572872 | tf_op jit(solution)/shard_map/ppermute | solution.py:203
  169.1 17.2 %collective-permute-start.29 = (bf16[4,512,128]{2,1,0:T(8,128)(2,1)S(1)}, bf16[4,512,128]{2,1,0:T(8,128)(2,1)S(1)}, u32[]{:S(2)}, u32[]{:S(2)}) collective-permute-start(bf16[4,512,128]{2,1,0:T(8,128)(2,1)S(1)} %add_convert_fusion), channel_id=1, source_target_pairs={{1,0},{2,3},{5,4},{6,7},{9,8},{10,11},{13,12},{14,15},{17,16},{18,... | collective-permute-start | bytes 1572872 | tf_op jit(solution)/shard_map/ppermute | solution.py:200
  170.4 16.0 %collective-permute-start.28 = (bf16[4,512,128]{2,1,0:T(8,128)(2,1)S(1)}, bf16[4,512,128]{2,1,0:T(8,128)(2,1)S(1)}, u32[]{:S(2)}, u32[]{:S(2)}) collective-permute-start(bf16[4,512,128]{2,1,0:T(8,128)(2,1)S(1)} %scores.5), channel_id=1, source_target_pairs={{0,2},{3,1},{4,6},{7,5},{8,10},{11,9},{12,14},{15,13},{16,18},{19,... | collective-permute-start | bytes 1572872 | tf_op jit(solution)/shard_map/ppermute | solution.py:200
  186.4 11.1 %collective-permute-start.34 = (bf16[2,512,128]{2,1,0:T(8,128)(2,1)S(1)}, bf16[2,512,128]{2,1,0:T(8,128)(2,1)S(1)}, u32[]{:S(2)}, u32[]{:S(2)}) collective-permute-start(bf16[2,512,128]{2,1,0:T(8,128)(2,1)S(1)} %get-tuple-element.163), channel_id=1, source_target_pairs={{0,3},{3,0},{4,7},{7,4},{8,11},{11,8},{12,15},{15,12},{16,19},{19,... | collective-permute-start | bytes 786440 | tf_op jit(solution)/shard_map/ppermute | solution.py:200
  190.8 9.4 %collective-permute-start.30 = (f32[520,128]{1,0:T(8,128)S(1)}, f32[520,128]{1,0:T(8,128)S(1)}, u32[]{:S(2)}, u32[]{:S(2)}) collective-permute-start(f32[520,128]{1,0:T(8,128)S(1)} %get-tuple-element.218), channel_id=1, source_target_pairs={{0,8},{4,12},{8,0},{12,4},{1,9},{5,13},{9,1},{13,5},{2,10},{6,14},... | collective-permute-start | bytes 798728 | tf_op jit(solution)/shard_map/ppermute | solution.py:203
  192.3 7.8 %collective-permute-start.31 = (f32[520,128]{1,0:T(8,128)S(1)}, f32[520,128]{1,0:T(8,128)S(1)}, u32[]{:S(2)}, u32[]{:S(2)}) collective-permute-start(f32[520,128]{1,0:T(8,128)S(1)} %get-tuple-element.219), channel_id=1, source_target_pairs={{0,4},{4,0},{8,12},{12,8},{1,5},{5,1},{9,13},{13,9},{2,6},{6,2},{1... | collective-permute-start | bytes 798728 | tf_op jit(solution)/shard_map/ppermute | solution.py:203
  192.3 12.6 %collective-permute-start.32 = (f32[520,128]{1,0:T(8,128)S(1)}, f32[520,128]{1,0:T(8,128)S(1)}, u32[]{:S(2)}, u32[]{:S(2)}) collective-permute-start(f32[520,128]{1,0:T(8,128)S(1)} %get-tuple-element.220), channel_id=1, source_target_pairs={{0,12},{4,8},{8,4},{12,0},{1,13},{5,9},{9,5},{13,1},{2,14},{6,10},... | collective-permute-start | bytes 798728 | tf_op jit(solution)/shard_map/ppermute | solution.py:203
  193.0 12.1 %collective-permute-start.33 = (bf16[2,528,128]{2,1,0:T(8,128)(2,1)S(1)}, bf16[2,528,128]{2,1,0:T(8,128)(2,1)S(1)}, u32[]{:S(2)}, u32[]{:S(2)}) collective-permute-start(bf16[2,528,128]{2,1,0:T(8,128)(2,1)S(1)} %get-tuple-element.162), channel_id=1, source_target_pairs={{0,3},{3,0},{4,7},{7,4},{8,11},{11,8},{12,15},{15,12},{16,19},{19,... | collective-permute-start | bytes 811016 | tf_op jit(solution)/shard_map/ppermute | solution.py:200
  197.5 12.7 %collective-permute-start.35 = (bf16[512,128]{1,0:T(8,128)(2,1)S(1)}, bf16[512,128]{1,0:T(8,128)(2,1)S(1)}, u32[]{:S(2)}, u32[]{:S(2)}) collective-permute-start(bf16[512,128]{1,0:T(8,128)(2,1)S(1)} %get-tuple-element.185), channel_id=1, source_target_pairs={{0,8},{4,12},{8,0},{12,4},{1,9},{5,13},{9,1},{13,5},{2,10},{6,14},... | collective-permute-start | bytes 393224 | tf_op jit(solution)/shard_map/ppermute | solution.py:203
  200.2 10.1 %collective-permute-start.37 = (bf16[512,128]{1,0:T(8,128)(2,1)S(1)}, bf16[512,128]{1,0:T(8,128)(2,1)S(1)}, u32[]{:S(2)}, u32[]{:S(2)}) collective-permute-start(bf16[512,128]{1,0:T(8,128)(2,1)S(1)} %get-tuple-element.184), channel_id=1, source_target_pairs={{0,12},{4,8},{8,4},{12,0},{1,13},{5,9},{9,5},{13,1},{2,14},{6,10},... | collective-permute-start | bytes 393224 | tf_op jit(solution)/shard_map/ppermute | solution.py:203
  205.0 4.5 %collective-permute-start.38 = (bf16[16,128]{1,0:T(8,128)(2,1)S(1)}, bf16[16,128]{1,0:T(8,128)(2,1)S(1)}, u32[]{:S(2)}, u32[]{:S(2)}) collective-permute-start(bf16[16,128]{1,0:T(8,128)(2,1)S(1)} %slice_bitcast_fusion.8), channel_id=1, source_target_pairs={{0,8},{4,12},{8,0},{12,4},{1,9},{5,13},{9,1},{13,5},{2,10},{6,14},... | collective-permute-start | bytes 12296 | tf_op jit(solution)/shard_map/ppermute | solution.py:203
  206.5 3.1 %collective-permute-start.39 = (bf16[16,128]{1,0:T(8,128)(2,1)S(1)}, bf16[16,128]{1,0:T(8,128)(2,1)S(1)}, u32[]{:S(2)}, u32[]{:S(2)}) collective-permute-start(bf16[16,128]{1,0:T(8,128)(2,1)S(1)} %slice_bitcast_fusion.8), channel_id=1, source_target_pairs={{0,12},{4,8},{8,4},{12,0},{1,13},{5,9},{9,5},{13,1},{2,14},{6,10},... | collective-permute-start | bytes 12296 | tf_op jit(solution)/shard_map/ppermute | solution.py:203
  207.5 2.1 collective-permute-start.36

commit v12 on v11

--- a/solution.py
+++ b/solution.py
@@ -40,7 +40,7 @@
 
 SMALL = pl.CostEstimate(flops=1, bytes_accessed=1, transcendentals=0)
 SOME = pl.CostEstimate(flops=2 * 10**9, bytes_accessed=2**20, transcendentals=0)
-MORE = pl.CostEstimate(flops=5 * 10**9, bytes_accessed=2**20, transcendentals=0)
+MORE = pl.CostEstimate(flops=7 * 10**9, bytes_accessed=2**20, transcendentals=0)
 PARAMS = pltpu.CompilerParams(vmem_limit_bytes=12 * 2**20)
 
 
@@ -166,9 +166,13 @@
         out[r - low, place] = value.astype(BF16)
         chosen = chosen + jnp.sum(value * counts[r, place], axis=0, keepdims=True)
     chosen_out[...] = jnp.broadcast_to(chosen, chosen_out.shape)
-    for n in range(2):
-        if out.shape[1] > train_rows:
-            out[n, train_rows:] = jnp.broadcast_to(chosen, (EXTRA, rows)).astype(BF16)
+    if out.shape[1] > train_rows:
+        high = chosen.astype(BF16).astype(F32)
+        both = jnp.concatenate(
+            [jnp.broadcast_to(value, (EXTRA // 2, rows)) for value in (high, chosen - high)]
+        )
+        for n in range(2):
+            out[n, train_rows:] = both.astype(BF16)
 
 
 def last_scores(kept, got, counts, before, grads, extra):
@@ -234,12 +238,11 @@
     other_core, other_chip = to_other(train_grads, 1), to_other(train_grads, 2)
     own, other_core = tied(test_grads, other_core)
     own, own_sent = core_sum(*product(flags, [own], fisher), sent_as=F32, cost=MORE)
-    counts = selected(chosen_ids)
     half = own_rows // 2
     other_both = [to_other(other_chip[:half], 1), to_other(other_chip[half:], 1)]
     grads = [train_grads, other_core, other_chip, *other_both]
-    pair_in, middle_in, own, own_sent, counts, chosen_ids, grads = tied(
-        pair_in, middle_in, own, own_sent, counts, chosen_ids, grads
+    pair_in, middle_in, own, own_sent, chosen_ids, grads = tied(
+        pair_in, middle_in, own, own_sent, chosen_ids, grads
     )
     places = ((0, 0), (1, 0), (2, 0), (3, 0), (3, half))
 
@@ -252,8 +255,9 @@
     third, third_sent = core_sum(*product(flags, [pair_in], fisher))
     (near,) = scores_of((near, near_got), cost=SOME)
     far_ids = along(chosen_ids, [(0, 3), (3, 0)])
-    far_in, second_edge, third, third_sent, own, own_got, near, far_ids, grads = tied(
-        far_in, second_edge, third, third_sent, own, own_got, near, far_ids, grads
+    counts = selected(chosen_ids)
+    far_in, second_edge, third, third_sent, own, own_got, near, far_ids, counts, grads = tied(
+        far_in, second_edge, third, third_sent, own, own_got, near, far_ids, counts, grads
     )
 
     first_edge = along(far_in, outward)
@@ -264,12 +268,15 @@
     second_got, near_in, near_across = tied(second_got, near_in, near_across)
     (second,) = scores_of((second, second_got))
     across = along(second, middle)
-    third, total = scores_of(
-        (third, to_other(third_sent, 2)), (own, own_got), out_as=(F32, F32)
-    )
+    (third,) = scores_of((third, to_other(third_sent, 2)), out_as=(F32,))
+    (own,) = scores_of((own, own_got), out_as=(F32,))
+    own = own + near_in.astype(F32) + near_across.astype(F32)
+    chosen = jnp.broadcast_to(jnp.sum(own * counts, axis=(0, 1)), (8, quarter))
+    early = [jnp.concatenate([part, chosen]) for part in own]
+    early = [early[0]] + [to_other(early[r], r) for r in range(1, 4)]
     far_counts = selected(far_ids)
-    first_edge, total, near_in, near_across, second, across, third, grads, far_counts = tied(
-        first_edge, total, near_in, near_across, second, across, third, grads, far_counts
+    first_edge, early, second, across, third, grads, counts, far_counts = tied(
+        first_edge, early, second, across, third, grads, counts, far_counts
     )
 
     third = along((third + across.astype(F32)).astype(BF16), outward)
@@ -281,23 +288,29 @@
     pieces = [(*place, grad) for place, grad in zip(places, grads)]
     away, chosen = last_scores(last, last_got, far_counts, none, pieces[2:], 0)
     away = along(away, ends)
-    away = [to_other(away[0], 2), to_other(away[1], 3)]
+    away, second, third = tied(away, second, third)
+    away = [to_other(away[0], 2).astype(F32), to_other(away[1], 3).astype(F32)]
     here, _ = last_scores(last, last_got, far_counts, chosen, pieces[:2], EXTRA)
-    here, second, third = tied(here, second, third)
     here = along(here, ends)
     here = [here[0], to_other(here[1], 1)]
-    chosen = [part[own_rows:] for part in here]
-    chosen += [to_other(chosen[0], 2), to_other(chosen[0], 3)]
-    last = in_order([part[:own_rows] for part in here] + away)
-    last_chosen = in_order(chosen)[0]
-
-    total = total + sum(value.astype(F32) for value in (near_in, near_across, second, third))
-    chosen = jnp.sum(total * counts, axis=(0, 1))
-    total = [jnp.concatenate([part, jnp.broadcast_to(chosen, (8, quarter))]) for part in total]
-    total = in_order([total[0]] + [to_other(total[r], r) for r in range(1, 4)])
-
-    scores = total[:own_rows] + last.astype(F32)
-    return scores, total[own_rows] + last_chosen.astype(F32)
+    sums = [part[own_rows:] for part in here]
+    sums += [to_other(sums[0], 2), to_other(sums[0], 3)]
+
+    late = second + third
+    chosen = jnp.sum(late.astype(F32) * counts, axis=(0, 1))
+    high = lax.reduce_precision(chosen, 8, 7)
+    chosen = [jnp.broadcast_to(value, (EXTRA // 2, quarter)) for value in (high, chosen - high)]
+    chosen = jnp.concatenate(chosen).astype(BF16)
+    late = [jnp.concatenate([part, chosen]) for part in late]
+    late = [late[0]] + [to_other(late[r], r) for r in range(1, 4)]
+
+    def of_sums(value):
+        return value[0].astype(F32) + value[EXTRA // 2].astype(F32)
+
+    early, late, sums = in_order(early), in_order(late), in_order(sums)
+    last = in_order([part[:own_rows].astype(F32) for part in here] + away)
+    scores = early[:own_rows] + late[:own_rows].astype(F32) + last
+    return scores, early[own_rows] + of_sums(late[own_rows:]) + of_sums(sums)
 
 
 def solution(mesh):

time: 212 us -> 219 us (1.033)
  waiting for transfers between devices: 91.5 us -> 67.3 us
  local copies, waits for them, and re-layouts: 5.94 us -> 17.4 us
  Pallas kernels: 53.9 us -> 63.7 us
  starting transfers between devices: 52.9 us -> 59.4 us
  other arithmetic: 6.08 us -> 9.64 us
    ppermute x27 -> x30, waiting for transfers between devices: 79.2 us -> 61.8 us  [to_other(): return lax.ppermute(value, 'train', [(k, k ^ r) for k in range(4)])]
    unnamed x12 -> x58, local copies, waits for them, and re-layouts: 4.98 us -> 17 us
    ppermute x13, waiting for transfers between devices: 12.3 us -> 5.53 us  [along(): return lax.ppermute(value, 'test', pairs)]
    ppermute x13, starting transfers between devices: 33.3 us -> 39.3 us  [along(): return lax.ppermute(value, 'test', pairs)]
    pallas_call x3 -> x4, Pallas kernels: 14.1 us -> 17.2 us  [partial_scores(): pl.pallas_call(functools.partial(scores_body, [piece[:2] for piece in gra...]
    pallas_call x5, Pallas kernels: 30.8 us -> 33.7 us  [product(): pl.pallas_call(functools.partial(product_body, len(blocks)), in_specs=[pl...]
    pallas_call x5, Pallas kernels: 4.11 us -> 6.66 us  [fold(): pl.pallas_call(fold_body, in_specs=[pl.BlockSpec(memory_space=pltpu.SMEM)...]
    ppermute x27 -> x30, starting transfers between devices: 19.7 us -> 20.2 us  [to_other(): return lax.ppermute(value, 'train', [(k, k ^ r) for k in range(4)])]
  transfers between devices with their start and end apart: 40 -> 43, of which waited for: 22 -> 19; matrix products, arithmetic and copies ran while one was open for 3% -> 4% of each run, Pallas kernels for 22% -> 26%
where the time goes in v12:
time: 219 us
  waiting for transfers between devices  67.3 us (31%)
  Pallas kernels  63.7 us (29%)
  starting transfers between devices  59.4 us (27%)
  local copies, waits for them, and re-layouts  17.4 us (8%)
  other arithmetic  9.64 us (4%)
    ppermute x30, waiting for transfers between devices, to_other(): return lax.ppermute(value, 'train', [(k, k ^ r) for k in range(4)])  61.8 us
    ppermute x13, starting transfers between devices, along(): return lax.ppermute(value, 'test', pairs)  39.3 us
    pallas_call x5, Pallas kernels, product(): pl.pallas_call(functools.partial(product_body, len(blocks)), in_specs=[pl...  33.7 us
    ppermute x30, starting transfers between devices, to_other(): return lax.ppermute(value, 'train', [(k, k ^ r) for k in range(4)])  20.2 us
    pallas_call x4, Pallas kernels, partial_scores(): pl.pallas_call(functools.partial(scores_body, [piece[:2] for piece in gra...  17.2 us
    unnamed x58, local copies, waits for them, and re-layouts  17 us
    pallas_call x5, Pallas kernels, fold(): pl.pallas_call(fold_body, in_specs=[pl.BlockSpec(memory_space=pltpu.SMEM)...  6.66 us
    pallas_call x2, Pallas kernels, last_scores(): pl.pallas_call(functools.partial(last_scores_body, [piece[:2] for piece i...  6.15 us
  transfers between devices with their start and end apart: 43, of which 19 were waited for; matrix products, arithmetic and copies ran while one was open for 4% of the time, Pallas kernels for 26%

profile of v12, /device:TPU:0, one launch (start us, length us, event | category | flops | bytes accessed | tf_op | source)
XLA Modules:
  0.0 218.7 jit_solution(14044931111374611832)
XLA Ops:
  1.1 2.6 %collective-permute-start.5 = (bf16[512,2048]{1,0:T(8,128)(2,1)}, bf16[512,2048]{1,0:T(8,128)(2,1)S(1)}, u32[]{:S(2)}, u32[]{:S(2)}) collective-permute-start(bf16[512,2048]{1,0:T(8,128)(2,1)} %refs_0_.1), channel_id=1, source_target_pairs={{0,8},{4,12},{8,0},{12,4},{1,9},{5,13},{9,1},{13,5},{2,10},{6,14},... | collective-permute-start | bytes 6291464 | tf_op jit(solution)/shard_map/ppermute | solution.py:207
  3.7 1.6 collective-permute-start
  5.3 2.0 collective-permute-start.1
  7.4 3.4 %copy-done = bf16[2048,2048]{1,0:T(8,128)(2,1)S(1)} copy-done((bf16[2048,2048]{1,0:T(8,128)(2,1)S(1)}, bf16[2048,2048]{1,0:T(8,128)(2,1)}, u32[]{:S(2)}) %copy-start) | copy-done | bytes 8388632
  10.7 1.6 copy-done.13
  12.3 5.6 %product.5 = (f32[256,2048]{1,0:T(8,128)S(1)}, bf16[128,2048]{1,0:T(8,128)(2,1)S(1)}, bf16[128,2048]{1,0:T(8,128)(2,1)S(1)}) custom-call(s32[3]{0:T(128)S(1)} %pad_add_fusion.flags, bf16[512,2048]{1,0:T(8,128)(2,1)S(1)} %copy-done.13, bf16[2048,2048]{1,0:T(8,128)(2,1)S(1)} %copy-done), custom_call_target="tpu_custom_call" | custom-call | flops 1 | bytes 1 | tf_op jit(solution)/shard_map/product/pallas_call | solution.py:80
  18.5 31.6 %collective-permute-done.5.refs_4_.refs_0_ = bf16[512,2048]{1,0:T(8,128)(2,1)S(1)} collective-permute-done((bf16[512,2048]{1,0:T(8,128)(2,1)}, bf16[512,2048]{1,0:T(8,128)(2,1)S(1)}, u32[]{:S(2)}, u32[]{:S(2)}) %collective-permute-start.5) | collective-permute-done | bytes 2097184 | tf_op jit(solution)/shard_map/ppermute | solution.py:207
  50.9 1.8 fold.5
  52.7 1.0 copy-done.14
  54.5 2.1 collective-permute-start.8
  56.7 1.3 collective-permute-start.9
  57.9 1.8 collective-permute-start.12
  59.8 8.3 %product.6 = (f32[256,2048]{1,0:T(8,128)S(1)}, bf16[128,2048]{1,0:T(8,128)(2,1)}, bf16[128,2048]{1,0:T(8,128)(2,1)}) custom-call(s32[3]{0:T(128)S(1)} %pad_add_fusion.flags, bf16[512,2048]{1,0:T(8,128)(2,1)} %collective-permute-done.1.refs_0_, bf16[512,2048]{1,0:T(8,128)(2,1)} %collective-permute-done.refs_1_.refs_0_, bf16[2048,2048]{1,0:T(8,128)(2,1)S(1)} %bitcast.120), custom_call_target="tpu_custom_call" | custom-call | flops 1 | bytes 1 | tf_op jit(solution)/shard_map/product/pallas_call | solution.py:80
  68.1 1.4 copy-done.11
  70.2 1.6 collective-permute-done.10.refs_0_
  72.5 1.6 copy-done.12
  74.1 1.5 fold.6
  75.6 7.9 %collective-permute-done.12.refs_1_ = f32[128,2048]{1,0:T(8,128)} collective-permute-done((f32[128,2048]{1,0:T(8,128)}, f32[128,2048]{1,0:T(8,128)}, u32[]{:S(2)}, u32[]{:S(2)}) %collective-permute-start.12) | collective-permute-done | bytes 1048608 | tf_op jit(solution)/shard_map/ppermute | solution.py:207
  83.5 1.7 collective-permute-start.15
  85.3 3.4 %copy-done.1 = bf16[2048,2048]{1,0:T(8,128)(2,1)S(1)} copy-done((bf16[2048,2048]{1,0:T(8,128)(2,1)S(1)}, bf16[2048,2048]{1,0:T(8,128)(2,1)}, u32[]{:S(2)}) %copy-start.1) | copy-done | bytes 8388632
  88.7 6.8 %product.7 = (f32[256,2048]{1,0:T(8,128)S(1)}, bf16[128,2048]{1,0:T(8,128)(2,1)S(1)}, bf16[128,2048]{1,0:T(8,128)(2,1)S(1)}) custom-call(s32[3]{0:T(128)S(1)} %pad_add_fusion.flags, bf16[512,2048]{1,0:T(8,128)(2,1)} %collective-permute-done.refs_1_.refs_0_, bf16[2048,2048]{1,0:T(8,128)(2,1)S(1)} %copy-done.1), custom_call_target="tpu_custom_call" | custom-call | flops 1 | bytes 1 | tf_op jit(solution)/shard_map/product/pallas_call | solution.py:80
  96.1 1.7 convert_add_fusion.2
  97.8 5.5 %collective-permute-start.16 = (s32[512,16]{0,1:T(8,128)S(1)}, s32[512,16]{0,1:T(8,128)S(1)}, u32[]{:S(2)}, u32[]{:S(2)}) collective-permute-start(s32[512,16]{0,1:T(8,128)S(1)} %copy-done.24), channel_id=1, source_target_pairs={{0,3},{3,0},{4,7},{7,4},{8,11},{11,8},{12,15},{15,12},{16,19},{19,... | collective-permute-start | bytes 98312 | tf_op jit(solution)/shard_map/ppermute | solution.py:204
  103.3 4.1 %scores.4 = bf16[4,512,128]{2,1,0:T(8,128)(2,1)S(1)} custom-call(f32[128,2048]{1,0:T(8,128)S(1)} %get-tuple-element.105.refs_0_, bf16[128,2048]{1,0:T(8,128)(2,1)S(1)} %collective-permute-done.15.refs_1_, bf16[512,2048]{1,0:T(8,128)(2,1)S(1)} %copy-done.2, bf16[512,2048]{1,0:T(8,128)(2,1)} %collective-permute-done.2.refs_3_.refs_1_, ...), custom_call_target="tpu_custom_call" | custom-call | flops 2000000000 | bytes 1048576 | tf_op jit(solution)/shard_map/scores/pallas_call | solution.py:144
  107.5 0.8 fold.7
  108.3 1.3 collective-permute-start.17
  109.7 7.3 %product.8 = (f32[256,2048]{1,0:T(8,128)S(1)}, bf16[128,2048]{1,0:T(8,128)(2,1)S(1)}, bf16[128,2048]{1,0:T(8,128)(2,1)S(1)}) custom-call(s32[3]{0:T(128)S(1)} %pad_add_fusion.flags, bf16[512,2048]{1,0:T(8,128)(2,1)} %collective-permute-done.8.refs_0_, bf16[512,2048]{1,0:T(8,128)(2,1)} %collective-permute-done.9.refs_1_, bf16[2048,2048]{1,0:T(8,128)(2,1)S(1)} %bitcast.122), custom_call_target="tpu_custom_call" | custom-call | flops 1 | bytes 1 | tf_op jit(solution)/shard_map/product/pallas_call | solution.py:80
  117.6 1.4 collective-permute-done.18.refs_0_
  120.6 1.1 collective-permute-start.20
  121.7 4.7 %collective-permute-start.21 = (bf16[4,512,128]{2,1,0:T(8,128)(2,1)S(1)}, bf16[4,512,128]{2,1,0:T(8,128)(2,1)S(1)}, u32[]{:S(2)}, u32[]{:S(2)}) collective-permute-start(bf16[4,512,128]{2,1,0:T(8,128)(2,1)S(1)} %scores.4), channel_id=1, source_target_pairs={{0,1},{3,2},{4,5},{7,6},{8,9},{11,10},{12,13},{15,14},{16,17},{19,... | collective-permute-start | bytes 1572872 | tf_op jit(solution)/shard_map/ppermute | solution.py:204
  126.4 0.9 collective-permute-start.22
  127.3 1.0 collective-permute-start.27
  128.3 4.3 %scores.5 = f32[4,512,128]{2,1,0:T(8,128)S(1)} custom-call(f32[128,2048]{1,0:T(8,128)S(1)} %copy-done.15, f32[128,2048]{1,0:T(8,128)} %collective-permute-done.12.refs_1_, bf16[512,2048]{1,0:T(8,128)(2,1)S(1)} %copy-done.2, bf16[512,2048]{1,0:T(8,128)(2,1)} %collective-permute-done.2.refs_3_.refs_1_, ...), custom_call_target="tpu_custom_call" | custom-call | flops 1 | bytes 1 | tf_op jit(solution)/shard_map/scores/pallas_call | solution.py:144
  132.7 2.7 %collective-permute-done.20.refs_1_ = bf16[128,2048]{1,0:T(8,128)(2,1)S(1)} collective-permute-done((bf16[128,2048]{1,0:T(8,128)(2,1)S(1)}, bf16[128,2048]{1,0:T(8,128)(2,1)S(1)}, u32[]{:S(2)}, u32[]{:S(2)}) %collective-permute-start.20) | collective-permute-done | bytes 524320 | tf_op jit(solution)/shard_map/ppermute | solution.py:207
  135.4 2.1 collective-permute-done.21
  137.6 4.8 %scores.6 = bf16[4,512,128]{2,1,0:T(8,128)(2,1)} custom-call(f32[128,2048]{1,0:T(8,128)S(1)} %get-tuple-element.133.refs_0_, bf16[128,2048]{1,0:T(8,128)(2,1)S(1)} %collective-permute-done.20.refs_1_, bf16[512,2048]{1,0:T(8,128)(2,1)S(1)} %copy-done.2, bf16[512,2048]{1,0:T(8,128)(2,1)} %collective-permute-done.2.refs_3_.refs_1_, ...), custom_call_target="tpu_custom_call" | custom-call | flops 1 | bytes 1 | tf_op jit(solution)/shard_map/scores/pallas_call | solution.py:144
  143.6 1.0 collective-permute-start.24
  144.7 1.2 collective-permute-done.27.refs_1_
  145.9 2.6 %convert_add_fusion.counts = f32[4,512,128]{2,1,0:T(8,128)} fusion(s32[128]{0:T(128)S(1)} %get-tuple-element.197, s32[128]{0:T(128)S(1)} %get-tuple-element.198, s32[128]{0:T(128)S(1)} %get-tuple-element.199, s32[128]{0:T(128)S(1)} %get-tuple-element.200, s32[128]{0:T(128)S(1)} %get-tuple-element.201, s32[128]{0:T(128)S(1)} %get-tuple-element.202, ...), kind=kLoop, calls=%fused_computation.5 | loop fusion | flops 12320768 | bytes 1064960 | tf_op jit(solution)/shard_map/add | solution.py:234
  148.4 4.0 %scores.7 = f32[4,512,128]{2,1,0:T(8,128)S(1)} custom-call(f32[128,2048]{1,0:T(8,128)S(1)} %get-tuple-element.135.refs_0_, bf16[128,2048]{1,0:T(8,128)(2,1)S(1)} %collective-permute-done.27.refs_1_, bf16[512,2048]{1,0:T(8,128)(2,1)S(1)} %copy-done.2, bf16[512,2048]{1,0:T(8,128)(2,1)} %collective-permute-done.2.refs_3_.refs_1_, ...), custom_call_target="tpu_custom_call" | custom-call | flops 1 | bytes 1 | tf_op jit(solution)/shard_map/scores/pallas_call | solution.py:144
  152.9 4.8 %collective-permute-done.25 = f32[520,128]{1,0:T(8,128)S(1)} collective-permute-done((f32[520,128]{1,0:T(8,128)S(1)}, f32[520,128]{1,0:T(8,128)S(1)}, u32[]{:S(2)}, u32[]{:S(2)}) %collective-permute-start.25) | collective-permute-done | bytes 266272 | tf_op jit(solution)/shard_map/ppermute | solution.py:207
  157.8 5.6 %product.9 = (f32[256,2048]{1,0:T(8,128)S(1)}, bf16[128,2048]{1,0:T(8,128)(2,1)S(1)}, bf16[128,2048]{1,0:T(8,128)(2,1)S(1)}) custom-call(s32[3]{0:T(128)S(1)} %pad_add_fusion.flags, bf16[512,2048]{1,0:T(8,128)(2,1)S(1)} %collective-permute-done.17.refs_0_, bf16[2048,2048]{1,0:T(8,128)(2,1)S(1)} %bitcast.122), custom_call_target="tpu_custom_call" | custom-call | flops 1 | bytes 1 | tf_op jit(solution)/shard_map/product/pallas_call | solution.py:80
  164.0 1.4 collective-permute-done.28.refs_0_
  166.1 1.7 fold.9
  167.8 1.0 copy-done.8
  168.8 0.9 collective-permute-start.30
  169.7 1.0 add_convert_fusion
  170.6 1.3 collective-permute-start.33
  171.9 10.1 %collective-permute-start.32 = (bf16[4,512,128]{2,1,0:T(8,128)(2,1)}, bf16[4,512,128]{2,1,0:T(8,128)(2,1)}, u32[]{:S(2)}, u32[]{:S(2)}) collective-permute-start(bf16[4,512,128]{2,1,0:T(8,128)(2,1)} %scores.6), channel_id=1, source_target_pairs={{0,2},{3,1},{4,6},{7,5},{8,10},{11,9},{12,14},{15,13},{16,18},{19,... | collective-permute-start | bytes 1572872 | tf_op jit(solution)/shard_map/ppermute | solution.py:204
  182.0 1.1 collective-permute-done.30.got
  183.1 1.2 copy-done.6
  184.3 1.2 copy-done.7
  185.6 1.2 copy-done.9
  186.8 2.4 %last_scores.2 = (bf16[2,512,128]{2,1,0:T(8,128)(2,1)S(1)}, f32[8,128]{1,0:T(8,128)S(1)}) custom-call(f32[128,2048]{1,0:T(8,128)S(1)} %copy-done.9, bf16[128,2048]{1,0:T(8,128)(2,1)} %collective-permute-done.30.got, f32[4,512,128]{2,1,0:T(8,128)S(1)} %copy-done.7, f32[8,128]{1,0:T(8,128)S(1)} %broadcast_in_dim.9.before, ...), custom_call_target="tpu_custom_call" | custom-call | flops 1 | bytes 1 | tf_op jit(solution)/shard_map/last_scores/pallas_call | solution.py:180
  189.2 5.3 %collective-permute-start.31 = (bf16[2,512,128]{2,1,0:T(8,128)(2,1)S(1)}, bf16[2,512,128]{2,1,0:T(8,128)(2,1)S(1)}, u32[]{:S(2)}, u32[]{:S(2)}) collective-permute-start(bf16[2,512,128]{2,1,0:T(8,128)(2,1)S(1)} %get-tuple-element.152), channel_id=1, source_target_pairs={{0,3},{3,0},{4,7},{7,4},{8,11},{11,8},{12,15},{15,12},{16,19},{19,... | collective-permute-start | bytes 786440 | tf_op jit(solution)/shard_map/ppermute | solution.py:204
  194.8 3.7 %last_scores.3 = (bf16[2,528,128]{2,1,0:T(8,128)(2,1)S(1)}, f32[8,128]{1,0:T(8,128)}) custom-call(f32[128,2048]{1,0:T(8,128)S(1)} %copy-done.10, bf16[128,2048]{1,0:T(8,128)(2,1)} %collective-permute-done.30.got, f32[4,512,128]{2,1,0:T(8,128)S(1)} %copy-done.7, f32[8,128]{1,0:T(8,128)S(1)} %get-tuple-element.159.before, bf16[512,2048]{1,0:T(8,128)(2,1)S(1)} %copy-done.3, ...), custom_call_target="tpu_custom_call" | custom-call | flops 1 | bytes 1 | tf_op jit(solution)/shard_map/last_scores/pallas_call | solution.py:180
  198.6 2.5 %collective-permute-start.37 = (bf16[2,528,128]{2,1,0:T(8,128)(2,1)S(1)}, bf16[2,528,128]{2,1,0:T(8,128)(2,1)S(1)}, u32[]{:S(2)}, u32[]{:S(2)}) collective-permute-start(bf16[2,528,128]{2,1,0:T(8,128)(2,1)S(1)} %get-tuple-element.162), channel_id=1, source_target_pairs={{0,3},{3,0},{4,7},{7,4},{8,11},{11,8},{12,15},{15,12},{16,19},{19,... | collective-permute-start | bytes 811016 | tf_op jit(solution)/shard_map/ppermute | solution.py:204
  201.4 1.5 multiply_reduce_fusion
  203.0 1.6 collective-permute-start.34
  205.3 1.6 collective-permute-start.38
  206.8 3.0 %collective-permute-done.37 = bf16[2,528,128]{2,1,0:T(8,128)(2,1)S(1)} collective-permute-done((bf16[2,528,128]{2,1,0:T(8,128)(2,1)S(1)}, bf16[2,528,128]{2,1,0:T(8,128)(2,1)S(1)}, u32[]{:S(2)}, u32[]{:S(2)}) %collective-permute-start.37) | collective-permute-done | bytes 270368 | tf_op jit(solution)/shard_map/ppermute | solution.py:204
  209.9 1.2 collective-permute-start.41
  212.3 4.5 %collective-permute-done.41 = bf16[16,128]{1,0:T(8,128)(2,1)S(1)} collective-permute-done((bf16[16,128]{1,0:T(8,128)(2,1)S(1)}, bf16[16,128]{1,0:T(8,128)(2,1)S(1)}, u32[]{:S(2)}, u32[]{:S(2)}) %collective-permute-start.41) | collective-permute-done | bytes 4128 | tf_op jit(solution)/shard_map/ppermute | solution.py:207
  217.5 1.2 fusion
  (131 shorter events, 13.2 us)
Async XLA Ops:
  0.6 6.7 %collective-permute-start.2 = (bf16[512,2048]{1,0:T(8,128)(2,1)}, bf16[512,2048]{1,0:T(8,128)(2,1)}, u32[]{:S(2)}, u32[]{:S(2)}) collective-permute-start(bf16[512,2048]{1,0:T(8,128)(2,1)} %refs_0_.1), channel_id=1, source_target_pairs={{0,4},{4,0},{8,12},{12,8},{1,5},{5,1},{9,13},{13,9},{2,6},{6,2},{1... | collective-permute-start | bytes 6291464 | tf_op jit(solution)/shard_map/ppermute | solution.py:207
  1.1 49.0 %collective-permute-start.5 = (bf16[512,2048]{1,0:T(8,128)(2,1)}, bf16[512,2048]{1,0:T(8,128)(2,1)S(1)}, u32[]{:S(2)}, u32[]{:S(2)}) collective-permute-start(bf16[512,2048]{1,0:T(8,128)(2,1)} %refs_0_.1), channel_id=1, source_target_pairs={{0,8},{4,12},{8,0},{12,4},{1,9},{5,13},{9,1},{13,5},{2,10},{6,14},... | collective-permute-start | bytes 6291464 | tf_op jit(solution)/shard_map/ppermute | solution.py:207
  3.7 50.0 %collective-permute-start = (bf16[512,2048]{1,0:T(8,128)(2,1)}, bf16[512,2048]{1,0:T(8,128)(2,1)}, u32[]{:S(2)}, u32[]{:S(2)}) collective-permute-start(bf16[512,2048]{1,0:T(8,128)(2,1)} %refs_0_), channel_id=1, source_target_pairs={{0,1},{1,0},{2,3},{3,2},{4,5},{5,4},{6,7},{7,6},{8,9},{9,8},{10,11... | collective-permute-start | bytes 6291464 | tf_op jit(solution)/shard_map/ppermute | solution.py:204
  5.3 48.4 %collective-permute-start.1 = (bf16[512,2048]{1,0:T(8,128)(2,1)}, bf16[512,2048]{1,0:T(8,128)(2,1)}, u32[]{:S(2)}, u32[]{:S(2)}) collective-permute-start(bf16[512,2048]{1,0:T(8,128)(2,1)} %refs_0_), channel_id=1, source_target_pairs={{1,2},{2,1},{5,6},{6,5},{9,10},{10,9},{13,14},{14,13},{17,18},{18,... | collective-permute-start | bytes 6291464 | tf_op jit(solution)/shard_map/ppermute | solution.py:204
  7.4 3.4 %copy-start = (bf16[2048,2048]{1,0:T(8,128)(2,1)S(1)}, bf16[2048,2048]{1,0:T(8,128)(2,1)}, u32[]{:S(2)}) copy-start(bf16[2048,2048]{1,0:T(8,128)(2,1)} %refs_1_.5) | copy-start | bytes 25165828
  17.9 32.5 %collective-permute-start.3 = (bf16[128,2048]{1,0:T(8,128)(2,1)S(1)}, bf16[128,2048]{1,0:T(8,128)(2,1)S(1)}, u32[]{:S(2)}, u32[]{:S(2)}) collective-permute-start(bf16[128,2048]{1,0:T(8,128)(2,1)S(1)} %get-tuple-element.85), channel_id=1, source_target_pairs={{0,4},{4,0},{8,12},{12,8},{1,5},{5,1},{9,13},{13,9},{2,6},{6,2},{1... | collective-permute-start | bytes 1572872 | tf_op jit(solution)/shard_map/ppermute | solution.py:207
  18.0 32.9 %collective-permute-start.4 = (bf16[128,2048]{1,0:T(8,128)(2,1)S(1)}, bf16[128,2048]{1,0:T(8,128)(2,1)S(1)}, u32[]{:S(2)}, u32[]{:S(2)}) collective-permute-start(bf16[128,2048]{1,0:T(8,128)(2,1)S(1)} %get-tuple-element.86), channel_id=1, source_target_pairs={{0,4},{4,0},{8,12},{12,8},{1,5},{5,1},{9,13},{13,9},{2,6},{6,2},{1... | collective-permute-start | bytes 1572872 | tf_op jit(solution)/shard_map/ppermute | solution.py:207
  50.3 3.4 %collective-permute-start.6 = (bf16[256,2048]{1,0:T(8,128)(2,1)S(1)}, bf16[256,2048]{1,0:T(8,128)(2,1)S(1)}, u32[]{:S(2)}, u32[]{:S(2)}) collective-permute-start(bf16[256,2048]{1,0:T(8,128)(2,1)S(1)} %get-tuple-element.169), channel_id=1, source_target_pairs={{0,4},{4,0},{8,12},{12,8},{1,5},{5,1},{9,13},{13,9},{2,6},{6,2},{1... | collective-permute-start | bytes 3145736 | tf_op jit(solution)/shard_map/ppermute | solution.py:207
  50.4 4.1 %collective-permute-start.7 = (bf16[256,2048]{1,0:T(8,128)(2,1)S(1)}, bf16[256,2048]{1,0:T(8,128)(2,1)S(1)}, u32[]{:S(2)}, u32[]{:S(2)}) collective-permute-start(bf16[256,2048]{1,0:T(8,128)(2,1)S(1)} %get-tuple-element.168), channel_id=1, source_target_pairs={{0,4},{4,0},{8,12},{12,8},{1,5},{5,1},{9,13},{13,9},{2,6},{6,2},{1... | collective-permute-start | bytes 3145736 | tf_op jit(solution)/shard_map/ppermute | solution.py:207
  50.9 8.9 %slice-start = ((s8[8388608]{0:T(1024)(128)(4,1)}), s8[4194304]{0:T(1024)(128)(4,1)S(1)}, s32[]{:S(2)}) async-start(s8[8388608]{0:T(1024)(128)(4,1)} %bitcast.119), calls=%async_computation | async-start | bytes 8388608
  50.9 8.9 %slice-start.1 = ((s8[8388608]{0:T(1024)(128)(4,1)}), s8[4194304]{0:T(1024)(128)(4,1)S(1)}, s32[]{:S(2)}) async-start(s8[8388608]{0:T(1024)(128)(4,1)} %bitcast.119), calls=%async_computation.1 | async-start | bytes 8388608
  54.5 13.6 %copy-start.4 = (bf16[256,2048]{1,0:T(8,128)(2,1)}, bf16[256,2048]{1,0:T(8,128)(2,1)S(1)}, u32[]{:S(2)}) copy-start(bf16[256,2048]{1,0:T(8,128)(2,1)S(1)} %collective-permute-done.7.refs_6_.refs_2_) | copy-start | bytes 3145732
  54.5 15.6 %copy-start.24 = (s32[512,16]{0,1:T(8,128)S(1)}, s32[512,16]{0,1:T(8,128)}, u32[]{:S(2)}) copy-start(s32[512,16]{0,1:T(8,128)} %param.7) | copy-start | bytes 98308
  54.5 53.8 %collective-permute-start.8 = (bf16[512,2048]{1,0:T(8,128)(2,1)}, bf16[512,2048]{1,0:T(8,128)(2,1)}, u32[]{:S(2)}, u32[]{:S(2)}) collective-permute-start(bf16[512,2048]{1,0:T(8,128)(2,1)} %collective-permute-done.refs_1_.refs_0_), channel_id=1, source_target_pairs={{1,2},{2,1},{5,6},{6,5},{9,10},{10,9},{13,14},{14,13},{17,18},{18,... | collective-permute-start | bytes 6291464 | tf_op jit(solution)/shard_map/ppermute | solution.py:204
  56.7 51.7 %collective-permute-start.9 = (bf16[512,2048]{1,0:T(8,128)(2,1)}, bf16[512,2048]{1,0:T(8,128)(2,1)}, u32[]{:S(2)}, u32[]{:S(2)}) collective-permute-start(bf16[512,2048]{1,0:T(8,128)(2,1)} %collective-permute-done.1.refs_0_), channel_id=1, source_target_pairs={{1,0},{2,3},{5,4},{6,7},{9,8},{10,11},{13,12},{14,15},{17,16},{18,... | collective-permute-start | bytes 6291464 | tf_op jit(solution)/shard_map/ppermute | solution.py:204
  57.9 25.6 %collective-permute-start.12 = (f32[128,2048]{1,0:T(8,128)}, f32[128,2048]{1,0:T(8,128)}, u32[]{:S(2)}, u32[]{:S(2)}) collective-permute-start(f32[128,2048]{1,0:T(8,128)} %get-tuple-element.96), channel_id=1, source_target_pairs={{0,8},{4,12},{8,0},{12,4},{1,9},{5,13},{9,1},{13,5},{2,10},{6,14},... | collective-permute-start | bytes 3145736 | tf_op jit(solution)/shard_map/ppermute | solution.py:207
  69.5 2.3 %collective-permute-start.10 = (bf16[128,2048]{1,0:T(8,128)(2,1)}, bf16[128,2048]{1,0:T(8,128)(2,1)}, u32[]{:S(2)}, u32[]{:S(2)}) collective-permute-start(bf16[128,2048]{1,0:T(8,128)(2,1)} %get-tuple-element.93), channel_id=1, source_target_pairs={{0,4},{4,0},{8,12},{12,8},{1,5},{5,1},{9,13},{13,9},{2,6},{6,2},{1... | collective-permute-start | bytes 1572872 | tf_op jit(solution)/shard_map/ppermute | solution.py:207
  69.5 3.0 %collective-permute-start.11 = (bf16[128,2048]{1,0:T(8,128)(2,1)}, bf16[128,2048]{1,0:T(8,128)(2,1)}, u32[]{:S(2)}, u32[]{:S(2)}) collective-permute-start(bf16[128,2048]{1,0:T(8,128)(2,1)} %get-tuple-element.94), channel_id=1, source_target_pairs={{0,4},{4,0},{8,12},{12,8},{1,5},{5,1},{9,13},{13,9},{2,6},{6,2},{1... | collective-permute-start | bytes 1572872 | tf_op jit(solution)/shard_map/ppermute | solution.py:207
  83.5 14.2 %collective-permute-start.15 = (bf16[128,2048]{1,0:T(8,128)(2,1)S(1)}, bf16[128,2048]{1,0:T(8,128)(2,1)S(1)}, u32[]{:S(2)}, u32[]{:S(2)}) collective-permute-start(bf16[128,2048]{1,0:T(8,128)(2,1)S(1)} %get-tuple-element.106), channel_id=1, source_target_pairs={{0,8},{4,12},{8,0},{12,4},{1,9},{5,13},{9,1},{13,5},{2,10},{6,14},... | collective-permute-start | bytes 1572872 | tf_op jit(solution)/shard_map/ppermute | solution.py:207
  85.3 3.4 %copy-start.1 = (bf16[2048,2048]{1,0:T(8,128)(2,1)S(1)}, bf16[2048,2048]{1,0:T(8,128)(2,1)}, u32[]{:S(2)}) copy-start(bf16[2048,2048]{1,0:T(8,128)(2,1)} %refs_1_.5) | copy-start | bytes 25165828
  88.7 14.7 %copy-start.2 = (bf16[512,2048]{1,0:T(8,128)(2,1)S(1)}, bf16[512,2048]{1,0:T(8,128)(2,1)}, u32[]{:S(2)}) copy-start(bf16[512,2048]{1,0:T(8,128)(2,1)} %refs_0_.1) | copy-start | bytes 6291460
  88.7 14.7 %copy-start.5 = (bf16[256,2048]{1,0:T(8,128)(2,1)S(1)}, bf16[256,2048]{1,0:T(8,128)(2,1)}, u32[]{:S(2)}) copy-start(bf16[256,2048]{1,0:T(8,128)(2,1)} %copy-done.4) | copy-start | bytes 3145732
  88.7 21.0 %slice-start.2 = ((s8[8388608]{0:T(1024)(128)(4,1)}), s8[4194304]{0:T(1024)(128)(4,1)S(1)}, s32[]{:S(2)}) async-start(s8[8388608]{0:T(1024)(128)(4,1)} %bitcast.121), calls=%async_computation.2 | async-start | bytes 8388608
  95.5 11.9 %collective-permute-start.13 = (bf16[128,2048]{1,0:T(8,128)(2,1)S(1)}, bf16[128,2048]{1,0:T(8,128)(2,1)S(1)}, u32[]{:S(2)}, u32[]{:S(2)}) collective-permute-start(bf16[128,2048]{1,0:T(8,128)(2,1)S(1)} %get-tuple-element.99), channel_id=1, source_target_pairs={{0,4},{4,0},{8,12},{12,8},{1,5},{5,1},{9,13},{13,9},{2,6},{6,2},{1... | collective-permute-start | bytes 1572872 | tf_op jit(solution)/shard_map/ppermute | solution.py:207
  95.6 11.9 %collective-permute-start.14 = (bf16[128,2048]{1,0:T(8,128)(2,1)S(1)}, bf16[128,2048]{1,0:T(8,128)(2,1)S(1)}, u32[]{:S(2)}, u32[]{:S(2)}) collective-permute-start(bf16[128,2048]{1,0:T(8,128)(2,1)S(1)} %get-tuple-element.100), channel_id=1, source_target_pairs={{0,4},{4,0},{8,12},{12,8},{1,5},{5,1},{9,13},{13,9},{2,6},{6,2},{1... | collective-permute-start | bytes 1572872 | tf_op jit(solution)/shard_map/ppermute | solution.py:207
  97.8 45.3 %copy-start.16 = (f32[4,512,128]{2,1,0:T(8,128)}, f32[4,512,128]{2,1,0:T(8,128)S(1)}, u32[]{:S(2)}) copy-start(f32[4,512,128]{2,1,0:T(8,128)S(1)} %convert_add_fusion.2) | copy-start | bytes 3145732
  97.8 10.5 %collective-permute-start.16 = (s32[512,16]{0,1:T(8,128)S(1)}, s32[512,16]{0,1:T(8,128)S(1)}, u32[]{:S(2)}, u32[]{:S(2)}) collective-permute-start(s32[512,16]{0,1:T(8,128)S(1)} %copy-done.24), channel_id=1, source_target_pairs={{0,3},{3,0},{4,7},{7,4},{8,11},{11,8},{12,15},{15,12},{16,19},{19,... | collective-permute-start | bytes 98312 | tf_op jit(solution)/shard_map/ppermute | solution.py:204
  103.3 6.3 %slice-start.3 = ((s8[8388608]{0:T(1024)(128)(4,1)}), s8[4194304]{0:T(1024)(128)(4,1)S(1)}, s32[]{:S(2)}) async-start(s8[8388608]{0:T(1024)(128)(4,1)} %bitcast.121), calls=%async_computation.3 | async-start | bytes 8388608
  108.3 49.4 %collective-permute-start.17 = (bf16[512,2048]{1,0:T(8,128)(2,1)}, bf16[512,2048]{1,0:T(8,128)(2,1)S(1)}, u32[]{:S(2)}, u32[]{:S(2)}) collective-permute-start(bf16[512,2048]{1,0:T(8,128)(2,1)} %collective-permute-done.8.refs_0_), channel_id=1, source_target_pairs={{1,0},{2,3},{5,4},{6,7},{9,8},{10,11},{13,12},{14,15},{17,16},{18,... | collective-permute-start | bytes 6291464 | tf_op jit(solution)/shard_map/ppermute | solution.py:204
  117.0 11.3 %copy-start.15 = (f32[128,2048]{1,0:T(8,128)S(1)}, f32[128,2048]{1,0:T(8,128)}, u32[]{:S(2)}) copy-start(f32[128,2048]{1,0:T(8,128)} %copy-done.14) | copy-start | bytes 3145732
  117.0 2.0 collective-permute-start.18
  117.1 2.6 %collective-permute-start.19 = (bf16[128,2048]{1,0:T(8,128)(2,1)S(1)}, bf16[128,2048]{1,0:T(8,128)(2,1)S(1)}, u32[]{:S(2)}, u32[]{:S(2)}) collective-permute-start(bf16[128,2048]{1,0:T(8,128)(2,1)S(1)} %get-tuple-element.124), channel_id=1, source_target_pairs={{0,4},{4,0},{8,12},{12,8},{1,5},{5,1},{9,13},{13,9},{2,6},{6,2},{1... | collective-permute-start | bytes 1572872 | tf_op jit(solution)/shard_map/ppermute | solution.py:207
  120.6 14.8 %collective-permute-start.20 = (bf16[128,2048]{1,0:T(8,128)(2,1)S(1)}, bf16[128,2048]{1,0:T(8,128)(2,1)S(1)}, u32[]{:S(2)}, u32[]{:S(2)}) collective-permute-start(bf16[128,2048]{1,0:T(8,128)(2,1)S(1)} %get-tuple-element.128), channel_id=1, source_target_pairs={{0,8},{4,12},{8,0},{12,4},{1,9},{5,13},{9,1},{13,5},{2,10},{6,14},... | collective-permute-start | bytes 1572872 | tf_op jit(solution)/shard_map/ppermute | solution.py:207
  121.7 15.9 %collective-permute-start.21 = (bf16[4,512,128]{2,1,0:T(8,128)(2,1)S(1)}, bf16[4,512,128]{2,1,0:T(8,128)(2,1)S(1)}, u32[]{:S(2)}, u32[]{:S(2)}) collective-permute-start(bf16[4,512,128]{2,1,0:T(8,128)(2,1)S(1)} %scores.4), channel_id=1, source_target_pairs={{0,1},{3,2},{4,5},{7,6},{8,9},{11,10},{12,13},{15,14},{16,17},{19,... | collective-permute-start | bytes 1572872 | tf_op jit(solution)/shard_map/ppermute | solution.py:204
  126.4 11.2 %collective-permute-start.22 = (bf16[4,512,128]{2,1,0:T(8,128)(2,1)S(1)}, bf16[4,512,128]{2,1,0:T(8,128)(2,1)S(1)}, u32[]{:S(2)}, u32[]{:S(2)}) collective-permute-start(bf16[4,512,128]{2,1,0:T(8,128)(2,1)S(1)} %scores.4), channel_id=1, source_target_pairs={{1,2},{2,1},{5,6},{6,5},{9,10},{10,9},{13,14},{14,13},{17,18},{18,... | collective-permute-start | bytes 1572872 | tf_op jit(solution)/shard_map/ppermute | solution.py:204
  127.3 18.6 %collective-permute-start.27 = (bf16[128,2048]{1,0:T(8,128)(2,1)S(1)}, bf16[128,2048]{1,0:T(8,128)(2,1)S(1)}, u32[]{:S(2)}, u32[]{:S(2)}) collective-permute-start(bf16[128,2048]{1,0:T(8,128)(2,1)S(1)} %get-tuple-element.136), channel_id=1, source_target_pairs={{0,8},{4,12},{8,0},{12,4},{1,9},{5,13},{9,1},{13,5},{2,10},{6,14},... | collective-permute-start | bytes 1572872 | tf_op jit(solution)/shard_map/ppermute | solution.py:207
  142.3 15.3 %collective-permute-start.26 = (bf16[4,512,128]{2,1,0:T(8,128)(2,1)}, bf16[4,512,128]{2,1,0:T(8,128)(2,1)S(1)}, u32[]{:S(2)}, u32[]{:S(2)}) collective-permute-start(bf16[4,512,128]{2,1,0:T(8,128)(2,1)} %scores.6), channel_id=1, source_target_pairs={{1,2},{2,1},{5,6},{6,5},{9,10},{10,9},{13,14},{14,13},{17,18},{18,... | collective-permute-start | bytes 1572872 | tf_op jit(solution)/shard_map/ppermute | solution.py:204
  143.5 8.9 %collective-permute-start.23 = (f32[520,128]{1,0:T(8,128)S(1)}, f32[520,128]{1,0:T(8,128)S(1)}, u32[]{:S(2)}, u32[]{:S(2)}) collective-permute-start(f32[520,128]{1,0:T(8,128)S(1)} %get-tuple-element.232), channel_id=1, source_target_pairs={{0,4},{4,0},{8,12},{12,8},{1,5},{5,1},{9,13},{13,9},{2,6},{6,2},{1... | collective-permute-start | bytes 798728 | tf_op jit(solution)/shard_map/ppermute | solution.py:207
  143.6 9.3 %collective-permute-start.24 = (f32[520,128]{1,0:T(8,128)S(1)}, f32[520,128]{1,0:T(8,128)S(1)}, u32[]{:S(2)}, u32[]{:S(2)}) collective-permute-start(f32[520,128]{1,0:T(8,128)S(1)} %get-tuple-element.233), channel_id=1, source_target_pairs={{0,8},{4,12},{8,0},{12,4},{1,9},{5,13},{9,1},{13,5},{2,10},{6,14},... | collective-permute-start | bytes 798728 | tf_op jit(solution)/shard_map/ppermute | solution.py:207
  145.8 11.8 %collective-permute-start.25 = (f32[520,128]{1,0:T(8,128)S(1)}, f32[520,128]{1,0:T(8,128)S(1)}, u32[]{:S(2)}, u32[]{:S(2)}) collective-permute-start(f32[520,128]{1,0:T(8,128)S(1)} %get-tuple-element.231), channel_id=1, source_target_pairs={{0,12},{4,8},{8,4},{12,0},{1,13},{5,9},{9,5},{13,1},{2,14},{6,10},... | collective-permute-start | bytes 798728 | tf_op jit(solution)/shard_map/ppermute | solution.py:207
  152.4 5.4 %copy-start.18 = (f32[520,128]{1,0:T(8,128)}, f32[520,128]{1,0:T(8,128)S(1)}, u32[]{:S(2)}) copy-start(f32[520,128]{1,0:T(8,128)S(1)} %collective-permute-done.23) | copy-start | bytes 798724
  152.9 4.9 %copy-start.20 = (f32[520,128]{1,0:T(8,128)}, f32[520,128]{1,0:T(8,128)S(1)}, u32[]{:S(2)}) copy-start(f32[520,128]{1,0:T(8,128)S(1)} %collective-permute-done.24) | copy-start | bytes 798724
  157.7 5.7 %copy-start.22 = (f32[520,128]{1,0:T(8,128)}, f32[520,128]{1,0:T(8,128)S(1)}, u32[]{:S(2)}) copy-start(f32[520,128]{1,0:T(8,128)S(1)} %collective-permute-done.25) | copy-start | bytes 798724
  163.4 2.0 collective-permute-start.28
  163.7 2.5 %collective-permute-start.29 = (bf16[128,2048]{1,0:T(8,128)(2,1)S(1)}, bf16[128,2048]{1,0:T(8,128)(2,1)S(1)}, u32[]{:S(2)}, u32[]{:S(2)}) collective-permute-start(bf16[128,2048]{1,0:T(8,128)(2,1)S(1)} %get-tuple-element.145), channel_id=1, source_target_pairs={{0,4},{4,0},{8,12},{12,8},{1,5},{5,1},{9,13},{13,9},{2,6},{6,2},{1... | collective-permute-start | bytes 1572872 | tf_op jit(solution)/shard_map/ppermute | solution.py:207
  168.8 14.3 %collective-permute-start.30 = (bf16[128,2048]{1,0:T(8,128)(2,1)}, bf16[128,2048]{1,0:T(8,128)(2,1)}, u32[]{:S(2)}, u32[]{:S(2)}) collective-permute-start(bf16[128,2048]{1,0:T(8,128)(2,1)} %get-tuple-element.147), channel_id=1, source_target_pairs={{0,8},{4,12},{8,0},{12,4},{1,9},{5,13},{9,1},{13,5},{2,10},{6,14},... | collective-permute-start | bytes 1572872 | tf_op jit(solution)/shard_map/ppermute | solution.py:207
  170.6 30.5 %collective-permute-start.33 = (bf16[4,512,128]{2,1,0:T(8,128)(2,1)}, bf16[4,512,128]{2,1,0:T(8,128)(2,1)}, u32[]{:S(2)}, u32[]{:S(2)}) collective-permute-start(bf16[4,512,128]{2,1,0:T(8,128)(2,1)} %add_convert_fusion), channel_id=1, source_target_pairs={{1,0},{2,3},{5,4},{6,7},{9,8},{10,11},{13,12},{14,15},{17,16},{18,... | collective-permute-start | bytes 1572872 | tf_op jit(solution)/shard_map/ppermute | solution.py:204
  171.9 29.2 %collective-permute-start.32 = (bf16[4,512,128]{2,1,0:T(8,128)(2,1)}, bf16[4,512,128]{2,1,0:T(8,128)(2,1)}, u32[]{:S(2)}, u32[]{:S(2)}) collective-permute-start(bf16[4,512,128]{2,1,0:T(8,128)(2,1)} %scores.6), channel_id=1, source_target_pairs={{0,2},{3,1},{4,6},{7,5},{8,10},{11,9},{12,14},{15,13},{16,18},{19,... | collective-permute-start | bytes 1572872 | tf_op jit(solution)/shard_map/ppermute | solution.py:204
  186.8 7.8 %copy-start.19 = (f32[520,128]{1,0:T(8,128)S(1)}, f32[520,128]{1,0:T(8,128)}, u32[]{:S(2)}) copy-start(f32[520,128]{1,0:T(8,128)} %copy-done.18) | copy-start | bytes 798724
  186.8 7.8 %copy-start.21 = (f32[520,128]{1,0:T(8,128)S(1)}, f32[520,128]{1,0:T(8,128)}, u32[]{:S(2)}) copy-start(f32[520,128]{1,0:T(8,128)} %copy-done.20) | copy-start | bytes 798724
  186.8 7.8 %copy-start.23 = (f32[520,128]{1,0:T(8,128)S(1)}, f32[520,128]{1,0:T(8,128)}, u32[]{:S(2)}) copy-start(f32[520,128]{1,0:T(8,128)} %copy-done.22) | copy-start | bytes 798724
  189.2 5.6 %copy-start.3 = (bf16[512,2048]{1,0:T(8,128)(2,1)S(1)}, bf16[512,2048]{1,0:T(8,128)(2,1)}, u32[]{:S(2)}) copy-start(bf16[512,2048]{1,0:T(8,128)(2,1)} %refs_0_.1) | copy-start | bytes 6291460
  189.2 5.6 %copy-start.10 = (f32[128,2048]{1,0:T(8,128)S(1)}, f32[128,2048]{1,0:T(8,128)}, u32[]{:S(2)}) copy-start(f32[128,2048]{1,0:T(8,128)} %copy-done.8) | copy-start | bytes 3145732
  189.2 12.2 %collective-permute-start.31 = (bf16[2,512,128]{2,1,0:T(8,128)(2,1)S(1)}, bf16[2,512,128]{2,1,0:T(8,128)(2,1)S(1)}, u32[]{:S(2)}, u32[]{:S(2)}) collective-permute-start(bf16[2,512,128]{2,1,0:T(8,128)(2,1)S(1)} %get-tuple-element.152), channel_id=1, source_target_pairs={{0,3},{3,0},{4,7},{7,4},{8,11},{11,8},{12,15},{15,12},{16,19},{19,... | collective-permute-start | bytes 786440 | tf_op jit(solution)/shard_map/ppermute | solution.py:204
  194.8 6.6 %copy-start.17 = (f32[4,512,128]{2,1,0:T(8,128)S(1)}, f32[4,512,128]{2,1,0:T(8,128)}, u32[]{:S(2)}) copy-start(f32[4,512,128]{2,1,0:T(8,128)} %copy-done.16) | copy-start | bytes 3145732
  198.6 11.3 %collective-permute-start.37 = (bf16[2,528,128]{2,1,0:T(8,128)(2,1)S(1)}, bf16[2,528,128]{2,1,0:T(8,128)(2,1)S(1)}, u32[]{:S(2)}, u32[]{:S(2)}) collective-permute-start(bf16[2,528,128]{2,1,0:T(8,128)(2,1)S(1)} %get-tuple-element.162), channel_id=1, source_target_pairs={{0,3},{3,0},{4,7},{7,4},{8,11},{11,8},{12,15},{15,12},{16,19},{19,... | collective-permute-start | bytes 811016 | tf_op jit(solution)/shard_map/ppermute | solution.py:204
  203.0 6.8 %collective-permute-start.34 = (bf16[528,128]{1,0:T(8,128)(2,1)S(1)}, bf16[528,128]{1,0:T(8,128)(2,1)S(1)}, u32[]{:S(2)}, u32[]{:S(2)}) collective-permute-start(bf16[528,128]{1,0:T(8,128)(2,1)S(1)} %get-tuple-element.228), channel_id=1, source_target_pairs={{0,8},{4,12},{8,0},{12,4},{1,9},{5,13},{9,1},{13,5},{2,10},{6,14},... | collective-permute-start | bytes 405512 | tf_op jit(solution)/shard_map/ppermute | solution.py:207
  204.6 6.5 %collective-permute-start.35 = (bf16[528,128]{1,0:T(8,128)(2,1)S(1)}, bf16[528,128]{1,0:T(8,128)(2,1)S(1)}, u32[]{:S(2)}, u32[]{:S(2)}) collective-permute-start(bf16[528,128]{1,0:T(8,128)(2,1)S(1)} %get-tuple-element.229), channel_id=1, source_target_pairs={{0,4},{4,0},{8,12},{12,8},{1,5},{5,1},{9,13},{13,9},{2,6},{6,2},{1... | collective-permute-start | bytes 405512 | tf_op jit(solution)/shard_map/ppermute | solution.py:207
  204.6 7.3 %collective-permute-start.36 = (bf16[528,128]{1,0:T(8,128)(2,1)S(1)}, bf16[528,128]{1,0:T(8,128)(2,1)S(1)}, u32[]{:S(2)}, u32[]{:S(2)}) collective-permute-start(bf16[528,128]{1,0:T(8,128)(2,1)S(1)} %get-tuple-element.230), channel_id=1, source_target_pairs={{0,12},{4,8},{8,4},{12,0},{1,13},{5,9},{9,5},{13,1},{2,14},{6,10},... | collective-permute-start | bytes 405512 | tf_op jit(solution)/shard_map/ppermute | solution.py:207
  205.3 12.1 %collective-permute-start.38 = (bf16[512,128]{1,0:T(8,128)(2,1)S(1)}, bf16[512,128]{1,0:T(8,128)(2,1)S(1)}, u32[]{:S(2)}, u32[]{:S(2)}) collective-permute-start(bf16[512,128]{1,0:T(8,128)(2,1)S(1)} %get-tuple-element.194), channel_id=1, source_target_pairs={{0,8},{4,12},{8,0},{12,4},{1,9},{5,13},{9,1},{13,5},{2,10},{6,14},... | collective-permute-start | bytes 393224 | tf_op jit(solution)/shard_map/ppermute | solution.py:207
  209.8 7.5 %collective-permute-start.40 = (bf16[512,128]{1,0:T(8,128)(2,1)S(1)}, bf16[512,128]{1,0:T(8,128)(2,1)S(1)}, u32[]{:S(2)}, u32[]{:S(2)}) collective-permute-start(bf16[512,128]{1,0:T(8,128)(2,1)S(1)} %get-tuple-element.195), channel_id=1, source_target_pairs={{0,12},{4,8},{8,4},{12,0},{1,13},{5,9},{9,5},{13,1},{2,14},{6,10},... | collective-permute-start | bytes 393224 | tf_op jit(solution)/shard_map/ppermute | solution.py:207
  209.9 6.9 %collective-permute-start.41 = (bf16[16,128]{1,0:T(8,128)(2,1)S(1)}, bf16[16,128]{1,0:T(8,128)(2,1)S(1)}, u32[]{:S(2)}, u32[]{:S(2)}) collective-permute-start(bf16[16,128]{1,0:T(8,128)(2,1)S(1)} %slice_bitcast_fusion.12), channel_id=1, source_target_pairs={{0,8},{4,12},{8,0},{12,4},{1,9},{5,13},{9,1},{13,5},{2,10},{6,14},... | collective-permute-start | bytes 12296 | tf_op jit(solution)/shard_map/ppermute | solution.py:207
  211.1 5.7 %collective-permute-start.42 = (bf16[16,128]{1,0:T(8,128)(2,1)S(1)}, bf16[16,128]{1,0:T(8,128)(2,1)S(1)}, u32[]{:S(2)}, u32[]{:S(2)}) collective-permute-start(bf16[16,128]{1,0:T(8,128)(2,1)S(1)} %slice_bitcast_fusion.12), channel_id=1, source_target_pairs={{0,12},{4,8},{8,4},{12,0},{1,13},{5,9},{9,5},{13,1},{2,14},{6,10},... | collective-permute-start | bytes 12296 | tf_op jit(solution)/shard_map/ppermute | solution.py:207
  211.9 4.9 %collective-permute-start.39 = (bf16[528,128]{1,0:T(8,128)(2,1)S(1)}, bf16[528,128]{1,0:T(8,128)(2,1)S(1)}, u32[]{:S(2)}, u32[]{:S(2)}) collective-permute-start(bf16[528,128]{1,0:T(8,128)(2,1)S(1)} %slice_bitcast_fusion.4), channel_id=1, source_target_pairs={{0,4},{4,0},{8,12},{12,8},{1,5},{5,1},{9,13},{13,9},{2,6},{6,2},{1... | collective-permute-start | bytes 405512 | tf_op jit(solution)/shard_map/ppermute | solution.py:207
  (8 other events, 10.2 us)

commit v13 on v12

--- a/solution.py
+++ b/solution.py
@@ -41,7 +41,7 @@
 SMALL = pl.CostEstimate(flops=1, bytes_accessed=1, transcendentals=0)
 SOME = pl.CostEstimate(flops=2 * 10**9, bytes_accessed=2**20, transcendentals=0)
 MORE = pl.CostEstimate(flops=7 * 10**9, bytes_accessed=2**20, transcendentals=0)
-PARAMS = pltpu.CompilerParams(vmem_limit_bytes=12 * 2**20)
+PARAMS = pltpu.CompilerParams(vmem_limit_bytes=8 * 2**20)
 
 
 VMEM = pl.BlockSpec(memory_space=pltpu.VMEM)
@@ -265,7 +265,6 @@
     second, second_sent, near = tied(second, second_sent, near)
     second_got = to_other(second_sent, 2)
     near_in, near_across = along(near, inward), along(near, middle)
-    second_got, near_in, near_across = tied(second_got, near_in, near_across)
     (second,) = scores_of((second, second_got))
     across = along(second, middle)
     (third,) = scores_of((third, to_other(third_sent, 2)), out_as=(F32,))

time: 219 us -> 219 us (level)
    ppermute x30, waiting for transfers between devices: 61.8 us -> 64.1 us  [to_other(): return lax.ppermute(value, 'train', [(k, k ^ r) for k in range(4)])]
    unnamed x58 -> x60, local copies, waits for them, and re-layouts: 17 us -> 17.1 us
  transfers between devices with their start and end apart: 43 -> 43, of which waited for: 19 -> 16; matrix products, arithmetic and copies ran while one was open for 4% -> 4% of each run, Pallas kernels for 26% -> 26%
where the time goes in v13:
time: 219 us
  waiting for transfers between devices  68.9 us (31%)
  Pallas kernels  63.7 us (29%)
  starting transfers between devices  57.7 us (26%)
  local copies, waits for them, and re-layouts  17.4 us (8%)
  other arithmetic  9.6 us (4%)
    ppermute x30, waiting for transfers between devices, to_other(): return lax.ppermute(value, 'train', [(k, k ^ r) for k in range(4)])  64.1 us
    ppermute x13, starting transfers between devices, along(): return lax.ppermute(value, 'test', pairs)  37.1 us
    pallas_call x5, Pallas kernels, product(): pl.pallas_call(functools.partial(product_body, len(blocks)), in_specs=[pl...  33.7 us
    ppermute x30, starting transfers between devices, to_other(): return lax.ppermute(value, 'train', [(k, k ^ r) for k in range(4)])  20.6 us
    pallas_call x4, Pallas kernels, partial_scores(): pl.pallas_call(functools.partial(scores_body, [piece[:2] for piece in gra...  17.2 us
    unnamed x60, local copies, waits for them, and re-layouts  17.1 us
    pallas_call x5, Pallas kernels, fold(): pl.pallas_call(fold_body, in_specs=[pl.BlockSpec(memory_space=pltpu.SMEM)...  6.68 us
    pallas_call x2, Pallas kernels, last_scores(): pl.pallas_call(functools.partial(last_scores_body, [piece[:2] for piece i...  6.15 us
  transfers between devices with their start and end apart: 43, of which 16 were waited for; matrix products, arithmetic and copies ran while one was open for 4% of the time, Pallas kernels for 26%

profile of v13, /device:TPU:0, one launch (start us, length us, event | category | flops | bytes accessed | tf_op | source)
XLA Modules:
  0.0 218.5 jit_solution(13189926115300916094)
XLA Ops:
  1.1 2.6 %collective-permute-start.5 = (bf16[512,2048]{1,0:T(8,128)(2,1)}, bf16[512,2048]{1,0:T(8,128)(2,1)S(1)}, u32[]{:S(2)}, u32[]{:S(2)}) collective-permute-start(bf16[512,2048]{1,0:T(8,128)(2,1)} %refs_0_.1), channel_id=1, source_target_pairs={{0,8},{4,12},{8,0},{12,4},{1,9},{5,13},{9,1},{13,5},{2,10},{6,14},... | collective-permute-start | bytes 6291464 | tf_op jit(solution)/shard_map/ppermute | solution.py:207
  3.7 1.6 collective-permute-start
  5.3 2.0 collective-permute-start.1
  7.4 3.4 %copy-done = bf16[2048,2048]{1,0:T(8,128)(2,1)S(1)} copy-done((bf16[2048,2048]{1,0:T(8,128)(2,1)S(1)}, bf16[2048,2048]{1,0:T(8,128)(2,1)}, u32[]{:S(2)}) %copy-start) | copy-done | bytes 8388632
  10.7 1.6 copy-done.14
  12.3 5.6 %product.5 = (f32[256,2048]{1,0:T(8,128)S(1)}, bf16[128,2048]{1,0:T(8,128)(2,1)S(1)}, bf16[128,2048]{1,0:T(8,128)(2,1)S(1)}) custom-call(s32[3]{0:T(128)S(1)} %pad_add_fusion.flags, bf16[512,2048]{1,0:T(8,128)(2,1)S(1)} %copy-done.14, bf16[2048,2048]{1,0:T(8,128)(2,1)S(1)} %copy-done), custom_call_target="tpu_custom_call" | custom-call | flops 1 | bytes 1 | tf_op jit(solution)/shard_map/product/pallas_call | solution.py:80
  18.5 31.7 %collective-permute-done.5.refs_4_.refs_0_ = bf16[512,2048]{1,0:T(8,128)(2,1)S(1)} collective-permute-done((bf16[512,2048]{1,0:T(8,128)(2,1)}, bf16[512,2048]{1,0:T(8,128)(2,1)S(1)}, u32[]{:S(2)}, u32[]{:S(2)}) %collective-permute-start.5) | collective-permute-done | bytes 2097184 | tf_op jit(solution)/shard_map/ppermute | solution.py:207
  50.9 1.8 fold.5
  52.7 1.0 copy-done.15
  54.5 2.1 collective-permute-start.8
  56.7 1.3 collective-permute-start.9
  57.9 1.8 collective-permute-start.12
  59.8 8.3 %product.6 = (f32[256,2048]{1,0:T(8,128)S(1)}, bf16[128,2048]{1,0:T(8,128)(2,1)}, bf16[128,2048]{1,0:T(8,128)(2,1)}) custom-call(s32[3]{0:T(128)S(1)} %pad_add_fusion.flags, bf16[512,2048]{1,0:T(8,128)(2,1)} %collective-permute-done.1.refs_0_, bf16[512,2048]{1,0:T(8,128)(2,1)} %collective-permute-done.refs_1_.refs_0_, bf16[2048,2048]{1,0:T(8,128)(2,1)S(1)} %bitcast.120), custom_call_target="tpu_custom_call" | custom-call | flops 1 | bytes 1 | tf_op jit(solution)/shard_map/product/pallas_call | solution.py:80
  68.1 1.4 copy-done.12
  70.2 1.6 collective-permute-done.10.refs_0_
  72.5 1.6 copy-done.13
  74.1 1.5 fold.6
  75.6 7.9 %collective-permute-done.12.refs_1_ = f32[128,2048]{1,0:T(8,128)} collective-permute-done((f32[128,2048]{1,0:T(8,128)}, f32[128,2048]{1,0:T(8,128)}, u32[]{:S(2)}, u32[]{:S(2)}) %collective-permute-start.12) | collective-permute-done | bytes 1048608 | tf_op jit(solution)/shard_map/ppermute | solution.py:207
  83.5 1.7 collective-permute-start.15
  85.3 3.4 %copy-done.1 = bf16[2048,2048]{1,0:T(8,128)(2,1)S(1)} copy-done((bf16[2048,2048]{1,0:T(8,128)(2,1)S(1)}, bf16[2048,2048]{1,0:T(8,128)(2,1)}, u32[]{:S(2)}) %copy-start.1) | copy-done | bytes 8388632
  88.7 6.8 %product.7 = (f32[256,2048]{1,0:T(8,128)S(1)}, bf16[128,2048]{1,0:T(8,128)(2,1)S(1)}, bf16[128,2048]{1,0:T(8,128)(2,1)S(1)}) custom-call(s32[3]{0:T(128)S(1)} %pad_add_fusion.flags, bf16[512,2048]{1,0:T(8,128)(2,1)} %collective-permute-done.refs_1_.refs_0_, bf16[2048,2048]{1,0:T(8,128)(2,1)S(1)} %copy-done.1), custom_call_target="tpu_custom_call" | custom-call | flops 1 | bytes 1 | tf_op jit(solution)/shard_map/product/pallas_call | solution.py:80
  96.1 1.7 convert_add_fusion.2
  97.8 5.5 %collective-permute-start.16 = (s32[512,16]{0,1:T(8,128)S(1)}, s32[512,16]{0,1:T(8,128)S(1)}, u32[]{:S(2)}, u32[]{:S(2)}) collective-permute-start(s32[512,16]{0,1:T(8,128)S(1)} %copy-done.25), channel_id=1, source_target_pairs={{0,3},{3,0},{4,7},{7,4},{8,11},{11,8},{12,15},{15,12},{16,19},{19,... | collective-permute-start | bytes 98312 | tf_op jit(solution)/shard_map/ppermute | solution.py:204
  103.3 4.1 %scores.4 = bf16[4,512,128]{2,1,0:T(8,128)(2,1)S(1)} custom-call(f32[128,2048]{1,0:T(8,128)S(1)} %get-tuple-element.102.refs_0_, bf16[128,2048]{1,0:T(8,128)(2,1)S(1)} %collective-permute-done.15.refs_1_, bf16[512,2048]{1,0:T(8,128)(2,1)S(1)} %copy-done.2, bf16[512,2048]{1,0:T(8,128)(2,1)} %collective-permute-done.2.refs_3_.refs_1_, ...), custom_call_target="tpu_custom_call" | custom-call | flops 2000000000 | bytes 1048576 | tf_op jit(solution)/shard_map/scores/pallas_call | solution.py:144
  108.4 1.3 collective-permute-start.17
  109.7 7.3 %product.8 = (f32[256,2048]{1,0:T(8,128)S(1)}, bf16[128,2048]{1,0:T(8,128)(2,1)S(1)}, bf16[128,2048]{1,0:T(8,128)(2,1)S(1)}) custom-call(s32[3]{0:T(128)S(1)} %pad_add_fusion.flags, bf16[512,2048]{1,0:T(8,128)(2,1)} %collective-permute-done.8.refs_0_, bf16[512,2048]{1,0:T(8,128)(2,1)} %collective-permute-done.9.refs_1_, bf16[2048,2048]{1,0:T(8,128)(2,1)S(1)} %bitcast.122), custom_call_target="tpu_custom_call" | custom-call | flops 1 | bytes 1 | tf_op jit(solution)/shard_map/product/pallas_call | solution.py:80
  117.6 1.4 collective-permute-done.18.refs_0_
  120.6 1.1 collective-permute-start.25
  121.7 4.7 %collective-permute-start.20 = (bf16[4,512,128]{2,1,0:T(8,128)(2,1)S(1)}, bf16[4,512,128]{2,1,0:T(8,128)(2,1)S(1)}, u32[]{:S(2)}, u32[]{:S(2)}) collective-permute-start(bf16[4,512,128]{2,1,0:T(8,128)(2,1)S(1)} %scores.4), channel_id=1, source_target_pairs={{0,1},{3,2},{4,5},{7,6},{8,9},{11,10},{12,13},{15,14},{16,17},{19,... | collective-permute-start | bytes 1572872 | tf_op jit(solution)/shard_map/ppermute | solution.py:204
  127.3 1.1 collective-permute-start.27
  128.3 4.3 %scores.5 = f32[4,512,128]{2,1,0:T(8,128)S(1)} custom-call(f32[128,2048]{1,0:T(8,128)S(1)} %copy-done.16, f32[128,2048]{1,0:T(8,128)} %collective-permute-done.12.refs_1_, bf16[512,2048]{1,0:T(8,128)(2,1)S(1)} %copy-done.2, bf16[512,2048]{1,0:T(8,128)(2,1)} %collective-permute-done.2.refs_3_.refs_1_, ...), custom_call_target="tpu_custom_call" | custom-call | flops 1 | bytes 1 | tf_op jit(solution)/shard_map/scores/pallas_call | solution.py:144
  132.7 2.7 %collective-permute-done.25.refs_1_ = bf16[128,2048]{1,0:T(8,128)(2,1)S(1)} collective-permute-done((bf16[128,2048]{1,0:T(8,128)(2,1)S(1)}, bf16[128,2048]{1,0:T(8,128)(2,1)S(1)}, u32[]{:S(2)}, u32[]{:S(2)}) %collective-permute-start.25) | collective-permute-done | bytes 524320 | tf_op jit(solution)/shard_map/ppermute | solution.py:207
  135.4 4.8 %scores.6 = bf16[4,512,128]{2,1,0:T(8,128)(2,1)} custom-call(f32[128,2048]{1,0:T(8,128)S(1)} %get-tuple-element.127.refs_0_, bf16[128,2048]{1,0:T(8,128)(2,1)S(1)} %collective-permute-done.25.refs_1_, bf16[512,2048]{1,0:T(8,128)(2,1)S(1)} %copy-done.2, bf16[512,2048]{1,0:T(8,128)(2,1)} %collective-permute-done.2.refs_3_.refs_1_, ...), custom_call_target="tpu_custom_call" | custom-call | flops 1 | bytes 1 | tf_op jit(solution)/shard_map/scores/pallas_call | solution.py:144
  141.5 1.1 collective-permute-start.23
  142.6 4.1 %collective-permute-done.27.refs_1_ = bf16[128,2048]{1,0:T(8,128)(2,1)S(1)} collective-permute-done((bf16[128,2048]{1,0:T(8,128)(2,1)S(1)}, bf16[128,2048]{1,0:T(8,128)(2,1)S(1)}, u32[]{:S(2)}, u32[]{:S(2)}) %collective-permute-start.27) | collective-permute-done | bytes 524320 | tf_op jit(solution)/shard_map/ppermute | solution.py:207
  146.7 2.6 %convert_add_fusion.counts = f32[4,512,128]{2,1,0:T(8,128)} fusion(s32[128]{0:T(128)S(1)} %get-tuple-element.191, s32[128]{0:T(128)S(1)} %get-tuple-element.192, s32[128]{0:T(128)S(1)} %get-tuple-element.193, s32[128]{0:T(128)S(1)} %get-tuple-element.194, s32[128]{0:T(128)S(1)} %get-tuple-element.195, s32[128]{0:T(128)S(1)} %get-tuple-element.196, ...), kind=kLoop, calls=%fused_computation.5 | loop fusion | flops 12320768 | bytes 1064960 | tf_op jit(solution)/shard_map/add | solution.py:234
  149.2 4.0 %scores.7 = f32[4,512,128]{2,1,0:T(8,128)S(1)} custom-call(f32[128,2048]{1,0:T(8,128)S(1)} %get-tuple-element.129.refs_0_, bf16[128,2048]{1,0:T(8,128)(2,1)S(1)} %collective-permute-done.27.refs_1_, bf16[512,2048]{1,0:T(8,128)(2,1)S(1)} %copy-done.2, bf16[512,2048]{1,0:T(8,128)(2,1)} %collective-permute-done.2.refs_3_.refs_1_, ...), custom_call_target="tpu_custom_call" | custom-call | flops 1 | bytes 1 | tf_op jit(solution)/shard_map/scores/pallas_call | solution.py:144
  153.3 3.2 %collective-permute-done.24 = f32[520,128]{1,0:T(8,128)S(1)} collective-permute-done((f32[520,128]{1,0:T(8,128)S(1)}, f32[520,128]{1,0:T(8,128)S(1)}, u32[]{:S(2)}, u32[]{:S(2)}) %collective-permute-start.24) | collective-permute-done | bytes 266272 | tf_op jit(solution)/shard_map/ppermute | solution.py:207
  156.5 1.3 collective-permute-done.17.refs_0_
  157.8 5.6 %product.9 = (f32[256,2048]{1,0:T(8,128)S(1)}, bf16[128,2048]{1,0:T(8,128)(2,1)S(1)}, bf16[128,2048]{1,0:T(8,128)(2,1)S(1)}) custom-call(s32[3]{0:T(128)S(1)} %pad_add_fusion.flags, bf16[512,2048]{1,0:T(8,128)(2,1)S(1)} %collective-permute-done.17.refs_0_, bf16[2048,2048]{1,0:T(8,128)(2,1)S(1)} %bitcast.122), custom_call_target="tpu_custom_call" | custom-call | flops 1 | bytes 1 | tf_op jit(solution)/shard_map/product/pallas_call | solution.py:80
  164.0 1.4 collective-permute-done.28.refs_0_
  166.1 1.7 fold.9
  167.8 1.0 copy-done.9
  168.8 0.9 collective-permute-start.30
  169.7 0.9 add_convert_fusion
  170.7 1.3 collective-permute-start.33
  172.0 7.9 %collective-permute-start.32 = (bf16[4,512,128]{2,1,0:T(8,128)(2,1)}, bf16[4,512,128]{2,1,0:T(8,128)(2,1)}, u32[]{:S(2)}, u32[]{:S(2)}) collective-permute-start(bf16[4,512,128]{2,1,0:T(8,128)(2,1)} %scores.6), channel_id=1, source_target_pairs={{0,2},{3,1},{4,6},{7,5},{8,10},{11,9},{12,14},{15,13},{16,18},{19,... | collective-permute-start | bytes 1572872 | tf_op jit(solution)/shard_map/ppermute | solution.py:204
  179.9 3.3 %collective-permute-done.30.got = bf16[128,2048]{1,0:T(8,128)(2,1)} collective-permute-done((bf16[128,2048]{1,0:T(8,128)(2,1)}, bf16[128,2048]{1,0:T(8,128)(2,1)}, u32[]{:S(2)}, u32[]{:S(2)}) %collective-permute-start.30) | collective-permute-done | bytes 524320 | tf_op jit(solution)/shard_map/ppermute | solution.py:207
  183.2 1.2 copy-done.6
  184.4 1.2 copy-done.7
  185.7 1.2 copy-done.10
  186.9 2.4 %last_scores.2 = (bf16[2,512,128]{2,1,0:T(8,128)(2,1)S(1)}, f32[8,128]{1,0:T(8,128)S(1)}) custom-call(f32[128,2048]{1,0:T(8,128)S(1)} %copy-done.10, bf16[128,2048]{1,0:T(8,128)(2,1)} %collective-permute-done.30.got, f32[4,512,128]{2,1,0:T(8,128)S(1)} %copy-done.7, f32[8,128]{1,0:T(8,128)S(1)} %broadcast_in_dim.9.before, ...), custom_call_target="tpu_custom_call" | custom-call | flops 1 | bytes 1 | tf_op jit(solution)/shard_map/last_scores/pallas_call | solution.py:180
  189.3 4.9 %collective-permute-start.31 = (bf16[2,512,128]{2,1,0:T(8,128)(2,1)S(1)}, bf16[2,512,128]{2,1,0:T(8,128)(2,1)S(1)}, u32[]{:S(2)}, u32[]{:S(2)}) collective-permute-start(bf16[2,512,128]{2,1,0:T(8,128)(2,1)S(1)} %get-tuple-element.146), channel_id=1, source_target_pairs={{0,3},{3,0},{4,7},{7,4},{8,11},{11,8},{12,15},{15,12},{16,19},{19,... | collective-permute-start | bytes 786440 | tf_op jit(solution)/shard_map/ppermute | solution.py:204
  194.5 3.7 %last_scores.3 = (bf16[2,528,128]{2,1,0:T(8,128)(2,1)S(1)}, f32[8,128]{1,0:T(8,128)}) custom-call(f32[128,2048]{1,0:T(8,128)S(1)} %copy-done.11, bf16[128,2048]{1,0:T(8,128)(2,1)} %collective-permute-done.30.got, f32[4,512,128]{2,1,0:T(8,128)S(1)} %copy-done.8, f32[8,128]{1,0:T(8,128)S(1)} %get-tuple-element.153.before, bf16[512,2048]{1,0:T(8,128)(2,1)S(1)} %copy-done.3, ...), custom_call_target="tpu_custom_call" | custom-call | flops 1 | bytes 1 | tf_op jit(solution)/shard_map/last_scores/pallas_call | solution.py:180
  198.2 3.0 %collective-permute-start.37 = (bf16[2,528,128]{2,1,0:T(8,128)(2,1)S(1)}, bf16[2,528,128]{2,1,0:T(8,128)(2,1)S(1)}, u32[]{:S(2)}, u32[]{:S(2)}) collective-permute-start(bf16[2,528,128]{2,1,0:T(8,128)(2,1)S(1)} %get-tuple-element.156), channel_id=1, source_target_pairs={{0,3},{3,0},{4,7},{7,4},{8,11},{11,8},{12,15},{15,12},{16,19},{19,... | collective-permute-start | bytes 811016 | tf_op jit(solution)/shard_map/ppermute | solution.py:204
  201.3 1.5 multiply_reduce_fusion
  202.9 1.1 collective-permute-start.34
  204.0 1.1 collective-permute-start.36
  205.1 1.1 collective-permute-start.38
  206.2 3.4 %collective-permute-done.37 = bf16[2,528,128]{2,1,0:T(8,128)(2,1)S(1)} collective-permute-done((bf16[2,528,128]{2,1,0:T(8,128)(2,1)S(1)}, bf16[2,528,128]{2,1,0:T(8,128)(2,1)S(1)}, u32[]{:S(2)}, u32[]{:S(2)}) %collective-permute-start.37) | collective-permute-done | bytes 270368 | tf_op jit(solution)/shard_map/ppermute | solution.py:204
  209.6 1.6 collective-permute-start.41
  211.2 1.5 collective-permute-start.42
  212.9 3.7 %collective-permute-done.41 = bf16[16,128]{1,0:T(8,128)(2,1)S(1)} collective-permute-done((bf16[16,128]{1,0:T(8,128)(2,1)S(1)}, bf16[16,128]{1,0:T(8,128)(2,1)S(1)}, u32[]{:S(2)}, u32[]{:S(2)}) %collective-permute-start.41) | collective-permute-done | bytes 4128 | tf_op jit(solution)/shard_map/ppermute | solution.py:207
  217.4 1.2 fusion
  (133 shorter events, 12.5 us)
Async XLA Ops:
  0.6 6.7 %collective-permute-start.2 = (bf16[512,2048]{1,0:T(8,128)(2,1)}, bf16[512,2048]{1,0:T(8,128)(2,1)}, u32[]{:S(2)}, u32[]{:S(2)}) collective-permute-start(bf16[512,2048]{1,0:T(8,128)(2,1)} %refs_0_.1), channel_id=1, source_target_pairs={{0,4},{4,0},{8,12},{12,8},{1,5},{5,1},{9,13},{13,9},{2,6},{6,2},{1... | collective-permute-start | bytes 6291464 | tf_op jit(solution)/shard_map/ppermute | solution.py:207
  1.1 49.0 %collective-permute-start.5 = (bf16[512,2048]{1,0:T(8,128)(2,1)}, bf16[512,2048]{1,0:T(8,128)(2,1)S(1)}, u32[]{:S(2)}, u32[]{:S(2)}) collective-permute-start(bf16[512,2048]{1,0:T(8,128)(2,1)} %refs_0_.1), channel_id=1, source_target_pairs={{0,8},{4,12},{8,0},{12,4},{1,9},{5,13},{9,1},{13,5},{2,10},{6,14},... | collective-permute-start | bytes 6291464 | tf_op jit(solution)/shard_map/ppermute | solution.py:207
  3.7 50.0 %collective-permute-start = (bf16[512,2048]{1,0:T(8,128)(2,1)}, bf16[512,2048]{1,0:T(8,128)(2,1)}, u32[]{:S(2)}, u32[]{:S(2)}) collective-permute-start(bf16[512,2048]{1,0:T(8,128)(2,1)} %refs_0_), channel_id=1, source_target_pairs={{0,1},{1,0},{2,3},{3,2},{4,5},{5,4},{6,7},{7,6},{8,9},{9,8},{10,11... | collective-permute-start | bytes 6291464 | tf_op jit(solution)/shard_map/ppermute | solution.py:204
  5.3 48.4 %collective-permute-start.1 = (bf16[512,2048]{1,0:T(8,128)(2,1)}, bf16[512,2048]{1,0:T(8,128)(2,1)}, u32[]{:S(2)}, u32[]{:S(2)}) collective-permute-start(bf16[512,2048]{1,0:T(8,128)(2,1)} %refs_0_), channel_id=1, source_target_pairs={{1,2},{2,1},{5,6},{6,5},{9,10},{10,9},{13,14},{14,13},{17,18},{18,... | collective-permute-start | bytes 6291464 | tf_op jit(solution)/shard_map/ppermute | solution.py:204
  7.4 3.4 %copy-start = (bf16[2048,2048]{1,0:T(8,128)(2,1)S(1)}, bf16[2048,2048]{1,0:T(8,128)(2,1)}, u32[]{:S(2)}) copy-start(bf16[2048,2048]{1,0:T(8,128)(2,1)} %refs_1_.5) | copy-start | bytes 25165828
  17.9 32.4 %collective-permute-start.3 = (bf16[128,2048]{1,0:T(8,128)(2,1)S(1)}, bf16[128,2048]{1,0:T(8,128)(2,1)S(1)}, u32[]{:S(2)}, u32[]{:S(2)}) collective-permute-start(bf16[128,2048]{1,0:T(8,128)(2,1)S(1)} %get-tuple-element.82), channel_id=1, source_target_pairs={{0,4},{4,0},{8,12},{12,8},{1,5},{5,1},{9,13},{13,9},{2,6},{6,2},{1... | collective-permute-start | bytes 1572872 | tf_op jit(solution)/shard_map/ppermute | solution.py:207
  18.0 32.9 %collective-permute-start.4 = (bf16[128,2048]{1,0:T(8,128)(2,1)S(1)}, bf16[128,2048]{1,0:T(8,128)(2,1)S(1)}, u32[]{:S(2)}, u32[]{:S(2)}) collective-permute-start(bf16[128,2048]{1,0:T(8,128)(2,1)S(1)} %get-tuple-element.83), channel_id=1, source_target_pairs={{0,4},{4,0},{8,12},{12,8},{1,5},{5,1},{9,13},{13,9},{2,6},{6,2},{1... | collective-permute-start | bytes 1572872 | tf_op jit(solution)/shard_map/ppermute | solution.py:207
  50.3 3.4 %collective-permute-start.6 = (bf16[256,2048]{1,0:T(8,128)(2,1)S(1)}, bf16[256,2048]{1,0:T(8,128)(2,1)S(1)}, u32[]{:S(2)}, u32[]{:S(2)}) collective-permute-start(bf16[256,2048]{1,0:T(8,128)(2,1)S(1)} %get-tuple-element.163), channel_id=1, source_target_pairs={{0,4},{4,0},{8,12},{12,8},{1,5},{5,1},{9,13},{13,9},{2,6},{6,2},{1... | collective-permute-start | bytes 3145736 | tf_op jit(solution)/shard_map/ppermute | solution.py:207
  50.4 4.1 %collective-permute-start.7 = (bf16[256,2048]{1,0:T(8,128)(2,1)S(1)}, bf16[256,2048]{1,0:T(8,128)(2,1)S(1)}, u32[]{:S(2)}, u32[]{:S(2)}) collective-permute-start(bf16[256,2048]{1,0:T(8,128)(2,1)S(1)} %get-tuple-element.162), channel_id=1, source_target_pairs={{0,4},{4,0},{8,12},{12,8},{1,5},{5,1},{9,13},{13,9},{2,6},{6,2},{1... | collective-permute-start | bytes 3145736 | tf_op jit(solution)/shard_map/ppermute | solution.py:207
  50.9 8.9 %slice-start = ((s8[8388608]{0:T(1024)(128)(4,1)}), s8[4194304]{0:T(1024)(128)(4,1)S(1)}, s32[]{:S(2)}) async-start(s8[8388608]{0:T(1024)(128)(4,1)} %bitcast.119), calls=%async_computation | async-start | bytes 8388608
  50.9 8.9 %slice-start.1 = ((s8[8388608]{0:T(1024)(128)(4,1)}), s8[4194304]{0:T(1024)(128)(4,1)S(1)}, s32[]{:S(2)}) async-start(s8[8388608]{0:T(1024)(128)(4,1)} %bitcast.119), calls=%async_computation.1 | async-start | bytes 8388608
  54.5 13.6 %copy-start.4 = (bf16[256,2048]{1,0:T(8,128)(2,1)}, bf16[256,2048]{1,0:T(8,128)(2,1)S(1)}, u32[]{:S(2)}) copy-start(bf16[256,2048]{1,0:T(8,128)(2,1)S(1)} %collective-permute-done.7.refs_6_.refs_2_) | copy-start | bytes 3145732
  54.5 15.7 %copy-start.25 = (s32[512,16]{0,1:T(8,128)S(1)}, s32[512,16]{0,1:T(8,128)}, u32[]{:S(2)}) copy-start(s32[512,16]{0,1:T(8,128)} %param.7) | copy-start | bytes 98308
  54.5 53.8 %collective-permute-start.8 = (bf16[512,2048]{1,0:T(8,128)(2,1)}, bf16[512,2048]{1,0:T(8,128)(2,1)}, u32[]{:S(2)}, u32[]{:S(2)}) collective-permute-start(bf16[512,2048]{1,0:T(8,128)(2,1)} %collective-permute-done.refs_1_.refs_0_), channel_id=1, source_target_pairs={{1,2},{2,1},{5,6},{6,5},{9,10},{10,9},{13,14},{14,13},{17,18},{18,... | collective-permute-start | bytes 6291464 | tf_op jit(solution)/shard_map/ppermute | solution.py:204
  56.7 51.7 %collective-permute-start.9 = (bf16[512,2048]{1,0:T(8,128)(2,1)}, bf16[512,2048]{1,0:T(8,128)(2,1)}, u32[]{:S(2)}, u32[]{:S(2)}) collective-permute-start(bf16[512,2048]{1,0:T(8,128)(2,1)} %collective-permute-done.1.refs_0_), channel_id=1, source_target_pairs={{1,0},{2,3},{5,4},{6,7},{9,8},{10,11},{13,12},{14,15},{17,16},{18,... | collective-permute-start | bytes 6291464 | tf_op jit(solution)/shard_map/ppermute | solution.py:204
  57.9 25.6 %collective-permute-start.12 = (f32[128,2048]{1,0:T(8,128)}, f32[128,2048]{1,0:T(8,128)}, u32[]{:S(2)}, u32[]{:S(2)}) collective-permute-start(f32[128,2048]{1,0:T(8,128)} %get-tuple-element.93), channel_id=1, source_target_pairs={{0,8},{4,12},{8,0},{12,4},{1,9},{5,13},{9,1},{13,5},{2,10},{6,14},... | collective-permute-start | bytes 3145736 | tf_op jit(solution)/shard_map/ppermute | solution.py:207
  69.5 2.3 %collective-permute-start.10 = (bf16[128,2048]{1,0:T(8,128)(2,1)}, bf16[128,2048]{1,0:T(8,128)(2,1)}, u32[]{:S(2)}, u32[]{:S(2)}) collective-permute-start(bf16[128,2048]{1,0:T(8,128)(2,1)} %get-tuple-element.90), channel_id=1, source_target_pairs={{0,4},{4,0},{8,12},{12,8},{1,5},{5,1},{9,13},{13,9},{2,6},{6,2},{1... | collective-permute-start | bytes 1572872 | tf_op jit(solution)/shard_map/ppermute | solution.py:207
  69.5 3.0 %collective-permute-start.11 = (bf16[128,2048]{1,0:T(8,128)(2,1)}, bf16[128,2048]{1,0:T(8,128)(2,1)}, u32[]{:S(2)}, u32[]{:S(2)}) collective-permute-start(bf16[128,2048]{1,0:T(8,128)(2,1)} %get-tuple-element.91), channel_id=1, source_target_pairs={{0,4},{4,0},{8,12},{12,8},{1,5},{5,1},{9,13},{13,9},{2,6},{6,2},{1... | collective-permute-start | bytes 1572872 | tf_op jit(solution)/shard_map/ppermute | solution.py:207
  83.5 14.2 %collective-permute-start.15 = (bf16[128,2048]{1,0:T(8,128)(2,1)S(1)}, bf16[128,2048]{1,0:T(8,128)(2,1)S(1)}, u32[]{:S(2)}, u32[]{:S(2)}) collective-permute-start(bf16[128,2048]{1,0:T(8,128)(2,1)S(1)} %get-tuple-element.103), channel_id=1, source_target_pairs={{0,8},{4,12},{8,0},{12,4},{1,9},{5,13},{9,1},{13,5},{2,10},{6,14},... | collective-permute-start | bytes 1572872 | tf_op jit(solution)/shard_map/ppermute | solution.py:207
  85.3 3.4 %copy-start.1 = (bf16[2048,2048]{1,0:T(8,128)(2,1)S(1)}, bf16[2048,2048]{1,0:T(8,128)(2,1)}, u32[]{:S(2)}) copy-start(bf16[2048,2048]{1,0:T(8,128)(2,1)} %refs_1_.5) | copy-start | bytes 25165828
  88.7 14.6 %copy-start.2 = (bf16[512,2048]{1,0:T(8,128)(2,1)S(1)}, bf16[512,2048]{1,0:T(8,128)(2,1)}, u32[]{:S(2)}) copy-start(bf16[512,2048]{1,0:T(8,128)(2,1)} %refs_0_.1) | copy-start | bytes 6291460
  88.7 14.7 %copy-start.5 = (bf16[256,2048]{1,0:T(8,128)(2,1)S(1)}, bf16[256,2048]{1,0:T(8,128)(2,1)}, u32[]{:S(2)}) copy-start(bf16[256,2048]{1,0:T(8,128)(2,1)} %copy-done.4) | copy-start | bytes 3145732
  88.7 21.0 %slice-start.2 = ((s8[8388608]{0:T(1024)(128)(4,1)}), s8[4194304]{0:T(1024)(128)(4,1)S(1)}, s32[]{:S(2)}) async-start(s8[8388608]{0:T(1024)(128)(4,1)} %bitcast.121), calls=%async_computation.2 | async-start | bytes 8388608
  95.5 11.9 %collective-permute-start.13 = (bf16[128,2048]{1,0:T(8,128)(2,1)S(1)}, bf16[128,2048]{1,0:T(8,128)(2,1)S(1)}, u32[]{:S(2)}, u32[]{:S(2)}) collective-permute-start(bf16[128,2048]{1,0:T(8,128)(2,1)S(1)} %get-tuple-element.96), channel_id=1, source_target_pairs={{0,4},{4,0},{8,12},{12,8},{1,5},{5,1},{9,13},{13,9},{2,6},{6,2},{1... | collective-permute-start | bytes 1572872 | tf_op jit(solution)/shard_map/ppermute | solution.py:207
  95.6 11.9 %collective-permute-start.14 = (bf16[128,2048]{1,0:T(8,128)(2,1)S(1)}, bf16[128,2048]{1,0:T(8,128)(2,1)S(1)}, u32[]{:S(2)}, u32[]{:S(2)}) collective-permute-start(bf16[128,2048]{1,0:T(8,128)(2,1)S(1)} %get-tuple-element.97), channel_id=1, source_target_pairs={{0,4},{4,0},{8,12},{12,8},{1,5},{5,1},{9,13},{13,9},{2,6},{6,2},{1... | collective-permute-start | bytes 1572872 | tf_op jit(solution)/shard_map/ppermute | solution.py:207
  97.8 43.2 %copy-start.17 = (f32[4,512,128]{2,1,0:T(8,128)}, f32[4,512,128]{2,1,0:T(8,128)S(1)}, u32[]{:S(2)}) copy-start(f32[4,512,128]{2,1,0:T(8,128)S(1)} %convert_add_fusion.2) | copy-start | bytes 3145732
  97.8 10.5 %collective-permute-start.16 = (s32[512,16]{0,1:T(8,128)S(1)}, s32[512,16]{0,1:T(8,128)S(1)}, u32[]{:S(2)}, u32[]{:S(2)}) collective-permute-start(s32[512,16]{0,1:T(8,128)S(1)} %copy-done.25), channel_id=1, source_target_pairs={{0,3},{3,0},{4,7},{7,4},{8,11},{11,8},{12,15},{15,12},{16,19},{19,... | collective-permute-start | bytes 98312 | tf_op jit(solution)/shard_map/ppermute | solution.py:204
  103.3 6.3 %slice-start.3 = ((s8[8388608]{0:T(1024)(128)(4,1)}), s8[4194304]{0:T(1024)(128)(4,1)S(1)}, s32[]{:S(2)}) async-start(s8[8388608]{0:T(1024)(128)(4,1)} %bitcast.121), calls=%async_computation.3 | async-start | bytes 8388608
  108.4 49.4 %collective-permute-start.17 = (bf16[512,2048]{1,0:T(8,128)(2,1)}, bf16[512,2048]{1,0:T(8,128)(2,1)S(1)}, u32[]{:S(2)}, u32[]{:S(2)}) collective-permute-start(bf16[512,2048]{1,0:T(8,128)(2,1)} %collective-permute-done.8.refs_0_), channel_id=1, source_target_pairs={{1,0},{2,3},{5,4},{6,7},{9,8},{10,11},{13,12},{14,15},{17,16},{18,... | collective-permute-start | bytes 6291464 | tf_op jit(solution)/shard_map/ppermute | solution.py:204
  117.1 11.3 %copy-start.16 = (f32[128,2048]{1,0:T(8,128)S(1)}, f32[128,2048]{1,0:T(8,128)}, u32[]{:S(2)}) copy-start(f32[128,2048]{1,0:T(8,128)} %copy-done.15) | copy-start | bytes 3145732
  117.1 2.0 collective-permute-start.18
  117.1 2.6 %collective-permute-start.19 = (bf16[128,2048]{1,0:T(8,128)(2,1)S(1)}, bf16[128,2048]{1,0:T(8,128)(2,1)S(1)}, u32[]{:S(2)}, u32[]{:S(2)}) collective-permute-start(bf16[128,2048]{1,0:T(8,128)(2,1)S(1)} %get-tuple-element.121), channel_id=1, source_target_pairs={{0,4},{4,0},{8,12},{12,8},{1,5},{5,1},{9,13},{13,9},{2,6},{6,2},{1... | collective-permute-start | bytes 1572872 | tf_op jit(solution)/shard_map/ppermute | solution.py:207
  120.6 14.8 %collective-permute-start.25 = (bf16[128,2048]{1,0:T(8,128)(2,1)S(1)}, bf16[128,2048]{1,0:T(8,128)(2,1)S(1)}, u32[]{:S(2)}, u32[]{:S(2)}) collective-permute-start(bf16[128,2048]{1,0:T(8,128)(2,1)S(1)} %get-tuple-element.128), channel_id=1, source_target_pairs={{0,8},{4,12},{8,0},{12,4},{1,9},{5,13},{9,1},{13,5},{2,10},{6,14},... | collective-permute-start | bytes 1572872 | tf_op jit(solution)/shard_map/ppermute | solution.py:207
  121.7 19.2 %collective-permute-start.20 = (bf16[4,512,128]{2,1,0:T(8,128)(2,1)S(1)}, bf16[4,512,128]{2,1,0:T(8,128)(2,1)S(1)}, u32[]{:S(2)}, u32[]{:S(2)}) collective-permute-start(bf16[4,512,128]{2,1,0:T(8,128)(2,1)S(1)} %scores.4), channel_id=1, source_target_pairs={{0,1},{3,2},{4,5},{7,6},{8,9},{11,10},{12,13},{15,14},{16,17},{19,... | collective-permute-start | bytes 1572872 | tf_op jit(solution)/shard_map/ppermute | solution.py:204
  126.4 14.5 %collective-permute-start.21 = (bf16[4,512,128]{2,1,0:T(8,128)(2,1)S(1)}, bf16[4,512,128]{2,1,0:T(8,128)(2,1)S(1)}, u32[]{:S(2)}, u32[]{:S(2)}) collective-permute-start(bf16[4,512,128]{2,1,0:T(8,128)(2,1)S(1)} %scores.4), channel_id=1, source_target_pairs={{1,2},{2,1},{5,6},{6,5},{9,10},{10,9},{13,14},{14,13},{17,18},{18,... | collective-permute-start | bytes 1572872 | tf_op jit(solution)/shard_map/ppermute | solution.py:204
  127.3 19.4 %collective-permute-start.27 = (bf16[128,2048]{1,0:T(8,128)(2,1)S(1)}, bf16[128,2048]{1,0:T(8,128)(2,1)S(1)}, u32[]{:S(2)}, u32[]{:S(2)}) collective-permute-start(bf16[128,2048]{1,0:T(8,128)(2,1)S(1)} %get-tuple-element.130), channel_id=1, source_target_pairs={{0,8},{4,12},{8,0},{12,4},{1,9},{5,13},{9,1},{13,5},{2,10},{6,14},... | collective-permute-start | bytes 1572872 | tf_op jit(solution)/shard_map/ppermute | solution.py:207
  140.2 16.3 %collective-permute-start.26 = (bf16[4,512,128]{2,1,0:T(8,128)(2,1)}, bf16[4,512,128]{2,1,0:T(8,128)(2,1)S(1)}, u32[]{:S(2)}, u32[]{:S(2)}) collective-permute-start(bf16[4,512,128]{2,1,0:T(8,128)(2,1)} %scores.6), channel_id=1, source_target_pairs={{1,2},{2,1},{5,6},{6,5},{9,10},{10,9},{13,14},{14,13},{17,18},{18,... | collective-permute-start | bytes 1572872 | tf_op jit(solution)/shard_map/ppermute | solution.py:204
  141.5 11.8 %collective-permute-start.22 = (f32[520,128]{1,0:T(8,128)S(1)}, f32[520,128]{1,0:T(8,128)S(1)}, u32[]{:S(2)}, u32[]{:S(2)}) collective-permute-start(f32[520,128]{1,0:T(8,128)S(1)} %get-tuple-element.226), channel_id=1, source_target_pairs={{0,4},{4,0},{8,12},{12,8},{1,5},{5,1},{9,13},{13,9},{2,6},{6,2},{1... | collective-permute-start | bytes 798728 | tf_op jit(solution)/shard_map/ppermute | solution.py:207
  141.5 11.7 %collective-permute-start.23 = (f32[520,128]{1,0:T(8,128)S(1)}, f32[520,128]{1,0:T(8,128)S(1)}, u32[]{:S(2)}, u32[]{:S(2)}) collective-permute-start(f32[520,128]{1,0:T(8,128)S(1)} %get-tuple-element.227), channel_id=1, source_target_pairs={{0,8},{4,12},{8,0},{12,4},{1,9},{5,13},{9,1},{13,5},{2,10},{6,14},... | collective-permute-start | bytes 798728 | tf_op jit(solution)/shard_map/ppermute | solution.py:207
  146.7 9.8 %collective-permute-start.24 = (f32[520,128]{1,0:T(8,128)S(1)}, f32[520,128]{1,0:T(8,128)S(1)}, u32[]{:S(2)}, u32[]{:S(2)}) collective-permute-start(f32[520,128]{1,0:T(8,128)S(1)} %get-tuple-element.225), channel_id=1, source_target_pairs={{0,12},{4,8},{8,4},{12,0},{1,13},{5,9},{9,5},{13,1},{2,14},{6,10},... | collective-permute-start | bytes 798728 | tf_op jit(solution)/shard_map/ppermute | solution.py:207
  153.2 10.2 %copy-start.19 = (f32[520,128]{1,0:T(8,128)}, f32[520,128]{1,0:T(8,128)S(1)}, u32[]{:S(2)}) copy-start(f32[520,128]{1,0:T(8,128)S(1)} %collective-permute-done.22) | copy-start | bytes 798724
  153.3 4.6 %copy-start.21 = (f32[520,128]{1,0:T(8,128)}, f32[520,128]{1,0:T(8,128)S(1)}, u32[]{:S(2)}) copy-start(f32[520,128]{1,0:T(8,128)S(1)} %collective-permute-done.23) | copy-start | bytes 798724
  163.4 2.0 collective-permute-start.28
  163.8 2.4 %collective-permute-start.29 = (bf16[128,2048]{1,0:T(8,128)(2,1)S(1)}, bf16[128,2048]{1,0:T(8,128)(2,1)S(1)}, u32[]{:S(2)}, u32[]{:S(2)}) collective-permute-start(bf16[128,2048]{1,0:T(8,128)(2,1)S(1)} %get-tuple-element.139), channel_id=1, source_target_pairs={{0,4},{4,0},{8,12},{12,8},{1,5},{5,1},{9,13},{13,9},{2,6},{6,2},{1... | collective-permute-start | bytes 1572872 | tf_op jit(solution)/shard_map/ppermute | solution.py:207
  168.8 14.4 %collective-permute-start.30 = (bf16[128,2048]{1,0:T(8,128)(2,1)}, bf16[128,2048]{1,0:T(8,128)(2,1)}, u32[]{:S(2)}, u32[]{:S(2)}) collective-permute-start(bf16[128,2048]{1,0:T(8,128)(2,1)} %get-tuple-element.141), channel_id=1, source_target_pairs={{0,8},{4,12},{8,0},{12,4},{1,9},{5,13},{9,1},{13,5},{2,10},{6,14},... | collective-permute-start | bytes 1572872 | tf_op jit(solution)/shard_map/ppermute | solution.py:207
  170.7 30.6 %collective-permute-start.33 = (bf16[4,512,128]{2,1,0:T(8,128)(2,1)}, bf16[4,512,128]{2,1,0:T(8,128)(2,1)}, u32[]{:S(2)}, u32[]{:S(2)}) collective-permute-start(bf16[4,512,128]{2,1,0:T(8,128)(2,1)} %add_convert_fusion), channel_id=1, source_target_pairs={{1,0},{2,3},{5,4},{6,7},{9,8},{10,11},{13,12},{14,15},{17,16},{18,... | collective-permute-start | bytes 1572872 | tf_op jit(solution)/shard_map/ppermute | solution.py:204
  172.0 29.3 %collective-permute-start.32 = (bf16[4,512,128]{2,1,0:T(8,128)(2,1)}, bf16[4,512,128]{2,1,0:T(8,128)(2,1)}, u32[]{:S(2)}, u32[]{:S(2)}) collective-permute-start(bf16[4,512,128]{2,1,0:T(8,128)(2,1)} %scores.6), channel_id=1, source_target_pairs={{0,2},{3,1},{4,6},{7,5},{8,10},{11,9},{12,14},{15,13},{16,18},{19,... | collective-permute-start | bytes 1572872 | tf_op jit(solution)/shard_map/ppermute | solution.py:204
  186.9 7.4 %copy-start.20 = (f32[520,128]{1,0:T(8,128)S(1)}, f32[520,128]{1,0:T(8,128)}, u32[]{:S(2)}) copy-start(f32[520,128]{1,0:T(8,128)} %copy-done.19) | copy-start | bytes 798724
  186.9 7.4 %copy-start.22 = (f32[520,128]{1,0:T(8,128)S(1)}, f32[520,128]{1,0:T(8,128)}, u32[]{:S(2)}) copy-start(f32[520,128]{1,0:T(8,128)} %copy-done.21) | copy-start | bytes 798724
  186.9 7.4 %copy-start.24 = (f32[520,128]{1,0:T(8,128)S(1)}, f32[520,128]{1,0:T(8,128)}, u32[]{:S(2)}) copy-start(f32[520,128]{1,0:T(8,128)} %copy-done.23) | copy-start | bytes 798724
  189.3 5.2 %copy-start.3 = (bf16[512,2048]{1,0:T(8,128)(2,1)S(1)}, bf16[512,2048]{1,0:T(8,128)(2,1)}, u32[]{:S(2)}) copy-start(bf16[512,2048]{1,0:T(8,128)(2,1)} %refs_0_.1) | copy-start | bytes 6291460
  189.3 5.2 %copy-start.8 = (f32[4,512,128]{2,1,0:T(8,128)S(1)}, f32[4,512,128]{2,1,0:T(8,128)}, u32[]{:S(2)}) copy-start(f32[4,512,128]{2,1,0:T(8,128)} %convert_add_fusion.counts) | copy-start | bytes 3145732
  189.3 5.2 %copy-start.11 = (f32[128,2048]{1,0:T(8,128)S(1)}, f32[128,2048]{1,0:T(8,128)}, u32[]{:S(2)}) copy-start(f32[128,2048]{1,0:T(8,128)} %copy-done.9) | copy-start | bytes 3145732
  189.3 11.9 %collective-permute-start.31 = (bf16[2,512,128]{2,1,0:T(8,128)(2,1)S(1)}, bf16[2,512,128]{2,1,0:T(8,128)(2,1)S(1)}, u32[]{:S(2)}, u32[]{:S(2)}) collective-permute-start(bf16[2,512,128]{2,1,0:T(8,128)(2,1)S(1)} %get-tuple-element.146), channel_id=1, source_target_pairs={{0,3},{3,0},{4,7},{7,4},{8,11},{11,8},{12,15},{15,12},{16,19},{19,... | collective-permute-start | bytes 786440 | tf_op jit(solution)/shard_map/ppermute | solution.py:204
  194.5 6.8 %copy-start.18 = (f32[4,512,128]{2,1,0:T(8,128)S(1)}, f32[4,512,128]{2,1,0:T(8,128)}, u32[]{:S(2)}) copy-start(f32[4,512,128]{2,1,0:T(8,128)} %copy-done.17) | copy-start | bytes 3145732
  198.2 11.3 %collective-permute-start.37 = (bf16[2,528,128]{2,1,0:T(8,128)(2,1)S(1)}, bf16[2,528,128]{2,1,0:T(8,128)(2,1)S(1)}, u32[]{:S(2)}, u32[]{:S(2)}) collective-permute-start(bf16[2,528,128]{2,1,0:T(8,128)(2,1)S(1)} %get-tuple-element.156), channel_id=1, source_target_pairs={{0,3},{3,0},{4,7},{7,4},{8,11},{11,8},{12,15},{15,12},{16,19},{19,... | collective-permute-start | bytes 811016 | tf_op jit(solution)/shard_map/ppermute | solution.py:204
  202.9 6.7 %collective-permute-start.34 = (bf16[528,128]{1,0:T(8,128)(2,1)S(1)}, bf16[528,128]{1,0:T(8,128)(2,1)S(1)}, u32[]{:S(2)}, u32[]{:S(2)}) collective-permute-start(bf16[528,128]{1,0:T(8,128)(2,1)S(1)} %get-tuple-element.222), channel_id=1, source_target_pairs={{0,8},{4,12},{8,0},{12,4},{1,9},{5,13},{9,1},{13,5},{2,10},{6,14},... | collective-permute-start | bytes 405512 | tf_op jit(solution)/shard_map/ppermute | solution.py:207
  204.0 7.2 %collective-permute-start.35 = (bf16[528,128]{1,0:T(8,128)(2,1)S(1)}, bf16[528,128]{1,0:T(8,128)(2,1)S(1)}, u32[]{:S(2)}, u32[]{:S(2)}) collective-permute-start(bf16[528,128]{1,0:T(8,128)(2,1)S(1)} %get-tuple-element.223), channel_id=1, source_target_pairs={{0,4},{4,0},{8,12},{12,8},{1,5},{5,1},{9,13},{13,9},{2,6},{6,2},{1... | collective-permute-start | bytes 405512 | tf_op jit(solution)/shard_map/ppermute | solution.py:207
  204.0 8.7 %collective-permute-start.36 = (bf16[528,128]{1,0:T(8,128)(2,1)S(1)}, bf16[528,128]{1,0:T(8,128)(2,1)S(1)}, u32[]{:S(2)}, u32[]{:S(2)}) collective-permute-start(bf16[528,128]{1,0:T(8,128)(2,1)S(1)} %get-tuple-element.224), channel_id=1, source_target_pairs={{0,12},{4,8},{8,4},{12,0},{1,13},{5,9},{9,5},{13,1},{2,14},{6,10},... | collective-permute-start | bytes 405512 | tf_op jit(solution)/shard_map/ppermute | solution.py:207
  205.1 12.1 %collective-permute-start.38 = (bf16[512,128]{1,0:T(8,128)(2,1)S(1)}, bf16[512,128]{1,0:T(8,128)(2,1)S(1)}, u32[]{:S(2)}, u32[]{:S(2)}) collective-permute-start(bf16[512,128]{1,0:T(8,128)(2,1)S(1)} %get-tuple-element.188), channel_id=1, source_target_pairs={{0,8},{4,12},{8,0},{12,4},{1,9},{5,13},{9,1},{13,5},{2,10},{6,14},... | collective-permute-start | bytes 393224 | tf_op jit(solution)/shard_map/ppermute | solution.py:207
  209.6 7.7 %collective-permute-start.40 = (bf16[512,128]{1,0:T(8,128)(2,1)S(1)}, bf16[512,128]{1,0:T(8,128)(2,1)S(1)}, u32[]{:S(2)}, u32[]{:S(2)}) collective-permute-start(bf16[512,128]{1,0:T(8,128)(2,1)S(1)} %get-tuple-element.189), channel_id=1, source_target_pairs={{0,12},{4,8},{8,4},{12,0},{1,13},{5,9},{9,5},{13,1},{2,14},{6,10},... | collective-permute-start | bytes 393224 | tf_op jit(solution)/shard_map/ppermute | solution.py:207
  209.6 7.0 %collective-permute-start.41 = (bf16[16,128]{1,0:T(8,128)(2,1)S(1)}, bf16[16,128]{1,0:T(8,128)(2,1)S(1)}, u32[]{:S(2)}, u32[]{:S(2)}) collective-permute-start(bf16[16,128]{1,0:T(8,128)(2,1)S(1)} %slice_bitcast_fusion.12), channel_id=1, source_target_pairs={{0,8},{4,12},{8,0},{12,4},{1,9},{5,13},{9,1},{13,5},{2,10},{6,14},... | collective-permute-start | bytes 12296 | tf_op jit(solution)/shard_map/ppermute | solution.py:207
  211.2 5.4 %collective-permute-start.42 = (bf16[16,128]{1,0:T(8,128)(2,1)S(1)}, bf16[16,128]{1,0:T(8,128)(2,1)S(1)}, u32[]{:S(2)}, u32[]{:S(2)}) collective-permute-start(bf16[16,128]{1,0:T(8,128)(2,1)S(1)} %slice_bitcast_fusion.12), channel_id=1, source_target_pairs={{0,12},{4,8},{8,4},{12,0},{1,13},{5,9},{9,5},{13,1},{2,14},{6,10},... | collective-permute-start | bytes 12296 | tf_op jit(solution)/shard_map/ppermute | solution.py:207
  212.7 4.0 %collective-permute-start.39 = (bf16[528,128]{1,0:T(8,128)(2,1)S(1)}, bf16[528,128]{1,0:T(8,128)(2,1)S(1)}, u32[]{:S(2)}, u32[]{:S(2)}) collective-permute-start(bf16[528,128]{1,0:T(8,128)(2,1)S(1)} %slice_bitcast_fusion.4), channel_id=1, source_target_pairs={{0,4},{4,0},{8,12},{12,8},{1,5},{5,1},{9,13},{13,9},{2,6},{6,2},{1... | collective-permute-start | bytes 405512 | tf_op jit(solution)/shard_map/ppermute | solution.py:207
  (9 other events, 11.6 us)

commit v14 on v11

--- a/solution.py
+++ b/solution.py
@@ -40,7 +40,7 @@
 
 SMALL = pl.CostEstimate(flops=1, bytes_accessed=1, transcendentals=0)
 SOME = pl.CostEstimate(flops=2 * 10**9, bytes_accessed=2**20, transcendentals=0)
-MORE = pl.CostEstimate(flops=5 * 10**9, bytes_accessed=2**20, transcendentals=0)
+MORE = pl.CostEstimate(flops=7 * 10**9, bytes_accessed=2**20, transcendentals=0)
 PARAMS = pltpu.CompilerParams(vmem_limit_bytes=12 * 2**20)
 
 
@@ -234,12 +234,11 @@
     other_core, other_chip = to_other(train_grads, 1), to_other(train_grads, 2)
     own, other_core = tied(test_grads, other_core)
     own, own_sent = core_sum(*product(flags, [own], fisher), sent_as=F32, cost=MORE)
-    counts = selected(chosen_ids)
     half = own_rows // 2
     other_both = [to_other(other_chip[:half], 1), to_other(other_chip[half:], 1)]
     grads = [train_grads, other_core, other_chip, *other_both]
-    pair_in, middle_in, own, own_sent, counts, chosen_ids, grads = tied(
-        pair_in, middle_in, own, own_sent, counts, chosen_ids, grads
+    pair_in, middle_in, own, own_sent, chosen_ids, grads = tied(
+        pair_in, middle_in, own, own_sent, chosen_ids, grads
     )
     places = ((0, 0), (1, 0), (2, 0), (3, 0), (3, half))
 
@@ -252,8 +251,9 @@
     third, third_sent = core_sum(*product(flags, [pair_in], fisher))
     (near,) = scores_of((near, near_got), cost=SOME)
     far_ids = along(chosen_ids, [(0, 3), (3, 0)])
-    far_in, second_edge, third, third_sent, own, own_got, near, far_ids, grads = tied(
-        far_in, second_edge, third, third_sent, own, own_got, near, far_ids, grads
+    counts = selected(chosen_ids)
+    far_in, second_edge, third, third_sent, own, own_got, near, far_ids, counts, grads = tied(
+        far_in, second_edge, third, third_sent, own, own_got, near, far_ids, counts, grads
     )
 
     first_edge = along(far_in, outward)

time: 212 us -> 212 us (level)
  waiting for transfers between devices: 91.5 us -> 78.1 us
  local copies, waits for them, and re-layouts: 5.94 us -> 12.7 us
  Pallas kernels: 53.9 us -> 58.9 us
    ppermute x27, waiting for transfers between devices: 79.2 us -> 69.6 us  [to_other(): return lax.ppermute(value, 'train', [(k, k ^ r) for k in range(4)])]
    unnamed x12 -> x30, local copies, waits for them, and re-layouts: 4.98 us -> 11.4 us
    ppermute x13, waiting for transfers between devices: 12.3 us -> 8.49 us  [along(): return lax.ppermute(value, 'test', pairs)]
    pallas_call x5, Pallas kernels: 30.8 us -> 33.7 us  [product(): pl.pallas_call(functools.partial(product_body, len(blocks)), in_specs=[pl...]
  transfers between devices with their start and end apart: 40 -> 40, of which waited for: 22 -> 21; matrix products, arithmetic and copies ran while one was open for 3% -> 3% of each run, Pallas kernels for 22% -> 25%
where the time goes in v14:
time: 212 us; the launch traced here: 211 us
  waiting for transfers between devices  78.1 us (37%)
  Pallas kernels  58.9 us (28%)
  starting transfers between devices  54.4 us (26%)
  local copies, waits for them, and re-layouts  12.7 us (6%)
  other arithmetic  6.08 us (3%)
    ppermute x27, waiting for transfers between devices, to_other(): return lax.ppermute(value, 'train', [(k, k ^ r) for k in range(4)])  69.6 us
    ppermute x13, starting transfers between devices, along(): return lax.ppermute(value, 'test', pairs)  35.4 us
    pallas_call x5, Pallas kernels, product(): pl.pallas_call(functools.partial(product_body, len(blocks)), in_specs=[pl...  33.7 us
    ppermute x27, starting transfers between devices, to_other(): return lax.ppermute(value, 'train', [(k, k ^ r) for k in range(4)])  19 us
    pallas_call x3, Pallas kernels, partial_scores(): pl.pallas_call(functools.partial(scores_body, [piece[:2] for piece in gra...  14.6 us
    unnamed x30, local copies, waits for them, and re-layouts  11.4 us
    ppermute x13, waiting for transfers between devices, along(): return lax.ppermute(value, 'test', pairs)  8.49 us
    pallas_call x5, Pallas kernels, fold(): pl.pallas_call(fold_body, in_specs=[pl.BlockSpec(memory_space=pltpu.SMEM)...  5.8 us
  transfers between devices with their start and end apart: 40, of which 21 were waited for; matrix products, arithmetic and copies ran while one was open for 3% of the time, Pallas kernels for 25%

profile of v14, /device:TPU:0, one launch (start us, length us, event | category | flops | bytes accessed | tf_op | source)
XLA Modules:
  0.0 211.2 jit_solution(686724940329805784)
XLA Ops:
  1.1 2.6 %collective-permute-start.5 = (bf16[512,2048]{1,0:T(8,128)(2,1)}, bf16[512,2048]{1,0:T(8,128)(2,1)S(1)}, u32[]{:S(2)}, u32[]{:S(2)}) collective-permute-start(bf16[512,2048]{1,0:T(8,128)(2,1)} %refs_0_.1), channel_id=1, source_target_pairs={{0,8},{4,12},{8,0},{12,4},{1,9},{5,13},{9,1},{13,5},{2,10},{6,14},... | collective-permute-start | bytes 6291464 | tf_op jit(solution)/shard_map/ppermute | solution.py:203
  3.7 1.6 collective-permute-start
  5.3 2.0 collective-permute-start.1
  7.4 3.4 %copy-done = bf16[2048,2048]{1,0:T(8,128)(2,1)S(1)} copy-done((bf16[2048,2048]{1,0:T(8,128)(2,1)S(1)}, bf16[2048,2048]{1,0:T(8,128)(2,1)}, u32[]{:S(2)}) %copy-start) | copy-done | bytes 8388632
  10.8 1.6 copy-done.7
  12.4 5.6 %product.5 = (f32[256,2048]{1,0:T(8,128)S(1)}, bf16[128,2048]{1,0:T(8,128)(2,1)S(1)}, bf16[128,2048]{1,0:T(8,128)(2,1)S(1)}) custom-call(s32[3]{0:T(128)S(1)} %pad_add_fusion.flags, bf16[512,2048]{1,0:T(8,128)(2,1)S(1)} %copy-done.7, bf16[2048,2048]{1,0:T(8,128)(2,1)S(1)} %copy-done), custom_call_target="tpu_custom_call" | custom-call | flops 1 | bytes 1 | tf_op jit(solution)/shard_map/product/pallas_call | solution.py:80
  18.5 31.6 %collective-permute-done.5.refs_4_.refs_6_.refs_0_ = bf16[512,2048]{1,0:T(8,128)(2,1)S(1)} collective-permute-done((bf16[512,2048]{1,0:T(8,128)(2,1)}, bf16[512,2048]{1,0:T(8,128)(2,1)S(1)}, u32[]{:S(2)}, u32[]{:S(2)}) %collective-permute-start.5) | collective-permute-done | bytes 2097184 | tf_op jit(solution)/shard_map/ppermute | solution.py:203
  50.9 1.8 fold.5
  53.0 1.5 collective-permute-done.7.refs_6_.refs_8_.refs_2_
  54.5 2.2 %collective-permute-start.8 = (bf16[512,2048]{1,0:T(8,128)(2,1)}, bf16[512,2048]{1,0:T(8,128)(2,1)}, u32[]{:S(2)}, u32[]{:S(2)}) collective-permute-start(bf16[512,2048]{1,0:T(8,128)(2,1)} %collective-permute-done.refs_1_.refs_0_), channel_id=1, source_target_pairs={{1,2},{2,1},{5,6},{6,5},{9,10},{10,9},{13,14},{14,13},{17,18},{18,... | collective-permute-start | bytes 6291464 | tf_op jit(solution)/shard_map/ppermute | solution.py:200
  56.7 1.3 collective-permute-start.9
  58.0 1.8 collective-permute-start.12
  59.8 8.3 %product.6 = (f32[256,2048]{1,0:T(8,128)S(1)}, bf16[128,2048]{1,0:T(8,128)(2,1)}, bf16[128,2048]{1,0:T(8,128)(2,1)}) custom-call(s32[3]{0:T(128)S(1)} %pad_add_fusion.flags, bf16[512,2048]{1,0:T(8,128)(2,1)} %collective-permute-done.1.refs_0_, bf16[512,2048]{1,0:T(8,128)(2,1)} %collective-permute-done.refs_1_.refs_0_, bf16[2048,2048]{1,0:T(8,128)(2,1)S(1)} %bitcast.115), custom_call_target="tpu_custom_call" | custom-call | flops 1 | bytes 1 | tf_op jit(solution)/shard_map/product/pallas_call | solution.py:80
  68.2 1.4 copy-done.5
  70.3 1.6 collective-permute-done.10.refs_0_
  71.9 0.7 collective-permute-done.11.refs_1_
  72.6 1.6 copy-done.6
  74.2 1.5 fold.6
  75.8 7.8 %collective-permute-done.12.refs_3_ = f32[128,2048]{1,0:T(8,128)} collective-permute-done((f32[128,2048]{1,0:T(8,128)}, f32[128,2048]{1,0:T(8,128)}, u32[]{:S(2)}, u32[]{:S(2)}) %collective-permute-start.12) | collective-permute-done | bytes 1048608 | tf_op jit(solution)/shard_map/ppermute | solution.py:203
  83.6 1.7 collective-permute-start.15
  85.3 3.4 %copy-done.1 = bf16[2048,2048]{1,0:T(8,128)(2,1)S(1)} copy-done((bf16[2048,2048]{1,0:T(8,128)(2,1)S(1)}, bf16[2048,2048]{1,0:T(8,128)(2,1)}, u32[]{:S(2)}) %copy-start.1) | copy-done | bytes 8388632
  88.7 6.9 %product.7 = (f32[256,2048]{1,0:T(8,128)S(1)}, bf16[128,2048]{1,0:T(8,128)(2,1)S(1)}, bf16[128,2048]{1,0:T(8,128)(2,1)S(1)}) custom-call(s32[3]{0:T(128)S(1)} %pad_add_fusion.flags, bf16[512,2048]{1,0:T(8,128)(2,1)} %collective-permute-done.refs_1_.refs_0_, bf16[2048,2048]{1,0:T(8,128)(2,1)S(1)} %copy-done.1), custom_call_target="tpu_custom_call" | custom-call | flops 1 | bytes 1 | tf_op jit(solution)/shard_map/product/pallas_call | solution.py:80
  96.2 1.7 convert_add_fusion.1
  97.8 5.5 %collective-permute-start.16 = (s32[512,16]{0,1:T(8,128)S(1)}, s32[512,16]{0,1:T(8,128)S(1)}, u32[]{:S(2)}, u32[]{:S(2)}) collective-permute-start(s32[512,16]{0,1:T(8,128)S(1)} %copy-done.10), channel_id=1, source_target_pairs={{0,3},{3,0},{4,7},{7,4},{8,11},{11,8},{12,15},{15,12},{16,19},{19,... | collective-permute-start | bytes 98312 | tf_op jit(solution)/shard_map/ppermute | solution.py:200
  103.4 4.1 %scores.3 = bf16[4,512,128]{2,1,0:T(8,128)(2,1)S(1)} custom-call(f32[128,2048]{1,0:T(8,128)S(1)} %get-tuple-element.105.refs_0_, bf16[128,2048]{1,0:T(8,128)(2,1)S(1)} %collective-permute-done.15.refs_1_, bf16[512,2048]{1,0:T(8,128)(2,1)S(1)} %copy-done.2, bf16[512,2048]{1,0:T(8,128)(2,1)} %collective-permute-done.2.refs_3_.refs_5_.refs_1_, ...), custom_call_target="tpu_custom_call" | custom-call | flops 2000000000 | bytes 1048576 | tf_op jit(solution)/shard_map/scores/pallas_call | solution.py:144
  107.5 0.8 fold.7
  108.4 1.3 collective-permute-start.17
  109.7 7.3 %product.8 = (f32[256,2048]{1,0:T(8,128)S(1)}, bf16[128,2048]{1,0:T(8,128)(2,1)S(1)}, bf16[128,2048]{1,0:T(8,128)(2,1)S(1)}) custom-call(s32[3]{0:T(128)S(1)} %pad_add_fusion.flags, bf16[512,2048]{1,0:T(8,128)(2,1)} %collective-permute-done.8.refs_0_, bf16[512,2048]{1,0:T(8,128)(2,1)} %collective-permute-done.9.refs_1_, bf16[2048,2048]{1,0:T(8,128)(2,1)S(1)} %bitcast.117), custom_call_target="tpu_custom_call" | custom-call | flops 1 | bytes 1 | tf_op jit(solution)/shard_map/product/pallas_call | solution.py:80
  117.7 1.4 collective-permute-done.19.refs_0_
  119.1 0.7 collective-permute-done.20.refs_1_
  119.8 0.8 fold.8
  120.6 1.1 collective-permute-start.21
  121.7 4.7 %collective-permute-start.22 = (bf16[4,512,128]{2,1,0:T(8,128)(2,1)S(1)}, bf16[4,512,128]{2,1,0:T(8,128)(2,1)S(1)}, u32[]{:S(2)}, u32[]{:S(2)}) collective-permute-start(bf16[4,512,128]{2,1,0:T(8,128)(2,1)S(1)} %scores.3), channel_id=1, source_target_pairs={{0,1},{3,2},{4,5},{7,6},{8,9},{11,10},{12,13},{15,14},{16,17},{19,... | collective-permute-start | bytes 1572872 | tf_op jit(solution)/shard_map/ppermute | solution.py:200
  126.4 0.9 collective-permute-start.23
  127.3 1.1 collective-permute-start.18
  128.4 7.1 %collective-permute-done.21.refs_1_ = bf16[128,2048]{1,0:T(8,128)(2,1)S(1)} collective-permute-done((bf16[128,2048]{1,0:T(8,128)(2,1)S(1)}, bf16[128,2048]{1,0:T(8,128)(2,1)S(1)}, u32[]{:S(2)}, u32[]{:S(2)}) %collective-permute-start.21) | collective-permute-done | bytes 524320 | tf_op jit(solution)/shard_map/ppermute | solution.py:203
  135.5 2.1 collective-permute-done.22
  137.6 4.0 %scores.5 = bf16[4,512,128]{2,1,0:T(8,128)(2,1)S(1)} custom-call(f32[128,2048]{1,0:T(8,128)S(1)} %get-tuple-element.135.refs_0_, bf16[128,2048]{1,0:T(8,128)(2,1)S(1)} %collective-permute-done.21.refs_1_, bf16[512,2048]{1,0:T(8,128)(2,1)S(1)} %copy-done.2, bf16[512,2048]{1,0:T(8,128)(2,1)} %collective-permute-done.2.refs_3_.refs_5_.refs_1_, ...), custom_call_target="tpu_custom_call" | custom-call | flops 1 | bytes 1 | tf_op jit(solution)/shard_map/scores/pallas_call | solution.py:144
  141.5 0.7 collective-permute-start.24
  142.3 1.7 convert_add_fusion.counts
  143.9 2.0 collective-permute-done.18.refs_1_
  145.9 6.5 %scores.4 = (f32[4,512,128]{2,1,0:T(8,128)S(1)}, f32[4,512,128]{2,1,0:T(8,128)S(1)}) custom-call(f32[128,2048]{1,0:T(8,128)S(1)} %get-tuple-element.114.refs_0_, bf16[128,2048]{1,0:T(8,128)(2,1)S(1)} %collective-permute-done.18.refs_1_, f32[128,2048]{1,0:T(8,128)S(1)} %copy-done.9, f32[128,2048]{1,0:T(8,128)} %collective-permute-done.12.refs_3_, ...), custom_call_target="tpu_custom_call" | custom-call | flops 1 | bytes 1 | tf_op jit(solution)/shard_map/scores/pallas_call | solution.py:144
  152.4 5.4 %collective-permute-done.17.refs_0_ = bf16[512,2048]{1,0:T(8,128)(2,1)S(1)} collective-permute-done((bf16[512,2048]{1,0:T(8,128)(2,1)}, bf16[512,2048]{1,0:T(8,128)(2,1)S(1)}, u32[]{:S(2)}, u32[]{:S(2)}) %collective-permute-start.17) | collective-permute-done | bytes 2097184 | tf_op jit(solution)/shard_map/ppermute | solution.py:200
  157.8 5.6 %product.9 = (f32[256,2048]{1,0:T(8,128)S(1)}, bf16[128,2048]{1,0:T(8,128)(2,1)S(1)}, bf16[128,2048]{1,0:T(8,128)(2,1)S(1)}) custom-call(s32[3]{0:T(128)S(1)} %pad_add_fusion.flags, bf16[512,2048]{1,0:T(8,128)(2,1)S(1)} %collective-permute-done.17.refs_0_, bf16[2048,2048]{1,0:T(8,128)(2,1)S(1)} %bitcast.117), custom_call_target="tpu_custom_call" | custom-call | flops 1 | bytes 1 | tf_op jit(solution)/shard_map/product/pallas_call | solution.py:80
  164.0 1.4 collective-permute-done.25.refs_0_
  165.4 0.7 collective-permute-done.26.refs_1_
  166.1 0.8 fold.9
  167.0 0.6 collective-permute-start.27
  167.7 1.3 collective-permute-start.29
  169.0 6.4 %collective-permute-start.28 = (bf16[4,512,128]{2,1,0:T(8,128)(2,1)S(1)}, bf16[4,512,128]{2,1,0:T(8,128)(2,1)S(1)}, u32[]{:S(2)}, u32[]{:S(2)}) collective-permute-start(bf16[4,512,128]{2,1,0:T(8,128)(2,1)S(1)} %scores.5), channel_id=1, source_target_pairs={{0,2},{3,1},{4,6},{7,5},{8,10},{11,9},{12,14},{15,13},{16,18},{19,... | collective-permute-start | bytes 1572872 | tf_op jit(solution)/shard_map/ppermute | solution.py:200
  175.3 5.6 %collective-permute-done.27.got = bf16[128,2048]{1,0:T(8,128)(2,1)S(1)} collective-permute-done((bf16[128,2048]{1,0:T(8,128)(2,1)S(1)}, bf16[128,2048]{1,0:T(8,128)(2,1)S(1)}, u32[]{:S(2)}, u32[]{:S(2)}) %collective-permute-start.27) | collective-permute-done | bytes 524320 | tf_op jit(solution)/shard_map/ppermute | solution.py:203
  181.0 1.3 last_scores.2
  182.3 3.5 %last_scores.3 = (bf16[2,528,128]{2,1,0:T(8,128)(2,1)S(1)}, f32[8,128]{1,0:T(8,128)}) custom-call(f32[128,2048]{1,0:T(8,128)S(1)} %get-tuple-element.146.kept, bf16[128,2048]{1,0:T(8,128)(2,1)S(1)} %collective-permute-done.27.got, f32[4,512,128]{2,1,0:T(8,128)S(1)} %convert_add_fusion.counts, f32[8,128]{1,0:T(8,128)S(1)} %get-tuple-element.152.before, ...), custom_call_target="tpu_custom_call" | custom-call | flops 1 | bytes 1 | tf_op jit(solution)/shard_map/last_scores/pallas_call | solution.py:176
  186.2 3.7 %collective-permute-start.34 = (bf16[2,512,128]{2,1,0:T(8,128)(2,1)S(1)}, bf16[2,512,128]{2,1,0:T(8,128)(2,1)}, u32[]{:S(2)}, u32[]{:S(2)}) collective-permute-start(bf16[2,512,128]{2,1,0:T(8,128)(2,1)S(1)} %get-tuple-element.163), channel_id=1, source_target_pairs={{0,3},{3,0},{4,7},{7,4},{8,11},{11,8},{12,15},{15,12},{16,19},{19,... | collective-permute-start | bytes 786440 | tf_op jit(solution)/shard_map/ppermute | solution.py:200
  190.5 1.6 collective-permute-start.30
  192.1 0.6 collective-permute-start.32
  192.7 3.9 %collective-permute-start.33 = (bf16[2,528,128]{2,1,0:T(8,128)(2,1)S(1)}, bf16[2,528,128]{2,1,0:T(8,128)(2,1)S(1)}, u32[]{:S(2)}, u32[]{:S(2)}) collective-permute-start(bf16[2,528,128]{2,1,0:T(8,128)(2,1)S(1)} %get-tuple-element.162), channel_id=1, source_target_pairs={{0,3},{3,0},{4,7},{7,4},{8,11},{11,8},{12,15},{15,12},{16,19},{19,... | collective-permute-start | bytes 811016 | tf_op jit(solution)/shard_map/ppermute | solution.py:200
  197.1 1.0 slice_bitcast_fusion.5
  198.1 1.5 collective-permute-start.35
  199.9 4.7 %collective-permute-done.32 = f32[520,128]{1,0:T(8,128)S(1)} collective-permute-done((f32[520,128]{1,0:T(8,128)S(1)}, f32[520,128]{1,0:T(8,128)S(1)}, u32[]{:S(2)}, u32[]{:S(2)}) %collective-permute-start.32) | collective-permute-done | bytes 266272 | tf_op jit(solution)/shard_map/ppermute | solution.py:203
  204.8 1.5 collective-permute-start.38
  206.3 1.0 collective-permute-start.39
  207.5 1.9 collective-permute-done.38
  210.0 1.1 slice_add_fusion
  (88 shorter events, 7.5 us)
Async XLA Ops:
  0.6 6.8 %collective-permute-start.2 = (bf16[512,2048]{1,0:T(8,128)(2,1)}, bf16[512,2048]{1,0:T(8,128)(2,1)}, u32[]{:S(2)}, u32[]{:S(2)}) collective-permute-start(bf16[512,2048]{1,0:T(8,128)(2,1)} %refs_0_.1), channel_id=1, source_target_pairs={{0,4},{4,0},{8,12},{12,8},{1,5},{5,1},{9,13},{13,9},{2,6},{6,2},{1... | collective-permute-start | bytes 6291464 | tf_op jit(solution)/shard_map/ppermute | solution.py:203
  1.1 49.0 %collective-permute-start.5 = (bf16[512,2048]{1,0:T(8,128)(2,1)}, bf16[512,2048]{1,0:T(8,128)(2,1)S(1)}, u32[]{:S(2)}, u32[]{:S(2)}) collective-permute-start(bf16[512,2048]{1,0:T(8,128)(2,1)} %refs_0_.1), channel_id=1, source_target_pairs={{0,8},{4,12},{8,0},{12,4},{1,9},{5,13},{9,1},{13,5},{2,10},{6,14},... | collective-permute-start | bytes 6291464 | tf_op jit(solution)/shard_map/ppermute | solution.py:203
  3.7 49.0 %collective-permute-start = (bf16[512,2048]{1,0:T(8,128)(2,1)}, bf16[512,2048]{1,0:T(8,128)(2,1)}, u32[]{:S(2)}, u32[]{:S(2)}) collective-permute-start(bf16[512,2048]{1,0:T(8,128)(2,1)} %refs_0_), channel_id=1, source_target_pairs={{0,1},{1,0},{2,3},{3,2},{4,5},{5,4},{6,7},{7,6},{8,9},{9,8},{10,11... | collective-permute-start | bytes 6291464 | tf_op jit(solution)/shard_map/ppermute | solution.py:200
  5.3 47.4 %collective-permute-start.1 = (bf16[512,2048]{1,0:T(8,128)(2,1)}, bf16[512,2048]{1,0:T(8,128)(2,1)}, u32[]{:S(2)}, u32[]{:S(2)}) collective-permute-start(bf16[512,2048]{1,0:T(8,128)(2,1)} %refs_0_), channel_id=1, source_target_pairs={{1,2},{2,1},{5,6},{6,5},{9,10},{10,9},{13,14},{14,13},{17,18},{18,... | collective-permute-start | bytes 6291464 | tf_op jit(solution)/shard_map/ppermute | solution.py:200
  7.4 3.4 %copy-start = (bf16[2048,2048]{1,0:T(8,128)(2,1)S(1)}, bf16[2048,2048]{1,0:T(8,128)(2,1)}, u32[]{:S(2)}) copy-start(bf16[2048,2048]{1,0:T(8,128)(2,1)} %refs_1_.5) | copy-start | bytes 25165828
  10.8 1.6 copy-start.7
  17.9 32.4 %collective-permute-start.3 = (bf16[128,2048]{1,0:T(8,128)(2,1)S(1)}, bf16[128,2048]{1,0:T(8,128)(2,1)S(1)}, u32[]{:S(2)}, u32[]{:S(2)}) collective-permute-start(bf16[128,2048]{1,0:T(8,128)(2,1)S(1)} %get-tuple-element.85), channel_id=1, source_target_pairs={{0,4},{4,0},{8,12},{12,8},{1,5},{5,1},{9,13},{13,9},{2,6},{6,2},{1... | collective-permute-start | bytes 1572872 | tf_op jit(solution)/shard_map/ppermute | solution.py:203
  18.0 32.9 %collective-permute-start.4 = (bf16[128,2048]{1,0:T(8,128)(2,1)S(1)}, bf16[128,2048]{1,0:T(8,128)(2,1)S(1)}, u32[]{:S(2)}, u32[]{:S(2)}) collective-permute-start(bf16[128,2048]{1,0:T(8,128)(2,1)S(1)} %get-tuple-element.86), channel_id=1, source_target_pairs={{0,4},{4,0},{8,12},{12,8},{1,5},{5,1},{9,13},{13,9},{2,6},{6,2},{1... | collective-permute-start | bytes 1572872 | tf_op jit(solution)/shard_map/ppermute | solution.py:203
  50.3 2.7 %collective-permute-start.6 = (bf16[256,2048]{1,0:T(8,128)(2,1)S(1)}, bf16[256,2048]{1,0:T(8,128)(2,1)S(1)}, u32[]{:S(2)}, u32[]{:S(2)}) collective-permute-start(bf16[256,2048]{1,0:T(8,128)(2,1)S(1)} %get-tuple-element.167), channel_id=1, source_target_pairs={{0,4},{4,0},{8,12},{12,8},{1,5},{5,1},{9,13},{13,9},{2,6},{6,2},{1... | collective-permute-start | bytes 3145736 | tf_op jit(solution)/shard_map/ppermute | solution.py:203
  50.4 4.1 %collective-permute-start.7 = (bf16[256,2048]{1,0:T(8,128)(2,1)S(1)}, bf16[256,2048]{1,0:T(8,128)(2,1)S(1)}, u32[]{:S(2)}, u32[]{:S(2)}) collective-permute-start(bf16[256,2048]{1,0:T(8,128)(2,1)S(1)} %get-tuple-element.166), channel_id=1, source_target_pairs={{0,4},{4,0},{8,12},{12,8},{1,5},{5,1},{9,13},{13,9},{2,6},{6,2},{1... | collective-permute-start | bytes 3145736 | tf_op jit(solution)/shard_map/ppermute | solution.py:203
  50.9 8.9 %slice-start = ((s8[8388608]{0:T(1024)(128)(4,1)}), s8[4194304]{0:T(1024)(128)(4,1)S(1)}, s32[]{:S(2)}) async-start(s8[8388608]{0:T(1024)(128)(4,1)} %bitcast.114), calls=%async_computation | async-start | bytes 8388608
  50.9 8.9 %slice-start.1 = ((s8[8388608]{0:T(1024)(128)(4,1)}), s8[4194304]{0:T(1024)(128)(4,1)S(1)}, s32[]{:S(2)}) async-start(s8[8388608]{0:T(1024)(128)(4,1)} %bitcast.114), calls=%async_computation.1 | async-start | bytes 8388608
  52.7 15.5 %copy-start.8 = (f32[128,2048]{1,0:T(8,128)}, f32[128,2048]{1,0:T(8,128)S(1)}, u32[]{:S(2)}) copy-start(f32[128,2048]{1,0:T(8,128)S(1)} %get-tuple-element.116.refs_2_) | copy-start | bytes 3145732
  54.5 13.6 %copy-start.3 = (bf16[256,2048]{1,0:T(8,128)(2,1)}, bf16[256,2048]{1,0:T(8,128)(2,1)S(1)}, u32[]{:S(2)}) copy-start(bf16[256,2048]{1,0:T(8,128)(2,1)S(1)} %collective-permute-done.7.refs_6_.refs_8_.refs_2_) | copy-start | bytes 3145732
  54.5 15.8 %copy-start.10 = (s32[512,16]{0,1:T(8,128)S(1)}, s32[512,16]{0,1:T(8,128)}, u32[]{:S(2)}) copy-start(s32[512,16]{0,1:T(8,128)} %param.7) | copy-start | bytes 98308
  54.5 53.9 %collective-permute-start.8 = (bf16[512,2048]{1,0:T(8,128)(2,1)}, bf16[512,2048]{1,0:T(8,128)(2,1)}, u32[]{:S(2)}, u32[]{:S(2)}) collective-permute-start(bf16[512,2048]{1,0:T(8,128)(2,1)} %collective-permute-done.refs_1_.refs_0_), channel_id=1, source_target_pairs={{1,2},{2,1},{5,6},{6,5},{9,10},{10,9},{13,14},{14,13},{17,18},{18,... | collective-permute-start | bytes 6291464 | tf_op jit(solution)/shard_map/ppermute | solution.py:200
  56.7 51.7 %collective-permute-start.9 = (bf16[512,2048]{1,0:T(8,128)(2,1)}, bf16[512,2048]{1,0:T(8,128)(2,1)}, u32[]{:S(2)}, u32[]{:S(2)}) collective-permute-start(bf16[512,2048]{1,0:T(8,128)(2,1)} %collective-permute-done.1.refs_0_), channel_id=1, source_target_pairs={{1,0},{2,3},{5,4},{6,7},{9,8},{10,11},{13,12},{14,15},{17,16},{18,... | collective-permute-start | bytes 6291464 | tf_op jit(solution)/shard_map/ppermute | solution.py:200
  58.0 25.6 %collective-permute-start.12 = (f32[128,2048]{1,0:T(8,128)}, f32[128,2048]{1,0:T(8,128)}, u32[]{:S(2)}, u32[]{:S(2)}) collective-permute-start(f32[128,2048]{1,0:T(8,128)} %get-tuple-element.96), channel_id=1, source_target_pairs={{0,8},{4,12},{8,0},{12,4},{1,9},{5,13},{9,1},{13,5},{2,10},{6,14},... | collective-permute-start | bytes 3145736 | tf_op jit(solution)/shard_map/ppermute | solution.py:203
  68.2 1.5 copy-start.5
  69.6 2.3 %collective-permute-start.10 = (bf16[128,2048]{1,0:T(8,128)(2,1)}, bf16[128,2048]{1,0:T(8,128)(2,1)}, u32[]{:S(2)}, u32[]{:S(2)}) collective-permute-start(bf16[128,2048]{1,0:T(8,128)(2,1)} %get-tuple-element.93), channel_id=1, source_target_pairs={{0,4},{4,0},{8,12},{12,8},{1,5},{5,1},{9,13},{13,9},{2,6},{6,2},{1... | collective-permute-start | bytes 1572872 | tf_op jit(solution)/shard_map/ppermute | solution.py:203
  69.6 3.0 %collective-permute-start.11 = (bf16[128,2048]{1,0:T(8,128)(2,1)}, bf16[128,2048]{1,0:T(8,128)(2,1)}, u32[]{:S(2)}, u32[]{:S(2)}) collective-permute-start(bf16[128,2048]{1,0:T(8,128)(2,1)} %get-tuple-element.94), channel_id=1, source_target_pairs={{0,4},{4,0},{8,12},{12,8},{1,5},{5,1},{9,13},{13,9},{2,6},{6,2},{1... | collective-permute-start | bytes 1572872 | tf_op jit(solution)/shard_map/ppermute | solution.py:203
  72.6 1.6 copy-start.6
  83.6 14.2 %collective-permute-start.15 = (bf16[128,2048]{1,0:T(8,128)(2,1)S(1)}, bf16[128,2048]{1,0:T(8,128)(2,1)S(1)}, u32[]{:S(2)}, u32[]{:S(2)}) collective-permute-start(bf16[128,2048]{1,0:T(8,128)(2,1)S(1)} %get-tuple-element.106), channel_id=1, source_target_pairs={{0,8},{4,12},{8,0},{12,4},{1,9},{5,13},{9,1},{13,5},{2,10},{6,14},... | collective-permute-start | bytes 1572872 | tf_op jit(solution)/shard_map/ppermute | solution.py:203
  85.3 3.4 %copy-start.1 = (bf16[2048,2048]{1,0:T(8,128)(2,1)S(1)}, bf16[2048,2048]{1,0:T(8,128)(2,1)}, u32[]{:S(2)}) copy-start(bf16[2048,2048]{1,0:T(8,128)(2,1)} %refs_1_.5) | copy-start | bytes 25165828
  88.7 14.6 %copy-start.2 = (bf16[512,2048]{1,0:T(8,128)(2,1)S(1)}, bf16[512,2048]{1,0:T(8,128)(2,1)}, u32[]{:S(2)}) copy-start(bf16[512,2048]{1,0:T(8,128)(2,1)} %refs_0_.1) | copy-start | bytes 6291460
  88.7 14.6 %copy-start.4 = (bf16[256,2048]{1,0:T(8,128)(2,1)S(1)}, bf16[256,2048]{1,0:T(8,128)(2,1)}, u32[]{:S(2)}) copy-start(bf16[256,2048]{1,0:T(8,128)(2,1)} %copy-done.3) | copy-start | bytes 3145732
  88.7 21.0 %slice-start.2 = ((s8[8388608]{0:T(1024)(128)(4,1)}), s8[4194304]{0:T(1024)(128)(4,1)S(1)}, s32[]{:S(2)}) async-start(s8[8388608]{0:T(1024)(128)(4,1)} %bitcast.116), calls=%async_computation.2 | async-start | bytes 8388608
  95.6 11.9 %collective-permute-start.13 = (bf16[128,2048]{1,0:T(8,128)(2,1)S(1)}, bf16[128,2048]{1,0:T(8,128)(2,1)S(1)}, u32[]{:S(2)}, u32[]{:S(2)}) collective-permute-start(bf16[128,2048]{1,0:T(8,128)(2,1)S(1)} %get-tuple-element.99), channel_id=1, source_target_pairs={{0,4},{4,0},{8,12},{12,8},{1,5},{5,1},{9,13},{13,9},{2,6},{6,2},{1... | collective-permute-start | bytes 1572872 | tf_op jit(solution)/shard_map/ppermute | solution.py:203
  95.7 11.9 %collective-permute-start.14 = (bf16[128,2048]{1,0:T(8,128)(2,1)S(1)}, bf16[128,2048]{1,0:T(8,128)(2,1)S(1)}, u32[]{:S(2)}, u32[]{:S(2)}) collective-permute-start(bf16[128,2048]{1,0:T(8,128)(2,1)S(1)} %get-tuple-element.100), channel_id=1, source_target_pairs={{0,4},{4,0},{8,12},{12,8},{1,5},{5,1},{9,13},{13,9},{2,6},{6,2},{1... | collective-permute-start | bytes 1572872 | tf_op jit(solution)/shard_map/ppermute | solution.py:203
  97.8 10.5 %collective-permute-start.16 = (s32[512,16]{0,1:T(8,128)S(1)}, s32[512,16]{0,1:T(8,128)S(1)}, u32[]{:S(2)}, u32[]{:S(2)}) collective-permute-start(s32[512,16]{0,1:T(8,128)S(1)} %copy-done.10), channel_id=1, source_target_pairs={{0,3},{3,0},{4,7},{7,4},{8,11},{11,8},{12,15},{15,12},{16,19},{19,... | collective-permute-start | bytes 98312 | tf_op jit(solution)/shard_map/ppermute | solution.py:200
  103.4 6.3 %slice-start.3 = ((s8[8388608]{0:T(1024)(128)(4,1)}), s8[4194304]{0:T(1024)(128)(4,1)S(1)}, s32[]{:S(2)}) async-start(s8[8388608]{0:T(1024)(128)(4,1)} %bitcast.116), calls=%async_computation.3 | async-start | bytes 8388608
  108.4 49.4 %collective-permute-start.17 = (bf16[512,2048]{1,0:T(8,128)(2,1)}, bf16[512,2048]{1,0:T(8,128)(2,1)S(1)}, u32[]{:S(2)}, u32[]{:S(2)}) collective-permute-start(bf16[512,2048]{1,0:T(8,128)(2,1)} %collective-permute-done.8.refs_0_), channel_id=1, source_target_pairs={{1,0},{2,3},{5,4},{6,7},{9,8},{10,11},{13,12},{14,15},{17,16},{18,... | collective-permute-start | bytes 6291464 | tf_op jit(solution)/shard_map/ppermute | solution.py:200
  117.1 2.0 collective-permute-start.19
  117.2 2.6 %collective-permute-start.20 = (bf16[128,2048]{1,0:T(8,128)(2,1)S(1)}, bf16[128,2048]{1,0:T(8,128)(2,1)S(1)}, u32[]{:S(2)}, u32[]{:S(2)}) collective-permute-start(bf16[128,2048]{1,0:T(8,128)(2,1)S(1)} %get-tuple-element.127), channel_id=1, source_target_pairs={{0,4},{4,0},{8,12},{12,8},{1,5},{5,1},{9,13},{13,9},{2,6},{6,2},{1... | collective-permute-start | bytes 1572872 | tf_op jit(solution)/shard_map/ppermute | solution.py:203
  120.6 14.8 %collective-permute-start.21 = (bf16[128,2048]{1,0:T(8,128)(2,1)S(1)}, bf16[128,2048]{1,0:T(8,128)(2,1)S(1)}, u32[]{:S(2)}, u32[]{:S(2)}) collective-permute-start(bf16[128,2048]{1,0:T(8,128)(2,1)S(1)} %get-tuple-element.131), channel_id=1, source_target_pairs={{0,8},{4,12},{8,0},{12,4},{1,9},{5,13},{9,1},{13,5},{2,10},{6,14},... | collective-permute-start | bytes 1572872 | tf_op jit(solution)/shard_map/ppermute | solution.py:203
  121.7 15.9 %collective-permute-start.22 = (bf16[4,512,128]{2,1,0:T(8,128)(2,1)S(1)}, bf16[4,512,128]{2,1,0:T(8,128)(2,1)S(1)}, u32[]{:S(2)}, u32[]{:S(2)}) collective-permute-start(bf16[4,512,128]{2,1,0:T(8,128)(2,1)S(1)} %scores.3), channel_id=1, source_target_pairs={{0,1},{3,2},{4,5},{7,6},{8,9},{11,10},{12,13},{15,14},{16,17},{19,... | collective-permute-start | bytes 1572872 | tf_op jit(solution)/shard_map/ppermute | solution.py:200
  126.4 11.2 %collective-permute-start.23 = (bf16[4,512,128]{2,1,0:T(8,128)(2,1)S(1)}, bf16[4,512,128]{2,1,0:T(8,128)(2,1)S(1)}, u32[]{:S(2)}, u32[]{:S(2)}) collective-permute-start(bf16[4,512,128]{2,1,0:T(8,128)(2,1)S(1)} %scores.3), channel_id=1, source_target_pairs={{1,2},{2,1},{5,6},{6,5},{9,10},{10,9},{13,14},{14,13},{17,18},{18,... | collective-permute-start | bytes 1572872 | tf_op jit(solution)/shard_map/ppermute | solution.py:200
  127.3 18.6 %collective-permute-start.18 = (bf16[128,2048]{1,0:T(8,128)(2,1)S(1)}, bf16[128,2048]{1,0:T(8,128)(2,1)S(1)}, u32[]{:S(2)}, u32[]{:S(2)}) collective-permute-start(bf16[128,2048]{1,0:T(8,128)(2,1)S(1)} %get-tuple-element.115), channel_id=1, source_target_pairs={{0,8},{4,12},{8,0},{12,4},{1,9},{5,13},{9,1},{13,5},{2,10},{6,14},... | collective-permute-start | bytes 1572872 | tf_op jit(solution)/shard_map/ppermute | solution.py:203
  128.4 17.5 %copy-start.9 = (f32[128,2048]{1,0:T(8,128)S(1)}, f32[128,2048]{1,0:T(8,128)}, u32[]{:S(2)}) copy-start(f32[128,2048]{1,0:T(8,128)} %copy-done.8) | copy-start | bytes 3145732
  141.5 10.9 %collective-permute-start.24 = (bf16[4,512,128]{2,1,0:T(8,128)(2,1)S(1)}, bf16[4,512,128]{2,1,0:T(8,128)(2,1)S(1)}, u32[]{:S(2)}, u32[]{:S(2)}) collective-permute-start(bf16[4,512,128]{2,1,0:T(8,128)(2,1)S(1)} %scores.5), channel_id=1, source_target_pairs={{1,2},{2,1},{5,6},{6,5},{9,10},{10,9},{13,14},{14,13},{17,18},{18,... | collective-permute-start | bytes 1572872 | tf_op jit(solution)/shard_map/ppermute | solution.py:200
  163.4 2.0 collective-permute-start.25
  163.5 2.6 %collective-permute-start.26 = (bf16[128,2048]{1,0:T(8,128)(2,1)S(1)}, bf16[128,2048]{1,0:T(8,128)(2,1)S(1)}, u32[]{:S(2)}, u32[]{:S(2)}) collective-permute-start(bf16[128,2048]{1,0:T(8,128)(2,1)S(1)} %get-tuple-element.145), channel_id=1, source_target_pairs={{0,4},{4,0},{8,12},{12,8},{1,5},{5,1},{9,13},{13,9},{2,6},{6,2},{1... | collective-permute-start | bytes 1572872 | tf_op jit(solution)/shard_map/ppermute | solution.py:203
  167.0 14.0 %collective-permute-start.27 = (bf16[128,2048]{1,0:T(8,128)(2,1)S(1)}, bf16[128,2048]{1,0:T(8,128)(2,1)S(1)}, u32[]{:S(2)}, u32[]{:S(2)}) collective-permute-start(bf16[128,2048]{1,0:T(8,128)(2,1)S(1)} %get-tuple-element.147), channel_id=1, source_target_pairs={{0,8},{4,12},{8,0},{12,4},{1,9},{5,13},{9,1},{13,5},{2,10},{6,14},... | collective-permute-start | bytes 1572872 | tf_op jit(solution)/shard_map/ppermute | solution.py:203
  167.7 18.1 %collective-permute-start.29 = (bf16[4,512,128]{2,1,0:T(8,128)(2,1)S(1)}, bf16[4,512,128]{2,1,0:T(8,128)(2,1)S(1)}, u32[]{:S(2)}, u32[]{:S(2)}) collective-permute-start(bf16[4,512,128]{2,1,0:T(8,128)(2,1)S(1)} %add_convert_fusion), channel_id=1, source_target_pairs={{1,0},{2,3},{5,4},{6,7},{9,8},{10,11},{13,12},{14,15},{17,16},{18,... | collective-permute-start | bytes 1572872 | tf_op jit(solution)/shard_map/ppermute | solution.py:200
  169.0 17.2 %collective-permute-start.28 = (bf16[4,512,128]{2,1,0:T(8,128)(2,1)S(1)}, bf16[4,512,128]{2,1,0:T(8,128)(2,1)S(1)}, u32[]{:S(2)}, u32[]{:S(2)}) collective-permute-start(bf16[4,512,128]{2,1,0:T(8,128)(2,1)S(1)} %scores.5), channel_id=1, source_target_pairs={{0,2},{3,1},{4,6},{7,5},{8,10},{11,9},{12,14},{15,13},{16,18},{19,... | collective-permute-start | bytes 1572872 | tf_op jit(solution)/shard_map/ppermute | solution.py:200
  186.2 10.9 %collective-permute-start.34 = (bf16[2,512,128]{2,1,0:T(8,128)(2,1)S(1)}, bf16[2,512,128]{2,1,0:T(8,128)(2,1)}, u32[]{:S(2)}, u32[]{:S(2)}) collective-permute-start(bf16[2,512,128]{2,1,0:T(8,128)(2,1)S(1)} %get-tuple-element.163), channel_id=1, source_target_pairs={{0,3},{3,0},{4,7},{7,4},{8,11},{11,8},{12,15},{15,12},{16,19},{19,... | collective-permute-start | bytes 786440 | tf_op jit(solution)/shard_map/ppermute | solution.py:200
  190.5 9.4 %collective-permute-start.30 = (f32[520,128]{1,0:T(8,128)S(1)}, f32[520,128]{1,0:T(8,128)S(1)}, u32[]{:S(2)}, u32[]{:S(2)}) collective-permute-start(f32[520,128]{1,0:T(8,128)S(1)} %get-tuple-element.218), channel_id=1, source_target_pairs={{0,8},{4,12},{8,0},{12,4},{1,9},{5,13},{9,1},{13,5},{2,10},{6,14},... | collective-permute-start | bytes 798728 | tf_op jit(solution)/shard_map/ppermute | solution.py:203
  192.1 7.8 %collective-permute-start.31 = (f32[520,128]{1,0:T(8,128)S(1)}, f32[520,128]{1,0:T(8,128)S(1)}, u32[]{:S(2)}, u32[]{:S(2)}) collective-permute-start(f32[520,128]{1,0:T(8,128)S(1)} %get-tuple-element.219), channel_id=1, source_target_pairs={{0,4},{4,0},{8,12},{12,8},{1,5},{5,1},{9,13},{13,9},{2,6},{6,2},{1... | collective-permute-start | bytes 798728 | tf_op jit(solution)/shard_map/ppermute | solution.py:203
  192.1 12.6 %collective-permute-start.32 = (f32[520,128]{1,0:T(8,128)S(1)}, f32[520,128]{1,0:T(8,128)S(1)}, u32[]{:S(2)}, u32[]{:S(2)}) collective-permute-start(f32[520,128]{1,0:T(8,128)S(1)} %get-tuple-element.220), channel_id=1, source_target_pairs={{0,12},{4,8},{8,4},{12,0},{1,13},{5,9},{9,5},{13,1},{2,14},{6,10},... | collective-permute-start | bytes 798728 | tf_op jit(solution)/shard_map/ppermute | solution.py:203
  192.7 12.1 %collective-permute-start.33 = (bf16[2,528,128]{2,1,0:T(8,128)(2,1)S(1)}, bf16[2,528,128]{2,1,0:T(8,128)(2,1)S(1)}, u32[]{:S(2)}, u32[]{:S(2)}) collective-permute-start(bf16[2,528,128]{2,1,0:T(8,128)(2,1)S(1)} %get-tuple-element.162), channel_id=1, source_target_pairs={{0,3},{3,0},{4,7},{7,4},{8,11},{11,8},{12,15},{15,12},{16,19},{19,... | collective-permute-start | bytes 811016 | tf_op jit(solution)/shard_map/ppermute | solution.py:200
  198.1 11.9 %collective-permute-start.35 = (bf16[512,128]{1,0:T(8,128)(2,1)S(1)}, bf16[512,128]{1,0:T(8,128)(2,1)S(1)}, u32[]{:S(2)}, u32[]{:S(2)}) collective-permute-start(bf16[512,128]{1,0:T(8,128)(2,1)S(1)} %get-tuple-element.185), channel_id=1, source_target_pairs={{0,8},{4,12},{8,0},{12,4},{1,9},{5,13},{9,1},{13,5},{2,10},{6,14},... | collective-permute-start | bytes 393224 | tf_op jit(solution)/shard_map/ppermute | solution.py:203
  199.9 10.1 %collective-permute-start.37 = (bf16[512,128]{1,0:T(8,128)(2,1)S(1)}, bf16[512,128]{1,0:T(8,128)(2,1)S(1)}, u32[]{:S(2)}, u32[]{:S(2)}) collective-permute-start(bf16[512,128]{1,0:T(8,128)(2,1)S(1)} %get-tuple-element.184), channel_id=1, source_target_pairs={{0,12},{4,8},{8,4},{12,0},{1,13},{5,9},{9,5},{13,1},{2,14},{6,10},... | collective-permute-start | bytes 393224 | tf_op jit(solution)/shard_map/ppermute | solution.py:203
  204.8 4.5 %collective-permute-start.38 = (bf16[16,128]{1,0:T(8,128)(2,1)S(1)}, bf16[16,128]{1,0:T(8,128)(2,1)S(1)}, u32[]{:S(2)}, u32[]{:S(2)}) collective-permute-start(bf16[16,128]{1,0:T(8,128)(2,1)S(1)} %slice_bitcast_fusion.8), channel_id=1, source_target_pairs={{0,8},{4,12},{8,0},{12,4},{1,9},{5,13},{9,1},{13,5},{2,10},{6,14},... | collective-permute-start | bytes 12296 | tf_op jit(solution)/shard_map/ppermute | solution.py:203
  206.3 3.1 %collective-permute-start.39 = (bf16[16,128]{1,0:T(8,128)(2,1)S(1)}, bf16[16,128]{1,0:T(8,128)(2,1)S(1)}, u32[]{:S(2)}, u32[]{:S(2)}) collective-permute-start(bf16[16,128]{1,0:T(8,128)(2,1)S(1)} %slice_bitcast_fusion.8), channel_id=1, source_target_pairs={{0,12},{4,8},{8,4},{12,0},{1,13},{5,9},{9,5},{13,1},{2,14},{6,10},... | collective-permute-start | bytes 12296 | tf_op jit(solution)/shard_map/ppermute | solution.py:203
  207.3 2.1 collective-permute-start.36

commit v15 on v14

--- a/solution.py
+++ b/solution.py
@@ -248,7 +248,9 @@
     own_got = to_other(own_sent, 2)
     near_sent, own_got, pair_in = tied(near_sent, own_got, pair_in)
     near_got = to_other(near_sent, 2)
-    third, third_sent = core_sum(*product(flags, [pair_in], fisher))
+    third, *third_sent = product(flags, [pair_in], fisher)
+    third, second_edge = tied(third, second_edge)
+    third, third_sent = core_sum(third, *third_sent, cost=SOME)
     (near,) = scores_of((near, near_got), cost=SOME)
     far_ids = along(chosen_ids, [(0, 3), (3, 0)])
     counts = selected(chosen_ids)

time: 212 us -> 212 us (level)
  no operation moved by 1% of the time
where the time goes in v15:
time: 212 us; the launch traced here: 211 us
  waiting for transfers between devices  77.8 us (37%)
  Pallas kernels  58.9 us (28%)
  starting transfers between devices  54.9 us (26%)
  local copies, waits for them, and re-layouts  12.7 us (6%)
  other arithmetic  6.08 us (3%)
    ppermute x27, waiting for transfers between devices, to_other(): return lax.ppermute(value, 'train', [(k, k ^ r) for k in range(4)])  68.1 us
    ppermute x13, starting transfers between devices, along(): return lax.ppermute(value, 'test', pairs)  35.8 us
    pallas_call x5, Pallas kernels, product(): pl.pallas_call(functools.partial(product_body, len(blocks)), in_specs=[pl...  33.7 us
    ppermute x27, starting transfers between devices, to_other(): return lax.ppermute(value, 'train', [(k, k ^ r) for k in range(4)])  19.1 us
    pallas_call x3, Pallas kernels, partial_scores(): pl.pallas_call(functools.partial(scores_body, [piece[:2] for piece in gra...  14.6 us
    unnamed x30, local copies, waits for them, and re-layouts  11.4 us
    ppermute x13, waiting for transfers between devices, along(): return lax.ppermute(value, 'test', pairs)  9.66 us
    pallas_call x5, Pallas kernels, fold(): pl.pallas_call(fold_body, in_specs=[pl.BlockSpec(memory_space=pltpu.SMEM)...  5.8 us
  transfers between devices with their start and end apart: 40, of which 21 were waited for; matrix products, arithmetic and copies ran while one was open for 3% of the time, Pallas kernels for 25%

profile of v15, /device:TPU:0, one launch (start us, length us, event | category | flops | bytes accessed | tf_op | source)
XLA Modules:
  0.0 211.4 jit_solution(5260653130482569324)
XLA Ops:
  1.1 2.6 %collective-permute-start.5 = (bf16[512,2048]{1,0:T(8,128)(2,1)}, bf16[512,2048]{1,0:T(8,128)(2,1)S(1)}, u32[]{:S(2)}, u32[]{:S(2)}) collective-permute-start(bf16[512,2048]{1,0:T(8,128)(2,1)} %refs_0_.1), channel_id=1, source_target_pairs={{0,8},{4,12},{8,0},{12,4},{1,9},{5,13},{9,1},{13,5},{2,10},{6,14},... | collective-permute-start | bytes 6291464 | tf_op jit(solution)/shard_map/ppermute | solution.py:203
  3.7 1.6 collective-permute-start
  5.3 2.0 collective-permute-start.1
  7.4 3.4 %copy-done = bf16[2048,2048]{1,0:T(8,128)(2,1)S(1)} copy-done((bf16[2048,2048]{1,0:T(8,128)(2,1)S(1)}, bf16[2048,2048]{1,0:T(8,128)(2,1)}, u32[]{:S(2)}) %copy-start) | copy-done | bytes 8388632
  10.8 1.6 copy-done.7
  12.4 5.6 %product.5 = (f32[256,2048]{1,0:T(8,128)S(1)}, bf16[128,2048]{1,0:T(8,128)(2,1)S(1)}, bf16[128,2048]{1,0:T(8,128)(2,1)S(1)}) custom-call(s32[3]{0:T(128)S(1)} %pad_add_fusion.flags, bf16[512,2048]{1,0:T(8,128)(2,1)S(1)} %copy-done.7, bf16[2048,2048]{1,0:T(8,128)(2,1)S(1)} %copy-done), custom_call_target="tpu_custom_call" | custom-call | flops 1 | bytes 1 | tf_op jit(solution)/shard_map/product/pallas_call | solution.py:80
  18.5 31.6 %collective-permute-done.5.refs_4_.refs_6_.refs_0_ = bf16[512,2048]{1,0:T(8,128)(2,1)S(1)} collective-permute-done((bf16[512,2048]{1,0:T(8,128)(2,1)}, bf16[512,2048]{1,0:T(8,128)(2,1)S(1)}, u32[]{:S(2)}, u32[]{:S(2)}) %collective-permute-start.5) | collective-permute-done | bytes 2097184 | tf_op jit(solution)/shard_map/ppermute | solution.py:203
  50.9 1.8 fold.5
  53.0 1.5 collective-permute-done.7.refs_6_.refs_8_.refs_2_
  54.5 1.4 collective-permute-start.12
  55.9 2.1 collective-permute-start.8
  58.0 1.8 collective-permute-start.11
  59.8 8.3 %product.6 = (f32[256,2048]{1,0:T(8,128)S(1)}, bf16[128,2048]{1,0:T(8,128)(2,1)}, bf16[128,2048]{1,0:T(8,128)(2,1)}) custom-call(s32[3]{0:T(128)S(1)} %pad_add_fusion.flags, bf16[512,2048]{1,0:T(8,128)(2,1)} %collective-permute-done.1.refs_0_, bf16[512,2048]{1,0:T(8,128)(2,1)} %collective-permute-done.refs_1_.refs_0_, bf16[2048,2048]{1,0:T(8,128)(2,1)S(1)} %bitcast.115), custom_call_target="tpu_custom_call" | custom-call | flops 1 | bytes 1 | tf_op jit(solution)/shard_map/product/pallas_call | solution.py:80
  68.1 1.4 copy-done.5
  70.2 1.6 collective-permute-done.10.refs_1_
  71.8 0.7 collective-permute-done.9.refs_0_
  72.6 1.6 copy-done.6
  74.2 1.5 fold.6
  75.7 7.8 %collective-permute-done.11.refs_3_ = f32[128,2048]{1,0:T(8,128)} collective-permute-done((f32[128,2048]{1,0:T(8,128)}, f32[128,2048]{1,0:T(8,128)}, u32[]{:S(2)}, u32[]{:S(2)}) %collective-permute-start.11) | collective-permute-done | bytes 1048608 | tf_op jit(solution)/shard_map/ppermute | solution.py:203
  83.5 1.7 collective-permute-start.15
  85.3 3.4 %copy-done.1 = bf16[2048,2048]{1,0:T(8,128)(2,1)S(1)} copy-done((bf16[2048,2048]{1,0:T(8,128)(2,1)S(1)}, bf16[2048,2048]{1,0:T(8,128)(2,1)}, u32[]{:S(2)}) %copy-start.1) | copy-done | bytes 8388632
  88.7 6.9 %product.7 = (f32[256,2048]{1,0:T(8,128)S(1)}, bf16[128,2048]{1,0:T(8,128)(2,1)S(1)}, bf16[128,2048]{1,0:T(8,128)(2,1)S(1)}) custom-call(s32[3]{0:T(128)S(1)} %pad_add_fusion.flags, bf16[512,2048]{1,0:T(8,128)(2,1)} %collective-permute-done.refs_1_.refs_0_, bf16[2048,2048]{1,0:T(8,128)(2,1)S(1)} %copy-done.1), custom_call_target="tpu_custom_call" | custom-call | flops 1 | bytes 1 | tf_op jit(solution)/shard_map/product/pallas_call | solution.py:80
  96.1 1.7 convert_add_fusion.1
  97.8 5.5 %collective-permute-start.16 = (s32[512,16]{0,1:T(8,128)S(1)}, s32[512,16]{0,1:T(8,128)S(1)}, u32[]{:S(2)}, u32[]{:S(2)}) collective-permute-start(s32[512,16]{0,1:T(8,128)S(1)} %copy-done.10), channel_id=1, source_target_pairs={{0,3},{3,0},{4,7},{7,4},{8,11},{11,8},{12,15},{15,12},{16,19},{19,... | collective-permute-start | bytes 98312 | tf_op jit(solution)/shard_map/ppermute | solution.py:200
  103.3 4.1 %scores.3 = bf16[4,512,128]{2,1,0:T(8,128)(2,1)S(1)} custom-call(f32[128,2048]{1,0:T(8,128)S(1)} %get-tuple-element.109.refs_0_, bf16[128,2048]{1,0:T(8,128)(2,1)S(1)} %collective-permute-done.15.refs_1_, bf16[512,2048]{1,0:T(8,128)(2,1)S(1)} %copy-done.2, bf16[512,2048]{1,0:T(8,128)(2,1)} %collective-permute-done.2.refs_3_.refs_5_.refs_1_, ...), custom_call_target="tpu_custom_call" | custom-call | flops 2000000000 | bytes 1048576 | tf_op jit(solution)/shard_map/scores/pallas_call | solution.py:144
  107.5 0.8 fold.7
  108.3 1.3 collective-permute-start.17
  109.7 7.3 %product.8 = (f32[256,2048]{1,0:T(8,128)S(1)}, bf16[128,2048]{1,0:T(8,128)(2,1)S(1)}, bf16[128,2048]{1,0:T(8,128)(2,1)S(1)}) custom-call(s32[3]{0:T(128)S(1)} %pad_add_fusion.flags, bf16[512,2048]{1,0:T(8,128)(2,1)} %collective-permute-done.8.refs_0_, bf16[512,2048]{1,0:T(8,128)(2,1)} %collective-permute-done.12.refs_1_, bf16[2048,2048]{1,0:T(8,128)(2,1)S(1)} %bitcast.117), custom_call_target="tpu_custom_call" | custom-call | flops 1 | bytes 1 | tf_op jit(solution)/shard_map/product/pallas_call | solution.py:80
  117.6 1.4 collective-permute-done.19.refs_0_
  119.0 0.7 collective-permute-done.20.refs_1_
  119.8 0.8 fold.8
  120.6 0.7 collective-permute-start.21
  121.3 6.0 %collective-permute-start.22 = (bf16[4,512,128]{2,1,0:T(8,128)(2,1)S(1)}, bf16[4,512,128]{2,1,0:T(8,128)(2,1)S(1)}, u32[]{:S(2)}, u32[]{:S(2)}) collective-permute-start(bf16[4,512,128]{2,1,0:T(8,128)(2,1)S(1)} %scores.3), channel_id=1, source_target_pairs={{0,1},{3,2},{4,5},{7,6},{8,9},{11,10},{12,13},{15,14},{16,17},{19,... | collective-permute-start | bytes 1572872 | tf_op jit(solution)/shard_map/ppermute | solution.py:200
  127.3 0.9 collective-permute-start.23
  128.1 0.6 collective-permute-start.18
  128.8 6.7 %collective-permute-done.21.refs_1_ = bf16[128,2048]{1,0:T(8,128)(2,1)S(1)} collective-permute-done((bf16[128,2048]{1,0:T(8,128)(2,1)S(1)}, bf16[128,2048]{1,0:T(8,128)(2,1)S(1)}, u32[]{:S(2)}, u32[]{:S(2)}) %collective-permute-start.21) | collective-permute-done | bytes 524320 | tf_op jit(solution)/shard_map/ppermute | solution.py:203
  135.4 3.0 %collective-permute-done.22 = bf16[4,512,128]{2,1,0:T(8,128)(2,1)S(1)} collective-permute-done((bf16[4,512,128]{2,1,0:T(8,128)(2,1)S(1)}, bf16[4,512,128]{2,1,0:T(8,128)(2,1)S(1)}, u32[]{:S(2)}, u32[]{:S(2)}) %collective-permute-start.22) | collective-permute-done | bytes 524320 | tf_op jit(solution)/shard_map/ppermute | solution.py:200
  138.4 4.0 %scores.5 = bf16[4,512,128]{2,1,0:T(8,128)(2,1)S(1)} custom-call(f32[128,2048]{1,0:T(8,128)S(1)} %get-tuple-element.139.refs_0_, bf16[128,2048]{1,0:T(8,128)(2,1)S(1)} %collective-permute-done.21.refs_1_, bf16[512,2048]{1,0:T(8,128)(2,1)S(1)} %copy-done.2, bf16[512,2048]{1,0:T(8,128)(2,1)} %collective-permute-done.2.refs_3_.refs_5_.refs_1_, ...), custom_call_target="tpu_custom_call" | custom-call | flops 1 | bytes 1 | tf_op jit(solution)/shard_map/scores/pallas_call | solution.py:144
  142.4 0.7 collective-permute-start.24
  143.1 1.7 convert_add_fusion.counts
  144.8 1.1 collective-permute-done.18.refs_1_
  145.8 6.5 %scores.4 = (f32[4,512,128]{2,1,0:T(8,128)S(1)}, f32[4,512,128]{2,1,0:T(8,128)S(1)}) custom-call(f32[128,2048]{1,0:T(8,128)S(1)} %get-tuple-element.118.refs_0_, bf16[128,2048]{1,0:T(8,128)(2,1)S(1)} %collective-permute-done.18.refs_1_, f32[128,2048]{1,0:T(8,128)S(1)} %copy-done.9, f32[128,2048]{1,0:T(8,128)} %collective-permute-done.11.refs_3_, ...), custom_call_target="tpu_custom_call" | custom-call | flops 1 | bytes 1 | tf_op jit(solution)/shard_map/scores/pallas_call | solution.py:144
  152.4 5.6 %collective-permute-done.17.refs_0_ = bf16[512,2048]{1,0:T(8,128)(2,1)S(1)} collective-permute-done((bf16[512,2048]{1,0:T(8,128)(2,1)}, bf16[512,2048]{1,0:T(8,128)(2,1)S(1)}, u32[]{:S(2)}, u32[]{:S(2)}) %collective-permute-start.17) | collective-permute-done | bytes 2097184 | tf_op jit(solution)/shard_map/ppermute | solution.py:200
  158.0 5.6 %product.9 = (f32[256,2048]{1,0:T(8,128)S(1)}, bf16[128,2048]{1,0:T(8,128)(2,1)S(1)}, bf16[128,2048]{1,0:T(8,128)(2,1)S(1)}) custom-call(s32[3]{0:T(128)S(1)} %pad_add_fusion.flags, bf16[512,2048]{1,0:T(8,128)(2,1)S(1)} %collective-permute-done.17.refs_0_, bf16[2048,2048]{1,0:T(8,128)(2,1)S(1)} %bitcast.117), custom_call_target="tpu_custom_call" | custom-call | flops 1 | bytes 1 | tf_op jit(solution)/shard_map/product/pallas_call | solution.py:80
  164.2 1.4 collective-permute-done.25.refs_0_
  165.6 0.7 collective-permute-done.26.refs_1_
  166.3 0.8 fold.9
  167.1 1.6 collective-permute-start.27
  168.8 1.3 collective-permute-start.29
  170.1 5.5 %collective-permute-start.28 = (bf16[4,512,128]{2,1,0:T(8,128)(2,1)S(1)}, bf16[4,512,128]{2,1,0:T(8,128)(2,1)S(1)}, u32[]{:S(2)}, u32[]{:S(2)}) collective-permute-start(bf16[4,512,128]{2,1,0:T(8,128)(2,1)S(1)} %scores.5), channel_id=1, source_target_pairs={{0,2},{3,1},{4,6},{7,5},{8,10},{11,9},{12,14},{15,13},{16,18},{19,... | collective-permute-start | bytes 1572872 | tf_op jit(solution)/shard_map/ppermute | solution.py:200
  175.6 5.6 %collective-permute-done.27.got = bf16[128,2048]{1,0:T(8,128)(2,1)S(1)} collective-permute-done((bf16[128,2048]{1,0:T(8,128)(2,1)S(1)}, bf16[128,2048]{1,0:T(8,128)(2,1)S(1)}, u32[]{:S(2)}, u32[]{:S(2)}) %collective-permute-start.27) | collective-permute-done | bytes 524320 | tf_op jit(solution)/shard_map/ppermute | solution.py:203
  181.2 1.3 last_scores.2
  182.5 3.5 %last_scores.3 = (bf16[2,528,128]{2,1,0:T(8,128)(2,1)S(1)}, f32[8,128]{1,0:T(8,128)}) custom-call(f32[128,2048]{1,0:T(8,128)S(1)} %get-tuple-element.150.kept, bf16[128,2048]{1,0:T(8,128)(2,1)S(1)} %collective-permute-done.27.got, f32[4,512,128]{2,1,0:T(8,128)S(1)} %convert_add_fusion.counts, f32[8,128]{1,0:T(8,128)S(1)} %get-tuple-element.156.before, ...), custom_call_target="tpu_custom_call" | custom-call | flops 1 | bytes 1 | tf_op jit(solution)/shard_map/last_scores/pallas_call | solution.py:176
  186.4 3.8 %collective-permute-start.34 = (bf16[2,512,128]{2,1,0:T(8,128)(2,1)S(1)}, bf16[2,512,128]{2,1,0:T(8,128)(2,1)}, u32[]{:S(2)}, u32[]{:S(2)}) collective-permute-start(bf16[2,512,128]{2,1,0:T(8,128)(2,1)S(1)} %get-tuple-element.167), channel_id=1, source_target_pairs={{0,3},{3,0},{4,7},{7,4},{8,11},{11,8},{12,15},{15,12},{16,19},{19,... | collective-permute-start | bytes 786440 | tf_op jit(solution)/shard_map/ppermute | solution.py:200
  190.8 1.5 collective-permute-start.30
  192.3 0.7 collective-permute-start.32
  193.0 3.9 %collective-permute-start.33 = (bf16[2,528,128]{2,1,0:T(8,128)(2,1)S(1)}, bf16[2,528,128]{2,1,0:T(8,128)(2,1)S(1)}, u32[]{:S(2)}, u32[]{:S(2)}) collective-permute-start(bf16[2,528,128]{2,1,0:T(8,128)(2,1)S(1)} %get-tuple-element.166), channel_id=1, source_target_pairs={{0,3},{3,0},{4,7},{7,4},{8,11},{11,8},{12,15},{15,12},{16,19},{19,... | collective-permute-start | bytes 811016 | tf_op jit(solution)/shard_map/ppermute | solution.py:200
  197.3 1.0 slice_bitcast_fusion.5
  198.3 1.6 collective-permute-start.35
  200.2 4.7 %collective-permute-done.32 = f32[520,128]{1,0:T(8,128)S(1)} collective-permute-done((f32[520,128]{1,0:T(8,128)S(1)}, f32[520,128]{1,0:T(8,128)S(1)}, u32[]{:S(2)}, u32[]{:S(2)}) %collective-permute-start.32) | collective-permute-done | bytes 266272 | tf_op jit(solution)/shard_map/ppermute | solution.py:203
  205.0 1.5 collective-permute-start.38
  206.5 1.0 collective-permute-start.39
  207.7 1.9 collective-permute-done.38
  210.3 1.1 slice_add_fusion
  (88 shorter events, 7.5 us)
Async XLA Ops:
  0.6 6.8 %collective-permute-start.2 = (bf16[512,2048]{1,0:T(8,128)(2,1)}, bf16[512,2048]{1,0:T(8,128)(2,1)}, u32[]{:S(2)}, u32[]{:S(2)}) collective-permute-start(bf16[512,2048]{1,0:T(8,128)(2,1)} %refs_0_.1), channel_id=1, source_target_pairs={{0,4},{4,0},{8,12},{12,8},{1,5},{5,1},{9,13},{13,9},{2,6},{6,2},{1... | collective-permute-start | bytes 6291464 | tf_op jit(solution)/shard_map/ppermute | solution.py:203
  1.1 49.0 %collective-permute-start.5 = (bf16[512,2048]{1,0:T(8,128)(2,1)}, bf16[512,2048]{1,0:T(8,128)(2,1)S(1)}, u32[]{:S(2)}, u32[]{:S(2)}) collective-permute-start(bf16[512,2048]{1,0:T(8,128)(2,1)} %refs_0_.1), channel_id=1, source_target_pairs={{0,8},{4,12},{8,0},{12,4},{1,9},{5,13},{9,1},{13,5},{2,10},{6,14},... | collective-permute-start | bytes 6291464 | tf_op jit(solution)/shard_map/ppermute | solution.py:203
  3.7 49.0 %collective-permute-start = (bf16[512,2048]{1,0:T(8,128)(2,1)}, bf16[512,2048]{1,0:T(8,128)(2,1)}, u32[]{:S(2)}, u32[]{:S(2)}) collective-permute-start(bf16[512,2048]{1,0:T(8,128)(2,1)} %refs_0_), channel_id=1, source_target_pairs={{0,1},{1,0},{2,3},{3,2},{4,5},{5,4},{6,7},{7,6},{8,9},{9,8},{10,11... | collective-permute-start | bytes 6291464 | tf_op jit(solution)/shard_map/ppermute | solution.py:200
  5.3 47.4 %collective-permute-start.1 = (bf16[512,2048]{1,0:T(8,128)(2,1)}, bf16[512,2048]{1,0:T(8,128)(2,1)}, u32[]{:S(2)}, u32[]{:S(2)}) collective-permute-start(bf16[512,2048]{1,0:T(8,128)(2,1)} %refs_0_), channel_id=1, source_target_pairs={{1,2},{2,1},{5,6},{6,5},{9,10},{10,9},{13,14},{14,13},{17,18},{18,... | collective-permute-start | bytes 6291464 | tf_op jit(solution)/shard_map/ppermute | solution.py:200
  7.4 3.4 %copy-start = (bf16[2048,2048]{1,0:T(8,128)(2,1)S(1)}, bf16[2048,2048]{1,0:T(8,128)(2,1)}, u32[]{:S(2)}) copy-start(bf16[2048,2048]{1,0:T(8,128)(2,1)} %refs_1_.5) | copy-start | bytes 25165828
  10.8 1.6 copy-start.7
  17.9 32.4 %collective-permute-start.3 = (bf16[128,2048]{1,0:T(8,128)(2,1)S(1)}, bf16[128,2048]{1,0:T(8,128)(2,1)S(1)}, u32[]{:S(2)}, u32[]{:S(2)}) collective-permute-start(bf16[128,2048]{1,0:T(8,128)(2,1)S(1)} %get-tuple-element.87), channel_id=1, source_target_pairs={{0,4},{4,0},{8,12},{12,8},{1,5},{5,1},{9,13},{13,9},{2,6},{6,2},{1... | collective-permute-start | bytes 1572872 | tf_op jit(solution)/shard_map/ppermute | solution.py:203
  18.0 32.9 %collective-permute-start.4 = (bf16[128,2048]{1,0:T(8,128)(2,1)S(1)}, bf16[128,2048]{1,0:T(8,128)(2,1)S(1)}, u32[]{:S(2)}, u32[]{:S(2)}) collective-permute-start(bf16[128,2048]{1,0:T(8,128)(2,1)S(1)} %get-tuple-element.88), channel_id=1, source_target_pairs={{0,4},{4,0},{8,12},{12,8},{1,5},{5,1},{9,13},{13,9},{2,6},{6,2},{1... | collective-permute-start | bytes 1572872 | tf_op jit(solution)/shard_map/ppermute | solution.py:203
  50.3 2.7 %collective-permute-start.6 = (bf16[256,2048]{1,0:T(8,128)(2,1)S(1)}, bf16[256,2048]{1,0:T(8,128)(2,1)S(1)}, u32[]{:S(2)}, u32[]{:S(2)}) collective-permute-start(bf16[256,2048]{1,0:T(8,128)(2,1)S(1)} %get-tuple-element.171), channel_id=1, source_target_pairs={{0,4},{4,0},{8,12},{12,8},{1,5},{5,1},{9,13},{13,9},{2,6},{6,2},{1... | collective-permute-start | bytes 3145736 | tf_op jit(solution)/shard_map/ppermute | solution.py:203
  50.4 4.1 %collective-permute-start.7 = (bf16[256,2048]{1,0:T(8,128)(2,1)S(1)}, bf16[256,2048]{1,0:T(8,128)(2,1)S(1)}, u32[]{:S(2)}, u32[]{:S(2)}) collective-permute-start(bf16[256,2048]{1,0:T(8,128)(2,1)S(1)} %get-tuple-element.170), channel_id=1, source_target_pairs={{0,4},{4,0},{8,12},{12,8},{1,5},{5,1},{9,13},{13,9},{2,6},{6,2},{1... | collective-permute-start | bytes 3145736 | tf_op jit(solution)/shard_map/ppermute | solution.py:203
  50.9 8.9 %slice-start = ((s8[8388608]{0:T(1024)(128)(4,1)}), s8[4194304]{0:T(1024)(128)(4,1)S(1)}, s32[]{:S(2)}) async-start(s8[8388608]{0:T(1024)(128)(4,1)} %bitcast.114), calls=%async_computation | async-start | bytes 8388608
  50.9 8.9 %slice-start.1 = ((s8[8388608]{0:T(1024)(128)(4,1)}), s8[4194304]{0:T(1024)(128)(4,1)S(1)}, s32[]{:S(2)}) async-start(s8[8388608]{0:T(1024)(128)(4,1)} %bitcast.114), calls=%async_computation.1 | async-start | bytes 8388608
  52.7 15.4 %copy-start.8 = (f32[128,2048]{1,0:T(8,128)}, f32[128,2048]{1,0:T(8,128)S(1)}, u32[]{:S(2)}) copy-start(f32[128,2048]{1,0:T(8,128)S(1)} %get-tuple-element.120.refs_2_) | copy-start | bytes 3145732
  54.5 13.6 %copy-start.3 = (bf16[256,2048]{1,0:T(8,128)(2,1)}, bf16[256,2048]{1,0:T(8,128)(2,1)S(1)}, u32[]{:S(2)}) copy-start(bf16[256,2048]{1,0:T(8,128)(2,1)S(1)} %collective-permute-done.7.refs_6_.refs_8_.refs_2_) | copy-start | bytes 3145732
  54.5 15.7 %copy-start.10 = (s32[512,16]{0,1:T(8,128)S(1)}, s32[512,16]{0,1:T(8,128)}, u32[]{:S(2)}) copy-start(s32[512,16]{0,1:T(8,128)} %param.7) | copy-start | bytes 98308
  54.5 53.0 %collective-permute-start.12 = (bf16[512,2048]{1,0:T(8,128)(2,1)}, bf16[512,2048]{1,0:T(8,128)(2,1)}, u32[]{:S(2)}, u32[]{:S(2)}) collective-permute-start(bf16[512,2048]{1,0:T(8,128)(2,1)} %collective-permute-done.1.refs_0_), channel_id=1, source_target_pairs={{1,0},{2,3},{5,4},{6,7},{9,8},{10,11},{13,12},{14,15},{17,16},{18,... | collective-permute-start | bytes 6291464 | tf_op jit(solution)/shard_map/ppermute | solution.py:200
  55.9 52.4 %collective-permute-start.8 = (bf16[512,2048]{1,0:T(8,128)(2,1)}, bf16[512,2048]{1,0:T(8,128)(2,1)}, u32[]{:S(2)}, u32[]{:S(2)}) collective-permute-start(bf16[512,2048]{1,0:T(8,128)(2,1)} %collective-permute-done.refs_1_.refs_0_), channel_id=1, source_target_pairs={{1,2},{2,1},{5,6},{6,5},{9,10},{10,9},{13,14},{14,13},{17,18},{18,... | collective-permute-start | bytes 6291464 | tf_op jit(solution)/shard_map/ppermute | solution.py:200
  58.0 25.5 %collective-permute-start.11 = (f32[128,2048]{1,0:T(8,128)}, f32[128,2048]{1,0:T(8,128)}, u32[]{:S(2)}, u32[]{:S(2)}) collective-permute-start(f32[128,2048]{1,0:T(8,128)} %get-tuple-element.98), channel_id=1, source_target_pairs={{0,8},{4,12},{8,0},{12,4},{1,9},{5,13},{9,1},{13,5},{2,10},{6,14},... | collective-permute-start | bytes 3145736 | tf_op jit(solution)/shard_map/ppermute | solution.py:203
  68.1 1.5 copy-start.5
  69.6 2.3 %collective-permute-start.10 = (bf16[128,2048]{1,0:T(8,128)(2,1)}, bf16[128,2048]{1,0:T(8,128)(2,1)}, u32[]{:S(2)}, u32[]{:S(2)}) collective-permute-start(bf16[128,2048]{1,0:T(8,128)(2,1)} %get-tuple-element.96), channel_id=1, source_target_pairs={{0,4},{4,0},{8,12},{12,8},{1,5},{5,1},{9,13},{13,9},{2,6},{6,2},{1... | collective-permute-start | bytes 1572872 | tf_op jit(solution)/shard_map/ppermute | solution.py:203
  69.6 3.0 %collective-permute-start.9 = (bf16[128,2048]{1,0:T(8,128)(2,1)}, bf16[128,2048]{1,0:T(8,128)(2,1)}, u32[]{:S(2)}, u32[]{:S(2)}) collective-permute-start(bf16[128,2048]{1,0:T(8,128)(2,1)} %get-tuple-element.95), channel_id=1, source_target_pairs={{0,4},{4,0},{8,12},{12,8},{1,5},{5,1},{9,13},{13,9},{2,6},{6,2},{1... | collective-permute-start | bytes 1572872 | tf_op jit(solution)/shard_map/ppermute | solution.py:203
  72.6 1.6 copy-start.6
  83.5 14.2 %collective-permute-start.15 = (bf16[128,2048]{1,0:T(8,128)(2,1)S(1)}, bf16[128,2048]{1,0:T(8,128)(2,1)S(1)}, u32[]{:S(2)}, u32[]{:S(2)}) collective-permute-start(bf16[128,2048]{1,0:T(8,128)(2,1)S(1)} %get-tuple-element.110), channel_id=1, source_target_pairs={{0,8},{4,12},{8,0},{12,4},{1,9},{5,13},{9,1},{13,5},{2,10},{6,14},... | collective-permute-start | bytes 1572872 | tf_op jit(solution)/shard_map/ppermute | solution.py:203
  85.3 3.4 %copy-start.1 = (bf16[2048,2048]{1,0:T(8,128)(2,1)S(1)}, bf16[2048,2048]{1,0:T(8,128)(2,1)}, u32[]{:S(2)}) copy-start(bf16[2048,2048]{1,0:T(8,128)(2,1)} %refs_1_.5) | copy-start | bytes 25165828
  88.7 14.7 %copy-start.2 = (bf16[512,2048]{1,0:T(8,128)(2,1)S(1)}, bf16[512,2048]{1,0:T(8,128)(2,1)}, u32[]{:S(2)}) copy-start(bf16[512,2048]{1,0:T(8,128)(2,1)} %refs_0_.1) | copy-start | bytes 6291460
  88.7 14.7 %copy-start.4 = (bf16[256,2048]{1,0:T(8,128)(2,1)S(1)}, bf16[256,2048]{1,0:T(8,128)(2,1)}, u32[]{:S(2)}) copy-start(bf16[256,2048]{1,0:T(8,128)(2,1)} %copy-done.3) | copy-start | bytes 3145732
  95.5 12.0 %collective-permute-start.13 = (bf16[128,2048]{1,0:T(8,128)(2,1)S(1)}, bf16[128,2048]{1,0:T(8,128)(2,1)S(1)}, u32[]{:S(2)}, u32[]{:S(2)}) collective-permute-start(bf16[128,2048]{1,0:T(8,128)(2,1)S(1)} %get-tuple-element.103), channel_id=1, source_target_pairs={{0,4},{4,0},{8,12},{12,8},{1,5},{5,1},{9,13},{13,9},{2,6},{6,2},{1... | collective-permute-start | bytes 1572872 | tf_op jit(solution)/shard_map/ppermute | solution.py:203
  95.6 11.9 %collective-permute-start.14 = (bf16[128,2048]{1,0:T(8,128)(2,1)S(1)}, bf16[128,2048]{1,0:T(8,128)(2,1)S(1)}, u32[]{:S(2)}, u32[]{:S(2)}) collective-permute-start(bf16[128,2048]{1,0:T(8,128)(2,1)S(1)} %get-tuple-element.104), channel_id=1, source_target_pairs={{0,4},{4,0},{8,12},{12,8},{1,5},{5,1},{9,13},{13,9},{2,6},{6,2},{1... | collective-permute-start | bytes 1572872 | tf_op jit(solution)/shard_map/ppermute | solution.py:203
  97.8 10.5 %collective-permute-start.16 = (s32[512,16]{0,1:T(8,128)S(1)}, s32[512,16]{0,1:T(8,128)S(1)}, u32[]{:S(2)}, u32[]{:S(2)}) collective-permute-start(s32[512,16]{0,1:T(8,128)S(1)} %copy-done.10), channel_id=1, source_target_pairs={{0,3},{3,0},{4,7},{7,4},{8,11},{11,8},{12,15},{15,12},{16,19},{19,... | collective-permute-start | bytes 98312 | tf_op jit(solution)/shard_map/ppermute | solution.py:200
  103.3 6.3 %slice-start.2 = ((s8[8388608]{0:T(1024)(128)(4,1)}), s8[4194304]{0:T(1024)(128)(4,1)S(1)}, s32[]{:S(2)}) async-start(s8[8388608]{0:T(1024)(128)(4,1)} %bitcast.116), calls=%async_computation.2 | async-start | bytes 8388608
  103.3 6.3 %slice-start.3 = ((s8[8388608]{0:T(1024)(128)(4,1)}), s8[4194304]{0:T(1024)(128)(4,1)S(1)}, s32[]{:S(2)}) async-start(s8[8388608]{0:T(1024)(128)(4,1)} %bitcast.116), calls=%async_computation.3 | async-start | bytes 8388608
  108.3 49.7 %collective-permute-start.17 = (bf16[512,2048]{1,0:T(8,128)(2,1)}, bf16[512,2048]{1,0:T(8,128)(2,1)S(1)}, u32[]{:S(2)}, u32[]{:S(2)}) collective-permute-start(bf16[512,2048]{1,0:T(8,128)(2,1)} %collective-permute-done.8.refs_0_), channel_id=1, source_target_pairs={{1,0},{2,3},{5,4},{6,7},{9,8},{10,11},{13,12},{14,15},{17,16},{18,... | collective-permute-start | bytes 6291464 | tf_op jit(solution)/shard_map/ppermute | solution.py:200
  117.0 2.0 collective-permute-start.19
  117.1 2.6 %collective-permute-start.20 = (bf16[128,2048]{1,0:T(8,128)(2,1)S(1)}, bf16[128,2048]{1,0:T(8,128)(2,1)S(1)}, u32[]{:S(2)}, u32[]{:S(2)}) collective-permute-start(bf16[128,2048]{1,0:T(8,128)(2,1)S(1)} %get-tuple-element.131), channel_id=1, source_target_pairs={{0,4},{4,0},{8,12},{12,8},{1,5},{5,1},{9,13},{13,9},{2,6},{6,2},{1... | collective-permute-start | bytes 1572872 | tf_op jit(solution)/shard_map/ppermute | solution.py:203
  120.6 14.8 %collective-permute-start.21 = (bf16[128,2048]{1,0:T(8,128)(2,1)S(1)}, bf16[128,2048]{1,0:T(8,128)(2,1)S(1)}, u32[]{:S(2)}, u32[]{:S(2)}) collective-permute-start(bf16[128,2048]{1,0:T(8,128)(2,1)S(1)} %get-tuple-element.135), channel_id=1, source_target_pairs={{0,8},{4,12},{8,0},{12,4},{1,9},{5,13},{9,1},{13,5},{2,10},{6,14},... | collective-permute-start | bytes 1572872 | tf_op jit(solution)/shard_map/ppermute | solution.py:203
  121.3 17.2 %collective-permute-start.22 = (bf16[4,512,128]{2,1,0:T(8,128)(2,1)S(1)}, bf16[4,512,128]{2,1,0:T(8,128)(2,1)S(1)}, u32[]{:S(2)}, u32[]{:S(2)}) collective-permute-start(bf16[4,512,128]{2,1,0:T(8,128)(2,1)S(1)} %scores.3), channel_id=1, source_target_pairs={{0,1},{3,2},{4,5},{7,6},{8,9},{11,10},{12,13},{15,14},{16,17},{19,... | collective-permute-start | bytes 1572872 | tf_op jit(solution)/shard_map/ppermute | solution.py:200
  127.3 11.2 %collective-permute-start.23 = (bf16[4,512,128]{2,1,0:T(8,128)(2,1)S(1)}, bf16[4,512,128]{2,1,0:T(8,128)(2,1)S(1)}, u32[]{:S(2)}, u32[]{:S(2)}) collective-permute-start(bf16[4,512,128]{2,1,0:T(8,128)(2,1)S(1)} %scores.3), channel_id=1, source_target_pairs={{1,2},{2,1},{5,6},{6,5},{9,10},{10,9},{13,14},{14,13},{17,18},{18,... | collective-permute-start | bytes 1572872 | tf_op jit(solution)/shard_map/ppermute | solution.py:200
  128.1 17.7 %collective-permute-start.18 = (bf16[128,2048]{1,0:T(8,128)(2,1)S(1)}, bf16[128,2048]{1,0:T(8,128)(2,1)S(1)}, u32[]{:S(2)}, u32[]{:S(2)}) collective-permute-start(bf16[128,2048]{1,0:T(8,128)(2,1)S(1)} %get-tuple-element.119), channel_id=1, source_target_pairs={{0,8},{4,12},{8,0},{12,4},{1,9},{5,13},{9,1},{13,5},{2,10},{6,14},... | collective-permute-start | bytes 1572872 | tf_op jit(solution)/shard_map/ppermute | solution.py:203
  128.8 17.1 %copy-start.9 = (f32[128,2048]{1,0:T(8,128)S(1)}, f32[128,2048]{1,0:T(8,128)}, u32[]{:S(2)}) copy-start(f32[128,2048]{1,0:T(8,128)} %copy-done.8) | copy-start | bytes 3145732
  142.4 10.0 %collective-permute-start.24 = (bf16[4,512,128]{2,1,0:T(8,128)(2,1)S(1)}, bf16[4,512,128]{2,1,0:T(8,128)(2,1)S(1)}, u32[]{:S(2)}, u32[]{:S(2)}) collective-permute-start(bf16[4,512,128]{2,1,0:T(8,128)(2,1)S(1)} %scores.5), channel_id=1, source_target_pairs={{1,2},{2,1},{5,6},{6,5},{9,10},{10,9},{13,14},{14,13},{17,18},{18,... | collective-permute-start | bytes 1572872 | tf_op jit(solution)/shard_map/ppermute | solution.py:200
  163.6 2.0 collective-permute-start.25
  163.7 2.6 %collective-permute-start.26 = (bf16[128,2048]{1,0:T(8,128)(2,1)S(1)}, bf16[128,2048]{1,0:T(8,128)(2,1)S(1)}, u32[]{:S(2)}, u32[]{:S(2)}) collective-permute-start(bf16[128,2048]{1,0:T(8,128)(2,1)S(1)} %get-tuple-element.149), channel_id=1, source_target_pairs={{0,4},{4,0},{8,12},{12,8},{1,5},{5,1},{9,13},{13,9},{2,6},{6,2},{1... | collective-permute-start | bytes 1572872 | tf_op jit(solution)/shard_map/ppermute | solution.py:203
  167.1 14.0 %collective-permute-start.27 = (bf16[128,2048]{1,0:T(8,128)(2,1)S(1)}, bf16[128,2048]{1,0:T(8,128)(2,1)S(1)}, u32[]{:S(2)}, u32[]{:S(2)}) collective-permute-start(bf16[128,2048]{1,0:T(8,128)(2,1)S(1)} %get-tuple-element.151), channel_id=1, source_target_pairs={{0,8},{4,12},{8,0},{12,4},{1,9},{5,13},{9,1},{13,5},{2,10},{6,14},... | collective-permute-start | bytes 1572872 | tf_op jit(solution)/shard_map/ppermute | solution.py:203
  168.8 17.2 %collective-permute-start.29 = (bf16[4,512,128]{2,1,0:T(8,128)(2,1)S(1)}, bf16[4,512,128]{2,1,0:T(8,128)(2,1)S(1)}, u32[]{:S(2)}, u32[]{:S(2)}) collective-permute-start(bf16[4,512,128]{2,1,0:T(8,128)(2,1)S(1)} %add_convert_fusion), channel_id=1, source_target_pairs={{1,0},{2,3},{5,4},{6,7},{9,8},{10,11},{13,12},{14,15},{17,16},{18,... | collective-permute-start | bytes 1572872 | tf_op jit(solution)/shard_map/ppermute | solution.py:200
  170.1 16.3 %collective-permute-start.28 = (bf16[4,512,128]{2,1,0:T(8,128)(2,1)S(1)}, bf16[4,512,128]{2,1,0:T(8,128)(2,1)S(1)}, u32[]{:S(2)}, u32[]{:S(2)}) collective-permute-start(bf16[4,512,128]{2,1,0:T(8,128)(2,1)S(1)} %scores.5), channel_id=1, source_target_pairs={{0,2},{3,1},{4,6},{7,5},{8,10},{11,9},{12,14},{15,13},{16,18},{19,... | collective-permute-start | bytes 1572872 | tf_op jit(solution)/shard_map/ppermute | solution.py:200
  186.4 10.9 %collective-permute-start.34 = (bf16[2,512,128]{2,1,0:T(8,128)(2,1)S(1)}, bf16[2,512,128]{2,1,0:T(8,128)(2,1)}, u32[]{:S(2)}, u32[]{:S(2)}) collective-permute-start(bf16[2,512,128]{2,1,0:T(8,128)(2,1)S(1)} %get-tuple-element.167), channel_id=1, source_target_pairs={{0,3},{3,0},{4,7},{7,4},{8,11},{11,8},{12,15},{15,12},{16,19},{19,... | collective-permute-start | bytes 786440 | tf_op jit(solution)/shard_map/ppermute | solution.py:200
  190.8 9.4 %collective-permute-start.30 = (f32[520,128]{1,0:T(8,128)S(1)}, f32[520,128]{1,0:T(8,128)S(1)}, u32[]{:S(2)}, u32[]{:S(2)}) collective-permute-start(f32[520,128]{1,0:T(8,128)S(1)} %get-tuple-element.222), channel_id=1, source_target_pairs={{0,8},{4,12},{8,0},{12,4},{1,9},{5,13},{9,1},{13,5},{2,10},{6,14},... | collective-permute-start | bytes 798728 | tf_op jit(solution)/shard_map/ppermute | solution.py:203
  192.3 7.9 %collective-permute-start.31 = (f32[520,128]{1,0:T(8,128)S(1)}, f32[520,128]{1,0:T(8,128)S(1)}, u32[]{:S(2)}, u32[]{:S(2)}) collective-permute-start(f32[520,128]{1,0:T(8,128)S(1)} %get-tuple-element.223), channel_id=1, source_target_pairs={{0,4},{4,0},{8,12},{12,8},{1,5},{5,1},{9,13},{13,9},{2,6},{6,2},{1... | collective-permute-start | bytes 798728 | tf_op jit(solution)/shard_map/ppermute | solution.py:203
  192.3 12.6 %collective-permute-start.32 = (f32[520,128]{1,0:T(8,128)S(1)}, f32[520,128]{1,0:T(8,128)S(1)}, u32[]{:S(2)}, u32[]{:S(2)}) collective-permute-start(f32[520,128]{1,0:T(8,128)S(1)} %get-tuple-element.224), channel_id=1, source_target_pairs={{0,12},{4,8},{8,4},{12,0},{1,13},{5,9},{9,5},{13,1},{2,14},{6,10},... | collective-permute-start | bytes 798728 | tf_op jit(solution)/shard_map/ppermute | solution.py:203
  193.0 12.1 %collective-permute-start.33 = (bf16[2,528,128]{2,1,0:T(8,128)(2,1)S(1)}, bf16[2,528,128]{2,1,0:T(8,128)(2,1)S(1)}, u32[]{:S(2)}, u32[]{:S(2)}) collective-permute-start(bf16[2,528,128]{2,1,0:T(8,128)(2,1)S(1)} %get-tuple-element.166), channel_id=1, source_target_pairs={{0,3},{3,0},{4,7},{7,4},{8,11},{11,8},{12,15},{15,12},{16,19},{19,... | collective-permute-start | bytes 811016 | tf_op jit(solution)/shard_map/ppermute | solution.py:200
  198.3 11.9 %collective-permute-start.35 = (bf16[512,128]{1,0:T(8,128)(2,1)S(1)}, bf16[512,128]{1,0:T(8,128)(2,1)S(1)}, u32[]{:S(2)}, u32[]{:S(2)}) collective-permute-start(bf16[512,128]{1,0:T(8,128)(2,1)S(1)} %get-tuple-element.189), channel_id=1, source_target_pairs={{0,8},{4,12},{8,0},{12,4},{1,9},{5,13},{9,1},{13,5},{2,10},{6,14},... | collective-permute-start | bytes 393224 | tf_op jit(solution)/shard_map/ppermute | solution.py:203
  200.2 10.1 %collective-permute-start.37 = (bf16[512,128]{1,0:T(8,128)(2,1)S(1)}, bf16[512,128]{1,0:T(8,128)(2,1)S(1)}, u32[]{:S(2)}, u32[]{:S(2)}) collective-permute-start(bf16[512,128]{1,0:T(8,128)(2,1)S(1)} %get-tuple-element.188), channel_id=1, source_target_pairs={{0,12},{4,8},{8,4},{12,0},{1,13},{5,9},{9,5},{13,1},{2,14},{6,10},... | collective-permute-start | bytes 393224 | tf_op jit(solution)/shard_map/ppermute | solution.py:203
  205.0 4.5 %collective-permute-start.38 = (bf16[16,128]{1,0:T(8,128)(2,1)S(1)}, bf16[16,128]{1,0:T(8,128)(2,1)S(1)}, u32[]{:S(2)}, u32[]{:S(2)}) collective-permute-start(bf16[16,128]{1,0:T(8,128)(2,1)S(1)} %slice_bitcast_fusion.8), channel_id=1, source_target_pairs={{0,8},{4,12},{8,0},{12,4},{1,9},{5,13},{9,1},{13,5},{2,10},{6,14},... | collective-permute-start | bytes 12296 | tf_op jit(solution)/shard_map/ppermute | solution.py:203
  206.5 3.1 %collective-permute-start.39 = (bf16[16,128]{1,0:T(8,128)(2,1)S(1)}, bf16[16,128]{1,0:T(8,128)(2,1)S(1)}, u32[]{:S(2)}, u32[]{:S(2)}) collective-permute-start(bf16[16,128]{1,0:T(8,128)(2,1)S(1)} %slice_bitcast_fusion.8), channel_id=1, source_target_pairs={{0,12},{4,8},{8,4},{12,0},{1,13},{5,9},{9,5},{13,1},{2,14},{6,10},... | collective-permute-start | bytes 12296 | tf_op jit(solution)/shard_map/ppermute | solution.py:203
  207.5 2.1 collective-permute-start.36

commit v16 on v15

--- a/solution.py
+++ b/solution.py
@@ -252,10 +252,9 @@
     third, second_edge = tied(third, second_edge)
     third, third_sent = core_sum(third, *third_sent, cost=SOME)
     (near,) = scores_of((near, near_got), cost=SOME)
-    far_ids = along(chosen_ids, [(0, 3), (3, 0)])
     counts = selected(chosen_ids)
-    far_in, second_edge, third, third_sent, own, own_got, near, far_ids, counts, grads = tied(
-        far_in, second_edge, third, third_sent, own, own_got, near, far_ids, counts, grads
+    far_in, second_edge, third, third_sent, own, own_got, near, counts, chosen_ids, grads = tied(
+        far_in, second_edge, third, third_sent, own, own_got, near, counts, chosen_ids, grads
     )
 
     first_edge = along(far_in, outward)
@@ -263,20 +262,24 @@
     second, second_sent, near = tied(second, second_sent, near)
     second_got = to_other(second_sent, 2)
     near_in, near_across = along(near, inward), along(near, middle)
-    second_got, near_in, near_across = tied(second_got, near_in, near_across)
+    second_got, near_in, near_across, chosen_ids = tied(
+        second_got, near_in, near_across, chosen_ids
+    )
+    far_ids = along(chosen_ids, [(0, 3), (3, 0)])
     (second,) = scores_of((second, second_got))
     across = along(second, middle)
     third, total = scores_of(
         (third, to_other(third_sent, 2)), (own, own_got), out_as=(F32, F32)
     )
+    first_edge, total, near_in, near_across, second, across, third, grads, far_ids = tied(
+        first_edge, total, near_in, near_across, second, across, third, grads, far_ids
+    )
     far_counts = selected(far_ids)
-    first_edge, total, near_in, near_across, second, across, third, grads, far_counts = tied(
-        first_edge, total, near_in, near_across, second, across, third, grads, far_counts
-    )
-
+
+    last, last_sent = core_sum(*product(flags, [first_edge], fisher))
+    last, second, third = tied(last, second, third)
     third = along((third + across.astype(F32)).astype(BF16), outward)
     second = along(second, [(0, 2), (3, 1)])
-    last, last_sent = core_sum(*product(flags, [first_edge], fisher))
     last_got = to_other(last_sent, 2)
     ends = [(0, 3), (3, 0)]
     none = jnp.zeros((8, quarter), F32)

time: 212 us -> 214 us (level)
    ppermute x13, waiting for transfers between devices: 9.66 us -> 13.4 us  [along(): return lax.ppermute(value, 'test', pairs)]
    ppermute x27, waiting for transfers between devices: 68.1 us -> 64.6 us  [to_other(): return lax.ppermute(value, 'train', [(k, k ^ r) for k in range(4)])]
  transfers between devices with their start and end apart: 40 -> 40, of which waited for: 21 -> 20; matrix products, arithmetic and copies ran while one was open for 3% -> 3% of each run, Pallas kernels for 25% -> 25%
where the time goes in v16:
time: 214 us; the launch traced here: 213 us
  waiting for transfers between devices  77.9 us (36%)
  Pallas kernels  58.9 us (28%)
  starting transfers between devices  56.2 us (26%)
  local copies, waits for them, and re-layouts  12.7 us (6%)
  other arithmetic  6.06 us (3%)
    ppermute x27, waiting for transfers between devices, to_other(): return lax.ppermute(value, 'train', [(k, k ^ r) for k in range(4)])  64.6 us
    ppermute x13, starting transfers between devices, along(): return lax.ppermute(value, 'test', pairs)  36 us
    pallas_call x5, Pallas kernels, product(): pl.pallas_call(functools.partial(product_body, len(blocks)), in_specs=[pl...  33.7 us
    ppermute x27, starting transfers between devices, to_other(): return lax.ppermute(value, 'train', [(k, k ^ r) for k in range(4)])  20.2 us
    pallas_call x3, Pallas kernels, partial_scores(): pl.pallas_call(functools.partial(scores_body, [piece[:2] for piece in gra...  14.6 us
    ppermute x13, waiting for transfers between devices, along(): return lax.ppermute(value, 'test', pairs)  13.4 us
    unnamed x30, local copies, waits for them, and re-layouts  11.4 us
    pallas_call x5, Pallas kernels, fold(): pl.pallas_call(fold_body, in_specs=[pl.BlockSpec(memory_space=pltpu.SMEM)...  5.8 us
  transfers between devices with their start and end apart: 40, of which 20 were waited for; matrix products, arithmetic and copies ran while one was open for 3% of the time, Pallas kernels for 25%

profile of v16, /device:TPU:0, one launch (start us, length us, event | category | flops | bytes accessed | tf_op | source)
XLA Modules:
  0.0 212.8 jit_solution(10388468488871616028)
XLA Ops:
  1.1 2.6 %collective-permute-start.5 = (bf16[512,2048]{1,0:T(8,128)(2,1)}, bf16[512,2048]{1,0:T(8,128)(2,1)S(1)}, u32[]{:S(2)}, u32[]{:S(2)}) collective-permute-start(bf16[512,2048]{1,0:T(8,128)(2,1)} %refs_0_.1), channel_id=1, source_target_pairs={{0,8},{4,12},{8,0},{12,4},{1,9},{5,13},{9,1},{13,5},{2,10},{6,14},... | collective-permute-start | bytes 6291464 | tf_op jit(solution)/shard_map/ppermute | solution.py:203
  3.7 1.6 collective-permute-start
  5.3 2.0 collective-permute-start.1
  7.4 3.4 %copy-done = bf16[2048,2048]{1,0:T(8,128)(2,1)S(1)} copy-done((bf16[2048,2048]{1,0:T(8,128)(2,1)S(1)}, bf16[2048,2048]{1,0:T(8,128)(2,1)}, u32[]{:S(2)}) %copy-start) | copy-done | bytes 8388632
  10.8 1.6 copy-done.7
  12.4 5.6 %product.5 = (f32[256,2048]{1,0:T(8,128)S(1)}, bf16[128,2048]{1,0:T(8,128)(2,1)S(1)}, bf16[128,2048]{1,0:T(8,128)(2,1)S(1)}) custom-call(s32[3]{0:T(128)S(1)} %pad_add_fusion.flags, bf16[512,2048]{1,0:T(8,128)(2,1)S(1)} %copy-done.7, bf16[2048,2048]{1,0:T(8,128)(2,1)S(1)} %copy-done), custom_call_target="tpu_custom_call" | custom-call | flops 1 | bytes 1 | tf_op jit(solution)/shard_map/product/pallas_call | solution.py:80
  18.5 31.6 %collective-permute-done.5.refs_4_.refs_6_.refs_0_ = bf16[512,2048]{1,0:T(8,128)(2,1)S(1)} collective-permute-done((bf16[512,2048]{1,0:T(8,128)(2,1)}, bf16[512,2048]{1,0:T(8,128)(2,1)S(1)}, u32[]{:S(2)}, u32[]{:S(2)}) %collective-permute-start.5) | collective-permute-done | bytes 2097184 | tf_op jit(solution)/shard_map/ppermute | solution.py:203
  50.9 1.8 fold.5
  53.0 1.5 collective-permute-done.7.refs_6_.refs_8_.refs_2_
  54.5 1.4 collective-permute-start.12
  55.9 2.1 collective-permute-start.8
  58.0 1.8 collective-permute-start.11
  59.8 8.3 %product.6 = (f32[256,2048]{1,0:T(8,128)S(1)}, bf16[128,2048]{1,0:T(8,128)(2,1)}, bf16[128,2048]{1,0:T(8,128)(2,1)}) custom-call(s32[3]{0:T(128)S(1)} %pad_add_fusion.flags, bf16[512,2048]{1,0:T(8,128)(2,1)} %collective-permute-done.1.refs_0_, bf16[512,2048]{1,0:T(8,128)(2,1)} %collective-permute-done.refs_1_.refs_0_, bf16[2048,2048]{1,0:T(8,128)(2,1)S(1)} %bitcast.115), custom_call_target="tpu_custom_call" | custom-call | flops 1 | bytes 1 | tf_op jit(solution)/shard_map/product/pallas_call | solution.py:80
  68.1 1.4 copy-done.5
  70.2 1.6 collective-permute-done.10.refs_1_
  71.8 0.7 collective-permute-done.9.refs_0_
  72.6 1.6 copy-done.6
  74.2 1.5 fold.6
  75.7 7.8 %collective-permute-done.11.refs_3_ = f32[128,2048]{1,0:T(8,128)} collective-permute-done((f32[128,2048]{1,0:T(8,128)}, f32[128,2048]{1,0:T(8,128)}, u32[]{:S(2)}, u32[]{:S(2)}) %collective-permute-start.11) | collective-permute-done | bytes 1048608 | tf_op jit(solution)/shard_map/ppermute | solution.py:203
  83.5 1.7 collective-permute-start.15
  85.3 3.4 %copy-done.1 = bf16[2048,2048]{1,0:T(8,128)(2,1)S(1)} copy-done((bf16[2048,2048]{1,0:T(8,128)(2,1)S(1)}, bf16[2048,2048]{1,0:T(8,128)(2,1)}, u32[]{:S(2)}) %copy-start.1) | copy-done | bytes 8388632
  88.7 6.9 %product.7 = (f32[256,2048]{1,0:T(8,128)S(1)}, bf16[128,2048]{1,0:T(8,128)(2,1)S(1)}, bf16[128,2048]{1,0:T(8,128)(2,1)S(1)}) custom-call(s32[3]{0:T(128)S(1)} %pad_add_fusion.flags, bf16[512,2048]{1,0:T(8,128)(2,1)} %collective-permute-done.refs_1_.refs_0_, bf16[2048,2048]{1,0:T(8,128)(2,1)S(1)} %copy-done.1), custom_call_target="tpu_custom_call" | custom-call | flops 1 | bytes 1 | tf_op jit(solution)/shard_map/product/pallas_call | solution.py:80
  96.1 1.7 convert_add_fusion.1
  97.8 4.1 %scores.3 = bf16[4,512,128]{2,1,0:T(8,128)(2,1)S(1)} custom-call(f32[128,2048]{1,0:T(8,128)S(1)} %get-tuple-element.113.refs_0_, bf16[128,2048]{1,0:T(8,128)(2,1)S(1)} %collective-permute-done.15.refs_1_, bf16[512,2048]{1,0:T(8,128)(2,1)S(1)} %copy-done.2, bf16[512,2048]{1,0:T(8,128)(2,1)} %collective-permute-done.2.refs_3_.refs_5_.refs_1_, ...), custom_call_target="tpu_custom_call" | custom-call | flops 2000000000 | bytes 1048576 | tf_op jit(solution)/shard_map/scores/pallas_call | solution.py:144
  102.0 2.6 %collective-permute-done.12.refs_1_ = bf16[512,2048]{1,0:T(8,128)(2,1)} collective-permute-done((bf16[512,2048]{1,0:T(8,128)(2,1)}, bf16[512,2048]{1,0:T(8,128)(2,1)}, u32[]{:S(2)}, u32[]{:S(2)}) %collective-permute-start.12) | collective-permute-done | bytes 2097184 | tf_op jit(solution)/shard_map/ppermute | solution.py:200
  104.5 0.8 fold.7
  105.4 1.3 collective-permute-start.16
  106.7 7.3 %product.8 = (f32[256,2048]{1,0:T(8,128)S(1)}, bf16[128,2048]{1,0:T(8,128)(2,1)S(1)}, bf16[128,2048]{1,0:T(8,128)(2,1)S(1)}) custom-call(s32[3]{0:T(128)S(1)} %pad_add_fusion.flags, bf16[512,2048]{1,0:T(8,128)(2,1)} %collective-permute-done.8.refs_0_, bf16[512,2048]{1,0:T(8,128)(2,1)} %collective-permute-done.12.refs_1_, bf16[2048,2048]{1,0:T(8,128)(2,1)S(1)} %bitcast.117), custom_call_target="tpu_custom_call" | custom-call | flops 1 | bytes 1 | tf_op jit(solution)/shard_map/product/pallas_call | solution.py:80
  114.6 1.4 collective-permute-done.18.refs_0_
  116.0 0.7 collective-permute-done.19.refs_1_
  116.8 0.8 fold.8
  117.6 1.8 collective-permute-start.20
  119.4 7.1 %collective-permute-start.21 = (bf16[4,512,128]{2,1,0:T(8,128)(2,1)S(1)}, bf16[4,512,128]{2,1,0:T(8,128)(2,1)S(1)}, u32[]{:S(2)}, u32[]{:S(2)}) collective-permute-start(bf16[4,512,128]{2,1,0:T(8,128)(2,1)S(1)} %scores.3), channel_id=1, source_target_pairs={{0,1},{3,2},{4,5},{7,6},{8,9},{11,10},{12,13},{15,14},{16,17},{19,... | collective-permute-start | bytes 1572872 | tf_op jit(solution)/shard_map/ppermute | solution.py:200
  126.6 0.9 collective-permute-start.22
  128.0 4.4 %collective-permute-done.20.refs_1_ = bf16[128,2048]{1,0:T(8,128)(2,1)S(1)} collective-permute-done((bf16[128,2048]{1,0:T(8,128)(2,1)S(1)}, bf16[128,2048]{1,0:T(8,128)(2,1)S(1)}, u32[]{:S(2)}, u32[]{:S(2)}) %collective-permute-start.20) | collective-permute-done | bytes 524320 | tf_op jit(solution)/shard_map/ppermute | solution.py:203
  132.4 5.3 %collective-permute-done.21 = bf16[4,512,128]{2,1,0:T(8,128)(2,1)S(1)} collective-permute-done((bf16[4,512,128]{2,1,0:T(8,128)(2,1)S(1)}, bf16[4,512,128]{2,1,0:T(8,128)(2,1)S(1)}, u32[]{:S(2)}, u32[]{:S(2)}) %collective-permute-start.21) | collective-permute-done | bytes 524320 | tf_op jit(solution)/shard_map/ppermute | solution.py:200
  137.7 4.0 %scores.5 = bf16[4,512,128]{2,1,0:T(8,128)(2,1)S(1)} custom-call(f32[128,2048]{1,0:T(8,128)S(1)} %get-tuple-element.144.refs_0_, bf16[128,2048]{1,0:T(8,128)(2,1)S(1)} %collective-permute-done.20.refs_1_, bf16[512,2048]{1,0:T(8,128)(2,1)S(1)} %copy-done.2, bf16[512,2048]{1,0:T(8,128)(2,1)} %collective-permute-done.2.refs_3_.refs_5_.refs_1_, ...), custom_call_target="tpu_custom_call" | custom-call | flops 1 | bytes 1 | tf_op jit(solution)/shard_map/scores/pallas_call | solution.py:144
  141.7 0.7 collective-permute-start.23
  142.4 4.5 %collective-permute-start.24 = (s32[512,16]{0,1:T(8,128)S(1)}, s32[512,16]{0,1:T(8,128)S(1)}, u32[]{:S(2)}, u32[]{:S(2)}) collective-permute-start(s32[512,16]{0,1:T(8,128)S(1)} %copy-done.10), channel_id=1, source_target_pairs={{0,3},{3,0},{4,7},{7,4},{8,11},{11,8},{12,15},{15,12},{16,19},{19,... | collective-permute-start | bytes 98312 | tf_op jit(solution)/shard_map/ppermute | solution.py:200
  147.0 6.5 %scores.4 = (f32[4,512,128]{2,1,0:T(8,128)S(1)}, f32[4,512,128]{2,1,0:T(8,128)S(1)}) custom-call(f32[128,2048]{1,0:T(8,128)S(1)} %get-tuple-element.122.refs_0_, bf16[128,2048]{1,0:T(8,128)(2,1)S(1)} %collective-permute-done.17.refs_1_, f32[128,2048]{1,0:T(8,128)S(1)} %copy-done.9, f32[128,2048]{1,0:T(8,128)} %collective-permute-done.11.refs_3_, ...), custom_call_target="tpu_custom_call" | custom-call | flops 1 | bytes 1 | tf_op jit(solution)/shard_map/scores/pallas_call | solution.py:144
  153.5 4.5 %collective-permute-done.16.refs_0_ = bf16[512,2048]{1,0:T(8,128)(2,1)S(1)} collective-permute-done((bf16[512,2048]{1,0:T(8,128)(2,1)}, bf16[512,2048]{1,0:T(8,128)(2,1)S(1)}, u32[]{:S(2)}, u32[]{:S(2)}) %collective-permute-start.16) | collective-permute-done | bytes 2097184 | tf_op jit(solution)/shard_map/ppermute | solution.py:200
  158.0 5.6 %product.9 = (f32[256,2048]{1,0:T(8,128)S(1)}, bf16[128,2048]{1,0:T(8,128)(2,1)S(1)}, bf16[128,2048]{1,0:T(8,128)(2,1)S(1)}) custom-call(s32[3]{0:T(128)S(1)} %pad_add_fusion.flags, bf16[512,2048]{1,0:T(8,128)(2,1)S(1)} %collective-permute-done.16.refs_0_, bf16[2048,2048]{1,0:T(8,128)(2,1)S(1)} %bitcast.117), custom_call_target="tpu_custom_call" | custom-call | flops 1 | bytes 1 | tf_op jit(solution)/shard_map/product/pallas_call | solution.py:80
  164.2 1.4 collective-permute-done.25.refs_0_
  165.6 0.7 collective-permute-done.26.refs_1_
  166.3 0.8 fold.9
  167.3 1.3 collective-permute-start.29
  168.6 1.6 collective-permute-start.27
  170.1 5.4 %collective-permute-start.28 = (bf16[4,512,128]{2,1,0:T(8,128)(2,1)S(1)}, bf16[4,512,128]{2,1,0:T(8,128)(2,1)S(1)}, u32[]{:S(2)}, u32[]{:S(2)}) collective-permute-start(bf16[4,512,128]{2,1,0:T(8,128)(2,1)S(1)} %scores.5), channel_id=1, source_target_pairs={{0,2},{3,1},{4,6},{7,5},{8,10},{11,9},{12,14},{15,13},{16,18},{19,... | collective-permute-start | bytes 1572872 | tf_op jit(solution)/shard_map/ppermute | solution.py:200
  175.6 1.7 convert_add_fusion.counts
  177.2 5.3 %collective-permute-done.27.got = bf16[128,2048]{1,0:T(8,128)(2,1)S(1)} collective-permute-done((bf16[128,2048]{1,0:T(8,128)(2,1)S(1)}, bf16[128,2048]{1,0:T(8,128)(2,1)S(1)}, u32[]{:S(2)}, u32[]{:S(2)}) %collective-permute-start.27) | collective-permute-done | bytes 524320 | tf_op jit(solution)/shard_map/ppermute | solution.py:203
  182.6 1.3 last_scores.2
  183.9 3.5 %last_scores.3 = (bf16[2,528,128]{2,1,0:T(8,128)(2,1)S(1)}, f32[8,128]{1,0:T(8,128)}) custom-call(f32[128,2048]{1,0:T(8,128)S(1)} %get-tuple-element.158.kept, bf16[128,2048]{1,0:T(8,128)(2,1)S(1)} %collective-permute-done.27.got, f32[4,512,128]{2,1,0:T(8,128)S(1)} %convert_add_fusion.counts, f32[8,128]{1,0:T(8,128)S(1)} %get-tuple-element.164.before, ...), custom_call_target="tpu_custom_call" | custom-call | flops 1 | bytes 1 | tf_op jit(solution)/shard_map/last_scores/pallas_call | solution.py:176
  187.4 4.2 %collective-permute-start.34 = (bf16[2,512,128]{2,1,0:T(8,128)(2,1)S(1)}, bf16[2,512,128]{2,1,0:T(8,128)(2,1)}, u32[]{:S(2)}, u32[]{:S(2)}) collective-permute-start(bf16[2,512,128]{2,1,0:T(8,128)(2,1)S(1)} %get-tuple-element.175), channel_id=1, source_target_pairs={{0,3},{3,0},{4,7},{7,4},{8,11},{11,8},{12,15},{15,12},{16,19},{19,... | collective-permute-start | bytes 786440 | tf_op jit(solution)/shard_map/ppermute | solution.py:200
  192.2 1.6 collective-permute-start.30
  193.7 0.6 collective-permute-start.32
  194.4 3.4 %collective-permute-start.33 = (bf16[2,528,128]{2,1,0:T(8,128)(2,1)S(1)}, bf16[2,528,128]{2,1,0:T(8,128)(2,1)S(1)}, u32[]{:S(2)}, u32[]{:S(2)}) collective-permute-start(bf16[2,528,128]{2,1,0:T(8,128)(2,1)S(1)} %get-tuple-element.174), channel_id=1, source_target_pairs={{0,3},{3,0},{4,7},{7,4},{8,11},{11,8},{12,15},{15,12},{16,19},{19,... | collective-permute-start | bytes 811016 | tf_op jit(solution)/shard_map/ppermute | solution.py:200
  197.8 0.9 collective-permute-done.34
  198.7 1.0 slice_bitcast_fusion.5
  199.7 1.6 collective-permute-start.35
  201.6 4.7 %collective-permute-done.32 = f32[520,128]{1,0:T(8,128)S(1)} collective-permute-done((f32[520,128]{1,0:T(8,128)S(1)}, f32[520,128]{1,0:T(8,128)S(1)}, u32[]{:S(2)}, u32[]{:S(2)}) %collective-permute-start.32) | collective-permute-done | bytes 266272 | tf_op jit(solution)/shard_map/ppermute | solution.py:203
  206.5 1.5 collective-permute-start.38
  207.9 1.0 collective-permute-start.39
  209.1 1.9 collective-permute-done.38
  211.7 1.1 slice_add_fusion
  (88 shorter events, 7.2 us)
Async XLA Ops:
  0.6 6.8 %collective-permute-start.2 = (bf16[512,2048]{1,0:T(8,128)(2,1)}, bf16[512,2048]{1,0:T(8,128)(2,1)}, u32[]{:S(2)}, u32[]{:S(2)}) collective-permute-start(bf16[512,2048]{1,0:T(8,128)(2,1)} %refs_0_.1), channel_id=1, source_target_pairs={{0,4},{4,0},{8,12},{12,8},{1,5},{5,1},{9,13},{13,9},{2,6},{6,2},{1... | collective-permute-start | bytes 6291464 | tf_op jit(solution)/shard_map/ppermute | solution.py:203
  1.1 49.0 %collective-permute-start.5 = (bf16[512,2048]{1,0:T(8,128)(2,1)}, bf16[512,2048]{1,0:T(8,128)(2,1)S(1)}, u32[]{:S(2)}, u32[]{:S(2)}) collective-permute-start(bf16[512,2048]{1,0:T(8,128)(2,1)} %refs_0_.1), channel_id=1, source_target_pairs={{0,8},{4,12},{8,0},{12,4},{1,9},{5,13},{9,1},{13,5},{2,10},{6,14},... | collective-permute-start | bytes 6291464 | tf_op jit(solution)/shard_map/ppermute | solution.py:203
  3.7 49.0 %collective-permute-start = (bf16[512,2048]{1,0:T(8,128)(2,1)}, bf16[512,2048]{1,0:T(8,128)(2,1)}, u32[]{:S(2)}, u32[]{:S(2)}) collective-permute-start(bf16[512,2048]{1,0:T(8,128)(2,1)} %refs_0_), channel_id=1, source_target_pairs={{0,1},{1,0},{2,3},{3,2},{4,5},{5,4},{6,7},{7,6},{8,9},{9,8},{10,11... | collective-permute-start | bytes 6291464 | tf_op jit(solution)/shard_map/ppermute | solution.py:200
  5.3 47.4 %collective-permute-start.1 = (bf16[512,2048]{1,0:T(8,128)(2,1)}, bf16[512,2048]{1,0:T(8,128)(2,1)}, u32[]{:S(2)}, u32[]{:S(2)}) collective-permute-start(bf16[512,2048]{1,0:T(8,128)(2,1)} %refs_0_), channel_id=1, source_target_pairs={{1,2},{2,1},{5,6},{6,5},{9,10},{10,9},{13,14},{14,13},{17,18},{18,... | collective-permute-start | bytes 6291464 | tf_op jit(solution)/shard_map/ppermute | solution.py:200
  7.4 3.4 %copy-start = (bf16[2048,2048]{1,0:T(8,128)(2,1)S(1)}, bf16[2048,2048]{1,0:T(8,128)(2,1)}, u32[]{:S(2)}) copy-start(bf16[2048,2048]{1,0:T(8,128)(2,1)} %refs_1_.5) | copy-start | bytes 25165828
  10.8 1.6 copy-start.7
  17.9 32.4 %collective-permute-start.3 = (bf16[128,2048]{1,0:T(8,128)(2,1)S(1)}, bf16[128,2048]{1,0:T(8,128)(2,1)S(1)}, u32[]{:S(2)}, u32[]{:S(2)}) collective-permute-start(bf16[128,2048]{1,0:T(8,128)(2,1)S(1)} %get-tuple-element.91), channel_id=1, source_target_pairs={{0,4},{4,0},{8,12},{12,8},{1,5},{5,1},{9,13},{13,9},{2,6},{6,2},{1... | collective-permute-start | bytes 1572872 | tf_op jit(solution)/shard_map/ppermute | solution.py:203
  18.0 32.9 %collective-permute-start.4 = (bf16[128,2048]{1,0:T(8,128)(2,1)S(1)}, bf16[128,2048]{1,0:T(8,128)(2,1)S(1)}, u32[]{:S(2)}, u32[]{:S(2)}) collective-permute-start(bf16[128,2048]{1,0:T(8,128)(2,1)S(1)} %get-tuple-element.92), channel_id=1, source_target_pairs={{0,4},{4,0},{8,12},{12,8},{1,5},{5,1},{9,13},{13,9},{2,6},{6,2},{1... | collective-permute-start | bytes 1572872 | tf_op jit(solution)/shard_map/ppermute | solution.py:203
  50.3 2.7 %collective-permute-start.6 = (bf16[256,2048]{1,0:T(8,128)(2,1)S(1)}, bf16[256,2048]{1,0:T(8,128)(2,1)S(1)}, u32[]{:S(2)}, u32[]{:S(2)}) collective-permute-start(bf16[256,2048]{1,0:T(8,128)(2,1)S(1)} %get-tuple-element.179), channel_id=1, source_target_pairs={{0,4},{4,0},{8,12},{12,8},{1,5},{5,1},{9,13},{13,9},{2,6},{6,2},{1... | collective-permute-start | bytes 3145736 | tf_op jit(solution)/shard_map/ppermute | solution.py:203
  50.4 4.1 %collective-permute-start.7 = (bf16[256,2048]{1,0:T(8,128)(2,1)S(1)}, bf16[256,2048]{1,0:T(8,128)(2,1)S(1)}, u32[]{:S(2)}, u32[]{:S(2)}) collective-permute-start(bf16[256,2048]{1,0:T(8,128)(2,1)S(1)} %get-tuple-element.178), channel_id=1, source_target_pairs={{0,4},{4,0},{8,12},{12,8},{1,5},{5,1},{9,13},{13,9},{2,6},{6,2},{1... | collective-permute-start | bytes 3145736 | tf_op jit(solution)/shard_map/ppermute | solution.py:203
  50.9 8.9 %slice-start = ((s8[8388608]{0:T(1024)(128)(4,1)}), s8[4194304]{0:T(1024)(128)(4,1)S(1)}, s32[]{:S(2)}) async-start(s8[8388608]{0:T(1024)(128)(4,1)} %bitcast.114), calls=%async_computation | async-start | bytes 8388608
  50.9 8.9 %slice-start.1 = ((s8[8388608]{0:T(1024)(128)(4,1)}), s8[4194304]{0:T(1024)(128)(4,1)S(1)}, s32[]{:S(2)}) async-start(s8[8388608]{0:T(1024)(128)(4,1)} %bitcast.114), calls=%async_computation.1 | async-start | bytes 8388608
  52.7 15.4 %copy-start.8 = (f32[128,2048]{1,0:T(8,128)}, f32[128,2048]{1,0:T(8,128)S(1)}, u32[]{:S(2)}) copy-start(f32[128,2048]{1,0:T(8,128)S(1)} %get-tuple-element.124.refs_2_) | copy-start | bytes 3145732
  54.5 13.6 %copy-start.3 = (bf16[256,2048]{1,0:T(8,128)(2,1)}, bf16[256,2048]{1,0:T(8,128)(2,1)S(1)}, u32[]{:S(2)}) copy-start(bf16[256,2048]{1,0:T(8,128)(2,1)S(1)} %collective-permute-done.7.refs_6_.refs_8_.refs_2_) | copy-start | bytes 3145732
  54.5 15.7 %copy-start.10 = (s32[512,16]{0,1:T(8,128)S(1)}, s32[512,16]{0,1:T(8,128)}, u32[]{:S(2)}) copy-start(s32[512,16]{0,1:T(8,128)} %param.7) | copy-start | bytes 98308
  54.5 50.0 %collective-permute-start.12 = (bf16[512,2048]{1,0:T(8,128)(2,1)}, bf16[512,2048]{1,0:T(8,128)(2,1)}, u32[]{:S(2)}, u32[]{:S(2)}) collective-permute-start(bf16[512,2048]{1,0:T(8,128)(2,1)} %collective-permute-done.1.refs_0_), channel_id=1, source_target_pairs={{1,0},{2,3},{5,4},{6,7},{9,8},{10,11},{13,12},{14,15},{17,16},{18,... | collective-permute-start | bytes 6291464 | tf_op jit(solution)/shard_map/ppermute | solution.py:200
  55.9 49.4 %collective-permute-start.8 = (bf16[512,2048]{1,0:T(8,128)(2,1)}, bf16[512,2048]{1,0:T(8,128)(2,1)}, u32[]{:S(2)}, u32[]{:S(2)}) collective-permute-start(bf16[512,2048]{1,0:T(8,128)(2,1)} %collective-permute-done.refs_1_.refs_0_), channel_id=1, source_target_pairs={{1,2},{2,1},{5,6},{6,5},{9,10},{10,9},{13,14},{14,13},{17,18},{18,... | collective-permute-start | bytes 6291464 | tf_op jit(solution)/shard_map/ppermute | solution.py:200
  58.0 25.5 %collective-permute-start.11 = (f32[128,2048]{1,0:T(8,128)}, f32[128,2048]{1,0:T(8,128)}, u32[]{:S(2)}, u32[]{:S(2)}) collective-permute-start(f32[128,2048]{1,0:T(8,128)} %get-tuple-element.102), channel_id=1, source_target_pairs={{0,8},{4,12},{8,0},{12,4},{1,9},{5,13},{9,1},{13,5},{2,10},{6,14},... | collective-permute-start | bytes 3145736 | tf_op jit(solution)/shard_map/ppermute | solution.py:203
  68.1 1.5 copy-start.5
  69.6 2.3 %collective-permute-start.10 = (bf16[128,2048]{1,0:T(8,128)(2,1)}, bf16[128,2048]{1,0:T(8,128)(2,1)}, u32[]{:S(2)}, u32[]{:S(2)}) collective-permute-start(bf16[128,2048]{1,0:T(8,128)(2,1)} %get-tuple-element.100), channel_id=1, source_target_pairs={{0,4},{4,0},{8,12},{12,8},{1,5},{5,1},{9,13},{13,9},{2,6},{6,2},{1... | collective-permute-start | bytes 1572872 | tf_op jit(solution)/shard_map/ppermute | solution.py:203
  69.6 3.0 %collective-permute-start.9 = (bf16[128,2048]{1,0:T(8,128)(2,1)}, bf16[128,2048]{1,0:T(8,128)(2,1)}, u32[]{:S(2)}, u32[]{:S(2)}) collective-permute-start(bf16[128,2048]{1,0:T(8,128)(2,1)} %get-tuple-element.99), channel_id=1, source_target_pairs={{0,4},{4,0},{8,12},{12,8},{1,5},{5,1},{9,13},{13,9},{2,6},{6,2},{1... | collective-permute-start | bytes 1572872 | tf_op jit(solution)/shard_map/ppermute | solution.py:203
  72.6 1.6 copy-start.6
  83.5 14.2 %collective-permute-start.15 = (bf16[128,2048]{1,0:T(8,128)(2,1)S(1)}, bf16[128,2048]{1,0:T(8,128)(2,1)S(1)}, u32[]{:S(2)}, u32[]{:S(2)}) collective-permute-start(bf16[128,2048]{1,0:T(8,128)(2,1)S(1)} %get-tuple-element.114), channel_id=1, source_target_pairs={{0,8},{4,12},{8,0},{12,4},{1,9},{5,13},{9,1},{13,5},{2,10},{6,14},... | collective-permute-start | bytes 1572872 | tf_op jit(solution)/shard_map/ppermute | solution.py:203
  85.3 3.4 %copy-start.1 = (bf16[2048,2048]{1,0:T(8,128)(2,1)S(1)}, bf16[2048,2048]{1,0:T(8,128)(2,1)}, u32[]{:S(2)}) copy-start(bf16[2048,2048]{1,0:T(8,128)(2,1)} %refs_1_.5) | copy-start | bytes 25165828
  88.7 9.1 %copy-start.2 = (bf16[512,2048]{1,0:T(8,128)(2,1)S(1)}, bf16[512,2048]{1,0:T(8,128)(2,1)}, u32[]{:S(2)}) copy-start(bf16[512,2048]{1,0:T(8,128)(2,1)} %refs_0_.1) | copy-start | bytes 6291460
  88.7 9.1 %copy-start.4 = (bf16[256,2048]{1,0:T(8,128)(2,1)S(1)}, bf16[256,2048]{1,0:T(8,128)(2,1)}, u32[]{:S(2)}) copy-start(bf16[256,2048]{1,0:T(8,128)(2,1)} %copy-done.3) | copy-start | bytes 3145732
  95.5 9.0 %collective-permute-start.13 = (bf16[128,2048]{1,0:T(8,128)(2,1)S(1)}, bf16[128,2048]{1,0:T(8,128)(2,1)S(1)}, u32[]{:S(2)}, u32[]{:S(2)}) collective-permute-start(bf16[128,2048]{1,0:T(8,128)(2,1)S(1)} %get-tuple-element.107), channel_id=1, source_target_pairs={{0,4},{4,0},{8,12},{12,8},{1,5},{5,1},{9,13},{13,9},{2,6},{6,2},{1... | collective-permute-start | bytes 1572872 | tf_op jit(solution)/shard_map/ppermute | solution.py:203
  95.6 8.9 %collective-permute-start.14 = (bf16[128,2048]{1,0:T(8,128)(2,1)S(1)}, bf16[128,2048]{1,0:T(8,128)(2,1)S(1)}, u32[]{:S(2)}, u32[]{:S(2)}) collective-permute-start(bf16[128,2048]{1,0:T(8,128)(2,1)S(1)} %get-tuple-element.108), channel_id=1, source_target_pairs={{0,4},{4,0},{8,12},{12,8},{1,5},{5,1},{9,13},{13,9},{2,6},{6,2},{1... | collective-permute-start | bytes 1572872 | tf_op jit(solution)/shard_map/ppermute | solution.py:203
  97.8 8.9 %slice-start.2 = ((s8[8388608]{0:T(1024)(128)(4,1)}), s8[4194304]{0:T(1024)(128)(4,1)S(1)}, s32[]{:S(2)}) async-start(s8[8388608]{0:T(1024)(128)(4,1)} %bitcast.116), calls=%async_computation.2 | async-start | bytes 8388608
  97.8 8.9 %slice-start.3 = ((s8[8388608]{0:T(1024)(128)(4,1)}), s8[4194304]{0:T(1024)(128)(4,1)S(1)}, s32[]{:S(2)}) async-start(s8[8388608]{0:T(1024)(128)(4,1)} %bitcast.116), calls=%async_computation.3 | async-start | bytes 8388608
  105.4 52.6 %collective-permute-start.16 = (bf16[512,2048]{1,0:T(8,128)(2,1)}, bf16[512,2048]{1,0:T(8,128)(2,1)S(1)}, u32[]{:S(2)}, u32[]{:S(2)}) collective-permute-start(bf16[512,2048]{1,0:T(8,128)(2,1)} %collective-permute-done.8.refs_0_), channel_id=1, source_target_pairs={{1,0},{2,3},{5,4},{6,7},{9,8},{10,11},{13,12},{14,15},{17,16},{18,... | collective-permute-start | bytes 6291464 | tf_op jit(solution)/shard_map/ppermute | solution.py:200
  114.0 2.0 collective-permute-start.18
  114.1 2.6 %collective-permute-start.19 = (bf16[128,2048]{1,0:T(8,128)(2,1)S(1)}, bf16[128,2048]{1,0:T(8,128)(2,1)S(1)}, u32[]{:S(2)}, u32[]{:S(2)}) collective-permute-start(bf16[128,2048]{1,0:T(8,128)(2,1)S(1)} %get-tuple-element.135), channel_id=1, source_target_pairs={{0,4},{4,0},{8,12},{12,8},{1,5},{5,1},{9,13},{13,9},{2,6},{6,2},{1... | collective-permute-start | bytes 1572872 | tf_op jit(solution)/shard_map/ppermute | solution.py:203
  117.6 29.4 %copy-start.9 = (f32[128,2048]{1,0:T(8,128)S(1)}, f32[128,2048]{1,0:T(8,128)}, u32[]{:S(2)}) copy-start(f32[128,2048]{1,0:T(8,128)} %copy-done.8) | copy-start | bytes 3145732
  117.6 14.8 %collective-permute-start.20 = (bf16[128,2048]{1,0:T(8,128)(2,1)S(1)}, bf16[128,2048]{1,0:T(8,128)(2,1)S(1)}, u32[]{:S(2)}, u32[]{:S(2)}) collective-permute-start(bf16[128,2048]{1,0:T(8,128)(2,1)S(1)} %get-tuple-element.139), channel_id=1, source_target_pairs={{0,8},{4,12},{8,0},{12,4},{1,9},{5,13},{9,1},{13,5},{2,10},{6,14},... | collective-permute-start | bytes 1572872 | tf_op jit(solution)/shard_map/ppermute | solution.py:203
  119.4 18.3 %collective-permute-start.21 = (bf16[4,512,128]{2,1,0:T(8,128)(2,1)S(1)}, bf16[4,512,128]{2,1,0:T(8,128)(2,1)S(1)}, u32[]{:S(2)}, u32[]{:S(2)}) collective-permute-start(bf16[4,512,128]{2,1,0:T(8,128)(2,1)S(1)} %scores.3), channel_id=1, source_target_pairs={{0,1},{3,2},{4,5},{7,6},{8,9},{11,10},{12,13},{15,14},{16,17},{19,... | collective-permute-start | bytes 1572872 | tf_op jit(solution)/shard_map/ppermute | solution.py:200
  126.6 11.2 %collective-permute-start.22 = (bf16[4,512,128]{2,1,0:T(8,128)(2,1)S(1)}, bf16[4,512,128]{2,1,0:T(8,128)(2,1)S(1)}, u32[]{:S(2)}, u32[]{:S(2)}) collective-permute-start(bf16[4,512,128]{2,1,0:T(8,128)(2,1)S(1)} %scores.3), channel_id=1, source_target_pairs={{1,2},{2,1},{5,6},{6,5},{9,10},{10,9},{13,14},{14,13},{17,18},{18,... | collective-permute-start | bytes 1572872 | tf_op jit(solution)/shard_map/ppermute | solution.py:200
  127.5 19.5 %collective-permute-start.17 = (bf16[128,2048]{1,0:T(8,128)(2,1)S(1)}, bf16[128,2048]{1,0:T(8,128)(2,1)S(1)}, u32[]{:S(2)}, u32[]{:S(2)}) collective-permute-start(bf16[128,2048]{1,0:T(8,128)(2,1)S(1)} %get-tuple-element.123), channel_id=1, source_target_pairs={{0,8},{4,12},{8,0},{12,4},{1,9},{5,13},{9,1},{13,5},{2,10},{6,14},... | collective-permute-start | bytes 1572872 | tf_op jit(solution)/shard_map/ppermute | solution.py:203
  141.7 11.8 %collective-permute-start.23 = (bf16[4,512,128]{2,1,0:T(8,128)(2,1)S(1)}, bf16[4,512,128]{2,1,0:T(8,128)(2,1)S(1)}, u32[]{:S(2)}, u32[]{:S(2)}) collective-permute-start(bf16[4,512,128]{2,1,0:T(8,128)(2,1)S(1)} %scores.5), channel_id=1, source_target_pairs={{1,2},{2,1},{5,6},{6,5},{9,10},{10,9},{13,14},{14,13},{17,18},{18,... | collective-permute-start | bytes 1572872 | tf_op jit(solution)/shard_map/ppermute | solution.py:200
  142.4 11.1 %collective-permute-start.24 = (s32[512,16]{0,1:T(8,128)S(1)}, s32[512,16]{0,1:T(8,128)S(1)}, u32[]{:S(2)}, u32[]{:S(2)}) collective-permute-start(s32[512,16]{0,1:T(8,128)S(1)} %copy-done.10), channel_id=1, source_target_pairs={{0,3},{3,0},{4,7},{7,4},{8,11},{11,8},{12,15},{15,12},{16,19},{19,... | collective-permute-start | bytes 98312 | tf_op jit(solution)/shard_map/ppermute | solution.py:200
  163.6 2.0 collective-permute-start.25
  163.7 2.6 %collective-permute-start.26 = (bf16[128,2048]{1,0:T(8,128)(2,1)S(1)}, bf16[128,2048]{1,0:T(8,128)(2,1)S(1)}, u32[]{:S(2)}, u32[]{:S(2)}) collective-permute-start(bf16[128,2048]{1,0:T(8,128)(2,1)S(1)} %get-tuple-element.154), channel_id=1, source_target_pairs={{0,4},{4,0},{8,12},{12,8},{1,5},{5,1},{9,13},{13,9},{2,6},{6,2},{1... | collective-permute-start | bytes 1572872 | tf_op jit(solution)/shard_map/ppermute | solution.py:203
  167.3 20.2 %collective-permute-start.29 = (bf16[4,512,128]{2,1,0:T(8,128)(2,1)S(1)}, bf16[4,512,128]{2,1,0:T(8,128)(2,1)S(1)}, u32[]{:S(2)}, u32[]{:S(2)}) collective-permute-start(bf16[4,512,128]{2,1,0:T(8,128)(2,1)S(1)} %add_convert_fusion), channel_id=1, source_target_pairs={{1,0},{2,3},{5,4},{6,7},{9,8},{10,11},{13,12},{14,15},{17,16},{18,... | collective-permute-start | bytes 1572872 | tf_op jit(solution)/shard_map/ppermute | solution.py:200
  168.6 14.0 %collective-permute-start.27 = (bf16[128,2048]{1,0:T(8,128)(2,1)S(1)}, bf16[128,2048]{1,0:T(8,128)(2,1)S(1)}, u32[]{:S(2)}, u32[]{:S(2)}) collective-permute-start(bf16[128,2048]{1,0:T(8,128)(2,1)S(1)} %get-tuple-element.159), channel_id=1, source_target_pairs={{0,8},{4,12},{8,0},{12,4},{1,9},{5,13},{9,1},{13,5},{2,10},{6,14},... | collective-permute-start | bytes 1572872 | tf_op jit(solution)/shard_map/ppermute | solution.py:203
  170.1 17.3 %collective-permute-start.28 = (bf16[4,512,128]{2,1,0:T(8,128)(2,1)S(1)}, bf16[4,512,128]{2,1,0:T(8,128)(2,1)S(1)}, u32[]{:S(2)}, u32[]{:S(2)}) collective-permute-start(bf16[4,512,128]{2,1,0:T(8,128)(2,1)S(1)} %scores.5), channel_id=1, source_target_pairs={{0,2},{3,1},{4,6},{7,5},{8,10},{11,9},{12,14},{15,13},{16,18},{19,... | collective-permute-start | bytes 1572872 | tf_op jit(solution)/shard_map/ppermute | solution.py:200
  187.4 11.3 %collective-permute-start.34 = (bf16[2,512,128]{2,1,0:T(8,128)(2,1)S(1)}, bf16[2,512,128]{2,1,0:T(8,128)(2,1)}, u32[]{:S(2)}, u32[]{:S(2)}) collective-permute-start(bf16[2,512,128]{2,1,0:T(8,128)(2,1)S(1)} %get-tuple-element.175), channel_id=1, source_target_pairs={{0,3},{3,0},{4,7},{7,4},{8,11},{11,8},{12,15},{15,12},{16,19},{19,... | collective-permute-start | bytes 786440 | tf_op jit(solution)/shard_map/ppermute | solution.py:200
  192.2 9.4 %collective-permute-start.30 = (f32[520,128]{1,0:T(8,128)S(1)}, f32[520,128]{1,0:T(8,128)S(1)}, u32[]{:S(2)}, u32[]{:S(2)}) collective-permute-start(f32[520,128]{1,0:T(8,128)S(1)} %get-tuple-element.230), channel_id=1, source_target_pairs={{0,8},{4,12},{8,0},{12,4},{1,9},{5,13},{9,1},{13,5},{2,10},{6,14},... | collective-permute-start | bytes 798728 | tf_op jit(solution)/shard_map/ppermute | solution.py:203
  193.7 7.9 %collective-permute-start.31 = (f32[520,128]{1,0:T(8,128)S(1)}, f32[520,128]{1,0:T(8,128)S(1)}, u32[]{:S(2)}, u32[]{:S(2)}) collective-permute-start(f32[520,128]{1,0:T(8,128)S(1)} %get-tuple-element.231), channel_id=1, source_target_pairs={{0,4},{4,0},{8,12},{12,8},{1,5},{5,1},{9,13},{13,9},{2,6},{6,2},{1... | collective-permute-start | bytes 798728 | tf_op jit(solution)/shard_map/ppermute | solution.py:203
  193.7 12.6 %collective-permute-start.32 = (f32[520,128]{1,0:T(8,128)S(1)}, f32[520,128]{1,0:T(8,128)S(1)}, u32[]{:S(2)}, u32[]{:S(2)}) collective-permute-start(f32[520,128]{1,0:T(8,128)S(1)} %get-tuple-element.232), channel_id=1, source_target_pairs={{0,12},{4,8},{8,4},{12,0},{1,13},{5,9},{9,5},{13,1},{2,14},{6,10},... | collective-permute-start | bytes 798728 | tf_op jit(solution)/shard_map/ppermute | solution.py:203
  194.4 12.1 %collective-permute-start.33 = (bf16[2,528,128]{2,1,0:T(8,128)(2,1)S(1)}, bf16[2,528,128]{2,1,0:T(8,128)(2,1)S(1)}, u32[]{:S(2)}, u32[]{:S(2)}) collective-permute-start(bf16[2,528,128]{2,1,0:T(8,128)(2,1)S(1)} %get-tuple-element.174), channel_id=1, source_target_pairs={{0,3},{3,0},{4,7},{7,4},{8,11},{11,8},{12,15},{15,12},{16,19},{19,... | collective-permute-start | bytes 811016 | tf_op jit(solution)/shard_map/ppermute | solution.py:200
  199.7 11.9 %collective-permute-start.35 = (bf16[512,128]{1,0:T(8,128)(2,1)S(1)}, bf16[512,128]{1,0:T(8,128)(2,1)S(1)}, u32[]{:S(2)}, u32[]{:S(2)}) collective-permute-start(bf16[512,128]{1,0:T(8,128)(2,1)S(1)} %get-tuple-element.197), channel_id=1, source_target_pairs={{0,8},{4,12},{8,0},{12,4},{1,9},{5,13},{9,1},{13,5},{2,10},{6,14},... | collective-permute-start | bytes 393224 | tf_op jit(solution)/shard_map/ppermute | solution.py:203
  201.6 10.0 %collective-permute-start.37 = (bf16[512,128]{1,0:T(8,128)(2,1)S(1)}, bf16[512,128]{1,0:T(8,128)(2,1)S(1)}, u32[]{:S(2)}, u32[]{:S(2)}) collective-permute-start(bf16[512,128]{1,0:T(8,128)(2,1)S(1)} %get-tuple-element.196), channel_id=1, source_target_pairs={{0,12},{4,8},{8,4},{12,0},{1,13},{5,9},{9,5},{13,1},{2,14},{6,10},... | collective-permute-start | bytes 393224 | tf_op jit(solution)/shard_map/ppermute | solution.py:203
  206.5 4.5 %collective-permute-start.38 = (bf16[16,128]{1,0:T(8,128)(2,1)S(1)}, bf16[16,128]{1,0:T(8,128)(2,1)S(1)}, u32[]{:S(2)}, u32[]{:S(2)}) collective-permute-start(bf16[16,128]{1,0:T(8,128)(2,1)S(1)} %slice_bitcast_fusion.8), channel_id=1, source_target_pairs={{0,8},{4,12},{8,0},{12,4},{1,9},{5,13},{9,1},{13,5},{2,10},{6,14},... | collective-permute-start | bytes 12296 | tf_op jit(solution)/shard_map/ppermute | solution.py:203
  207.9 3.1 %collective-permute-start.39 = (bf16[16,128]{1,0:T(8,128)(2,1)S(1)}, bf16[16,128]{1,0:T(8,128)(2,1)S(1)}, u32[]{:S(2)}, u32[]{:S(2)}) collective-permute-start(bf16[16,128]{1,0:T(8,128)(2,1)S(1)} %slice_bitcast_fusion.8), channel_id=1, source_target_pairs={{0,12},{4,8},{8,4},{12,0},{1,13},{5,9},{9,5},{13,1},{2,14},{6,10},... | collective-permute-start | bytes 12296 | tf_op jit(solution)/shard_map/ppermute | solution.py:203
  208.9 2.1 collective-permute-start.36

commit v17 on v14

--- a/solution.py
+++ b/solution.py
@@ -187,6 +187,23 @@
     )(kept, got, counts, before, *[piece[2] for piece in grads])
 
 
+def hold_body(*refs):
+    for n in range(len(refs) // 2):
+        refs[len(refs) // 2 + n][...] = refs[n][...]
+
+
+def hold(values):
+    return pl.pallas_call(
+        hold_body,
+        in_specs=[VMEM] * len(values),
+        out_specs=[VMEM] * len(values),
+        out_shape=[jax.ShapeDtypeStruct(value.shape, value.dtype) for value in values],
+        compiler_params=PARAMS,
+        cost_estimate=SMALL,
+        name="hold",
+    )(*values)
+
+
 def four_by_four(train_grads, test_grads, fisher, chosen_ids):
     z = lax.axis_index("test")
     i = lax.axis_index("train")
@@ -232,11 +249,12 @@
     pair_in = along(test_grads, pair)
     middle_in = along(test_grads, middle)
     other_core, other_chip = to_other(train_grads, 1), to_other(train_grads, 2)
-    own, other_core = tied(test_grads, other_core)
+    mine, other_core = hold([train_grads, other_core])
+    own, mine, other_core = tied(test_grads, mine, other_core)
     own, own_sent = core_sum(*product(flags, [own], fisher), sent_as=F32, cost=MORE)
     half = own_rows // 2
     other_both = [to_other(other_chip[:half], 1), to_other(other_chip[half:], 1)]
-    grads = [train_grads, other_core, other_chip, *other_both]
+    grads = [mine, other_core, other_chip, *other_both]
     pair_in, middle_in, own, own_sent, chosen_ids, grads = tied(
         pair_in, middle_in, own, own_sent, chosen_ids, grads
     )

time: 212 us -> 210 us (level)
  Pallas kernels: 58.9 us -> 55.3 us
  local copies, waits for them, and re-layouts: 12.7 us -> 15.3 us
    ppermute x27, waiting for transfers between devices: 69.6 us -> 64.6 us  [to_other(): return lax.ppermute(value, 'train', [(k, k ^ r) for k in range(4)])]
    ppermute x13, waiting for transfers between devices: 8.49 us -> 13.2 us  [along(): return lax.ppermute(value, 'test', pairs)]
    pallas_call x3, Pallas kernels: 14.6 us -> 10.6 us  [partial_scores(): pl.pallas_call(functools.partial(scores_body, [piece[:2] for piece in gra...]
    unnamed x30 -> x38, local copies, waits for them, and re-layouts: 11.4 us -> 14 us
  transfers between devices with their start and end apart: 40 -> 40, of which waited for: 21 -> 22; matrix products, arithmetic and copies ran while one was open for 3% -> 3% of each run, Pallas kernels for 25% -> 23%
where the time goes in v17:
time: 210 us
  waiting for transfers between devices  77.8 us (37%)
  Pallas kernels  55.3 us (26%)
  starting transfers between devices  54.1 us (26%)
  local copies, waits for them, and re-layouts  15.3 us (7%)
  other arithmetic  6.06 us (3%)
    ppermute x27, waiting for transfers between devices, to_other(): return lax.ppermute(value, 'train', [(k, k ^ r) for k in range(4)])  64.6 us
    ppermute x13, starting transfers between devices, along(): return lax.ppermute(value, 'test', pairs)  35.3 us
    pallas_call x5, Pallas kernels, product(): pl.pallas_call(functools.partial(product_body, len(blocks)), in_specs=[pl...  33.7 us
    ppermute x27, starting transfers between devices, to_other(): return lax.ppermute(value, 'train', [(k, k ^ r) for k in range(4)])  18.8 us
    unnamed x38, local copies, waits for them, and re-layouts  14 us
    ppermute x13, waiting for transfers between devices, along(): return lax.ppermute(value, 'test', pairs)  13.2 us
    pallas_call x3, Pallas kernels, partial_scores(): pl.pallas_call(functools.partial(scores_body, [piece[:2] for piece in gra...  10.6 us
    pallas_call x5, Pallas kernels, fold(): pl.pallas_call(fold_body, in_specs=[pl.BlockSpec(memory_space=pltpu.SMEM)...  5.82 us
  transfers between devices with their start and end apart: 40, of which 22 were waited for; matrix products, arithmetic and copies ran while one was open for 3% of the time, Pallas kernels for 23%

profile of v17, /device:TPU:0, one launch (start us, length us, event | category | flops | bytes accessed | tf_op | source)
XLA Modules:
  0.0 209.6 jit_solution(2257985711617704357)
XLA Ops:
  1.1 2.6 %collective-permute-start.5 = (bf16[512,2048]{1,0:T(8,128)(2,1)}, bf16[512,2048]{1,0:T(8,128)(2,1)S(1)}, u32[]{:S(2)}, u32[]{:S(2)}) collective-permute-start(bf16[512,2048]{1,0:T(8,128)(2,1)} %refs_0_.1), channel_id=1, source_target_pairs={{0,8},{4,12},{8,0},{12,4},{1,9},{5,13},{9,1},{13,5},{2,10},{6,14},... | collective-permute-start | bytes 6291464 | tf_op jit(solution)/shard_map/ppermute | solution.py:220
  3.7 1.6 collective-permute-start
  5.3 2.0 collective-permute-start.1
  7.4 1.6 copy-done.8
  9.0 2.0 hold.1
  11.0 1.4 copy-done.2
  12.4 1.3 copy-done.4
  13.7 3.4 %copy-done = bf16[2048,2048]{1,0:T(8,128)(2,1)S(1)} copy-done((bf16[2048,2048]{1,0:T(8,128)(2,1)S(1)}, bf16[2048,2048]{1,0:T(8,128)(2,1)}, u32[]{:S(2)}) %copy-start) | copy-done | bytes 8388632
  17.1 5.6 %product.5 = (f32[256,2048]{1,0:T(8,128)S(1)}, bf16[128,2048]{1,0:T(8,128)(2,1)S(1)}, bf16[128,2048]{1,0:T(8,128)(2,1)S(1)}) custom-call(s32[3]{0:T(128)S(1)} %pad_add_fusion.flags, bf16[512,2048]{1,0:T(8,128)(2,1)S(1)} %copy-done.11, bf16[2048,2048]{1,0:T(8,128)(2,1)S(1)} %copy-done), custom_call_target="tpu_custom_call" | custom-call | flops 1 | bytes 1 | tf_op jit(solution)/shard_map/product/pallas_call | solution.py:80
  23.3 26.9 %collective-permute-done.5.refs_4_.refs_6_.refs_0_ = bf16[512,2048]{1,0:T(8,128)(2,1)S(1)} collective-permute-done((bf16[512,2048]{1,0:T(8,128)(2,1)}, bf16[512,2048]{1,0:T(8,128)(2,1)S(1)}, u32[]{:S(2)}, u32[]{:S(2)}) %collective-permute-start.5) | collective-permute-done | bytes 2097184 | tf_op jit(solution)/shard_map/ppermute | solution.py:220
  50.9 1.8 fold.5
  53.0 1.5 collective-permute-done.7.refs_6_.refs_8_.refs_2_
  54.5 2.1 %collective-permute-start.8 = (bf16[512,2048]{1,0:T(8,128)(2,1)}, bf16[512,2048]{1,0:T(8,128)(2,1)}, u32[]{:S(2)}, u32[]{:S(2)}) collective-permute-start(bf16[512,2048]{1,0:T(8,128)(2,1)} %collective-permute-done.refs_1_.refs_0_), channel_id=1, source_target_pairs={{1,2},{2,1},{5,6},{6,5},{9,10},{10,9},{13,14},{14,13},{17,18},{18,... | collective-permute-start | bytes 6291464 | tf_op jit(solution)/shard_map/ppermute | solution.py:217
  56.7 1.3 collective-permute-start.9
  57.9 1.8 collective-permute-start.12
  59.8 8.3 %product.6 = (f32[256,2048]{1,0:T(8,128)S(1)}, bf16[128,2048]{1,0:T(8,128)(2,1)}, bf16[128,2048]{1,0:T(8,128)(2,1)}) custom-call(s32[3]{0:T(128)S(1)} %pad_add_fusion.flags, bf16[512,2048]{1,0:T(8,128)(2,1)} %collective-permute-done.1.refs_0_, bf16[512,2048]{1,0:T(8,128)(2,1)} %collective-permute-done.refs_1_.refs_0_, bf16[2048,2048]{1,0:T(8,128)(2,1)S(1)} %bitcast.115), custom_call_target="tpu_custom_call" | custom-call | flops 1 | bytes 1 | tf_op jit(solution)/shard_map/product/pallas_call | solution.py:80
  68.1 1.3 copy-done.9
  70.1 1.6 collective-permute-done.10.refs_0_
  71.7 0.7 collective-permute-done.11.refs_1_
  72.4 1.6 copy-done.10
  74.0 1.5 fold.6
  75.6 8.0 %collective-permute-done.12.refs_3_ = f32[128,2048]{1,0:T(8,128)} collective-permute-done((f32[128,2048]{1,0:T(8,128)}, f32[128,2048]{1,0:T(8,128)}, u32[]{:S(2)}, u32[]{:S(2)}) %collective-permute-start.12) | collective-permute-done | bytes 1048608 | tf_op jit(solution)/shard_map/ppermute | solution.py:220
  83.5 1.7 collective-permute-start.15
  85.3 3.4 %copy-done.1 = bf16[2048,2048]{1,0:T(8,128)(2,1)S(1)} copy-done((bf16[2048,2048]{1,0:T(8,128)(2,1)S(1)}, bf16[2048,2048]{1,0:T(8,128)(2,1)}, u32[]{:S(2)}) %copy-start.1) | copy-done | bytes 8388632
  88.7 6.8 %product.7 = (f32[256,2048]{1,0:T(8,128)S(1)}, bf16[128,2048]{1,0:T(8,128)(2,1)S(1)}, bf16[128,2048]{1,0:T(8,128)(2,1)S(1)}) custom-call(s32[3]{0:T(128)S(1)} %pad_add_fusion.flags, bf16[512,2048]{1,0:T(8,128)(2,1)} %collective-permute-done.refs_1_.refs_0_, bf16[2048,2048]{1,0:T(8,128)(2,1)S(1)} %copy-done.1), custom_call_target="tpu_custom_call" | custom-call | flops 1 | bytes 1 | tf_op jit(solution)/shard_map/product/pallas_call | solution.py:80
  96.1 1.7 convert_add_fusion.1
  97.8 5.5 %collective-permute-start.16 = (s32[512,16]{0,1:T(8,128)S(1)}, s32[512,16]{0,1:T(8,128)S(1)}, u32[]{:S(2)}, u32[]{:S(2)}) collective-permute-start(s32[512,16]{0,1:T(8,128)S(1)} %copy-done.14), channel_id=1, source_target_pairs={{0,3},{3,0},{4,7},{7,4},{8,11},{11,8},{12,15},{15,12},{16,19},{19,... | collective-permute-start | bytes 98312 | tf_op jit(solution)/shard_map/ppermute | solution.py:217
  103.4 2.4 %scores.3 = bf16[4,512,128]{2,1,0:T(8,128)(2,1)S(1)} custom-call(f32[128,2048]{1,0:T(8,128)S(1)} %get-tuple-element.111.refs_0_, bf16[128,2048]{1,0:T(8,128)(2,1)S(1)} %collective-permute-done.15.refs_1_, bf16[512,2048]{1,0:T(8,128)(2,1)S(1)} %copy-done.3, bf16[512,2048]{1,0:T(8,128)(2,1)S(1)} %copy-done.5, ...), custom_call_target="tpu_custom_call" | custom-call | flops 2000000000 | bytes 1048576 | tf_op jit(solution)/shard_map/scores/pallas_call | solution.py:144
  105.8 0.8 fold.7
  106.6 1.3 collective-permute-done.9.refs_1_
  107.9 1.3 collective-permute-start.17
  109.2 7.3 %product.8 = (f32[256,2048]{1,0:T(8,128)S(1)}, bf16[128,2048]{1,0:T(8,128)(2,1)S(1)}, bf16[128,2048]{1,0:T(8,128)(2,1)S(1)}) custom-call(s32[3]{0:T(128)S(1)} %pad_add_fusion.flags, bf16[512,2048]{1,0:T(8,128)(2,1)} %collective-permute-done.8.refs_0_, bf16[512,2048]{1,0:T(8,128)(2,1)} %collective-permute-done.9.refs_1_, bf16[2048,2048]{1,0:T(8,128)(2,1)S(1)} %bitcast.117), custom_call_target="tpu_custom_call" | custom-call | flops 1 | bytes 1 | tf_op jit(solution)/shard_map/product/pallas_call | solution.py:80
  117.2 1.4 collective-permute-done.19.refs_0_
  119.3 0.8 fold.8
  120.1 1.6 collective-permute-start.21
  121.7 4.7 %collective-permute-start.22 = (bf16[4,512,128]{2,1,0:T(8,128)(2,1)S(1)}, bf16[4,512,128]{2,1,0:T(8,128)(2,1)S(1)}, u32[]{:S(2)}, u32[]{:S(2)}) collective-permute-start(bf16[4,512,128]{2,1,0:T(8,128)(2,1)S(1)} %scores.3), channel_id=1, source_target_pairs={{0,1},{3,2},{4,5},{7,6},{8,9},{11,10},{12,13},{15,14},{16,17},{19,... | collective-permute-start | bytes 1572872 | tf_op jit(solution)/shard_map/ppermute | solution.py:217
  126.4 0.9 collective-permute-start.23
  127.9 7.1 %collective-permute-done.21.refs_1_ = bf16[128,2048]{1,0:T(8,128)(2,1)S(1)} collective-permute-done((bf16[128,2048]{1,0:T(8,128)(2,1)S(1)}, bf16[128,2048]{1,0:T(8,128)(2,1)S(1)}, u32[]{:S(2)}, u32[]{:S(2)}) %collective-permute-start.21) | collective-permute-done | bytes 524320 | tf_op jit(solution)/shard_map/ppermute | solution.py:220
  135.0 2.6 %collective-permute-done.22 = bf16[4,512,128]{2,1,0:T(8,128)(2,1)S(1)} collective-permute-done((bf16[4,512,128]{2,1,0:T(8,128)(2,1)S(1)}, bf16[4,512,128]{2,1,0:T(8,128)(2,1)S(1)}, u32[]{:S(2)}, u32[]{:S(2)}) %collective-permute-start.22) | collective-permute-done | bytes 524320 | tf_op jit(solution)/shard_map/ppermute | solution.py:217
  137.6 2.4 %scores.5 = bf16[4,512,128]{2,1,0:T(8,128)(2,1)S(1)} custom-call(f32[128,2048]{1,0:T(8,128)S(1)} %get-tuple-element.141.refs_0_, bf16[128,2048]{1,0:T(8,128)(2,1)S(1)} %collective-permute-done.21.refs_1_, bf16[512,2048]{1,0:T(8,128)(2,1)S(1)} %copy-done.3, bf16[512,2048]{1,0:T(8,128)(2,1)S(1)} %copy-done.5, ...), custom_call_target="tpu_custom_call" | custom-call | flops 1 | bytes 1 | tf_op jit(solution)/shard_map/scores/pallas_call | solution.py:144
  140.7 1.7 convert_add_fusion.counts
  142.3 3.1 %collective-permute-done.18.refs_1_ = bf16[128,2048]{1,0:T(8,128)(2,1)S(1)} collective-permute-done((bf16[128,2048]{1,0:T(8,128)(2,1)S(1)}, bf16[128,2048]{1,0:T(8,128)(2,1)S(1)}, u32[]{:S(2)}, u32[]{:S(2)}) %collective-permute-start.18) | collective-permute-done | bytes 524320 | tf_op jit(solution)/shard_map/ppermute | solution.py:220
  145.4 5.8 %scores.4 = (f32[4,512,128]{2,1,0:T(8,128)S(1)}, f32[4,512,128]{2,1,0:T(8,128)S(1)}) custom-call(f32[128,2048]{1,0:T(8,128)S(1)} %get-tuple-element.120.refs_0_, bf16[128,2048]{1,0:T(8,128)(2,1)S(1)} %collective-permute-done.18.refs_1_, f32[128,2048]{1,0:T(8,128)S(1)} %copy-done.13, f32[128,2048]{1,0:T(8,128)} %collective-permute-done.12.refs_3_, ...), custom_call_target="tpu_custom_call" | custom-call | flops 1 | bytes 1 | tf_op jit(solution)/shard_map/scores/pallas_call | solution.py:144
  151.2 5.6 %collective-permute-done.17.refs_0_ = bf16[512,2048]{1,0:T(8,128)(2,1)S(1)} collective-permute-done((bf16[512,2048]{1,0:T(8,128)(2,1)}, bf16[512,2048]{1,0:T(8,128)(2,1)S(1)}, u32[]{:S(2)}, u32[]{:S(2)}) %collective-permute-start.17) | collective-permute-done | bytes 2097184 | tf_op jit(solution)/shard_map/ppermute | solution.py:217
  156.8 5.6 %product.9 = (f32[256,2048]{1,0:T(8,128)S(1)}, bf16[128,2048]{1,0:T(8,128)(2,1)S(1)}, bf16[128,2048]{1,0:T(8,128)(2,1)S(1)}) custom-call(s32[3]{0:T(128)S(1)} %pad_add_fusion.flags, bf16[512,2048]{1,0:T(8,128)(2,1)S(1)} %collective-permute-done.17.refs_0_, bf16[2048,2048]{1,0:T(8,128)(2,1)S(1)} %bitcast.117), custom_call_target="tpu_custom_call" | custom-call | flops 1 | bytes 1 | tf_op jit(solution)/shard_map/product/pallas_call | solution.py:80
  163.0 1.4 collective-permute-done.25.refs_0_
  165.1 0.8 fold.9
  166.0 1.6 collective-permute-start.27
  167.7 1.3 collective-permute-start.29
  169.0 6.3 %collective-permute-start.28 = (bf16[4,512,128]{2,1,0:T(8,128)(2,1)S(1)}, bf16[4,512,128]{2,1,0:T(8,128)(2,1)S(1)}, u32[]{:S(2)}, u32[]{:S(2)}) collective-permute-start(bf16[4,512,128]{2,1,0:T(8,128)(2,1)S(1)} %scores.5), channel_id=1, source_target_pairs={{0,2},{3,1},{4,6},{7,5},{8,10},{11,9},{12,14},{15,13},{16,18},{19,... | collective-permute-start | bytes 1572872 | tf_op jit(solution)/shard_map/ppermute | solution.py:217
  175.3 4.7 %collective-permute-done.27.got = bf16[128,2048]{1,0:T(8,128)(2,1)S(1)} collective-permute-done((bf16[128,2048]{1,0:T(8,128)(2,1)S(1)}, bf16[128,2048]{1,0:T(8,128)(2,1)S(1)}, u32[]{:S(2)}, u32[]{:S(2)}) %collective-permute-start.27) | collective-permute-done | bytes 524320 | tf_op jit(solution)/shard_map/ppermute | solution.py:220
  180.0 1.3 last_scores.2
  181.3 1.9 last_scores.3
  183.3 2.9 %collective-permute-done.28 = bf16[4,512,128]{2,1,0:T(8,128)(2,1)S(1)} collective-permute-done((bf16[4,512,128]{2,1,0:T(8,128)(2,1)S(1)}, bf16[4,512,128]{2,1,0:T(8,128)(2,1)S(1)}, u32[]{:S(2)}, u32[]{:S(2)}) %collective-permute-start.28) | collective-permute-done | bytes 524320 | tf_op jit(solution)/shard_map/ppermute | solution.py:217
  186.2 2.5 %collective-permute-start.34 = (bf16[2,512,128]{2,1,0:T(8,128)(2,1)S(1)}, bf16[2,512,128]{2,1,0:T(8,128)(2,1)}, u32[]{:S(2)}, u32[]{:S(2)}) collective-permute-start(bf16[2,512,128]{2,1,0:T(8,128)(2,1)S(1)} %get-tuple-element.169), channel_id=1, source_target_pairs={{0,3},{3,0},{4,7},{7,4},{8,11},{11,8},{12,15},{15,12},{16,19},{19,... | collective-permute-start | bytes 786440 | tf_op jit(solution)/shard_map/ppermute | solution.py:217
  189.3 1.2 collective-permute-start.30
  190.5 1.0 collective-permute-start.32
  191.5 5.1 %collective-permute-start.33 = (bf16[2,528,128]{2,1,0:T(8,128)(2,1)S(1)}, bf16[2,528,128]{2,1,0:T(8,128)(2,1)S(1)}, u32[]{:S(2)}, u32[]{:S(2)}) collective-permute-start(bf16[2,528,128]{2,1,0:T(8,128)(2,1)S(1)} %get-tuple-element.168), channel_id=1, source_target_pairs={{0,3},{3,0},{4,7},{7,4},{8,11},{11,8},{12,15},{15,12},{16,19},{19,... | collective-permute-start | bytes 811016 | tf_op jit(solution)/shard_map/ppermute | solution.py:217
  196.8 1.0 slice_bitcast_fusion.5
  198.7 4.3 %collective-permute-done.32 = f32[520,128]{1,0:T(8,128)S(1)} collective-permute-done((f32[520,128]{1,0:T(8,128)S(1)}, f32[520,128]{1,0:T(8,128)S(1)}, u32[]{:S(2)}, u32[]{:S(2)}) %collective-permute-start.32) | collective-permute-done | bytes 266272 | tf_op jit(solution)/shard_map/ppermute | solution.py:220
  203.6 1.1 collective-permute-start.38
  204.7 1.0 collective-permute-start.39
  205.9 1.9 collective-permute-done.38
  208.4 1.1 slice_add_fusion
  (97 shorter events, 10.7 us)
Async XLA Ops:
  0.6 6.8 %collective-permute-start.2 = (bf16[512,2048]{1,0:T(8,128)(2,1)}, bf16[512,2048]{1,0:T(8,128)(2,1)}, u32[]{:S(2)}, u32[]{:S(2)}) collective-permute-start(bf16[512,2048]{1,0:T(8,128)(2,1)} %refs_0_.1), channel_id=1, source_target_pairs={{0,4},{4,0},{8,12},{12,8},{1,5},{5,1},{9,13},{13,9},{2,6},{6,2},{1... | collective-permute-start | bytes 6291464 | tf_op jit(solution)/shard_map/ppermute | solution.py:220
  1.1 49.0 %collective-permute-start.5 = (bf16[512,2048]{1,0:T(8,128)(2,1)}, bf16[512,2048]{1,0:T(8,128)(2,1)S(1)}, u32[]{:S(2)}, u32[]{:S(2)}) collective-permute-start(bf16[512,2048]{1,0:T(8,128)(2,1)} %refs_0_.1), channel_id=1, source_target_pairs={{0,8},{4,12},{8,0},{12,4},{1,9},{5,13},{9,1},{13,5},{2,10},{6,14},... | collective-permute-start | bytes 6291464 | tf_op jit(solution)/shard_map/ppermute | solution.py:220
  3.7 49.0 %collective-permute-start = (bf16[512,2048]{1,0:T(8,128)(2,1)}, bf16[512,2048]{1,0:T(8,128)(2,1)}, u32[]{:S(2)}, u32[]{:S(2)}) collective-permute-start(bf16[512,2048]{1,0:T(8,128)(2,1)} %refs_0_.2), channel_id=1, source_target_pairs={{0,1},{1,0},{2,3},{3,2},{4,5},{5,4},{6,7},{7,6},{8,9},{9,8},{10,11... | collective-permute-start | bytes 6291464 | tf_op jit(solution)/shard_map/ppermute | solution.py:217
  5.3 47.4 %collective-permute-start.1 = (bf16[512,2048]{1,0:T(8,128)(2,1)}, bf16[512,2048]{1,0:T(8,128)(2,1)}, u32[]{:S(2)}, u32[]{:S(2)}) collective-permute-start(bf16[512,2048]{1,0:T(8,128)(2,1)} %refs_0_.2), channel_id=1, source_target_pairs={{1,2},{2,1},{5,6},{6,5},{9,10},{10,9},{13,14},{14,13},{17,18},{18,... | collective-permute-start | bytes 6291464 | tf_op jit(solution)/shard_map/ppermute | solution.py:217
  7.4 1.6 copy-start.8
  9.0 4.7 %copy-start.11 = (bf16[512,2048]{1,0:T(8,128)(2,1)S(1)}, bf16[512,2048]{1,0:T(8,128)(2,1)}, u32[]{:S(2)}) copy-start(bf16[512,2048]{1,0:T(8,128)(2,1)} %refs_0_.2) | copy-start | bytes 6291460
  11.0 1.4 copy-start.2
  12.4 1.3 copy-start.4
  13.7 3.4 %copy-start = (bf16[2048,2048]{1,0:T(8,128)(2,1)S(1)}, bf16[2048,2048]{1,0:T(8,128)(2,1)}, u32[]{:S(2)}) copy-start(bf16[2048,2048]{1,0:T(8,128)(2,1)} %refs_1_.5) | copy-start | bytes 25165828
  22.7 27.7 %collective-permute-start.3 = (bf16[128,2048]{1,0:T(8,128)(2,1)S(1)}, bf16[128,2048]{1,0:T(8,128)(2,1)S(1)}, u32[]{:S(2)}, u32[]{:S(2)}) collective-permute-start(bf16[128,2048]{1,0:T(8,128)(2,1)S(1)} %get-tuple-element.90), channel_id=1, source_target_pairs={{0,4},{4,0},{8,12},{12,8},{1,5},{5,1},{9,13},{13,9},{2,6},{6,2},{1... | collective-permute-start | bytes 1572872 | tf_op jit(solution)/shard_map/ppermute | solution.py:220
  22.8 28.1 %collective-permute-start.4 = (bf16[128,2048]{1,0:T(8,128)(2,1)S(1)}, bf16[128,2048]{1,0:T(8,128)(2,1)S(1)}, u32[]{:S(2)}, u32[]{:S(2)}) collective-permute-start(bf16[128,2048]{1,0:T(8,128)(2,1)S(1)} %get-tuple-element.91), channel_id=1, source_target_pairs={{0,4},{4,0},{8,12},{12,8},{1,5},{5,1},{9,13},{13,9},{2,6},{6,2},{1... | collective-permute-start | bytes 1572872 | tf_op jit(solution)/shard_map/ppermute | solution.py:220
  50.3 2.7 %collective-permute-start.6 = (bf16[256,2048]{1,0:T(8,128)(2,1)S(1)}, bf16[256,2048]{1,0:T(8,128)(2,1)S(1)}, u32[]{:S(2)}, u32[]{:S(2)}) collective-permute-start(bf16[256,2048]{1,0:T(8,128)(2,1)S(1)} %get-tuple-element.173), channel_id=1, source_target_pairs={{0,4},{4,0},{8,12},{12,8},{1,5},{5,1},{9,13},{13,9},{2,6},{6,2},{1... | collective-permute-start | bytes 3145736 | tf_op jit(solution)/shard_map/ppermute | solution.py:220
  50.4 4.1 %collective-permute-start.7 = (bf16[256,2048]{1,0:T(8,128)(2,1)S(1)}, bf16[256,2048]{1,0:T(8,128)(2,1)S(1)}, u32[]{:S(2)}, u32[]{:S(2)}) collective-permute-start(bf16[256,2048]{1,0:T(8,128)(2,1)S(1)} %get-tuple-element.172), channel_id=1, source_target_pairs={{0,4},{4,0},{8,12},{12,8},{1,5},{5,1},{9,13},{13,9},{2,6},{6,2},{1... | collective-permute-start | bytes 3145736 | tf_op jit(solution)/shard_map/ppermute | solution.py:220
  50.9 8.9 %slice-start = ((s8[8388608]{0:T(1024)(128)(4,1)}), s8[4194304]{0:T(1024)(128)(4,1)S(1)}, s32[]{:S(2)}) async-start(s8[8388608]{0:T(1024)(128)(4,1)} %bitcast.114), calls=%async_computation | async-start | bytes 8388608
  50.9 8.9 %slice-start.1 = ((s8[8388608]{0:T(1024)(128)(4,1)}), s8[4194304]{0:T(1024)(128)(4,1)S(1)}, s32[]{:S(2)}) async-start(s8[8388608]{0:T(1024)(128)(4,1)} %bitcast.114), calls=%async_computation.1 | async-start | bytes 8388608
  52.7 15.4 %copy-start.12 = (f32[128,2048]{1,0:T(8,128)}, f32[128,2048]{1,0:T(8,128)S(1)}, u32[]{:S(2)}) copy-start(f32[128,2048]{1,0:T(8,128)S(1)} %get-tuple-element.122.refs_2_) | copy-start | bytes 3145732
  54.5 13.6 %copy-start.6 = (bf16[256,2048]{1,0:T(8,128)(2,1)}, bf16[256,2048]{1,0:T(8,128)(2,1)S(1)}, u32[]{:S(2)}) copy-start(bf16[256,2048]{1,0:T(8,128)(2,1)S(1)} %collective-permute-done.7.refs_6_.refs_8_.refs_2_) | copy-start | bytes 3145732
  54.5 15.6 %copy-start.14 = (s32[512,16]{0,1:T(8,128)S(1)}, s32[512,16]{0,1:T(8,128)}, u32[]{:S(2)}) copy-start(s32[512,16]{0,1:T(8,128)} %param.7) | copy-start | bytes 98308
  54.5 52.1 %collective-permute-start.8 = (bf16[512,2048]{1,0:T(8,128)(2,1)}, bf16[512,2048]{1,0:T(8,128)(2,1)}, u32[]{:S(2)}, u32[]{:S(2)}) collective-permute-start(bf16[512,2048]{1,0:T(8,128)(2,1)} %collective-permute-done.refs_1_.refs_0_), channel_id=1, source_target_pairs={{1,2},{2,1},{5,6},{6,5},{9,10},{10,9},{13,14},{14,13},{17,18},{18,... | collective-permute-start | bytes 6291464 | tf_op jit(solution)/shard_map/ppermute | solution.py:217
  56.7 51.3 %collective-permute-start.9 = (bf16[512,2048]{1,0:T(8,128)(2,1)}, bf16[512,2048]{1,0:T(8,128)(2,1)}, u32[]{:S(2)}, u32[]{:S(2)}) collective-permute-start(bf16[512,2048]{1,0:T(8,128)(2,1)} %collective-permute-done.1.refs_0_), channel_id=1, source_target_pairs={{1,0},{2,3},{5,4},{6,7},{9,8},{10,11},{13,12},{14,15},{17,16},{18,... | collective-permute-start | bytes 6291464 | tf_op jit(solution)/shard_map/ppermute | solution.py:217
  57.9 25.6 %collective-permute-start.12 = (f32[128,2048]{1,0:T(8,128)}, f32[128,2048]{1,0:T(8,128)}, u32[]{:S(2)}, u32[]{:S(2)}) collective-permute-start(f32[128,2048]{1,0:T(8,128)} %get-tuple-element.102), channel_id=1, source_target_pairs={{0,8},{4,12},{8,0},{12,4},{1,9},{5,13},{9,1},{13,5},{2,10},{6,14},... | collective-permute-start | bytes 3145736 | tf_op jit(solution)/shard_map/ppermute | solution.py:220
  68.1 1.3 copy-start.9
  69.4 2.3 %collective-permute-start.10 = (bf16[128,2048]{1,0:T(8,128)(2,1)}, bf16[128,2048]{1,0:T(8,128)(2,1)}, u32[]{:S(2)}, u32[]{:S(2)}) collective-permute-start(bf16[128,2048]{1,0:T(8,128)(2,1)} %get-tuple-element.99), channel_id=1, source_target_pairs={{0,4},{4,0},{8,12},{12,8},{1,5},{5,1},{9,13},{13,9},{2,6},{6,2},{1... | collective-permute-start | bytes 1572872 | tf_op jit(solution)/shard_map/ppermute | solution.py:220
  69.4 3.0 %collective-permute-start.11 = (bf16[128,2048]{1,0:T(8,128)(2,1)}, bf16[128,2048]{1,0:T(8,128)(2,1)}, u32[]{:S(2)}, u32[]{:S(2)}) collective-permute-start(bf16[128,2048]{1,0:T(8,128)(2,1)} %get-tuple-element.100), channel_id=1, source_target_pairs={{0,4},{4,0},{8,12},{12,8},{1,5},{5,1},{9,13},{13,9},{2,6},{6,2},{1... | collective-permute-start | bytes 1572872 | tf_op jit(solution)/shard_map/ppermute | solution.py:220
  72.4 1.6 copy-start.10
  83.5 14.2 %collective-permute-start.15 = (bf16[128,2048]{1,0:T(8,128)(2,1)S(1)}, bf16[128,2048]{1,0:T(8,128)(2,1)S(1)}, u32[]{:S(2)}, u32[]{:S(2)}) collective-permute-start(bf16[128,2048]{1,0:T(8,128)(2,1)S(1)} %get-tuple-element.112), channel_id=1, source_target_pairs={{0,8},{4,12},{8,0},{12,4},{1,9},{5,13},{9,1},{13,5},{2,10},{6,14},... | collective-permute-start | bytes 1572872 | tf_op jit(solution)/shard_map/ppermute | solution.py:220
  85.3 3.4 %copy-start.1 = (bf16[2048,2048]{1,0:T(8,128)(2,1)S(1)}, bf16[2048,2048]{1,0:T(8,128)(2,1)}, u32[]{:S(2)}) copy-start(bf16[2048,2048]{1,0:T(8,128)(2,1)} %refs_1_.5) | copy-start | bytes 25165828
  88.7 14.6 %copy-start.3 = (bf16[512,2048]{1,0:T(8,128)(2,1)S(1)}, bf16[512,2048]{1,0:T(8,128)(2,1)}, u32[]{:S(2)}) copy-start(bf16[512,2048]{1,0:T(8,128)(2,1)} %copy-done.2) | copy-start | bytes 6291460
  88.7 14.7 %copy-start.5 = (bf16[512,2048]{1,0:T(8,128)(2,1)S(1)}, bf16[512,2048]{1,0:T(8,128)(2,1)}, u32[]{:S(2)}) copy-start(bf16[512,2048]{1,0:T(8,128)(2,1)} %copy-done.4) | copy-start | bytes 6291460
  88.7 14.7 %copy-start.7 = (bf16[256,2048]{1,0:T(8,128)(2,1)S(1)}, bf16[256,2048]{1,0:T(8,128)(2,1)}, u32[]{:S(2)}) copy-start(bf16[256,2048]{1,0:T(8,128)(2,1)} %copy-done.6) | copy-start | bytes 3145732
  88.7 20.5 %slice-start.2 = ((s8[8388608]{0:T(1024)(128)(4,1)}), s8[4194304]{0:T(1024)(128)(4,1)S(1)}, s32[]{:S(2)}) async-start(s8[8388608]{0:T(1024)(128)(4,1)} %bitcast.116), calls=%async_computation.2 | async-start | bytes 8388608
  95.5 10.2 %collective-permute-start.13 = (bf16[128,2048]{1,0:T(8,128)(2,1)S(1)}, bf16[128,2048]{1,0:T(8,128)(2,1)S(1)}, u32[]{:S(2)}, u32[]{:S(2)}) collective-permute-start(bf16[128,2048]{1,0:T(8,128)(2,1)S(1)} %get-tuple-element.105), channel_id=1, source_target_pairs={{0,4},{4,0},{8,12},{12,8},{1,5},{5,1},{9,13},{13,9},{2,6},{6,2},{1... | collective-permute-start | bytes 1572872 | tf_op jit(solution)/shard_map/ppermute | solution.py:220
  95.6 10.1 %collective-permute-start.14 = (bf16[128,2048]{1,0:T(8,128)(2,1)S(1)}, bf16[128,2048]{1,0:T(8,128)(2,1)S(1)}, u32[]{:S(2)}, u32[]{:S(2)}) collective-permute-start(bf16[128,2048]{1,0:T(8,128)(2,1)S(1)} %get-tuple-element.106), channel_id=1, source_target_pairs={{0,4},{4,0},{8,12},{12,8},{1,5},{5,1},{9,13},{13,9},{2,6},{6,2},{1... | collective-permute-start | bytes 1572872 | tf_op jit(solution)/shard_map/ppermute | solution.py:220
  97.8 8.8 %collective-permute-start.16 = (s32[512,16]{0,1:T(8,128)S(1)}, s32[512,16]{0,1:T(8,128)S(1)}, u32[]{:S(2)}, u32[]{:S(2)}) collective-permute-start(s32[512,16]{0,1:T(8,128)S(1)} %copy-done.14), channel_id=1, source_target_pairs={{0,3},{3,0},{4,7},{7,4},{8,11},{11,8},{12,15},{15,12},{16,19},{19,... | collective-permute-start | bytes 98312 | tf_op jit(solution)/shard_map/ppermute | solution.py:217
  103.3 5.9 %slice-start.3 = ((s8[8388608]{0:T(1024)(128)(4,1)}), s8[4194304]{0:T(1024)(128)(4,1)S(1)}, s32[]{:S(2)}) async-start(s8[8388608]{0:T(1024)(128)(4,1)} %bitcast.116), calls=%async_computation.3 | async-start | bytes 8388608
  107.9 48.9 %collective-permute-start.17 = (bf16[512,2048]{1,0:T(8,128)(2,1)}, bf16[512,2048]{1,0:T(8,128)(2,1)S(1)}, u32[]{:S(2)}, u32[]{:S(2)}) collective-permute-start(bf16[512,2048]{1,0:T(8,128)(2,1)} %collective-permute-done.8.refs_0_), channel_id=1, source_target_pairs={{1,0},{2,3},{5,4},{6,7},{9,8},{10,11},{13,12},{14,15},{17,16},{18,... | collective-permute-start | bytes 6291464 | tf_op jit(solution)/shard_map/ppermute | solution.py:217
  116.6 2.0 collective-permute-start.19
  116.7 2.6 %collective-permute-start.20 = (bf16[128,2048]{1,0:T(8,128)(2,1)S(1)}, bf16[128,2048]{1,0:T(8,128)(2,1)S(1)}, u32[]{:S(2)}, u32[]{:S(2)}) collective-permute-start(bf16[128,2048]{1,0:T(8,128)(2,1)S(1)} %get-tuple-element.133), channel_id=1, source_target_pairs={{0,4},{4,0},{8,12},{12,8},{1,5},{5,1},{9,13},{13,9},{2,6},{6,2},{1... | collective-permute-start | bytes 1572872 | tf_op jit(solution)/shard_map/ppermute | solution.py:220
  120.1 14.8 %collective-permute-start.21 = (bf16[128,2048]{1,0:T(8,128)(2,1)S(1)}, bf16[128,2048]{1,0:T(8,128)(2,1)S(1)}, u32[]{:S(2)}, u32[]{:S(2)}) collective-permute-start(bf16[128,2048]{1,0:T(8,128)(2,1)S(1)} %get-tuple-element.137), channel_id=1, source_target_pairs={{0,8},{4,12},{8,0},{12,4},{1,9},{5,13},{9,1},{13,5},{2,10},{6,14},... | collective-permute-start | bytes 1572872 | tf_op jit(solution)/shard_map/ppermute | solution.py:220
  121.7 15.9 %collective-permute-start.22 = (bf16[4,512,128]{2,1,0:T(8,128)(2,1)S(1)}, bf16[4,512,128]{2,1,0:T(8,128)(2,1)S(1)}, u32[]{:S(2)}, u32[]{:S(2)}) collective-permute-start(bf16[4,512,128]{2,1,0:T(8,128)(2,1)S(1)} %scores.3), channel_id=1, source_target_pairs={{0,1},{3,2},{4,5},{7,6},{8,9},{11,10},{12,13},{15,14},{16,17},{19,... | collective-permute-start | bytes 1572872 | tf_op jit(solution)/shard_map/ppermute | solution.py:217
  126.4 11.2 %collective-permute-start.23 = (bf16[4,512,128]{2,1,0:T(8,128)(2,1)S(1)}, bf16[4,512,128]{2,1,0:T(8,128)(2,1)S(1)}, u32[]{:S(2)}, u32[]{:S(2)}) collective-permute-start(bf16[4,512,128]{2,1,0:T(8,128)(2,1)S(1)} %scores.3), channel_id=1, source_target_pairs={{1,2},{2,1},{5,6},{6,5},{9,10},{10,9},{13,14},{14,13},{17,18},{18,... | collective-permute-start | bytes 1572872 | tf_op jit(solution)/shard_map/ppermute | solution.py:217
  127.3 18.1 %collective-permute-start.18 = (bf16[128,2048]{1,0:T(8,128)(2,1)S(1)}, bf16[128,2048]{1,0:T(8,128)(2,1)S(1)}, u32[]{:S(2)}, u32[]{:S(2)}) collective-permute-start(bf16[128,2048]{1,0:T(8,128)(2,1)S(1)} %get-tuple-element.121), channel_id=1, source_target_pairs={{0,8},{4,12},{8,0},{12,4},{1,9},{5,13},{9,1},{13,5},{2,10},{6,14},... | collective-permute-start | bytes 1572872 | tf_op jit(solution)/shard_map/ppermute | solution.py:220
  127.9 17.5 %copy-start.13 = (f32[128,2048]{1,0:T(8,128)S(1)}, f32[128,2048]{1,0:T(8,128)}, u32[]{:S(2)}) copy-start(f32[128,2048]{1,0:T(8,128)} %copy-done.12) | copy-start | bytes 3145732
  140.0 11.3 %collective-permute-start.24 = (bf16[4,512,128]{2,1,0:T(8,128)(2,1)S(1)}, bf16[4,512,128]{2,1,0:T(8,128)(2,1)S(1)}, u32[]{:S(2)}, u32[]{:S(2)}) collective-permute-start(bf16[4,512,128]{2,1,0:T(8,128)(2,1)S(1)} %scores.5), channel_id=1, source_target_pairs={{1,2},{2,1},{5,6},{6,5},{9,10},{10,9},{13,14},{14,13},{17,18},{18,... | collective-permute-start | bytes 1572872 | tf_op jit(solution)/shard_map/ppermute | solution.py:217
  162.4 2.0 collective-permute-start.25
  162.5 2.6 %collective-permute-start.26 = (bf16[128,2048]{1,0:T(8,128)(2,1)S(1)}, bf16[128,2048]{1,0:T(8,128)(2,1)S(1)}, u32[]{:S(2)}, u32[]{:S(2)}) collective-permute-start(bf16[128,2048]{1,0:T(8,128)(2,1)S(1)} %get-tuple-element.151), channel_id=1, source_target_pairs={{0,4},{4,0},{8,12},{12,8},{1,5},{5,1},{9,13},{13,9},{2,6},{6,2},{1... | collective-permute-start | bytes 1572872 | tf_op jit(solution)/shard_map/ppermute | solution.py:220
  166.0 14.0 %collective-permute-start.27 = (bf16[128,2048]{1,0:T(8,128)(2,1)S(1)}, bf16[128,2048]{1,0:T(8,128)(2,1)S(1)}, u32[]{:S(2)}, u32[]{:S(2)}) collective-permute-start(bf16[128,2048]{1,0:T(8,128)(2,1)S(1)} %get-tuple-element.153), channel_id=1, source_target_pairs={{0,8},{4,12},{8,0},{12,4},{1,9},{5,13},{9,1},{13,5},{2,10},{6,14},... | collective-permute-start | bytes 1572872 | tf_op jit(solution)/shard_map/ppermute | solution.py:220
  167.7 15.6 %collective-permute-start.29 = (bf16[4,512,128]{2,1,0:T(8,128)(2,1)S(1)}, bf16[4,512,128]{2,1,0:T(8,128)(2,1)S(1)}, u32[]{:S(2)}, u32[]{:S(2)}) collective-permute-start(bf16[4,512,128]{2,1,0:T(8,128)(2,1)S(1)} %add_convert_fusion), channel_id=1, source_target_pairs={{1,0},{2,3},{5,4},{6,7},{9,8},{10,11},{13,12},{14,15},{17,16},{18,... | collective-permute-start | bytes 1572872 | tf_op jit(solution)/shard_map/ppermute | solution.py:217
  169.0 17.2 %collective-permute-start.28 = (bf16[4,512,128]{2,1,0:T(8,128)(2,1)S(1)}, bf16[4,512,128]{2,1,0:T(8,128)(2,1)S(1)}, u32[]{:S(2)}, u32[]{:S(2)}) collective-permute-start(bf16[4,512,128]{2,1,0:T(8,128)(2,1)S(1)} %scores.5), channel_id=1, source_target_pairs={{0,2},{3,1},{4,6},{7,5},{8,10},{11,9},{12,14},{15,13},{16,18},{19,... | collective-permute-start | bytes 1572872 | tf_op jit(solution)/shard_map/ppermute | solution.py:217
  186.2 10.7 %collective-permute-start.34 = (bf16[2,512,128]{2,1,0:T(8,128)(2,1)S(1)}, bf16[2,512,128]{2,1,0:T(8,128)(2,1)}, u32[]{:S(2)}, u32[]{:S(2)}) collective-permute-start(bf16[2,512,128]{2,1,0:T(8,128)(2,1)S(1)} %get-tuple-element.169), channel_id=1, source_target_pairs={{0,3},{3,0},{4,7},{7,4},{8,11},{11,8},{12,15},{15,12},{16,19},{19,... | collective-permute-start | bytes 786440 | tf_op jit(solution)/shard_map/ppermute | solution.py:217
  189.3 9.4 %collective-permute-start.30 = (f32[520,128]{1,0:T(8,128)S(1)}, f32[520,128]{1,0:T(8,128)S(1)}, u32[]{:S(2)}, u32[]{:S(2)}) collective-permute-start(f32[520,128]{1,0:T(8,128)S(1)} %get-tuple-element.224), channel_id=1, source_target_pairs={{0,8},{4,12},{8,0},{12,4},{1,9},{5,13},{9,1},{13,5},{2,10},{6,14},... | collective-permute-start | bytes 798728 | tf_op jit(solution)/shard_map/ppermute | solution.py:220
  190.5 8.2 %collective-permute-start.31 = (f32[520,128]{1,0:T(8,128)S(1)}, f32[520,128]{1,0:T(8,128)S(1)}, u32[]{:S(2)}, u32[]{:S(2)}) collective-permute-start(f32[520,128]{1,0:T(8,128)S(1)} %get-tuple-element.225), channel_id=1, source_target_pairs={{0,4},{4,0},{8,12},{12,8},{1,5},{5,1},{9,13},{13,9},{2,6},{6,2},{1... | collective-permute-start | bytes 798728 | tf_op jit(solution)/shard_map/ppermute | solution.py:220
  190.5 12.6 %collective-permute-start.32 = (f32[520,128]{1,0:T(8,128)S(1)}, f32[520,128]{1,0:T(8,128)S(1)}, u32[]{:S(2)}, u32[]{:S(2)}) collective-permute-start(f32[520,128]{1,0:T(8,128)S(1)} %get-tuple-element.226), channel_id=1, source_target_pairs={{0,12},{4,8},{8,4},{12,0},{1,13},{5,9},{9,5},{13,1},{2,14},{6,10},... | collective-permute-start | bytes 798728 | tf_op jit(solution)/shard_map/ppermute | solution.py:220
  191.5 12.1 %collective-permute-start.33 = (bf16[2,528,128]{2,1,0:T(8,128)(2,1)S(1)}, bf16[2,528,128]{2,1,0:T(8,128)(2,1)S(1)}, u32[]{:S(2)}, u32[]{:S(2)}) collective-permute-start(bf16[2,528,128]{2,1,0:T(8,128)(2,1)S(1)} %get-tuple-element.168), channel_id=1, source_target_pairs={{0,3},{3,0},{4,7},{7,4},{8,11},{11,8},{12,15},{15,12},{16,19},{19,... | collective-permute-start | bytes 811016 | tf_op jit(solution)/shard_map/ppermute | solution.py:217
  197.8 10.5 %collective-permute-start.35 = (bf16[512,128]{1,0:T(8,128)(2,1)S(1)}, bf16[512,128]{1,0:T(8,128)(2,1)S(1)}, u32[]{:S(2)}, u32[]{:S(2)}) collective-permute-start(bf16[512,128]{1,0:T(8,128)(2,1)S(1)} %get-tuple-element.191), channel_id=1, source_target_pairs={{0,8},{4,12},{8,0},{12,4},{1,9},{5,13},{9,1},{13,5},{2,10},{6,14},... | collective-permute-start | bytes 393224 | tf_op jit(solution)/shard_map/ppermute | solution.py:220
  198.7 9.7 %collective-permute-start.37 = (bf16[512,128]{1,0:T(8,128)(2,1)S(1)}, bf16[512,128]{1,0:T(8,128)(2,1)S(1)}, u32[]{:S(2)}, u32[]{:S(2)}) collective-permute-start(bf16[512,128]{1,0:T(8,128)(2,1)S(1)} %get-tuple-element.190), channel_id=1, source_target_pairs={{0,12},{4,8},{8,4},{12,0},{1,13},{5,9},{9,5},{13,1},{2,14},{6,10},... | collective-permute-start | bytes 393224 | tf_op jit(solution)/shard_map/ppermute | solution.py:220
  203.6 4.2 %collective-permute-start.38 = (bf16[16,128]{1,0:T(8,128)(2,1)S(1)}, bf16[16,128]{1,0:T(8,128)(2,1)S(1)}, u32[]{:S(2)}, u32[]{:S(2)}) collective-permute-start(bf16[16,128]{1,0:T(8,128)(2,1)S(1)} %slice_bitcast_fusion.8), channel_id=1, source_target_pairs={{0,8},{4,12},{8,0},{12,4},{1,9},{5,13},{9,1},{13,5},{2,10},{6,14},... | collective-permute-start | bytes 12296 | tf_op jit(solution)/shard_map/ppermute | solution.py:220
  204.7 3.1 %collective-permute-start.39 = (bf16[16,128]{1,0:T(8,128)(2,1)S(1)}, bf16[16,128]{1,0:T(8,128)(2,1)S(1)}, u32[]{:S(2)}, u32[]{:S(2)}) collective-permute-start(bf16[16,128]{1,0:T(8,128)(2,1)S(1)} %slice_bitcast_fusion.8), channel_id=1, source_target_pairs={{0,12},{4,8},{8,4},{12,0},{1,13},{5,9},{9,5},{13,1},{2,14},{6,10},... | collective-permute-start | bytes 12296 | tf_op jit(solution)/shard_map/ppermute | solution.py:220
  205.7 2.1 %collective-permute-start.36 = (bf16[528,128]{1,0:T(8,128)(2,1)S(1)}, bf16[528,128]{1,0:T(8,128)(2,1)S(1)}, u32[]{:S(2)}, u32[]{:S(2)}) collective-permute-start(bf16[528,128]{1,0:T(8,128)(2,1)S(1)} %slice_bitcast_fusion.4), channel_id=1, source_target_pairs={{0,4},{4,0},{8,12},{12,8},{1,5},{5,1},{9,13},{13,9},{2,6},{6,2},{1... | collective-permute-start | bytes 405512 | tf_op jit(solution)/shard_map/ppermute | solution.py:220

commit v18 on v17

--- a/solution.py
+++ b/solution.py
@@ -182,7 +182,7 @@
             jax.ShapeDtypeStruct((8, rows), F32),
         ],
         compiler_params=PARAMS,
-        cost_estimate=SMALL,
+        cost_estimate=SOME,
         name="last_scores",
     )(kept, got, counts, before, *[piece[2] for piece in grads])
 
@@ -268,10 +268,9 @@
     near_got = to_other(near_sent, 2)
     third, third_sent = core_sum(*product(flags, [pair_in], fisher))
     (near,) = scores_of((near, near_got), cost=SOME)
-    far_ids = along(chosen_ids, [(0, 3), (3, 0)])
     counts = selected(chosen_ids)
-    far_in, second_edge, third, third_sent, own, own_got, near, far_ids, counts, grads = tied(
-        far_in, second_edge, third, third_sent, own, own_got, near, far_ids, counts, grads
+    far_in, second_edge, third, third_sent, own, own_got, near, counts, chosen_ids, grads = tied(
+        far_in, second_edge, third, third_sent, own, own_got, near, counts, chosen_ids, grads
     )
 
     first_edge = along(far_in, outward)
@@ -279,20 +278,24 @@
     second, second_sent, near = tied(second, second_sent, near)
     second_got = to_other(second_sent, 2)
     near_in, near_across = along(near, inward), along(near, middle)
-    second_got, near_in, near_across = tied(second_got, near_in, near_across)
+    second_got, near_in, near_across, chosen_ids = tied(
+        second_got, near_in, near_across, chosen_ids
+    )
+    far_ids = along(chosen_ids, [(0, 3), (3, 0)])
     (second,) = scores_of((second, second_got))
     across = along(second, middle)
     third, total = scores_of(
         (third, to_other(third_sent, 2)), (own, own_got), out_as=(F32, F32)
     )
+    first_edge, total, near_in, near_across, second, across, third, grads, far_ids = tied(
+        first_edge, total, near_in, near_across, second, across, third, grads, far_ids
+    )
     far_counts = selected(far_ids)
-    first_edge, total, near_in, near_across, second, across, third, grads, far_counts = tied(
-        first_edge, total, near_in, near_across, second, across, third, grads, far_counts
-    )
-
+
+    last, last_sent = core_sum(*product(flags, [first_edge], fisher))
+    last, second, third = tied(last, second, third)
     third = along((third + across.astype(F32)).astype(BF16), outward)
     second = along(second, [(0, 2), (3, 1)])
-    last, last_sent = core_sum(*product(flags, [first_edge], fisher))
     last_got = to_other(last_sent, 2)
     ends = [(0, 3), (3, 0)]
     none = jnp.zeros((8, quarter), F32)

time: 210 us -> 210 us (level)
    ppermute x13, waiting for transfers between devices: 13.2 us -> 17.9 us  [along(): return lax.ppermute(value, 'test', pairs)]
    ppermute x27, waiting for transfers between devices: 64.6 us -> 60.3 us  [to_other(): return lax.ppermute(value, 'train', [(k, k ^ r) for k in range(4)])]
where the time goes in v18:
time: 210 us
  waiting for transfers between devices  78.2 us (37%)
  Pallas kernels  55.3 us (26%)
  starting transfers between devices  53.6 us (26%)
  local copies, waits for them, and re-layouts  15.2 us (7%)
  other arithmetic  6.09 us (3%)
    ppermute x27, waiting for transfers between devices, to_other(): return lax.ppermute(value, 'train', [(k, k ^ r) for k in range(4)])  60.3 us
    ppermute x13, starting transfers between devices, along(): return lax.ppermute(value, 'test', pairs)  34.9 us
    pallas_call x5, Pallas kernels, product(): pl.pallas_call(functools.partial(product_body, len(blocks)), in_specs=[pl...  33.7 us
    ppermute x27, starting transfers between devices, to_other(): return lax.ppermute(value, 'train', [(k, k ^ r) for k in range(4)])  18.8 us
    ppermute x13, waiting for transfers between devices, along(): return lax.ppermute(value, 'test', pairs)  17.9 us
    unnamed x38, local copies, waits for them, and re-layouts  14 us
    pallas_call x3, Pallas kernels, partial_scores(): pl.pallas_call(functools.partial(scores_body, [piece[:2] for piece in gra...  10.6 us
    pallas_call x5, Pallas kernels, fold(): pl.pallas_call(fold_body, in_specs=[pl.BlockSpec(memory_space=pltpu.SMEM)...  5.82 us
  transfers between devices with their start and end apart: 40, of which 22 were waited for; matrix products, arithmetic and copies ran while one was open for 3% of the time, Pallas kernels for 23%

profile of v18, /device:TPU:0, one launch (start us, length us, event | category | flops | bytes accessed | tf_op | source)
XLA Modules:
  0.0 209.6 jit_solution(7896755700275332769)
XLA Ops:
  1.1 2.6 %collective-permute-start.5 = (bf16[512,2048]{1,0:T(8,128)(2,1)}, bf16[512,2048]{1,0:T(8,128)(2,1)S(1)}, u32[]{:S(2)}, u32[]{:S(2)}) collective-permute-start(bf16[512,2048]{1,0:T(8,128)(2,1)} %refs_0_.1), channel_id=1, source_target_pairs={{0,8},{4,12},{8,0},{12,4},{1,9},{5,13},{9,1},{13,5},{2,10},{6,14},... | collective-permute-start | bytes 6291464 | tf_op jit(solution)/shard_map/ppermute | solution.py:220
  3.7 1.6 collective-permute-start
  5.3 2.0 collective-permute-start.1
  7.4 1.6 copy-done.8
  9.0 2.0 hold.1
  11.0 1.4 copy-done.2
  12.4 1.3 copy-done.4
  13.7 3.4 %copy-done = bf16[2048,2048]{1,0:T(8,128)(2,1)S(1)} copy-done((bf16[2048,2048]{1,0:T(8,128)(2,1)S(1)}, bf16[2048,2048]{1,0:T(8,128)(2,1)}, u32[]{:S(2)}) %copy-start) | copy-done | bytes 8388632
  17.1 5.6 %product.5 = (f32[256,2048]{1,0:T(8,128)S(1)}, bf16[128,2048]{1,0:T(8,128)(2,1)S(1)}, bf16[128,2048]{1,0:T(8,128)(2,1)S(1)}) custom-call(s32[3]{0:T(128)S(1)} %pad_add_fusion.flags, bf16[512,2048]{1,0:T(8,128)(2,1)S(1)} %copy-done.11, bf16[2048,2048]{1,0:T(8,128)(2,1)S(1)} %copy-done), custom_call_target="tpu_custom_call" | custom-call | flops 1 | bytes 1 | tf_op jit(solution)/shard_map/product/pallas_call | solution.py:80
  23.3 26.9 %collective-permute-done.5.refs_4_.refs_6_.refs_0_ = bf16[512,2048]{1,0:T(8,128)(2,1)S(1)} collective-permute-done((bf16[512,2048]{1,0:T(8,128)(2,1)}, bf16[512,2048]{1,0:T(8,128)(2,1)S(1)}, u32[]{:S(2)}, u32[]{:S(2)}) %collective-permute-start.5) | collective-permute-done | bytes 2097184 | tf_op jit(solution)/shard_map/ppermute | solution.py:220
  50.9 1.8 fold.5
  53.0 1.5 collective-permute-done.7.refs_6_.refs_8_.refs_2_
  54.5 2.1 %collective-permute-start.8 = (bf16[512,2048]{1,0:T(8,128)(2,1)}, bf16[512,2048]{1,0:T(8,128)(2,1)}, u32[]{:S(2)}, u32[]{:S(2)}) collective-permute-start(bf16[512,2048]{1,0:T(8,128)(2,1)} %collective-permute-done.refs_1_.refs_0_), channel_id=1, source_target_pairs={{1,2},{2,1},{5,6},{6,5},{9,10},{10,9},{13,14},{14,13},{17,18},{18,... | collective-permute-start | bytes 6291464 | tf_op jit(solution)/shard_map/ppermute | solution.py:217
  56.7 1.3 collective-permute-start.9
  57.9 1.8 collective-permute-start.12
  59.8 8.3 %product.6 = (f32[256,2048]{1,0:T(8,128)S(1)}, bf16[128,2048]{1,0:T(8,128)(2,1)}, bf16[128,2048]{1,0:T(8,128)(2,1)}) custom-call(s32[3]{0:T(128)S(1)} %pad_add_fusion.flags, bf16[512,2048]{1,0:T(8,128)(2,1)} %collective-permute-done.1.refs_0_, bf16[512,2048]{1,0:T(8,128)(2,1)} %collective-permute-done.refs_1_.refs_0_, bf16[2048,2048]{1,0:T(8,128)(2,1)S(1)} %bitcast.115), custom_call_target="tpu_custom_call" | custom-call | flops 1 | bytes 1 | tf_op jit(solution)/shard_map/product/pallas_call | solution.py:80
  68.1 1.3 copy-done.9
  70.1 1.6 collective-permute-done.10.refs_0_
  71.7 0.7 collective-permute-done.11.refs_1_
  72.4 1.6 copy-done.10
  74.0 1.5 fold.6
  75.6 8.0 %collective-permute-done.12.refs_3_ = f32[128,2048]{1,0:T(8,128)} collective-permute-done((f32[128,2048]{1,0:T(8,128)}, f32[128,2048]{1,0:T(8,128)}, u32[]{:S(2)}, u32[]{:S(2)}) %collective-permute-start.12) | collective-permute-done | bytes 1048608 | tf_op jit(solution)/shard_map/ppermute | solution.py:220
  83.5 1.7 collective-permute-start.15
  85.3 3.4 %copy-done.1 = bf16[2048,2048]{1,0:T(8,128)(2,1)S(1)} copy-done((bf16[2048,2048]{1,0:T(8,128)(2,1)S(1)}, bf16[2048,2048]{1,0:T(8,128)(2,1)}, u32[]{:S(2)}) %copy-start.1) | copy-done | bytes 8388632
  88.7 6.9 %product.7 = (f32[256,2048]{1,0:T(8,128)S(1)}, bf16[128,2048]{1,0:T(8,128)(2,1)S(1)}, bf16[128,2048]{1,0:T(8,128)(2,1)S(1)}) custom-call(s32[3]{0:T(128)S(1)} %pad_add_fusion.flags, bf16[512,2048]{1,0:T(8,128)(2,1)} %collective-permute-done.refs_1_.refs_0_, bf16[2048,2048]{1,0:T(8,128)(2,1)S(1)} %copy-done.1), custom_call_target="tpu_custom_call" | custom-call | flops 1 | bytes 1 | tf_op jit(solution)/shard_map/product/pallas_call | solution.py:80
  96.1 1.7 convert_add_fusion.1
  98.3 0.8 fold.7
  99.1 2.4 %scores.3 = bf16[4,512,128]{2,1,0:T(8,128)(2,1)S(1)} custom-call(f32[128,2048]{1,0:T(8,128)S(1)} %get-tuple-element.115.refs_0_, bf16[128,2048]{1,0:T(8,128)(2,1)S(1)} %collective-permute-done.15.refs_1_, bf16[512,2048]{1,0:T(8,128)(2,1)S(1)} %copy-done.3, bf16[512,2048]{1,0:T(8,128)(2,1)S(1)} %copy-done.5, ...), custom_call_target="tpu_custom_call" | custom-call | flops 2000000000 | bytes 1048576 | tf_op jit(solution)/shard_map/scores/pallas_call | solution.py:144
  101.5 5.7 %collective-permute-done.9.refs_1_ = bf16[512,2048]{1,0:T(8,128)(2,1)} collective-permute-done((bf16[512,2048]{1,0:T(8,128)(2,1)}, bf16[512,2048]{1,0:T(8,128)(2,1)}, u32[]{:S(2)}, u32[]{:S(2)}) %collective-permute-start.9) | collective-permute-done | bytes 2097184 | tf_op jit(solution)/shard_map/ppermute | solution.py:217
  107.2 1.3 collective-permute-start.16
  108.5 7.3 %product.8 = (f32[256,2048]{1,0:T(8,128)S(1)}, bf16[128,2048]{1,0:T(8,128)(2,1)S(1)}, bf16[128,2048]{1,0:T(8,128)(2,1)S(1)}) custom-call(s32[3]{0:T(128)S(1)} %pad_add_fusion.flags, bf16[512,2048]{1,0:T(8,128)(2,1)} %collective-permute-done.8.refs_0_, bf16[512,2048]{1,0:T(8,128)(2,1)} %collective-permute-done.9.refs_1_, bf16[2048,2048]{1,0:T(8,128)(2,1)S(1)} %bitcast.117), custom_call_target="tpu_custom_call" | custom-call | flops 1 | bytes 1 | tf_op jit(solution)/shard_map/product/pallas_call | solution.py:80
  116.5 1.4 collective-permute-done.18.refs_0_
  117.9 0.7 collective-permute-done.19.refs_1_
  118.6 0.8 fold.8
  119.4 1.6 collective-permute-start.20
  121.0 4.7 %collective-permute-start.21 = (bf16[4,512,128]{2,1,0:T(8,128)(2,1)S(1)}, bf16[4,512,128]{2,1,0:T(8,128)(2,1)S(1)}, u32[]{:S(2)}, u32[]{:S(2)}) collective-permute-start(bf16[4,512,128]{2,1,0:T(8,128)(2,1)S(1)} %scores.3), channel_id=1, source_target_pairs={{0,1},{3,2},{4,5},{7,6},{8,9},{11,10},{12,13},{15,14},{16,17},{19,... | collective-permute-start | bytes 1572872 | tf_op jit(solution)/shard_map/ppermute | solution.py:217
  125.7 0.9 collective-permute-start.22
  127.2 7.1 %collective-permute-done.20.refs_1_ = bf16[128,2048]{1,0:T(8,128)(2,1)S(1)} collective-permute-done((bf16[128,2048]{1,0:T(8,128)(2,1)S(1)}, bf16[128,2048]{1,0:T(8,128)(2,1)S(1)}, u32[]{:S(2)}, u32[]{:S(2)}) %collective-permute-start.20) | collective-permute-done | bytes 524320 | tf_op jit(solution)/shard_map/ppermute | solution.py:220
  134.3 2.6 %collective-permute-done.21 = bf16[4,512,128]{2,1,0:T(8,128)(2,1)S(1)} collective-permute-done((bf16[4,512,128]{2,1,0:T(8,128)(2,1)S(1)}, bf16[4,512,128]{2,1,0:T(8,128)(2,1)S(1)}, u32[]{:S(2)}, u32[]{:S(2)}) %collective-permute-start.21) | collective-permute-done | bytes 524320 | tf_op jit(solution)/shard_map/ppermute | solution.py:217
  136.9 2.4 %scores.5 = bf16[4,512,128]{2,1,0:T(8,128)(2,1)S(1)} custom-call(f32[128,2048]{1,0:T(8,128)S(1)} %get-tuple-element.146.refs_0_, bf16[128,2048]{1,0:T(8,128)(2,1)S(1)} %collective-permute-done.20.refs_1_, bf16[512,2048]{1,0:T(8,128)(2,1)S(1)} %copy-done.3, bf16[512,2048]{1,0:T(8,128)(2,1)S(1)} %copy-done.5, ...), custom_call_target="tpu_custom_call" | custom-call | flops 1 | bytes 1 | tf_op jit(solution)/shard_map/scores/pallas_call | solution.py:144
  140.0 5.1 %collective-permute-start.24 = (s32[512,16]{0,1:T(8,128)S(1)}, s32[512,16]{0,1:T(8,128)S(1)}, u32[]{:S(2)}, u32[]{:S(2)}) collective-permute-start(s32[512,16]{0,1:T(8,128)S(1)} %copy-done.14), channel_id=1, source_target_pairs={{0,3},{3,0},{4,7},{7,4},{8,11},{11,8},{12,15},{15,12},{16,19},{19,... | collective-permute-start | bytes 98312 | tf_op jit(solution)/shard_map/ppermute | solution.py:217
  145.1 5.8 %scores.4 = (f32[4,512,128]{2,1,0:T(8,128)S(1)}, f32[4,512,128]{2,1,0:T(8,128)S(1)}) custom-call(f32[128,2048]{1,0:T(8,128)S(1)} %get-tuple-element.124.refs_0_, bf16[128,2048]{1,0:T(8,128)(2,1)S(1)} %collective-permute-done.17.refs_1_, f32[128,2048]{1,0:T(8,128)S(1)} %copy-done.13, f32[128,2048]{1,0:T(8,128)} %collective-permute-done.12.refs_3_, ...), custom_call_target="tpu_custom_call" | custom-call | flops 1 | bytes 1 | tf_op jit(solution)/shard_map/scores/pallas_call | solution.py:144
  150.9 5.9 %collective-permute-done.16.refs_0_ = bf16[512,2048]{1,0:T(8,128)(2,1)S(1)} collective-permute-done((bf16[512,2048]{1,0:T(8,128)(2,1)}, bf16[512,2048]{1,0:T(8,128)(2,1)S(1)}, u32[]{:S(2)}, u32[]{:S(2)}) %collective-permute-start.16) | collective-permute-done | bytes 2097184 | tf_op jit(solution)/shard_map/ppermute | solution.py:217
  156.8 5.6 %product.9 = (f32[256,2048]{1,0:T(8,128)S(1)}, bf16[128,2048]{1,0:T(8,128)(2,1)S(1)}, bf16[128,2048]{1,0:T(8,128)(2,1)S(1)}) custom-call(s32[3]{0:T(128)S(1)} %pad_add_fusion.flags, bf16[512,2048]{1,0:T(8,128)(2,1)S(1)} %collective-permute-done.16.refs_0_, bf16[2048,2048]{1,0:T(8,128)(2,1)S(1)} %bitcast.117), custom_call_target="tpu_custom_call" | custom-call | flops 1 | bytes 1 | tf_op jit(solution)/shard_map/product/pallas_call | solution.py:80
  163.0 1.4 collective-permute-done.25.refs_0_
  165.1 0.8 fold.9
  166.0 1.6 collective-permute-start.27
  167.7 1.3 collective-permute-start.29
  169.0 6.3 %collective-permute-start.28 = (bf16[4,512,128]{2,1,0:T(8,128)(2,1)S(1)}, bf16[4,512,128]{2,1,0:T(8,128)(2,1)S(1)}, u32[]{:S(2)}, u32[]{:S(2)}) collective-permute-start(bf16[4,512,128]{2,1,0:T(8,128)(2,1)S(1)} %scores.5), channel_id=1, source_target_pairs={{0,2},{3,1},{4,6},{7,5},{8,10},{11,9},{12,14},{15,13},{16,18},{19,... | collective-permute-start | bytes 1572872 | tf_op jit(solution)/shard_map/ppermute | solution.py:217
  175.3 1.7 convert_add_fusion.counts
  177.0 3.0 %collective-permute-done.27.got = bf16[128,2048]{1,0:T(8,128)(2,1)S(1)} collective-permute-done((bf16[128,2048]{1,0:T(8,128)(2,1)S(1)}, bf16[128,2048]{1,0:T(8,128)(2,1)S(1)}, u32[]{:S(2)}, u32[]{:S(2)}) %collective-permute-start.27) | collective-permute-done | bytes 524320 | tf_op jit(solution)/shard_map/ppermute | solution.py:220
  180.0 1.3 last_scores.2
  181.3 1.9 last_scores.3
  183.3 2.9 %collective-permute-done.28 = bf16[4,512,128]{2,1,0:T(8,128)(2,1)S(1)} collective-permute-done((bf16[4,512,128]{2,1,0:T(8,128)(2,1)S(1)}, bf16[4,512,128]{2,1,0:T(8,128)(2,1)S(1)}, u32[]{:S(2)}, u32[]{:S(2)}) %collective-permute-start.28) | collective-permute-done | bytes 524320 | tf_op jit(solution)/shard_map/ppermute | solution.py:217
  186.2 2.5 %collective-permute-start.34 = (bf16[2,512,128]{2,1,0:T(8,128)(2,1)S(1)}, bf16[2,512,128]{2,1,0:T(8,128)(2,1)}, u32[]{:S(2)}, u32[]{:S(2)}) collective-permute-start(bf16[2,512,128]{2,1,0:T(8,128)(2,1)S(1)} %get-tuple-element.177), channel_id=1, source_target_pairs={{0,3},{3,0},{4,7},{7,4},{8,11},{11,8},{12,15},{15,12},{16,19},{19,... | collective-permute-start | bytes 786440 | tf_op jit(solution)/shard_map/ppermute | solution.py:217
  189.3 1.2 collective-permute-start.30
  190.5 1.0 collective-permute-start.32
  191.5 5.1 %collective-permute-start.33 = (bf16[2,528,128]{2,1,0:T(8,128)(2,1)S(1)}, bf16[2,528,128]{2,1,0:T(8,128)(2,1)S(1)}, u32[]{:S(2)}, u32[]{:S(2)}) collective-permute-start(bf16[2,528,128]{2,1,0:T(8,128)(2,1)S(1)} %get-tuple-element.176), channel_id=1, source_target_pairs={{0,3},{3,0},{4,7},{7,4},{8,11},{11,8},{12,15},{15,12},{16,19},{19,... | collective-permute-start | bytes 811016 | tf_op jit(solution)/shard_map/ppermute | solution.py:217
  196.9 1.0 slice_bitcast_fusion.5
  198.7 4.3 %collective-permute-done.32 = f32[520,128]{1,0:T(8,128)S(1)} collective-permute-done((f32[520,128]{1,0:T(8,128)S(1)}, f32[520,128]{1,0:T(8,128)S(1)}, u32[]{:S(2)}, u32[]{:S(2)}) %collective-permute-start.32) | collective-permute-done | bytes 266272 | tf_op jit(solution)/shard_map/ppermute | solution.py:220
  203.6 1.1 collective-permute-start.38
  204.7 1.0 collective-permute-start.39
  205.9 1.8 collective-permute-done.38
  208.4 1.1 slice_add_fusion
  (97 shorter events, 10.5 us)
Async XLA Ops:
  0.6 6.8 %collective-permute-start.2 = (bf16[512,2048]{1,0:T(8,128)(2,1)}, bf16[512,2048]{1,0:T(8,128)(2,1)}, u32[]{:S(2)}, u32[]{:S(2)}) collective-permute-start(bf16[512,2048]{1,0:T(8,128)(2,1)} %refs_0_.1), channel_id=1, source_target_pairs={{0,4},{4,0},{8,12},{12,8},{1,5},{5,1},{9,13},{13,9},{2,6},{6,2},{1... | collective-permute-start | bytes 6291464 | tf_op jit(solution)/shard_map/ppermute | solution.py:220
  1.1 49.0 %collective-permute-start.5 = (bf16[512,2048]{1,0:T(8,128)(2,1)}, bf16[512,2048]{1,0:T(8,128)(2,1)S(1)}, u32[]{:S(2)}, u32[]{:S(2)}) collective-permute-start(bf16[512,2048]{1,0:T(8,128)(2,1)} %refs_0_.1), channel_id=1, source_target_pairs={{0,8},{4,12},{8,0},{12,4},{1,9},{5,13},{9,1},{13,5},{2,10},{6,14},... | collective-permute-start | bytes 6291464 | tf_op jit(solution)/shard_map/ppermute | solution.py:220
  3.7 49.0 %collective-permute-start = (bf16[512,2048]{1,0:T(8,128)(2,1)}, bf16[512,2048]{1,0:T(8,128)(2,1)}, u32[]{:S(2)}, u32[]{:S(2)}) collective-permute-start(bf16[512,2048]{1,0:T(8,128)(2,1)} %refs_0_.2), channel_id=1, source_target_pairs={{0,1},{1,0},{2,3},{3,2},{4,5},{5,4},{6,7},{7,6},{8,9},{9,8},{10,11... | collective-permute-start | bytes 6291464 | tf_op jit(solution)/shard_map/ppermute | solution.py:217
  5.3 47.4 %collective-permute-start.1 = (bf16[512,2048]{1,0:T(8,128)(2,1)}, bf16[512,2048]{1,0:T(8,128)(2,1)}, u32[]{:S(2)}, u32[]{:S(2)}) collective-permute-start(bf16[512,2048]{1,0:T(8,128)(2,1)} %refs_0_.2), channel_id=1, source_target_pairs={{1,2},{2,1},{5,6},{6,5},{9,10},{10,9},{13,14},{14,13},{17,18},{18,... | collective-permute-start | bytes 6291464 | tf_op jit(solution)/shard_map/ppermute | solution.py:217
  7.4 1.6 copy-start.8
  9.0 4.7 %copy-start.11 = (bf16[512,2048]{1,0:T(8,128)(2,1)S(1)}, bf16[512,2048]{1,0:T(8,128)(2,1)}, u32[]{:S(2)}) copy-start(bf16[512,2048]{1,0:T(8,128)(2,1)} %refs_0_.2) | copy-start | bytes 6291460
  11.0 1.4 copy-start.2
  12.4 1.3 copy-start.4
  13.7 3.4 %copy-start = (bf16[2048,2048]{1,0:T(8,128)(2,1)S(1)}, bf16[2048,2048]{1,0:T(8,128)(2,1)}, u32[]{:S(2)}) copy-start(bf16[2048,2048]{1,0:T(8,128)(2,1)} %refs_1_.5) | copy-start | bytes 25165828
  22.7 27.7 %collective-permute-start.3 = (bf16[128,2048]{1,0:T(8,128)(2,1)S(1)}, bf16[128,2048]{1,0:T(8,128)(2,1)S(1)}, u32[]{:S(2)}, u32[]{:S(2)}) collective-permute-start(bf16[128,2048]{1,0:T(8,128)(2,1)S(1)} %get-tuple-element.94), channel_id=1, source_target_pairs={{0,4},{4,0},{8,12},{12,8},{1,5},{5,1},{9,13},{13,9},{2,6},{6,2},{1... | collective-permute-start | bytes 1572872 | tf_op jit(solution)/shard_map/ppermute | solution.py:220
  22.8 28.1 %collective-permute-start.4 = (bf16[128,2048]{1,0:T(8,128)(2,1)S(1)}, bf16[128,2048]{1,0:T(8,128)(2,1)S(1)}, u32[]{:S(2)}, u32[]{:S(2)}) collective-permute-start(bf16[128,2048]{1,0:T(8,128)(2,1)S(1)} %get-tuple-element.95), channel_id=1, source_target_pairs={{0,4},{4,0},{8,12},{12,8},{1,5},{5,1},{9,13},{13,9},{2,6},{6,2},{1... | collective-permute-start | bytes 1572872 | tf_op jit(solution)/shard_map/ppermute | solution.py:220
  50.3 2.7 %collective-permute-start.6 = (bf16[256,2048]{1,0:T(8,128)(2,1)S(1)}, bf16[256,2048]{1,0:T(8,128)(2,1)S(1)}, u32[]{:S(2)}, u32[]{:S(2)}) collective-permute-start(bf16[256,2048]{1,0:T(8,128)(2,1)S(1)} %get-tuple-element.181), channel_id=1, source_target_pairs={{0,4},{4,0},{8,12},{12,8},{1,5},{5,1},{9,13},{13,9},{2,6},{6,2},{1... | collective-permute-start | bytes 3145736 | tf_op jit(solution)/shard_map/ppermute | solution.py:220
  50.4 4.1 %collective-permute-start.7 = (bf16[256,2048]{1,0:T(8,128)(2,1)S(1)}, bf16[256,2048]{1,0:T(8,128)(2,1)S(1)}, u32[]{:S(2)}, u32[]{:S(2)}) collective-permute-start(bf16[256,2048]{1,0:T(8,128)(2,1)S(1)} %get-tuple-element.180), channel_id=1, source_target_pairs={{0,4},{4,0},{8,12},{12,8},{1,5},{5,1},{9,13},{13,9},{2,6},{6,2},{1... | collective-permute-start | bytes 3145736 | tf_op jit(solution)/shard_map/ppermute | solution.py:220
  50.9 8.9 %slice-start = ((s8[8388608]{0:T(1024)(128)(4,1)}), s8[4194304]{0:T(1024)(128)(4,1)S(1)}, s32[]{:S(2)}) async-start(s8[8388608]{0:T(1024)(128)(4,1)} %bitcast.114), calls=%async_computation | async-start | bytes 8388608
  50.9 8.9 %slice-start.1 = ((s8[8388608]{0:T(1024)(128)(4,1)}), s8[4194304]{0:T(1024)(128)(4,1)S(1)}, s32[]{:S(2)}) async-start(s8[8388608]{0:T(1024)(128)(4,1)} %bitcast.114), calls=%async_computation.1 | async-start | bytes 8388608
  52.7 15.4 %copy-start.12 = (f32[128,2048]{1,0:T(8,128)}, f32[128,2048]{1,0:T(8,128)S(1)}, u32[]{:S(2)}) copy-start(f32[128,2048]{1,0:T(8,128)S(1)} %get-tuple-element.126.refs_2_) | copy-start | bytes 3145732
  54.5 13.6 %copy-start.6 = (bf16[256,2048]{1,0:T(8,128)(2,1)}, bf16[256,2048]{1,0:T(8,128)(2,1)S(1)}, u32[]{:S(2)}) copy-start(bf16[256,2048]{1,0:T(8,128)(2,1)S(1)} %collective-permute-done.7.refs_6_.refs_8_.refs_2_) | copy-start | bytes 3145732
  54.5 15.6 %copy-start.14 = (s32[512,16]{0,1:T(8,128)S(1)}, s32[512,16]{0,1:T(8,128)}, u32[]{:S(2)}) copy-start(s32[512,16]{0,1:T(8,128)} %param.7) | copy-start | bytes 98308
  54.5 47.0 %collective-permute-start.8 = (bf16[512,2048]{1,0:T(8,128)(2,1)}, bf16[512,2048]{1,0:T(8,128)(2,1)}, u32[]{:S(2)}, u32[]{:S(2)}) collective-permute-start(bf16[512,2048]{1,0:T(8,128)(2,1)} %collective-permute-done.refs_1_.refs_0_), channel_id=1, source_target_pairs={{1,2},{2,1},{5,6},{6,5},{9,10},{10,9},{13,14},{14,13},{17,18},{18,... | collective-permute-start | bytes 6291464 | tf_op jit(solution)/shard_map/ppermute | solution.py:217
  56.7 50.6 %collective-permute-start.9 = (bf16[512,2048]{1,0:T(8,128)(2,1)}, bf16[512,2048]{1,0:T(8,128)(2,1)}, u32[]{:S(2)}, u32[]{:S(2)}) collective-permute-start(bf16[512,2048]{1,0:T(8,128)(2,1)} %collective-permute-done.1.refs_0_), channel_id=1, source_target_pairs={{1,0},{2,3},{5,4},{6,7},{9,8},{10,11},{13,12},{14,15},{17,16},{18,... | collective-permute-start | bytes 6291464 | tf_op jit(solution)/shard_map/ppermute | solution.py:217
  57.9 25.6 %collective-permute-start.12 = (f32[128,2048]{1,0:T(8,128)}, f32[128,2048]{1,0:T(8,128)}, u32[]{:S(2)}, u32[]{:S(2)}) collective-permute-start(f32[128,2048]{1,0:T(8,128)} %get-tuple-element.106), channel_id=1, source_target_pairs={{0,8},{4,12},{8,0},{12,4},{1,9},{5,13},{9,1},{13,5},{2,10},{6,14},... | collective-permute-start | bytes 3145736 | tf_op jit(solution)/shard_map/ppermute | solution.py:220
  68.1 1.3 copy-start.9
  69.4 2.3 %collective-permute-start.10 = (bf16[128,2048]{1,0:T(8,128)(2,1)}, bf16[128,2048]{1,0:T(8,128)(2,1)}, u32[]{:S(2)}, u32[]{:S(2)}) collective-permute-start(bf16[128,2048]{1,0:T(8,128)(2,1)} %get-tuple-element.103), channel_id=1, source_target_pairs={{0,4},{4,0},{8,12},{12,8},{1,5},{5,1},{9,13},{13,9},{2,6},{6,2},{1... | collective-permute-start | bytes 1572872 | tf_op jit(solution)/shard_map/ppermute | solution.py:220
  69.4 3.0 %collective-permute-start.11 = (bf16[128,2048]{1,0:T(8,128)(2,1)}, bf16[128,2048]{1,0:T(8,128)(2,1)}, u32[]{:S(2)}, u32[]{:S(2)}) collective-permute-start(bf16[128,2048]{1,0:T(8,128)(2,1)} %get-tuple-element.104), channel_id=1, source_target_pairs={{0,4},{4,0},{8,12},{12,8},{1,5},{5,1},{9,13},{13,9},{2,6},{6,2},{1... | collective-permute-start | bytes 1572872 | tf_op jit(solution)/shard_map/ppermute | solution.py:220
  72.4 1.6 copy-start.10
  83.5 15.5 %collective-permute-start.15 = (bf16[128,2048]{1,0:T(8,128)(2,1)S(1)}, bf16[128,2048]{1,0:T(8,128)(2,1)S(1)}, u32[]{:S(2)}, u32[]{:S(2)}) collective-permute-start(bf16[128,2048]{1,0:T(8,128)(2,1)S(1)} %get-tuple-element.116), channel_id=1, source_target_pairs={{0,8},{4,12},{8,0},{12,4},{1,9},{5,13},{9,1},{13,5},{2,10},{6,14},... | collective-permute-start | bytes 1572872 | tf_op jit(solution)/shard_map/ppermute | solution.py:220
  85.3 3.4 %copy-start.1 = (bf16[2048,2048]{1,0:T(8,128)(2,1)S(1)}, bf16[2048,2048]{1,0:T(8,128)(2,1)}, u32[]{:S(2)}) copy-start(bf16[2048,2048]{1,0:T(8,128)(2,1)} %refs_1_.5) | copy-start | bytes 25165828
  88.7 10.4 %copy-start.7 = (bf16[256,2048]{1,0:T(8,128)(2,1)S(1)}, bf16[256,2048]{1,0:T(8,128)(2,1)}, u32[]{:S(2)}) copy-start(bf16[256,2048]{1,0:T(8,128)(2,1)} %copy-done.6) | copy-start | bytes 3145732
  88.7 19.8 %slice-start.2 = ((s8[8388608]{0:T(1024)(128)(4,1)}), s8[4194304]{0:T(1024)(128)(4,1)S(1)}, s32[]{:S(2)}) async-start(s8[8388608]{0:T(1024)(128)(4,1)} %bitcast.116), calls=%async_computation.2 | async-start | bytes 8388608
  95.5 2.3 %collective-permute-start.13 = (bf16[128,2048]{1,0:T(8,128)(2,1)S(1)}, bf16[128,2048]{1,0:T(8,128)(2,1)S(1)}, u32[]{:S(2)}, u32[]{:S(2)}) collective-permute-start(bf16[128,2048]{1,0:T(8,128)(2,1)S(1)} %get-tuple-element.109), channel_id=1, source_target_pairs={{0,4},{4,0},{8,12},{12,8},{1,5},{5,1},{9,13},{13,9},{2,6},{6,2},{1... | collective-permute-start | bytes 1572872 | tf_op jit(solution)/shard_map/ppermute | solution.py:220
  95.6 2.6 %collective-permute-start.14 = (bf16[128,2048]{1,0:T(8,128)(2,1)S(1)}, bf16[128,2048]{1,0:T(8,128)(2,1)S(1)}, u32[]{:S(2)}, u32[]{:S(2)}) collective-permute-start(bf16[128,2048]{1,0:T(8,128)(2,1)S(1)} %get-tuple-element.110), channel_id=1, source_target_pairs={{0,4},{4,0},{8,12},{12,8},{1,5},{5,1},{9,13},{13,9},{2,6},{6,2},{1... | collective-permute-start | bytes 1572872 | tf_op jit(solution)/shard_map/ppermute | solution.py:220
  96.1 3.0 %copy-start.3 = (bf16[512,2048]{1,0:T(8,128)(2,1)S(1)}, bf16[512,2048]{1,0:T(8,128)(2,1)}, u32[]{:S(2)}) copy-start(bf16[512,2048]{1,0:T(8,128)(2,1)} %copy-done.2) | copy-start | bytes 6291460
  96.1 3.0 %copy-start.5 = (bf16[512,2048]{1,0:T(8,128)(2,1)S(1)}, bf16[512,2048]{1,0:T(8,128)(2,1)}, u32[]{:S(2)}) copy-start(bf16[512,2048]{1,0:T(8,128)(2,1)} %copy-done.4) | copy-start | bytes 6291460
  98.3 10.3 %slice-start.3 = ((s8[8388608]{0:T(1024)(128)(4,1)}), s8[4194304]{0:T(1024)(128)(4,1)S(1)}, s32[]{:S(2)}) async-start(s8[8388608]{0:T(1024)(128)(4,1)} %bitcast.116), calls=%async_computation.3 | async-start | bytes 8388608
  107.2 49.6 %collective-permute-start.16 = (bf16[512,2048]{1,0:T(8,128)(2,1)}, bf16[512,2048]{1,0:T(8,128)(2,1)S(1)}, u32[]{:S(2)}, u32[]{:S(2)}) collective-permute-start(bf16[512,2048]{1,0:T(8,128)(2,1)} %collective-permute-done.8.refs_0_), channel_id=1, source_target_pairs={{1,0},{2,3},{5,4},{6,7},{9,8},{10,11},{13,12},{14,15},{17,16},{18,... | collective-permute-start | bytes 6291464 | tf_op jit(solution)/shard_map/ppermute | solution.py:217
  115.9 2.0 collective-permute-start.18
  116.0 2.6 %collective-permute-start.19 = (bf16[128,2048]{1,0:T(8,128)(2,1)S(1)}, bf16[128,2048]{1,0:T(8,128)(2,1)S(1)}, u32[]{:S(2)}, u32[]{:S(2)}) collective-permute-start(bf16[128,2048]{1,0:T(8,128)(2,1)S(1)} %get-tuple-element.137), channel_id=1, source_target_pairs={{0,4},{4,0},{8,12},{12,8},{1,5},{5,1},{9,13},{13,9},{2,6},{6,2},{1... | collective-permute-start | bytes 1572872 | tf_op jit(solution)/shard_map/ppermute | solution.py:220
  119.4 25.6 %copy-start.13 = (f32[128,2048]{1,0:T(8,128)S(1)}, f32[128,2048]{1,0:T(8,128)}, u32[]{:S(2)}) copy-start(f32[128,2048]{1,0:T(8,128)} %copy-done.12) | copy-start | bytes 3145732
  119.4 14.8 %collective-permute-start.20 = (bf16[128,2048]{1,0:T(8,128)(2,1)S(1)}, bf16[128,2048]{1,0:T(8,128)(2,1)S(1)}, u32[]{:S(2)}, u32[]{:S(2)}) collective-permute-start(bf16[128,2048]{1,0:T(8,128)(2,1)S(1)} %get-tuple-element.141), channel_id=1, source_target_pairs={{0,8},{4,12},{8,0},{12,4},{1,9},{5,13},{9,1},{13,5},{2,10},{6,14},... | collective-permute-start | bytes 1572872 | tf_op jit(solution)/shard_map/ppermute | solution.py:220
  121.0 15.9 %collective-permute-start.21 = (bf16[4,512,128]{2,1,0:T(8,128)(2,1)S(1)}, bf16[4,512,128]{2,1,0:T(8,128)(2,1)S(1)}, u32[]{:S(2)}, u32[]{:S(2)}) collective-permute-start(bf16[4,512,128]{2,1,0:T(8,128)(2,1)S(1)} %scores.3), channel_id=1, source_target_pairs={{0,1},{3,2},{4,5},{7,6},{8,9},{11,10},{12,13},{15,14},{16,17},{19,... | collective-permute-start | bytes 1572872 | tf_op jit(solution)/shard_map/ppermute | solution.py:217
  125.7 11.2 %collective-permute-start.22 = (bf16[4,512,128]{2,1,0:T(8,128)(2,1)S(1)}, bf16[4,512,128]{2,1,0:T(8,128)(2,1)S(1)}, u32[]{:S(2)}, u32[]{:S(2)}) collective-permute-start(bf16[4,512,128]{2,1,0:T(8,128)(2,1)S(1)} %scores.3), channel_id=1, source_target_pairs={{1,2},{2,1},{5,6},{6,5},{9,10},{10,9},{13,14},{14,13},{17,18},{18,... | collective-permute-start | bytes 1572872 | tf_op jit(solution)/shard_map/ppermute | solution.py:217
  126.6 18.5 %collective-permute-start.17 = (bf16[128,2048]{1,0:T(8,128)(2,1)S(1)}, bf16[128,2048]{1,0:T(8,128)(2,1)S(1)}, u32[]{:S(2)}, u32[]{:S(2)}) collective-permute-start(bf16[128,2048]{1,0:T(8,128)(2,1)S(1)} %get-tuple-element.125), channel_id=1, source_target_pairs={{0,8},{4,12},{8,0},{12,4},{1,9},{5,13},{9,1},{13,5},{2,10},{6,14},... | collective-permute-start | bytes 1572872 | tf_op jit(solution)/shard_map/ppermute | solution.py:220
  139.3 11.7 %collective-permute-start.23 = (bf16[4,512,128]{2,1,0:T(8,128)(2,1)S(1)}, bf16[4,512,128]{2,1,0:T(8,128)(2,1)S(1)}, u32[]{:S(2)}, u32[]{:S(2)}) collective-permute-start(bf16[4,512,128]{2,1,0:T(8,128)(2,1)S(1)} %scores.5), channel_id=1, source_target_pairs={{1,2},{2,1},{5,6},{6,5},{9,10},{10,9},{13,14},{14,13},{17,18},{18,... | collective-permute-start | bytes 1572872 | tf_op jit(solution)/shard_map/ppermute | solution.py:217
  140.0 10.9 %collective-permute-start.24 = (s32[512,16]{0,1:T(8,128)S(1)}, s32[512,16]{0,1:T(8,128)S(1)}, u32[]{:S(2)}, u32[]{:S(2)}) collective-permute-start(s32[512,16]{0,1:T(8,128)S(1)} %copy-done.14), channel_id=1, source_target_pairs={{0,3},{3,0},{4,7},{7,4},{8,11},{11,8},{12,15},{15,12},{16,19},{19,... | collective-permute-start | bytes 98312 | tf_op jit(solution)/shard_map/ppermute | solution.py:217
  162.4 2.0 collective-permute-start.25
  162.5 2.6 %collective-permute-start.26 = (bf16[128,2048]{1,0:T(8,128)(2,1)S(1)}, bf16[128,2048]{1,0:T(8,128)(2,1)S(1)}, u32[]{:S(2)}, u32[]{:S(2)}) collective-permute-start(bf16[128,2048]{1,0:T(8,128)(2,1)S(1)} %get-tuple-element.156), channel_id=1, source_target_pairs={{0,4},{4,0},{8,12},{12,8},{1,5},{5,1},{9,13},{13,9},{2,6},{6,2},{1... | collective-permute-start | bytes 1572872 | tf_op jit(solution)/shard_map/ppermute | solution.py:220
  166.0 14.0 %collective-permute-start.27 = (bf16[128,2048]{1,0:T(8,128)(2,1)S(1)}, bf16[128,2048]{1,0:T(8,128)(2,1)S(1)}, u32[]{:S(2)}, u32[]{:S(2)}) collective-permute-start(bf16[128,2048]{1,0:T(8,128)(2,1)S(1)} %get-tuple-element.161), channel_id=1, source_target_pairs={{0,8},{4,12},{8,0},{12,4},{1,9},{5,13},{9,1},{13,5},{2,10},{6,14},... | collective-permute-start | bytes 1572872 | tf_op jit(solution)/shard_map/ppermute | solution.py:220
  167.7 15.6 %collective-permute-start.29 = (bf16[4,512,128]{2,1,0:T(8,128)(2,1)S(1)}, bf16[4,512,128]{2,1,0:T(8,128)(2,1)S(1)}, u32[]{:S(2)}, u32[]{:S(2)}) collective-permute-start(bf16[4,512,128]{2,1,0:T(8,128)(2,1)S(1)} %add_convert_fusion), channel_id=1, source_target_pairs={{1,0},{2,3},{5,4},{6,7},{9,8},{10,11},{13,12},{14,15},{17,16},{18,... | collective-permute-start | bytes 1572872 | tf_op jit(solution)/shard_map/ppermute | solution.py:217
  169.0 17.2 %collective-permute-start.28 = (bf16[4,512,128]{2,1,0:T(8,128)(2,1)S(1)}, bf16[4,512,128]{2,1,0:T(8,128)(2,1)S(1)}, u32[]{:S(2)}, u32[]{:S(2)}) collective-permute-start(bf16[4,512,128]{2,1,0:T(8,128)(2,1)S(1)} %scores.5), channel_id=1, source_target_pairs={{0,2},{3,1},{4,6},{7,5},{8,10},{11,9},{12,14},{15,13},{16,18},{19,... | collective-permute-start | bytes 1572872 | tf_op jit(solution)/shard_map/ppermute | solution.py:217
  186.2 10.7 %collective-permute-start.34 = (bf16[2,512,128]{2,1,0:T(8,128)(2,1)S(1)}, bf16[2,512,128]{2,1,0:T(8,128)(2,1)}, u32[]{:S(2)}, u32[]{:S(2)}) collective-permute-start(bf16[2,512,128]{2,1,0:T(8,128)(2,1)S(1)} %get-tuple-element.177), channel_id=1, source_target_pairs={{0,3},{3,0},{4,7},{7,4},{8,11},{11,8},{12,15},{15,12},{16,19},{19,... | collective-permute-start | bytes 786440 | tf_op jit(solution)/shard_map/ppermute | solution.py:217
  189.3 9.4 %collective-permute-start.30 = (f32[520,128]{1,0:T(8,128)S(1)}, f32[520,128]{1,0:T(8,128)S(1)}, u32[]{:S(2)}, u32[]{:S(2)}) collective-permute-start(f32[520,128]{1,0:T(8,128)S(1)} %get-tuple-element.232), channel_id=1, source_target_pairs={{0,8},{4,12},{8,0},{12,4},{1,9},{5,13},{9,1},{13,5},{2,10},{6,14},... | collective-permute-start | bytes 798728 | tf_op jit(solution)/shard_map/ppermute | solution.py:220
  190.5 8.3 %collective-permute-start.31 = (f32[520,128]{1,0:T(8,128)S(1)}, f32[520,128]{1,0:T(8,128)S(1)}, u32[]{:S(2)}, u32[]{:S(2)}) collective-permute-start(f32[520,128]{1,0:T(8,128)S(1)} %get-tuple-element.233), channel_id=1, source_target_pairs={{0,4},{4,0},{8,12},{12,8},{1,5},{5,1},{9,13},{13,9},{2,6},{6,2},{1... | collective-permute-start | bytes 798728 | tf_op jit(solution)/shard_map/ppermute | solution.py:220
  190.5 12.6 %collective-permute-start.32 = (f32[520,128]{1,0:T(8,128)S(1)}, f32[520,128]{1,0:T(8,128)S(1)}, u32[]{:S(2)}, u32[]{:S(2)}) collective-permute-start(f32[520,128]{1,0:T(8,128)S(1)} %get-tuple-element.234), channel_id=1, source_target_pairs={{0,12},{4,8},{8,4},{12,0},{1,13},{5,9},{9,5},{13,1},{2,14},{6,10},... | collective-permute-start | bytes 798728 | tf_op jit(solution)/shard_map/ppermute | solution.py:220
  191.5 12.1 %collective-permute-start.33 = (bf16[2,528,128]{2,1,0:T(8,128)(2,1)S(1)}, bf16[2,528,128]{2,1,0:T(8,128)(2,1)S(1)}, u32[]{:S(2)}, u32[]{:S(2)}) collective-permute-start(bf16[2,528,128]{2,1,0:T(8,128)(2,1)S(1)} %get-tuple-element.176), channel_id=1, source_target_pairs={{0,3},{3,0},{4,7},{7,4},{8,11},{11,8},{12,15},{15,12},{16,19},{19,... | collective-permute-start | bytes 811016 | tf_op jit(solution)/shard_map/ppermute | solution.py:217
  197.9 10.5 %collective-permute-start.35 = (bf16[512,128]{1,0:T(8,128)(2,1)S(1)}, bf16[512,128]{1,0:T(8,128)(2,1)S(1)}, u32[]{:S(2)}, u32[]{:S(2)}) collective-permute-start(bf16[512,128]{1,0:T(8,128)(2,1)S(1)} %get-tuple-element.199), channel_id=1, source_target_pairs={{0,8},{4,12},{8,0},{12,4},{1,9},{5,13},{9,1},{13,5},{2,10},{6,14},... | collective-permute-start | bytes 393224 | tf_op jit(solution)/shard_map/ppermute | solution.py:220
  198.7 9.7 %collective-permute-start.37 = (bf16[512,128]{1,0:T(8,128)(2,1)S(1)}, bf16[512,128]{1,0:T(8,128)(2,1)S(1)}, u32[]{:S(2)}, u32[]{:S(2)}) collective-permute-start(bf16[512,128]{1,0:T(8,128)(2,1)S(1)} %get-tuple-element.198), channel_id=1, source_target_pairs={{0,12},{4,8},{8,4},{12,0},{1,13},{5,9},{9,5},{13,1},{2,14},{6,10},... | collective-permute-start | bytes 393224 | tf_op jit(solution)/shard_map/ppermute | solution.py:220
  203.6 4.1 %collective-permute-start.38 = (bf16[16,128]{1,0:T(8,128)(2,1)S(1)}, bf16[16,128]{1,0:T(8,128)(2,1)S(1)}, u32[]{:S(2)}, u32[]{:S(2)}) collective-permute-start(bf16[16,128]{1,0:T(8,128)(2,1)S(1)} %slice_bitcast_fusion.8), channel_id=1, source_target_pairs={{0,8},{4,12},{8,0},{12,4},{1,9},{5,13},{9,1},{13,5},{2,10},{6,14},... | collective-permute-start | bytes 12296 | tf_op jit(solution)/shard_map/ppermute | solution.py:220
  204.7 3.1 %collective-permute-start.39 = (bf16[16,128]{1,0:T(8,128)(2,1)S(1)}, bf16[16,128]{1,0:T(8,128)(2,1)S(1)}, u32[]{:S(2)}, u32[]{:S(2)}) collective-permute-start(bf16[16,128]{1,0:T(8,128)(2,1)S(1)} %slice_bitcast_fusion.8), channel_id=1, source_target_pairs={{0,12},{4,8},{8,4},{12,0},{1,13},{5,9},{9,5},{13,1},{2,14},{6,10},... | collective-permute-start | bytes 12296 | tf_op jit(solution)/shard_map/ppermute | solution.py:220
  205.7 2.1 %collective-permute-start.36 = (bf16[528,128]{1,0:T(8,128)(2,1)S(1)}, bf16[528,128]{1,0:T(8,128)(2,1)S(1)}, u32[]{:S(2)}, u32[]{:S(2)}) collective-permute-start(bf16[528,128]{1,0:T(8,128)(2,1)S(1)} %slice_bitcast_fusion.4), channel_id=1, source_target_pairs={{0,4},{4,0},{8,12},{12,8},{1,5},{5,1},{9,13},{13,9},{2,6},{6,2},{1... | collective-permute-start | bytes 405512 | tf_op jit(solution)/shard_map/ppermute | solution.py:220

commit v19 on v18

--- a/solution.py
+++ b/solution.py
@@ -266,7 +266,9 @@
     own_got = to_other(own_sent, 2)
     near_sent, own_got, pair_in = tied(near_sent, own_got, pair_in)
     near_got = to_other(near_sent, 2)
-    third, third_sent = core_sum(*product(flags, [pair_in], fisher))
+    third, *third_sent = product(flags, [pair_in], fisher)
+    third, second_edge = tied(third, second_edge)
+    third, third_sent = core_sum(third, *third_sent, cost=SOME)
     (near,) = scores_of((near, near_got), cost=SOME)
     counts = selected(chosen_ids)
     far_in, second_edge, third, third_sent, own, own_got, near, counts, chosen_ids, grads = tied(

time: 210 us -> 211 us (level)
    ppermute x27, waiting for transfers between devices: 60.3 us -> 57.7 us  [to_other(): return lax.ppermute(value, 'train', [(k, k ^ r) for k in range(4)])]
  transfers between devices with their start and end apart: 40 -> 40, of which waited for: 22 -> 21; matrix products, arithmetic and copies ran while one was open for 3% -> 3% of each run, Pallas kernels for 23% -> 23%
where the time goes in v19:
time: 211 us
  waiting for transfers between devices  77.6 us (37%)
  Pallas kernels  55.3 us (26%)
  starting transfers between devices  55.2 us (26%)
  local copies, waits for them, and re-layouts  15.3 us (7%)
  other arithmetic  6.09 us (3%)
    ppermute x27, waiting for transfers between devices, to_other(): return lax.ppermute(value, 'train', [(k, k ^ r) for k in range(4)])  57.7 us
    ppermute x13, starting transfers between devices, along(): return lax.ppermute(value, 'test', pairs)  36 us
    pallas_call x5, Pallas kernels, product(): pl.pallas_call(functools.partial(product_body, len(blocks)), in_specs=[pl...  33.7 us
    ppermute x13, waiting for transfers between devices, along(): return lax.ppermute(value, 'test', pairs)  19.9 us
    ppermute x27, starting transfers between devices, to_other(): return lax.ppermute(value, 'train', [(k, k ^ r) for k in range(4)])  19.2 us
    unnamed x38, local copies, waits for them, and re-layouts  14.1 us
    pallas_call x3, Pallas kernels, partial_scores(): pl.pallas_call(functools.partial(scores_body, [piece[:2] for piece in gra...  10.6 us
    pallas_call x5, Pallas kernels, fold(): pl.pallas_call(fold_body, in_specs=[pl.BlockSpec(memory_space=pltpu.SMEM)...  5.83 us
  transfers between devices with their start and end apart: 40, of which 21 were waited for; matrix products, arithmetic and copies ran while one was open for 3% of the time, Pallas kernels for 23%

profile of v19, /device:TPU:0, one launch (start us, length us, event | category | flops | bytes accessed | tf_op | source)
XLA Modules:
  0.0 210.6 jit_solution(483279072803656753)
XLA Ops:
  1.1 2.6 %collective-permute-start.5 = (bf16[512,2048]{1,0:T(8,128)(2,1)}, bf16[512,2048]{1,0:T(8,128)(2,1)S(1)}, u32[]{:S(2)}, u32[]{:S(2)}) collective-permute-start(bf16[512,2048]{1,0:T(8,128)(2,1)} %refs_0_.1), channel_id=1, source_target_pairs={{0,8},{4,12},{8,0},{12,4},{1,9},{5,13},{9,1},{13,5},{2,10},{6,14},... | collective-permute-start | bytes 6291464 | tf_op jit(solution)/shard_map/ppermute | solution.py:220
  3.7 1.6 collective-permute-start
  5.3 2.0 collective-permute-start.1
  7.4 1.6 copy-done.8
  9.0 2.0 hold.1
  11.0 1.3 copy-done.2
  12.3 1.4 copy-done.4
  13.8 3.4 %copy-done = bf16[2048,2048]{1,0:T(8,128)(2,1)S(1)} copy-done((bf16[2048,2048]{1,0:T(8,128)(2,1)S(1)}, bf16[2048,2048]{1,0:T(8,128)(2,1)}, u32[]{:S(2)}) %copy-start) | copy-done | bytes 8388632
  17.1 5.6 %product.5 = (f32[256,2048]{1,0:T(8,128)S(1)}, bf16[128,2048]{1,0:T(8,128)(2,1)S(1)}, bf16[128,2048]{1,0:T(8,128)(2,1)S(1)}) custom-call(s32[3]{0:T(128)S(1)} %pad_add_fusion.flags, bf16[512,2048]{1,0:T(8,128)(2,1)S(1)} %copy-done.11, bf16[2048,2048]{1,0:T(8,128)(2,1)S(1)} %copy-done), custom_call_target="tpu_custom_call" | custom-call | flops 1 | bytes 1 | tf_op jit(solution)/shard_map/product/pallas_call | solution.py:80
  23.3 26.8 %collective-permute-done.5.refs_4_.refs_6_.refs_0_ = bf16[512,2048]{1,0:T(8,128)(2,1)S(1)} collective-permute-done((bf16[512,2048]{1,0:T(8,128)(2,1)}, bf16[512,2048]{1,0:T(8,128)(2,1)S(1)}, u32[]{:S(2)}, u32[]{:S(2)}) %collective-permute-start.5) | collective-permute-done | bytes 2097184 | tf_op jit(solution)/shard_map/ppermute | solution.py:220
  50.9 1.8 fold.5
  53.0 1.5 collective-permute-done.7.refs_6_.refs_8_.refs_2_
  54.5 1.4 collective-permute-start.12
  55.9 2.0 collective-permute-start.8
  58.0 1.8 collective-permute-start.11
  59.7 8.3 %product.6 = (f32[256,2048]{1,0:T(8,128)S(1)}, bf16[128,2048]{1,0:T(8,128)(2,1)}, bf16[128,2048]{1,0:T(8,128)(2,1)}) custom-call(s32[3]{0:T(128)S(1)} %pad_add_fusion.flags, bf16[512,2048]{1,0:T(8,128)(2,1)} %collective-permute-done.1.refs_0_, bf16[512,2048]{1,0:T(8,128)(2,1)} %collective-permute-done.refs_1_.refs_0_, bf16[2048,2048]{1,0:T(8,128)(2,1)S(1)} %bitcast.115), custom_call_target="tpu_custom_call" | custom-call | flops 1 | bytes 1 | tf_op jit(solution)/shard_map/product/pallas_call | solution.py:80
  68.1 1.3 copy-done.9
  70.0 1.6 collective-permute-done.10.refs_1_
  71.6 0.7 collective-permute-done.9.refs_0_
  72.4 1.6 copy-done.10
  74.0 1.5 fold.6
  75.5 8.0 %collective-permute-done.11.refs_3_ = f32[128,2048]{1,0:T(8,128)} collective-permute-done((f32[128,2048]{1,0:T(8,128)}, f32[128,2048]{1,0:T(8,128)}, u32[]{:S(2)}, u32[]{:S(2)}) %collective-permute-start.11) | collective-permute-done | bytes 1048608 | tf_op jit(solution)/shard_map/ppermute | solution.py:220
  83.5 1.7 collective-permute-start.15
  85.2 3.4 %copy-done.1 = bf16[2048,2048]{1,0:T(8,128)(2,1)S(1)} copy-done((bf16[2048,2048]{1,0:T(8,128)(2,1)S(1)}, bf16[2048,2048]{1,0:T(8,128)(2,1)}, u32[]{:S(2)}) %copy-start.1) | copy-done | bytes 8388632
  88.6 6.9 %product.7 = (f32[256,2048]{1,0:T(8,128)S(1)}, bf16[128,2048]{1,0:T(8,128)(2,1)S(1)}, bf16[128,2048]{1,0:T(8,128)(2,1)S(1)}) custom-call(s32[3]{0:T(128)S(1)} %pad_add_fusion.flags, bf16[512,2048]{1,0:T(8,128)(2,1)} %collective-permute-done.refs_1_.refs_0_, bf16[2048,2048]{1,0:T(8,128)(2,1)S(1)} %copy-done.1), custom_call_target="tpu_custom_call" | custom-call | flops 1 | bytes 1 | tf_op jit(solution)/shard_map/product/pallas_call | solution.py:80
  96.1 1.7 convert_add_fusion.1
  97.8 2.4 %scores.3 = bf16[4,512,128]{2,1,0:T(8,128)(2,1)S(1)} custom-call(f32[128,2048]{1,0:T(8,128)S(1)} %get-tuple-element.119.refs_0_, bf16[128,2048]{1,0:T(8,128)(2,1)S(1)} %collective-permute-done.15.refs_1_, bf16[512,2048]{1,0:T(8,128)(2,1)S(1)} %copy-done.3, bf16[512,2048]{1,0:T(8,128)(2,1)S(1)} %copy-done.5, ...), custom_call_target="tpu_custom_call" | custom-call | flops 2000000000 | bytes 1048576 | tf_op jit(solution)/shard_map/scores/pallas_call | solution.py:144
  100.2 4.4 %collective-permute-done.12.refs_1_ = bf16[512,2048]{1,0:T(8,128)(2,1)} collective-permute-done((bf16[512,2048]{1,0:T(8,128)(2,1)}, bf16[512,2048]{1,0:T(8,128)(2,1)}, u32[]{:S(2)}, u32[]{:S(2)}) %collective-permute-start.12) | collective-permute-done | bytes 2097184 | tf_op jit(solution)/shard_map/ppermute | solution.py:217
  104.5 0.8 fold.7
  105.4 1.3 collective-permute-start.16
  106.7 7.3 %product.8 = (f32[256,2048]{1,0:T(8,128)S(1)}, bf16[128,2048]{1,0:T(8,128)(2,1)S(1)}, bf16[128,2048]{1,0:T(8,128)(2,1)S(1)}) custom-call(s32[3]{0:T(128)S(1)} %pad_add_fusion.flags, bf16[512,2048]{1,0:T(8,128)(2,1)} %collective-permute-done.8.refs_0_, bf16[512,2048]{1,0:T(8,128)(2,1)} %collective-permute-done.12.refs_1_, bf16[2048,2048]{1,0:T(8,128)(2,1)S(1)} %bitcast.117), custom_call_target="tpu_custom_call" | custom-call | flops 1 | bytes 1 | tf_op jit(solution)/shard_map/product/pallas_call | solution.py:80
  114.6 1.4 collective-permute-done.18.refs_0_
  116.0 0.7 collective-permute-done.19.refs_1_
  116.8 0.8 fold.8
  117.6 1.8 collective-permute-start.20
  119.4 7.2 %collective-permute-start.21 = (bf16[4,512,128]{2,1,0:T(8,128)(2,1)S(1)}, bf16[4,512,128]{2,1,0:T(8,128)(2,1)S(1)}, u32[]{:S(2)}, u32[]{:S(2)}) collective-permute-start(bf16[4,512,128]{2,1,0:T(8,128)(2,1)S(1)} %scores.3), channel_id=1, source_target_pairs={{0,1},{3,2},{4,5},{7,6},{8,9},{11,10},{12,13},{15,14},{16,17},{19,... | collective-permute-start | bytes 1572872 | tf_op jit(solution)/shard_map/ppermute | solution.py:217
  126.7 0.9 collective-permute-start.22
  128.1 4.3 %collective-permute-done.20.refs_1_ = bf16[128,2048]{1,0:T(8,128)(2,1)S(1)} collective-permute-done((bf16[128,2048]{1,0:T(8,128)(2,1)S(1)}, bf16[128,2048]{1,0:T(8,128)(2,1)S(1)}, u32[]{:S(2)}, u32[]{:S(2)}) %collective-permute-start.20) | collective-permute-done | bytes 524320 | tf_op jit(solution)/shard_map/ppermute | solution.py:220
  132.4 5.4 %collective-permute-done.21 = bf16[4,512,128]{2,1,0:T(8,128)(2,1)S(1)} collective-permute-done((bf16[4,512,128]{2,1,0:T(8,128)(2,1)S(1)}, bf16[4,512,128]{2,1,0:T(8,128)(2,1)S(1)}, u32[]{:S(2)}, u32[]{:S(2)}) %collective-permute-start.21) | collective-permute-done | bytes 524320 | tf_op jit(solution)/shard_map/ppermute | solution.py:217
  137.8 2.4 %scores.5 = bf16[4,512,128]{2,1,0:T(8,128)(2,1)S(1)} custom-call(f32[128,2048]{1,0:T(8,128)S(1)} %get-tuple-element.150.refs_0_, bf16[128,2048]{1,0:T(8,128)(2,1)S(1)} %collective-permute-done.20.refs_1_, bf16[512,2048]{1,0:T(8,128)(2,1)S(1)} %copy-done.3, bf16[512,2048]{1,0:T(8,128)(2,1)S(1)} %copy-done.5, ...), custom_call_target="tpu_custom_call" | custom-call | flops 1 | bytes 1 | tf_op jit(solution)/shard_map/scores/pallas_call | solution.py:144
  140.9 4.5 %collective-permute-start.24 = (s32[512,16]{0,1:T(8,128)S(1)}, s32[512,16]{0,1:T(8,128)S(1)}, u32[]{:S(2)}, u32[]{:S(2)}) collective-permute-start(s32[512,16]{0,1:T(8,128)S(1)} %copy-done.14), channel_id=1, source_target_pairs={{0,3},{3,0},{4,7},{7,4},{8,11},{11,8},{12,15},{15,12},{16,19},{19,... | collective-permute-start | bytes 98312 | tf_op jit(solution)/shard_map/ppermute | solution.py:217
  145.5 5.8 %scores.4 = (f32[4,512,128]{2,1,0:T(8,128)S(1)}, f32[4,512,128]{2,1,0:T(8,128)S(1)}) custom-call(f32[128,2048]{1,0:T(8,128)S(1)} %get-tuple-element.128.refs_0_, bf16[128,2048]{1,0:T(8,128)(2,1)S(1)} %collective-permute-done.17.refs_1_, f32[128,2048]{1,0:T(8,128)S(1)} %copy-done.13, f32[128,2048]{1,0:T(8,128)} %collective-permute-done.11.refs_3_, ...), custom_call_target="tpu_custom_call" | custom-call | flops 1 | bytes 1 | tf_op jit(solution)/shard_map/scores/pallas_call | solution.py:144
  151.3 6.8 %collective-permute-done.16.refs_0_ = bf16[512,2048]{1,0:T(8,128)(2,1)S(1)} collective-permute-done((bf16[512,2048]{1,0:T(8,128)(2,1)}, bf16[512,2048]{1,0:T(8,128)(2,1)S(1)}, u32[]{:S(2)}, u32[]{:S(2)}) %collective-permute-start.16) | collective-permute-done | bytes 2097184 | tf_op jit(solution)/shard_map/ppermute | solution.py:217
  158.1 5.6 %product.9 = (f32[256,2048]{1,0:T(8,128)S(1)}, bf16[128,2048]{1,0:T(8,128)(2,1)S(1)}, bf16[128,2048]{1,0:T(8,128)(2,1)S(1)}) custom-call(s32[3]{0:T(128)S(1)} %pad_add_fusion.flags, bf16[512,2048]{1,0:T(8,128)(2,1)S(1)} %collective-permute-done.16.refs_0_, bf16[2048,2048]{1,0:T(8,128)(2,1)S(1)} %bitcast.117), custom_call_target="tpu_custom_call" | custom-call | flops 1 | bytes 1 | tf_op jit(solution)/shard_map/product/pallas_call | solution.py:80
  164.3 1.4 collective-permute-done.25.refs_0_
  166.4 0.8 fold.9
  167.3 1.6 collective-permute-start.27
  168.9 1.3 collective-permute-start.29
  170.2 5.5 %collective-permute-start.28 = (bf16[4,512,128]{2,1,0:T(8,128)(2,1)S(1)}, bf16[4,512,128]{2,1,0:T(8,128)(2,1)S(1)}, u32[]{:S(2)}, u32[]{:S(2)}) collective-permute-start(bf16[4,512,128]{2,1,0:T(8,128)(2,1)S(1)} %scores.5), channel_id=1, source_target_pairs={{0,2},{3,1},{4,6},{7,5},{8,10},{11,9},{12,14},{15,13},{16,18},{19,... | collective-permute-start | bytes 1572872 | tf_op jit(solution)/shard_map/ppermute | solution.py:217
  175.7 1.7 convert_add_fusion.counts
  177.4 3.9 %collective-permute-done.27.got = bf16[128,2048]{1,0:T(8,128)(2,1)S(1)} collective-permute-done((bf16[128,2048]{1,0:T(8,128)(2,1)S(1)}, bf16[128,2048]{1,0:T(8,128)(2,1)S(1)}, u32[]{:S(2)}, u32[]{:S(2)}) %collective-permute-start.27) | collective-permute-done | bytes 524320 | tf_op jit(solution)/shard_map/ppermute | solution.py:220
  181.3 1.3 last_scores.2
  182.6 1.9 last_scores.3
  184.5 2.0 collective-permute-done.28
  186.6 3.4 %collective-permute-start.34 = (bf16[2,512,128]{2,1,0:T(8,128)(2,1)S(1)}, bf16[2,512,128]{2,1,0:T(8,128)(2,1)}, u32[]{:S(2)}, u32[]{:S(2)}) collective-permute-start(bf16[2,512,128]{2,1,0:T(8,128)(2,1)S(1)} %get-tuple-element.181), channel_id=1, source_target_pairs={{0,3},{3,0},{4,7},{7,4},{8,11},{11,8},{12,15},{15,12},{16,19},{19,... | collective-permute-start | bytes 786440 | tf_op jit(solution)/shard_map/ppermute | solution.py:217
  191.1 1.6 collective-permute-start.32
  192.7 4.2 %collective-permute-start.33 = (bf16[2,528,128]{2,1,0:T(8,128)(2,1)S(1)}, bf16[2,528,128]{2,1,0:T(8,128)(2,1)S(1)}, u32[]{:S(2)}, u32[]{:S(2)}) collective-permute-start(bf16[2,528,128]{2,1,0:T(8,128)(2,1)S(1)} %get-tuple-element.180), channel_id=1, source_target_pairs={{0,3},{3,0},{4,7},{7,4},{8,11},{11,8},{12,15},{15,12},{16,19},{19,... | collective-permute-start | bytes 811016 | tf_op jit(solution)/shard_map/ppermute | solution.py:217
  197.2 1.0 slice_bitcast_fusion.5
  198.8 1.1 collective-permute-done.30
  199.9 3.8 %collective-permute-done.32 = f32[520,128]{1,0:T(8,128)S(1)} collective-permute-done((f32[520,128]{1,0:T(8,128)S(1)}, f32[520,128]{1,0:T(8,128)S(1)}, u32[]{:S(2)}, u32[]{:S(2)}) %collective-permute-start.32) | collective-permute-done | bytes 266272 | tf_op jit(solution)/shard_map/ppermute | solution.py:220
  203.8 1.0 collective-permute-done.33
  205.4 1.9 collective-permute-start.39
  207.4 1.3 collective-permute-done.38
  209.4 1.1 slice_add_fusion
  (97 shorter events, 10.3 us)
Async XLA Ops:
  0.6 6.8 %collective-permute-start.2 = (bf16[512,2048]{1,0:T(8,128)(2,1)}, bf16[512,2048]{1,0:T(8,128)(2,1)}, u32[]{:S(2)}, u32[]{:S(2)}) collective-permute-start(bf16[512,2048]{1,0:T(8,128)(2,1)} %refs_0_.1), channel_id=1, source_target_pairs={{0,4},{4,0},{8,12},{12,8},{1,5},{5,1},{9,13},{13,9},{2,6},{6,2},{1... | collective-permute-start | bytes 6291464 | tf_op jit(solution)/shard_map/ppermute | solution.py:220
  1.1 49.0 %collective-permute-start.5 = (bf16[512,2048]{1,0:T(8,128)(2,1)}, bf16[512,2048]{1,0:T(8,128)(2,1)S(1)}, u32[]{:S(2)}, u32[]{:S(2)}) collective-permute-start(bf16[512,2048]{1,0:T(8,128)(2,1)} %refs_0_.1), channel_id=1, source_target_pairs={{0,8},{4,12},{8,0},{12,4},{1,9},{5,13},{9,1},{13,5},{2,10},{6,14},... | collective-permute-start | bytes 6291464 | tf_op jit(solution)/shard_map/ppermute | solution.py:220
  3.7 49.0 %collective-permute-start = (bf16[512,2048]{1,0:T(8,128)(2,1)}, bf16[512,2048]{1,0:T(8,128)(2,1)}, u32[]{:S(2)}, u32[]{:S(2)}) collective-permute-start(bf16[512,2048]{1,0:T(8,128)(2,1)} %refs_0_.2), channel_id=1, source_target_pairs={{0,1},{1,0},{2,3},{3,2},{4,5},{5,4},{6,7},{7,6},{8,9},{9,8},{10,11... | collective-permute-start | bytes 6291464 | tf_op jit(solution)/shard_map/ppermute | solution.py:217
  5.3 47.4 %collective-permute-start.1 = (bf16[512,2048]{1,0:T(8,128)(2,1)}, bf16[512,2048]{1,0:T(8,128)(2,1)}, u32[]{:S(2)}, u32[]{:S(2)}) collective-permute-start(bf16[512,2048]{1,0:T(8,128)(2,1)} %refs_0_.2), channel_id=1, source_target_pairs={{1,2},{2,1},{5,6},{6,5},{9,10},{10,9},{13,14},{14,13},{17,18},{18,... | collective-permute-start | bytes 6291464 | tf_op jit(solution)/shard_map/ppermute | solution.py:217
  7.4 1.6 copy-start.8
  9.0 4.8 %copy-start.11 = (bf16[512,2048]{1,0:T(8,128)(2,1)S(1)}, bf16[512,2048]{1,0:T(8,128)(2,1)}, u32[]{:S(2)}) copy-start(bf16[512,2048]{1,0:T(8,128)(2,1)} %refs_0_.2) | copy-start | bytes 6291460
  11.0 1.3 copy-start.2
  12.3 1.4 copy-start.4
  13.8 3.4 %copy-start = (bf16[2048,2048]{1,0:T(8,128)(2,1)S(1)}, bf16[2048,2048]{1,0:T(8,128)(2,1)}, u32[]{:S(2)}) copy-start(bf16[2048,2048]{1,0:T(8,128)(2,1)} %refs_1_.5) | copy-start | bytes 25165828
  22.7 27.7 %collective-permute-start.3 = (bf16[128,2048]{1,0:T(8,128)(2,1)S(1)}, bf16[128,2048]{1,0:T(8,128)(2,1)S(1)}, u32[]{:S(2)}, u32[]{:S(2)}) collective-permute-start(bf16[128,2048]{1,0:T(8,128)(2,1)S(1)} %get-tuple-element.96), channel_id=1, source_target_pairs={{0,4},{4,0},{8,12},{12,8},{1,5},{5,1},{9,13},{13,9},{2,6},{6,2},{1... | collective-permute-start | bytes 1572872 | tf_op jit(solution)/shard_map/ppermute | solution.py:220
  22.8 28.1 %collective-permute-start.4 = (bf16[128,2048]{1,0:T(8,128)(2,1)S(1)}, bf16[128,2048]{1,0:T(8,128)(2,1)S(1)}, u32[]{:S(2)}, u32[]{:S(2)}) collective-permute-start(bf16[128,2048]{1,0:T(8,128)(2,1)S(1)} %get-tuple-element.97), channel_id=1, source_target_pairs={{0,4},{4,0},{8,12},{12,8},{1,5},{5,1},{9,13},{13,9},{2,6},{6,2},{1... | collective-permute-start | bytes 1572872 | tf_op jit(solution)/shard_map/ppermute | solution.py:220
  50.3 2.7 %collective-permute-start.6 = (bf16[256,2048]{1,0:T(8,128)(2,1)S(1)}, bf16[256,2048]{1,0:T(8,128)(2,1)S(1)}, u32[]{:S(2)}, u32[]{:S(2)}) collective-permute-start(bf16[256,2048]{1,0:T(8,128)(2,1)S(1)} %get-tuple-element.185), channel_id=1, source_target_pairs={{0,4},{4,0},{8,12},{12,8},{1,5},{5,1},{9,13},{13,9},{2,6},{6,2},{1... | collective-permute-start | bytes 3145736 | tf_op jit(solution)/shard_map/ppermute | solution.py:220
  50.4 4.1 %collective-permute-start.7 = (bf16[256,2048]{1,0:T(8,128)(2,1)S(1)}, bf16[256,2048]{1,0:T(8,128)(2,1)S(1)}, u32[]{:S(2)}, u32[]{:S(2)}) collective-permute-start(bf16[256,2048]{1,0:T(8,128)(2,1)S(1)} %get-tuple-element.184), channel_id=1, source_target_pairs={{0,4},{4,0},{8,12},{12,8},{1,5},{5,1},{9,13},{13,9},{2,6},{6,2},{1... | collective-permute-start | bytes 3145736 | tf_op jit(solution)/shard_map/ppermute | solution.py:220
  50.9 8.8 %slice-start = ((s8[8388608]{0:T(1024)(128)(4,1)}), s8[4194304]{0:T(1024)(128)(4,1)S(1)}, s32[]{:S(2)}) async-start(s8[8388608]{0:T(1024)(128)(4,1)} %bitcast.114), calls=%async_computation | async-start | bytes 8388608
  50.9 8.8 %slice-start.1 = ((s8[8388608]{0:T(1024)(128)(4,1)}), s8[4194304]{0:T(1024)(128)(4,1)S(1)}, s32[]{:S(2)}) async-start(s8[8388608]{0:T(1024)(128)(4,1)} %bitcast.114), calls=%async_computation.1 | async-start | bytes 8388608
  52.7 15.4 %copy-start.12 = (f32[128,2048]{1,0:T(8,128)}, f32[128,2048]{1,0:T(8,128)S(1)}, u32[]{:S(2)}) copy-start(f32[128,2048]{1,0:T(8,128)S(1)} %get-tuple-element.130.refs_2_) | copy-start | bytes 3145732
  54.5 13.5 %copy-start.6 = (bf16[256,2048]{1,0:T(8,128)(2,1)}, bf16[256,2048]{1,0:T(8,128)(2,1)S(1)}, u32[]{:S(2)}) copy-start(bf16[256,2048]{1,0:T(8,128)(2,1)S(1)} %collective-permute-done.7.refs_6_.refs_8_.refs_2_) | copy-start | bytes 3145732
  54.5 15.5 %copy-start.14 = (s32[512,16]{0,1:T(8,128)S(1)}, s32[512,16]{0,1:T(8,128)}, u32[]{:S(2)}) copy-start(s32[512,16]{0,1:T(8,128)} %param.7) | copy-start | bytes 98308
  54.5 50.0 %collective-permute-start.12 = (bf16[512,2048]{1,0:T(8,128)(2,1)}, bf16[512,2048]{1,0:T(8,128)(2,1)}, u32[]{:S(2)}, u32[]{:S(2)}) collective-permute-start(bf16[512,2048]{1,0:T(8,128)(2,1)} %collective-permute-done.1.refs_0_), channel_id=1, source_target_pairs={{1,0},{2,3},{5,4},{6,7},{9,8},{10,11},{13,12},{14,15},{17,16},{18,... | collective-permute-start | bytes 6291464 | tf_op jit(solution)/shard_map/ppermute | solution.py:217
  55.9 49.4 %collective-permute-start.8 = (bf16[512,2048]{1,0:T(8,128)(2,1)}, bf16[512,2048]{1,0:T(8,128)(2,1)}, u32[]{:S(2)}, u32[]{:S(2)}) collective-permute-start(bf16[512,2048]{1,0:T(8,128)(2,1)} %collective-permute-done.refs_1_.refs_0_), channel_id=1, source_target_pairs={{1,2},{2,1},{5,6},{6,5},{9,10},{10,9},{13,14},{14,13},{17,18},{18,... | collective-permute-start | bytes 6291464 | tf_op jit(solution)/shard_map/ppermute | solution.py:217
  58.0 25.5 %collective-permute-start.11 = (f32[128,2048]{1,0:T(8,128)}, f32[128,2048]{1,0:T(8,128)}, u32[]{:S(2)}, u32[]{:S(2)}) collective-permute-start(f32[128,2048]{1,0:T(8,128)} %get-tuple-element.108), channel_id=1, source_target_pairs={{0,8},{4,12},{8,0},{12,4},{1,9},{5,13},{9,1},{13,5},{2,10},{6,14},... | collective-permute-start | bytes 3145736 | tf_op jit(solution)/shard_map/ppermute | solution.py:220
  68.1 1.3 copy-start.9
  69.4 2.3 %collective-permute-start.10 = (bf16[128,2048]{1,0:T(8,128)(2,1)}, bf16[128,2048]{1,0:T(8,128)(2,1)}, u32[]{:S(2)}, u32[]{:S(2)}) collective-permute-start(bf16[128,2048]{1,0:T(8,128)(2,1)} %get-tuple-element.106), channel_id=1, source_target_pairs={{0,4},{4,0},{8,12},{12,8},{1,5},{5,1},{9,13},{13,9},{2,6},{6,2},{1... | collective-permute-start | bytes 1572872 | tf_op jit(solution)/shard_map/ppermute | solution.py:220
  69.4 3.0 %collective-permute-start.9 = (bf16[128,2048]{1,0:T(8,128)(2,1)}, bf16[128,2048]{1,0:T(8,128)(2,1)}, u32[]{:S(2)}, u32[]{:S(2)}) collective-permute-start(bf16[128,2048]{1,0:T(8,128)(2,1)} %get-tuple-element.105), channel_id=1, source_target_pairs={{0,4},{4,0},{8,12},{12,8},{1,5},{5,1},{9,13},{13,9},{2,6},{6,2},{1... | collective-permute-start | bytes 1572872 | tf_op jit(solution)/shard_map/ppermute | solution.py:220
  72.4 1.6 copy-start.10
  83.5 14.2 %collective-permute-start.15 = (bf16[128,2048]{1,0:T(8,128)(2,1)S(1)}, bf16[128,2048]{1,0:T(8,128)(2,1)S(1)}, u32[]{:S(2)}, u32[]{:S(2)}) collective-permute-start(bf16[128,2048]{1,0:T(8,128)(2,1)S(1)} %get-tuple-element.120), channel_id=1, source_target_pairs={{0,8},{4,12},{8,0},{12,4},{1,9},{5,13},{9,1},{13,5},{2,10},{6,14},... | collective-permute-start | bytes 1572872 | tf_op jit(solution)/shard_map/ppermute | solution.py:220
  85.2 3.4 %copy-start.1 = (bf16[2048,2048]{1,0:T(8,128)(2,1)S(1)}, bf16[2048,2048]{1,0:T(8,128)(2,1)}, u32[]{:S(2)}) copy-start(bf16[2048,2048]{1,0:T(8,128)(2,1)} %refs_1_.5) | copy-start | bytes 25165828
  88.6 9.1 %copy-start.3 = (bf16[512,2048]{1,0:T(8,128)(2,1)S(1)}, bf16[512,2048]{1,0:T(8,128)(2,1)}, u32[]{:S(2)}) copy-start(bf16[512,2048]{1,0:T(8,128)(2,1)} %copy-done.2) | copy-start | bytes 6291460
  88.6 9.1 %copy-start.5 = (bf16[512,2048]{1,0:T(8,128)(2,1)S(1)}, bf16[512,2048]{1,0:T(8,128)(2,1)}, u32[]{:S(2)}) copy-start(bf16[512,2048]{1,0:T(8,128)(2,1)} %copy-done.4) | copy-start | bytes 6291460
  88.6 9.2 %copy-start.7 = (bf16[256,2048]{1,0:T(8,128)(2,1)S(1)}, bf16[256,2048]{1,0:T(8,128)(2,1)}, u32[]{:S(2)}) copy-start(bf16[256,2048]{1,0:T(8,128)(2,1)} %copy-done.6) | copy-start | bytes 3145732
  95.5 9.0 %collective-permute-start.13 = (bf16[128,2048]{1,0:T(8,128)(2,1)S(1)}, bf16[128,2048]{1,0:T(8,128)(2,1)S(1)}, u32[]{:S(2)}, u32[]{:S(2)}) collective-permute-start(bf16[128,2048]{1,0:T(8,128)(2,1)S(1)} %get-tuple-element.113), channel_id=1, source_target_pairs={{0,4},{4,0},{8,12},{12,8},{1,5},{5,1},{9,13},{13,9},{2,6},{6,2},{1... | collective-permute-start | bytes 1572872 | tf_op jit(solution)/shard_map/ppermute | solution.py:220
  95.6 9.0 %collective-permute-start.14 = (bf16[128,2048]{1,0:T(8,128)(2,1)S(1)}, bf16[128,2048]{1,0:T(8,128)(2,1)S(1)}, u32[]{:S(2)}, u32[]{:S(2)}) collective-permute-start(bf16[128,2048]{1,0:T(8,128)(2,1)S(1)} %get-tuple-element.114), channel_id=1, source_target_pairs={{0,4},{4,0},{8,12},{12,8},{1,5},{5,1},{9,13},{13,9},{2,6},{6,2},{1... | collective-permute-start | bytes 1572872 | tf_op jit(solution)/shard_map/ppermute | solution.py:220
  97.7 8.9 %slice-start.2 = ((s8[8388608]{0:T(1024)(128)(4,1)}), s8[4194304]{0:T(1024)(128)(4,1)S(1)}, s32[]{:S(2)}) async-start(s8[8388608]{0:T(1024)(128)(4,1)} %bitcast.116), calls=%async_computation.2 | async-start | bytes 8388608
  97.8 8.9 %slice-start.3 = ((s8[8388608]{0:T(1024)(128)(4,1)}), s8[4194304]{0:T(1024)(128)(4,1)S(1)}, s32[]{:S(2)}) async-start(s8[8388608]{0:T(1024)(128)(4,1)} %bitcast.116), calls=%async_computation.3 | async-start | bytes 8388608
  105.4 52.7 %collective-permute-start.16 = (bf16[512,2048]{1,0:T(8,128)(2,1)}, bf16[512,2048]{1,0:T(8,128)(2,1)S(1)}, u32[]{:S(2)}, u32[]{:S(2)}) collective-permute-start(bf16[512,2048]{1,0:T(8,128)(2,1)} %collective-permute-done.8.refs_0_), channel_id=1, source_target_pairs={{1,0},{2,3},{5,4},{6,7},{9,8},{10,11},{13,12},{14,15},{17,16},{18,... | collective-permute-start | bytes 6291464 | tf_op jit(solution)/shard_map/ppermute | solution.py:217
  114.0 2.0 collective-permute-start.18
  114.1 2.6 %collective-permute-start.19 = (bf16[128,2048]{1,0:T(8,128)(2,1)S(1)}, bf16[128,2048]{1,0:T(8,128)(2,1)S(1)}, u32[]{:S(2)}, u32[]{:S(2)}) collective-permute-start(bf16[128,2048]{1,0:T(8,128)(2,1)S(1)} %get-tuple-element.141), channel_id=1, source_target_pairs={{0,4},{4,0},{8,12},{12,8},{1,5},{5,1},{9,13},{13,9},{2,6},{6,2},{1... | collective-permute-start | bytes 1572872 | tf_op jit(solution)/shard_map/ppermute | solution.py:220
  117.6 27.9 %copy-start.13 = (f32[128,2048]{1,0:T(8,128)S(1)}, f32[128,2048]{1,0:T(8,128)}, u32[]{:S(2)}) copy-start(f32[128,2048]{1,0:T(8,128)} %copy-done.12) | copy-start | bytes 3145732
  117.6 14.8 %collective-permute-start.20 = (bf16[128,2048]{1,0:T(8,128)(2,1)S(1)}, bf16[128,2048]{1,0:T(8,128)(2,1)S(1)}, u32[]{:S(2)}, u32[]{:S(2)}) collective-permute-start(bf16[128,2048]{1,0:T(8,128)(2,1)S(1)} %get-tuple-element.145), channel_id=1, source_target_pairs={{0,8},{4,12},{8,0},{12,4},{1,9},{5,13},{9,1},{13,5},{2,10},{6,14},... | collective-permute-start | bytes 1572872 | tf_op jit(solution)/shard_map/ppermute | solution.py:220
  119.4 18.4 %collective-permute-start.21 = (bf16[4,512,128]{2,1,0:T(8,128)(2,1)S(1)}, bf16[4,512,128]{2,1,0:T(8,128)(2,1)S(1)}, u32[]{:S(2)}, u32[]{:S(2)}) collective-permute-start(bf16[4,512,128]{2,1,0:T(8,128)(2,1)S(1)} %scores.3), channel_id=1, source_target_pairs={{0,1},{3,2},{4,5},{7,6},{8,9},{11,10},{12,13},{15,14},{16,17},{19,... | collective-permute-start | bytes 1572872 | tf_op jit(solution)/shard_map/ppermute | solution.py:217
  126.7 11.2 %collective-permute-start.22 = (bf16[4,512,128]{2,1,0:T(8,128)(2,1)S(1)}, bf16[4,512,128]{2,1,0:T(8,128)(2,1)S(1)}, u32[]{:S(2)}, u32[]{:S(2)}) collective-permute-start(bf16[4,512,128]{2,1,0:T(8,128)(2,1)S(1)} %scores.3), channel_id=1, source_target_pairs={{1,2},{2,1},{5,6},{6,5},{9,10},{10,9},{13,14},{14,13},{17,18},{18,... | collective-permute-start | bytes 1572872 | tf_op jit(solution)/shard_map/ppermute | solution.py:217
  127.5 17.9 %collective-permute-start.17 = (bf16[128,2048]{1,0:T(8,128)(2,1)S(1)}, bf16[128,2048]{1,0:T(8,128)(2,1)S(1)}, u32[]{:S(2)}, u32[]{:S(2)}) collective-permute-start(bf16[128,2048]{1,0:T(8,128)(2,1)S(1)} %get-tuple-element.129), channel_id=1, source_target_pairs={{0,8},{4,12},{8,0},{12,4},{1,9},{5,13},{9,1},{13,5},{2,10},{6,14},... | collective-permute-start | bytes 1572872 | tf_op jit(solution)/shard_map/ppermute | solution.py:220
  140.2 11.1 %collective-permute-start.23 = (bf16[4,512,128]{2,1,0:T(8,128)(2,1)S(1)}, bf16[4,512,128]{2,1,0:T(8,128)(2,1)S(1)}, u32[]{:S(2)}, u32[]{:S(2)}) collective-permute-start(bf16[4,512,128]{2,1,0:T(8,128)(2,1)S(1)} %scores.5), channel_id=1, source_target_pairs={{1,2},{2,1},{5,6},{6,5},{9,10},{10,9},{13,14},{14,13},{17,18},{18,... | collective-permute-start | bytes 1572872 | tf_op jit(solution)/shard_map/ppermute | solution.py:217
  140.9 10.4 %collective-permute-start.24 = (s32[512,16]{0,1:T(8,128)S(1)}, s32[512,16]{0,1:T(8,128)S(1)}, u32[]{:S(2)}, u32[]{:S(2)}) collective-permute-start(s32[512,16]{0,1:T(8,128)S(1)} %copy-done.14), channel_id=1, source_target_pairs={{0,3},{3,0},{4,7},{7,4},{8,11},{11,8},{12,15},{15,12},{16,19},{19,... | collective-permute-start | bytes 98312 | tf_op jit(solution)/shard_map/ppermute | solution.py:217
  163.7 2.0 collective-permute-start.25
  163.8 2.6 %collective-permute-start.26 = (bf16[128,2048]{1,0:T(8,128)(2,1)S(1)}, bf16[128,2048]{1,0:T(8,128)(2,1)S(1)}, u32[]{:S(2)}, u32[]{:S(2)}) collective-permute-start(bf16[128,2048]{1,0:T(8,128)(2,1)S(1)} %get-tuple-element.160), channel_id=1, source_target_pairs={{0,4},{4,0},{8,12},{12,8},{1,5},{5,1},{9,13},{13,9},{2,6},{6,2},{1... | collective-permute-start | bytes 1572872 | tf_op jit(solution)/shard_map/ppermute | solution.py:220
  167.3 14.0 %collective-permute-start.27 = (bf16[128,2048]{1,0:T(8,128)(2,1)S(1)}, bf16[128,2048]{1,0:T(8,128)(2,1)S(1)}, u32[]{:S(2)}, u32[]{:S(2)}) collective-permute-start(bf16[128,2048]{1,0:T(8,128)(2,1)S(1)} %get-tuple-element.165), channel_id=1, source_target_pairs={{0,8},{4,12},{8,0},{12,4},{1,9},{5,13},{9,1},{13,5},{2,10},{6,14},... | collective-permute-start | bytes 1572872 | tf_op jit(solution)/shard_map/ppermute | solution.py:220
  168.9 15.6 %collective-permute-start.29 = (bf16[4,512,128]{2,1,0:T(8,128)(2,1)S(1)}, bf16[4,512,128]{2,1,0:T(8,128)(2,1)S(1)}, u32[]{:S(2)}, u32[]{:S(2)}) collective-permute-start(bf16[4,512,128]{2,1,0:T(8,128)(2,1)S(1)} %add_convert_fusion), channel_id=1, source_target_pairs={{1,0},{2,3},{5,4},{6,7},{9,8},{10,11},{13,12},{14,15},{17,16},{18,... | collective-permute-start | bytes 1572872 | tf_op jit(solution)/shard_map/ppermute | solution.py:217
  170.2 16.3 %collective-permute-start.28 = (bf16[4,512,128]{2,1,0:T(8,128)(2,1)S(1)}, bf16[4,512,128]{2,1,0:T(8,128)(2,1)S(1)}, u32[]{:S(2)}, u32[]{:S(2)}) collective-permute-start(bf16[4,512,128]{2,1,0:T(8,128)(2,1)S(1)} %scores.5), channel_id=1, source_target_pairs={{0,2},{3,1},{4,6},{7,5},{8,10},{11,9},{12,14},{15,13},{16,18},{19,... | collective-permute-start | bytes 1572872 | tf_op jit(solution)/shard_map/ppermute | solution.py:217
  186.6 10.7 %collective-permute-start.34 = (bf16[2,512,128]{2,1,0:T(8,128)(2,1)S(1)}, bf16[2,512,128]{2,1,0:T(8,128)(2,1)}, u32[]{:S(2)}, u32[]{:S(2)}) collective-permute-start(bf16[2,512,128]{2,1,0:T(8,128)(2,1)S(1)} %get-tuple-element.181), channel_id=1, source_target_pairs={{0,3},{3,0},{4,7},{7,4},{8,11},{11,8},{12,15},{15,12},{16,19},{19,... | collective-permute-start | bytes 786440 | tf_op jit(solution)/shard_map/ppermute | solution.py:217
  190.5 9.4 %collective-permute-start.30 = (f32[520,128]{1,0:T(8,128)S(1)}, f32[520,128]{1,0:T(8,128)S(1)}, u32[]{:S(2)}, u32[]{:S(2)}) collective-permute-start(f32[520,128]{1,0:T(8,128)S(1)} %get-tuple-element.236), channel_id=1, source_target_pairs={{0,8},{4,12},{8,0},{12,4},{1,9},{5,13},{9,1},{13,5},{2,10},{6,14},... | collective-permute-start | bytes 798728 | tf_op jit(solution)/shard_map/ppermute | solution.py:220
  191.1 8.8 %collective-permute-start.31 = (f32[520,128]{1,0:T(8,128)S(1)}, f32[520,128]{1,0:T(8,128)S(1)}, u32[]{:S(2)}, u32[]{:S(2)}) collective-permute-start(f32[520,128]{1,0:T(8,128)S(1)} %get-tuple-element.237), channel_id=1, source_target_pairs={{0,4},{4,0},{8,12},{12,8},{1,5},{5,1},{9,13},{13,9},{2,6},{6,2},{1... | collective-permute-start | bytes 798728 | tf_op jit(solution)/shard_map/ppermute | solution.py:220
  191.1 12.6 %collective-permute-start.32 = (f32[520,128]{1,0:T(8,128)S(1)}, f32[520,128]{1,0:T(8,128)S(1)}, u32[]{:S(2)}, u32[]{:S(2)}) collective-permute-start(f32[520,128]{1,0:T(8,128)S(1)} %get-tuple-element.238), channel_id=1, source_target_pairs={{0,12},{4,8},{8,4},{12,0},{1,13},{5,9},{9,5},{13,1},{2,14},{6,10},... | collective-permute-start | bytes 798728 | tf_op jit(solution)/shard_map/ppermute | solution.py:220
  192.7 12.1 %collective-permute-start.33 = (bf16[2,528,128]{2,1,0:T(8,128)(2,1)S(1)}, bf16[2,528,128]{2,1,0:T(8,128)(2,1)S(1)}, u32[]{:S(2)}, u32[]{:S(2)}) collective-permute-start(bf16[2,528,128]{2,1,0:T(8,128)(2,1)S(1)} %get-tuple-element.180), channel_id=1, source_target_pairs={{0,3},{3,0},{4,7},{7,4},{8,11},{11,8},{12,15},{15,12},{16,19},{19,... | collective-permute-start | bytes 811016 | tf_op jit(solution)/shard_map/ppermute | solution.py:217
  198.2 11.1 %collective-permute-start.35 = (bf16[512,128]{1,0:T(8,128)(2,1)S(1)}, bf16[512,128]{1,0:T(8,128)(2,1)S(1)}, u32[]{:S(2)}, u32[]{:S(2)}) collective-permute-start(bf16[512,128]{1,0:T(8,128)(2,1)S(1)} %get-tuple-element.203), channel_id=1, source_target_pairs={{0,8},{4,12},{8,0},{12,4},{1,9},{5,13},{9,1},{13,5},{2,10},{6,14},... | collective-permute-start | bytes 393224 | tf_op jit(solution)/shard_map/ppermute | solution.py:220
  199.9 9.4 %collective-permute-start.37 = (bf16[512,128]{1,0:T(8,128)(2,1)S(1)}, bf16[512,128]{1,0:T(8,128)(2,1)S(1)}, u32[]{:S(2)}, u32[]{:S(2)}) collective-permute-start(bf16[512,128]{1,0:T(8,128)(2,1)S(1)} %get-tuple-element.202), channel_id=1, source_target_pairs={{0,12},{4,8},{8,4},{12,0},{1,13},{5,9},{9,5},{13,1},{2,14},{6,10},... | collective-permute-start | bytes 393224 | tf_op jit(solution)/shard_map/ppermute | solution.py:220
  204.8 3.9 %collective-permute-start.38 = (bf16[16,128]{1,0:T(8,128)(2,1)S(1)}, bf16[16,128]{1,0:T(8,128)(2,1)S(1)}, u32[]{:S(2)}, u32[]{:S(2)}) collective-permute-start(bf16[16,128]{1,0:T(8,128)(2,1)S(1)} %slice_bitcast_fusion.8), channel_id=1, source_target_pairs={{0,8},{4,12},{8,0},{12,4},{1,9},{5,13},{9,1},{13,5},{2,10},{6,14},... | collective-permute-start | bytes 12296 | tf_op jit(solution)/shard_map/ppermute | solution.py:220
  205.4 3.4 %collective-permute-start.39 = (bf16[16,128]{1,0:T(8,128)(2,1)S(1)}, bf16[16,128]{1,0:T(8,128)(2,1)S(1)}, u32[]{:S(2)}, u32[]{:S(2)}) collective-permute-start(bf16[16,128]{1,0:T(8,128)(2,1)S(1)} %slice_bitcast_fusion.8), channel_id=1, source_target_pairs={{0,12},{4,8},{8,4},{12,0},{1,13},{5,9},{9,5},{13,1},{2,14},{6,10},... | collective-permute-start | bytes 12296 | tf_op jit(solution)/shard_map/ppermute | solution.py:220
  207.2 1.5 collective-permute-start.36

commit v20 on v17

--- a/solution.py
+++ b/solution.py
@@ -301,7 +301,7 @@
     away = along(away, ends)
     away = [to_other(away[0], 2), to_other(away[1], 3)]
     here, _ = last_scores(last, last_got, far_counts, chosen, pieces[:2], EXTRA)
-    here, second, third = tied(here, second, third)
+    here, third = tied(here, third)
     here = along(here, ends)
     here = [here[0], to_other(here[1], 1)]
     chosen = [part[own_rows:] for part in here]

time: 210 us -> 210 us (level)
    ppermute x13, waiting for transfers between devices: 13.2 us -> 10.5 us  [along(): return lax.ppermute(value, 'test', pairs)]
  transfers between devices with their start and end apart: 40 -> 40, of which waited for: 22 -> 21; matrix products, arithmetic and copies ran while one was open for 3% -> 3% of each run, Pallas kernels for 23% -> 23%
where the time goes in v20:
time: 210 us
  waiting for transfers between devices  76.5 us (36%)
  starting transfers between devices  55.4 us (26%)
  Pallas kernels  55.3 us (26%)
  local copies, waits for them, and re-layouts  15.3 us (7%)
  other arithmetic  6.06 us (3%)
    ppermute x27, waiting for transfers between devices, to_other(): return lax.ppermute(value, 'train', [(k, k ^ r) for k in range(4)])  66 us
    ppermute x13, starting transfers between devices, along(): return lax.ppermute(value, 'test', pairs)  35.3 us
    pallas_call x5, Pallas kernels, product(): pl.pallas_call(functools.partial(product_body, len(blocks)), in_specs=[pl...  33.7 us
    ppermute x27, starting transfers between devices, to_other(): return lax.ppermute(value, 'train', [(k, k ^ r) for k in range(4)])  20.1 us
    unnamed x38, local copies, waits for them, and re-layouts  14 us
    pallas_call x3, Pallas kernels, partial_scores(): pl.pallas_call(functools.partial(scores_body, [piece[:2] for piece in gra...  10.6 us
    ppermute x13, waiting for transfers between devices, along(): return lax.ppermute(value, 'test', pairs)  10.5 us
    pallas_call x5, Pallas kernels, fold(): pl.pallas_call(fold_body, in_specs=[pl.BlockSpec(memory_space=pltpu.SMEM)...  5.82 us
  transfers between devices with their start and end apart: 40, of which 21 were waited for; matrix products, arithmetic and copies ran while one was open for 3% of the time, Pallas kernels for 23%

profile of v20, /device:TPU:0, one launch (start us, length us, event | category | flops | bytes accessed | tf_op | source)
XLA Modules:
  0.0 209.6 jit_solution(11472843487859491651)
XLA Ops:
  1.1 2.6 %collective-permute-start.5 = (bf16[512,2048]{1,0:T(8,128)(2,1)}, bf16[512,2048]{1,0:T(8,128)(2,1)S(1)}, u32[]{:S(2)}, u32[]{:S(2)}) collective-permute-start(bf16[512,2048]{1,0:T(8,128)(2,1)} %refs_0_.1), channel_id=1, source_target_pairs={{0,8},{4,12},{8,0},{12,4},{1,9},{5,13},{9,1},{13,5},{2,10},{6,14},... | collective-permute-start | bytes 6291464 | tf_op jit(solution)/shard_map/ppermute | solution.py:220
  3.7 1.6 collective-permute-start
  5.3 2.0 collective-permute-start.1
  7.4 1.6 copy-done.8
  9.0 2.0 hold.1
  11.0 1.4 copy-done.2
  12.4 1.3 copy-done.4
  13.7 3.4 %copy-done = bf16[2048,2048]{1,0:T(8,128)(2,1)S(1)} copy-done((bf16[2048,2048]{1,0:T(8,128)(2,1)S(1)}, bf16[2048,2048]{1,0:T(8,128)(2,1)}, u32[]{:S(2)}) %copy-start) | copy-done | bytes 8388632
  17.1 5.6 %product.5 = (f32[256,2048]{1,0:T(8,128)S(1)}, bf16[128,2048]{1,0:T(8,128)(2,1)S(1)}, bf16[128,2048]{1,0:T(8,128)(2,1)S(1)}) custom-call(s32[3]{0:T(128)S(1)} %pad_add_fusion.flags, bf16[512,2048]{1,0:T(8,128)(2,1)S(1)} %copy-done.11, bf16[2048,2048]{1,0:T(8,128)(2,1)S(1)} %copy-done), custom_call_target="tpu_custom_call" | custom-call | flops 1 | bytes 1 | tf_op jit(solution)/shard_map/product/pallas_call | solution.py:80
  23.3 26.9 %collective-permute-done.5.refs_4_.refs_6_.refs_0_ = bf16[512,2048]{1,0:T(8,128)(2,1)S(1)} collective-permute-done((bf16[512,2048]{1,0:T(8,128)(2,1)}, bf16[512,2048]{1,0:T(8,128)(2,1)S(1)}, u32[]{:S(2)}, u32[]{:S(2)}) %collective-permute-start.5) | collective-permute-done | bytes 2097184 | tf_op jit(solution)/shard_map/ppermute | solution.py:220
  50.9 1.8 fold.5
  53.0 1.5 collective-permute-done.7.refs_6_.refs_8_.refs_2_
  54.5 2.1 %collective-permute-start.8 = (bf16[512,2048]{1,0:T(8,128)(2,1)}, bf16[512,2048]{1,0:T(8,128)(2,1)}, u32[]{:S(2)}, u32[]{:S(2)}) collective-permute-start(bf16[512,2048]{1,0:T(8,128)(2,1)} %collective-permute-done.refs_1_.refs_0_), channel_id=1, source_target_pairs={{1,2},{2,1},{5,6},{6,5},{9,10},{10,9},{13,14},{14,13},{17,18},{18,... | collective-permute-start | bytes 6291464 | tf_op jit(solution)/shard_map/ppermute | solution.py:217
  56.7 1.3 collective-permute-start.9
  57.9 1.8 collective-permute-start.12
  59.8 8.3 %product.6 = (f32[256,2048]{1,0:T(8,128)S(1)}, bf16[128,2048]{1,0:T(8,128)(2,1)}, bf16[128,2048]{1,0:T(8,128)(2,1)}) custom-call(s32[3]{0:T(128)S(1)} %pad_add_fusion.flags, bf16[512,2048]{1,0:T(8,128)(2,1)} %collective-permute-done.1.refs_0_, bf16[512,2048]{1,0:T(8,128)(2,1)} %collective-permute-done.refs_1_.refs_0_, bf16[2048,2048]{1,0:T(8,128)(2,1)S(1)} %bitcast.115), custom_call_target="tpu_custom_call" | custom-call | flops 1 | bytes 1 | tf_op jit(solution)/shard_map/product/pallas_call | solution.py:80
  68.1 1.3 copy-done.9
  70.1 1.6 collective-permute-done.10.refs_0_
  72.4 1.6 copy-done.10
  74.0 1.5 fold.6
  75.6 8.0 %collective-permute-done.12.refs_3_ = f32[128,2048]{1,0:T(8,128)} collective-permute-done((f32[128,2048]{1,0:T(8,128)}, f32[128,2048]{1,0:T(8,128)}, u32[]{:S(2)}, u32[]{:S(2)}) %collective-permute-start.12) | collective-permute-done | bytes 1048608 | tf_op jit(solution)/shard_map/ppermute | solution.py:220
  83.5 1.7 collective-permute-start.15
  85.3 3.4 %copy-done.1 = bf16[2048,2048]{1,0:T(8,128)(2,1)S(1)} copy-done((bf16[2048,2048]{1,0:T(8,128)(2,1)S(1)}, bf16[2048,2048]{1,0:T(8,128)(2,1)}, u32[]{:S(2)}) %copy-start.1) | copy-done | bytes 8388632
  88.7 6.8 %product.7 = (f32[256,2048]{1,0:T(8,128)S(1)}, bf16[128,2048]{1,0:T(8,128)(2,1)S(1)}, bf16[128,2048]{1,0:T(8,128)(2,1)S(1)}) custom-call(s32[3]{0:T(128)S(1)} %pad_add_fusion.flags, bf16[512,2048]{1,0:T(8,128)(2,1)} %collective-permute-done.refs_1_.refs_0_, bf16[2048,2048]{1,0:T(8,128)(2,1)S(1)} %copy-done.1), custom_call_target="tpu_custom_call" | custom-call | flops 1 | bytes 1 | tf_op jit(solution)/shard_map/product/pallas_call | solution.py:80
  96.1 1.7 convert_add_fusion.1
  97.8 5.5 %collective-permute-start.16 = (s32[512,16]{0,1:T(8,128)S(1)}, s32[512,16]{0,1:T(8,128)S(1)}, u32[]{:S(2)}, u32[]{:S(2)}) collective-permute-start(s32[512,16]{0,1:T(8,128)S(1)} %copy-done.14), channel_id=1, source_target_pairs={{0,3},{3,0},{4,7},{7,4},{8,11},{11,8},{12,15},{15,12},{16,19},{19,... | collective-permute-start | bytes 98312 | tf_op jit(solution)/shard_map/ppermute | solution.py:217
  103.4 2.4 %scores.3 = bf16[4,512,128]{2,1,0:T(8,128)(2,1)S(1)} custom-call(f32[128,2048]{1,0:T(8,128)S(1)} %get-tuple-element.110.refs_0_, bf16[128,2048]{1,0:T(8,128)(2,1)S(1)} %collective-permute-done.15.refs_1_, bf16[512,2048]{1,0:T(8,128)(2,1)S(1)} %copy-done.3, bf16[512,2048]{1,0:T(8,128)(2,1)S(1)} %copy-done.5, ...), custom_call_target="tpu_custom_call" | custom-call | flops 2000000000 | bytes 1048576 | tf_op jit(solution)/shard_map/scores/pallas_call | solution.py:144
  105.8 0.8 fold.7
  106.6 1.3 collective-permute-done.9.refs_1_
  107.9 1.3 collective-permute-start.17
  109.2 7.3 %product.8 = (f32[256,2048]{1,0:T(8,128)S(1)}, bf16[128,2048]{1,0:T(8,128)(2,1)S(1)}, bf16[128,2048]{1,0:T(8,128)(2,1)S(1)}) custom-call(s32[3]{0:T(128)S(1)} %pad_add_fusion.flags, bf16[512,2048]{1,0:T(8,128)(2,1)} %collective-permute-done.8.refs_0_, bf16[512,2048]{1,0:T(8,128)(2,1)} %collective-permute-done.9.refs_1_, bf16[2048,2048]{1,0:T(8,128)(2,1)S(1)} %bitcast.117), custom_call_target="tpu_custom_call" | custom-call | flops 1 | bytes 1 | tf_op jit(solution)/shard_map/product/pallas_call | solution.py:80
  117.2 1.4 collective-permute-done.19.refs_0_
  119.3 0.8 fold.8
  120.1 1.6 collective-permute-start.21
  121.7 4.7 %collective-permute-start.22 = (bf16[4,512,128]{2,1,0:T(8,128)(2,1)S(1)}, bf16[4,512,128]{2,1,0:T(8,128)(2,1)S(1)}, u32[]{:S(2)}, u32[]{:S(2)}) collective-permute-start(bf16[4,512,128]{2,1,0:T(8,128)(2,1)S(1)} %scores.3), channel_id=1, source_target_pairs={{0,1},{3,2},{4,5},{7,6},{8,9},{11,10},{12,13},{15,14},{16,17},{19,... | collective-permute-start | bytes 1572872 | tf_op jit(solution)/shard_map/ppermute | solution.py:217
  126.4 0.9 collective-permute-start.23
  127.9 7.1 %collective-permute-done.21.refs_1_ = bf16[128,2048]{1,0:T(8,128)(2,1)S(1)} collective-permute-done((bf16[128,2048]{1,0:T(8,128)(2,1)S(1)}, bf16[128,2048]{1,0:T(8,128)(2,1)S(1)}, u32[]{:S(2)}, u32[]{:S(2)}) %collective-permute-start.21) | collective-permute-done | bytes 524320 | tf_op jit(solution)/shard_map/ppermute | solution.py:220
  135.0 2.6 %collective-permute-done.22 = bf16[4,512,128]{2,1,0:T(8,128)(2,1)S(1)} collective-permute-done((bf16[4,512,128]{2,1,0:T(8,128)(2,1)S(1)}, bf16[4,512,128]{2,1,0:T(8,128)(2,1)S(1)}, u32[]{:S(2)}, u32[]{:S(2)}) %collective-permute-start.22) | collective-permute-done | bytes 524320 | tf_op jit(solution)/shard_map/ppermute | solution.py:217
  137.6 2.4 %scores.5 = bf16[4,512,128]{2,1,0:T(8,128)(2,1)S(1)} custom-call(f32[128,2048]{1,0:T(8,128)S(1)} %get-tuple-element.140.refs_0_, bf16[128,2048]{1,0:T(8,128)(2,1)S(1)} %collective-permute-done.21.refs_1_, bf16[512,2048]{1,0:T(8,128)(2,1)S(1)} %copy-done.3, bf16[512,2048]{1,0:T(8,128)(2,1)S(1)} %copy-done.5, ...), custom_call_target="tpu_custom_call" | custom-call | flops 1 | bytes 1 | tf_op jit(solution)/shard_map/scores/pallas_call | solution.py:144
  140.7 1.7 convert_add_fusion.counts
  142.3 3.1 %collective-permute-done.18.refs_1_ = bf16[128,2048]{1,0:T(8,128)(2,1)S(1)} collective-permute-done((bf16[128,2048]{1,0:T(8,128)(2,1)S(1)}, bf16[128,2048]{1,0:T(8,128)(2,1)S(1)}, u32[]{:S(2)}, u32[]{:S(2)}) %collective-permute-start.18) | collective-permute-done | bytes 524320 | tf_op jit(solution)/shard_map/ppermute | solution.py:220
  145.4 5.8 %scores.4 = (f32[4,512,128]{2,1,0:T(8,128)S(1)}, f32[4,512,128]{2,1,0:T(8,128)S(1)}) custom-call(f32[128,2048]{1,0:T(8,128)S(1)} %get-tuple-element.119.refs_0_, bf16[128,2048]{1,0:T(8,128)(2,1)S(1)} %collective-permute-done.18.refs_1_, f32[128,2048]{1,0:T(8,128)S(1)} %copy-done.13, f32[128,2048]{1,0:T(8,128)} %collective-permute-done.12.refs_3_, ...), custom_call_target="tpu_custom_call" | custom-call | flops 1 | bytes 1 | tf_op jit(solution)/shard_map/scores/pallas_call | solution.py:144
  151.2 5.6 %collective-permute-done.17.refs_0_ = bf16[512,2048]{1,0:T(8,128)(2,1)S(1)} collective-permute-done((bf16[512,2048]{1,0:T(8,128)(2,1)}, bf16[512,2048]{1,0:T(8,128)(2,1)S(1)}, u32[]{:S(2)}, u32[]{:S(2)}) %collective-permute-start.17) | collective-permute-done | bytes 2097184 | tf_op jit(solution)/shard_map/ppermute | solution.py:217
  156.8 5.6 %product.9 = (f32[256,2048]{1,0:T(8,128)S(1)}, bf16[128,2048]{1,0:T(8,128)(2,1)S(1)}, bf16[128,2048]{1,0:T(8,128)(2,1)S(1)}) custom-call(s32[3]{0:T(128)S(1)} %pad_add_fusion.flags, bf16[512,2048]{1,0:T(8,128)(2,1)S(1)} %collective-permute-done.17.refs_0_, bf16[2048,2048]{1,0:T(8,128)(2,1)S(1)} %bitcast.117), custom_call_target="tpu_custom_call" | custom-call | flops 1 | bytes 1 | tf_op jit(solution)/shard_map/product/pallas_call | solution.py:80
  163.0 1.4 collective-permute-done.26.refs_0_
  165.1 0.8 fold.9
  166.0 1.6 collective-permute-start.28
  167.7 1.3 collective-permute-start.29
  169.0 6.3 %collective-permute-start.25 = (bf16[4,512,128]{2,1,0:T(8,128)(2,1)S(1)}, bf16[4,512,128]{2,1,0:T(8,128)(2,1)S(1)}, u32[]{:S(2)}, u32[]{:S(2)}) collective-permute-start(bf16[4,512,128]{2,1,0:T(8,128)(2,1)S(1)} %scores.5), channel_id=1, source_target_pairs={{0,2},{3,1},{4,6},{7,5},{8,10},{11,9},{12,14},{15,13},{16,18},{19,... | collective-permute-start | bytes 1572872 | tf_op jit(solution)/shard_map/ppermute | solution.py:217
  175.3 4.7 %collective-permute-done.28.got = bf16[128,2048]{1,0:T(8,128)(2,1)S(1)} collective-permute-done((bf16[128,2048]{1,0:T(8,128)(2,1)S(1)}, bf16[128,2048]{1,0:T(8,128)(2,1)S(1)}, u32[]{:S(2)}, u32[]{:S(2)}) %collective-permute-start.28) | collective-permute-done | bytes 524320 | tf_op jit(solution)/shard_map/ppermute | solution.py:220
  180.0 1.3 last_scores.2
  181.3 1.9 last_scores.3
  183.3 5.1 %collective-permute-start.34 = (bf16[2,512,128]{2,1,0:T(8,128)(2,1)S(1)}, bf16[2,512,128]{2,1,0:T(8,128)(2,1)}, u32[]{:S(2)}, u32[]{:S(2)}) collective-permute-start(bf16[2,512,128]{2,1,0:T(8,128)(2,1)S(1)} %get-tuple-element.167), channel_id=1, source_target_pairs={{0,3},{3,0},{4,7},{7,4},{8,11},{11,8},{12,15},{15,12},{16,19},{19,... | collective-permute-start | bytes 786440 | tf_op jit(solution)/shard_map/ppermute | solution.py:217
  188.9 1.6 collective-permute-start.30
  191.1 2.5 %collective-permute-start.33 = (bf16[2,528,128]{2,1,0:T(8,128)(2,1)S(1)}, bf16[2,528,128]{2,1,0:T(8,128)(2,1)S(1)}, u32[]{:S(2)}, u32[]{:S(2)}) collective-permute-start(bf16[2,528,128]{2,1,0:T(8,128)(2,1)S(1)} %get-tuple-element.166), channel_id=1, source_target_pairs={{0,3},{3,0},{4,7},{7,4},{8,11},{11,8},{12,15},{15,12},{16,19},{19,... | collective-permute-start | bytes 811016 | tf_op jit(solution)/shard_map/ppermute | solution.py:217
  193.7 0.9 collective-permute-done.34
  194.6 1.0 slice_bitcast_fusion.5
  195.5 1.6 collective-permute-start.35
  197.1 1.2 collective-permute-done.30
  198.3 4.7 %collective-permute-done.32 = f32[520,128]{1,0:T(8,128)S(1)} collective-permute-done((f32[520,128]{1,0:T(8,128)S(1)}, f32[520,128]{1,0:T(8,128)S(1)}, u32[]{:S(2)}, u32[]{:S(2)}) %collective-permute-start.32) | collective-permute-done | bytes 266272 | tf_op jit(solution)/shard_map/ppermute | solution.py:220
  203.2 1.5 collective-permute-start.38
  204.7 1.0 collective-permute-start.39
  205.8 1.9 collective-permute-done.38
  208.4 1.1 slice_add_fusion
  (97 shorter events, 10.5 us)
Async XLA Ops:
  0.6 6.8 %collective-permute-start.2 = (bf16[512,2048]{1,0:T(8,128)(2,1)}, bf16[512,2048]{1,0:T(8,128)(2,1)}, u32[]{:S(2)}, u32[]{:S(2)}) collective-permute-start(bf16[512,2048]{1,0:T(8,128)(2,1)} %refs_0_.1), channel_id=1, source_target_pairs={{0,4},{4,0},{8,12},{12,8},{1,5},{5,1},{9,13},{13,9},{2,6},{6,2},{1... | collective-permute-start | bytes 6291464 | tf_op jit(solution)/shard_map/ppermute | solution.py:220
  1.1 49.0 %collective-permute-start.5 = (bf16[512,2048]{1,0:T(8,128)(2,1)}, bf16[512,2048]{1,0:T(8,128)(2,1)S(1)}, u32[]{:S(2)}, u32[]{:S(2)}) collective-permute-start(bf16[512,2048]{1,0:T(8,128)(2,1)} %refs_0_.1), channel_id=1, source_target_pairs={{0,8},{4,12},{8,0},{12,4},{1,9},{5,13},{9,1},{13,5},{2,10},{6,14},... | collective-permute-start | bytes 6291464 | tf_op jit(solution)/shard_map/ppermute | solution.py:220
  3.7 49.0 %collective-permute-start = (bf16[512,2048]{1,0:T(8,128)(2,1)}, bf16[512,2048]{1,0:T(8,128)(2,1)}, u32[]{:S(2)}, u32[]{:S(2)}) collective-permute-start(bf16[512,2048]{1,0:T(8,128)(2,1)} %refs_0_.2), channel_id=1, source_target_pairs={{0,1},{1,0},{2,3},{3,2},{4,5},{5,4},{6,7},{7,6},{8,9},{9,8},{10,11... | collective-permute-start | bytes 6291464 | tf_op jit(solution)/shard_map/ppermute | solution.py:217
  5.3 47.4 %collective-permute-start.1 = (bf16[512,2048]{1,0:T(8,128)(2,1)}, bf16[512,2048]{1,0:T(8,128)(2,1)}, u32[]{:S(2)}, u32[]{:S(2)}) collective-permute-start(bf16[512,2048]{1,0:T(8,128)(2,1)} %refs_0_.2), channel_id=1, source_target_pairs={{1,2},{2,1},{5,6},{6,5},{9,10},{10,9},{13,14},{14,13},{17,18},{18,... | collective-permute-start | bytes 6291464 | tf_op jit(solution)/shard_map/ppermute | solution.py:217
  7.4 1.6 copy-start.8
  9.0 4.7 %copy-start.11 = (bf16[512,2048]{1,0:T(8,128)(2,1)S(1)}, bf16[512,2048]{1,0:T(8,128)(2,1)}, u32[]{:S(2)}) copy-start(bf16[512,2048]{1,0:T(8,128)(2,1)} %refs_0_.2) | copy-start | bytes 6291460
  11.0 1.4 copy-start.2
  12.4 1.3 copy-start.4
  13.7 3.4 %copy-start = (bf16[2048,2048]{1,0:T(8,128)(2,1)S(1)}, bf16[2048,2048]{1,0:T(8,128)(2,1)}, u32[]{:S(2)}) copy-start(bf16[2048,2048]{1,0:T(8,128)(2,1)} %refs_1_.5) | copy-start | bytes 25165828
  22.7 27.7 %collective-permute-start.3 = (bf16[128,2048]{1,0:T(8,128)(2,1)S(1)}, bf16[128,2048]{1,0:T(8,128)(2,1)S(1)}, u32[]{:S(2)}, u32[]{:S(2)}) collective-permute-start(bf16[128,2048]{1,0:T(8,128)(2,1)S(1)} %get-tuple-element.89), channel_id=1, source_target_pairs={{0,4},{4,0},{8,12},{12,8},{1,5},{5,1},{9,13},{13,9},{2,6},{6,2},{1... | collective-permute-start | bytes 1572872 | tf_op jit(solution)/shard_map/ppermute | solution.py:220
  22.8 28.1 %collective-permute-start.4 = (bf16[128,2048]{1,0:T(8,128)(2,1)S(1)}, bf16[128,2048]{1,0:T(8,128)(2,1)S(1)}, u32[]{:S(2)}, u32[]{:S(2)}) collective-permute-start(bf16[128,2048]{1,0:T(8,128)(2,1)S(1)} %get-tuple-element.90), channel_id=1, source_target_pairs={{0,4},{4,0},{8,12},{12,8},{1,5},{5,1},{9,13},{13,9},{2,6},{6,2},{1... | collective-permute-start | bytes 1572872 | tf_op jit(solution)/shard_map/ppermute | solution.py:220
  50.3 2.7 %collective-permute-start.6 = (bf16[256,2048]{1,0:T(8,128)(2,1)S(1)}, bf16[256,2048]{1,0:T(8,128)(2,1)S(1)}, u32[]{:S(2)}, u32[]{:S(2)}) collective-permute-start(bf16[256,2048]{1,0:T(8,128)(2,1)S(1)} %get-tuple-element.171), channel_id=1, source_target_pairs={{0,4},{4,0},{8,12},{12,8},{1,5},{5,1},{9,13},{13,9},{2,6},{6,2},{1... | collective-permute-start | bytes 3145736 | tf_op jit(solution)/shard_map/ppermute | solution.py:220
  50.4 4.1 %collective-permute-start.7 = (bf16[256,2048]{1,0:T(8,128)(2,1)S(1)}, bf16[256,2048]{1,0:T(8,128)(2,1)S(1)}, u32[]{:S(2)}, u32[]{:S(2)}) collective-permute-start(bf16[256,2048]{1,0:T(8,128)(2,1)S(1)} %get-tuple-element.170), channel_id=1, source_target_pairs={{0,4},{4,0},{8,12},{12,8},{1,5},{5,1},{9,13},{13,9},{2,6},{6,2},{1... | collective-permute-start | bytes 3145736 | tf_op jit(solution)/shard_map/ppermute | solution.py:220
  50.9 8.9 %slice-start = ((s8[8388608]{0:T(1024)(128)(4,1)}), s8[4194304]{0:T(1024)(128)(4,1)S(1)}, s32[]{:S(2)}) async-start(s8[8388608]{0:T(1024)(128)(4,1)} %bitcast.114), calls=%async_computation | async-start | bytes 8388608
  50.9 8.9 %slice-start.1 = ((s8[8388608]{0:T(1024)(128)(4,1)}), s8[4194304]{0:T(1024)(128)(4,1)S(1)}, s32[]{:S(2)}) async-start(s8[8388608]{0:T(1024)(128)(4,1)} %bitcast.114), calls=%async_computation.1 | async-start | bytes 8388608
  52.7 15.4 %copy-start.12 = (f32[128,2048]{1,0:T(8,128)}, f32[128,2048]{1,0:T(8,128)S(1)}, u32[]{:S(2)}) copy-start(f32[128,2048]{1,0:T(8,128)S(1)} %get-tuple-element.121.refs_2_) | copy-start | bytes 3145732
  54.5 13.6 %copy-start.6 = (bf16[256,2048]{1,0:T(8,128)(2,1)}, bf16[256,2048]{1,0:T(8,128)(2,1)S(1)}, u32[]{:S(2)}) copy-start(bf16[256,2048]{1,0:T(8,128)(2,1)S(1)} %collective-permute-done.7.refs_6_.refs_8_.refs_2_) | copy-start | bytes 3145732
  54.5 15.6 %copy-start.14 = (s32[512,16]{0,1:T(8,128)S(1)}, s32[512,16]{0,1:T(8,128)}, u32[]{:S(2)}) copy-start(s32[512,16]{0,1:T(8,128)} %param.7) | copy-start | bytes 98308
  54.5 52.1 %collective-permute-start.8 = (bf16[512,2048]{1,0:T(8,128)(2,1)}, bf16[512,2048]{1,0:T(8,128)(2,1)}, u32[]{:S(2)}, u32[]{:S(2)}) collective-permute-start(bf16[512,2048]{1,0:T(8,128)(2,1)} %collective-permute-done.refs_1_.refs_0_), channel_id=1, source_target_pairs={{1,2},{2,1},{5,6},{6,5},{9,10},{10,9},{13,14},{14,13},{17,18},{18,... | collective-permute-start | bytes 6291464 | tf_op jit(solution)/shard_map/ppermute | solution.py:217
  56.7 51.3 %collective-permute-start.9 = (bf16[512,2048]{1,0:T(8,128)(2,1)}, bf16[512,2048]{1,0:T(8,128)(2,1)}, u32[]{:S(2)}, u32[]{:S(2)}) collective-permute-start(bf16[512,2048]{1,0:T(8,128)(2,1)} %collective-permute-done.1.refs_0_), channel_id=1, source_target_pairs={{1,0},{2,3},{5,4},{6,7},{9,8},{10,11},{13,12},{14,15},{17,16},{18,... | collective-permute-start | bytes 6291464 | tf_op jit(solution)/shard_map/ppermute | solution.py:217
  57.9 25.6 %collective-permute-start.12 = (f32[128,2048]{1,0:T(8,128)}, f32[128,2048]{1,0:T(8,128)}, u32[]{:S(2)}, u32[]{:S(2)}) collective-permute-start(f32[128,2048]{1,0:T(8,128)} %get-tuple-element.101), channel_id=1, source_target_pairs={{0,8},{4,12},{8,0},{12,4},{1,9},{5,13},{9,1},{13,5},{2,10},{6,14},... | collective-permute-start | bytes 3145736 | tf_op jit(solution)/shard_map/ppermute | solution.py:220
  68.1 1.3 copy-start.9
  69.4 2.3 %collective-permute-start.10 = (bf16[128,2048]{1,0:T(8,128)(2,1)}, bf16[128,2048]{1,0:T(8,128)(2,1)}, u32[]{:S(2)}, u32[]{:S(2)}) collective-permute-start(bf16[128,2048]{1,0:T(8,128)(2,1)} %get-tuple-element.98), channel_id=1, source_target_pairs={{0,4},{4,0},{8,12},{12,8},{1,5},{5,1},{9,13},{13,9},{2,6},{6,2},{1... | collective-permute-start | bytes 1572872 | tf_op jit(solution)/shard_map/ppermute | solution.py:220
  69.4 3.0 %collective-permute-start.11 = (bf16[128,2048]{1,0:T(8,128)(2,1)}, bf16[128,2048]{1,0:T(8,128)(2,1)}, u32[]{:S(2)}, u32[]{:S(2)}) collective-permute-start(bf16[128,2048]{1,0:T(8,128)(2,1)} %get-tuple-element.99), channel_id=1, source_target_pairs={{0,4},{4,0},{8,12},{12,8},{1,5},{5,1},{9,13},{13,9},{2,6},{6,2},{1... | collective-permute-start | bytes 1572872 | tf_op jit(solution)/shard_map/ppermute | solution.py:220
  72.4 1.6 copy-start.10
  83.5 14.2 %collective-permute-start.15 = (bf16[128,2048]{1,0:T(8,128)(2,1)S(1)}, bf16[128,2048]{1,0:T(8,128)(2,1)S(1)}, u32[]{:S(2)}, u32[]{:S(2)}) collective-permute-start(bf16[128,2048]{1,0:T(8,128)(2,1)S(1)} %get-tuple-element.111), channel_id=1, source_target_pairs={{0,8},{4,12},{8,0},{12,4},{1,9},{5,13},{9,1},{13,5},{2,10},{6,14},... | collective-permute-start | bytes 1572872 | tf_op jit(solution)/shard_map/ppermute | solution.py:220
  85.3 3.4 %copy-start.1 = (bf16[2048,2048]{1,0:T(8,128)(2,1)S(1)}, bf16[2048,2048]{1,0:T(8,128)(2,1)}, u32[]{:S(2)}) copy-start(bf16[2048,2048]{1,0:T(8,128)(2,1)} %refs_1_.5) | copy-start | bytes 25165828
  88.7 14.6 %copy-start.3 = (bf16[512,2048]{1,0:T(8,128)(2,1)S(1)}, bf16[512,2048]{1,0:T(8,128)(2,1)}, u32[]{:S(2)}) copy-start(bf16[512,2048]{1,0:T(8,128)(2,1)} %copy-done.2) | copy-start | bytes 6291460
  88.7 14.7 %copy-start.5 = (bf16[512,2048]{1,0:T(8,128)(2,1)S(1)}, bf16[512,2048]{1,0:T(8,128)(2,1)}, u32[]{:S(2)}) copy-start(bf16[512,2048]{1,0:T(8,128)(2,1)} %copy-done.4) | copy-start | bytes 6291460
  88.7 14.7 %copy-start.7 = (bf16[256,2048]{1,0:T(8,128)(2,1)S(1)}, bf16[256,2048]{1,0:T(8,128)(2,1)}, u32[]{:S(2)}) copy-start(bf16[256,2048]{1,0:T(8,128)(2,1)} %copy-done.6) | copy-start | bytes 3145732
  88.7 20.5 %slice-start.2 = ((s8[8388608]{0:T(1024)(128)(4,1)}), s8[4194304]{0:T(1024)(128)(4,1)S(1)}, s32[]{:S(2)}) async-start(s8[8388608]{0:T(1024)(128)(4,1)} %bitcast.116), calls=%async_computation.2 | async-start | bytes 8388608
  95.5 10.2 %collective-permute-start.13 = (bf16[128,2048]{1,0:T(8,128)(2,1)S(1)}, bf16[128,2048]{1,0:T(8,128)(2,1)S(1)}, u32[]{:S(2)}, u32[]{:S(2)}) collective-permute-start(bf16[128,2048]{1,0:T(8,128)(2,1)S(1)} %get-tuple-element.104), channel_id=1, source_target_pairs={{0,4},{4,0},{8,12},{12,8},{1,5},{5,1},{9,13},{13,9},{2,6},{6,2},{1... | collective-permute-start | bytes 1572872 | tf_op jit(solution)/shard_map/ppermute | solution.py:220
  95.6 10.1 %collective-permute-start.14 = (bf16[128,2048]{1,0:T(8,128)(2,1)S(1)}, bf16[128,2048]{1,0:T(8,128)(2,1)S(1)}, u32[]{:S(2)}, u32[]{:S(2)}) collective-permute-start(bf16[128,2048]{1,0:T(8,128)(2,1)S(1)} %get-tuple-element.105), channel_id=1, source_target_pairs={{0,4},{4,0},{8,12},{12,8},{1,5},{5,1},{9,13},{13,9},{2,6},{6,2},{1... | collective-permute-start | bytes 1572872 | tf_op jit(solution)/shard_map/ppermute | solution.py:220
  97.8 8.8 %collective-permute-start.16 = (s32[512,16]{0,1:T(8,128)S(1)}, s32[512,16]{0,1:T(8,128)S(1)}, u32[]{:S(2)}, u32[]{:S(2)}) collective-permute-start(s32[512,16]{0,1:T(8,128)S(1)} %copy-done.14), channel_id=1, source_target_pairs={{0,3},{3,0},{4,7},{7,4},{8,11},{11,8},{12,15},{15,12},{16,19},{19,... | collective-permute-start | bytes 98312 | tf_op jit(solution)/shard_map/ppermute | solution.py:217
  103.3 5.9 %slice-start.3 = ((s8[8388608]{0:T(1024)(128)(4,1)}), s8[4194304]{0:T(1024)(128)(4,1)S(1)}, s32[]{:S(2)}) async-start(s8[8388608]{0:T(1024)(128)(4,1)} %bitcast.116), calls=%async_computation.3 | async-start | bytes 8388608
  107.9 48.9 %collective-permute-start.17 = (bf16[512,2048]{1,0:T(8,128)(2,1)}, bf16[512,2048]{1,0:T(8,128)(2,1)S(1)}, u32[]{:S(2)}, u32[]{:S(2)}) collective-permute-start(bf16[512,2048]{1,0:T(8,128)(2,1)} %collective-permute-done.8.refs_0_), channel_id=1, source_target_pairs={{1,0},{2,3},{5,4},{6,7},{9,8},{10,11},{13,12},{14,15},{17,16},{18,... | collective-permute-start | bytes 6291464 | tf_op jit(solution)/shard_map/ppermute | solution.py:217
  116.6 2.0 collective-permute-start.19
  116.7 2.6 %collective-permute-start.20 = (bf16[128,2048]{1,0:T(8,128)(2,1)S(1)}, bf16[128,2048]{1,0:T(8,128)(2,1)S(1)}, u32[]{:S(2)}, u32[]{:S(2)}) collective-permute-start(bf16[128,2048]{1,0:T(8,128)(2,1)S(1)} %get-tuple-element.132), channel_id=1, source_target_pairs={{0,4},{4,0},{8,12},{12,8},{1,5},{5,1},{9,13},{13,9},{2,6},{6,2},{1... | collective-permute-start | bytes 1572872 | tf_op jit(solution)/shard_map/ppermute | solution.py:220
  120.1 14.8 %collective-permute-start.21 = (bf16[128,2048]{1,0:T(8,128)(2,1)S(1)}, bf16[128,2048]{1,0:T(8,128)(2,1)S(1)}, u32[]{:S(2)}, u32[]{:S(2)}) collective-permute-start(bf16[128,2048]{1,0:T(8,128)(2,1)S(1)} %get-tuple-element.136), channel_id=1, source_target_pairs={{0,8},{4,12},{8,0},{12,4},{1,9},{5,13},{9,1},{13,5},{2,10},{6,14},... | collective-permute-start | bytes 1572872 | tf_op jit(solution)/shard_map/ppermute | solution.py:220
  121.7 15.9 %collective-permute-start.22 = (bf16[4,512,128]{2,1,0:T(8,128)(2,1)S(1)}, bf16[4,512,128]{2,1,0:T(8,128)(2,1)S(1)}, u32[]{:S(2)}, u32[]{:S(2)}) collective-permute-start(bf16[4,512,128]{2,1,0:T(8,128)(2,1)S(1)} %scores.3), channel_id=1, source_target_pairs={{0,1},{3,2},{4,5},{7,6},{8,9},{11,10},{12,13},{15,14},{16,17},{19,... | collective-permute-start | bytes 1572872 | tf_op jit(solution)/shard_map/ppermute | solution.py:217
  126.4 11.2 %collective-permute-start.23 = (bf16[4,512,128]{2,1,0:T(8,128)(2,1)S(1)}, bf16[4,512,128]{2,1,0:T(8,128)(2,1)S(1)}, u32[]{:S(2)}, u32[]{:S(2)}) collective-permute-start(bf16[4,512,128]{2,1,0:T(8,128)(2,1)S(1)} %scores.3), channel_id=1, source_target_pairs={{1,2},{2,1},{5,6},{6,5},{9,10},{10,9},{13,14},{14,13},{17,18},{18,... | collective-permute-start | bytes 1572872 | tf_op jit(solution)/shard_map/ppermute | solution.py:217
  127.3 18.1 %collective-permute-start.18 = (bf16[128,2048]{1,0:T(8,128)(2,1)S(1)}, bf16[128,2048]{1,0:T(8,128)(2,1)S(1)}, u32[]{:S(2)}, u32[]{:S(2)}) collective-permute-start(bf16[128,2048]{1,0:T(8,128)(2,1)S(1)} %get-tuple-element.120), channel_id=1, source_target_pairs={{0,8},{4,12},{8,0},{12,4},{1,9},{5,13},{9,1},{13,5},{2,10},{6,14},... | collective-permute-start | bytes 1572872 | tf_op jit(solution)/shard_map/ppermute | solution.py:220
  127.9 17.5 %copy-start.13 = (f32[128,2048]{1,0:T(8,128)S(1)}, f32[128,2048]{1,0:T(8,128)}, u32[]{:S(2)}) copy-start(f32[128,2048]{1,0:T(8,128)} %copy-done.12) | copy-start | bytes 3145732
  140.0 11.3 %collective-permute-start.24 = (bf16[4,512,128]{2,1,0:T(8,128)(2,1)S(1)}, bf16[4,512,128]{2,1,0:T(8,128)(2,1)S(1)}, u32[]{:S(2)}, u32[]{:S(2)}) collective-permute-start(bf16[4,512,128]{2,1,0:T(8,128)(2,1)S(1)} %scores.5), channel_id=1, source_target_pairs={{1,2},{2,1},{5,6},{6,5},{9,10},{10,9},{13,14},{14,13},{17,18},{18,... | collective-permute-start | bytes 1572872 | tf_op jit(solution)/shard_map/ppermute | solution.py:217
  162.4 2.0 collective-permute-start.26
  162.5 2.6 %collective-permute-start.27 = (bf16[128,2048]{1,0:T(8,128)(2,1)S(1)}, bf16[128,2048]{1,0:T(8,128)(2,1)S(1)}, u32[]{:S(2)}, u32[]{:S(2)}) collective-permute-start(bf16[128,2048]{1,0:T(8,128)(2,1)S(1)} %get-tuple-element.151), channel_id=1, source_target_pairs={{0,4},{4,0},{8,12},{12,8},{1,5},{5,1},{9,13},{13,9},{2,6},{6,2},{1... | collective-permute-start | bytes 1572872 | tf_op jit(solution)/shard_map/ppermute | solution.py:220
  166.0 14.0 %collective-permute-start.28 = (bf16[128,2048]{1,0:T(8,128)(2,1)S(1)}, bf16[128,2048]{1,0:T(8,128)(2,1)S(1)}, u32[]{:S(2)}, u32[]{:S(2)}) collective-permute-start(bf16[128,2048]{1,0:T(8,128)(2,1)S(1)} %get-tuple-element.153), channel_id=1, source_target_pairs={{0,8},{4,12},{8,0},{12,4},{1,9},{5,13},{9,1},{13,5},{2,10},{6,14},... | collective-permute-start | bytes 1572872 | tf_op jit(solution)/shard_map/ppermute | solution.py:220
  167.7 15.6 %collective-permute-start.29 = (bf16[4,512,128]{2,1,0:T(8,128)(2,1)S(1)}, bf16[4,512,128]{2,1,0:T(8,128)(2,1)S(1)}, u32[]{:S(2)}, u32[]{:S(2)}) collective-permute-start(bf16[4,512,128]{2,1,0:T(8,128)(2,1)S(1)} %add_convert_fusion), channel_id=1, source_target_pairs={{1,0},{2,3},{5,4},{6,7},{9,8},{10,11},{13,12},{14,15},{17,16},{18,... | collective-permute-start | bytes 1572872 | tf_op jit(solution)/shard_map/ppermute | solution.py:217
  169.0 19.4 %collective-permute-start.25 = (bf16[4,512,128]{2,1,0:T(8,128)(2,1)S(1)}, bf16[4,512,128]{2,1,0:T(8,128)(2,1)S(1)}, u32[]{:S(2)}, u32[]{:S(2)}) collective-permute-start(bf16[4,512,128]{2,1,0:T(8,128)(2,1)S(1)} %scores.5), channel_id=1, source_target_pairs={{0,2},{3,1},{4,6},{7,5},{8,10},{11,9},{12,14},{15,13},{16,18},{19,... | collective-permute-start | bytes 1572872 | tf_op jit(solution)/shard_map/ppermute | solution.py:217
  183.3 11.3 %collective-permute-start.34 = (bf16[2,512,128]{2,1,0:T(8,128)(2,1)S(1)}, bf16[2,512,128]{2,1,0:T(8,128)(2,1)}, u32[]{:S(2)}, u32[]{:S(2)}) collective-permute-start(bf16[2,512,128]{2,1,0:T(8,128)(2,1)S(1)} %get-tuple-element.167), channel_id=1, source_target_pairs={{0,3},{3,0},{4,7},{7,4},{8,11},{11,8},{12,15},{15,12},{16,19},{19,... | collective-permute-start | bytes 786440 | tf_op jit(solution)/shard_map/ppermute | solution.py:217
  188.9 9.4 %collective-permute-start.30 = (f32[520,128]{1,0:T(8,128)S(1)}, f32[520,128]{1,0:T(8,128)S(1)}, u32[]{:S(2)}, u32[]{:S(2)}) collective-permute-start(f32[520,128]{1,0:T(8,128)S(1)} %get-tuple-element.222), channel_id=1, source_target_pairs={{0,8},{4,12},{8,0},{12,4},{1,9},{5,13},{9,1},{13,5},{2,10},{6,14},... | collective-permute-start | bytes 798728 | tf_op jit(solution)/shard_map/ppermute | solution.py:220
  190.5 7.8 %collective-permute-start.31 = (f32[520,128]{1,0:T(8,128)S(1)}, f32[520,128]{1,0:T(8,128)S(1)}, u32[]{:S(2)}, u32[]{:S(2)}) collective-permute-start(f32[520,128]{1,0:T(8,128)S(1)} %get-tuple-element.223), channel_id=1, source_target_pairs={{0,4},{4,0},{8,12},{12,8},{1,5},{5,1},{9,13},{13,9},{2,6},{6,2},{1... | collective-permute-start | bytes 798728 | tf_op jit(solution)/shard_map/ppermute | solution.py:220
  190.5 12.6 %collective-permute-start.32 = (f32[520,128]{1,0:T(8,128)S(1)}, f32[520,128]{1,0:T(8,128)S(1)}, u32[]{:S(2)}, u32[]{:S(2)}) collective-permute-start(f32[520,128]{1,0:T(8,128)S(1)} %get-tuple-element.224), channel_id=1, source_target_pairs={{0,12},{4,8},{8,4},{12,0},{1,13},{5,9},{9,5},{13,1},{2,14},{6,10},... | collective-permute-start | bytes 798728 | tf_op jit(solution)/shard_map/ppermute | solution.py:220
  191.1 12.1 %collective-permute-start.33 = (bf16[2,528,128]{2,1,0:T(8,128)(2,1)S(1)}, bf16[2,528,128]{2,1,0:T(8,128)(2,1)S(1)}, u32[]{:S(2)}, u32[]{:S(2)}) collective-permute-start(bf16[2,528,128]{2,1,0:T(8,128)(2,1)S(1)} %get-tuple-element.166), channel_id=1, source_target_pairs={{0,3},{3,0},{4,7},{7,4},{8,11},{11,8},{12,15},{15,12},{16,19},{19,... | collective-permute-start | bytes 811016 | tf_op jit(solution)/shard_map/ppermute | solution.py:217
  195.5 12.8 %collective-permute-start.35 = (bf16[512,128]{1,0:T(8,128)(2,1)S(1)}, bf16[512,128]{1,0:T(8,128)(2,1)S(1)}, u32[]{:S(2)}, u32[]{:S(2)}) collective-permute-start(bf16[512,128]{1,0:T(8,128)(2,1)S(1)} %get-tuple-element.189), channel_id=1, source_target_pairs={{0,8},{4,12},{8,0},{12,4},{1,9},{5,13},{9,1},{13,5},{2,10},{6,14},... | collective-permute-start | bytes 393224 | tf_op jit(solution)/shard_map/ppermute | solution.py:220
  198.3 10.1 %collective-permute-start.37 = (bf16[512,128]{1,0:T(8,128)(2,1)S(1)}, bf16[512,128]{1,0:T(8,128)(2,1)S(1)}, u32[]{:S(2)}, u32[]{:S(2)}) collective-permute-start(bf16[512,128]{1,0:T(8,128)(2,1)S(1)} %get-tuple-element.188), channel_id=1, source_target_pairs={{0,12},{4,8},{8,4},{12,0},{1,13},{5,9},{9,5},{13,1},{2,14},{6,10},... | collective-permute-start | bytes 393224 | tf_op jit(solution)/shard_map/ppermute | solution.py:220
  203.2 4.5 %collective-permute-start.38 = (bf16[16,128]{1,0:T(8,128)(2,1)S(1)}, bf16[16,128]{1,0:T(8,128)(2,1)S(1)}, u32[]{:S(2)}, u32[]{:S(2)}) collective-permute-start(bf16[16,128]{1,0:T(8,128)(2,1)S(1)} %slice_bitcast_fusion.8), channel_id=1, source_target_pairs={{0,8},{4,12},{8,0},{12,4},{1,9},{5,13},{9,1},{13,5},{2,10},{6,14},... | collective-permute-start | bytes 12296 | tf_op jit(solution)/shard_map/ppermute | solution.py:220
  204.7 3.1 %collective-permute-start.39 = (bf16[16,128]{1,0:T(8,128)(2,1)S(1)}, bf16[16,128]{1,0:T(8,128)(2,1)S(1)}, u32[]{:S(2)}, u32[]{:S(2)}) collective-permute-start(bf16[16,128]{1,0:T(8,128)(2,1)S(1)} %slice_bitcast_fusion.8), channel_id=1, source_target_pairs={{0,12},{4,8},{8,4},{12,0},{1,13},{5,9},{9,5},{13,1},{2,14},{6,10},... | collective-permute-start | bytes 12296 | tf_op jit(solution)/shard_map/ppermute | solution.py:220
  205.7 2.1 collective-permute-start.36
